TPU v7x, 32 devices: a whole 2x2x4 slice. The times are simulated.
32 devices in a mesh: section: 2 (over x), group: 4 (over y, core), dp: 4 (over z).
Axes of the slice: x: 2, y: 2, z: 4, core: 2. Of those that a mesh axis runs over, the one named last changes fastest.
Arguments:
- byte_states: bfloat16 [64, 1024, 1024], P(('group', 'dp')), may hold values from -6 to 6
- patch_lengths: int32 [64, 256], P(('group', 'dp')), may hold values from 1 to 8, 1024 in all within a row
- patch_docs: int32 [64, 256], P(('group', 'dp')), may hold values from 0 to 7, never falling along the last dimension, each value on 1 to 64 neighbouring positions
- attn_qkv: bfloat16 [2, 3, 1024, 1024], P('section', None, 'dp'), may hold values from -0.1875 to 0.1875
- attn_out: bfloat16 [2, 1024, 1024], P('section', 'dp'), may hold values from -0.75 to 0.75
- norm_gains: float32 [2, 2, 1024], P('section'), may hold values from 0.25 to 1.75
- ffn_in: bfloat16 [1024, 5632], P(('section', 'dp')), may hold values from -0.1875 to 0.1875
- ffn_down: bfloat16 [2816, 1024], P(('section', 'dp')), may hold values from -0.109375 to 0.109375
- cotangent: bfloat16 [64, 256, 1024], P(('group', 'dp')), may hold values from -6 to 6
Outputs:
- latents: bfloat16 [64, 256, 1024], P(('group', 'dp'), None, 'section')
- byte_grads: bfloat16 [64, 1024, 1024], P(('group', 'dp'), None, 'section')
- grad_attn_qkv: float32 [2, 3, 1024, 1024], P('section', None, 'dp')
- grad_attn_out: float32 [2, 1024, 1024], P('section', 'dp')
- grad_norm_gains: float32 [2, 2, 1024], P('section', None, 'dp')
- grad_ffn_in: float32 [1024, 5632], P(('section', 'dp'))
- grad_ffn_down: float32 [2816, 1024], P(('section', 'dp'))
Inputs may be any that keep to these rules, and one draw needn't show every extreme that they name: `patch_lengths`: each row's 256 patch lengths sum to 1024; in every row the longest patch has exactly 8 bytes. `patch_docs`: document numbers never fall along a row; each of the 8 documents of a row has 1 to 64 patches, and one has exactly that many.
All inputs are finite; a program needn't handle non-finite values.
Results may differ from a plain program's by a relative error of at most 0.023.
Values may be sent and summed in bfloat16 or wider, within the bound.
No kernel may reach another device: no remote copies, remote signals or barrier semaphores. Data moves between devices by JAX's collectives and lax.ppermute only.
A program may use at most 320 MiB of HBM per device.

v0:
```python
import jax
import jax.numpy as jnp
from jax import lax
from jax.sharding import PartitionSpec as P

D = 1024
HEADS = 16
HEAD_DIM = 64
FF = 2816
ROW_BYTES = 1024
MICRO = 4
PATCHES = 256


EPS = 1e-05
head_blocks = 4
masked_score = -1e30


def for_sending(x):
    return jax.tree.map(lambda a: a.astype(jnp.bfloat16) if a.dtype == jnp.float32 else a, x)


def passed_along(value, axis, steps):
    count = lax.axis_size(axis)
    leading, last = (max(0, -steps), min(count, count - steps))
    return lax.ppermute(value, axis, [(source, source + steps) for source in range(leading, last)])


def matmul(left, right):
    return jnp.dot(left, right, preferred_element_type=jnp.float32)


def matmul_tn(left, right):
    return lax.dot_general(
        left, right, (((0,), (0,)), ((), ())), preferred_element_type=jnp.float32
    )


def matmul_nt(left, right):
    return lax.dot_general(
        left, right, (((1,), (1,)), ((), ())), preferred_element_type=jnp.float32
    )


def norm_forward(values, gain_row):
    row_scale = lax.rsqrt(jnp.mean(values * values, axis=-1, keepdims=True) + EPS)
    return (values * row_scale * gain_row, row_scale)


def norm_backward(values, row_scale, gain_row, incoming):
    weighted = incoming * gain_row
    projection = jnp.mean(weighted * values, axis=-1, keepdims=True)
    grad_values = row_scale * weighted - values * (row_scale * row_scale * row_scale) * projection
    grad_gain = jnp.sum(incoming * values * row_scale, axis=0)
    return (grad_values, grad_gain)


def split_heads(matrix):
    return matrix.reshape(matrix.shape[0], head_blocks, HEADS // head_blocks, HEAD_DIM).transpose(
        1, 0, 2, 3
    )


def join_heads(blocks):
    return blocks.transpose(1, 0, 2, 3).reshape(blocks.shape[1], D)


def masked_scores(query_part, key_part, allowed):
    scores = jnp.einsum(
        "qhd,khd->hqk", query_part, key_part, preferred_element_type=jnp.float32
    ) * HEAD_DIM ** (-0.5)
    return jnp.where(allowed[None], scores, masked_score)


def attend(queries, key_rows, value_rows, allowed):

    def head_block(pieces):
        query_part, key_part, value_part = pieces
        scores = masked_scores(query_part, key_part, allowed)
        row_max = jnp.max(scores, axis=-1, keepdims=True)
        exponent = jnp.exp(scores - row_max)
        row_total = jnp.sum(exponent, axis=-1, keepdims=True)
        probabilities = (exponent / row_total).astype(jnp.bfloat16)
        context = jnp.einsum(
            "hqk,khd->qhd", probabilities, value_part, preferred_element_type=jnp.float32
        )
        return (context.astype(jnp.bfloat16), (row_max + jnp.log(row_total))[..., 0])

    context, log_total = lax.map(
        head_block, (split_heads(queries), split_heads(key_rows), split_heads(value_rows))
    )
    return (join_heads(context), log_total)


def attend_backward(queries, key_rows, value_rows, allowed, log_total, grad_context):

    def head_block(pieces):
        query_part, key_part, value_part, total_part, grad_part = pieces
        scores = masked_scores(query_part, key_part, allowed)
        probabilities = jnp.exp(scores - total_part[..., None])
        grad_probs = jnp.einsum(
            "qhd,khd->hqk", grad_part, value_part, preferred_element_type=jnp.float32
        )
        grad_value = jnp.einsum(
            "hqk,qhd->khd",
            probabilities.astype(jnp.bfloat16),
            grad_part,
            preferred_element_type=jnp.float32,
        )
        row_inner = jnp.sum(grad_probs * probabilities, axis=-1, keepdims=True)
        grad_scores = (probabilities * (grad_probs - row_inner)).astype(jnp.bfloat16)
        grad_query = jnp.einsum(
            "hqk,khd->qhd", grad_scores, key_part, preferred_element_type=jnp.float32
        ) * HEAD_DIM ** (-0.5)
        grad_key = jnp.einsum(
            "hqk,qhd->khd", grad_scores, query_part, preferred_element_type=jnp.float32
        ) * HEAD_DIM ** (-0.5)
        return (
            grad_query.astype(jnp.bfloat16),
            grad_key.astype(jnp.bfloat16),
            grad_value.astype(jnp.bfloat16),
        )

    results = lax.map(
        head_block,
        (
            split_heads(queries),
            split_heads(key_rows),
            split_heads(value_rows),
            log_total,
            split_heads(grad_context),
        ),
    )
    return (join_heads(results[0]), join_heads(results[1]), join_heads(results[2]))


def row_tables(lengths, doc_ids):
    patch_ends = jnp.cumsum(lengths)
    positions = lax.iota(jnp.int32, ROW_BYTES)
    patch_ids = lax.iota(jnp.int32, PATCHES)
    owning_patch = jnp.sum((patch_ends[None, :] <= positions[:, None]).astype(jnp.int32), axis=1)
    belongs = owning_patch[None, :] == patch_ids[:, None]
    byte_docs = jnp.sum(jnp.where(belongs, doc_ids[:, None], 0), axis=0)
    cross_mask = (byte_docs[None, :] == doc_ids[:, None]) & (
        positions[None, :] < patch_ends[:, None]
    )
    causal_mask = (doc_ids[None, :] == doc_ids[:, None]) & (
        patch_ids[None, :] <= patch_ids[:, None]
    )
    return (owning_patch, belongs.astype(jnp.bfloat16), cross_mask, causal_mask)


def pool_bytes(byte_row, member, lengths):
    return matmul(member, byte_row) / lengths.astype(jnp.float32)[:, None]


def first_inner(byte_row, pooled, cross_mask, weights, section_gains):
    byte_wide = byte_row.astype(jnp.float32)
    query_normed, query_scale = norm_forward(pooled, section_gains[0])
    key_normed, key_scale = norm_forward(byte_wide, section_gains[1])
    query_in = query_normed.astype(jnp.bfloat16)
    key_in = key_normed.astype(jnp.bfloat16)
    queries = matmul(query_in, weights[0]).astype(jnp.bfloat16)
    key_rows = matmul(key_in, weights[1]).astype(jnp.bfloat16)
    value_rows = matmul(key_in, weights[2]).astype(jnp.bfloat16)
    context, log_total = attend(queries, key_rows, value_rows, cross_mask)
    return (
        byte_wide,
        query_scale,
        key_scale,
        query_in,
        key_in,
        queries,
        key_rows,
        value_rows,
        context,
        log_total,
    )


def first_backward(byte_row, pooled, lengths, tables, weights, section_gains, incoming):
    owning_patch, member, cross_mask, causal_mask = tables
    (
        byte_wide,
        query_scale,
        key_scale,
        query_in,
        key_in,
        queries,
        key_rows,
        value_rows,
        context,
        log_total,
    ) = first_inner(byte_row, pooled, cross_mask, weights, section_gains)
    grad_context = matmul_nt(incoming, weights[3]).astype(jnp.bfloat16)
    grad_query, grad_key, grad_value = attend_backward(
        queries, key_rows, value_rows, cross_mask, log_total, grad_context
    )
    weight_grads = (
        matmul_tn(query_in, grad_query),
        matmul_tn(key_in, grad_key),
        matmul_tn(key_in, grad_value),
        matmul_tn(context, incoming),
    )
    grad_pooled, gain_query = norm_backward(
        pooled, query_scale, section_gains[0], matmul_nt(grad_query, weights[0])
    )
    grad_wide, gain_key = norm_backward(
        byte_wide,
        key_scale,
        section_gains[1],
        matmul_nt(grad_key, weights[1]) + matmul_nt(grad_value, weights[2]),
    )
    per_patch = (grad_pooled + incoming.astype(jnp.float32)) / lengths.astype(jnp.float32)[:, None]
    grad_bytes = grad_wide + jnp.take(per_patch, owning_patch, axis=0)
    return (grad_bytes.astype(jnp.bfloat16), weight_grads, jnp.stack([gain_query, gain_key]))


def second_inner(carried, causal_mask, weights, section_gains, w_in):
    carried_wide = carried.astype(jnp.float32)
    normed, first_scale = norm_forward(carried_wide, section_gains[0])
    normed_in = normed.astype(jnp.bfloat16)
    queries = matmul(normed_in, weights[0]).astype(jnp.bfloat16)
    key_rows = matmul(normed_in, weights[1]).astype(jnp.bfloat16)
    value_rows = matmul(normed_in, weights[2]).astype(jnp.bfloat16)
    context, log_total = attend(queries, key_rows, value_rows, causal_mask)
    residual = carried_wide + matmul(context, weights[3])
    mixed, second_scale = norm_forward(residual, section_gains[1])
    mix_in = mixed.astype(jnp.bfloat16)
    gate_up = matmul(mix_in, w_in)
    gate_value = gate_up[:, :FF]
    upward = gate_up[:, FF:]
    hidden = (jax.nn.silu(gate_value) * upward).astype(jnp.bfloat16)
    return (
        carried_wide,
        first_scale,
        normed_in,
        queries,
        key_rows,
        value_rows,
        context,
        log_total,
        residual,
        second_scale,
        mix_in,
        gate_value,
        upward,
        hidden,
    )


def second_backward(carried, causal_mask, weights, section_gains, w_in, w_down, cot_row):
    (
        carried_wide,
        first_scale,
        normed_in,
        queries,
        key_rows,
        value_rows,
        context,
        log_total,
        residual,
        second_scale,
        mix_in,
        gate_value,
        upward,
        hidden,
    ) = second_inner(carried, causal_mask, weights, section_gains, w_in)
    grad_down = matmul_tn(hidden, cot_row)
    grad_hidden = matmul_nt(cot_row, w_down)
    sigmoid_gate = jax.nn.sigmoid(gate_value)
    grad_gate = grad_hidden * upward * sigmoid_gate * (1.0 + gate_value * (1.0 - sigmoid_gate))
    grad_upward = grad_hidden * gate_value * sigmoid_gate
    grad_gate_up = jnp.concatenate([grad_gate, grad_upward], axis=1).astype(jnp.bfloat16)
    grad_in = matmul_tn(mix_in, grad_gate_up)
    grad_mix, gain_second = norm_backward(
        residual, second_scale, section_gains[1], matmul_nt(grad_gate_up, w_in)
    )
    grad_residual = grad_mix + cot_row.astype(jnp.float32)
    grad_branch = grad_residual.astype(jnp.bfloat16)
    grad_context = matmul_nt(grad_branch, weights[3]).astype(jnp.bfloat16)
    grad_query, grad_key, grad_value = attend_backward(
        queries, key_rows, value_rows, causal_mask, log_total, grad_context
    )
    weight_grads = (
        matmul_tn(normed_in, grad_query),
        matmul_tn(normed_in, grad_key),
        matmul_tn(normed_in, grad_value),
        matmul_tn(context, grad_branch),
    )
    grad_normed = (
        matmul_nt(grad_query, weights[0])
        + matmul_nt(grad_key, weights[1])
        + matmul_nt(grad_value, weights[2])
    )
    grad_carried, gain_first = norm_backward(
        carried_wide, first_scale, section_gains[0], grad_normed
    )
    outgoing = (grad_residual + grad_carried).astype(jnp.bfloat16)
    return (outgoing, weight_grads, jnp.stack([gain_first, gain_second]), grad_in, grad_down)


def shards(
    byte_states,
    patch_lengths,
    patch_docs,
    attn_qkv,
    attn_out,
    norm_gains,
    ffn_in,
    ffn_down,
    cotangent,
):
    is_first = lax.axis_index("section") == 0
    qkv_whole, out_whole = (
        lax.all_gather(attn_qkv, "dp", axis=2, tiled=True),
        lax.all_gather(attn_out, "dp", axis=1, tiled=True),
    )
    weights = (qkv_whole[0, 0], qkv_whole[0, 1], qkv_whole[0, 2], out_whole[0])
    section_gains = norm_gains[0]
    w_in, w_down = (
        lax.all_gather(ffn_in, ("section", "dp"), axis=0, tiled=True),
        lax.all_gather(ffn_down, ("section", "dp"), axis=0, tiled=True),
    )
    tables = [
        row_tables(patch_lengths[row_index], patch_docs[row_index]) for row_index in range(MICRO)
    ]
    blank_send = jnp.zeros((PATCHES, D), jnp.bfloat16)
    blank_keep = jnp.zeros((PATCHES, D), jnp.float32)
    blank_bytes = jnp.zeros((ROW_BYTES, D), jnp.bfloat16)
    arrived = blank_send
    pooled_rows = [blank_keep] * MICRO
    inputs_rows = [blank_send] * MICRO
    latent_rows = [blank_send] * MICRO
    for moment in range(MICRO + 1):
        early_row = min(moment, MICRO - 1)
        late_row = max(moment - 1, 0)

        def resting():
            return (blank_send, blank_keep)

        def run_first():
            pooled = pool_bytes(
                byte_states[early_row], tables[early_row][1], patch_lengths[early_row]
            )
            pieces = first_inner(
                byte_states[early_row], pooled, tables[early_row][2], weights, section_gains
            )
            output = pooled + matmul(pieces[8], weights[3])
            return (output.astype(jnp.bfloat16), pooled)

        def run_second():
            pieces = second_inner(arrived, tables[late_row][3], weights, section_gains, w_in)
            output = pieces[8] + matmul(pieces[13], w_down)
            return (output.astype(jnp.bfloat16), blank_keep)

        branch = jnp.where(is_first, 1 if moment < MICRO else 0, 2 if moment >= 1 else 0)
        outgoing, retained = lax.switch(branch, [resting, run_first, run_second])
        if moment < MICRO:
            pooled_rows[moment] = retained
        if moment >= 1:
            inputs_rows[moment - 1] = arrived
            latent_rows[moment - 1] = outgoing
        if moment < MICRO:
            arrived = jax.tree.map(
                lambda part, own: part.astype(own.dtype),
                passed_along(for_sending(outgoing), "section", 1),
                outgoing,
            )
    square_zero = jnp.zeros((D, D), jnp.float32)
    totals = (
        square_zero,
        square_zero,
        square_zero,
        square_zero,
        jnp.zeros((2, D), jnp.float32),
        jnp.zeros((D, 2 * FF), jnp.float32),
        jnp.zeros((FF, D), jnp.float32),
    )
    incoming = blank_send
    byte_rows = [blank_bytes] * MICRO
    for moment in range(MICRO + 1):
        second_row = max(MICRO - 1 - moment, 0)
        first_row = min(MICRO - moment, MICRO - 1)

        def resting_back(totals_in):
            return (blank_send, blank_bytes, totals_in)

        def first_back(totals_in):
            grad_bytes, weight_grads, gain_grads = first_backward(
                byte_states[first_row],
                pooled_rows[first_row],
                patch_lengths[first_row],
                tables[first_row],
                weights,
                section_gains,
                incoming,
            )
            additions = weight_grads + (gain_grads,)
            updated = tuple((left + right for left, right in zip(totals_in[:5], additions)))
            return (blank_send, grad_bytes, updated + (totals_in[5], totals_in[6]))

        def second_back(totals_in):
            outgoing, weight_grads, gain_grads, grad_in, grad_down = second_backward(
                inputs_rows[second_row],
                tables[second_row][3],
                weights,
                section_gains,
                w_in,
                w_down,
                cotangent[second_row],
            )
            additions = weight_grads + (gain_grads, grad_in, grad_down)
            updated = tuple((left + right for left, right in zip(totals_in, additions)))
            return (outgoing, blank_bytes, updated)

        branch = jnp.where(is_first, 1 if moment >= 1 else 0, 2 if moment < MICRO else 0)
        outgoing, grad_bytes, totals = lax.switch(
            branch, [resting_back, first_back, second_back], totals
        )
        if moment >= 1:
            byte_rows[MICRO - moment] = grad_bytes
        if moment < MICRO:
            incoming = jax.tree.map(
                lambda part, own: part.astype(own.dtype),
                passed_along(for_sending(outgoing), "section", -1),
                outgoing,
            )
    half_width = D // 2
    latents_all = jnp.stack(latent_rows)
    from_second = passed_along(for_sending(latents_all[..., :half_width]), "section", -1)
    latents_out = jnp.where(is_first, from_second, latents_all[..., half_width:])
    grads_all = jnp.stack(byte_rows)
    from_first = passed_along(for_sending(grads_all[..., half_width:]), "section", 1)
    bytes_out = jnp.where(is_first, grads_all[..., :half_width], from_first)
    grad_qkv = jnp.stack(totals[:3])[None]
    layer_qkv, layer_out, layer_gains = (
        lax.psum_scatter(
            grad_qkv.astype(jnp.bfloat16), "dp", scatter_dimension=2, tiled=True
        ).astype(jnp.float32),
        lax.psum_scatter(
            totals[3][None].astype(jnp.bfloat16), "dp", scatter_dimension=1, tiled=True
        ).astype(jnp.float32),
        lax.psum_scatter(
            totals[4][None].astype(jnp.bfloat16), "dp", scatter_dimension=2, tiled=True
        ).astype(jnp.float32),
    )
    ffn_gin, ffn_gdown = (
        lax.psum_scatter(
            totals[5].astype(jnp.bfloat16), ("section", "dp"), scatter_dimension=0, tiled=True
        ).astype(jnp.float32),
        lax.psum_scatter(
            totals[6].astype(jnp.bfloat16), ("section", "dp"), scatter_dimension=0, tiled=True
        ).astype(jnp.float32),
    )
    summed = (
        lax.psum(layer_qkv.astype(jnp.bfloat16), "group").astype(jnp.float32),
        lax.psum(layer_out.astype(jnp.bfloat16), "group").astype(jnp.float32),
        lax.psum(layer_gains.astype(jnp.bfloat16), "group").astype(jnp.float32),
        lax.psum(ffn_gin.astype(jnp.bfloat16), "group").astype(jnp.float32),
        lax.psum(ffn_gdown.astype(jnp.bfloat16), "group").astype(jnp.float32),
    )
    return (latents_out, bytes_out, summed[0], summed[1], summed[2], summed[3], summed[4])


def solution(mesh):
    in_specs = (
        P(("group", "dp"), None, None),
        P(("group", "dp"), None),
        P(("group", "dp"), None),
        P("section", None, "dp", None),
        P("section", "dp", None),
        P("section", None, None),
        P(("section", "dp"), None),
        P(("section", "dp"), None),
        P(("group", "dp"), None, None),
    )
    out_specs = (
        P(("group", "dp"), None, "section"),
        P(("group", "dp"), None, "section"),
        P("section", None, "dp", None),
        P("section", "dp", None),
        P("section", None, "dp"),
        P(("section", "dp"), None),
        P(("section", "dp"), None),
    )
    return jax.shard_map(shards, mesh=mesh, in_specs=in_specs, out_specs=out_specs, check_vma=False)
```

profile of v0, /device:TPU:0, one launch (start us, length us, event | category | flops | bytes accessed | tf_op | source)
XLA Modules:
  0.0 2127.8 jit_solution(12916275030923701979)
XLA Ops:
  15.4 112.2 %all-gather.5.cloned.1.call-done = bf16[1,3,1024,1024]{3,2,1,0:T(8,128)(2,1)} async-done(((bf16[1,3,256,1024]{3,2,1,0:T(8,128)(2,1)}), bf16[1,3,1024,1024]{3,2,1,0:T(8,128)(2,1)}) %all-gather.5.cloned.1.call-update) | async-done | bytes 6291472 | tf_op jit(solution)/shard_map/all_gather | solution.py:317
  133.3 40.1 %all-gather.7.cloned.1.call-done = bf16[1,1024,1024]{2,1,0:T(8,128)(2,1)} async-done(((bf16[1,256,1024]{2,1,0:T(8,128)(2,1)}), bf16[1,1024,1024]{2,1,0:T(8,128)(2,1)}) %all-gather.7.cloned.1.call-update) | async-done | bytes 2097168 | tf_op jit(solution)/shard_map/all_gather | solution.py:318
  173.4 93.5 %all-gather.11.cloned.1.call-done = bf16[2816,1024]{1,0:T(8,128)(2,1)} async-done(((bf16[352,1024]{1,0:T(8,128)(2,1)}), bf16[2816,1024]{1,0:T(8,128)(2,1)}) %all-gather.11.cloned.1.call-update) | async-done | bytes 5767184 | tf_op jit(solution)/shard_map/all_gather | solution.py:324
  266.9 163.8 %all-gather.9.cloned.1.call-done = bf16[1024,5632]{1,0:T(8,128)(2,1)} async-done(((bf16[128,5632]{1,0:T(8,128)(2,1)}), bf16[1024,5632]{1,0:T(8,128)(2,1)}) %all-gather.9.cloned.1.call-update) | async-done | bytes 11534352 | tf_op jit(solution)/shard_map/all_gather | solution.py:323
  430.7 58.6 %conditional.10 = (bf16[256,1024]{1,0:T(8,128)(2,1)S(1)}, f32[256,1024]{1,0:T(8,128)}) conditional(s32[]{:T(128)} %clamp.7, () %tuple.272, (bf16[4,1024,1024]{2,1,0:T(8,128)(2,1)}, bf16[256,1024]{1,0:T(8,128)(2,1)S(1)}, s32[4,256]{1,0:T(4,128)S(1)}, f32[2,1024]{1,0:T(2,128)S(1)}, bf16[1024,1024]{1,0:T(8,128)(2,1)S(1)}, ...), branch_computations={%region_8.9_spmd, %region_9.16_spmd, %region_16.22_spmd} | conditional | flops 6686707712 | bytes 76979440 | solution.py:359
  452.2 25.6 %while.330 = (s32[]{:T(128)}, bf16[4,256,4,64]{1,3,2,0:T(8,128)(2,1)}, bf16[4,1024,4,64]{1,3,2,0:T(8,128)(2,1)}, pred[256,1024]{1,0:T(8,128)(4,1)S(1)}, bf16[4,2...) while((s32[]{:T(128)}, bf16[4,256,4,64]{1,3,2,0:T(8,128)(2,1)}, ...), condition=%wide.region_15.15_spmd, body=%wide.region_12.14_spmd.sunk | while | flops 276890624 | bytes 18360404 | solution.py:90
  492.9 9.9 collective-permute-done
  503.6 62.4 %conditional.11 = (bf16[256,1024]{1,0:T(8,128)(2,1)}, f32[256,1024]{1,0:T(8,128)}, bf16[1,256,1024]{2,1,0:T(8,128)(2,1)S(1)}) conditional(s32[]{:T(128)} %clamp.6, () %tuple.270, (bf16[4,1024,1024]{2,1,0:T(8,128)(2,1)}, bf16[256,1024]{1,0:T(8,128)(2,1)}, s32[4,256]{1,0:T(4,128)S(1)}, f32[2,1024]{1,0:T(2,128)S(1)}, ...), branch_computations={%region_22.23_spmd, %region_23.30_spmd, %region_30.37_spmd} | conditional | flops 6691162112 | bytes 89052440 | solution.py:359
  523.1 29.7 %while.332 = (s32[]{:T(128)}, bf16[4,256,4,64]{1,3,2,0:T(8,128)(2,1)}, bf16[4,1024,4,64]{1,3,2,0:T(8,128)(2,1)}, pred[256,1024]{1,0:T(8,128)(4,1)}, bf16[4,256,4...) while((s32[]{:T(128)}, bf16[4,256,4,64]{1,3,2,0:T(8,128)(2,1)}, ...), condition=%wide.region_29.29_spmd, body=%wide.region_26.28_spmd.sunk | while | flops 276890624 | bytes 18360404 | solution.py:90
  569.0 9.0 collective-permute-done.1
  578.8 62.6 %conditional.12 = (bf16[256,1024]{1,0:T(8,128)(2,1)}, f32[256,1024]{1,0:T(8,128)}, bf16[1,256,1024]{2,1,0:T(8,128)(2,1)S(1)}) conditional(s32[]{:T(128)} %clamp.6, () %tuple.276, (bf16[4,1024,1024]{2,1,0:T(8,128)(2,1)}, bf16[256,1024]{1,0:T(8,128)(2,1)}, s32[4,256]{1,0:T(4,128)S(1)}, f32[2,1024]{1,0:T(2,128)S(1)}, ...), branch_computations={%region_41.42_spmd, %region_42.49_spmd, %region_49.56_spmd} | conditional | flops 6691162112 | bytes 89052440 | solution.py:359
  598.4 29.7 %while.334 = (s32[]{:T(128)}, bf16[4,256,4,64]{1,3,2,0:T(8,128)(2,1)}, bf16[4,1024,4,64]{1,3,2,0:T(8,128)(2,1)}, pred[256,1024]{1,0:T(8,128)(4,1)}, bf16[4,256,4...) while((s32[]{:T(128)}, bf16[4,256,4,64]{1,3,2,0:T(8,128)(2,1)}, ...), condition=%wide.region_48.48_spmd, body=%wide.region_45.47_spmd.sunk | while | flops 276890624 | bytes 18360404 | solution.py:90
  644.4 8.4 collective-permute-done.2
  653.6 58.2 %conditional.13 = (bf16[256,1024]{1,0:T(8,128)(2,1)}, f32[256,1024]{1,0:T(8,128)}, bf16[1,256,1024]{2,1,0:T(8,128)(2,1)S(1)}) conditional(s32[]{:T(128)} %clamp.6, () %tuple.279, (bf16[4,1024,1024]{2,1,0:T(8,128)(2,1)}, bf16[256,1024]{1,0:T(8,128)(2,1)}, s32[4,256]{1,0:T(4,128)S(1)}, f32[2,1024]{1,0:T(2,128)S(1)}, ...), branch_computations={%region_60.61_spmd, %region_61.68_spmd, %region_68.75_spmd} | conditional | flops 6691162112 | bytes 89052440 | solution.py:359
  673.2 25.6 %while.336 = (s32[]{:T(128)}, bf16[4,256,4,64]{1,3,2,0:T(8,128)(2,1)}, bf16[4,1024,4,64]{1,3,2,0:T(8,128)(2,1)}, pred[256,1024]{1,0:T(8,128)(4,1)S(1)}, bf16[4,2...) while((s32[]{:T(128)}, bf16[4,256,4,64]{1,3,2,0:T(8,128)(2,1)}, ...), condition=%wide.region_67.67_spmd, body=%wide.region_64.66_spmd.sunk | while | flops 276890624 | bytes 18360404 | solution.py:90
  714.1 9.3 collective-permute-done.3
  724.2 33.2 %conditional.15 = (bf16[256,1024]{1,0:T(8,128)(2,1)}, f32[1024,1024]{1,0:T(8,128)}, f32[1024,1024]{1,0:T(8,128)}, f32[1024,1024]{1,0:T(8,128)}, f32[1024,1024]{1...) conditional(s32[]{:T(128)} %clamp.8, () %tuple.284, ...), branch_computations={%region_90.91_spmd, %region_91.103_spmd, %region_103.117_spmd} | conditional | flops 18537709568 | bytes 351062240 | solution.py:419
  740.8 10.6 broadcast_in_dim.638
  758.7 98.9 %collective-permute-done.5 = bf16[256,1024]{1,0:T(8,128)(2,1)S(1)} collective-permute-done((bf16[256,1024]{1,0:T(8,128)(2,1)}, bf16[256,1024]{1,0:T(8,128)(2,1)S(1)}, u32[]{:S(2)}, u32[]{:S(2)}) %collective-permute-start.5) | collective-permute-done | bytes 524320 | tf_op jit(solution)/shard_map/ppermute | solution.py:27
  857.6 148.6 %conditional.16 = (bf16[256,1024]{1,0:T(8,128)(2,1)S(1)}, f32[1024,1024]{1,0:T(8,128)}, f32[1024,1024]{1,0:T(8,128)}, f32[1024,1024]{1,0:T(8,128)}, f32[1024,102...) conditional(s32[]{:T(128)} %clamp.6, (f32[1024,1024]{1,0:T(8,128)}, ...), branch_computations={%region_117.118_spmd, %region_118.133_spmd, %region_132.0_spmd} | conditional | flops 18550554624 | bytes 360769760 | solution.py:419
  884.3 22.3 %while.344 = (s32[]{:T(128)}, bf16[4,256,4,64]{1,3,2,0:T(8,128)(2,1)}, f32[4,4,256]{2,1,0:T(4,128)S(1)}, bf16[4,1024,4,64]{1,3,2,0:T(8,128)(2,1)}, pred[256,1024...) while((s32[]{:T(128)}, ...), condition=%wide.region_124.124_spmd, body=%wide.region_121.123_spmd.sunk | while | flops 281082880 | bytes 14714977 | solution.py:90
  911.9 37.1 %while.345 = (s32[]{:T(128)}, bf16[4,256,4,64]{1,3,2,0:T(8,128)(2,1)S(1)}, bf16[4,1024,4,64]{1,3,2,0:T(8,128)(2,1)}, bf16[4,1024,4,64]{1,3,2,0:T(8,128)(2,1)}, b...) while((s32[]{:T(128)}, ...), condition=%wide.region_127.127_spmd, body=%wide.region_125.126_spmd.sunk | while | flops 687733760 | bytes 37651604 | solution.py:125
  949.8 8.2 convolution_add_fusion.43
  1007.5 10.7 collective-permute-done.6
  1018.2 163.5 %conditional.17 = (bf16[256,1024]{1,0:T(8,128)(2,1)S(1)}, f32[1024,1024]{1,0:T(8,128)}, f32[1024,1024]{1,0:T(8,128)}, f32[1024,1024]{1,0:T(8,128)}, f32[1024,102...) conditional(s32[]{:T(128)} %clamp.6, (f32[1024,1024]{1,0:T(8,128)}, ...), branch_computations={%region_146.148_spmd, %region_147.162_spmd, %region_161.0_spmd} | conditional | flops 18550554624 | bytes 360507584 | solution.py:419
  1044.9 29.7 %while.348 = (s32[]{:T(128)}, bf16[4,256,4,64]{1,3,2,0:T(8,128)(2,1)}, f32[4,4,256]{2,1,0:T(4,128)S(1)}, bf16[4,1024,4,64]{1,3,2,0:T(8,128)(2,1)}, pred[256,1024...) while((s32[]{:T(128)}, ...), condition=%wide.region_153.154_spmd, body=%wide.region_150.153_spmd.sunk | while | flops 281082880 | bytes 14714977 | solution.py:90
  1079.8 45.0 %while.349 = (s32[]{:T(128)}, bf16[4,256,4,64]{1,3,2,0:T(8,128)(2,1)S(1)}, bf16[4,1024,4,64]{1,3,2,0:T(8,128)(2,1)}, bf16[4,1024,4,64]{1,3,2,0:T(8,128)(2,1)}, b...) while((s32[]{:T(128)}, ...), condition=%wide.region_156.157_spmd, body=%wide.region_154.156_spmd.sunk | while | flops 687733760 | bytes 37651604 | solution.py:125
  1125.6 8.2 convolution_add_fusion.48
  1143.3 7.0 convolution_add_fusion.47
  1183.0 9.8 collective-permute-done.7
  1192.8 163.8 %conditional.18 = (bf16[256,1024]{1,0:T(8,128)(2,1)S(1)}, f32[1024,1024]{1,0:T(8,128)}, f32[1024,1024]{1,0:T(8,128)}, f32[1024,1024]{1,0:T(8,128)}, f32[1024,102...) conditional(s32[]{:T(128)} %clamp.6, (f32[1024,1024]{1,0:T(8,128)}, ...), branch_computations={%region_175.177_spmd, %region_176.191_spmd, %region_190.0_spmd} | conditional | flops 18550554624 | bytes 350021728 | solution.py:419
  1219.5 29.9 %while.352 = (s32[]{:T(128)}, bf16[4,256,4,64]{1,3,2,0:T(8,128)(2,1)}, f32[4,4,256]{2,1,0:T(4,128)S(1)}, bf16[4,1024,4,64]{1,3,2,0:T(8,128)(2,1)}, pred[256,1024...) while((s32[]{:T(128)}, ...), condition=%wide.region_182.183_spmd, body=%wide.region_179.182_spmd.sunk | while | flops 281082880 | bytes 14714977 | solution.py:90
  1254.7 44.8 %while.353 = (s32[]{:T(128)}, bf16[4,256,4,64]{1,3,2,0:T(8,128)(2,1)S(1)}, bf16[4,1024,4,64]{1,3,2,0:T(8,128)(2,1)}, bf16[4,1024,4,64]{1,3,2,0:T(8,128)(2,1)}, b...) while((s32[]{:T(128)}, ...), condition=%wide.region_185.186_spmd, body=%wide.region_183.185_spmd.sunk | while | flops 687733760 | bytes 37651604 | solution.py:125
  1300.3 8.2 convolution_add_fusion.53
  1318.1 7.0 convolution_add_fusion.52
  1357.9 9.8 collective-permute-done.8
  1367.7 144.4 %conditional.19 = (f32[1024,1024]{1,0:T(8,128)}, f32[1024,1024]{1,0:T(8,128)}, f32[1024,1024]{1,0:T(8,128)}, f32[1024,1024]{1,0:T(8,128)}, f32[2,1024]{1,0:T(2,1...) conditional(s32[]{:T(128)} %clamp.7, (f32[1024,1024]{1,0:T(8,128)}, ...), branch_computations={%region_204.206_spmd, %region_205.220_spmd, %region_219.233_spmd} | conditional | flops 18547408896 | bytes 342142048 | solution.py:419
  1392.9 22.1 %while.356 = (s32[]{:T(128)}, bf16[4,256,4,64]{1,3,2,0:T(8,128)(2,1)}, f32[4,4,256]{2,1,0:T(4,128)S(1)}, bf16[4,1024,4,64]{1,3,2,0:T(8,128)(2,1)}, pred[256,1024...) while((s32[]{:T(128)}, ...), condition=%wide.region_211.212_spmd, body=%wide.region_208.211_spmd.sunk | while | flops 281082880 | bytes 14714977 | solution.py:90
  1420.2 37.3 %while.357 = (s32[]{:T(128)}, bf16[4,256,4,64]{1,3,2,0:T(8,128)(2,1)S(1)}, bf16[4,1024,4,64]{1,3,2,0:T(8,128)(2,1)}, bf16[4,1024,4,64]{1,3,2,0:T(8,128)(2,1)}, b...) while((s32[]{:T(128)}, ...), condition=%wide.region_214.215_spmd, body=%wide.region_212.214_spmd.sunk | while | flops 687733760 | bytes 37651604 | solution.py:125
  1458.3 8.2 convolution_add_fusion.58
  1476.1 7.0 convolution_add_fusion.57
  1516.1 7.7 convert_element_type.1192
  1535.0 12.3 convert_element_type.1190
  1567.8 120.7 %reduce-scatter.14.cloned.1.call-done = bf16[352,1024]{1,0:T(8,128)(2,1)} async-done(((bf16[2816,1024]{1,0:T(8,128)(2,1)}), bf16[352,1024]{1,0:T(8,128)(2,1)}) %reduce-scatter.14.cloned.1.call-update) | async-done | bytes 720912 | tf_op jit(solution)/shard_map/reduce_scatter | solution.py:453
  1688.5 117.0 %reduce-scatter.8.cloned.1.call-done = bf16[1,3,256,1024]{3,2,1,0:T(8,128)(2,1)} async-done(((bf16[1,3,1024,1024]{3,2,1,0:T(8,128)(2,1)}), bf16[1,3,256,1024]{3,2,1,0:T(8,128)(2,1)}) %reduce-scatter.8.cloned.1.call-update) | async-done | bytes 1572880 | tf_op jit(solution)/shard_map/reduce_scatter | solution.py:439
  1805.5 197.2 %reduce-scatter.12.cloned.1.call-done = bf16[128,5632]{1,0:T(8,128)(2,1)} async-done(((bf16[1024,5632]{1,0:T(8,128)(2,1)}), bf16[128,5632]{1,0:T(8,128)(2,1)}) %reduce-scatter.12.cloned.1.call-update) | async-done | bytes 1441808 | tf_op jit(solution)/shard_map/reduce_scatter | solution.py:450
  2005.4 25.6 %collective-permute-done.4 = bf16[4,256,512]{2,1,0:T(8,128)(2,1)S(1)} collective-permute-done((bf16[4,256,512]{2,1,0:T(8,128)(2,1)S(1)}, bf16[4,256,512]{2,1,0:T(8,128)(2,1)S(1)}, u32[]{:S(2)}, u32[]{:S(2)}) %collective-permute-start.4) | collective-permute-done | bytes 1048608 | tf_op jit(solution)/shard_map/ppermute | solution.py:27
  2044.6 67.3 %all-reduce.3.cloned.1.call-done = (bf16[1,3,256,1024]{3,2,1,0:T(8,128)(2,1)}, bf16[1,256,1024]{2,1,0:T(8,128)(2,1)}, bf16[128,5632]{1,0:T(8,128)(2,1)}, bf16[352,1024]{1,0:T(8,128)(2,1)}) async-done(((bf16[1,3,256,1024]{3,2,1,0:T(8,128)(2,1)}, bf16[1,256,1024]{2,1,0:T(8,128)(2,1)}, bf16[128,5632]{1,0:T(8,128)(2,1)}, bf16[352,1024]{1,0:T(8,128)(2,1)}), (bf16[1,3,256,1024]{3,2,1,0:T(8,128)(2,1)}, ...) | async-done | bytes 4259856 | tf_op jit(solution)/shard_map/psum | solution.py:458
  (759 shorter events, 833.8 us)
Async XLA Ops:
  7.2 120.5 %all-gather.5.cloned.1.call-start = ((), (), s32[]{:S(2)}) async-start(), calls=%async_computation.5 | async-start | bytes 7864320 | tf_op jit(solution)/shard_map/all_gather | solution.py:317
  7.9 165.5 %all-gather.7.cloned.1.call-start = ((), (), s32[]{:S(2)}) async-start(), calls=%async_computation.6 | async-start | bytes 2621440 | tf_op jit(solution)/shard_map/all_gather | solution.py:318
  8.7 258.2 %all-gather.11.cloned.1.call-start = ((), (), s32[]{:S(2)}) async-start(), calls=%async_computation.8 | async-start | bytes 6488064 | tf_op jit(solution)/shard_map/all_gather | solution.py:324
  9.4 421.3 %all-gather.9.cloned.1.call-start = ((), (), s32[]{:S(2)}) async-start(), calls=%async_computation.7 | async-start | bytes 12976128 | tf_op jit(solution)/shard_map/all_gather | solution.py:323
  10.0 1557.8 %reduce-scatter.10.cloned.1.call-start = ((), (), s32[]{:S(2)}) async-start(), calls=%async_computation.10 | async-start | bytes 2621440 | tf_op jit(solution)/shard_map/reduce_scatter | solution.py:442
  12.4 120.9 %copy-start.196 = (s32[1024]{0:T(1024)}, s32[1024]{0:T(1024)S(1)}, u32[]{:S(2)}) copy-start(s32[1024]{0:T(1024)S(1)} %convert_reduce_fusion.3) | copy-start | bytes 12292
  12.5 120.8 %copy-start.211 = (s32[256]{0:T(256)}, s32[256]{0:T(256)S(1)}, u32[]{:S(2)}) copy-start(s32[256]{0:T(256)S(1)} %add_bitcast_fusion.1) | copy-start | bytes 3076
  12.7 120.6 %copy-start.199 = (s32[1024]{0:T(1024)}, s32[1024]{0:T(1024)S(1)}, u32[]{:S(2)}) copy-start(s32[1024]{0:T(1024)S(1)} %convert_reduce_fusion.2) | copy-start | bytes 12292
  13.0 478.7 %copy-start.198 = (s32[1024]{0:T(1024)}, s32[1024]{0:T(1024)S(1)}, u32[]{:S(2)}) copy-start(s32[1024]{0:T(1024)S(1)} %convert_reduce_fusion.4) | copy-start | bytes 12292
  13.6 119.7 %copy-start.204 = (s32[1,256]{1,0:T(1,128)}, s32[1,256]{1,0:T(1,128)S(1)}, u32[]{:S(2)}) copy-start(s32[1,256]{1,0:T(1,128)S(1)} %get-tuple-element.2876) | copy-start | bytes 3076
  14.9 487.9 %copy-start.87 = (pred[256,256]{0,1:T(8,128)(4,1)}, pred[256,256]{0,1:T(8,128)(4,1)S(1)}, u32[]{:S(2)}) copy-start(pred[256,256]{0,1:T(8,128)(4,1)S(1)} %fusion.1167) | copy-start | bytes 196612
  15.4 415.3 %copy-start.29 = (pred[256,1024]{1,0:T(8,128)(4,1)}, pred[256,1024]{1,0:T(8,128)(4,1)S(1)}, u32[]{:S(2)}) copy-start(pred[256,1024]{1,0:T(8,128)(4,1)S(1)} %get-tuple-element.2888) | copy-start | bytes 786436
  15.4 415.3 %copy-start.163 = (f32[1,2,1024]{2,1,0:T(2,128)S(1)}, f32[1,2,1024]{2,1,0:T(2,128)}, u32[]{:S(2)}) copy-start(f32[1,2,1024]{2,1,0:T(2,128)} %param.106) | copy-start | bytes 24580
  133.3 590.1 %copy-start = (bf16[1024,1024]{1,0:T(8,128)(2,1)}, bf16[1024,1024]{1,0:T(8,128)(2,1)S(1)}, u32[]{:S(2)}) copy-start(bf16[1024,1024]{1,0:T(8,128)(2,1)S(1)} %get-tuple-element.2872) | copy-start | bytes 6291460
  490.1 12.6 collective-permute-start
  502.8 64.9 %copy-start.200 = (s32[1024]{0:T(1024)S(1)}, s32[1024]{0:T(1024)}, u32[]{:S(2)}) copy-start(s32[1024]{0:T(1024)} %copy-done.199) | copy-start | bytes 12292
  502.8 64.9 %copy-start.205 = (s32[1,256]{1,0:T(1,128)S(1)}, s32[1,256]{1,0:T(1,128)}, u32[]{:S(2)}) copy-start(s32[1,256]{1,0:T(1,128)} %copy-done.204) | copy-start | bytes 3076
  502.8 64.9 %copy-start.210 = (s32[1024]{0:T(1024)S(1)}, s32[1024]{0:T(1024)}, u32[]{:S(2)}) copy-start(s32[1024]{0:T(1024)} %select_reduce_fusion.1) | copy-start | bytes 12292
  502.8 64.9 %copy-start.212 = (s32[256]{0:T(256)S(1)}, s32[256]{0:T(256)}, u32[]{:S(2)}) copy-start(s32[256]{0:T(256)} %copy-done.211) | copy-start | bytes 3076
  566.0 12.0 collective-permute-start.1
  567.5 75.6 %copy-start.201 = (s32[1024]{0:T(1024)}, s32[1024]{0:T(1024)S(1)}, u32[]{:S(2)}) copy-start(s32[1024]{0:T(1024)S(1)} %convert_reduce_fusion.1) | copy-start | bytes 12292
  578.0 64.7 %copy-start.203 = (s32[1,256]{1,0:T(1,128)S(1)}, s32[1,256]{1,0:T(1,128)}, u32[]{:S(2)}) copy-start(s32[1,256]{1,0:T(1,128)} %get-tuple-element.2875) | copy-start | bytes 3076
  641.4 11.4 collective-permute-start.2
  644.4 213.2 %copy-start.27 = (pred[256,1024]{1,0:T(8,128)(4,1)}, pred[256,1024]{1,0:T(8,128)(4,1)S(1)}, u32[]{:S(2)}) copy-start(pred[256,1024]{1,0:T(8,128)(4,1)S(1)} %get-tuple-element.2882) | copy-start | bytes 786436
  712.6 10.8 collective-permute-start.3
  757.4 100.2 %collective-permute-start.5 = (bf16[256,1024]{1,0:T(8,128)(2,1)}, bf16[256,1024]{1,0:T(8,128)(2,1)S(1)}, u32[]{:S(2)}, u32[]{:S(2)}) collective-permute-start(bf16[256,1024]{1,0:T(8,128)(2,1)} %get-tuple-element.2154), channel_id=1, source_target_pairs={{16,0},{17,1},{18,2},{19,3},{20,4},{21,5},{22,6},{23,7},{24,8},{25... | collective-permute-start | bytes 1572872 | tf_op jit(solution)/shard_map/ppermute | solution.py:27
  857.6 160.6 %copy-start.112 = (pred[256,256]{0,1:T(8,128)(4,1)S(1)}, pred[256,256]{0,1:T(8,128)(4,1)}, u32[]{:S(2)}) copy-start(pred[256,256]{0,1:T(8,128)(4,1)} %copy-done.111) | copy-start | bytes 196612
  857.6 49.1 %copy-start.169 = (bf16[256,1024]{1,0:T(8,128)(2,1)}, bf16[256,1024]{1,0:T(8,128)(2,1)S(1)}, u32[]{:S(2)}) copy-start(bf16[256,1024]{1,0:T(8,128)(2,1)S(1)} %get-tuple-element.1753) | copy-start | bytes 1572868 | tf_op jit(solution)/shard_map/cond
  1006.2 12.0 collective-permute-start.6
  1018.2 174.6 %copy-start.88 = (pred[256,256]{0,1:T(8,128)(4,1)S(1)}, pred[256,256]{0,1:T(8,128)(4,1)}, u32[]{:S(2)}) copy-start(pred[256,256]{0,1:T(8,128)(4,1)} %copy-done.87) | copy-start | bytes 196612
  1018.2 56.4 %copy-start.171 = (bf16[256,1024]{1,0:T(8,128)(2,1)}, bf16[256,1024]{1,0:T(8,128)(2,1)S(1)}, u32[]{:S(2)}) copy-start(bf16[256,1024]{1,0:T(8,128)(2,1)S(1)} %get-tuple-element.1843) | copy-start | bytes 1572868 | tf_op jit(solution)/shard_map/cond
  1181.7 11.1 collective-permute-start.7
  1192.8 174.9 %copy-start.30 = (pred[256,1024]{1,0:T(8,128)(4,1)S(1)}, pred[256,1024]{1,0:T(8,128)(4,1)}, u32[]{:S(2)}) copy-start(pred[256,1024]{1,0:T(8,128)(4,1)} %copy-done.29) | copy-start | bytes 786436
  1192.8 174.9 %copy-start.197 = (s32[1024]{0:T(1024)S(1)}, s32[1024]{0:T(1024)}, u32[]{:S(2)}) copy-start(s32[1024]{0:T(1024)} %copy-done.196) | copy-start | bytes 12292
  1192.8 56.6 %copy-start.173 = (bf16[256,1024]{1,0:T(8,128)(2,1)}, bf16[256,1024]{1,0:T(8,128)(2,1)S(1)}, u32[]{:S(2)}) copy-start(bf16[256,1024]{1,0:T(8,128)(2,1)S(1)} %get-tuple-element.1933) | copy-start | bytes 1572868 | tf_op jit(solution)/shard_map/cond
  1192.8 11.7 copy-start.19
  1356.6 11.1 collective-permute-start.8
  1367.7 47.3 %copy-start.175 = (bf16[256,1024]{1,0:T(8,128)(2,1)}, bf16[256,1024]{1,0:T(8,128)(2,1)S(1)}, u32[]{:S(2)}) copy-start(bf16[256,1024]{1,0:T(8,128)(2,1)S(1)} %get-tuple-element.2023) | copy-start | bytes 1572868 | tf_op jit(solution)/shard_map/cond
  1516.0 172.5 %reduce-scatter.14.cloned.1.call-start = ((), (), s32[]{:S(2)}) async-start(), calls=%async_computation.12 | async-start | bytes 6488064 | tf_op jit(solution)/shard_map/reduce_scatter | solution.py:453
  1523.8 281.6 %reduce-scatter.8.cloned.1.call-start = ((), (), s32[]{:S(2)}) async-start(), calls=%async_computation.9 | async-start | bytes 7864320 | tf_op jit(solution)/shard_map/reduce_scatter | solution.py:439
  1534.9 467.7 %reduce-scatter.12.cloned.1.call-start = ((), (), s32[]{:S(2)}) async-start(), calls=%async_computation.11 | async-start | bytes 12976128 | tf_op jit(solution)/shard_map/reduce_scatter | solution.py:450
  1547.3 484.8 %reduce-scatter.16.cloned.1.call-start = ((), (), s32[]{:S(2)}) async-start(), calls=%async_computation.13 | async-start | bytes 327680
  1559.6 480.3 %collective-permute-start.9 = (bf16[4,1024,512]{2,1,0:T(8,128)(2,1)}, bf16[4,1024,512]{2,1,0:T(8,128)(2,1)}, u32[]{:S(2)}, u32[]{:S(2)}) collective-permute-start(bf16[4,1024,512]{2,1,0:T(8,128)(2,1)} %slice.404), channel_id=1, source_target_pairs={{0,16},{1,17},{2,18},{3,19},{4,20},{5,21},{6,22},{7,23},{8,24},{9,... | collective-permute-start | bytes 12582920 | tf_op jit(solution)/shard_map/ppermute | solution.py:27
  1564.2 547.6 %all-reduce.3.cloned.1.call-start = ((), (), s32[]{:S(2)}) async-start(), calls=%async_computation.14 | async-start | bytes 8519680 | tf_op jit(solution)/shard_map/psum | solution.py:458
  1567.7 435.0 %copy-start.182 = (bf16[1,256,1024]{2,1,0:T(8,128)(2,1)S(1)}, bf16[1,256,1024]{2,1,0:T(8,128)(2,1)}, u32[]{:S(2)}) copy-start(bf16[1,256,1024]{2,1,0:T(8,128)(2,1)} %copy-done.181) | copy-start | bytes 1572868
  1567.7 435.0 %copy-start.184 = (bf16[1,256,1024]{2,1,0:T(8,128)(2,1)S(1)}, bf16[1,256,1024]{2,1,0:T(8,128)(2,1)}, u32[]{:S(2)}) copy-start(bf16[1,256,1024]{2,1,0:T(8,128)(2,1)} %copy-done.183) | copy-start | bytes 1572868
  1567.7 435.0 %copy-start.186 = (bf16[1,256,1024]{2,1,0:T(8,128)(2,1)S(1)}, bf16[1,256,1024]{2,1,0:T(8,128)(2,1)}, u32[]{:S(2)}) copy-start(bf16[1,256,1024]{2,1,0:T(8,128)(2,1)} %copy-done.185) | copy-start | bytes 1572868
  2004.1 26.9 %collective-permute-start.4 = (bf16[4,256,512]{2,1,0:T(8,128)(2,1)S(1)}, bf16[4,256,512]{2,1,0:T(8,128)(2,1)S(1)}, u32[]{:S(2)}, u32[]{:S(2)}) collective-permute-start(bf16[4,256,512]{2,1,0:T(8,128)(2,1)S(1)} %slice.401), channel_id=1, source_target_pairs={{16,0},{17,1},{18,2},{19,3},{20,4},{21,5},{22,6},{23,7},{24,8},{25... | collective-permute-start | bytes 3145736 | tf_op jit(solution)/shard_map/ppermute | solution.py:27
  (97 other events, 509.4 us)
Sparse Core Ops, SparseCore 0:
  9.6 118.0 all-gather.4
  129.2 44.1 all-gather.6
  175.5 91.3 all-gather.10
  268.9 161.8 all-gather.8
  1516.2 46.9 reduce-scatter.9
  1567.1 121.3 reduce-scatter.13
  1690.9 114.5 reduce-scatter.7
  1809.5 193.1 reduce-scatter.11
  2005.0 18.7 reduce-scatter.15
  2026.2 85.5 all-reduce.2
where the time goes:
time: 2140 us; the launch traced here: 2130 us
  waiting for transfers between devices  1110 us (52%)
  matrix products  565 us (26%)
  other arithmetic  220 us (10%)
  local copies, waits for them, and re-layouts  106 us (5%)
  loops' own time  94.3 us (4%)
    reduce_scatter x1, waiting for transfers between devices, shards(): lax.psum_scatter(totals[5].astype(jnp.bfloat16), ('section', 'dp'), scatt...  197 us
    ppermute x10, waiting for transfers between devices, passed_along(): lax.ppermute(value, axis, [(source, source + steps) for source in range(l...  191 us
    all_gather x1, waiting for transfers between devices, shards(): lax.all_gather(ffn_in, ('section', 'dp'), axis=0, tiled=True)  164 us
    dot_general x32, matrix products, matmul(): return jnp.dot(left, right, preferred_element_type=jnp.float32)  139 us
    reduce_scatter x1, waiting for transfers between devices, shards(): lax.psum_scatter(totals[6].astype(jnp.bfloat16), ('section', 'dp'), scatt...  121 us
    reduce_scatter x1, waiting for transfers between devices, shards(): lax.psum_scatter(grad_qkv.astype(jnp.bfloat16), 'dp', scatter_dimension=2...  117 us
    all_gather x1, waiting for transfers between devices, shards(): lax.all_gather(attn_qkv, 'dp', axis=2, tiled=True)  112 us
    dot_general x16, matrix products, matmul_tn(): lax.dot_general(left, right, (((0,), (0,)), ((), ())), preferred_element_...  104 us
  transfers between devices with their start and end apart: 20, of which 17 were waited for; matrix products, arithmetic and copies ran while one was open for 3% of the time, Pallas kernels for 0%

commit v1 on v0

v1 whole, which is shorter than its diff:
```python
import functools

import jax
import jax.numpy as jnp
from jax import lax
from jax.experimental import pallas as pl
from jax.experimental.pallas import tpu as pltpu
from jax.sharding import PartitionSpec as P

D = 1024
HEADS = 16
HEAD_DIM = 64
PAIRS = HEADS // 2
FF = 2816
ROW_BYTES = 1024
PATCHES = 256
QT = 128
TILES = PATCHES // QT

EPS = 1e-05
SCALE = HEAD_DIM ** (-0.5)
EXCLUDED = -1e30

BF = jnp.bfloat16
F32 = jnp.float32


def nn(left, right):
    return jnp.dot(left, right, preferred_element_type=F32)


def tn(left, right):
    return lax.dot_general(left, right, (((0,), (0,)), ((), ())), preferred_element_type=F32)


def nt(left, right):
    return lax.dot_general(left, right, (((1,), (1,)), ((), ())), preferred_element_type=F32)


def two_heads(block):
    lane = lax.broadcasted_iota(jnp.int32, block.shape, 1)
    zero = jnp.zeros_like(block)
    first = lane < HEAD_DIM
    return jnp.concatenate([jnp.where(first, block, zero), jnp.where(first, zero, block)], axis=0)


def own_lanes(both):
    picked = jnp.concatenate([both[:HEAD_DIM, :QT], both[HEAD_DIM:, QT:]], axis=0)
    return picked.T


def twice(row):
    return jnp.concatenate([row, row], axis=1)


def attend_kernel(chunk, first_ref, stop_ref, lo_ref, hi_ref, q_ref, k_ref, v_ref, c_ref, l_ref, s_ref):
    row = pl.program_id(0)
    for tile in range(TILES):
        own = pl.ds(tile * QT, QT)
        queries = two_heads(q_ref[own, :].astype(F32) * SCALE).astype(BF)
        lo = twice(lo_ref[0, :, own])
        hi = twice(hi_ref[0, :, own])
        first = first_ref[row, tile]
        stop = stop_ref[row, tile]

        def scores(j, top):
            start = pl.multiple_of(j * chunk, chunk)
            part = nt(k_ref[pl.ds(start, chunk), :], queries)
            at = lax.broadcasted_iota(jnp.int32, part.shape, 0) + start
            part = jnp.where((at >= lo) & (at < hi), part, EXCLUDED)
            s_ref[pl.ds(start, chunk), :] = part
            return jnp.maximum(top, jnp.max(part, axis=0, keepdims=True))

        top = lax.fori_loop(first, stop, scores, jnp.full((1, 2 * QT), EXCLUDED, F32))

        def context(j, carry):
            total, acc = carry
            start = pl.multiple_of(j * chunk, chunk)
            weight = jnp.exp(s_ref[pl.ds(start, chunk), :] - top)
            total = total + jnp.sum(weight, axis=0, keepdims=True)
            acc = acc + tn(v_ref[pl.ds(start, chunk), :], weight.astype(BF))
            return (total, acc)

        total, acc = lax.fori_loop(
            first, stop, context, (jnp.zeros((1, 2 * QT), F32), jnp.zeros((2 * HEAD_DIM, 2 * QT), F32))
        )
        c_ref[own, :] = own_lanes(acc / total).astype(BF)
        l_ref[0, 0, tile : tile + 1, :] = top + jnp.log(total)


def attend_back_kernel(
    chunk, first_ref, stop_ref, lo_ref, hi_ref, q_ref, k_ref, v_ref, l_ref, c_ref, dc_ref,
    dq_ref, dk_ref, dv_ref, dk_acc, dv_acc,
):
    row = pl.program_id(0)
    dk_acc[...] = jnp.zeros_like(dk_acc)
    dv_acc[...] = jnp.zeros_like(dv_acc)
    for tile in range(TILES):
        own = pl.ds(tile * QT, QT)
        queries = two_heads(q_ref[own, :].astype(F32) * SCALE).astype(BF)
        grads = dc_ref[own, :].astype(F32)
        inner = (grads * c_ref[own, :].astype(F32)).T
        delta = jnp.concatenate(
            [
                jnp.sum(inner[:HEAD_DIM], axis=0, keepdims=True),
                jnp.sum(inner[HEAD_DIM:], axis=0, keepdims=True),
            ],
            axis=1,
        )
        grads = two_heads(grads).astype(BF)
        lo = twice(lo_ref[0, :, own])
        hi = twice(hi_ref[0, :, own])
        logsum = l_ref[0, 0, tile : tile + 1, :]

        def step(j, acc):
            start = pl.multiple_of(j * chunk, chunk)
            here = pl.ds(start, chunk)
            keys = k_ref[here, :]
            part = nt(keys, queries)
            at = lax.broadcasted_iota(jnp.int32, part.shape, 0) + start
            part = jnp.where((at >= lo) & (at < hi), part, EXCLUDED)
            prob = jnp.exp(part - logsum)
            slope = prob * (nt(v_ref[here, :], grads) - delta)
            slope = slope.astype(BF)
            dv_acc[here, :] += nn(prob.astype(BF), grads)
            dk_acc[here, :] += nn(slope, queries)
            return acc + tn(keys, slope)

        acc = lax.fori_loop(
            first_ref[row, tile], stop_ref[row, tile], step, jnp.zeros((2 * HEAD_DIM, 2 * QT), F32)
        )
        dq_ref[own, :] = (own_lanes(acc) * SCALE).astype(BF)
    dk_ref[...] = dk_acc[...].astype(BF)
    dv_ref[...] = dv_acc[...].astype(BF)


def attention_specs(keys):
    per_query = pl.BlockSpec((PATCHES, 2 * HEAD_DIM), lambda r, h, *_: (r, h))
    per_key = pl.BlockSpec((keys, 2 * HEAD_DIM), lambda r, h, *_: (r, h))
    bound = pl.BlockSpec((1, 1, PATCHES), lambda r, h, *_: (r, 0, 0))
    logs = pl.BlockSpec((1, 1, TILES, 2 * QT), lambda r, h, *_: (r, h, 0, 0))
    return per_query, per_key, bound, logs


def attend(bounds, q, k, v):
    first, stop, lo, hi, chunk = bounds
    rows = lo.shape[0]
    keys = k.shape[0] // rows
    per_query, per_key, bound, logs = attention_specs(keys)
    return pl.pallas_call(
        functools.partial(attend_kernel, chunk),
        grid_spec=pltpu.PrefetchScalarGridSpec(
            num_scalar_prefetch=2,
            grid=(rows, PAIRS),
            in_specs=[bound, bound, per_query, per_key, per_key],
            out_specs=[per_query, logs],
            scratch_shapes=[pltpu.VMEM((keys, 2 * QT), F32)],
        ),
        out_shape=[
            jax.ShapeDtypeStruct(q.shape, BF),
            jax.ShapeDtypeStruct((rows, PAIRS, TILES, 2 * QT), F32),
        ],
        compiler_params=pltpu.CompilerParams(vmem_limit_bytes=32 << 20),
        name="attend",
    )(first, stop, lo, hi, q, k, v)


def attend_back(bounds, q, k, v, logsum, context, grads):
    first, stop, lo, hi, chunk = bounds
    rows = lo.shape[0]
    keys = k.shape[0] // rows
    per_query, per_key, bound, logs = attention_specs(keys)
    return pl.pallas_call(
        functools.partial(attend_back_kernel, chunk),
        grid_spec=pltpu.PrefetchScalarGridSpec(
            num_scalar_prefetch=2,
            grid=(rows, PAIRS),
            in_specs=[bound, bound, per_query, per_key, per_key, logs, per_query, per_query],
            out_specs=[per_query, per_key, per_key],
            scratch_shapes=[pltpu.VMEM((keys, 2 * HEAD_DIM), F32)] * 2,
        ),
        out_shape=[
            jax.ShapeDtypeStruct(q.shape, BF),
            jax.ShapeDtypeStruct(k.shape, BF),
            jax.ShapeDtypeStruct(k.shape, BF),
        ],
        compiler_params=pltpu.CompilerParams(vmem_limit_bytes=32 << 20),
        name="attend_back",
    )(first, stop, lo, hi, q, k, v, logsum, context, grads)


def scale_of(values):
    return lax.rsqrt(jnp.mean(values * values, axis=-1, keepdims=True) + EPS)


def norm_backward(values, row_scale, gain_row, incoming):
    weighted = incoming * gain_row
    projection = jnp.mean(weighted * values, axis=-1, keepdims=True)
    grad_values = row_scale * weighted - values * (row_scale * row_scale * row_scale) * projection
    grad_gain = jnp.sum(incoming * values * row_scale, axis=0)
    return grad_values, grad_gain


def chunk_bounds(lo, hi, chunk):
    first = lo[:, ::QT] // chunk
    stop = (hi[:, QT - 1 :: QT] + chunk - 1) // chunk
    return first, stop, lo[:, None, :], hi[:, None, :], chunk


def shards(
    byte_states, patch_lengths, patch_docs, attn_qkv, attn_out, norm_gains, ffn_in, ffn_down, cotangent
):
    section = lax.axis_index("section")
    group = lax.axis_index("group")
    sections = lax.axis_size("section")
    groups = lax.axis_size("group")
    everyone = ("section", "dp", "group")

    def share(shard):
        rows = shard.shape[0] // groups
        return lax.dynamic_slice_in_dim(shard, group * rows, rows, 0)

    def whole(shard):
        return lax.all_gather(share(shard), everyone, axis=0, tiled=True)

    wq, wk, wv, wo = [
        whole(shard) for shard in (attn_qkv[0, 0], attn_qkv[0, 1], attn_qkv[0, 2], attn_out[0])
    ]
    w_in, w_down = whole(ffn_in), whole(ffn_down)
    gains = lax.all_gather(norm_gains, "section", axis=0, tiled=True)

    rows = byte_states.shape[0] // sections
    mine = lambda a: lax.dynamic_slice_in_dim(a, section * rows, rows, 0)
    states, lengths, docs, cot = [mine(a) for a in (byte_states, patch_lengths, patch_docs, cotangent)]
    cot = cot.reshape(rows * PATCHES, D)

    ends = jnp.cumsum(lengths, axis=1)
    earlier = docs[:, None, :] < docs[:, :, None]
    doc_start = jnp.sum(jnp.where(earlier, lengths[:, None, :], 0), axis=2)
    doc_first = jnp.sum(earlier.astype(jnp.int32), axis=2)
    cross = chunk_bounds(doc_start, ends, 256)
    ids = jnp.broadcast_to(lax.iota(jnp.int32, PATCHES) + 1, doc_first.shape)
    causal = chunk_bounds(doc_first, ids, 128)
    positions = lax.iota(jnp.int32, ROW_BYTES)
    member = (positions < ends[:, :, None]) & (positions >= (ends - lengths)[:, :, None])
    member = member.astype(BF)
    count = lengths.astype(F32).reshape(rows * PATCHES, 1)

    pooled = jnp.einsum("rpb,rbd->rpd", member, states, preferred_element_type=F32)
    pooled = pooled.reshape(rows * PATCHES, D) / count
    wide = states.reshape(rows * ROW_BYTES, D).astype(F32)
    query_scale, key_scale = scale_of(pooled), scale_of(wide)
    query_in = (pooled * query_scale * gains[0, 0]).astype(BF)
    key_in = (wide * key_scale * gains[0, 1]).astype(BF)
    q1 = nn(query_in, wq[:D]).astype(BF)
    k1 = nn(key_in, wk[:D]).astype(BF)
    v1 = nn(key_in, wv[:D]).astype(BF)
    c1, l1 = attend(cross, q1, k1, v1)
    carried = (pooled + nn(c1, wo[:D])).astype(BF)

    carried_wide = carried.astype(F32)
    first_scale = scale_of(carried_wide)
    normed_in = (carried_wide * first_scale * gains[1, 0]).astype(BF)
    q2 = nn(normed_in, wq[D:]).astype(BF)
    k2 = nn(normed_in, wk[D:]).astype(BF)
    v2 = nn(normed_in, wv[D:]).astype(BF)
    c2, l2 = attend(causal, q2, k2, v2)
    residual = carried_wide + nn(c2, wo[D:])
    second_scale = scale_of(residual)
    mix_in = (residual * second_scale * gains[1, 1]).astype(BF)
    gate_up = nn(mix_in, w_in)
    gate, up = gate_up[:, :FF], gate_up[:, FF:]
    sig = jax.nn.sigmoid(gate)
    hidden = (gate * sig * up).astype(BF)
    latents = (residual + nn(hidden, w_down)).astype(BF)

    grad_down = tn(hidden, cot).astype(BF)
    grad_hidden = nt(cot, w_down)
    grad_gate = grad_hidden * up * sig * (1.0 + gate * (1.0 - sig))
    grad_up = grad_hidden * gate * sig
    dgu = jnp.concatenate([grad_gate, grad_up], axis=1).astype(BF)
    grad_in = tn(mix_in, dgu).astype(BF)

    def summed(grad, axes):
        return lax.psum_scatter(grad, axes, scatter_dimension=0, tiled=True)

    sum_down = summed(grad_down, everyone)
    sum_in = summed(grad_in, everyone)

    grad_mix, gain_mix = norm_backward(residual, second_scale, gains[1, 1], nt(dgu, w_in))
    grad_residual = grad_mix + cot.astype(F32)
    branch = grad_residual.astype(BF)

    dc2 = nt(branch, wo[D:]).astype(BF)
    dq2, dk2, dv2 = attend_back(causal, q2, k2, v2, l2, c2, dc2)
    grads_two = [tn(normed_in, dq2), tn(normed_in, dk2), tn(normed_in, dv2), tn(c2, branch)]
    grad_normed = nt(dq2, wq[D:]) + nt(dk2, wk[D:]) + nt(dv2, wv[D:])
    grad_carried, gain_normed = norm_backward(carried_wide, first_scale, gains[1, 0], grad_normed)
    d_carried = (grad_residual + grad_carried).astype(BF)
    spread = ("dp", "group", "section")
    sums_two = [summed(g.astype(BF), spread) for g in grads_two]

    dc1 = nt(d_carried, wo[:D]).astype(BF)
    dq1, dk1, dv1 = attend_back(cross, q1, k1, v1, l1, c1, dc1)
    grads_one = [tn(query_in, dq1), tn(key_in, dk1), tn(key_in, dv1), tn(c1, d_carried)]
    sums_one = [summed(g.astype(BF), spread) for g in grads_one]
    grad_pooled, gain_query = norm_backward(pooled, query_scale, gains[0, 0], nt(dq1, wq[:D]))
    grad_wide, gain_key = norm_backward(
        wide, key_scale, gains[0, 1], nt(dk1, wk[:D]) + nt(dv1, wv[:D])
    )
    per_patch = (grad_pooled + d_carried.astype(F32)) / count
    spread_back = jnp.einsum(
        "rpb,rpd->rbd", member, per_patch.astype(BF).reshape(rows, PATCHES, D), preferred_element_type=F32
    )
    byte_grads = (grad_wide + spread_back.reshape(rows * ROW_BYTES, D)).astype(BF)

    half = D // sections
    swap = [(0, 1), (1, 0)]

    def halves(values, length):
        values = values.reshape(rows, length, D)
        other = lax.dynamic_slice_in_dim(values, (1 - section) * half, half, 2)
        own = lax.dynamic_slice_in_dim(values, section * half, half, 2)
        got = lax.ppermute(other, "section", swap)
        return jnp.where(
            section == 0, jnp.concatenate([own, got], axis=0), jnp.concatenate([got, own], axis=0)
        )

    latents_out = halves(latents, PATCHES)
    bytes_out = halves(byte_grads, ROW_BYTES)

    def to_group(part):
        return lax.all_gather(part, "group", axis=0, tiled=True)

    ffn_gin, ffn_gdown = to_group(sum_in).astype(F32), to_group(sum_down).astype(F32)
    ones, twos = jnp.stack(sums_one), jnp.stack(sums_two)
    kept = jnp.where(section == 0, ones, twos)
    sent = jnp.where(section == 0, twos, ones)
    got = lax.ppermute(sent, "section", swap)
    pieces = jnp.where(section == 0, jnp.stack([kept, got], axis=1), jnp.stack([got, kept], axis=1))
    quarter = pieces.reshape(4, -1, D)
    attn = lax.all_gather(quarter, "group", axis=1, tiled=True).astype(F32)
    gain_grads = jnp.stack([gain_query, gain_key, gain_normed, gain_mix])
    gain_grads = lax.psum(gain_grads, everyone).reshape(2, 2, D)
    gain_grads = lax.dynamic_slice_in_dim(gain_grads, section, 1, 0)
    width = D // lax.axis_size("dp")
    gain_out = lax.dynamic_slice_in_dim(gain_grads, lax.axis_index("dp") * width, width, 2)
    return (latents_out, bytes_out, attn[None, :3], attn[3][None], gain_out, ffn_gin, ffn_gdown)


def solution(mesh):
    in_specs = (
        P(("group", "dp"), None, None),
        P(("group", "dp"), None),
        P(("group", "dp"), None),
        P("section", None, "dp", None),
        P("section", "dp", None),
        P("section", None, None),
        P(("section", "dp"), None),
        P(("section", "dp"), None),
        P(("group", "dp"), None, None),
    )
    out_specs = (
        P(("group", "dp"), None, "section"),
        P(("group", "dp"), None, "section"),
        P("section", None, "dp", None),
        P("section", "dp", None),
        P("section", None, "dp"),
        P(("section", "dp"), None),
        P(("section", "dp"), None),
    )
    return jax.shard_map(shards, mesh=mesh, in_specs=in_specs, out_specs=out_specs, check_vma=False)
```

time: 2140 us -> 1910 us (0.89)
  matrix products: 565 us -> 168 us
  waiting for transfers between devices: 1110 us -> 1440 us
  other arithmetic: 220 us -> 30.8 us
  Pallas kernels: 0 us -> 144 us
  loops' own time: 94.3 us -> 0 us
  local copies, waits for them, and re-layouts: 106 us -> 41.5 us
  blocking collectives: 6.21 us -> 56.9 us
    reduce_scatter x4 -> x10, waiting for transfers between devices: 435 us -> 1150 us  [summed(): return lax.psum_scatter(grad, axes, scatter_dimension=0, tiled=True)]
    dot_general x208 -> x32, matrix products: 565 us -> 168 us  [the longest x10 61 us: nt(): lax.dot_general(left, right, (((1,), (1,)), ((), ())), preferred_element_...]
    ppermute x10 -> x3, waiting for transfers between devices: 191 us -> 5.23 us  [the longest x1 5.23 us: shards(): got = lax.ppermute(sent, 'section', swap)]
    pallas_call x0 -> x4, Pallas kernels: none -> 144 us  [the longest x2 77.4 us: attend_back(): pl.pallas_call(functools.partial(attend_back_kernel, chunk), grid_spec=pl...]
    all_gather x4 -> x8, waiting for transfers between devices: 410 us -> 290 us  [the longest x6 282 us: whole(): return lax.all_gather(share(shard), everyone, axis=0, tiled=True)]
    another operation x22 -> x0, loops' own time: 94.3 us -> none  [the longest x5 53.9 us: shards(): lax.switch(branch, [resting_back, first_back, second_back], totals)]
    psum x1 -> x0, waiting for transfers between devices: 67.3 us -> none  [shards(): lax.psum(layer_qkv.astype(jnp.bfloat16), 'group').astype(jnp.float32)]
    convert_element_type x37 -> x8, other arithmetic: 68.6 us -> 17.3 us  [the longest x1 4.99 us: shards(): (grad_wide + spread_back.reshape(rows * ROW_BYTES, D)).astype(BF)]
  transfers between devices with their start and end apart: 20 -> 21, of which waited for: 17 -> 17; matrix products, arithmetic and copies ran while one was open for 3% -> 9% of each run, Pallas kernels for 0% -> 8%
where the time goes in v1:
time: 1910 us; the launch traced here: 1900 us
  waiting for transfers between devices  1440 us (75%)
  matrix products  168 us (9%)
  Pallas kernels  144 us (8%)
  blocking collectives  56.9 us (3%)
  local copies, waits for them, and re-layouts  41.5 us (2%)
  other arithmetic  30.8 us (2%)
    reduce_scatter x10, waiting for transfers between devices, summed(): return lax.psum_scatter(grad, axes, scatter_dimension=0, tiled=True)  1150 us
    all_gather x6, waiting for transfers between devices, whole(): return lax.all_gather(share(shard), everyone, axis=0, tiled=True)  282 us
    pallas_call x2, Pallas kernels, attend_back(): pl.pallas_call(functools.partial(attend_back_kernel, chunk), grid_spec=pl...  77.4 us
    pallas_call x2, Pallas kernels, attend(): pl.pallas_call(functools.partial(attend_kernel, chunk), grid_spec=pltpu.P...  66.4 us
    dot_general x10, matrix products, nt(): lax.dot_general(left, right, (((1,), (1,)), ((), ())), preferred_element_...  61 us
    dot_general x10, matrix products, tn(): lax.dot_general(left, right, (((0,), (0,)), ((), ())), preferred_element_...  52.7 us
    dot_general x10, matrix products, nn(): return jnp.dot(left, right, preferred_element_type=F32)  49.5 us
    psum x1, blocking collectives, shards(): gain_grads = lax.psum(gain_grads, everyone).reshape(2, 2, D)  44.2 us
  transfers between devices with their start and end apart: 21, of which 17 were waited for; matrix products, arithmetic and copies ran while one was open for 9% of the time, Pallas kernels for 8%

profile of v1, /device:TPU:0, one launch (start us, length us, event | category | flops | bytes accessed | tf_op | source)
XLA Modules:
  0.0 1900.7 jit_solution(2375923363948494608)
XLA Ops:
  19.9 3.8 multiply_reduce_fusion.5
  25.8 5.4 all_gather.30
  35.5 40.8 %all-gather.21.cloned.1.call-done = bf16[1,1,2048,1024]{3,2,1,0:T(8,128)(2,1)} async-done(((bf16[1,1,64,1024]{3,2,1,0:T(8,128)(2,1)}), bf16[1,1,2048,1024]{3,2,1,0:T(8,128)(2,1)}) %all-gather.21.cloned.1.call-update) | async-done | bytes 4194320 | tf_op jit(solution)/shard_map/all_gather | solution.py:224
  79.2 61.2 %all-gather.23.cloned.1.call-done = bf16[1,1,2048,1024]{3,2,1,0:T(8,128)(2,1)} async-done(((bf16[1,1,64,1024]{3,2,1,0:T(8,128)(2,1)}), bf16[1,1,2048,1024]{3,2,1,0:T(8,128)(2,1)}) %all-gather.23.cloned.1.call-update) | async-done | bytes 4194320 | tf_op jit(solution)/shard_map/all_gather | solution.py:224
  140.4 9.4 convolution_convert_fusion.3.k_ref
  149.8 54.2 %all-gather.25.cloned.1.call-done = bf16[1,1,2048,1024]{3,2,1,0:T(8,128)(2,1)} async-done(((bf16[1,1,64,1024]{3,2,1,0:T(8,128)(2,1)}), bf16[1,1,2048,1024]{3,2,1,0:T(8,128)(2,1)}) %all-gather.25.cloned.1.call-update) | async-done | bytes 4194320 | tf_op jit(solution)/shard_map/all_gather | solution.py:224
  204.0 7.5 convolution_convert_fusion.2.v_ref
  211.5 42.8 %attend.2 = (bf16[512,1024]{1,0:T(8,128)(2,1)S(1)}, f32[2,8,2,256]{3,2,1,0:T(2,128)S(1)}) custom-call(s32[2,2]{1,0:T(2,128)S(1)} %get-tuple-element.76.first_ref, s32[2,2]{1,0:T(2,128)S(1)} %get-tuple-element.75.stop_ref, s32[2,1,256]{2,1,0:T(1,128)S(1)} %broadcast_in_dim.56.lo_ref, s32[2,1,256]{2,1,0:T(1,128)S(1)} %bitcast.181, ...), custom_call_target="tpu_custom_call" | custom-call | tf_op jit(solution)/shard_map/attend/pallas_call | solution.py:150
  256.3 11.4 all-gather.27.cloned.1.call-done
  267.6 3.7 fusion.10
  277.5 23.6 %attend.3 = (bf16[512,1024]{1,0:T(8,128)(2,1)S(1)}, f32[2,8,2,256]{3,2,1,0:T(2,128)S(1)}) custom-call(s32[2,2]{1,0:T(2,128)S(1)} %get-tuple-element.74.first_ref, s32[2,2]{1,0:T(2,128)S(1)} %get-tuple-element.73.stop_ref, s32[2,1,256]{2,1,0:T(1,128)S(1)} %broadcast_in_dim.61.lo_ref, s32[2,1,256]{2,1,0:T(1,128)S(1)} %broadcast_in_dim_broadcast_in_dim.5.hi_ref, ...), custom_call_target="tpu_custom_call" | custom-call | tf_op jit(solution)/shard_map/attend/pallas_call | solution.py:150
  303.8 57.8 %all-gather.13.cloned.1.call-done = bf16[1024,5632]{1,0:T(8,128)(2,1)} async-done(((bf16[32,5632]{1,0:T(8,128)(2,1)}), bf16[1024,5632]{1,0:T(8,128)(2,1)}) %all-gather.13.cloned.1.call-update) | async-done | bytes 11534352 | tf_op jit(solution)/shard_map/all_gather | solution.py:224
  361.6 12.2 fusion.58
  373.8 56.8 %all-gather.15.cloned.1.call-done = bf16[2816,1024]{1,0:T(8,128)(2,1)} async-done(((bf16[88,1024]{1,0:T(8,128)(2,1)}), bf16[2816,1024]{1,0:T(8,128)(2,1)}) %all-gather.15.cloned.1.call-update) | async-done | bytes 5767184 | tf_op jit(solution)/shard_map/all_gather | solution.py:224
  430.6 12.3 multiply_convert_fusion.1
  443.0 13.2 multiply_reduce_fusion
  456.2 3.6 convert_add_fusion.1
  459.7 4.2 convolution_convert_fusion.4
  464.1 3.7 fusion.39.dc_ref
  467.8 26.0 %attend_back.2 = (bf16[512,1024]{1,0:T(8,128)(2,1)S(1)}, bf16[512,1024]{1,0:T(8,128)(2,1)S(1)}, bf16[512,1024]{1,0:T(8,128)(2,1)S(1)}) custom-call(s32[2,2]{1,0:T(2,128)S(1)} %get-tuple-element.74.first_ref, s32[2,2]{1,0:T(2,128)S(1)} %get-tuple-element.73.stop_ref, s32[2,1,256]{2,1,0:T(1,128)S(1)} %broadcast_in_dim.61.lo_ref, ...), custom_call_target="tpu_custom_call" | custom-call | tf_op jit(solution)/shard_map/attend_back/pallas_call | solution.py:173
  504.9 3.9 convolution_convert_fusion.7
  509.1 3.0 fusion.26
  521.9 3.0 fusion.43.dc_ref
  526.0 51.4 %attend_back.3 = (bf16[512,1024]{1,0:T(8,128)(2,1)S(1)}, bf16[2048,1024]{1,0:T(8,128)(2,1)S(1)}, bf16[2048,1024]{1,0:T(8,128)(2,1)S(1)}) custom-call(s32[2,2]{1,0:T(2,128)S(1)} %get-tuple-element.76.first_ref, s32[2,2]{1,0:T(2,128)S(1)} %get-tuple-element.75.stop_ref, s32[2,1,256]{2,1,0:T(1,128)S(1)} %broadcast_in_dim.56.lo_ref, s32[2,1,256]{2,1,0:T(1,128)S(1)} %bitcast.182, ...), custom_call_target="tpu_custom_call" | custom-call | tf_op jit(solution)/shard_map/attend_back/pallas_call | solution.py:173
  581.5 5.8 convolution_convert_fusion.9
  587.6 9.4 convolution_convert_fusion.10
  602.9 11.8 convolution_convert_fusion
  614.8 121.9 %reduce-scatter.23.cloned.1.call-done = bf16[32,1024]{1,0:T(8,128)(2,1)} async-done(((bf16[1024,1024]{1,0:T(8,128)(2,1)}), bf16[32,1024]{1,0:T(8,128)(2,1)}) %reduce-scatter.23.cloned.1.call-update) | async-done | bytes 65552 | tf_op jit(solution)/shard_map/reduce_scatter | solution.py:285
  736.7 135.8 %reduce-scatter.21.cloned.1.call-done = bf16[32,1024]{1,0:T(8,128)(2,1)} async-done(((bf16[1024,1024]{1,0:T(8,128)(2,1)}), bf16[32,1024]{1,0:T(8,128)(2,1)}) %reduce-scatter.21.cloned.1.call-update) | async-done | bytes 65552 | tf_op jit(solution)/shard_map/reduce_scatter | solution.py:285
  872.4 135.6 %reduce-scatter.19.cloned.1.call-done = bf16[32,1024]{1,0:T(8,128)(2,1)} async-done(((bf16[1024,1024]{1,0:T(8,128)(2,1)}), bf16[32,1024]{1,0:T(8,128)(2,1)}) %reduce-scatter.19.cloned.1.call-update) | async-done | bytes 65552 | tf_op jit(solution)/shard_map/reduce_scatter | solution.py:285
  1008.1 135.5 %reduce-scatter.17.cloned.1.call-done = bf16[32,1024]{1,0:T(8,128)(2,1)} async-done(((bf16[1024,1024]{1,0:T(8,128)(2,1)}), bf16[32,1024]{1,0:T(8,128)(2,1)}) %reduce-scatter.17.cloned.1.call-update) | async-done | bytes 65552 | tf_op jit(solution)/shard_map/reduce_scatter | solution.py:285
  1143.5 135.3 %reduce-scatter.15.cloned.1.call-done = bf16[32,1024]{1,0:T(8,128)(2,1)} async-done(((bf16[1024,1024]{1,0:T(8,128)(2,1)}), bf16[32,1024]{1,0:T(8,128)(2,1)}) %reduce-scatter.15.cloned.1.call-update) | async-done | bytes 65552 | tf_op jit(solution)/shard_map/reduce_scatter | solution.py:285
  1278.8 135.6 %reduce-scatter.13.cloned.1.call-done = bf16[32,1024]{1,0:T(8,128)(2,1)} async-done(((bf16[1024,1024]{1,0:T(8,128)(2,1)}), bf16[32,1024]{1,0:T(8,128)(2,1)}) %reduce-scatter.13.cloned.1.call-update) | async-done | bytes 65552 | tf_op jit(solution)/shard_map/reduce_scatter | solution.py:285
  1414.4 136.2 %reduce-scatter.11.cloned.1.call-done = bf16[32,1024]{1,0:T(8,128)(2,1)} async-done(((bf16[1024,1024]{1,0:T(8,128)(2,1)}), bf16[32,1024]{1,0:T(8,128)(2,1)}) %reduce-scatter.11.cloned.1.call-update) | async-done | bytes 65552 | tf_op jit(solution)/shard_map/reduce_scatter | solution.py:285
  1553.1 5.2 collective-permute-done.2
  1559.3 6.8 convolution_convert_fusion.1
  1567.8 3.3 multiply_reduce_fusion.1
  1571.1 8.9 fusion.23
  1580.1 10.4 fusion.8
  1592.6 5.0 fusion
  1599.6 104.4 %reduce-scatter.27.cloned.1.call-done = bf16[32,5632]{1,0:T(8,128)(2,1)} async-done(((bf16[1024,5632]{1,0:T(8,128)(2,1)}), bf16[32,5632]{1,0:T(8,128)(2,1)}) %reduce-scatter.27.cloned.1.call-update) | async-done | bytes 360464 | tf_op jit(solution)/shard_map/reduce_scatter | solution.py:285
  1704.0 7.2 add_convert_fusion
  1712.8 44.2 %psum.7 = f32[2,2,1024]{2,1,0:T(2,128)S(1)} all-reduce(f32[2,2,1024]{2,1,0:T(2,128)S(1)} %reshape.322), channel_id=1, replica_groups=mesh['section'=2,'group'=4,'dp'=4] {'section','dp','group'}, use_global_device_ids=true, to_apply=%region_24.25 | all-reduce | flops 4096 | bytes 32768 | tf_op jit(solution)/shard_map/psum | solution.py:344
  1758.8 3.9 maximum_select_fusion
  1767.9 105.5 %reduce-scatter.29.cloned.1.call-done = bf16[88,1024]{1,0:T(8,128)(2,1)} async-done(((bf16[2816,1024]{1,0:T(8,128)(2,1)}), bf16[88,1024]{1,0:T(8,128)(2,1)}) %reduce-scatter.29.cloned.1.call-update) | async-done | bytes 180240 | tf_op jit(solution)/shard_map/reduce_scatter | solution.py:285
  1873.3 7.2 all_gather.39
  1881.8 8.3 all-gather.19.cloned.1.call-done
  1890.1 3.2 convert_element_type.159
  (253 shorter events, 83.5 us)
Async XLA Ops:
  7.2 24.0 %copy-start = (bf16[4,256,1024]{2,1,0:T(8,128)(2,1)S(1)}, bf16[4,256,1024]{2,1,0:T(8,128)(2,1)}, u32[]{:S(2)}) copy-start(bf16[4,256,1024]{2,1,0:T(8,128)(2,1)} %param.17) | copy-start | bytes 6291460
  7.2 69.1 %all-gather.21.cloned.1.call-start = ((), (), s32[]{:S(2)}) async-start(), calls=%async_computation.24 | async-start | bytes 4325376 | tf_op jit(solution)/shard_map/all_gather | solution.py:224
  9.7 8.3 copy-start.53
  9.7 8.3 copy-start.54
  11.3 129.1 %all-gather.23.cloned.1.call-start = ((), (), s32[]{:S(2)}) async-start(), calls=%async_computation.25 | async-start | bytes 4325376 | tf_op jit(solution)/shard_map/all_gather | solution.py:224
  12.1 191.9 %all-gather.25.cloned.1.call-start = ((), (), s32[]{:S(2)}) async-start(), calls=%async_computation.26 | async-start | bytes 4325376 | tf_op jit(solution)/shard_map/all_gather | solution.py:224
  12.8 254.8 %all-gather.27.cloned.1.call-start = ((), (), s32[]{:S(2)}) async-start(), calls=%async_computation.27 | async-start | bytes 4325376 | tf_op jit(solution)/shard_map/all_gather | solution.py:224
  14.4 347.2 %all-gather.13.cloned.1.call-start = ((), (), s32[]{:S(2)}) async-start(), calls=%async_computation.10 | async-start | bytes 11894784 | tf_op jit(solution)/shard_map/all_gather | solution.py:224
  16.3 414.4 %all-gather.15.cloned.1.call-start = ((), (), s32[]{:S(2)}) async-start(), calls=%async_computation.11 | async-start | bytes 5947392 | tf_op jit(solution)/shard_map/all_gather | solution.py:224
  17.9 596.8 %reduce-scatter.25.cloned.1.call-start = ((), (), s32[]{:S(2)}) async-start(), calls=%async_computation.19 | async-start | bytes 2162688 | tf_op jit(solution)/shard_map/reduce_scatter | solution.py:285
  19.8 12.6 copy-start.48
  23.8 8.6 copy-start.23
  25.7 6.9 copy-start.42
  32.7 43.7 %copy-start.33 = (f32[512,1024]{1,0:T(8,128)}, f32[512,1024]{1,0:T(8,128)S(1)}, u32[]{:S(2)}) copy-start(f32[512,1024]{1,0:T(8,128)S(1)} %bitcast_divide_fusion) | copy-start | bytes 6291460
  204.0 7.5 copy-start.2
  256.3 15.1 copy-start.8
  271.4 29.8 %copy-start.36 = (bf16[512,1024]{1,0:T(8,128)(2,1)}, bf16[512,1024]{1,0:T(8,128)(2,1)S(1)}, u32[]{:S(2)}) copy-start(bf16[512,1024]{1,0:T(8,128)(2,1)S(1)} %get-tuple-element.66) | copy-start | bytes 3145732
  276.1 25.0 %copy-start.61 = (bf16[1,2048,1024]{2,1,0:T(8,128)(2,1)S(1)}, bf16[1,2048,1024]{2,1,0:T(8,128)(2,1)}, u32[]{:S(2)}) copy-start(bf16[1,2048,1024]{2,1,0:T(8,128)(2,1)} %all-gather.27.cloned.1.call-done) | copy-start | bytes 12582916
  277.4 26.4 %copy-start.6 = (bf16[512,1024]{1,0:T(8,128)(2,1)}, bf16[512,1024]{1,0:T(8,128)(2,1)S(1)}, u32[]{:S(2)}) copy-start(bf16[512,1024]{1,0:T(8,128)(2,1)S(1)} %fusion.40.v_ref) | copy-start | bytes 3145732
  430.6 12.3 copy-start.31
  443.0 13.2 copy-start.26
  464.0 272.7 %reduce-scatter.23.cloned.1.call-start = ((), (), s32[]{:S(2)}) async-start(), calls=%async_computation.18 | async-start | bytes 2162688 | tf_op jit(solution)/shard_map/reduce_scatter | solution.py:285
  467.8 29.0 %copy-start.37 = (bf16[512,1024]{1,0:T(8,128)(2,1)S(1)}, bf16[512,1024]{1,0:T(8,128)(2,1)}, u32[]{:S(2)}) copy-start(bf16[512,1024]{1,0:T(8,128)(2,1)} %copy-done.36) | copy-start | bytes 3145732
  499.4 373.0 %reduce-scatter.21.cloned.1.call-start = ((), (), s32[]{:S(2)}) async-start(), calls=%async_computation.17 | async-start | bytes 2162688 | tf_op jit(solution)/shard_map/reduce_scatter | solution.py:285
  503.7 504.4 %reduce-scatter.19.cloned.1.call-start = ((), (), s32[]{:S(2)}) async-start(), calls=%async_computation.16 | async-start | bytes 2162688 | tf_op jit(solution)/shard_map/reduce_scatter | solution.py:285
  508.9 634.7 %reduce-scatter.17.cloned.1.call-start = ((), (), s32[]{:S(2)}) async-start(), calls=%async_computation.15 | async-start | bytes 2162688 | tf_op jit(solution)/shard_map/reduce_scatter | solution.py:285
  521.9 757.0 %reduce-scatter.15.cloned.1.call-start = ((), (), s32[]{:S(2)}) async-start(), calls=%async_computation.14 | async-start | bytes 2162688 | tf_op jit(solution)/shard_map/reduce_scatter | solution.py:285
  526.0 55.5 %copy-start.28 = (bf16[2048,1024]{1,0:T(8,128)(2,1)S(1)}, bf16[2048,1024]{1,0:T(8,128)(2,1)}, u32[]{:S(2)}) copy-start(bf16[2048,1024]{1,0:T(8,128)(2,1)} %fusion.3) | copy-start | bytes 12582916
  587.3 827.1 %reduce-scatter.13.cloned.1.call-start = ((), (), s32[]{:S(2)}) async-start(), calls=%async_computation.13 | async-start | bytes 2162688 | tf_op jit(solution)/shard_map/reduce_scatter | solution.py:285
  597.0 953.6 %reduce-scatter.11.cloned.1.call-start = ((), (), s32[]{:S(2)}) async-start(), calls=%async_computation.12 | async-start | bytes 2162688 | tf_op jit(solution)/shard_map/reduce_scatter | solution.py:285
  601.3 1102.7 %reduce-scatter.27.cloned.1.call-start = ((), (), s32[]{:S(2)}) async-start(), calls=%async_computation.21 | async-start | bytes 11894784 | tf_op jit(solution)/shard_map/reduce_scatter | solution.py:285
  614.7 1148.0 %all-gather.17.cloned.1.call-start = ((), (), s32[]{:S(2)}) async-start(), calls=%async_computation.20 | async-start | bytes 2621440 | tf_op jit(solution)/shard_map/all_gather | solution.py:342
  1550.6 8.7 copy-start.27
  1551.9 6.4 collective-permute-start.2
  1559.3 314.1 %reduce-scatter.29.cloned.1.call-start = ((), (), s32[]{:S(2)}) async-start(), calls=%async_computation.23 | async-start | bytes 5947392 | tf_op jit(solution)/shard_map/reduce_scatter | solution.py:285
  1566.2 323.9 %all-gather.19.cloned.1.call-start = ((), (), s32[]{:S(2)}) async-start(), calls=%async_computation.22 | async-start | bytes 1802240 | tf_op jit(solution)/shard_map/all_gather | solution.py:333
  1567.8 12.3 slice-start.2
  1571.1 9.0 copy-start.14
  1571.1 8.9 slice-start.3
  1571.1 8.9 copy-start.41
  1571.1 8.9 copy-start.45
  1571.1 8.9 copy-start.60
  1580.1 10.5 copy-start.24
  1580.1 10.5 copy-start.30
  1580.1 10.4 copy-start.49
  1599.5 159.3 %collective-permute-start.1 = (bf16[2,1024,512]{2,1,0:T(8,128)(2,1)}, bf16[2,1024,512]{2,1,0:T(8,128)(2,1)}, u32[]{:S(2)}, u32[]{:S(2)}) collective-permute-start(bf16[2,1024,512]{2,1,0:T(8,128)(2,1)} %get-tuple-element.43), channel_id=1, source_target_pairs={{0,16},{16,0},{1,17},{17,1},{2,18},{18,2},{3,19},{19,3},{4,20},{20... | collective-permute-start | bytes 6291464 | tf_op jit(solution)/shard_map/ppermute | solution.py:324
  1712.2 45.4 %collective-permute-start = (bf16[2,256,512]{2,1,0:T(8,128)(2,1)}, bf16[2,256,512]{2,1,0:T(8,128)(2,1)S(1)}, u32[]{:S(2)}, u32[]{:S(2)}) collective-permute-start(bf16[2,256,512]{2,1,0:T(8,128)(2,1)} %get-tuple-element.48), channel_id=1, source_target_pairs={{0,16},{16,0},{1,17},{17,1},{2,18},{18,2},{3,19},{19,3},{4,20},{20... | collective-permute-start | bytes 1572872 | tf_op jit(solution)/shard_map/ppermute | solution.py:324
  1880.6 12.8 copy-start.1
  (39 other events, 93.9 us)
Sparse Core Ops, SparseCore 0:
  11.5 64.7 all-gather.20
  79.8 60.5 all-gather.22
  143.3 60.6 all-gather.24
  206.7 60.8 all-gather.26
  270.9 90.6 all-gather.12
  364.9 65.6 all-gather.14
  464.1 136.6 reduce-scatter.24
  603.1 133.4 reduce-scatter.22
  738.9 133.4 reduce-scatter.20
  874.6 133.3 reduce-scatter.18
  1010.3 133.1 reduce-scatter.16
  1145.7 133.0 reduce-scatter.14
  1281.1 133.2 reduce-scatter.12
  1417.2 133.4 reduce-scatter.10
  1552.8 151.1 reduce-scatter.26
  1706.0 21.3 all-gather.16
  1729.6 143.7 reduce-scatter.28
  1874.8 15.3 all-gather.18

commit v2 on v1

--- a/solution.py
+++ b/solution.py
@@ -214,18 +214,18 @@
     group = lax.axis_index("group")
     sections = lax.axis_size("section")
     groups = lax.axis_size("group")
-    everyone = ("section", "dp", "group")
-
-    def share(shard):
+    core, side = group % 2, group // 2
+
+    def whole(shard):
         rows = shard.shape[0] // groups
-        return lax.dynamic_slice_in_dim(shard, group * rows, rows, 0)
-
-    def whole(shard):
-        return lax.all_gather(share(shard), everyone, axis=0, tiled=True)
-
-    wq, wk, wv, wo = [
-        whole(shard) for shard in (attn_qkv[0, 0], attn_qkv[0, 1], attn_qkv[0, 2], attn_out[0])
-    ]
+        part = lax.dynamic_slice_in_dim(shard, group * rows, rows, 0)
+        return lax.all_gather(part, ("section", "dp", "group"), axis=0, tiled=True)
+
+    four = jnp.concatenate([attn_qkv[0], attn_out], axis=0)
+    matrix = lax.dynamic_index_in_dim(four, group, 0, keepdims=False)
+    matrices = lax.all_gather(matrix, ("section", "group", "dp"), axis=0, tiled=True)
+    matrices = matrices.reshape(sections, groups, D, D)
+    wq, wk, wv, wo = [matrices[:, index] for index in range(4)]
     w_in, w_down = whole(ffn_in), whole(ffn_down)
     gains = lax.all_gather(norm_gains, "section", axis=0, tiled=True)
 
@@ -252,20 +252,20 @@
     query_scale, key_scale = scale_of(pooled), scale_of(wide)
     query_in = (pooled * query_scale * gains[0, 0]).astype(BF)
     key_in = (wide * key_scale * gains[0, 1]).astype(BF)
-    q1 = nn(query_in, wq[:D]).astype(BF)
-    k1 = nn(key_in, wk[:D]).astype(BF)
-    v1 = nn(key_in, wv[:D]).astype(BF)
+    q1 = nn(query_in, wq[0]).astype(BF)
+    k1 = nn(key_in, wk[0]).astype(BF)
+    v1 = nn(key_in, wv[0]).astype(BF)
     c1, l1 = attend(cross, q1, k1, v1)
-    carried = (pooled + nn(c1, wo[:D])).astype(BF)
+    carried = (pooled + nn(c1, wo[0])).astype(BF)
 
     carried_wide = carried.astype(F32)
     first_scale = scale_of(carried_wide)
     normed_in = (carried_wide * first_scale * gains[1, 0]).astype(BF)
-    q2 = nn(normed_in, wq[D:]).astype(BF)
-    k2 = nn(normed_in, wk[D:]).astype(BF)
-    v2 = nn(normed_in, wv[D:]).astype(BF)
+    q2 = nn(normed_in, wq[1]).astype(BF)
+    k2 = nn(normed_in, wk[1]).astype(BF)
+    v2 = nn(normed_in, wv[1]).astype(BF)
     c2, l2 = attend(causal, q2, k2, v2)
-    residual = carried_wide + nn(c2, wo[D:])
+    residual = carried_wide + nn(c2, wo[1])
     second_scale = scale_of(residual)
     mix_in = (residual * second_scale * gains[1, 1]).astype(BF)
     gate_up = nn(mix_in, w_in)
@@ -274,39 +274,65 @@
     hidden = (gate * sig * up).astype(BF)
     latents = (residual + nn(hidden, w_down)).astype(BF)
 
-    grad_down = tn(hidden, cot).astype(BF)
     grad_hidden = nt(cot, w_down)
     grad_gate = grad_hidden * up * sig * (1.0 + gate * (1.0 - sig))
     grad_up = grad_hidden * gate * sig
     dgu = jnp.concatenate([grad_gate, grad_up], axis=1).astype(BF)
-    grad_in = tn(mix_in, dgu).astype(BF)
-
-    def summed(grad, axes):
-        return lax.psum_scatter(grad, axes, scatter_dimension=0, tiled=True)
-
-    sum_down = summed(grad_down, everyone)
-    sum_in = summed(grad_in, everyone)
+
+    def exchanged(values, axis, part, pairs, where):
+        size = values.shape[where] // 2
+        other = lax.dynamic_slice_in_dim(values, (1 - part) * size, size, where)
+        own = lax.dynamic_slice_in_dim(values, part * size, size, where)
+        return (own.astype(F32) + lax.ppermute(other, axis, pairs).astype(F32)).astype(BF)
+
+    def over_section(values, where):
+        return exchanged(values, "section", section, [(0, 1), (1, 0)], where)
+
+    def over_side(values, where):
+        return exchanged(values, "group", side, [(0, 2), (1, 3), (2, 0), (3, 1)], where)
+
+    def chip_sum(half_of):
+        got = lax.ppermute(half_of(1 - core).astype(BF), "group", [(0, 1), (1, 0), (2, 3), (3, 2)])
+        return (half_of(core) + got.astype(F32)).astype(BF)
+
+    def columns(values, part):
+        size = values.shape[-1] // 2
+        return lax.dynamic_slice_in_dim(values, part * size, size, values.ndim - 1)
+
+    def line_sum(values, where):
+        return lax.psum_scatter(values, "dp", scatter_dimension=where, tiled=True)
+
+    sum_in = chip_sum(lambda part: tn(mix_in, columns(dgu, part)))
+    sum_in = line_sum(over_side(over_section(sum_in, 0), 1), 0)
+    sum_down = chip_sum(lambda part: tn(hidden, columns(cot, part)))
+    sum_down = line_sum(over_section(over_side(sum_down, 1), 0), 0)
 
     grad_mix, gain_mix = norm_backward(residual, second_scale, gains[1, 1], nt(dgu, w_in))
     grad_residual = grad_mix + cot.astype(F32)
     branch = grad_residual.astype(BF)
 
-    dc2 = nt(branch, wo[D:]).astype(BF)
+    dc2 = nt(branch, wo[1]).astype(BF)
     dq2, dk2, dv2 = attend_back(causal, q2, k2, v2, l2, c2, dc2)
-    grads_two = [tn(normed_in, dq2), tn(normed_in, dk2), tn(normed_in, dv2), tn(c2, branch)]
-    grad_normed = nt(dq2, wq[D:]) + nt(dk2, wk[D:]) + nt(dv2, wv[D:])
+
+    def four_sums(pairs):
+        def half_of(part):
+            return jnp.stack([tn(left, columns(right, part)) for left, right in pairs])
+
+        return chip_sum(half_of)
+
+    sums_two = four_sums([(normed_in, dq2), (normed_in, dk2), (normed_in, dv2), (c2, branch)])
+    sums_two = line_sum(over_section(over_side(sums_two, 2), 2), 1)
+    grad_normed = nt(dq2, wq[1]) + nt(dk2, wk[1]) + nt(dv2, wv[1])
     grad_carried, gain_normed = norm_backward(carried_wide, first_scale, gains[1, 0], grad_normed)
     d_carried = (grad_residual + grad_carried).astype(BF)
-    spread = ("dp", "group", "section")
-    sums_two = [summed(g.astype(BF), spread) for g in grads_two]
-
-    dc1 = nt(d_carried, wo[:D]).astype(BF)
+
+    dc1 = nt(d_carried, wo[0]).astype(BF)
     dq1, dk1, dv1 = attend_back(cross, q1, k1, v1, l1, c1, dc1)
-    grads_one = [tn(query_in, dq1), tn(key_in, dk1), tn(key_in, dv1), tn(c1, d_carried)]
-    sums_one = [summed(g.astype(BF), spread) for g in grads_one]
-    grad_pooled, gain_query = norm_backward(pooled, query_scale, gains[0, 0], nt(dq1, wq[:D]))
+    sums_one = four_sums([(query_in, dq1), (key_in, dk1), (key_in, dv1), (c1, d_carried)])
+    sums_one = line_sum(over_section(over_side(sums_one, 2), 2), 1)
+    grad_pooled, gain_query = norm_backward(pooled, query_scale, gains[0, 0], nt(dq1, wq[0]))
     grad_wide, gain_key = norm_backward(
-        wide, key_scale, gains[0, 1], nt(dk1, wk[:D]) + nt(dv1, wv[:D])
+        wide, key_scale, gains[0, 1], nt(dk1, wk[0]) + nt(dv1, wv[0])
     )
     per_patch = (grad_pooled + d_carried.astype(F32)) / count
     spread_back = jnp.einsum(
@@ -330,18 +356,21 @@
     bytes_out = halves(byte_grads, ROW_BYTES)
 
     def to_group(part):
-        return lax.all_gather(part, "group", axis=0, tiled=True)
-
-    ffn_gin, ffn_gdown = to_group(sum_in).astype(F32), to_group(sum_down).astype(F32)
-    ones, twos = jnp.stack(sums_one), jnp.stack(sums_two)
-    kept = jnp.where(section == 0, ones, twos)
-    sent = jnp.where(section == 0, twos, ones)
+        every = lax.all_gather(part, "group", axis=0, tiled=False)
+        every = every.reshape((2, 2) + part.shape)
+        every = jnp.moveaxis(every, (1, 0), (-3, -2))
+        return every.reshape(part.shape[:-1] + (-1,)).astype(F32)
+
+    ffn_gin, ffn_gdown = to_group(sum_in), to_group(sum_down)
+    kept = jnp.where(section == 0, sums_one, sums_two)
+    sent = jnp.where(section == 0, sums_two, sums_one)
     got = lax.ppermute(sent, "section", swap)
-    pieces = jnp.where(section == 0, jnp.stack([kept, got], axis=1), jnp.stack([got, kept], axis=1))
-    quarter = pieces.reshape(4, -1, D)
-    attn = lax.all_gather(quarter, "group", axis=1, tiled=True).astype(F32)
+    quarter = jnp.where(
+        section == 0, jnp.concatenate([kept, got], axis=2), jnp.concatenate([got, kept], axis=2)
+    )
+    attn = to_group(quarter)
     gain_grads = jnp.stack([gain_query, gain_key, gain_normed, gain_mix])
-    gain_grads = lax.psum(gain_grads, everyone).reshape(2, 2, D)
+    gain_grads = lax.psum(gain_grads, ("section", "group", "dp")).reshape(2, 2, D)
     gain_grads = lax.dynamic_slice_in_dim(gain_grads, section, 1, 0)
     width = D // lax.axis_size("dp")
     gain_out = lax.dynamic_slice_in_dim(gain_grads, lax.axis_index("dp") * width, width, 2)

time: 1910 us -> 904 us (0.47)
  waiting for transfers between devices: 1440 us -> 341 us
  blocking collectives: 56.9 us -> 93.3 us
  other arithmetic: 30.8 us -> 65.6 us
    reduce_scatter x10 -> x4, waiting for transfers between devices: 1150 us -> 0.04 us  [line_sum(): return lax.psum_scatter(values, 'dp', scatter_dimension=where, tiled=True)]
    ppermute x0 -> x12, waiting for transfers between devices: none -> 187 us  [the longest x8 187 us: exchanged(): lax.ppermute(other, axis, pairs).astype(F32)]
    all_gather x8 -> x5, waiting for transfers between devices: 290 us -> 153 us  [the longest x1 95.4 us: shards(): lax.all_gather(matrix, ('section', 'group', 'dp'), axis=0, tiled=True)]
    psum x1, blocking collectives: 44.2 us -> 78.4 us  [shards(): lax.psum(gain_grads, ('section', 'group', 'dp')).reshape(2, 2, D)]
    convert_element_type x3 -> x16, other arithmetic: 6.69 us -> 36.2 us  [the longest x8 20.2 us: exchanged(): (own.astype(F32) + lax.ppermute(other, axis, pairs).astype(F32)).astype(BF)]
    dot_general x10 -> x20, matrix products: 52.7 us -> 45.6 us  [tn(): lax.dot_general(left, right, (((0,), (0,)), ((), ())), preferred_element_...]
  transfers between devices with their start and end apart: 21 -> 24, of which waited for: 17 -> 11; matrix products, arithmetic and copies ran while one was open for 9% -> 20% of each run, Pallas kernels for 8% -> 7%
where the time goes in v2:
time: 904 us; the launch traced here: 900 us
  waiting for transfers between devices  341 us (38%)
  matrix products  166 us (18%)
  Pallas kernels  144 us (16%)
  blocking collectives  93.3 us (10%)
  other arithmetic  65.6 us (7%)
  local copies, waits for them, and re-layouts  59.8 us (7%)
  between operations  15.6 us (2%)
  starting transfers between devices  14.8 us (2%)
    ppermute x8, waiting for transfers between devices, exchanged(): lax.ppermute(other, axis, pairs).astype(F32)  187 us
    all_gather x1, waiting for transfers between devices, shards(): lax.all_gather(matrix, ('section', 'group', 'dp'), axis=0, tiled=True)  95.4 us
    psum x1, blocking collectives, shards(): lax.psum(gain_grads, ('section', 'group', 'dp')).reshape(2, 2, D)  78.4 us
    pallas_call x2, Pallas kernels, attend_back(): pl.pallas_call(functools.partial(attend_back_kernel, chunk), grid_spec=pl...  77.8 us
    dot_general x10, matrix products, nt(): lax.dot_general(left, right, (((1,), (1,)), ((), ())), preferred_element_...  70.3 us
    pallas_call x2, Pallas kernels, attend(): pl.pallas_call(functools.partial(attend_kernel, chunk), grid_spec=pltpu.P...  66.2 us
    all_gather x2, waiting for transfers between devices, whole(): return lax.all_gather(part, ('section', 'dp', 'group'), axis=0, tiled=True)  57.6 us
    dot_general x20, matrix products, tn(): lax.dot_general(left, right, (((0,), (0,)), ((), ())), preferred_element_...  45.6 us
  transfers between devices with their start and end apart: 24, of which 11 were waited for; matrix products, arithmetic and copies ran while one was open for 20% of the time, Pallas kernels for 7%

profile of v2, /device:TPU:0, one launch (start us, length us, event | category | flops | bytes accessed | tf_op | source)
XLA Modules:
  0.0 899.7 jit_solution(3265269232827744991)
XLA Ops:
  14.9 5.0 multiply_reduce_fusion.5
  21.0 5.4 all_gather.28
  27.6 4.3 fusion.5
  33.8 95.4 %all-gather.15.cloned.1.call-done = bf16[1,8192,1024]{2,1,0:T(8,128)(2,1)} async-done(((bf16[1,256,1024]{2,1,0:T(8,128)(2,1)}), bf16[1,8192,1024]{2,1,0:T(8,128)(2,1)}) %all-gather.15.cloned.1.call-update) | async-done | bytes 16777232 | tf_op jit(solution)/shard_map/all_gather | solution.py:226
  129.3 3.3 fusion.74.q_ref
  132.6 6.3 convolution_convert_fusion.3.k_ref
  138.9 7.9 convolution_convert_fusion.2.v_ref
  146.8 42.5 %attend.2 = (bf16[512,1024]{1,0:T(8,128)(2,1)S(1)}, f32[2,8,2,256]{3,2,1,0:T(2,128)S(1)}) custom-call(s32[2,2]{1,0:T(2,128)S(1)} %get-tuple-element.82.first_ref, s32[2,2]{1,0:T(2,128)S(1)} %get-tuple-element.81.stop_ref, s32[2,1,256]{2,1,0:T(1,128)S(1)} %broadcast_in_dim.56.lo_ref, s32[2,1,256]{2,1,0:T(1,128)S(1)} %bitcast.209, ...), custom_call_target="tpu_custom_call" | custom-call | tf_op jit(solution)/shard_map/attend/pallas_call | solution.py:150
  194.7 23.6 %attend.3 = (bf16[512,1024]{1,0:T(8,128)(2,1)S(1)}, f32[2,8,2,256]{3,2,1,0:T(2,128)S(1)}) custom-call(s32[2,2]{1,0:T(2,128)S(1)} %get-tuple-element.80.first_ref, s32[2,2]{1,0:T(2,128)S(1)} %get-tuple-element.79.stop_ref, s32[2,1,256]{2,1,0:T(1,128)S(1)} %broadcast_in_dim.61.lo_ref, s32[2,1,256]{2,1,0:T(1,128)S(1)} %broadcast_in_dim_broadcast_in_dim.5.hi_ref, ...), custom_call_target="tpu_custom_call" | custom-call | tf_op jit(solution)/shard_map/attend/pallas_call | solution.py:150
  222.8 12.0 %fusion.152 = f32[512,5632]{1,0:T(8,128)} fusion(bf16[512,1024]{1,0:T(8,128)(2,1)} %multiply_convert_fusion.4, bf16[1024,5632]{1,0:T(8,128)(2,1)} %all-gather.9.cloned.1.call-done), kind=kOutput, calls=%fused_computation.271 | convolution fusion | flops 5905580032 | bytes 24117248 | tf_op jit(solution)/shard_map/dot_general | solution.py:29
  234.8 57.1 %all-gather.11.cloned.1.call-done = bf16[2816,1024]{1,0:T(8,128)(2,1)} async-done(((bf16[88,1024]{1,0:T(8,128)(2,1)}), bf16[2816,1024]{1,0:T(8,128)(2,1)}) %all-gather.11.cloned.1.call-update) | async-done | bytes 5767184 | tf_op jit(solution)/shard_map/all_gather | solution.py:222
  292.0 12.3 %multiply_convert_fusion.1 = (bf16[512,2816]{1,0:T(8,128)(2,1)}, bf16[512,2816]{1,0:T(8,128)(2,1)}, bf16[512,2816]{1,0:T(8,128)(2,1)}) fusion(f32[512,5632]{1,0:T(8,128)} %fusion.152, bf16[512,1024]{1,0:T(8,128)(2,1)} %bitcast.218, bf16[2816,1024]{1,0:T(8,128)(2,1)} %all-gather.11.cloned.1.call-done), kind=kOutput, calls=%fused_computation.32 | convolution fusion | flops 2975858688 | bytes 27000832 | tf_op jit(solution)/shard_map/dot_general | solution.py:37
  304.3 13.4 %multiply_reduce_fusion = (f32[1024]{0:T(1024)}, f32[512]{0:T(512)S(1)}, f32[512,1024]{1,0:T(8,128)}) fusion(f32[512,1024]{1,0:T(8,128)S(1)} %copy-done.38, f32[512]{0:T(512)S(1)} %get-tuple-element.62, f32[1024]{0:T(1024)S(1)} %bitcast.243, bf16[1024,5632]{1,0:T(8,128)(2,1)} %all-gather.9.cloned.1.call-done, bf16[512,2816]{1,0:T(8,128)(2,1)} %get-tuple-element.42, ...), kind=kOutput, calls=%fused_computation.79 | convolution fusion | flops 5920258560 | bytes 21508096 | tf_op jit(solution)/shard_map/dot_general | solution.py:37
  320.0 3.3 fusion.69.dc_ref
  323.3 26.4 %attend_back.2 = (bf16[512,1024]{1,0:T(8,128)(2,1)S(1)}, bf16[512,1024]{1,0:T(8,128)(2,1)S(1)}, bf16[512,1024]{1,0:T(8,128)(2,1)S(1)}) custom-call(s32[2,2]{1,0:T(2,128)S(1)} %get-tuple-element.80.first_ref, s32[2,2]{1,0:T(2,128)S(1)} %get-tuple-element.79.stop_ref, s32[2,1,256]{2,1,0:T(1,128)S(1)} %broadcast_in_dim.61.lo_ref, ...), custom_call_target="tpu_custom_call" | custom-call | tf_op jit(solution)/shard_map/attend_back/pallas_call | solution.py:173
  349.7 4.0 fusion.45
  356.7 3.5 fusion.30
  360.8 3.3 fusion.73.dc_ref
  365.5 51.4 %attend_back.3 = (bf16[512,1024]{1,0:T(8,128)(2,1)S(1)}, bf16[2048,1024]{1,0:T(8,128)(2,1)S(1)}, bf16[2048,1024]{1,0:T(8,128)(2,1)S(1)}) custom-call(s32[2,2]{1,0:T(2,128)S(1)} %get-tuple-element.82.first_ref, s32[2,2]{1,0:T(2,128)S(1)} %get-tuple-element.81.stop_ref, s32[2,1,256]{2,1,0:T(1,128)S(1)} %broadcast_in_dim.56.lo_ref, s32[2,1,256]{2,1,0:T(1,128)S(1)} %bitcast.210, ...), custom_call_target="tpu_custom_call" | custom-call | tf_op jit(solution)/shard_map/attend_back/pallas_call | solution.py:173
  416.9 10.0 %fusion.42 = f32[2048,1024]{1,0:T(8,128)} fusion(bf16[2048,1024]{1,0:T(8,128)(2,1)S(1)} %get-tuple-element.24, bf16[2,4,1024,1024]{3,2,1,0:T(8,128)(2,1)} %bitcast.277), kind=kOutput, calls=%fused_computation.108 | convolution fusion | flops 4294967296 | bytes 14680064 | tf_op jit(solution)/shard_map/dot_general | solution.py:37
  427.6 12.5 %fusion.12 = (f32[1024]{0:T(1024)S(1)}, f32[2048]{0:T(1024)S(1)}, bf16[2048,1024]{1,0:T(8,128)(2,1)}, f32[2048,1024]{1,0:T(8,128)}) fusion(f32[2048]{0:T(1024)S(1)} %bitcast.245, bf16[4,1024,1024]{2,1,0:T(8,128)(2,1)} %param.9, s32[]{:T(128)S(6)} %select_n.169, f32[1024]{0:T(1024)S(1)} %bitcast.240, f32[2048,1024]{1,0:T(8,128)} %fusion.42, ...), kind=kOutput, calls=%fused_computation.22 | convolution fusion | flops 4318032896 | bytes 31481860 | tf_op jit(solution)/shard_map/dot_general | solution.py:37
  440.2 4.7 fusion.75
  452.7 5.4 convolution_convert_fusion
  468.2 4.7 fusion.60
  475.3 3.4 fusion
  482.2 5.1 collective-permute-start.3
  492.6 3.8 fusion.1
  498.1 36.0 %collective-permute-done.3 = bf16[4,1024,256]{2,1,0:T(8,128)(2,1)} collective-permute-done((bf16[4,1024,256]{2,1,0:T(8,128)(2,1)}, bf16[4,1024,256]{2,1,0:T(8,128)(2,1)}, u32[]{:S(2)}, u32[]{:S(2)}) %collective-permute-start.3) | collective-permute-done | bytes 2097184 | tf_op jit(solution)/shard_map/ppermute | solution.py:286
  539.2 6.1 add_convert_fusion
  549.8 14.0 %collective-permute-done.4 = bf16[4,1024,128]{2,1,0:T(8,128)(2,1)} collective-permute-done((bf16[4,1024,128]{2,1,0:T(8,128)(2,1)}, bf16[4,1024,128]{2,1,0:T(8,128)(2,1)}, u32[]{:S(2)}, u32[]{:S(2)}) %collective-permute-start.4) | collective-permute-done | bytes 1048608 | tf_op jit(solution)/shard_map/ppermute | solution.py:286
  566.3 5.3 convolution_convert_fusion.1
  571.7 6.9 collective-permute-done.6
  583.3 62.8 %collective-permute-done.7 = bf16[4,1024,128]{2,1,0:T(8,128)(2,1)} collective-permute-done((bf16[4,1024,128]{2,1,0:T(8,128)(2,1)}, bf16[4,1024,128]{2,1,0:T(8,128)(2,1)}, u32[]{:S(2)}, u32[]{:S(2)}) %collective-permute-start.7) | collective-permute-done | bytes 1048608 | tf_op jit(solution)/shard_map/ppermute | solution.py:286
  648.7 3.5 add_convert_fusion.2
  655.0 3.6 add_convert_fusion.1
  661.0 27.4 %collective-permute-done.11 = bf16[512,1408]{1,0:T(8,128)(2,1)} collective-permute-done((bf16[512,1408]{1,0:T(8,128)(2,1)}, bf16[512,1408]{1,0:T(8,128)(2,1)}, u32[]{:S(2)}, u32[]{:S(2)}) %collective-permute-start.11) | collective-permute-done | bytes 1441824 | tf_op jit(solution)/shard_map/ppermute | solution.py:286
  691.6 24.8 %collective-permute-done.13 = bf16[2816,256]{1,0:T(8,128)(2,1)} collective-permute-done((bf16[2816,256]{1,0:T(8,128)(2,1)S(1)}, bf16[2816,256]{1,0:T(8,128)(2,1)}, u32[]{:S(2)}, u32[]{:S(2)}) %collective-permute-start.13) | collective-permute-done | bytes 1441824 | tf_op jit(solution)/shard_map/ppermute | solution.py:286
  720.1 15.2 %collective-permute-done.14 = bf16[1408,256]{1,0:T(8,128)(2,1)} collective-permute-done((bf16[1408,256]{1,0:T(8,128)(2,1)}, bf16[1408,256]{1,0:T(8,128)(2,1)}, u32[]{:S(2)}, u32[]{:S(2)}) %collective-permute-start.14) | collective-permute-done | bytes 720928 | tf_op jit(solution)/shard_map/ppermute | solution.py:286
  739.1 5.2 multiply_reduce_fusion.1
  751.5 5.0 fusion.2
  759.2 7.2 add_convert_fusion.9
  768.6 78.4 %psum.7 = f32[2,2,1024]{2,1,0:T(2,128)S(1)} all-reduce(f32[2,2,1024]{2,1,0:T(2,128)S(1)} %reshape.331), channel_id=1, replica_groups=mesh['section'=2,'group'=4,'dp'=4] {'section','group','dp'}, use_global_device_ids=true, to_apply=%region_18.19 | all-reduce | flops 4096 | bytes 32768 | tf_op jit(solution)/shard_map/psum | solution.py:373
  848.8 4.1 maximum_select_fusion
  852.9 9.5 %all-gather.2 = bf16[1408,256]{1,0:T(8,128)(2,1)S(1)} all-gather(bf16[352,256]{1,0:T(8,128)(2,1)} %reduce-scatter.11.cloned.1.call-done), channel_id=4, replica_groups=mesh['section'=2,'group'=4,'dp'=4] {'group'}, dimensions={0}, use_global_device_ids=true | all-gather | bytes 901120 | tf_op jit(solution)/shard_map/all_gather | solution.py:359
  869.9 4.1 copy.38
  874.1 5.8 broadcast_in_dim.62
  884.1 3.8 copy.40
  887.9 5.1 reshape.333
  (310 shorter events, 120.3 us)
Async XLA Ops:
  7.2 19.3 %copy-start = (bf16[4,256,1024]{2,1,0:T(8,128)(2,1)S(1)}, bf16[4,256,1024]{2,1,0:T(8,128)(2,1)}, u32[]{:S(2)}) copy-start(bf16[4,256,1024]{2,1,0:T(8,128)(2,1)} %param.17) | copy-start | bytes 6291460
  7.2 122.1 %all-gather.15.cloned.1.call-start = ((), (), s32[]{:S(2)}) async-start(), calls=%async_computation.11 | async-start | bytes 17301504 | tf_op jit(solution)/shard_map/all_gather | solution.py:226
  9.4 213.4 %all-gather.9.cloned.1.call-start = ((), (), s32[]{:S(2)}) async-start(), calls=%async_computation.4 | async-start | bytes 11894784 | tf_op jit(solution)/shard_map/all_gather | solution.py:222
  11.3 280.7 %all-gather.11.cloned.1.call-start = ((), (), s32[]{:S(2)}) async-start(), calls=%async_computation.5 | async-start | bytes 5947392 | tf_op jit(solution)/shard_map/all_gather | solution.py:222
  13.0 724.7 %reduce-scatter.5.cloned.1.call-start = ((), (), s32[]{:S(2)}) async-start(), calls=%async_computation.6 | async-start | bytes 1310720 | tf_op jit(solution)/shard_map/reduce_scatter | solution.py:303
  14.8 17.1 %copy-start.61 = (f32[1,2,2,128]{3,1,2,0:T(2,128)}, f32[1,2,2,128]{3,1,2,0:T(2,128)S(1)}, u32[]{:S(2)}) copy-start(f32[1,2,2,128]{3,1,2,0:T(2,128)S(1)} %copy.44) | copy-start | bytes 6148
  32.2 157.2 %copy-start.26 = (f32[512,1024]{1,0:T(8,128)}, f32[512,1024]{1,0:T(8,128)S(1)}, u32[]{:S(2)}) copy-start(f32[512,1024]{1,0:T(8,128)S(1)} %bitcast_divide_fusion) | copy-start | bytes 6291460
  138.9 50.5 %slice-start.5 = ((s8[16777216]{0:T(1024)(128)(4,1)}), s8[4194304]{0:T(1024)(128)(4,1)S(1)}, s32[]{:S(2)}) async-start(s8[16777216]{0:T(1024)(128)(4,1)} %bitcast.280), calls=%async_computation.18 | async-start | bytes 8388608
  138.9 50.5 %slice-start.6 = ((s8[16777216]{0:T(1024)(128)(4,1)}), s8[4194304]{0:T(1024)(128)(4,1)S(1)}, s32[]{:S(2)}) async-start(s8[16777216]{0:T(1024)(128)(4,1)} %bitcast.280), calls=%async_computation.19 | async-start | bytes 8388608
  138.9 50.5 %slice-start.7 = ((s8[16777216]{0:T(1024)(128)(4,1)}), s8[4194304]{0:T(1024)(128)(4,1)S(1)}, s32[]{:S(2)}) async-start(s8[16777216]{0:T(1024)(128)(4,1)} %bitcast.280), calls=%async_computation.20 | async-start | bytes 8388608
  146.8 42.6 %copy-start.4 = (bf16[2048,1024]{1,0:T(8,128)(2,1)}, bf16[2048,1024]{1,0:T(8,128)(2,1)S(1)}, u32[]{:S(2)}) copy-start(bf16[2048,1024]{1,0:T(8,128)(2,1)S(1)} %convolution_convert_fusion.2.v_ref) | copy-start | bytes 12582916
  146.8 42.6 %slice-start.8 = ((s8[16777216]{0:T(1024)(128)(4,1)}), s8[4194304]{0:T(1024)(128)(4,1)S(1)}, s32[]{:S(2)}) async-start(s8[16777216]{0:T(1024)(128)(4,1)} %bitcast.280), calls=%async_computation.21 | async-start | bytes 8388608
  190.8 27.6 %copy-start.51 = (bf16[512,1024]{1,0:T(8,128)(2,1)}, bf16[512,1024]{1,0:T(8,128)(2,1)S(1)}, u32[]{:S(2)}) copy-start(bf16[512,1024]{1,0:T(8,128)(2,1)S(1)} %get-tuple-element.72) | copy-start | bytes 3145732
  194.7 25.1 %copy-start.6 = (bf16[512,1024]{1,0:T(8,128)(2,1)}, bf16[512,1024]{1,0:T(8,128)(2,1)S(1)}, u32[]{:S(2)}) copy-start(bf16[512,1024]{1,0:T(8,128)(2,1)S(1)} %fusion.70.v_ref) | copy-start | bytes 3145732
  292.0 12.3 %copy-start.38 = (f32[512,1024]{1,0:T(8,128)S(1)}, f32[512,1024]{1,0:T(8,128)}, u32[]{:S(2)}) copy-start(f32[512,1024]{1,0:T(8,128)} %copy-done.37) | copy-start | bytes 6291460
  304.3 13.4 %copy-start.42 = (bf16[2,256,1024]{2,1,0:T(8,128)(2,1)S(1)}, bf16[2,256,1024]{2,1,0:T(8,128)(2,1)}, u32[]{:S(2)}) copy-start(bf16[2,256,1024]{2,1,0:T(8,128)(2,1)} %constant_dynamic-slice_fusion.11) | copy-start | bytes 3145732
  349.7 109.3 %copy-start.21 = (bf16[512,1024]{1,0:T(8,128)(2,1)}, bf16[512,1024]{1,0:T(8,128)(2,1)S(1)}, u32[]{:S(2)}) copy-start(bf16[512,1024]{1,0:T(8,128)(2,1)S(1)} %get-tuple-element.23) | copy-start | bytes 3145732
  349.7 110.5 %copy-start.19 = (bf16[512,1024]{1,0:T(8,128)(2,1)}, bf16[512,1024]{1,0:T(8,128)(2,1)S(1)}, u32[]{:S(2)}) copy-start(bf16[512,1024]{1,0:T(8,128)(2,1)S(1)} %get-tuple-element.22) | copy-start | bytes 3145732
  349.7 111.4 %copy-start.17 = (bf16[512,1024]{1,0:T(8,128)(2,1)}, bf16[512,1024]{1,0:T(8,128)(2,1)S(1)}, u32[]{:S(2)}) copy-start(bf16[512,1024]{1,0:T(8,128)(2,1)S(1)} %get-tuple-element.21) | copy-start | bytes 3145732
  360.8 66.1 %copy-start.40 = (bf16[512,1024]{1,0:T(8,128)(2,1)}, bf16[512,1024]{1,0:T(8,128)(2,1)S(1)}, u32[]{:S(2)}) copy-start(bf16[512,1024]{1,0:T(8,128)(2,1)S(1)} %fusion.27) | copy-start | bytes 3145732
  416.9 23.2 %copy-start.12 = (bf16[2048,1024]{1,0:T(8,128)(2,1)}, bf16[2048,1024]{1,0:T(8,128)(2,1)S(1)}, u32[]{:S(2)}) copy-start(bf16[2048,1024]{1,0:T(8,128)(2,1)S(1)} %get-tuple-element.25) | copy-start | bytes 12582916
  416.9 28.0 %copy-start.10 = (bf16[2048,1024]{1,0:T(8,128)(2,1)}, bf16[2048,1024]{1,0:T(8,128)(2,1)S(1)}, u32[]{:S(2)}) copy-start(bf16[2048,1024]{1,0:T(8,128)(2,1)S(1)} %get-tuple-element.24) | copy-start | bytes 12582916
  450.6 24.7 %collective-permute-start.2 = (bf16[4,1024,512]{2,1,0:T(8,128)(2,1)}, bf16[4,1024,512]{2,1,0:T(8,128)(2,1)}, u32[]{:S(2)}, u32[]{:S(2)}) collective-permute-start(bf16[4,1024,512]{2,1,0:T(8,128)(2,1)} %pad_maximum_fusion.2), channel_id=1, source_target_pairs={{0,4},{4,0},{8,12},{12,8},{1,5},{5,1},{9,13},{13,9},{2,6},{6,2},{1... | collective-permute-start | bytes 12582920 | tf_op jit(solution)/shard_map/ppermute | solution.py:295
  458.1 81.0 %collective-permute-start.9 = (bf16[1024,2816]{1,0:T(8,128)(2,1)}, bf16[1024,2816]{1,0:T(8,128)(2,1)}, u32[]{:S(2)}, u32[]{:S(2)}) collective-permute-start(bf16[1024,2816]{1,0:T(8,128)(2,1)} %convolution_convert_fusion), channel_id=1, source_target_pairs={{0,4},{4,0},{8,12},{12,8},{1,5},{5,1},{9,13},{13,9},{2,6},{6,2},{1... | collective-permute-start | bytes 17301512 | tf_op jit(solution)/shard_map/ppermute | solution.py:295
  464.3 28.3 %collective-permute-start.5 = (bf16[4,1024,512]{2,1,0:T(8,128)(2,1)}, bf16[4,1024,512]{2,1,0:T(8,128)(2,1)}, u32[]{:S(2)}, u32[]{:S(2)}) collective-permute-start(bf16[4,1024,512]{2,1,0:T(8,128)(2,1)} %pad_maximum_fusion.3), channel_id=1, source_target_pairs={{0,4},{4,0},{8,12},{12,8},{1,5},{5,1},{9,13},{13,9},{2,6},{6,2},{1... | collective-permute-start | bytes 12582920 | tf_op jit(solution)/shard_map/ppermute | solution.py:295
  482.2 51.9 %collective-permute-start.3 = (bf16[4,1024,256]{2,1,0:T(8,128)(2,1)}, bf16[4,1024,256]{2,1,0:T(8,128)(2,1)}, u32[]{:S(2)}, u32[]{:S(2)}) collective-permute-start(bf16[4,1024,256]{2,1,0:T(8,128)(2,1)} %constant_dynamic-slice_fusion.8), channel_id=1, source_target_pairs={{0,8},{4,12},{8,0},{12,4},{1,9},{5,13},{9,1},{13,5},{2,10},{6,14},... | collective-permute-start | bytes 6291464 | tf_op jit(solution)/shard_map/ppermute | solution.py:286
  496.4 39.8 %copy-start.32 = (bf16[4,1024,512]{2,1,0:T(8,128)(2,1)}, bf16[4,1024,512]{2,1,0:T(8,128)(2,1)S(1)}, u32[]{:S(2)}) copy-start(bf16[4,1024,512]{2,1,0:T(8,128)(2,1)S(1)} %fusion.1) | copy-start | bytes 12582916
  496.4 37.7 %copy-start.35 = (bf16[4,1024,512]{2,1,0:T(8,128)(2,1)S(1)}, bf16[4,1024,512]{2,1,0:T(8,128)(2,1)}, u32[]{:S(2)}) copy-start(bf16[4,1024,512]{2,1,0:T(8,128)(2,1)} %copy-done.34) | copy-start | bytes 12582916
  497.9 41.3 %copy-start.45 = (bf16[512,1024]{1,0:T(8,128)(2,1)S(1)}, bf16[512,1024]{1,0:T(8,128)(2,1)}, u32[]{:S(2)}) copy-start(bf16[512,1024]{1,0:T(8,128)(2,1)} %multiply_convert_fusion.4) | copy-start | bytes 3145732
  497.9 41.3 %copy-start.48 = (bf16[512,2816]{1,0:T(8,128)(2,1)S(1)}, bf16[512,2816]{1,0:T(8,128)(2,1)}, u32[]{:S(2)}) copy-start(bf16[512,2816]{1,0:T(8,128)(2,1)} %get-tuple-element.41) | copy-start | bytes 8650756
  497.9 41.3 %copy-start.50 = (bf16[512,2816]{1,0:T(8,128)(2,1)S(1)}, bf16[512,2816]{1,0:T(8,128)(2,1)}, u32[]{:S(2)}) copy-start(bf16[512,2816]{1,0:T(8,128)(2,1)} %get-tuple-element.42) | copy-start | bytes 8650756
  497.9 80.7 %collective-permute-start.6 = (bf16[4,1024,256]{2,1,0:T(8,128)(2,1)}, bf16[4,1024,256]{2,1,0:T(8,128)(2,1)}, u32[]{:S(2)}, u32[]{:S(2)}) collective-permute-start(bf16[4,1024,256]{2,1,0:T(8,128)(2,1)} %constant_dynamic-slice_fusion.6), channel_id=1, source_target_pairs={{0,8},{4,12},{8,0},{12,4},{1,9},{5,13},{9,1},{13,5},{2,10},{6,14},... | collective-permute-start | bytes 6291464 | tf_op jit(solution)/shard_map/ppermute | solution.py:286
  537.4 26.4 %collective-permute-start.4 = (bf16[4,1024,128]{2,1,0:T(8,128)(2,1)}, bf16[4,1024,128]{2,1,0:T(8,128)(2,1)}, u32[]{:S(2)}, u32[]{:S(2)}) collective-permute-start(bf16[4,1024,128]{2,1,0:T(8,128)(2,1)} %constant_dynamic-slice_fusion.7), channel_id=1, source_target_pairs={{0,16},{16,0},{1,17},{17,1},{2,18},{18,2},{3,19},{19,3},{4,20},{20... | collective-permute-start | bytes 3145736 | tf_op jit(solution)/shard_map/ppermute | solution.py:286
  549.6 99.1 %collective-permute-start.10 = (bf16[512,2816]{1,0:T(8,128)(2,1)}, bf16[512,2816]{1,0:T(8,128)(2,1)}, u32[]{:S(2)}, u32[]{:S(2)}) collective-permute-start(bf16[512,2816]{1,0:T(8,128)(2,1)} %constant_dynamic-slice_fusion.3), channel_id=1, source_target_pairs={{0,16},{16,0},{1,17},{17,1},{2,18},{18,2},{3,19},{19,3},{4,20},{20... | collective-permute-start | bytes 8650760 | tf_op jit(solution)/shard_map/ppermute | solution.py:286
  566.3 171.4 %reduce-scatter.7.cloned.1.call-start = ((), (), s32[]{:S(2)}) async-start(), calls=%async_computation.7 | async-start | bytes 1310720 | tf_op jit(solution)/shard_map/reduce_scatter | solution.py:303
  571.7 83.3 %collective-permute-start.12 = (bf16[2816,512]{1,0:T(8,128)(2,1)}, bf16[2816,512]{1,0:T(8,128)(2,1)}, u32[]{:S(2)}, u32[]{:S(2)}) collective-permute-start(bf16[2816,512]{1,0:T(8,128)(2,1)} %convolution_convert_fusion.1), channel_id=1, source_target_pairs={{0,4},{4,0},{8,12},{12,8},{1,5},{5,1},{9,13},{13,9},{2,6},{6,2},{1... | collective-permute-start | bytes 8650760 | tf_op jit(solution)/shard_map/ppermute | solution.py:295
  581.8 64.3 %collective-permute-start.7 = (bf16[4,1024,128]{2,1,0:T(8,128)(2,1)}, bf16[4,1024,128]{2,1,0:T(8,128)(2,1)}, u32[]{:S(2)}, u32[]{:S(2)}) collective-permute-start(bf16[4,1024,128]{2,1,0:T(8,128)(2,1)} %constant_dynamic-slice_fusion.5), channel_id=1, source_target_pairs={{0,16},{16,0},{1,17},{17,1},{2,18},{18,2},{3,19},{19,3},{4,20},{20... | collective-permute-start | bytes 3145736 | tf_op jit(solution)/shard_map/ppermute | solution.py:286
  648.7 110.5 %reduce-scatter.9.cloned.1.call-start = ((), (), s32[]{:S(2)}) async-start(), calls=%async_computation.9 | async-start | bytes 1802240 | tf_op jit(solution)/shard_map/reduce_scatter | solution.py:303
  653.5 34.8 %collective-permute-start.11 = (bf16[512,1408]{1,0:T(8,128)(2,1)}, bf16[512,1408]{1,0:T(8,128)(2,1)}, u32[]{:S(2)}, u32[]{:S(2)}) collective-permute-start(bf16[512,1408]{1,0:T(8,128)(2,1)} %constant_dynamic-slice_fusion.2), channel_id=1, source_target_pairs={{0,8},{4,12},{8,0},{12,4},{1,9},{5,13},{9,1},{13,5},{2,10},{6,14},... | collective-permute-start | bytes 4325384 | tf_op jit(solution)/shard_map/ppermute | solution.py:286
  660.2 56.3 %collective-permute-start.13 = (bf16[2816,256]{1,0:T(8,128)(2,1)S(1)}, bf16[2816,256]{1,0:T(8,128)(2,1)}, u32[]{:S(2)}, u32[]{:S(2)}) collective-permute-start(bf16[2816,256]{1,0:T(8,128)(2,1)S(1)} %constant_dynamic-slice_fusion.1), channel_id=1, source_target_pairs={{0,8},{4,12},{8,0},{12,4},{1,9},{5,13},{9,1},{13,5},{2,10},{6,14},... | collective-permute-start | bytes 4325384 | tf_op jit(solution)/shard_map/ppermute | solution.py:286
  691.6 161.3 %reduce-scatter.11.cloned.1.call-start = ((), (), s32[]{:S(2)}) async-start(), calls=%async_computation.10 | async-start | bytes 901120 | tf_op jit(solution)/shard_map/reduce_scatter | solution.py:303
  718.6 19.1 %copy-start.58 = (f32[1,8,2,128]{3,2,1,0:T(2,128)S(1)}, f32[1,8,2,128]{3,2,1,0:T(2,128)}, u32[]{:S(2)}) copy-start(f32[1,8,2,128]{3,2,1,0:T(2,128)} %copy-done.57) | copy-start | bytes 24580
  719.5 15.7 %collective-permute-start.14 = (bf16[1408,256]{1,0:T(8,128)(2,1)}, bf16[1408,256]{1,0:T(8,128)(2,1)}, u32[]{:S(2)}, u32[]{:S(2)}) collective-permute-start(bf16[1408,256]{1,0:T(8,128)(2,1)} %constant_dynamic-slice_fusion), channel_id=1, source_target_pairs={{0,16},{16,0},{1,17},{17,1},{2,18},{18,2},{3,19},{19,3},{4,20},{20... | collective-permute-start | bytes 2162696 | tf_op jit(solution)/shard_map/ppermute | solution.py:286
  737.4 128.5 %all-gather.13.cloned.1.call-start = ((), (), s32[]{:S(2)}) async-start(), calls=%async_computation.8 | async-start | bytes 2621440 | tf_op jit(solution)/shard_map/all_gather | solution.py:359
  738.8 6.4 collective-permute-start.8
  746.2 136.3 %all-gather.17.cloned.1.call-start = ((), (), s32[]{:S(2)}) async-start(), calls=%async_computation.12 | async-start | bytes 1802240 | tf_op jit(solution)/shard_map/all_gather | solution.py:359
  758.3 90.4 %collective-permute-start.1 = (bf16[2,1024,512]{2,1,0:T(8,128)(2,1)}, bf16[2,1024,512]{2,1,0:T(8,128)(2,1)}, u32[]{:S(2)}, u32[]{:S(2)}) collective-permute-start(bf16[2,1024,512]{2,1,0:T(8,128)(2,1)} %get-tuple-element.46), channel_id=1, source_target_pairs={{0,16},{16,0},{1,17},{17,1},{2,18},{18,2},{3,19},{19,3},{4,20},{20... | collective-permute-start | bytes 6291464 | tf_op jit(solution)/shard_map/ppermute | solution.py:350
  767.4 80.3 %collective-permute-start = (bf16[2,256,512]{2,1,0:T(8,128)(2,1)}, bf16[2,256,512]{2,1,0:T(8,128)(2,1)S(1)}, u32[]{:S(2)}, u32[]{:S(2)}) collective-permute-start(bf16[2,256,512]{2,1,0:T(8,128)(2,1)} %get-tuple-element.48), channel_id=1, source_target_pairs={{0,16},{16,0},{1,17},{17,1},{2,18},{18,2},{3,19},{19,3},{4,20},{20... | collective-permute-start | bytes 1572872 | tf_op jit(solution)/shard_map/ppermute | solution.py:350
  (55 other events, 236.2 us)
Sparse Core Ops, SparseCore 0:
  11.6 117.6 all-gather.14
  132.7 90.0 all-gather.8
  226.3 65.6 all-gather.10
  566.4 26.7 reduce-scatter.4
  648.8 26.4 reduce-scatter.6
  691.7 32.5 reduce-scatter.8
  737.5 21.7 reduce-scatter.10
  760.8 21.9 all-gather.12
  784.4 18.9 all-gather.16

commit v3 on v2

--- a/solution.py
+++ b/solution.py
@@ -11,6 +11,7 @@
 HEADS = 16
 HEAD_DIM = 64
 PAIRS = HEADS // 2
+BLOCK = 512
 FF = 2816
 ROW_BYTES = 1024
 PATCHES = 256
@@ -142,6 +143,13 @@
     return per_query, per_key, bound, logs
 
 
+def kernel_cost(q, k, products):
+    scores = q.shape[0] * k.shape[0] // (q.shape[0] // PATCHES) * HEADS
+    return pl.CostEstimate(
+        flops=products * 2 * scores * 256, bytes_accessed=2 * q.nbytes + 4 * k.nbytes, transcendentals=scores
+    )
+
+
 def attend(bounds, q, k, v):
     first, stop, lo, hi, chunk = bounds
     rows = lo.shape[0]
@@ -161,6 +169,7 @@
             jax.ShapeDtypeStruct((rows, PAIRS, TILES, 2 * QT), F32),
         ],
         compiler_params=pltpu.CompilerParams(vmem_limit_bytes=32 << 20),
+        cost_estimate=kernel_cost(q, k, 2),
         name="attend",
     )(first, stop, lo, hi, q, k, v)
 
@@ -185,6 +194,7 @@
             jax.ShapeDtypeStruct(k.shape, BF),
         ],
         compiler_params=pltpu.CompilerParams(vmem_limit_bytes=32 << 20),
+        cost_estimate=kernel_cost(q, k, 5),
         name="attend_back",
     )(first, stop, lo, hi, q, k, v, logsum, context, grads)
 
@@ -216,17 +226,22 @@
     groups = lax.axis_size("group")
     core, side = group % 2, group // 2
 
-    def whole(shard):
-        rows = shard.shape[0] // groups
-        part = lax.dynamic_slice_in_dim(shard, group * rows, rows, 0)
-        return lax.all_gather(part, ("section", "dp", "group"), axis=0, tiled=True)
-
     four = jnp.concatenate([attn_qkv[0], attn_out], axis=0)
     matrix = lax.dynamic_index_in_dim(four, group, 0, keepdims=False)
     matrices = lax.all_gather(matrix, ("section", "group", "dp"), axis=0, tiled=True)
     matrices = matrices.reshape(sections, groups, D, D)
     wq, wk, wv, wo = [matrices[:, index] for index in range(4)]
-    w_in, w_down = whole(ffn_in), whole(ffn_down)
+    blocks = []
+    for shard in (ffn_in, ffn_down):
+        height = shard.shape[0] // groups
+        part = lax.dynamic_slice_in_dim(shard, group * height, height, 0)
+        blocks += [part[:, at : at + BLOCK] for at in range(0, part.shape[1], BLOCK)]
+    ffn = lax.all_gather(jnp.concatenate(blocks, axis=0), ("section", "dp", "group"), axis=0, tiled=False)
+    in_rows = ffn_in.size // groups // BLOCK
+    w_in, w_down = [
+        part.reshape(part.shape[0], width // BLOCK, -1, BLOCK).swapaxes(1, 2).reshape(-1, width)
+        for part, width in ((ffn[:, :in_rows], 2 * FF), (ffn[:, in_rows:], D))
+    ]
     gains = lax.all_gather(norm_gains, "section", axis=0, tiled=True)
 
     rows = byte_states.shape[0] // sections
@@ -279,6 +294,10 @@
     grad_up = grad_hidden * gate * sig
     dgu = jnp.concatenate([grad_gate, grad_up], axis=1).astype(BF)
 
+    core_pairs = [(0, 1), (1, 0), (2, 3), (3, 2)]
+    side_pairs = [(0, 2), (1, 3), (2, 0), (3, 1)]
+    swap = [(0, 1), (1, 0)]
+
     def exchanged(values, axis, part, pairs, where):
         size = values.shape[where] // 2
         other = lax.dynamic_slice_in_dim(values, (1 - part) * size, size, where)
@@ -286,14 +305,10 @@
         return (own.astype(F32) + lax.ppermute(other, axis, pairs).astype(F32)).astype(BF)
 
     def over_section(values, where):
-        return exchanged(values, "section", section, [(0, 1), (1, 0)], where)
+        return exchanged(values, "section", section, swap, where)
 
     def over_side(values, where):
-        return exchanged(values, "group", side, [(0, 2), (1, 3), (2, 0), (3, 1)], where)
-
-    def chip_sum(half_of):
-        got = lax.ppermute(half_of(1 - core).astype(BF), "group", [(0, 1), (1, 0), (2, 3), (3, 2)])
-        return (half_of(core) + got.astype(F32)).astype(BF)
+        return exchanged(values, "group", side, side_pairs, where)
 
     def columns(values, part):
         size = values.shape[-1] // 2
@@ -302,34 +317,57 @@
     def line_sum(values, where):
         return lax.psum_scatter(values, "dp", scatter_dimension=where, tiled=True)
 
-    sum_in = chip_sum(lambda part: tn(mix_in, columns(dgu, part)))
-    sum_in = line_sum(over_side(over_section(sum_in, 0), 1), 0)
-    sum_down = chip_sum(lambda part: tn(hidden, columns(cot, part)))
-    sum_down = line_sum(over_section(over_side(sum_down, 1), 0), 0)
-
-    grad_mix, gain_mix = norm_backward(residual, second_scale, gains[1, 1], nt(dgu, w_in))
+    def products(pairs, part):
+        out = [tn(left, columns(right, part)) for left, right in pairs]
+        return out[0] if len(out) == 1 else jnp.stack(out)
+
+    def to_core(pairs):
+        return products(pairs, 1 - core).astype(BF)
+
+    def of_chip(pairs, sent):
+        got = lax.ppermute(sent, "group", core_pairs)
+        return (products(pairs, core) + got.astype(F32)).astype(BF)
+
+    together = lax.optimization_barrier
+
+    in_pairs, down_pairs = [(mix_in, dgu)], [(hidden, cot)]
+    send_in, send_down = to_core(in_pairs), to_core(down_pairs)
+    dgu_next, send_in, send_down = together((dgu, send_in, send_down))
+    grad_mix, gain_mix = norm_backward(residual, second_scale, gains[1, 1], nt(dgu_next, w_in))
     grad_residual = grad_mix + cot.astype(F32)
     branch = grad_residual.astype(BF)
-
     dc2 = nt(branch, wo[1]).astype(BF)
+    half_in, half_down = of_chip(in_pairs, send_in), of_chip(down_pairs, send_down)
+    dc2, half_in, half_down = together((dc2, half_in, half_down))
+
     dq2, dk2, dv2 = attend_back(causal, q2, k2, v2, l2, c2, dc2)
-
-    def four_sums(pairs):
-        def half_of(part):
-            return jnp.stack([tn(left, columns(right, part)) for left, right in pairs])
-
-        return chip_sum(half_of)
-
-    sums_two = four_sums([(normed_in, dq2), (normed_in, dk2), (normed_in, dv2), (c2, branch)])
-    sums_two = line_sum(over_section(over_side(sums_two, 2), 2), 1)
+    two_pairs = [(normed_in, dq2), (normed_in, dk2), (normed_in, dv2), (c2, branch)]
+    send_two = to_core(two_pairs)
+    dq2, dk2, dv2, send_two = together((dq2, dk2, dv2, send_two))
     grad_normed = nt(dq2, wq[1]) + nt(dk2, wk[1]) + nt(dv2, wv[1])
     grad_carried, gain_normed = norm_backward(carried_wide, first_scale, gains[1, 0], grad_normed)
     d_carried = (grad_residual + grad_carried).astype(BF)
-
     dc1 = nt(d_carried, wo[0]).astype(BF)
+    half_in = over_section(half_in, 0)
+    half_two = of_chip(two_pairs, send_two)
+    dc1, half_in, half_two = together((dc1, half_in, half_two))
+    sum_down = over_side(over_section(line_sum(half_down.reshape(sections, -1, D // 2), 1), 0), 2)
+    sum_down = sum_down[0]
+
     dq1, dk1, dv1 = attend_back(cross, q1, k1, v1, l1, c1, dc1)
-    sums_one = four_sums([(query_in, dq1), (key_in, dk1), (key_in, dv1), (c1, d_carried)])
-    sums_one = line_sum(over_section(over_side(sums_one, 2), 2), 1)
+    half_in = over_side(half_in, 1)
+    half_two = over_side(half_two, 2)
+    one_pairs = [(query_in, dq1), (key_in, dk1)], [(key_in, dv1), (c1, d_carried)]
+    send_one = [to_core(pairs) for pairs in one_pairs]
+    dq1, dk1, dv1, send_one, half_in, half_two = together((dq1, dk1, dv1, send_one, half_in, half_two))
+    sum_in = line_sum(half_in, 0)
+    sum_two = line_sum(over_section(half_two, 2), 1)
+    half_one = [of_chip(pairs, sent) for pairs, sent in zip(one_pairs, send_one)]
+    dq1, dk1, dv1, half_one = together((dq1, dk1, dv1, half_one))
+    half_one = jnp.concatenate(
+        [over_side(over_section(half_one[0], 2), 2), over_section(over_side(half_one[1], 2), 2)], axis=0
+    )
+    sum_one = line_sum(half_one, 1)
     grad_pooled, gain_query = norm_backward(pooled, query_scale, gains[0, 0], nt(dq1, wq[0]))
     grad_wide, gain_key = norm_backward(
         wide, key_scale, gains[0, 1], nt(dk1, wk[0]) + nt(dv1, wv[0])
@@ -341,7 +379,6 @@
     byte_grads = (grad_wide + spread_back.reshape(rows * ROW_BYTES, D)).astype(BF)
 
     half = D // sections
-    swap = [(0, 1), (1, 0)]
 
     def halves(values, length):
         values = values.reshape(rows, length, D)
@@ -355,26 +392,36 @@
     latents_out = halves(latents, PATCHES)
     bytes_out = halves(byte_grads, ROW_BYTES)
 
-    def to_group(part):
+    def of_group(part):
         every = lax.all_gather(part, "group", axis=0, tiled=False)
-        every = every.reshape((2, 2) + part.shape)
-        every = jnp.moveaxis(every, (1, 0), (-3, -2))
-        return every.reshape(part.shape[:-1] + (-1,)).astype(F32)
-
-    ffn_gin, ffn_gdown = to_group(sum_in), to_group(sum_down)
-    kept = jnp.where(section == 0, sums_one, sums_two)
-    sent = jnp.where(section == 0, sums_two, sums_one)
+        return [every[index] for index in range(groups)]
+
+    def laid_out(parts, order):
+        return jnp.concatenate([parts[index] for index in order], axis=-1).astype(F32)
+
+    ffn_gin, ffn_gdown = [laid_out(of_group(part), (0, 2, 1, 3)) for part in (sum_in, sum_down)]
+
+    kept = jnp.where(section == 0, sum_one, sum_two)
+    sent = jnp.where(section == 0, sum_two, sum_one)
     got = lax.ppermute(sent, "section", swap)
-    quarter = jnp.where(
+    eighths = jnp.where(
         section == 0, jnp.concatenate([kept, got], axis=2), jnp.concatenate([got, kept], axis=2)
     )
-    attn = to_group(quarter)
+    width = eighths.shape[2] // 2
+    parts = [piece for every in of_group(eighths) for piece in (every[..., :width], every[..., width:])]
+    side_first = laid_out(parts, (0, 1, 4, 5, 2, 3, 6, 7))
+    section_first = laid_out([part[:2] for part in parts], (0, 4, 1, 5, 2, 6, 3, 7))
+    leading = jnp.where(section == 0, section_first, side_first[:2])
+    grad_qkv = jnp.concatenate([leading, side_first[2:3]], axis=0)[None]
+
     gain_grads = jnp.stack([gain_query, gain_key, gain_normed, gain_mix])
-    gain_grads = lax.psum(gain_grads, ("section", "group", "dp")).reshape(2, 2, D)
-    gain_grads = lax.dynamic_slice_in_dim(gain_grads, section, 1, 0)
+    for axis, pairs in (("group", core_pairs), ("group", side_pairs), ("section", swap)):
+        gain_grads = gain_grads + lax.ppermute(gain_grads, axis, pairs)
+    gain_grads = jnp.sum(lax.all_gather(gain_grads, "dp", axis=0, tiled=False), axis=0)
+    gain_grads = lax.dynamic_slice_in_dim(gain_grads.reshape(2, 2, D), section, 1, 0)
     width = D // lax.axis_size("dp")
     gain_out = lax.dynamic_slice_in_dim(gain_grads, lax.axis_index("dp") * width, width, 2)
-    return (latents_out, bytes_out, attn[None, :3], attn[3][None], gain_out, ffn_gin, ffn_gdown)
+    return (latents_out, bytes_out, grad_qkv, side_first[3:], gain_out, ffn_gin, ffn_gdown)
 
 
 def solution(mesh):

time: 904 us -> 819 us (0.906)
  waiting for transfers between devices: 341 us -> 267 us
  blocking collectives: 93.3 us -> 26.8 us
  local copies, waits for them, and re-layouts: 59.8 us -> 109 us
  other arithmetic: 65.6 us -> 75.5 us
    ppermute x8 -> x10, waiting for transfers between devices: 187 us -> 101 us  [exchanged(): lax.ppermute(other, axis, pairs).astype(F32)]
    psum x1 -> x0, blocking collectives: 78.4 us -> none  [shards(): lax.psum(gain_grads, ('section', 'group', 'dp')).reshape(2, 2, D)]
    ppermute x1, waiting for transfers between devices: 0.93 us -> 45.7 us  [shards(): got = lax.ppermute(sent, 'section', swap)]
    transpose x0 -> x2, local copies, waits for them, and re-layouts: none -> 39.4 us  [shards(): part.reshape(part.shape[0], width // BLOCK, -1, BLOCK).swapaxes(1, 2)]
    all_gather x4 -> x3, waiting for transfers between devices: 57.6 us -> 27.8 us  [the longest x1 27.8 us: shards(): lax.all_gather(jnp.concatenate(blocks, axis=0), ('section', 'dp', 'group'...]
    unnamed x160 -> x211, local copies, waits for them, and re-layouts: 17 us -> 45.8 us
    dot_general x10, matrix products: 70.3 us -> 55.5 us  [nt(): lax.dot_general(left, right, (((1,), (1,)), ((), ())), preferred_element_...]
    convert_element_type x4 -> x0, local copies, waits for them, and re-layouts: 12.2 us -> none  [to_group(): return every.reshape(part.shape[:-1] + (-1,)).astype(F32)]
  transfers between devices with their start and end apart: 24 -> 29, of which waited for: 11 -> 12; matrix products, arithmetic and copies ran while one was open for 20% -> 27% of each run, Pallas kernels for 7% -> 18%
where the time goes in v3:
time: 819 us; the launch traced here: 814 us
  waiting for transfers between devices  267 us (33%)
  matrix products  159 us (19%)
  Pallas kernels  144 us (18%)
  local copies, waits for them, and re-layouts  109 us (13%)
  other arithmetic  75.5 us (9%)
  blocking collectives  26.8 us (3%)
  starting transfers between devices  17.3 us (2%)
  between operations  15.9 us (2%)
    ppermute x10, waiting for transfers between devices, exchanged(): lax.ppermute(other, axis, pairs).astype(F32)  101 us
    all_gather x1, waiting for transfers between devices, shards(): lax.all_gather(matrix, ('section', 'group', 'dp'), axis=0, tiled=True)  87.6 us
    pallas_call x2, Pallas kernels, attend_back(): pl.pallas_call(functools.partial(attend_back_kernel, chunk), grid_spec=pl...  77.5 us
    pallas_call x2, Pallas kernels, attend(): pl.pallas_call(functools.partial(attend_kernel, chunk), grid_spec=pltpu.P...  66.7 us
    dot_general x20, matrix products, tn(): lax.dot_general(left, right, (((0,), (0,)), ((), ())), preferred_element_...  57.4 us
    dot_general x10, matrix products, nt(): lax.dot_general(left, right, (((1,), (1,)), ((), ())), preferred_element_...  55.5 us
    unnamed x211, local copies, waits for them, and re-layouts  45.8 us
    ppermute x1, waiting for transfers between devices, shards(): got = lax.ppermute(sent, 'section', swap)  45.7 us
  transfers between devices with their start and end apart: 29, of which 12 were waited for; matrix products, arithmetic and copies ran while one was open for 27% of the time, Pallas kernels for 18%

profile of v3, /device:TPU:0, one launch (start us, length us, event | category | flops | bytes accessed | tf_op | source)
XLA Modules:
  0.0 813.7 jit_solution(16358003359935105296)
XLA Ops:
  22.5 5.4 all_gather.31
  28.9 3.1 fusion.2
  32.1 3.8 multiply_reduce_fusion.5
  41.6 87.6 %all-gather.12.cloned.1.call-done = bf16[1,8192,1024]{2,1,0:T(8,128)(2,1)} async-done(((bf16[1,256,1024]{2,1,0:T(8,128)(2,1)}), bf16[1,8192,1024]{2,1,0:T(8,128)(2,1)}) %all-gather.12.cloned.1.call-update) | async-done | bytes 16777232 | tf_op jit(solution)/shard_map/all_gather | solution.py:231
  132.3 7.4 convolution_convert_fusion.2.v_ref
  139.8 4.7 convolution_convert_fusion.3.k_ref
  144.6 42.5 %attend.2 = (bf16[512,1024]{1,0:T(8,128)(2,1)S(1)}, f32[2,8,2,256]{3,2,1,0:T(2,128)S(1)}) custom-call(s32[2,2]{1,0:T(2,128)S(1)} %get-tuple-element.145.first_ref, s32[2,2]{1,0:T(2,128)S(1)} %get-tuple-element.144.stop_ref, s32[2,1,256]{2,1,0:T(1,128)S(1)} %broadcast_in_dim.56.lo_ref, s32[2,1,256]{2,1,0:T(1,128)S(1)} %bitcast.232, ...), custom_call_target="tpu_custom_call" | custom-call | flops 8589934592 | bytes 18874368 | tf_op jit(solution)/shard_map/attend/pallas_call | solution.py:158
  193.1 24.2 %attend.3 = (bf16[512,1024]{1,0:T(8,128)(2,1)S(1)}, f32[2,8,2,256]{3,2,1,0:T(2,128)S(1)}) custom-call(s32[2,2]{1,0:T(2,128)S(1)} %get-tuple-element.143.first_ref, s32[2,2]{1,0:T(2,128)S(1)} %get-tuple-element.142.stop_ref, s32[2,1,256]{2,1,0:T(1,128)S(1)} %broadcast_in_dim.61.lo_ref, s32[2,1,256]{2,1,0:T(1,128)S(1)} %broadcast_in_dim_broadcast_in_dim.5.hi_ref, ...), custom_call_target="tpu_custom_call" | custom-call | flops 2147483648 | bytes 6291456 | tf_op jit(solution)/shard_map/attend/pallas_call | solution.py:158
  221.2 27.8 %all-gather.14.cloned.1.call-done = bf16[16896,512]{1,0:T(8,128)(2,1)} async-done(((bf16[528,512]{1,0:T(8,128)(2,1)}), bf16[16896,512]{1,0:T(8,128)(2,1)}) %all-gather.14.cloned.1.call-update) | async-done | bytes 17301520 | tf_op jit(solution)/shard_map/all_gather | solution.py:239
  249.0 3.0 slice.307
  252.0 6.1 slice.304
  258.1 7.1 copy.34
  265.2 4.5 copy.39
  269.7 32.3 %copy.33 = bf16[32,32,11,512]{3,2,1,0:T(8,128)(2,1)S(1)} copy(bf16[32,32,11,512]{3,1,2,0:T(8,128)(2,1)S(1)} %bitcast.235) | data formatting | bytes 23068672 | tf_op jit(solution)/shard_map/transpose | solution.py:242
  302.0 21.3 %copy.38 = bf16[128,8,11,512]{3,1,2,0:T(8,128)(2,1)S(1)} copy(bf16[128,8,11,512]{3,2,1,0:T(8,128)(2,1)S(1)} %bitcast.234) | data formatting | bytes 23068672
  323.3 8.9 %fusion.153 = f32[512,5632]{1,0:T(8,128)} fusion(bf16[512,1024]{1,0:T(8,128)(2,1)S(1)} %copy-done.51, bf16[1024,5632]{1,0:T(8,128)(2,1)S(1)} %bitcast.245), kind=kOutput, calls=%fused_computation.311 | convolution fusion | flops 5905580032 | bytes 24117248 | tf_op jit(solution)/shard_map/dot_general | solution.py:30
  332.2 9.4 %multiply_convert_fusion.1 = (bf16[512,2816]{1,0:T(8,128)(2,1)S(1)}, bf16[512,2816]{1,0:T(8,128)(2,1)S(1)}, bf16[512,2816]{1,0:T(8,128)(2,1)}) fusion(f32[512,5632]{1,0:T(8,128)} %fusion.153, bf16[512,1024]{1,0:T(8,128)(2,1)S(1)} %bitcast.253, bf16[2816,1024]{1,0:T(8,128)(2,1)S(1)} %bitcast.249), kind=kOutput, calls=%fused_computation.29 | convolution fusion | flops 2975858688 | bytes 27000832 | tf_op jit(solution)/shard_map/dot_general | solution.py:38
  345.9 5.4 convolution_convert_fusion
  351.2 3.3 convolution_convert_fusion.1
  355.4 4.4 fusion.6
  359.9 6.8 add_convert_fusion.8
  368.9 9.3 %multiply_reduce_fusion = (f32[1024]{0:T(1024)}, f32[512]{0:T(512)S(1)}, f32[512,1024]{1,0:T(8,128)S(1)}) fusion(f32[512,1024]{1,0:T(8,128)S(1)} %copy-done.42, f32[512]{0:T(512)S(1)} %get-tuple-element.125, f32[1024]{0:T(1024)S(1)} %bitcast.280, bf16[512,5632]{1,0:T(8,128)(2,1)} %pad_maximum_fusion, bf16[1024,5632]{1,0:T(8,128)(2,1)S(1)} %bitcast.248), kind=kOutput, calls=%fused_computation.80 | convolution fusion | flops 5908724224 | bytes 21508096 | tf_op jit(solution)/shard_map/dot_general | solution.py:38
  384.0 4.0 fusion.69.dc_ref
  388.0 5.3 add_convert_fusion.2
  393.3 7.6 add_convert_fusion
  403.5 26.0 %attend_back.2 = (bf16[512,1024]{1,0:T(8,128)(2,1)S(1)}, bf16[512,1024]{1,0:T(8,128)(2,1)S(1)}, bf16[512,1024]{1,0:T(8,128)(2,1)S(1)}) custom-call(s32[2,2]{1,0:T(2,128)S(1)} %get-tuple-element.143.first_ref, s32[2,2]{1,0:T(2,128)S(1)} %get-tuple-element.142.stop_ref, s32[2,1,256]{2,1,0:T(1,128)S(1)} %broadcast_in_dim.61.lo_ref, ...), custom_call_target="tpu_custom_call" | custom-call | flops 5368709120 | bytes 6291456 | tf_op jit(solution)/shard_map/attend_back/pallas_call | solution.py:182
  441.0 3.6 fusion.30
  455.6 43.2 %collective-permute-done.3 = bf16[512,2816]{1,0:T(8,128)(2,1)S(1)} collective-permute-done((bf16[512,2816]{1,0:T(8,128)(2,1)S(1)}, bf16[512,2816]{1,0:T(8,128)(2,1)S(1)}, u32[]{:S(2)}, u32[]{:S(2)}) %collective-permute-start.3) | collective-permute-done | bytes 2883616 | tf_op jit(solution)/shard_map/ppermute | solution.py:305
  499.5 4.4 fusion
  509.1 51.6 %attend_back.3 = (bf16[512,1024]{1,0:T(8,128)(2,1)S(1)}, bf16[2048,1024]{1,0:T(8,128)(2,1)S(1)}, bf16[2048,1024]{1,0:T(8,128)(2,1)S(1)}) custom-call(s32[2,2]{1,0:T(2,128)S(1)} %copy-done.13, s32[2,2]{1,0:T(2,128)S(1)} %copy-done.11, s32[2,1,256]{2,1,0:T(1,128)S(1)} %copy-done.7, s32[2,1,256]{2,1,0:T(1,128)S(1)} %bitcast.233, ...), custom_call_target="tpu_custom_call" | custom-call | flops 21474836480 | bytes 18874368 | tf_op jit(solution)/shard_map/attend_back/pallas_call | solution.py:182
  572.3 11.1 %collective-permute-done.6 = bf16[4,1024,256]{2,1,0:T(8,128)(2,1)} collective-permute-done((bf16[4,1024,256]{2,1,0:T(8,128)(2,1)}, bf16[4,1024,256]{2,1,0:T(8,128)(2,1)}, u32[]{:S(2)}, u32[]{:S(2)}) %collective-permute-start.6) | collective-permute-done | bytes 2097184 | tf_op jit(solution)/shard_map/ppermute | solution.py:305
  583.4 4.0 add_convert_fusion.3
  593.3 5.9 fusion.57
  603.0 6.7 fusion.60
  613.4 20.0 %collective-permute-done.14 = bf16[4,1024,128]{2,1,0:T(8,128)(2,1)S(1)} collective-permute-done((bf16[4,1024,128]{2,1,0:T(8,128)(2,1)S(1)}, bf16[4,1024,128]{2,1,0:T(8,128)(2,1)S(1)}, u32[]{:S(2)}, u32[]{:S(2)}) %collective-permute-start.14) | collective-permute-done | bytes 1048608 | tf_op jit(solution)/shard_map/ppermute | solution.py:305
  635.0 3.7 fusion.12
  641.6 3.2 multiply_reduce_fusion.1
  648.2 20.7 %collective-permute-done.12 = bf16[2,1024,256]{2,1,0:T(8,128)(2,1)S(1)} collective-permute-done((bf16[2,1024,256]{2,1,0:T(8,128)(2,1)S(1)}, bf16[2,1024,256]{2,1,0:T(8,128)(2,1)S(1)}, u32[]{:S(2)}, u32[]{:S(2)}) %collective-permute-start.12) | collective-permute-done | bytes 1048608 | tf_op jit(solution)/shard_map/ppermute | solution.py:305
  672.1 4.6 fusion.53
  676.7 4.5 collective-permute-done.13
  683.7 7.1 fusion.42
  690.9 10.3 %fusion.11 = (f32[1024]{0:T(1024)S(1)}, f32[2048]{0:T(1024)S(1)}, f32[2048,1024]{1,0:T(8,128)}) fusion(f32[2048]{0:T(1024)S(1)} %bitcast.268, bf16[4,1024,1024]{2,1,0:T(8,128)(2,1)} %param.9, s32[]{:T(128)S(6)} %select_n.187, f32[1024]{0:T(1024)S(1)} %bitcast.272, f32[2048,1024]{1,0:T(8,128)S(1)} %fusion.42, bf16[2048,1024]{1,0:T(8,128)(2,1)S(1)} %copy-done.4, ...), kind=kOutput, calls=%fused_computation.20 | convolution fusion | flops 4311741440 | bytes 27287556 | tf_op jit(solution)/shard_map/dot_general | solution.py:38
  701.6 8.3 %fusion.1 = bf16[2048,1024]{1,0:T(8,128)(2,1)S(1)} fusion(f32[2,1024,1024]{2,1,0:T(8,128)} %fusion.53, f32[2048,1024]{1,0:T(8,128)} %get-tuple-element.141, f32[2048]{0:T(1024)S(1)} %broadcast_multiply_fusion, f32[2048]{0:T(1024)S(1)} %copy-done.69, f32[1024]{0:T(1024)S(1)} %bitcast.273, f32[2048]{0:T(1024)S(1)} %bitcast.269, ...), kind=kLoop, calls=%fused_computation.4 | loop fusion | flops 16777216 | bytes 25194500 | tf_op jit(solution)/shard_map/convert_element_type | solution.py:379
  716.0 45.7 %collective-permute-done.15 = bf16[4,256,128]{2,1,0:T(8,128)(2,1)S(1)} collective-permute-done((bf16[4,256,128]{2,1,0:T(8,128)(2,1)S(1)}, bf16[4,256,128]{2,1,0:T(8,128)(2,1)S(1)}, u32[]{:S(2)}, u32[]{:S(2)}) %collective-permute-start.15) | collective-permute-done | bytes 262176 | tf_op jit(solution)/shard_map/ppermute | solution.py:406
  762.6 8.3 %all_gather.40 = bf16[4,352,256]{2,1,0:T(8,128)(2,1)S(1)} all-gather(bf16[1,352,256]{2,1,0:T(8,128)(2,1)S(1)} %add_convert_fusion.13), channel_id=1, replica_groups=mesh['section'=2,'group'=4,'dp'=4] {'group'}, dimensions={0}, use_global_device_ids=true | all-gather | bytes 901120 | tf_op jit(solution)/shard_map/all_gather | solution.py:396
  771.6 3.5 collective-permute-done.17
  778.9 13.1 %all-gather.4 = f32[4,4,1024]{2,1,0:T(4,128)S(1)} all-gather(f32[1,4,1024]{2,1,0:T(4,128)S(1)} %add_bitcast_fusion), channel_id=4, replica_groups=mesh['section'=2,'group'=4,'dp'=4] {'dp'}, dimensions={0}, use_global_device_ids=true | all-gather | bytes 81920 | tf_op jit(solution)/shard_map/all_gather | solution.py:420
  792.7 3.9 maximum_select_fusion
  (383 shorter events, 139.2 us)
Async XLA Ops:
  7.2 20.7 %copy-start = (bf16[4,256,1024]{2,1,0:T(8,128)(2,1)S(1)}, bf16[4,256,1024]{2,1,0:T(8,128)(2,1)}, u32[]{:S(2)}) copy-start(bf16[4,256,1024]{2,1,0:T(8,128)(2,1)} %param.17) | copy-start | bytes 6291460
  7.2 122.0 %all-gather.12.cloned.1.call-start = ((), (), s32[]{:S(2)}) async-start(), calls=%async_computation.9 | async-start | bytes 17301504 | tf_op jit(solution)/shard_map/all_gather | solution.py:231
  7.3 15.2 %copy-start.77 = (f32[1,2,1024]{2,1,0:T(2,128)S(1)}, f32[1,2,1024]{2,1,0:T(2,128)}, u32[]{:S(2)}) copy-start(f32[1,2,1024]{2,1,0:T(2,128)} %param.14) | copy-start | bytes 24580
  9.5 239.5 %all-gather.14.cloned.1.call-start = ((), (), s32[]{:S(2)}) async-start(), calls=%async_computation.10 | async-start | bytes 17842176 | tf_op jit(solution)/shard_map/all_gather | solution.py:239
  20.5 578.8 %reduce-scatter.11.cloned.1.call-start = ((), (), s32[]{:S(2)}) async-start(), calls=%async_computation.8 | async-start | bytes 3604480 | tf_op jit(solution)/shard_map/reduce_scatter | solution.py:318
  21.1 123.4 %copy-start.6 = (s32[2,1,256]{2,1,0:T(1,128)}, s32[2,1,256]{2,1,0:T(1,128)S(1)}, u32[]{:S(2)}) copy-start(s32[2,1,256]{2,1,0:T(1,128)S(1)} %broadcast_in_dim.56.lo_ref) | copy-start | bytes 6148
  22.4 17.2 %copy-start.72 = (f32[1,2,2,128]{3,1,2,0:T(2,128)}, f32[1,2,2,128]{3,1,2,0:T(2,128)S(1)}, u32[]{:S(2)}) copy-start(f32[1,2,2,128]{3,1,2,0:T(2,128)S(1)} %copy.37) | copy-start | bytes 6148
  35.9 108.6 %copy-start.10 = (s32[2,2]{1,0:T(2,128)}, s32[2,2]{1,0:T(2,128)S(1)}, u32[]{:S(2)}) copy-start(s32[2,2]{1,0:T(2,128)S(1)} %get-tuple-element.144.stop_ref) | copy-start | bytes 52
  36.0 108.6 %copy-start.12 = (s32[2,2]{1,0:T(2,128)}, s32[2,2]{1,0:T(2,128)S(1)}, u32[]{:S(2)}) copy-start(s32[2,2]{1,0:T(2,128)S(1)} %get-tuple-element.145.first_ref) | copy-start | bytes 52
  36.0 108.5 %copy-start.8 = (s32[2,2,128]{2,1,0:T(2,128)}, s32[2,2,128]{2,1,0:T(2,128)S(1)}, u32[]{:S(2)}) copy-start(s32[2,2,128]{2,1,0:T(2,128)S(1)} %broadcast_add_fusion) | copy-start | bytes 6148
  36.1 319.3 %copy-start.66 = (f32[1,1,1024]{2,1,0:T(1,128)}, f32[1,1,1024]{2,1,0:T(1,128)S(1)}, u32[]{:S(2)}) copy-start(f32[1,1,1024]{2,1,0:T(1,128)S(1)} %get-tuple-element.116) | copy-start | bytes 12292
  144.5 42.6 %copy-start.24 = (bf16[2048,1024]{1,0:T(8,128)(2,1)}, bf16[2048,1024]{1,0:T(8,128)(2,1)S(1)}, u32[]{:S(2)}) copy-start(bf16[2048,1024]{1,0:T(8,128)(2,1)S(1)} %convolution_convert_fusion.3.k_ref) | copy-start | bytes 12582916
  144.6 42.5 %copy-start.29 = (f32[512,1024]{1,0:T(8,128)S(1)}, f32[512,1024]{1,0:T(8,128)}, u32[]{:S(2)}) copy-start(f32[512,1024]{1,0:T(8,128)} %bitcast_divide_fusion) | copy-start | bytes 6291460
  188.5 28.8 %copy-start.56 = (bf16[512,1024]{1,0:T(8,128)(2,1)}, bf16[512,1024]{1,0:T(8,128)(2,1)S(1)}, u32[]{:S(2)}) copy-start(bf16[512,1024]{1,0:T(8,128)(2,1)S(1)} %get-tuple-element.135) | copy-start | bytes 3145732
  269.7 62.6 %copy-start.44 = (bf16[352,8,2,512]{3,1,2,0:T(8,128)(2,1)}, bf16[352,8,2,512]{3,1,2,0:T(8,128)(2,1)S(1)}, u32[]{:S(2)}) copy-start(bf16[352,8,2,512]{3,1,2,0:T(8,128)(2,1)S(1)} %copy.39) | copy-start | bytes 17301508
  302.0 21.3 %copy-start.51 = (bf16[512,1024]{1,0:T(8,128)(2,1)S(1)}, bf16[512,1024]{1,0:T(8,128)(2,1)}, u32[]{:S(2)}) copy-start(bf16[512,1024]{1,0:T(8,128)(2,1)} %multiply_convert_fusion.4) | copy-start | bytes 3145732
  354.6 38.7 %collective-permute-start.1 = (bf16[1024,2816]{1,0:T(8,128)(2,1)}, bf16[1024,2816]{1,0:T(8,128)(2,1)}, u32[]{:S(2)}, u32[]{:S(2)}) collective-permute-start(bf16[1024,2816]{1,0:T(8,128)(2,1)} %convolution_convert_fusion), channel_id=1, source_target_pairs={{0,4},{4,0},{8,12},{12,8},{1,5},{5,1},{9,13},{13,9},{2,6},{6,2},{1... | collective-permute-start | bytes 17301512 | tf_op jit(solution)/shard_map/ppermute | solution.py:328
  367.8 219.6 %collective-permute-start = (bf16[2,256,512]{2,1,0:T(8,128)(2,1)}, bf16[2,256,512]{2,1,0:T(8,128)(2,1)}, u32[]{:S(2)}, u32[]{:S(2)}) collective-permute-start(bf16[2,256,512]{2,1,0:T(8,128)(2,1)} %get-tuple-element.107), channel_id=1, source_target_pairs={{0,16},{16,0},{1,17},{17,1},{2,18},{18,2},{3,19},{19,3},{4,20},{20... | collective-permute-start | bytes 1572872 | tf_op jit(solution)/shard_map/ppermute | solution.py:387
  368.9 19.1 %collective-permute-start.2 = (bf16[2816,512]{1,0:T(8,128)(2,1)}, bf16[2816,512]{1,0:T(8,128)(2,1)}, u32[]{:S(2)}, u32[]{:S(2)}) collective-permute-start(bf16[2816,512]{1,0:T(8,128)(2,1)} %convolution_convert_fusion.1), channel_id=1, source_target_pairs={{0,4},{4,0},{8,12},{12,8},{1,5},{5,1},{9,13},{13,9},{2,6},{6,2},{1... | collective-permute-start | bytes 8650760 | tf_op jit(solution)/shard_map/ppermute | solution.py:328
  401.0 300.3 %reduce-scatter.9.cloned.1.call-start = ((), (), s32[]{:S(2)}) async-start(), calls=%async_computation.7 | async-start | bytes 1802240 | tf_op jit(solution)/shard_map/reduce_scatter | solution.py:318
  403.5 26.0 %copy-start.57 = (bf16[512,1024]{1,0:T(8,128)(2,1)S(1)}, bf16[512,1024]{1,0:T(8,128)(2,1)}, u32[]{:S(2)}) copy-start(bf16[512,1024]{1,0:T(8,128)(2,1)} %copy-done.56) | copy-start | bytes 3145732
  433.4 66.1 %collective-permute-start.4 = (bf16[4,1024,512]{2,1,0:T(8,128)(2,1)S(1)}, bf16[4,1024,512]{2,1,0:T(8,128)(2,1)}, u32[]{:S(2)}, u32[]{:S(2)}) collective-permute-start(bf16[4,1024,512]{2,1,0:T(8,128)(2,1)S(1)} %pad_maximum_fusion.1), channel_id=1, source_target_pairs={{0,4},{4,0},{8,12},{12,8},{1,5},{5,1},{9,13},{13,9},{2,6},{6,2},{1... | collective-permute-start | bytes 12582920 | tf_op jit(solution)/shard_map/ppermute | solution.py:328
  434.6 64.2 %collective-permute-start.3 = (bf16[512,2816]{1,0:T(8,128)(2,1)S(1)}, bf16[512,2816]{1,0:T(8,128)(2,1)S(1)}, u32[]{:S(2)}, u32[]{:S(2)}) collective-permute-start(bf16[512,2816]{1,0:T(8,128)(2,1)S(1)} %constant_dynamic-slice_fusion.12), channel_id=1, source_target_pairs={{0,16},{16,0},{1,17},{17,1},{2,18},{18,2},{3,19},{19,3},{4,20},{20... | collective-permute-start | bytes 8650760 | tf_op jit(solution)/shard_map/ppermute | solution.py:305
  455.6 43.9 %copy-start.55 = (f32[1,1024,512]{2,1,0:T(8,128)S(1)}, f32[1,1024,512]{2,1,0:T(8,128)}, u32[]{:S(2)}) copy-start(f32[1,1024,512]{2,1,0:T(8,128)} %convolution_bitcast_fusion.2) | copy-start | bytes 6291460
  505.2 64.2 %collective-permute-start.5 = (bf16[512,1408]{1,0:T(8,128)(2,1)}, bf16[512,1408]{1,0:T(8,128)(2,1)}, u32[]{:S(2)}, u32[]{:S(2)}) collective-permute-start(bf16[512,1408]{1,0:T(8,128)(2,1)} %constant_dynamic-slice_fusion.11), channel_id=1, source_target_pairs={{0,8},{4,12},{8,0},{12,4},{1,9},{5,13},{9,1},{13,5},{2,10},{6,14},... | collective-permute-start | bytes 4325384 | tf_op jit(solution)/shard_map/ppermute | solution.py:305
  507.8 75.6 %collective-permute-start.6 = (bf16[4,1024,256]{2,1,0:T(8,128)(2,1)}, bf16[4,1024,256]{2,1,0:T(8,128)(2,1)}, u32[]{:S(2)}, u32[]{:S(2)}) collective-permute-start(bf16[4,1024,256]{2,1,0:T(8,128)(2,1)} %constant_dynamic-slice_fusion.10), channel_id=1, source_target_pairs={{0,8},{4,12},{8,0},{12,4},{1,9},{5,13},{9,1},{13,5},{2,10},{6,14},... | collective-permute-start | bytes 6291464 | tf_op jit(solution)/shard_map/ppermute | solution.py:305
  509.1 51.6 %copy-start.30 = (f32[512,1024]{1,0:T(8,128)S(1)}, f32[512,1024]{1,0:T(8,128)}, u32[]{:S(2)}) copy-start(f32[512,1024]{1,0:T(8,128)} %bitcast_divide_fusion) | copy-start | bytes 6291460
  509.1 51.6 %copy-start.63 = (f32[1,1,1024]{2,1,0:T(1,128)S(1)}, f32[1,1,1024]{2,1,0:T(1,128)}, u32[]{:S(2)}) copy-start(f32[1,1,1024]{2,1,0:T(1,128)} %copy-done.62) | copy-start | bytes 12292
  509.1 52.5 %copy-start.26 = (bf16[2048,1024]{1,0:T(8,128)(2,1)S(1)}, bf16[2048,1024]{1,0:T(8,128)(2,1)}, u32[]{:S(2)}) copy-start(bf16[2048,1024]{1,0:T(8,128)(2,1)} %fusion.6) | copy-start | bytes 12582916
  587.4 125.2 %reduce-scatter.7.cloned.1.call-start = ((), (), s32[]{:S(2)}) async-start(), calls=%async_computation.5 | async-start | bytes 1310720 | tf_op jit(solution)/shard_map/reduce_scatter | solution.py:318
  592.4 42.6 %collective-permute-start.7 = (bf16[2,1024,512]{2,1,0:T(8,128)(2,1)}, bf16[2,1024,512]{2,1,0:T(8,128)(2,1)}, u32[]{:S(2)}, u32[]{:S(2)}) collective-permute-start(bf16[2,1024,512]{2,1,0:T(8,128)(2,1)} %pad_maximum_fusion.2), channel_id=1, source_target_pairs={{0,4},{4,0},{8,12},{12,8},{1,5},{5,1},{9,13},{13,9},{2,6},{6,2},{1... | collective-permute-start | bytes 6291464 | tf_op jit(solution)/shard_map/ppermute | solution.py:328
  592.4 46.4 %collective-permute-start.8 = (bf16[2,1024,512]{2,1,0:T(8,128)(2,1)}, bf16[2,1024,512]{2,1,0:T(8,128)(2,1)}, u32[]{:S(2)}, u32[]{:S(2)}) collective-permute-start(bf16[2,1024,512]{2,1,0:T(8,128)(2,1)} %pad_maximum_fusion.3), channel_id=1, source_target_pairs={{0,4},{4,0},{8,12},{12,8},{1,5},{5,1},{9,13},{13,9},{2,6},{6,2},{1... | collective-permute-start | bytes 6291464 | tf_op jit(solution)/shard_map/ppermute | solution.py:328
  600.3 11.7 %collective-permute-start.19 = (bf16[1,352,512]{2,1,0:T(8,128)(2,1)S(1)}, bf16[1,352,512]{2,1,0:T(8,128)(2,1)S(1)}, u32[]{:S(2)}, u32[]{:S(2)}) collective-permute-start(bf16[1,352,512]{2,1,0:T(8,128)(2,1)S(1)} %constant_dynamic-slice_fusion.1), channel_id=1, source_target_pairs={{0,16},{16,0},{1,17},{17,1},{2,18},{18,2},{3,19},{19,3},{4,20},{20... | collective-permute-start | bytes 1081352 | tf_op jit(solution)/shard_map/ppermute | solution.py:305
  602.9 30.4 %collective-permute-start.14 = (bf16[4,1024,128]{2,1,0:T(8,128)(2,1)S(1)}, bf16[4,1024,128]{2,1,0:T(8,128)(2,1)S(1)}, u32[]{:S(2)}, u32[]{:S(2)}) collective-permute-start(bf16[4,1024,128]{2,1,0:T(8,128)(2,1)S(1)} %constant_dynamic-slice_fusion.3), channel_id=1, source_target_pairs={{0,16},{16,0},{1,17},{17,1},{2,18},{18,2},{3,19},{19,3},{4,20},{20... | collective-permute-start | bytes 3145736 | tf_op jit(solution)/shard_map/ppermute | solution.py:305
  609.7 23.6 %copy-start.39 = (bf16[4,1024,256]{2,1,0:T(8,128)(2,1)S(1)}, bf16[4,1024,256]{2,1,0:T(8,128)(2,1)}, u32[]{:S(2)}) copy-start(bf16[4,1024,256]{2,1,0:T(8,128)(2,1)} %add_convert_fusion.3) | copy-start | bytes 6291460
  612.8 102.1 %collective-permute-start.20 = (bf16[1,352,256]{2,1,0:T(8,128)(2,1)}, bf16[1,352,256]{2,1,0:T(8,128)(2,1)}, u32[]{:S(2)}, u32[]{:S(2)}) collective-permute-start(bf16[1,352,256]{2,1,0:T(8,128)(2,1)} %constant_dynamic-slice_fusion), channel_id=1, source_target_pairs={{0,8},{4,12},{8,0},{12,4},{1,9},{5,13},{9,1},{13,5},{2,10},{6,14},... | collective-permute-start | bytes 540680 | tf_op jit(solution)/shard_map/ppermute | solution.py:305
  634.7 77.9 %reduce-scatter.5.cloned.1.call-start = ((), (), s32[]{:S(2)}) async-start(), calls=%async_computation.4 | async-start | bytes 1310720 | tf_op jit(solution)/shard_map/reduce_scatter | solution.py:318
  644.9 24.0 %collective-permute-start.12 = (bf16[2,1024,256]{2,1,0:T(8,128)(2,1)S(1)}, bf16[2,1024,256]{2,1,0:T(8,128)(2,1)S(1)}, u32[]{:S(2)}, u32[]{:S(2)}) collective-permute-start(bf16[2,1024,256]{2,1,0:T(8,128)(2,1)S(1)} %constant_dynamic-slice_fusion.5), channel_id=1, source_target_pairs={{0,8},{4,12},{8,0},{12,4},{1,9},{5,13},{9,1},{13,5},{2,10},{6,14},... | collective-permute-start | bytes 3145736 | tf_op jit(solution)/shard_map/ppermute | solution.py:305
  645.6 25.2 %collective-permute-start.10 = (bf16[2,1024,256]{2,1,0:T(8,128)(2,1)S(1)}, bf16[2,1024,256]{2,1,0:T(8,128)(2,1)S(1)}, u32[]{:S(2)}, u32[]{:S(2)}) collective-permute-start(bf16[2,1024,256]{2,1,0:T(8,128)(2,1)S(1)} %constant_dynamic-slice_fusion.7), channel_id=1, source_target_pairs={{0,16},{16,0},{1,17},{17,1},{2,18},{18,2},{3,19},{19,3},{4,20},{20... | collective-permute-start | bytes 3145736 | tf_op jit(solution)/shard_map/ppermute | solution.py:305
  669.3 11.8 %collective-permute-start.13 = (bf16[2,1024,128]{2,1,0:T(8,128)(2,1)S(1)}, bf16[2,1024,128]{2,1,0:T(8,128)(2,1)S(1)}, u32[]{:S(2)}, u32[]{:S(2)}) collective-permute-start(bf16[2,1024,128]{2,1,0:T(8,128)(2,1)S(1)} %constant_dynamic-slice_fusion.4), channel_id=1, source_target_pairs={{0,16},{16,0},{1,17},{17,1},{2,18},{18,2},{3,19},{19,3},{4,20},{20... | collective-permute-start | bytes 1572872 | tf_op jit(solution)/shard_map/ppermute | solution.py:305
  671.2 11.2 %collective-permute-start.11 = (bf16[2,1024,128]{2,1,0:T(8,128)(2,1)S(1)}, bf16[2,1024,128]{2,1,0:T(8,128)(2,1)S(1)}, u32[]{:S(2)}, u32[]{:S(2)}) collective-permute-start(bf16[2,1024,128]{2,1,0:T(8,128)(2,1)S(1)} %constant_dynamic-slice_fusion.6), channel_id=1, source_target_pairs={{0,8},{4,12},{8,0},{12,4},{1,9},{5,13},{9,1},{13,5},{2,10},{6,14},... | collective-permute-start | bytes 1572872 | tf_op jit(solution)/shard_map/ppermute | solution.py:305
  683.7 113.0 %all-gather.16.cloned.1.call-start = ((), (), s32[]{:S(2)}) async-start(), calls=%async_computation.11 | async-start | bytes 1802240 | tf_op jit(solution)/shard_map/all_gather | solution.py:396
  701.2 98.7 %all-gather.10.cloned.1.call-start = ((), (), s32[]{:S(2)}) async-start(), calls=%async_computation.6 | async-start | bytes 2621440 | tf_op jit(solution)/shard_map/all_gather | solution.py:396
  711.7 81.0 %collective-permute-start.9 = (bf16[2,1024,512]{2,1,0:T(8,128)(2,1)}, bf16[2,1024,512]{2,1,0:T(8,128)(2,1)}, u32[]{:S(2)}, u32[]{:S(2)}) collective-permute-start(bf16[2,1024,512]{2,1,0:T(8,128)(2,1)} %get-tuple-element.95), channel_id=1, source_target_pairs={{0,16},{16,0},{1,17},{17,1},{2,18},{18,2},{3,19},{19,3},{4,20},{20... | collective-permute-start | bytes 6291464 | tf_op jit(solution)/shard_map/ppermute | solution.py:387
  713.7 48.0 %collective-permute-start.15 = (bf16[4,256,128]{2,1,0:T(8,128)(2,1)S(1)}, bf16[4,256,128]{2,1,0:T(8,128)(2,1)S(1)}, u32[]{:S(2)}, u32[]{:S(2)}) collective-permute-start(bf16[4,256,128]{2,1,0:T(8,128)(2,1)S(1)} %get-tuple-element.113), channel_id=1, source_target_pairs={{0,16},{16,0},{1,17},{17,1},{2,18},{18,2},{3,19},{19,3},{4,20},{20... | collective-permute-start | bytes 786440 | tf_op jit(solution)/shard_map/ppermute | solution.py:406
  715.9 55.0 %collective-permute-start.16 = (f32[4,1024]{1,0:T(4,128)S(1)}, f32[4,1024]{1,0:T(4,128)S(1)}, u32[]{:S(2)}, u32[]{:S(2)}) collective-permute-start(f32[4,1024]{1,0:T(4,128)S(1)} %pad_maximum_fusion.5), channel_id=1, source_target_pairs={{0,4},{4,0},{8,12},{12,8},{1,5},{5,1},{9,13},{13,9},{2,6},{6,2},{1... | collective-permute-start | bytes 49160 | tf_op jit(solution)/shard_map/ppermute | solution.py:419
  770.9 4.1 collective-permute-start.17
  775.1 3.8 collective-permute-start.18
  (74 other events, 394.3 us)
Sparse Core Ops, SparseCore 0:
  11.6 117.5 all-gather.11
  132.7 116.2 all-gather.13
  401.1 54.4 reduce-scatter.10
  587.5 32.6 reduce-scatter.8
  634.8 26.0 reduce-scatter.6
  683.8 25.6 reduce-scatter.4
  711.0 17.5 all-gather.15
  762.8 21.8 all-gather.9

commit v4 on v3

--- a/solution.py
+++ b/solution.py
@@ -10,13 +10,14 @@
 D = 1024
 HEADS = 16
 HEAD_DIM = 64
+PAIR = 2 * HEAD_DIM
 PAIRS = HEADS // 2
-BLOCK = 512
 FF = 2816
 ROW_BYTES = 1024
 PATCHES = 256
 QT = 128
 TILES = PATCHES // QT
+CAUSAL_SPANS = ((0, 1), (0, 2))
 
 EPS = 1e-05
 SCALE = HEAD_DIM ** (-0.5)
@@ -54,92 +55,119 @@
     return jnp.concatenate([row, row], axis=1)
 
 
-def attend_kernel(chunk, first_ref, stop_ref, lo_ref, hi_ref, q_ref, k_ref, v_ref, c_ref, l_ref, s_ref):
-    row = pl.program_id(0)
+def fill_bias(keys, lo_ref, hi_ref, bias_ref):
+    at = lax.broadcasted_iota(jnp.int32, (keys, QT), 0)
     for tile in range(TILES):
         own = pl.ds(tile * QT, QT)
-        queries = two_heads(q_ref[own, :].astype(F32) * SCALE).astype(BF)
-        lo = twice(lo_ref[0, :, own])
-        hi = twice(hi_ref[0, :, own])
-        first = first_ref[row, tile]
-        stop = stop_ref[row, tile]
-
-        def scores(j, top):
-            start = pl.multiple_of(j * chunk, chunk)
-            part = nt(k_ref[pl.ds(start, chunk), :], queries)
-            at = lax.broadcasted_iota(jnp.int32, part.shape, 0) + start
-            part = jnp.where((at >= lo) & (at < hi), part, EXCLUDED)
-            s_ref[pl.ds(start, chunk), :] = part
-            return jnp.maximum(top, jnp.max(part, axis=0, keepdims=True))
-
-        top = lax.fori_loop(first, stop, scores, jnp.full((1, 2 * QT), EXCLUDED, F32))
-
-        def context(j, carry):
-            total, acc = carry
-            start = pl.multiple_of(j * chunk, chunk)
-            weight = jnp.exp(s_ref[pl.ds(start, chunk), :] - top)
-            total = total + jnp.sum(weight, axis=0, keepdims=True)
-            acc = acc + tn(v_ref[pl.ds(start, chunk), :], weight.astype(BF))
-            return (total, acc)
-
-        total, acc = lax.fori_loop(
-            first, stop, context, (jnp.zeros((1, 2 * QT), F32), jnp.zeros((2 * HEAD_DIM, 2 * QT), F32))
-        )
-        c_ref[own, :] = own_lanes(acc / total).astype(BF)
-        l_ref[0, 0, tile : tile + 1, :] = top + jnp.log(total)
-
-
-def attend_back_kernel(
-    chunk, first_ref, stop_ref, lo_ref, hi_ref, q_ref, k_ref, v_ref, l_ref, c_ref, dc_ref,
-    dq_ref, dk_ref, dv_ref, dk_acc, dv_acc,
+        inside = (at >= lo_ref[0, :, own]) & (at < hi_ref[0, :, own])
+        bias_ref[tile] = jnp.where(inside, 0.0, EXCLUDED)
+
+
+def over_chunks(spans, tile, bounds, body, init):
+    if spans is None:
+        return lax.fori_loop(*bounds, body, init)
+    for j in range(*spans[tile]):
+        init = body(j, init)
+    return init
+
+
+def chunk_at(spans, chunk, j):
+    return pl.ds(j * chunk if spans is not None else pl.multiple_of(j * chunk, chunk), chunk)
+
+
+def attend_kernel(
+    chunk, spans, first_ref, stop_ref, lo_ref, hi_ref, q_ref, k_ref, v_ref, c_ref, l_ref, bias_ref, s_ref
 ):
     row = pl.program_id(0)
+    pairs = range(q_ref.shape[1] // PAIR)
+    lanes = [pl.ds(pair * PAIR, PAIR) for pair in pairs]
+    pl.when(pl.program_id(1) == 0)(lambda: fill_bias(k_ref.shape[0], lo_ref, hi_ref, bias_ref))
+    for tile in range(TILES):
+        own = pl.ds(tile * QT, QT)
+        queries = [two_heads(q_ref[own, at].astype(F32) * SCALE).astype(BF) for at in lanes]
+        bounds = (first_ref[row, tile], stop_ref[row, tile])
+
+        def scores(j, tops):
+            here = chunk_at(spans, chunk, j)
+            bias = twice(bias_ref[tile, here, :])
+            out = []
+            for pair in pairs:
+                part = nt(k_ref[here, lanes[pair]], queries[pair]) + bias
+                s_ref[pair, here, :] = part
+                out.append(jnp.maximum(tops[pair], jnp.max(part, axis=0, keepdims=True)))
+            return tuple(out)
+
+        tops = (jnp.full((1, 2 * QT), EXCLUDED, F32),) * len(pairs)
+        tops = over_chunks(spans, tile, bounds, scores, tops)
+
+        def context(j, sums):
+            here = chunk_at(spans, chunk, j)
+            out = []
+            for pair in pairs:
+                total, acc = sums[pair]
+                weight = jnp.exp(s_ref[pair, here, :] - tops[pair])
+                total = total + jnp.sum(weight, axis=0, keepdims=True)
+                out.append((total, acc + tn(v_ref[here, lanes[pair]], weight.astype(BF))))
+            return tuple(out)
+
+        sums = ((jnp.zeros((1, 2 * QT), F32), jnp.zeros((PAIR, 2 * QT), F32)),) * len(pairs)
+        sums = over_chunks(spans, tile, bounds, context, sums)
+        for pair in pairs:
+            total, acc = sums[pair]
+            c_ref[own, lanes[pair]] = own_lanes(acc / total).astype(BF)
+            l_ref[0, pair, tile : tile + 1, :] = tops[pair] + jnp.log(total)
+
+
+def attend_back_kernel(
+    chunk, spans, first_ref, stop_ref, lo_ref, hi_ref, q_ref, k_ref, v_ref, l_ref, c_ref, dc_ref,
+    dq_ref, dk_ref, dv_ref, bias_ref, dk_acc, dv_acc,
+):
+    row = pl.program_id(0)
+    pairs = range(q_ref.shape[1] // PAIR)
+    lanes = [pl.ds(pair * PAIR, PAIR) for pair in pairs]
+    pl.when(pl.program_id(1) == 0)(lambda: fill_bias(k_ref.shape[0], lo_ref, hi_ref, bias_ref))
     dk_acc[...] = jnp.zeros_like(dk_acc)
     dv_acc[...] = jnp.zeros_like(dv_acc)
     for tile in range(TILES):
         own = pl.ds(tile * QT, QT)
-        queries = two_heads(q_ref[own, :].astype(F32) * SCALE).astype(BF)
-        grads = dc_ref[own, :].astype(F32)
-        inner = (grads * c_ref[own, :].astype(F32)).T
-        delta = jnp.concatenate(
-            [
-                jnp.sum(inner[:HEAD_DIM], axis=0, keepdims=True),
-                jnp.sum(inner[HEAD_DIM:], axis=0, keepdims=True),
-            ],
-            axis=1,
-        )
-        grads = two_heads(grads).astype(BF)
-        lo = twice(lo_ref[0, :, own])
-        hi = twice(hi_ref[0, :, own])
-        logsum = l_ref[0, 0, tile : tile + 1, :]
-
-        def step(j, acc):
-            start = pl.multiple_of(j * chunk, chunk)
-            here = pl.ds(start, chunk)
-            keys = k_ref[here, :]
-            part = nt(keys, queries)
-            at = lax.broadcasted_iota(jnp.int32, part.shape, 0) + start
-            part = jnp.where((at >= lo) & (at < hi), part, EXCLUDED)
-            prob = jnp.exp(part - logsum)
-            slope = prob * (nt(v_ref[here, :], grads) - delta)
-            slope = slope.astype(BF)
-            dv_acc[here, :] += nn(prob.astype(BF), grads)
-            dk_acc[here, :] += nn(slope, queries)
-            return acc + tn(keys, slope)
-
-        acc = lax.fori_loop(
-            first_ref[row, tile], stop_ref[row, tile], step, jnp.zeros((2 * HEAD_DIM, 2 * QT), F32)
-        )
-        dq_ref[own, :] = (own_lanes(acc) * SCALE).astype(BF)
+        queries, grads, deltas, logs = [], [], [], []
+        for pair in pairs:
+            queries.append(two_heads(q_ref[own, lanes[pair]].astype(F32) * SCALE).astype(BF))
+            grad = dc_ref[own, lanes[pair]].astype(F32)
+            inner = (grad * c_ref[own, lanes[pair]].astype(F32)).T
+            heads = [jnp.sum(part, axis=0, keepdims=True) for part in (inner[:HEAD_DIM], inner[HEAD_DIM:])]
+            deltas.append(jnp.concatenate(heads, axis=1))
+            grads.append(two_heads(grad).astype(BF))
+            logs.append(l_ref[0, pair, tile : tile + 1, :])
+
+        def step(j, accs):
+            here = chunk_at(spans, chunk, j)
+            bias = twice(bias_ref[tile, here, :])
+            out = []
+            for pair in pairs:
+                keys = k_ref[here, lanes[pair]]
+                prob = jnp.exp(nt(keys, queries[pair]) + bias - logs[pair])
+                slope = prob * (nt(v_ref[here, lanes[pair]], grads[pair]) - deltas[pair])
+                slope = slope.astype(BF)
+                dv_acc[here, lanes[pair]] += nn(prob.astype(BF), grads[pair])
+                dk_acc[here, lanes[pair]] += nn(slope, queries[pair])
+                out.append(accs[pair] + tn(keys, slope))
+            return tuple(out)
+
+        bounds = (first_ref[row, tile], stop_ref[row, tile])
+        accs = (jnp.zeros((PAIR, 2 * QT), F32),) * len(pairs)
+        accs = over_chunks(spans, tile, bounds, step, accs)
+        for pair in pairs:
+            dq_ref[own, lanes[pair]] = (own_lanes(accs[pair]) * SCALE).astype(BF)
     dk_ref[...] = dk_acc[...].astype(BF)
     dv_ref[...] = dv_acc[...].astype(BF)
 
 
-def attention_specs(keys):
-    per_query = pl.BlockSpec((PATCHES, 2 * HEAD_DIM), lambda r, h, *_: (r, h))
-    per_key = pl.BlockSpec((keys, 2 * HEAD_DIM), lambda r, h, *_: (r, h))
+def attention_specs(keys, wide):
+    per_query = pl.BlockSpec((PATCHES, wide * PAIR), lambda r, h, *_: (r, h))
+    per_key = pl.BlockSpec((keys, wide * PAIR), lambda r, h, *_: (r, h))
     bound = pl.BlockSpec((1, 1, PATCHES), lambda r, h, *_: (r, 0, 0))
-    logs = pl.BlockSpec((1, 1, TILES, 2 * QT), lambda r, h, *_: (r, h, 0, 0))
+    logs = pl.BlockSpec((1, wide, TILES, 2 * QT), lambda r, h, *_: (r, h, 0, 0))
     return per_query, per_key, bound, logs
 
 
@@ -150,50 +178,50 @@
     )
 
 
-def attend(bounds, q, k, v):
+def attend(bounds, q, k, v, wide, spans=None):
     first, stop, lo, hi, chunk = bounds
     rows = lo.shape[0]
     keys = k.shape[0] // rows
-    per_query, per_key, bound, logs = attention_specs(keys)
+    per_query, per_key, bound, logs = attention_specs(keys, wide)
     return pl.pallas_call(
-        functools.partial(attend_kernel, chunk),
+        functools.partial(attend_kernel, chunk, spans),
         grid_spec=pltpu.PrefetchScalarGridSpec(
             num_scalar_prefetch=2,
-            grid=(rows, PAIRS),
+            grid=(rows, PAIRS // wide),
             in_specs=[bound, bound, per_query, per_key, per_key],
             out_specs=[per_query, logs],
-            scratch_shapes=[pltpu.VMEM((keys, 2 * QT), F32)],
+            scratch_shapes=[pltpu.VMEM((TILES, keys, QT), F32), pltpu.VMEM((wide, keys, 2 * QT), F32)],
         ),
         out_shape=[
             jax.ShapeDtypeStruct(q.shape, BF),
             jax.ShapeDtypeStruct((rows, PAIRS, TILES, 2 * QT), F32),
         ],
-        compiler_params=pltpu.CompilerParams(vmem_limit_bytes=32 << 20),
+        compiler_params=pltpu.CompilerParams(vmem_limit_bytes=48 << 20),
         cost_estimate=kernel_cost(q, k, 2),
         name="attend",
     )(first, stop, lo, hi, q, k, v)
 
 
-def attend_back(bounds, q, k, v, logsum, context, grads):
+def attend_back(bounds, q, k, v, logsum, context, grads, wide, spans=None):
     first, stop, lo, hi, chunk = bounds
     rows = lo.shape[0]
     keys = k.shape[0] // rows
-    per_query, per_key, bound, logs = attention_specs(keys)
+    per_query, per_key, bound, logs = attention_specs(keys, wide)
     return pl.pallas_call(
-        functools.partial(attend_back_kernel, chunk),
+        functools.partial(attend_back_kernel, chunk, spans),
         grid_spec=pltpu.PrefetchScalarGridSpec(
             num_scalar_prefetch=2,
-            grid=(rows, PAIRS),
+            grid=(rows, PAIRS // wide),
             in_specs=[bound, bound, per_query, per_key, per_key, logs, per_query, per_query],
             out_specs=[per_query, per_key, per_key],
-            scratch_shapes=[pltpu.VMEM((keys, 2 * HEAD_DIM), F32)] * 2,
+            scratch_shapes=[pltpu.VMEM((TILES, keys, QT), F32)] + [pltpu.VMEM((keys, wide * PAIR), F32)] * 2,
         ),
         out_shape=[
             jax.ShapeDtypeStruct(q.shape, BF),
             jax.ShapeDtypeStruct(k.shape, BF),
             jax.ShapeDtypeStruct(k.shape, BF),
         ],
-        compiler_params=pltpu.CompilerParams(vmem_limit_bytes=32 << 20),
+        compiler_params=pltpu.CompilerParams(vmem_limit_bytes=48 << 20),
         cost_estimate=kernel_cost(q, k, 5),
         name="attend_back",
     )(first, stop, lo, hi, q, k, v, logsum, context, grads)
@@ -226,23 +254,36 @@
     groups = lax.axis_size("group")
     core, side = group % 2, group // 2
 
+    core_pairs = [(0, 1), (1, 0), (2, 3), (3, 2)]
+    side_pairs = [(0, 2), (1, 3), (2, 0), (3, 1)]
+    swap = [(0, 1), (1, 0)]
+    together = lax.optimization_barrier
+
     four = jnp.concatenate([attn_qkv[0], attn_out], axis=0)
     matrix = lax.dynamic_index_in_dim(four, group, 0, keepdims=False)
     matrices = lax.all_gather(matrix, ("section", "group", "dp"), axis=0, tiled=True)
+
+    def quarter_of(shard):
+        height = shard.shape[0] // groups
+        return lax.dynamic_slice_in_dim(shard, group * height, height, 0)
+
+    w_in = lax.all_gather(quarter_of(ffn_in), ("section", "dp", "group"), axis=0, tiled=True)
+    gains = lax.all_gather(norm_gains, "section", axis=0, tiled=True)
+
+    def both(values, part, axis, pairs):
+        got = lax.ppermute(values, axis, pairs)
+        return jnp.where(part == 0, jnp.stack([values, got]), jnp.stack([got, values]))
+
+    line, place = lax.axis_size("dp"), lax.axis_index("dp")
+    quarter = quarter_of(ffn_down)
+    down = jnp.zeros((line,) + quarter.shape, BF)
+    for step in range(line):
+        moved = lax.ppermute(quarter, "dp", [(i, (i + step) % line) for i in range(line)]) if step else quarter
+        down = lax.dynamic_update_slice_in_dim(down, moved[None], (place - step) % line, 0)
+    matrices, down = together((matrices, down))
     matrices = matrices.reshape(sections, groups, D, D)
     wq, wk, wv, wo = [matrices[:, index] for index in range(4)]
-    blocks = []
-    for shard in (ffn_in, ffn_down):
-        height = shard.shape[0] // groups
-        part = lax.dynamic_slice_in_dim(shard, group * height, height, 0)
-        blocks += [part[:, at : at + BLOCK] for at in range(0, part.shape[1], BLOCK)]
-    ffn = lax.all_gather(jnp.concatenate(blocks, axis=0), ("section", "dp", "group"), axis=0, tiled=False)
-    in_rows = ffn_in.size // groups // BLOCK
-    w_in, w_down = [
-        part.reshape(part.shape[0], width // BLOCK, -1, BLOCK).swapaxes(1, 2).reshape(-1, width)
-        for part, width in ((ffn[:, :in_rows], 2 * FF), (ffn[:, in_rows:], D))
-    ]
-    gains = lax.all_gather(norm_gains, "section", axis=0, tiled=True)
+    down = both(down, section, "section", swap)
 
     rows = byte_states.shape[0] // sections
     mine = lambda a: lax.dynamic_slice_in_dim(a, section * rows, rows, 0)
@@ -253,7 +294,7 @@
     earlier = docs[:, None, :] < docs[:, :, None]
     doc_start = jnp.sum(jnp.where(earlier, lengths[:, None, :], 0), axis=2)
     doc_first = jnp.sum(earlier.astype(jnp.int32), axis=2)
-    cross = chunk_bounds(doc_start, ends, 256)
+    cross, cross_back = chunk_bounds(doc_start, ends, 256), chunk_bounds(doc_start, ends, 512)
     ids = jnp.broadcast_to(lax.iota(jnp.int32, PATCHES) + 1, doc_first.shape)
     causal = chunk_bounds(doc_first, ids, 128)
     positions = lax.iota(jnp.int32, ROW_BYTES)
@@ -270,7 +311,12 @@
     q1 = nn(query_in, wq[0]).astype(BF)
     k1 = nn(key_in, wk[0]).astype(BF)
     v1 = nn(key_in, wv[0]).astype(BF)
-    c1, l1 = attend(cross, q1, k1, v1)
+    v1, down = together((v1, down))
+    down = both(down, side, "group", side_pairs)
+    c1, l1 = attend(cross, q1, k1, v1, 8)
+    c1, down = together((c1, down))
+    down = both(down, core, "group", core_pairs)
+    w_down = down.transpose(2, 3, 1, 0, 4, 5).reshape(FF, D)
     carried = (pooled + nn(c1, wo[0])).astype(BF)
 
     carried_wide = carried.astype(F32)
@@ -279,7 +325,7 @@
     q2 = nn(normed_in, wq[1]).astype(BF)
     k2 = nn(normed_in, wk[1]).astype(BF)
     v2 = nn(normed_in, wv[1]).astype(BF)
-    c2, l2 = attend(causal, q2, k2, v2)
+    c2, l2 = attend(causal, q2, k2, v2, 8, CAUSAL_SPANS)
     residual = carried_wide + nn(c2, wo[1])
     second_scale = scale_of(residual)
     mix_in = (residual * second_scale * gains[1, 1]).astype(BF)
@@ -294,10 +340,6 @@
     grad_up = grad_hidden * gate * sig
     dgu = jnp.concatenate([grad_gate, grad_up], axis=1).astype(BF)
 
-    core_pairs = [(0, 1), (1, 0), (2, 3), (3, 2)]
-    side_pairs = [(0, 2), (1, 3), (2, 0), (3, 1)]
-    swap = [(0, 1), (1, 0)]
-
     def exchanged(values, axis, part, pairs, where):
         size = values.shape[where] // 2
         other = lax.dynamic_slice_in_dim(values, (1 - part) * size, size, where)
@@ -327,8 +369,6 @@
     def of_chip(pairs, sent):
         got = lax.ppermute(sent, "group", core_pairs)
         return (products(pairs, core) + got.astype(F32)).astype(BF)
-
-    together = lax.optimization_barrier
 
     in_pairs, down_pairs = [(mix_in, dgu)], [(hidden, cot)]
     send_in, send_down = to_core(in_pairs), to_core(down_pairs)
@@ -340,7 +380,7 @@
     half_in, half_down = of_chip(in_pairs, send_in), of_chip(down_pairs, send_down)
     dc2, half_in, half_down = together((dc2, half_in, half_down))
 
-    dq2, dk2, dv2 = attend_back(causal, q2, k2, v2, l2, c2, dc2)
+    dq2, dk2, dv2 = attend_back(causal, q2, k2, v2, l2, c2, dc2, 8, CAUSAL_SPANS)
     two_pairs = [(normed_in, dq2), (normed_in, dk2), (normed_in, dv2), (c2, branch)]
     send_two = to_core(two_pairs)
     dq2, dk2, dv2, send_two = together((dq2, dk2, dv2, send_two))
@@ -354,7 +394,7 @@
     sum_down = over_side(over_section(line_sum(half_down.reshape(sections, -1, D // 2), 1), 0), 2)
     sum_down = sum_down[0]
 
-    dq1, dk1, dv1 = attend_back(cross, q1, k1, v1, l1, c1, dc1)
+    dq1, dk1, dv1 = attend_back(cross_back, q1, k1, v1, l1, c1, dc1, 4)
     half_in = over_side(half_in, 1)
     half_two = over_side(half_two, 2)
     one_pairs = [(query_in, dq1), (key_in, dk1)], [(key_in, dv1), (c1, d_carried)]

time: 819 us -> 728 us (0.89)
  Pallas kernels: 144 us -> 62.1 us
  local copies, waits for them, and re-layouts: 109 us -> 31 us
  waiting for transfers between devices: 267 us -> 295 us
  matrix products: 159 us -> 180 us
  starting transfers between devices: 17.3 us -> 28.1 us
  other arithmetic: 75.5 us -> 85 us
    pallas_call x4, Pallas kernels: 144 us -> 62.1 us  [the longest x2 41.9 us: attend_back(): pl.pallas_call(functools.partial(attend_back_kernel, chunk, spans), grid_...]
    transpose x2 -> x0, local copies, waits for them, and re-layouts: 39.4 us -> none  [shards(): part.reshape(part.shape[0], width // BLOCK, -1, BLOCK).swapaxes(1, 2)]
    unnamed x211 -> x185, local copies, waits for them, and re-layouts: 45.8 us -> 7.78 us
    ppermute x0 -> x6, waiting for transfers between devices: none -> 23 us  [the longest x3 23 us: both(): got = lax.ppermute(values, axis, pairs)]
    all_gather x1, waiting for transfers between devices: 27.8 us -> 7.96 us  [shards(): lax.all_gather(quarter_of(ffn_in), ('section', 'dp', 'group'), axis=0, ti...]
    ppermute x10, waiting for transfers between devices: 101 us -> 120 us  [exchanged(): lax.ppermute(other, axis, pairs).astype(F32)]
    dot_general x10, matrix products: 37.5 us -> 54.7 us  [nn(): return jnp.dot(left, right, preferred_element_type=F32)]
    ppermute x0 -> x6, starting transfers between devices: none -> 9.82 us  [the longest x3 6.96 us: shards(): lax.ppermute(quarter, 'dp', [(i, (i + step) % line) for i in range(line)])]
  transfers between devices with their start and end apart: 29 -> 35, of which waited for: 12 -> 13; matrix products, arithmetic and copies ran while one was open for 27% -> 35% of each run, Pallas kernels for 18% -> 9%
where the time goes in v4:
time: 728 us; the launch traced here: 723 us
  waiting for transfers between devices  295 us (41%)
  matrix products  180 us (25%)
  other arithmetic  85 us (12%)
  Pallas kernels  62.1 us (9%)
  local copies, waits for them, and re-layouts  31 us (4%)
  starting transfers between devices  28.1 us (4%)
  blocking collectives  25.9 us (4%)
  between operations  16.2 us (2%)
    ppermute x10, waiting for transfers between devices, exchanged(): lax.ppermute(other, axis, pairs).astype(F32)  120 us
    all_gather x1, waiting for transfers between devices, shards(): lax.all_gather(matrix, ('section', 'group', 'dp'), axis=0, tiled=True)  91.4 us
    dot_general x10, matrix products, nt(): lax.dot_general(left, right, (((1,), (1,)), ((), ())), preferred_element_...  61.5 us
    dot_general x20, matrix products, tn(): lax.dot_general(left, right, (((0,), (0,)), ((), ())), preferred_element_...  55.2 us
    dot_general x10, matrix products, nn(): return jnp.dot(left, right, preferred_element_type=F32)  54.7 us
    ppermute x1, waiting for transfers between devices, shards(): got = lax.ppermute(sent, 'section', swap)  47 us
    pallas_call x2, Pallas kernels, attend_back(): pl.pallas_call(functools.partial(attend_back_kernel, chunk, spans), grid_...  41.9 us
    ppermute x3, waiting for transfers between devices, both(): got = lax.ppermute(values, axis, pairs)  23 us
  transfers between devices with their start and end apart: 35, of which 13 were waited for; matrix products, arithmetic and copies ran while one was open for 35% of the time, Pallas kernels for 9%

profile of v4, /device:TPU:0, one launch (start us, length us, event | category | flops | bytes accessed | tf_op | source)
XLA Modules:
  0.0 723.4 jit_solution(1046856343567752204)
XLA Ops:
  23.2 4.4 all_gather.28
  30.8 3.8 multiply_reduce_fusion.5
  45.9 91.4 %all-gather.13.cloned.1.call-done = bf16[1,8192,1024]{2,1,0:T(8,128)(2,1)} async-done(((bf16[1,256,1024]{2,1,0:T(8,128)(2,1)}), bf16[1,8192,1024]{2,1,0:T(8,128)(2,1)}) %all-gather.13.cloned.1.call-update) | async-done | bytes 16777232 | tf_op jit(solution)/shard_map/all_gather | solution.py:264
  138.6 9.5 %convolution_convert_fusion.2.v_ref = bf16[2048,1024]{1,0:T(8,128)(2,1)} fusion(bf16[2048,1024]{1,0:T(8,128)(2,1)} %bitcast.249, bf16[2,4,1024,1024]{3,2,1,0:T(8,128)(2,1)} %bitcast.312), kind=kOutput, calls=%fused_computation.49 | convolution fusion | flops 4297064448 | bytes 10485760 | tf_op jit(solution)/shard_map/dot_general | solution.py:31
  148.1 10.3 %collective-permute-done.3 = bf16[4,88,1024]{2,1,0:T(8,128)(2,1)S(1)} collective-permute-done((bf16[4,88,1024]{2,1,0:T(8,128)(2,1)}, bf16[4,88,1024]{2,1,0:T(8,128)(2,1)S(1)}, u32[]{:S(2)}, u32[]{:S(2)}) %collective-permute-start.3) | collective-permute-done | bytes 720928 | tf_op jit(solution)/shard_map/ppermute | solution.py:274
  161.7 7.6 %convolution_convert_fusion.3.k_ref = bf16[2048,1024]{1,0:T(8,128)(2,1)} fusion(bf16[2048,1024]{1,0:T(8,128)(2,1)S(1)} %bitcast.250, bf16[2,4,1024,1024]{3,2,1,0:T(8,128)(2,1)} %bitcast.313), kind=kOutput, calls=%fused_computation.50 | convolution fusion | flops 4297064448 | bytes 10485760 | tf_op jit(solution)/shard_map/dot_general | solution.py:31
  172.1 16.2 %attend.2 = (bf16[512,1024]{1,0:T(8,128)(2,1)S(1)}, f32[2,8,2,256]{3,2,1,0:T(2,128)S(1)}) custom-call(s32[2,2]{1,0:T(2,128)S(1)} %get-tuple-element.160.first_ref, s32[2,2]{1,0:T(2,128)S(1)} %get-tuple-element.143.stop_ref, s32[2,1,256]{2,1,0:T(1,128)S(1)} %broadcast_in_dim.73.lo_ref, s32[2,1,256]{2,1,0:T(1,128)S(1)} %bitcast.237, ...), custom_call_target="tpu_custom_call" | custom-call | flops 8589934592 | bytes 18874368 | tf_op jit(solution)/shard_map/attend/pallas_call | solution.py:186
  188.3 12.7 %collective-permute-done.4 = bf16[2,4,88,1024]{3,2,1,0:T(8,128)(2,1)S(1)} collective-permute-done((bf16[2,4,88,1024]{3,2,1,0:T(8,128)(2,1)S(1)}, bf16[2,4,88,1024]{3,2,1,0:T(8,128)(2,1)S(1)}, u32[]{:S(2)}, u32[]{:S(2)}) %collective-permute-start.4) | collective-permute-done | bytes 1441824 | tf_op jit(solution)/shard_map/ppermute | solution.py:274
  213.2 3.3 fusion.70.v_ref
  216.5 4.0 attend.3
  220.6 3.3 multiply_reduce_fusion.4
  226.5 8.0 %all-gather.9.cloned.1.call-done = bf16[1024,5632]{1,0:T(8,128)(2,1)} async-done(((bf16[32,5632]{1,0:T(8,128)(2,1)}), bf16[1024,5632]{1,0:T(8,128)(2,1)}) %all-gather.9.cloned.1.call-update) | async-done | bytes 11534352 | tf_op jit(solution)/shard_map/all_gather | solution.py:270
  234.5 11.8 %fusion.153 = f32[512,5632]{1,0:T(8,128)} fusion(bf16[512,1024]{1,0:T(8,128)(2,1)} %multiply_convert_fusion.4, bf16[1024,5632]{1,0:T(8,128)(2,1)} %all-gather.9.cloned.1.call-done), kind=kOutput, calls=%fused_computation.315 | convolution fusion | flops 5905580032 | bytes 24117248 | tf_op jit(solution)/shard_map/dot_general | solution.py:31
  246.2 5.2 maximum_select_fusion
  251.4 11.5 %multiply_convert_fusion.1 = (bf16[512,2816]{1,0:T(8,128)(2,1)S(1)}, bf16[512,2816]{1,0:T(8,128)(2,1)S(1)}, bf16[512,2816]{1,0:T(8,128)(2,1)}) fusion(f32[512,5632]{1,0:T(8,128)} %fusion.153, bf16[512,1024]{1,0:T(8,128)(2,1)S(1)} %bitcast.251, bf16[2816,1024]{1,0:T(8,128)(2,1)S(1)} %bitcast.246), kind=kOutput, calls=%fused_computation.30 | convolution fusion | flops 2975858688 | bytes 27000832 | tf_op jit(solution)/shard_map/dot_general | solution.py:39
  267.3 5.2 convolution_convert_fusion
  272.5 3.3 convolution_convert_fusion.1
  276.7 4.4 fusion.6
  281.1 6.9 add_convert_fusion.8
  289.9 10.1 %multiply_reduce_fusion = (f32[1024]{0:T(1024)}, f32[512]{0:T(512)S(1)}, f32[512,1024]{1,0:T(8,128)S(1)}) fusion(f32[512,1024]{1,0:T(8,128)S(1)} %copy-done.32, f32[512]{0:T(512)S(1)} %get-tuple-element.139, f32[1024]{0:T(1024)S(1)} %bitcast.280, bf16[512,5632]{1,0:T(8,128)(2,1)S(1)} %bitcast.245, bf16[1024,5632]{1,0:T(8,128)(2,1)} %all-gather.9.cloned.1.call-done), kind=kOutput, calls=%fused_computation.82 | convolution fusion | flops 5908724224 | bytes 21508096 | tf_op jit(solution)/shard_map/dot_general | solution.py:39
  305.8 4.0 fusion.69.dc_ref
  309.9 5.3 add_convert_fusion.2
  315.3 6.1 add_convert_fusion
  321.4 13.6 %attend_back.2 = (bf16[512,1024]{1,0:T(8,128)(2,1)S(1)}, bf16[512,1024]{1,0:T(8,128)(2,1)S(1)}, bf16[512,1024]{1,0:T(8,128)(2,1)S(1)}) custom-call(s32[2,2]{1,0:T(2,128)S(1)} %get-tuple-element.163.first_ref, s32[2,2]{1,0:T(2,128)S(1)} %get-tuple-element.162.stop_ref, s32[2,1,256]{2,1,0:T(1,128)S(1)} %broadcast_in_dim.83.lo_ref, ...), custom_call_target="tpu_custom_call" | custom-call | flops 5368709120 | bytes 6291456 | tf_op jit(solution)/shard_map/attend_back/pallas_call | solution.py:210
  343.8 4.2 fusion.45
  348.2 3.3 fusion.47
  351.5 4.5 fusion.30
  365.3 42.2 %collective-permute-done.9 = bf16[512,2816]{1,0:T(8,128)(2,1)} collective-permute-done((bf16[512,2816]{1,0:T(8,128)(2,1)}, bf16[512,2816]{1,0:T(8,128)(2,1)}, u32[]{:S(2)}, u32[]{:S(2)}) %collective-permute-start.9) | collective-permute-done | bytes 2883616 | tf_op jit(solution)/shard_map/ppermute | solution.py:347
  409.9 3.3 fusion
  418.1 28.2 %attend_back.3 = (bf16[512,1024]{1,0:T(8,128)(2,1)S(1)}, bf16[2048,1024]{1,0:T(8,128)(2,1)}, bf16[2048,1024]{1,0:T(8,128)(2,1)}) custom-call(s32[2,2]{1,0:T(2,128)S(1)} %get-tuple-element.161.first_ref, s32[2,2]{1,0:T(2,128)S(1)} %get-tuple-element.142.stop_ref, s32[2,1,256]{2,1,0:T(1,128)S(1)} %broadcast_in_dim.73.lo_ref, s32[2,1,256]{2,1,0:T(1,128)S(1)} %bitcast.238, ...), custom_call_target="tpu_custom_call" | custom-call | flops 21474836480 | bytes 18874368 | tf_op jit(solution)/shard_map/attend_back/pallas_call | solution.py:210
  447.2 4.0 fusion.78
  459.4 33.1 %collective-permute-done.12 = bf16[4,1024,256]{2,1,0:T(8,128)(2,1)} collective-permute-done((bf16[4,1024,256]{2,1,0:T(8,128)(2,1)}, bf16[4,1024,256]{2,1,0:T(8,128)(2,1)}, u32[]{:S(2)}, u32[]{:S(2)}) %collective-permute-start.12) | collective-permute-done | bytes 2097184 | tf_op jit(solution)/shard_map/ppermute | solution.py:347
  492.5 4.1 add_convert_fusion.3
  502.8 5.3 fusion.57
  512.6 6.6 fusion.60
  522.9 19.2 %collective-permute-done.20 = bf16[4,1024,128]{2,1,0:T(8,128)(2,1)S(1)} collective-permute-done((bf16[4,1024,128]{2,1,0:T(8,128)(2,1)S(1)}, bf16[4,1024,128]{2,1,0:T(8,128)(2,1)S(1)}, u32[]{:S(2)}, u32[]{:S(2)}) %collective-permute-start.20) | collective-permute-done | bytes 1048608 | tf_op jit(solution)/shard_map/ppermute | solution.py:347
  543.6 3.7 fusion.12
  557.5 20.5 %collective-permute-done.18 = bf16[2,1024,256]{2,1,0:T(8,128)(2,1)S(1)} collective-permute-done((bf16[2,1024,256]{2,1,0:T(8,128)(2,1)S(1)}, bf16[2,1024,256]{2,1,0:T(8,128)(2,1)S(1)}, u32[]{:S(2)}, u32[]{:S(2)}) %collective-permute-start.18) | collective-permute-done | bytes 1048608 | tf_op jit(solution)/shard_map/ppermute | solution.py:347
  581.5 4.6 fusion.53
  586.1 4.3 collective-permute-done.19
  592.9 7.1 fusion.42
  600.1 10.2 %fusion.11 = (f32[1024]{0:T(1024)S(1)}, f32[2048]{0:T(1024)S(1)}, f32[2048,1024]{1,0:T(8,128)}) fusion(f32[2048]{0:T(1024)S(1)} %bitcast.268, bf16[4,1024,1024]{2,1,0:T(8,128)(2,1)} %param.9, s32[]{:T(128)S(6)} %select_n.245, f32[1024]{0:T(1024)S(1)} %bitcast.272, f32[2048,1024]{1,0:T(8,128)S(1)} %fusion.42, bf16[2048,1024]{1,0:T(8,128)(2,1)S(1)} %copy-done.43, ...), kind=kOutput, calls=%fused_computation.20 | convolution fusion | flops 4311741440 | bytes 27287556 | tf_op jit(solution)/shard_map/dot_general | solution.py:39
  610.7 8.3 %fusion.1 = bf16[2048,1024]{1,0:T(8,128)(2,1)S(1)} fusion(f32[2,1024,1024]{2,1,0:T(8,128)} %fusion.53, f32[2048,1024]{1,0:T(8,128)} %get-tuple-element.159, f32[2048]{0:T(1024)S(1)} %broadcast_multiply_fusion, f32[2048]{0:T(1024)S(1)} %copy-done.63, f32[1024]{0:T(1024)S(1)} %bitcast.273, f32[2048]{0:T(1024)S(1)} %bitcast.269, ...), kind=kLoop, calls=%fused_computation.4 | loop fusion | flops 16777216 | bytes 25194500 | tf_op jit(solution)/shard_map/convert_element_type | solution.py:419
  624.2 47.0 %collective-permute-done.21 = bf16[4,256,128]{2,1,0:T(8,128)(2,1)S(1)} collective-permute-done((bf16[4,256,128]{2,1,0:T(8,128)(2,1)S(1)}, bf16[4,256,128]{2,1,0:T(8,128)(2,1)S(1)}, u32[]{:S(2)}, u32[]{:S(2)}) %collective-permute-start.21) | collective-permute-done | bytes 262176 | tf_op jit(solution)/shard_map/ppermute | solution.py:446
  672.2 8.3 %all_gather.36 = bf16[4,352,256]{2,1,0:T(8,128)(2,1)S(1)} all-gather(bf16[1,352,256]{2,1,0:T(8,128)(2,1)S(1)} %add_convert_fusion.13), channel_id=1, replica_groups=mesh['section'=2,'group'=4,'dp'=4] {'group'}, dimensions={0}, use_global_device_ids=true | all-gather | bytes 901120 | tf_op jit(solution)/shard_map/all_gather | solution.py:436
  681.1 3.5 collective-permute-done.23
  688.5 13.1 %all-gather.3 = f32[4,4,1024]{2,1,0:T(4,128)S(1)} all-gather(f32[1,4,1024]{2,1,0:T(4,128)S(1)} %add_bitcast_fusion), channel_id=3, replica_groups=mesh['section'=2,'group'=4,'dp'=4] {'dp'}, dimensions={0}, use_global_device_ids=true | all-gather | bytes 81920 | tf_op jit(solution)/shard_map/all_gather | solution.py:460
  702.3 3.9 maximum_select_fusion.1
  (372 shorter events, 152.7 us)
Async XLA Ops:
  7.2 34.7 %copy-start = (bf16[4,256,1024]{2,1,0:T(8,128)(2,1)S(1)}, bf16[4,256,1024]{2,1,0:T(8,128)(2,1)}, u32[]{:S(2)}) copy-start(bf16[4,256,1024]{2,1,0:T(8,128)(2,1)} %param.17) | copy-start | bytes 6291460
  7.2 130.2 %all-gather.13.cloned.1.call-start = ((), (), s32[]{:S(2)}) async-start(), calls=%async_computation.10 | async-start | bytes 17301504 | tf_op jit(solution)/shard_map/all_gather | solution.py:264
  9.4 225.0 %all-gather.9.cloned.1.call-start = ((), (), s32[]{:S(2)}) async-start(), calls=%async_computation.4 | async-start | bytes 11894784 | tf_op jit(solution)/shard_map/all_gather | solution.py:270
  11.3 496.9 %reduce-scatter.11.cloned.1.call-start = ((), (), s32[]{:S(2)}) async-start(), calls=%async_computation.9 | async-start | bytes 3604480 | tf_op jit(solution)/shard_map/reduce_scatter | solution.py:360
  13.9 28.1 %collective-permute-start = (bf16[88,1024]{1,0:T(8,128)(2,1)S(1)}, bf16[88,1024]{1,0:T(8,128)(2,1)}, u32[]{:S(2)}, u32[]{:S(2)}) collective-permute-start(bf16[88,1024]{1,0:T(8,128)(2,1)S(1)} %get-tuple-element.102), channel_id=1, source_target_pairs={{0,1},{1,2},{2,3},{3,0},{4,5},{5,6},{6,7},{7,4},{8,9},{9,10},{10,1... | collective-permute-start | bytes 540680 | tf_op jit(solution)/shard_map/ppermute | solution.py:281
  16.9 26.7 %collective-permute-start.1 = (bf16[88,1024]{1,0:T(8,128)(2,1)S(1)}, bf16[88,1024]{1,0:T(8,128)(2,1)}, u32[]{:S(2)}, u32[]{:S(2)}) collective-permute-start(bf16[88,1024]{1,0:T(8,128)(2,1)S(1)} %get-tuple-element.102), channel_id=1, source_target_pairs={{0,2},{1,3},{2,0},{3,1},{4,6},{5,7},{6,4},{7,5},{8,10},{9,11},{10,... | collective-permute-start | bytes 540680 | tf_op jit(solution)/shard_map/ppermute | solution.py:281
  19.5 25.7 %collective-permute-start.2 = (bf16[88,1024]{1,0:T(8,128)(2,1)S(1)}, bf16[88,1024]{1,0:T(8,128)(2,1)S(1)}, u32[]{:S(2)}, u32[]{:S(2)}) collective-permute-start(bf16[88,1024]{1,0:T(8,128)(2,1)S(1)} %get-tuple-element.102), channel_id=1, source_target_pairs={{0,3},{1,0},{2,1},{3,2},{4,7},{5,4},{6,5},{7,6},{8,11},{9,8},{10,9... | collective-permute-start | bytes 540680 | tf_op jit(solution)/shard_map/ppermute | solution.py:281
  36.0 240.7 %copy-start.56 = (f32[1,1,1024]{2,1,0:T(1,128)}, f32[1,1,1024]{2,1,0:T(1,128)S(1)}, u32[]{:S(2)}) copy-start(f32[1,1,1024]{2,1,0:T(1,128)S(1)} %get-tuple-element.130) | copy-start | bytes 12292
  137.4 21.1 %collective-permute-start.3 = (bf16[4,88,1024]{2,1,0:T(8,128)(2,1)}, bf16[4,88,1024]{2,1,0:T(8,128)(2,1)S(1)}, u32[]{:S(2)}, u32[]{:S(2)}) collective-permute-start(bf16[4,88,1024]{2,1,0:T(8,128)(2,1)} %bitcast_dynamic-update-slice_fusion), channel_id=1, source_target_pairs={{0,16},{16,0},{1,17},{17,1},{2,18},{18,2},{3,19},{19,3},{4,20},{20... | collective-permute-start | bytes 2162696 | tf_op jit(solution)/shard_map/ppermute | solution.py:274
  138.6 23.1 %copy-start.35 = (bf16[2,1024,1024]{2,1,0:T(8,128)(2,1)S(1)}, bf16[2,1024,1024]{2,1,0:T(8,128)(2,1)}, u32[]{:S(2)}) copy-start(bf16[2,1024,1024]{2,1,0:T(8,128)(2,1)} %fusion.4) | copy-start | bytes 12582916
  160.1 40.9 %collective-permute-start.4 = (bf16[2,4,88,1024]{3,2,1,0:T(8,128)(2,1)S(1)}, bf16[2,4,88,1024]{3,2,1,0:T(8,128)(2,1)S(1)}, u32[]{:S(2)}, u32[]{:S(2)}) collective-permute-start(bf16[2,4,88,1024]{3,2,1,0:T(8,128)(2,1)S(1)} %maximum_select_fusion.3), channel_id=1, source_target_pairs={{0,8},{4,12},{8,0},{12,4},{1,9},{5,13},{9,1},{13,5},{2,10},{6,14},... | collective-permute-start | bytes 4325384 | tf_op jit(solution)/shard_map/ppermute | solution.py:274
  203.1 43.1 %collective-permute-start.5 = (bf16[2,2,4,88,1024]{4,3,0,2,1:T(8,128)(2,1)}, bf16[2,2,4,88,1024]{4,3,0,2,1:T(8,128)(2,1)}, u32[]{:S(2)}, u32[]{:S(2)}) collective-permute-start(bf16[2,2,4,88,1024]{4,3,0,2,1:T(8,128)(2,1)} %maximum_select_fusion.2), channel_id=1, source_target_pairs={{0,4},{4,0},{8,12},{12,8},{1,5},{5,1},{9,13},{13,9},{2,6},{6,2},{1... | collective-permute-start | bytes 8650760 | tf_op jit(solution)/shard_map/ppermute | solution.py:274
  220.6 83.2 %copy-start.7 = (bf16[512,1024]{1,0:T(8,128)(2,1)}, bf16[512,1024]{1,0:T(8,128)(2,1)S(1)}, u32[]{:S(2)}) copy-start(bf16[512,1024]{1,0:T(8,128)(2,1)S(1)} %get-tuple-element.54.c_ref) | copy-start | bytes 3145732
  275.7 39.5 %collective-permute-start.7 = (bf16[1024,2816]{1,0:T(8,128)(2,1)}, bf16[1024,2816]{1,0:T(8,128)(2,1)}, u32[]{:S(2)}, u32[]{:S(2)}) collective-permute-start(bf16[1024,2816]{1,0:T(8,128)(2,1)} %convolution_convert_fusion), channel_id=1, source_target_pairs={{0,4},{4,0},{8,12},{12,8},{1,5},{5,1},{9,13},{13,9},{2,6},{6,2},{1... | collective-permute-start | bytes 17301512 | tf_op jit(solution)/shard_map/ppermute | solution.py:370
  276.0 274.4 %copy-start.58 = (f32[1,2,2,128]{3,1,2,0:T(2,128)}, f32[1,2,2,128]{3,1,2,0:T(2,128)S(1)}, u32[]{:S(2)}) copy-start(f32[1,2,2,128]{3,1,2,0:T(2,128)S(1)} %copy.30) | copy-start | bytes 6148
  288.9 207.7 %collective-permute-start.6 = (bf16[2,256,512]{2,1,0:T(8,128)(2,1)}, bf16[2,256,512]{2,1,0:T(8,128)(2,1)}, u32[]{:S(2)}, u32[]{:S(2)}) collective-permute-start(bf16[2,256,512]{2,1,0:T(8,128)(2,1)} %get-tuple-element.121), channel_id=1, source_target_pairs={{0,16},{16,0},{1,17},{17,1},{2,18},{18,2},{3,19},{19,3},{4,20},{20... | collective-permute-start | bytes 1572872 | tf_op jit(solution)/shard_map/ppermute | solution.py:427
  289.9 20.0 %collective-permute-start.8 = (bf16[2816,512]{1,0:T(8,128)(2,1)S(1)}, bf16[2816,512]{1,0:T(8,128)(2,1)}, u32[]{:S(2)}, u32[]{:S(2)}) collective-permute-start(bf16[2816,512]{1,0:T(8,128)(2,1)S(1)} %copy-done.77), channel_id=1, source_target_pairs={{0,4},{4,0},{8,12},{12,8},{1,5},{5,1},{9,13},{13,9},{2,6},{6,2},{1... | collective-permute-start | bytes 8650760 | tf_op jit(solution)/shard_map/ppermute | solution.py:370
  321.4 19.6 %copy-start.17 = (bf16[1024,2816]{1,0:T(8,128)(2,1)}, bf16[1024,2816]{1,0:T(8,128)(2,1)S(1)}, u32[]{:S(2)}) copy-start(bf16[1024,2816]{1,0:T(8,128)(2,1)S(1)} %add_convert_fusion) | copy-start | bytes 17301508
  340.4 69.5 %collective-permute-start.10 = (bf16[4,1024,512]{2,1,0:T(8,128)(2,1)}, bf16[4,1024,512]{2,1,0:T(8,128)(2,1)}, u32[]{:S(2)}, u32[]{:S(2)}) collective-permute-start(bf16[4,1024,512]{2,1,0:T(8,128)(2,1)} %pad_maximum_fusion.1), channel_id=1, source_target_pairs={{0,4},{4,0},{8,12},{12,8},{1,5},{5,1},{9,13},{13,9},{2,6},{6,2},{1... | collective-permute-start | bytes 12582920 | tf_op jit(solution)/shard_map/ppermute | solution.py:370
  342.7 64.7 %collective-permute-start.9 = (bf16[512,2816]{1,0:T(8,128)(2,1)}, bf16[512,2816]{1,0:T(8,128)(2,1)}, u32[]{:S(2)}, u32[]{:S(2)}) collective-permute-start(bf16[512,2816]{1,0:T(8,128)(2,1)} %constant_dynamic-slice_fusion.12), channel_id=1, source_target_pairs={{0,16},{16,0},{1,17},{17,1},{2,18},{18,2},{3,19},{19,3},{4,20},{20... | collective-permute-start | bytes 8650760 | tf_op jit(solution)/shard_map/ppermute | solution.py:347
  348.1 262.3 %reduce-scatter.9.cloned.1.call-start = ((), (), s32[]{:S(2)}) async-start(), calls=%async_computation.8 | async-start | bytes 1802240 | tf_op jit(solution)/shard_map/reduce_scatter | solution.py:360
  361.1 46.3 %slice-start.2 = ((s8[5767168]{0:T(1024)(128)(4,1)}), s8[4194304]{0:T(1024)(128)(4,1)S(1)}, s32[]{:S(2)}) async-start(s8[5767168]{0:T(1024)(128)(4,1)} %bitcast.241), calls=%async_computation.14 | async-start | bytes 8388608
  362.0 45.4 %slice-start.3 = ((s8[5767168]{0:T(1024)(128)(4,1)}), s8[1572864]{0:T(1024)(128)(4,1)S(1)}, s32[]{:S(2)}) async-start(s8[5767168]{0:T(1024)(128)(4,1)} %bitcast.241), calls=%async_computation.15 | async-start | bytes 3145728
  365.3 44.7 %copy-start.41 = (f32[1,1024,512]{2,1,0:T(8,128)S(1)}, f32[1,1024,512]{2,1,0:T(8,128)}, u32[]{:S(2)}) copy-start(f32[1,1024,512]{2,1,0:T(8,128)} %convolution_bitcast_fusion.2) | copy-start | bytes 6291460
  414.6 43.4 %collective-permute-start.11 = (bf16[512,1408]{1,0:T(8,128)(2,1)}, bf16[512,1408]{1,0:T(8,128)(2,1)S(1)}, u32[]{:S(2)}, u32[]{:S(2)}) collective-permute-start(bf16[512,1408]{1,0:T(8,128)(2,1)} %constant_dynamic-slice_fusion.11), channel_id=1, source_target_pairs={{0,8},{4,12},{8,0},{12,4},{1,9},{5,13},{9,1},{13,5},{2,10},{6,14},... | collective-permute-start | bytes 4325384 | tf_op jit(solution)/shard_map/ppermute | solution.py:347
  417.2 75.3 %collective-permute-start.12 = (bf16[4,1024,256]{2,1,0:T(8,128)(2,1)}, bf16[4,1024,256]{2,1,0:T(8,128)(2,1)}, u32[]{:S(2)}, u32[]{:S(2)}) collective-permute-start(bf16[4,1024,256]{2,1,0:T(8,128)(2,1)} %constant_dynamic-slice_fusion.10), channel_id=1, source_target_pairs={{0,8},{4,12},{8,0},{12,4},{1,9},{5,13},{9,1},{13,5},{2,10},{6,14},... | collective-permute-start | bytes 6291464 | tf_op jit(solution)/shard_map/ppermute | solution.py:347
  418.1 28.2 %copy-start.21 = (f32[512,1024]{1,0:T(8,128)S(1)}, f32[512,1024]{1,0:T(8,128)}, u32[]{:S(2)}) copy-start(f32[512,1024]{1,0:T(8,128)} %bitcast_divide_fusion) | copy-start | bytes 6291460
  418.1 28.2 %copy-start.52 = (f32[1,1,1024]{2,1,0:T(1,128)S(1)}, f32[1,1,1024]{2,1,0:T(1,128)}, u32[]{:S(2)}) copy-start(f32[1,1,1024]{2,1,0:T(1,128)} %copy-done.51) | copy-start | bytes 12292
  418.1 29.1 %copy-start.15 = (bf16[2048,1024]{1,0:T(8,128)(2,1)S(1)}, bf16[2048,1024]{1,0:T(8,128)(2,1)}, u32[]{:S(2)}) copy-start(bf16[2048,1024]{1,0:T(8,128)(2,1)} %fusion.6) | copy-start | bytes 12582916
  496.6 125.3 %reduce-scatter.7.cloned.1.call-start = ((), (), s32[]{:S(2)}) async-start(), calls=%async_computation.6 | async-start | bytes 1310720 | tf_op jit(solution)/shard_map/reduce_scatter | solution.py:360
  502.3 41.3 %collective-permute-start.13 = (bf16[2,1024,512]{2,1,0:T(8,128)(2,1)}, bf16[2,1024,512]{2,1,0:T(8,128)(2,1)}, u32[]{:S(2)}, u32[]{:S(2)}) collective-permute-start(bf16[2,1024,512]{2,1,0:T(8,128)(2,1)} %pad_maximum_fusion.2), channel_id=1, source_target_pairs={{0,4},{4,0},{8,12},{12,8},{1,5},{5,1},{9,13},{13,9},{2,6},{6,2},{1... | collective-permute-start | bytes 6291464 | tf_op jit(solution)/shard_map/ppermute | solution.py:370
  502.3 45.1 %collective-permute-start.14 = (bf16[2,1024,512]{2,1,0:T(8,128)(2,1)}, bf16[2,1024,512]{2,1,0:T(8,128)(2,1)}, u32[]{:S(2)}, u32[]{:S(2)}) collective-permute-start(bf16[2,1024,512]{2,1,0:T(8,128)(2,1)} %pad_maximum_fusion.3), channel_id=1, source_target_pairs={{0,4},{4,0},{8,12},{12,8},{1,5},{5,1},{9,13},{13,9},{2,6},{6,2},{1... | collective-permute-start | bytes 6291464 | tf_op jit(solution)/shard_map/ppermute | solution.py:370
  509.2 12.3 %collective-permute-start.25 = (bf16[1,352,512]{2,1,0:T(8,128)(2,1)S(1)}, bf16[1,352,512]{2,1,0:T(8,128)(2,1)S(1)}, u32[]{:S(2)}, u32[]{:S(2)}) collective-permute-start(bf16[1,352,512]{2,1,0:T(8,128)(2,1)S(1)} %constant_dynamic-slice_fusion.1), channel_id=1, source_target_pairs={{0,16},{16,0},{1,17},{17,1},{2,18},{18,2},{3,19},{19,3},{4,20},{20... | collective-permute-start | bytes 1081352 | tf_op jit(solution)/shard_map/ppermute | solution.py:347
  511.7 30.4 %collective-permute-start.20 = (bf16[4,1024,128]{2,1,0:T(8,128)(2,1)S(1)}, bf16[4,1024,128]{2,1,0:T(8,128)(2,1)S(1)}, u32[]{:S(2)}, u32[]{:S(2)}) collective-permute-start(bf16[4,1024,128]{2,1,0:T(8,128)(2,1)S(1)} %constant_dynamic-slice_fusion.3), channel_id=1, source_target_pairs={{0,16},{16,0},{1,17},{17,1},{2,18},{18,2},{3,19},{19,3},{4,20},{20... | collective-permute-start | bytes 3145736 | tf_op jit(solution)/shard_map/ppermute | solution.py:347
  519.2 22.8 %copy-start.29 = (bf16[4,1024,256]{2,1,0:T(8,128)(2,1)S(1)}, bf16[4,1024,256]{2,1,0:T(8,128)(2,1)}, u32[]{:S(2)}) copy-start(bf16[4,1024,256]{2,1,0:T(8,128)(2,1)} %add_convert_fusion.3) | copy-start | bytes 6291460
  521.6 102.4 %collective-permute-start.26 = (bf16[1,352,256]{2,1,0:T(8,128)(2,1)S(1)}, bf16[1,352,256]{2,1,0:T(8,128)(2,1)S(1)}, u32[]{:S(2)}, u32[]{:S(2)}) collective-permute-start(bf16[1,352,256]{2,1,0:T(8,128)(2,1)S(1)} %constant_dynamic-slice_fusion), channel_id=1, source_target_pairs={{0,8},{4,12},{8,0},{12,4},{1,9},{5,13},{9,1},{13,5},{2,10},{6,14},... | collective-permute-start | bytes 540680 | tf_op jit(solution)/shard_map/ppermute | solution.py:347
  543.3 78.5 %reduce-scatter.5.cloned.1.call-start = ((), (), s32[]{:S(2)}) async-start(), calls=%async_computation.5 | async-start | bytes 1310720 | tf_op jit(solution)/shard_map/reduce_scatter | solution.py:360
  553.8 24.2 %collective-permute-start.18 = (bf16[2,1024,256]{2,1,0:T(8,128)(2,1)S(1)}, bf16[2,1024,256]{2,1,0:T(8,128)(2,1)S(1)}, u32[]{:S(2)}, u32[]{:S(2)}) collective-permute-start(bf16[2,1024,256]{2,1,0:T(8,128)(2,1)S(1)} %constant_dynamic-slice_fusion.5), channel_id=1, source_target_pairs={{0,8},{4,12},{8,0},{12,4},{1,9},{5,13},{9,1},{13,5},{2,10},{6,14},... | collective-permute-start | bytes 3145736 | tf_op jit(solution)/shard_map/ppermute | solution.py:347
  555.1 24.5 %collective-permute-start.16 = (bf16[2,1024,256]{2,1,0:T(8,128)(2,1)S(1)}, bf16[2,1024,256]{2,1,0:T(8,128)(2,1)S(1)}, u32[]{:S(2)}, u32[]{:S(2)}) collective-permute-start(bf16[2,1024,256]{2,1,0:T(8,128)(2,1)S(1)} %constant_dynamic-slice_fusion.7), channel_id=1, source_target_pairs={{0,16},{16,0},{1,17},{17,1},{2,18},{18,2},{3,19},{19,3},{4,20},{20... | collective-permute-start | bytes 3145736 | tf_op jit(solution)/shard_map/ppermute | solution.py:347
  578.4 12.0 %collective-permute-start.19 = (bf16[2,1024,128]{2,1,0:T(8,128)(2,1)S(1)}, bf16[2,1024,128]{2,1,0:T(8,128)(2,1)S(1)}, u32[]{:S(2)}, u32[]{:S(2)}) collective-permute-start(bf16[2,1024,128]{2,1,0:T(8,128)(2,1)S(1)} %constant_dynamic-slice_fusion.4), channel_id=1, source_target_pairs={{0,16},{16,0},{1,17},{17,1},{2,18},{18,2},{3,19},{19,3},{4,20},{20... | collective-permute-start | bytes 1572872 | tf_op jit(solution)/shard_map/ppermute | solution.py:347
  580.0 11.7 %collective-permute-start.17 = (bf16[2,1024,128]{2,1,0:T(8,128)(2,1)S(1)}, bf16[2,1024,128]{2,1,0:T(8,128)(2,1)S(1)}, u32[]{:S(2)}, u32[]{:S(2)}) collective-permute-start(bf16[2,1024,128]{2,1,0:T(8,128)(2,1)S(1)} %constant_dynamic-slice_fusion.6), channel_id=1, source_target_pairs={{0,8},{4,12},{8,0},{12,4},{1,9},{5,13},{9,1},{13,5},{2,10},{6,14},... | collective-permute-start | bytes 1572872 | tf_op jit(solution)/shard_map/ppermute | solution.py:347
  592.9 113.3 %all-gather.15.cloned.1.call-start = ((), (), s32[]{:S(2)}) async-start(), calls=%async_computation.11 | async-start | bytes 1802240 | tf_op jit(solution)/shard_map/all_gather | solution.py:436
  610.4 99.1 %all-gather.11.cloned.1.call-start = ((), (), s32[]{:S(2)}) async-start(), calls=%async_computation.7 | async-start | bytes 2621440 | tf_op jit(solution)/shard_map/all_gather | solution.py:436
  620.9 81.5 %collective-permute-start.15 = (bf16[2,1024,512]{2,1,0:T(8,128)(2,1)}, bf16[2,1024,512]{2,1,0:T(8,128)(2,1)}, u32[]{:S(2)}, u32[]{:S(2)}) collective-permute-start(bf16[2,1024,512]{2,1,0:T(8,128)(2,1)} %get-tuple-element.109), channel_id=1, source_target_pairs={{0,16},{16,0},{1,17},{17,1},{2,18},{18,2},{3,19},{19,3},{4,20},{20... | collective-permute-start | bytes 6291464 | tf_op jit(solution)/shard_map/ppermute | solution.py:427
  622.9 48.3 %collective-permute-start.21 = (bf16[4,256,128]{2,1,0:T(8,128)(2,1)S(1)}, bf16[4,256,128]{2,1,0:T(8,128)(2,1)S(1)}, u32[]{:S(2)}, u32[]{:S(2)}) collective-permute-start(bf16[4,256,128]{2,1,0:T(8,128)(2,1)S(1)} %get-tuple-element.127), channel_id=1, source_target_pairs={{0,16},{16,0},{1,17},{17,1},{2,18},{18,2},{3,19},{19,3},{4,20},{20... | collective-permute-start | bytes 786440 | tf_op jit(solution)/shard_map/ppermute | solution.py:446
  624.2 56.4 %collective-permute-start.22 = (f32[4,1024]{1,0:T(4,128)S(1)}, f32[4,1024]{1,0:T(4,128)S(1)}, u32[]{:S(2)}, u32[]{:S(2)}) collective-permute-start(f32[4,1024]{1,0:T(4,128)S(1)} %pad_maximum_fusion.5), channel_id=1, source_target_pairs={{0,4},{4,0},{8,12},{12,8},{1,5},{5,1},{9,13},{13,9},{2,6},{6,2},{1... | collective-permute-start | bytes 49160 | tf_op jit(solution)/shard_map/ppermute | solution.py:459
  680.5 4.1 collective-permute-start.23
  684.7 3.8 collective-permute-start.24
  (74 other events, 420.3 us)
Sparse Core Ops, SparseCore 0:
  11.6 125.7 all-gather.12
  140.8 93.6 all-gather.8
  348.2 54.1 reduce-scatter.10
  496.7 31.7 reduce-scatter.8
  543.5 25.8 reduce-scatter.6
  593.0 25.5 reduce-scatter.4
  620.1 17.5 all-gather.14
  672.3 21.6 all-gather.10

commit v5 on v4

--- a/solution.py
+++ b/solution.py
@@ -263,16 +263,28 @@
     matrix = lax.dynamic_index_in_dim(four, group, 0, keepdims=False)
     matrices = lax.all_gather(matrix, ("section", "group", "dp"), axis=0, tiled=True)
 
+    gains = lax.all_gather(norm_gains, "section", axis=0, tiled=True)
+
     def quarter_of(shard):
         height = shard.shape[0] // groups
         return lax.dynamic_slice_in_dim(shard, group * height, height, 0)
 
-    w_in = lax.all_gather(quarter_of(ffn_in), ("section", "dp", "group"), axis=0, tiled=True)
-    gains = lax.all_gather(norm_gains, "section", axis=0, tiled=True)
+    def in_order(part, own, got):
+        return jnp.where(part == 0, jnp.stack([own, got]), jnp.stack([got, own]))
 
     def both(values, part, axis, pairs):
-        got = lax.ppermute(values, axis, pairs)
-        return jnp.where(part == 0, jnp.stack([values, got]), jnp.stack([got, values]))
+        return in_order(part, values, lax.ppermute(values, axis, pairs))
+
+    units = FF // sections
+
+    def of_units(values, part):
+        halves = [lax.dynamic_slice_in_dim(values, at + part * units, units, 1) for at in (0, FF)]
+        return jnp.concatenate(halves, axis=1)
+
+    quarter = quarter_of(ffn_in)
+    got = lax.ppermute(of_units(quarter, 1 - section), "section", swap)
+    w_in = in_order(section, of_units(quarter, section), got)
+    w_in = lax.all_gather(w_in, ("dp", "group"), axis=1, tiled=True).reshape(D, 2 * units)
 
     line, place = lax.axis_size("dp"), lax.axis_index("dp")
     quarter = quarter_of(ffn_down)
@@ -283,12 +295,15 @@
     matrices, down = together((matrices, down))
     matrices = matrices.reshape(sections, groups, D, D)
     wq, wk, wv, wo = [matrices[:, index] for index in range(4)]
-    down = both(down, section, "section", swap)
+    down = both(down, side, "group", side_pairs)
 
     rows = byte_states.shape[0] // sections
     mine = lambda a: lax.dynamic_slice_in_dim(a, section * rows, rows, 0)
     states, lengths, docs, cot = [mine(a) for a in (byte_states, patch_lengths, patch_docs, cotangent)]
-    cot = cot.reshape(rows * PATCHES, D)
+    tokens = rows * PATCHES
+    cot = cot.reshape(tokens, D)
+    other_cot = lax.dynamic_slice_in_dim(cotangent, (1 - section) * rows, rows, 0).reshape(tokens, D)
+    cots = jnp.concatenate([cot, other_cot], axis=0)
 
     ends = jnp.cumsum(lengths, axis=1)
     earlier = docs[:, None, :] < docs[:, :, None]
@@ -312,11 +327,10 @@
     k1 = nn(key_in, wk[0]).astype(BF)
     v1 = nn(key_in, wv[0]).astype(BF)
     v1, down = together((v1, down))
-    down = both(down, side, "group", side_pairs)
+    down = both(down, core, "group", core_pairs)
     c1, l1 = attend(cross, q1, k1, v1, 8)
     c1, down = together((c1, down))
-    down = both(down, core, "group", core_pairs)
-    w_down = down.transpose(2, 3, 1, 0, 4, 5).reshape(FF, D)
+    w_down = down.transpose(2, 1, 0, 3, 4).reshape(units, D)
     carried = (pooled + nn(c1, wo[0])).astype(BF)
 
     carried_wide = carried.astype(F32)
@@ -329,13 +343,13 @@
     residual = carried_wide + nn(c2, wo[1])
     second_scale = scale_of(residual)
     mix_in = (residual * second_scale * gains[1, 1]).astype(BF)
-    gate_up = nn(mix_in, w_in)
-    gate, up = gate_up[:, :FF], gate_up[:, FF:]
+    mixed = jnp.concatenate([mix_in, lax.ppermute(mix_in, "section", swap)], axis=0)
+    gate_up = nn(mixed, w_in)
+    gate, up = gate_up[:, :units], gate_up[:, units:]
     sig = jax.nn.sigmoid(gate)
     hidden = (gate * sig * up).astype(BF)
-    latents = (residual + nn(hidden, w_down)).astype(BF)
-
-    grad_hidden = nt(cot, w_down)
+
+    grad_hidden = nt(cots, w_down)
     grad_gate = grad_hidden * up * sig * (1.0 + gate * (1.0 - sig))
     grad_up = grad_hidden * gate * sig
     dgu = jnp.concatenate([grad_gate, grad_up], axis=1).astype(BF)
@@ -370,10 +384,24 @@
         got = lax.ppermute(sent, "group", core_pairs)
         return (products(pairs, core) + got.astype(F32)).astype(BF)
 
-    in_pairs, down_pairs = [(mix_in, dgu)], [(hidden, cot)]
+    in_pairs, down_pairs = [(mixed, dgu)], [(hidden, cots)]
+    mix_other = nt(dgu[tokens:], w_in).astype(BF)
     send_in, send_down = to_core(in_pairs), to_core(down_pairs)
-    dgu_next, send_in, send_down = together((dgu, send_in, send_down))
-    grad_mix, gain_mix = norm_backward(residual, second_scale, gains[1, 1], nt(dgu_next, w_in))
+    dgu_own, mix_other, send_in, send_down = together((dgu[:tokens], mix_other, send_in, send_down))
+    mix_got = lax.ppermute(mix_other, "section", swap)
+
+    half = D // sections
+    parts = nn(hidden, w_down)
+    parts = jnp.concatenate([residual + parts[:tokens], parts[tokens:]], axis=0)
+    sent = lax.dynamic_slice_in_dim(parts, (1 - section) * half, half, 1).astype(BF)
+    kept = lax.dynamic_slice_in_dim(parts, section * half, half, 1)
+    dgu_own, sent = together((dgu_own, sent))
+    got = lax.ppermute(sent, "section", swap).astype(F32)
+    latents = in_order(section, kept[:tokens] + got[tokens:], kept[tokens:] + got[:tokens])
+    latents_out = latents.astype(BF).reshape(sections * rows, PATCHES, half)
+
+    grad_mixed = nt(dgu_own, w_in) + mix_got.astype(F32)
+    grad_mix, gain_mix = norm_backward(residual, second_scale, gains[1, 1], grad_mixed)
     grad_residual = grad_mix + cot.astype(F32)
     branch = grad_residual.astype(BF)
     dc2 = nt(branch, wo[1]).astype(BF)
@@ -388,20 +416,21 @@
     grad_carried, gain_normed = norm_backward(carried_wide, first_scale, gains[1, 0], grad_normed)
     d_carried = (grad_residual + grad_carried).astype(BF)
     dc1 = nt(d_carried, wo[0]).astype(BF)
-    half_in = over_section(half_in, 0)
+    half_in = over_side(half_in.reshape(sections, line, 2, -1, units), 2)
     half_two = of_chip(two_pairs, send_two)
     dc1, half_in, half_two = together((dc1, half_in, half_two))
-    sum_down = over_side(over_section(line_sum(half_down.reshape(sections, -1, D // 2), 1), 0), 2)
-    sum_down = sum_down[0]
+    sum_down = over_side(line_sum(half_down, 0), 1)
+    sum_in = line_sum(half_in, 1).reshape(sections, -1, units)
+    sum_in = jnp.stack([lax.dynamic_index_in_dim(sum_in, section, 0, False),
+                        lax.ppermute(lax.dynamic_index_in_dim(sum_in, 1 - section, 0, False), "section", swap)])
+    sum_in = jnp.where(section == 0, sum_in, sum_in[::-1])
 
     dq1, dk1, dv1 = attend_back(cross_back, q1, k1, v1, l1, c1, dc1, 4)
-    half_in = over_side(half_in, 1)
-    half_two = over_side(half_two, 2)
+    half_two = over_section(half_two, 2)
     one_pairs = [(query_in, dq1), (key_in, dk1)], [(key_in, dv1), (c1, d_carried)]
     send_one = [to_core(pairs) for pairs in one_pairs]
-    dq1, dk1, dv1, send_one, half_in, half_two = together((dq1, dk1, dv1, send_one, half_in, half_two))
-    sum_in = line_sum(half_in, 0)
-    sum_two = line_sum(over_section(half_two, 2), 1)
+    dq1, dk1, dv1, send_one, half_two = together((dq1, dk1, dv1, send_one, half_two))
+    sum_two = line_sum(over_side(half_two, 2), 1)
     half_one = [of_chip(pairs, sent) for pairs, sent in zip(one_pairs, send_one)]
     dq1, dk1, dv1, half_one = together((dq1, dk1, dv1, half_one))
     half_one = jnp.concatenate(
@@ -418,19 +447,11 @@
     )
     byte_grads = (grad_wide + spread_back.reshape(rows * ROW_BYTES, D)).astype(BF)
 
-    half = D // sections
-
-    def halves(values, length):
-        values = values.reshape(rows, length, D)
-        other = lax.dynamic_slice_in_dim(values, (1 - section) * half, half, 2)
-        own = lax.dynamic_slice_in_dim(values, section * half, half, 2)
-        got = lax.ppermute(other, "section", swap)
-        return jnp.where(
-            section == 0, jnp.concatenate([own, got], axis=0), jnp.concatenate([got, own], axis=0)
-        )
-
-    latents_out = halves(latents, PATCHES)
-    bytes_out = halves(byte_grads, ROW_BYTES)
+    byte_grads = byte_grads.reshape(rows, ROW_BYTES, D)
+    other = lax.dynamic_slice_in_dim(byte_grads, (1 - section) * half, half, 2)
+    own = lax.dynamic_slice_in_dim(byte_grads, section * half, half, 2)
+    bytes_out = in_order(section, own, lax.ppermute(other, "section", swap))
+    bytes_out = bytes_out.reshape(sections * rows, ROW_BYTES, half)
 
     def of_group(part):
         every = lax.all_gather(part, "group", axis=0, tiled=False)
@@ -439,7 +460,12 @@
     def laid_out(parts, order):
         return jnp.concatenate([parts[index] for index in order], axis=-1).astype(F32)
 
-    ffn_gin, ffn_gdown = [laid_out(of_group(part), (0, 2, 1, 3)) for part in (sum_in, sum_down)]
+    ffn_gdown = laid_out(of_group(sum_down), (0, 2, 1, 3))
+    every = of_group(sum_in)
+    ffn_gin = jnp.concatenate(
+        [laid_out([every[at][t] for at in (2 * y, 2 * y + 1) for t in range(sections)], range(4)) for y in (0, 1)],
+        axis=0,
+    )
 
     kept = jnp.where(section == 0, sum_one, sum_two)
     sent = jnp.where(section == 0, sum_two, sum_one)
@@ -449,10 +475,10 @@
     )
     width = eighths.shape[2] // 2
     parts = [piece for every in of_group(eighths) for piece in (every[..., :width], every[..., width:])]
-    side_first = laid_out(parts, (0, 1, 4, 5, 2, 3, 6, 7))
-    section_first = laid_out([part[:2] for part in parts], (0, 4, 1, 5, 2, 6, 3, 7))
-    leading = jnp.where(section == 0, section_first, side_first[:2])
-    grad_qkv = jnp.concatenate([leading, side_first[2:3]], axis=0)[None]
+    section_first = laid_out(parts, (0, 4, 1, 5, 2, 6, 3, 7))
+    side_first = laid_out([part[2:] for part in parts], (0, 1, 4, 5, 2, 3, 6, 7))
+    last = jnp.where(section == 0, side_first, section_first[2:])
+    grad_qkv = jnp.concatenate([section_first[:2], last[:1]], axis=0)[None]
 
     gain_grads = jnp.stack([gain_query, gain_key, gain_normed, gain_mix])
     for axis, pairs in (("group", core_pairs), ("group", side_pairs), ("section", swap)):
@@ -461,7 +487,7 @@
     gain_grads = lax.dynamic_slice_in_dim(gain_grads.reshape(2, 2, D), section, 1, 0)
     width = D // lax.axis_size("dp")
     gain_out = lax.dynamic_slice_in_dim(gain_grads, lax.axis_index("dp") * width, width, 2)
-    return (latents_out, bytes_out, grad_qkv, side_first[3:], gain_out, ffn_gin, ffn_gdown)
+    return (latents_out, bytes_out, grad_qkv, last[1:], gain_out, ffn_gin, ffn_gdown)
 
 
 def solution(mesh):

time: 728 us -> 673 us (0.924)
  waiting for transfers between devices: 295 us -> 234 us
  other arithmetic: 85 us -> 96.1 us
    ppermute x10 -> x8, waiting for transfers between devices: 120 us -> 48.5 us  [exchanged(): lax.ppermute(other, axis, pairs).astype(F32)]
    ppermute x1, waiting for transfers between devices: 47 us -> 3.79 us  [shards(): got = lax.ppermute(sent, 'section', swap)]
    ppermute x5 -> x8, waiting for transfers between devices: 23 us -> 60 us  [the longest x1 18.3 us: shards(): lax.ppermute(mix_in, 'section', swap)]
    ppermute x3, waiting for transfers between devices: 5.55 us -> 33.1 us  [shards(): gain_grads = gain_grads + lax.ppermute(gain_grads, axis, pairs)]
    concatenate x0 -> x3, other arithmetic: none -> 9.52 us  [the longest x1 8.65 us: shards(): jnp.concatenate([laid_out([every[at][t] for at in (2 * y, 2 * y + 1) for...]
    all_gather x1, waiting for transfers between devices: 7.96 us -> 0.01 us  [shards(): lax.all_gather(w_in, ('dp', 'group'), axis=1, tiled=True)]
    dot_general x10 -> x11, matrix products: 61.5 us -> 59.6 us  [nt(): lax.dot_general(left, right, (((1,), (1,)), ((), ())), preferred_element_...]
  transfers between devices with their start and end apart: 35 -> 36, of which waited for: 13 -> 15; matrix products, arithmetic and copies ran while one was open for 35% -> 35% of each run, Pallas kernels for 9% -> 7%
where the time goes in v5:
time: 673 us; the launch traced here: 668 us
  waiting for transfers between devices  234 us (35%)
  matrix products  176 us (26%)
  other arithmetic  96.1 us (14%)
  Pallas kernels  60.1 us (9%)
  local copies, waits for them, and re-layouts  37.4 us (6%)
  blocking collectives  25.2 us (4%)
  starting transfers between devices  22.7 us (3%)
  between operations  16.4 us (2%)
    all_gather x1, waiting for transfers between devices, shards(): lax.all_gather(matrix, ('section', 'group', 'dp'), axis=0, tiled=True)  88.5 us
    dot_general x11, matrix products, nt(): lax.dot_general(left, right, (((1,), (1,)), ((), ())), preferred_element_...  59.6 us
    dot_general x20, matrix products, tn(): lax.dot_general(left, right, (((0,), (0,)), ((), ())), preferred_element_...  54.9 us
    dot_general x10, matrix products, nn(): return jnp.dot(left, right, preferred_element_type=F32)  53.4 us
    ppermute x8, waiting for transfers between devices, exchanged(): lax.ppermute(other, axis, pairs).astype(F32)  48.5 us
    pallas_call x2, Pallas kernels, attend_back(): pl.pallas_call(functools.partial(attend_back_kernel, chunk, spans), grid_...  39.7 us
    ppermute x3, waiting for transfers between devices, shards(): gain_grads = gain_grads + lax.ppermute(gain_grads, axis, pairs)  33.1 us
    pallas_call x2, Pallas kernels, attend(): pl.pallas_call(functools.partial(attend_kernel, chunk, spans), grid_spec=...  20.4 us
  transfers between devices with their start and end apart: 36, of which 15 were waited for; matrix products, arithmetic and copies ran while one was open for 35% of the time, Pallas kernels for 7%

profile of v5, /device:TPU:0, one launch (start us, length us, event | category | flops | bytes accessed | tf_op | source)
XLA Modules:
  0.0 668.2 jit_solution(12743900234099627291)
XLA Ops:
  22.7 4.4 all_gather.31
  27.1 3.7 multiply_reduce_fusion.5
  36.5 4.7 fusion.4
  45.1 88.5 %all-gather.14.cloned.1.call-done = bf16[1,8192,1024]{2,1,0:T(8,128)(2,1)} async-done(((bf16[1,256,1024]{2,1,0:T(8,128)(2,1)}), bf16[1,8192,1024]{2,1,0:T(8,128)(2,1)}) %all-gather.14.cloned.1.call-update) | async-done | bytes 16777232 | tf_op jit(solution)/shard_map/all_gather | solution.py:264
  135.1 9.5 %convolution_convert_fusion.1.v_ref = bf16[2048,1024]{1,0:T(8,128)(2,1)} fusion(bf16[2048,1024]{1,0:T(8,128)(2,1)} %bitcast.282, bf16[2,4,1024,1024]{3,2,1,0:T(8,128)(2,1)} %bitcast.351), kind=kOutput, calls=%fused_computation.52 | convolution fusion | flops 4297064448 | bytes 10485760 | tf_op jit(solution)/shard_map/dot_general | solution.py:31
  144.6 11.2 %collective-permute-done.3 = bf16[4,88,1024]{2,1,0:T(8,128)(2,1)S(1)} collective-permute-done((bf16[4,88,1024]{2,1,0:T(8,128)(2,1)S(1)}, bf16[4,88,1024]{2,1,0:T(8,128)(2,1)S(1)}, u32[]{:S(2)}, u32[]{:S(2)}) %collective-permute-start.3) | collective-permute-done | bytes 720928 | tf_op jit(solution)/shard_map/ppermute | solution.py:276
  156.0 7.7 %convolution_convert_fusion.2.k_ref = bf16[2048,1024]{1,0:T(8,128)(2,1)} fusion(bf16[2048,1024]{1,0:T(8,128)(2,1)S(1)} %bitcast.283, bf16[2,4,1024,1024]{3,2,1,0:T(8,128)(2,1)} %bitcast.352), kind=kOutput, calls=%fused_computation.53 | convolution fusion | flops 4297064448 | bytes 10485760 | tf_op jit(solution)/shard_map/dot_general | solution.py:31
  166.7 16.3 %attend.2 = (bf16[512,1024]{1,0:T(8,128)(2,1)S(1)}, f32[2,8,2,256]{3,2,1,0:T(2,128)S(1)}) custom-call(s32[2,2]{1,0:T(2,128)S(1)} %get-tuple-element.182.first_ref, s32[2,2]{1,0:T(2,128)S(1)} %get-tuple-element.165.stop_ref, s32[2,1,256]{2,1,0:T(1,128)S(1)} %broadcast_in_dim.73.lo_ref, s32[2,1,256]{2,1,0:T(1,128)S(1)} %bitcast.274, ...), custom_call_target="tpu_custom_call" | custom-call | flops 8589934592 | bytes 18874368 | tf_op jit(solution)/shard_map/attend/pallas_call | solution.py:186
  199.0 4.1 attend.3
  203.1 3.3 multiply_reduce_fusion.4
  211.0 4.1 fusion.6
  215.2 18.3 %collective-permute-done.5 = bf16[512,1024]{1,0:T(8,128)(2,1)} collective-permute-done((bf16[512,1024]{1,0:T(8,128)(2,1)}, bf16[512,1024]{1,0:T(8,128)(2,1)}, u32[]{:S(2)}, u32[]{:S(2)}) %collective-permute-start.5) | collective-permute-done | bytes 1048608 | tf_op jit(solution)/shard_map/ppermute | solution.py:346
  233.5 11.9 %fusion.110 = f32[1024,2816]{1,0:T(8,128)} fusion(bf16[1024,2816]{1,0:T(8,128)(2,1)} %bitcast.367, bf16[512,1024]{1,0:T(8,128)(2,1)} %collective-permute-done.5, bf16[512,1024]{1,0:T(8,128)(2,1)} %multiply_convert_fusion.4), kind=kOutput, calls=%fused_computation.197 | convolution fusion | flops 5909774336 | bytes 19398656 | tf_op jit(solution)/shard_map/dot_general | solution.py:31
  245.4 10.9 %multiply_convert_fusion = (bf16[1024,1408]{1,0:T(8,128)(2,1)S(1)}, bf16[1024,1408]{1,0:T(8,128)(2,1)S(1)}, bf16[1024,1408]{1,0:T(8,128)(2,1)}) fusion(f32[1024,2816]{1,0:T(8,128)} %fusion.110, bf16[1408,1024]{1,0:T(8,128)(2,1)S(1)} %bitcast.285, bf16[512,1024]{1,0:T(8,128)(2,1)S(1)} %bitcast.293, bf16[512,1024]{1,0:T(8,128)(2,1)S(1)} %bitcast.278), kind=kOutput, calls=%fused_computation.29 | convolution fusion | flops 2980052992 | bytes 25165824 | tf_op jit(solution)/shard_map/dot_general | solution.py:39
  256.4 7.9 %fusion.81 = bf16[512,1024]{1,0:T(8,128)(2,1)S(1)} fusion(bf16[1024,2816]{1,0:T(8,128)(2,1)} %bitcast.368, bf16[1024,1408]{1,0:T(8,128)(2,1)S(1)} %get-tuple-element.110, bf16[1024,1408]{1,0:T(8,128)(2,1)S(1)} %get-tuple-element.109), kind=kOutput, calls=%fused_computation.167 | convolution fusion | flops 2959081472 | bytes 12582912 | tf_op jit(solution)/shard_map/dot_general | solution.py:39
  268.9 7.2 %convolution_convert_fusion = bf16[1024,1408]{1,0:T(8,128)(2,1)} fusion(s32[]{:T(128)S(6)} %select_n.319, bf16[1024,1408]{1,0:T(8,128)(2,1)S(1)} %get-tuple-element.110, bf16[1024,1408]{1,0:T(8,128)(2,1)S(1)} %get-tuple-element.109, bf16[512,1024]{1,0:T(8,128)(2,1)} %collective-permute-done.5, bf16[512,1024]{1,0:T(8,128)(2,1)} %multiply_convert_fusion.4), kind=kOutput, calls=%fused_computation.51 | convolution fusion | flops 2964193280 | bytes 10747908 | tf_op jit(solution)/shard_map/dot_general | solution.py:35
  276.9 5.2 fusion.175
  285.2 16.6 %collective-permute-done.8 = bf16[512,1024]{1,0:T(8,128)(2,1)S(1)} collective-permute-done((bf16[512,1024]{1,0:T(8,128)(2,1)S(1)}, bf16[512,1024]{1,0:T(8,128)(2,1)S(1)}, u32[]{:S(2)}, u32[]{:S(2)}) %collective-permute-start.8) | collective-permute-done | bytes 1048608 | tf_op jit(solution)/shard_map/ppermute | solution.py:391
  301.8 3.5 multiply_reduce_fusion
  309.2 4.0 fusion.75.dc_ref
  316.1 8.8 %add_convert_fusion = bf16[1024,1408]{1,0:T(8,128)(2,1)} fusion(bf16[1024,1408]{1,0:T(8,128)(2,1)} %collective-permute-done.9, s32[]{:T(128)S(6)} %select_n.326, bf16[1024,1408]{1,0:T(8,128)(2,1)} %copy-done.44, bf16[1024,1408]{1,0:T(8,128)(2,1)S(1)} %copy-done.43, bf16[512,1024]{1,0:T(8,128)(2,1)} %collective-permute-done.5, ...), kind=kOutput, calls=%fused_computation.28 | convolution fusion | flops 2967076864 | bytes 13631492 | tf_op jit(solution)/shard_map/dot_general | solution.py:35
  324.9 11.5 %attend_back.2 = (bf16[512,1024]{1,0:T(8,128)(2,1)S(1)}, bf16[512,1024]{1,0:T(8,128)(2,1)S(1)}, bf16[512,1024]{1,0:T(8,128)(2,1)S(1)}) custom-call(s32[2,2]{1,0:T(2,128)S(1)} %get-tuple-element.185.first_ref, s32[2,2]{1,0:T(2,128)S(1)} %get-tuple-element.184.stop_ref, s32[2,1,256]{2,1,0:T(1,128)S(1)} %broadcast_in_dim.83.lo_ref, ...), custom_call_target="tpu_custom_call" | custom-call | flops 5368709120 | bytes 6291456 | tf_op jit(solution)/shard_map/attend_back/pallas_call | solution.py:210
  353.4 3.6 fusion.32
  369.7 10.0 %collective-permute-done.11 = bf16[2,4,1,64,1408]{4,3,2,1,0:T(8,128)(2,1)S(1)} collective-permute-done((bf16[2,4,1,64,1408]{4,3,2,1,0:T(8,128)(2,1)S(1)}, bf16[2,4,1,64,1408]{4,3,2,1,0:T(8,128)(2,1)S(1)}, u32[]{:S(2)}, u32[]{:S(2)}) %collective-permute-start.11) | collective-permute-done | bytes 1441824 | tf_op jit(solution)/shard_map/ppermute | solution.py:361
  381.2 5.2 fusion
  388.7 28.2 %attend_back.3 = (bf16[512,1024]{1,0:T(8,128)(2,1)S(1)}, bf16[2048,1024]{1,0:T(8,128)(2,1)}, bf16[2048,1024]{1,0:T(8,128)(2,1)}) custom-call(s32[2,2]{1,0:T(2,128)S(1)} %get-tuple-element.183.first_ref, s32[2,2]{1,0:T(2,128)S(1)} %get-tuple-element.164.stop_ref, s32[2,1,256]{2,1,0:T(1,128)S(1)} %broadcast_in_dim.73.lo_ref, s32[2,1,256]{2,1,0:T(1,128)S(1)} %bitcast.275, ...), custom_call_target="tpu_custom_call" | custom-call | flops 21474836480 | bytes 18874368 | tf_op jit(solution)/shard_map/attend_back/pallas_call | solution.py:210
  416.9 4.1 fusion.84
  428.5 7.0 %collective-permute-done.13 = bf16[4,1024,256]{2,1,0:T(8,128)(2,1)} collective-permute-done((bf16[4,1024,256]{2,1,0:T(8,128)(2,1)}, bf16[4,1024,256]{2,1,0:T(8,128)(2,1)}, u32[]{:S(2)}, u32[]{:S(2)}) %collective-permute-start.13) | collective-permute-done | bytes 2097184 | tf_op jit(solution)/shard_map/ppermute | solution.py:361
  435.4 3.5 add_convert_fusion.1
  444.5 4.4 fusion.66
  454.3 3.6 fusion.13
  465.7 13.2 %collective-permute-done.21 = bf16[4,1024,128]{2,1,0:T(8,128)(2,1)} collective-permute-done((bf16[4,1024,128]{2,1,0:T(8,128)(2,1)}, bf16[4,1024,128]{2,1,0:T(8,128)(2,1)}, u32[]{:S(2)}, u32[]{:S(2)}) %collective-permute-start.21) | collective-permute-done | bytes 1048608 | tf_op jit(solution)/shard_map/ppermute | solution.py:361
  482.9 6.1 collective-permute-done.17
  492.5 8.9 %collective-permute-done.19 = bf16[2,1024,256]{2,1,0:T(8,128)(2,1)} collective-permute-done((bf16[2,1024,256]{2,1,0:T(8,128)(2,1)}, bf16[2,1024,256]{2,1,0:T(8,128)(2,1)}, u32[]{:S(2)}, u32[]{:S(2)}) %collective-permute-start.19) | collective-permute-done | bytes 1048608 | tf_op jit(solution)/shard_map/ppermute | solution.py:361
  504.0 7.4 %collective-permute-done.7 = bf16[1024,512]{1,0:T(8,128)(2,1)} collective-permute-done((bf16[1024,512]{1,0:T(8,128)(2,1)}, bf16[1024,512]{1,0:T(8,128)(2,1)}, u32[]{:S(2)}, u32[]{:S(2)}) %collective-permute-start.7) | collective-permute-done | bytes 1048608 | tf_op jit(solution)/shard_map/ppermute | solution.py:399
  518.1 3.3 collective-permute-done.20
  527.0 7.7 %all-gather.3 = bf16[1408,256]{1,0:T(8,128)(2,1)S(1)} all-gather(bf16[352,256]{1,0:T(8,128)(2,1)S(1)} %add_convert_fusion.10), channel_id=5, replica_groups=mesh['section'=2,'group'=4,'dp'=4] {'group'}, dimensions={0}, use_global_device_ids=true | all-gather | bytes 901120 | tf_op jit(solution)/shard_map/all_gather | solution.py:457
  536.1 6.5 collective-permute-done.26
  543.8 7.2 %fusion.48 = f32[2048,1024]{1,0:T(8,128)S(1)} fusion(bf16[2048,1024]{1,0:T(8,128)(2,1)} %get-tuple-element.86, bf16[2,4,1024,1024]{3,2,1,0:T(8,128)(2,1)} %bitcast.364), kind=kOutput, calls=%fused_computation.132 | convolution fusion | flops 4294967296 | bytes 14680064 | tf_op jit(solution)/shard_map/dot_general | solution.py:39
  551.0 10.3 %fusion.11 = (f32[1024]{0:T(1024)S(1)}, f32[2048]{0:T(1024)S(1)}, f32[2048,1024]{1,0:T(8,128)}) fusion(f32[2048]{0:T(1024)S(1)} %bitcast.307, bf16[4,1024,1024]{2,1,0:T(8,128)(2,1)} %param.9, s32[]{:T(128)S(6)} %select_n.283, f32[1024]{0:T(1024)S(1)} %bitcast.311, f32[2048,1024]{1,0:T(8,128)S(1)} %fusion.48, bf16[2048,1024]{1,0:T(8,128)(2,1)S(1)} %copy-done.53, ...), kind=kOutput, calls=%fused_computation.19 | convolution fusion | flops 4311741440 | bytes 27287556 | tf_op jit(solution)/shard_map/dot_general | solution.py:39
  561.3 3.3 multiply_reduce_fusion.1
  567.0 4.6 fusion.59
  571.6 3.8 collective-permute-done.22
  576.4 8.4 %fusion.1 = bf16[2048,1024]{1,0:T(8,128)(2,1)S(1)} fusion(f32[2,1024,1024]{2,1,0:T(8,128)} %fusion.59, f32[2048,1024]{1,0:T(8,128)} %get-tuple-element.181, f32[2048]{0:T(1024)S(1)} %broadcast_multiply_fusion, f32[2048]{0:T(1024)S(1)} %multiply_multiply_fusion, f32[1024]{0:T(1024)S(1)} %bitcast.312, f32[2048]{0:T(1024)S(1)} %bitcast.308, ...), kind=kLoop, calls=%fused_computation.3 | loop fusion | flops 16777216 | bytes 25194500 | tf_op jit(solution)/shard_map/convert_element_type | solution.py:448
  593.9 8.6 %maximum_convert_fusion = f32[128,5632]{1,0:T(8,128)} fusion(bf16[64,1408]{1,0:T(8,128)(2,1)S(1)} %get-tuple-element.131, bf16[64,1408]{1,0:T(8,128)(2,1)S(1)} %get-tuple-element.132, bf16[64,1408]{1,0:T(8,128)(2,1)S(1)} %get-tuple-element.133, bf16[64,1408]{1,0:T(8,128)(2,1)S(1)} %get-tuple-element.134, bf16[64,1408]{1,0:T(8,128)(2,1)S(1)} %get-tuple-element.135, ...), kind=kLoop, calls=%fused_computation.169 | loop fusion | flops 11534336 | bytes 4325376 | tf_op jit(solution)/shard_map/concatenate | solution.py:465
  602.5 32.0 %collective-permute-done.25 = f32[4,1024]{1,0:T(4,128)S(1)} collective-permute-done((f32[4,1024]{1,0:T(4,128)S(1)}, f32[4,1024]{1,0:T(4,128)S(1)}, u32[]{:S(2)}, u32[]{:S(2)}) %collective-permute-start.25) | collective-permute-done | bytes 16416 | tf_op jit(solution)/shard_map/ppermute | solution.py:485
  634.5 13.1 %all-gather.4 = f32[4,4,1024]{2,1,0:T(4,128)S(1)} all-gather(f32[1,4,1024]{2,1,0:T(4,128)S(1)} %add_bitcast_fusion), channel_id=3, replica_groups=mesh['section'=2,'group'=4,'dp'=4] {'dp'}, dimensions={0}, use_global_device_ids=true | all-gather | bytes 81920 | tf_op jit(solution)/shard_map/all_gather | solution.py:486
  648.3 4.5 maximum_select_fusion
  (367 shorter events, 170.0 us)
Async XLA Ops:
  7.2 126.4 %all-gather.14.cloned.1.call-start = ((), (), s32[]{:S(2)}) async-start(), calls=%async_computation.8 | async-start | bytes 17301504 | tf_op jit(solution)/shard_map/all_gather | solution.py:264
  9.3 205.9 %all-gather.10.cloned.1.call-start = ((), (), s32[]{:S(2)}) async-start(), calls=%async_computation.3 | async-start | bytes 6127616 | tf_op jit(solution)/shard_map/all_gather | solution.py:287
  10.4 33.7 %collective-permute-start = (bf16[88,1024]{1,0:T(8,128)(2,1)S(1)}, bf16[88,1024]{1,0:T(8,128)(2,1)}, u32[]{:S(2)}, u32[]{:S(2)}) collective-permute-start(bf16[88,1024]{1,0:T(8,128)(2,1)S(1)} %get-tuple-element.108), channel_id=1, source_target_pairs={{0,1},{1,2},{2,3},{3,0},{4,5},{5,6},{6,7},{7,4},{8,9},{9,10},{10,1... | collective-permute-start | bytes 540680 | tf_op jit(solution)/shard_map/ppermute | solution.py:293
  13.5 31.5 %collective-permute-start.1 = (bf16[88,1024]{1,0:T(8,128)(2,1)S(1)}, bf16[88,1024]{1,0:T(8,128)(2,1)S(1)}, u32[]{:S(2)}, u32[]{:S(2)}) collective-permute-start(bf16[88,1024]{1,0:T(8,128)(2,1)S(1)} %get-tuple-element.108), channel_id=1, source_target_pairs={{0,2},{1,3},{2,0},{3,1},{4,6},{5,7},{6,4},{7,5},{8,10},{9,11},{10,... | collective-permute-start | bytes 540680 | tf_op jit(solution)/shard_map/ppermute | solution.py:293
  16.1 29.0 %collective-permute-start.2 = (bf16[88,1024]{1,0:T(8,128)(2,1)S(1)}, bf16[88,1024]{1,0:T(8,128)(2,1)S(1)}, u32[]{:S(2)}, u32[]{:S(2)}) collective-permute-start(bf16[88,1024]{1,0:T(8,128)(2,1)S(1)} %get-tuple-element.108), channel_id=1, source_target_pairs={{0,3},{1,0},{2,1},{3,2},{4,7},{5,4},{6,5},{7,6},{8,11},{9,8},{10,9... | collective-permute-start | bytes 540680 | tf_op jit(solution)/shard_map/ppermute | solution.py:293
  19.4 11.5 %collective-permute-start.6 = (bf16[32,2816]{1,0:T(8,128)(2,1)}, bf16[32,2816]{1,0:T(8,128)(2,1)}, u32[]{:S(2)}, u32[]{:S(2)}) collective-permute-start(bf16[32,2816]{1,0:T(8,128)(2,1)} %pad_maximum_fusion.11), channel_id=1, source_target_pairs={{0,16},{16,0},{1,17},{17,1},{2,18},{18,2},{3,19},{19,3},{4,20},{20... | collective-permute-start | bytes 540680 | tf_op jit(solution)/shard_map/ppermute | solution.py:285
  22.6 18.5 %copy-start.69 = (f32[1,2,2,128]{3,1,2,0:T(2,128)}, f32[1,2,2,128]{3,1,2,0:T(2,128)S(1)}, u32[]{:S(2)}) copy-start(f32[1,2,2,128]{3,1,2,0:T(2,128)S(1)} %copy.30) | copy-start | bytes 6148
  33.1 481.3 %reduce-scatter.11.cloned.1.call-start = ((), (), s32[]{:S(2)}) async-start(), calls=%async_computation.7 | async-start | bytes 1802240 | tf_op jit(solution)/shard_map/reduce_scatter | solution.py:374
  36.4 171.5 %copy-start.63 = (f32[1,8,2,128]{3,2,1,0:T(2,128)}, f32[1,8,2,128]{3,2,1,0:T(2,128)S(1)}, u32[]{:S(2)}) copy-start(f32[1,8,2,128]{3,2,1,0:T(2,128)S(1)} %get-tuple-element.154) | copy-start | bytes 24580
  36.4 174.6 %copy-start.65 = (f32[1,1,1024]{2,1,0:T(1,128)}, f32[1,1,1024]{2,1,0:T(1,128)S(1)}, u32[]{:S(2)}) copy-start(f32[1,1,1024]{2,1,0:T(1,128)S(1)} %get-tuple-element.152) | copy-start | bytes 12292
  133.6 22.2 %collective-permute-start.3 = (bf16[4,88,1024]{2,1,0:T(8,128)(2,1)S(1)}, bf16[4,88,1024]{2,1,0:T(8,128)(2,1)S(1)}, u32[]{:S(2)}, u32[]{:S(2)}) collective-permute-start(bf16[4,88,1024]{2,1,0:T(8,128)(2,1)S(1)} %bitcast_dynamic-update-slice_fusion), channel_id=1, source_target_pairs={{0,8},{4,12},{8,0},{12,4},{1,9},{5,13},{9,1},{13,5},{2,10},{6,14},... | collective-permute-start | bytes 2162696 | tf_op jit(solution)/shard_map/ppermute | solution.py:276
  135.1 20.9 %copy-start.33 = (bf16[2,1024,1024]{2,1,0:T(8,128)(2,1)S(1)}, bf16[2,1024,1024]{2,1,0:T(8,128)(2,1)}, u32[]{:S(2)}) copy-start(bf16[2,1024,1024]{2,1,0:T(8,128)(2,1)} %fusion.4) | copy-start | bytes 12582916
  156.0 27.0 %collective-permute-start.4 = (bf16[2,4,88,1024]{3,2,0,1:T(8,128)(2,1)S(1)}, bf16[2,4,88,1024]{3,2,0,1:T(8,128)(2,1)S(1)}, u32[]{:S(2)}, u32[]{:S(2)}) collective-permute-start(bf16[2,4,88,1024]{3,2,0,1:T(8,128)(2,1)S(1)} %maximum_select_fusion.3), channel_id=1, source_target_pairs={{0,4},{4,0},{8,12},{12,8},{1,5},{5,1},{9,13},{13,9},{2,6},{6,2},{1... | collective-permute-start | bytes 4325384 | tf_op jit(solution)/shard_map/ppermute | solution.py:276
  166.7 16.3 %copy-start.14 = (bf16[512,1024]{1,0:T(8,128)(2,1)}, bf16[512,1024]{1,0:T(8,128)(2,1)S(1)}, u32[]{:S(2)}) copy-start(bf16[512,1024]{1,0:T(8,128)(2,1)S(1)} %fusion.80.q_ref) | copy-start | bytes 3145732
  203.1 104.4 %copy-start.7 = (bf16[512,1024]{1,0:T(8,128)(2,1)}, bf16[512,1024]{1,0:T(8,128)(2,1)S(1)}, u32[]{:S(2)}) copy-start(bf16[512,1024]{1,0:T(8,128)(2,1)S(1)} %get-tuple-element.56.c_ref) | copy-start | bytes 3145732
  207.7 25.8 %collective-permute-start.5 = (bf16[512,1024]{1,0:T(8,128)(2,1)}, bf16[512,1024]{1,0:T(8,128)(2,1)}, u32[]{:S(2)}, u32[]{:S(2)}) collective-permute-start(bf16[512,1024]{1,0:T(8,128)(2,1)} %multiply_convert_fusion.4), channel_id=1, source_target_pairs={{0,16},{16,0},{1,17},{17,1},{2,18},{18,2},{3,19},{19,3},{4,20},{20... | collective-permute-start | bytes 3145736 | tf_op jit(solution)/shard_map/ppermute | solution.py:346
  268.9 32.9 %slice-start = ((s8[5767168]{0:T(1024)(128)(4,1)}), s8[4194304]{0:T(1024)(128)(4,1)S(1)}, s32[]{:S(2)}) async-start(s8[5767168]{0:T(1024)(128)(4,1)} %bitcast.369), calls=%async_computation.11 | async-start | bytes 8388608
  276.0 25.7 %slice-start.1 = ((s8[5767168]{0:T(1024)(128)(4,1)}), s8[1572864]{0:T(1024)(128)(4,1)S(1)}, s32[]{:S(2)}) async-start(s8[5767168]{0:T(1024)(128)(4,1)} %bitcast.369), calls=%async_computation.12 | async-start | bytes 3145728
  276.0 37.2 %collective-permute-start.10 = (bf16[1408,512]{1,0:T(8,128)(2,1)}, bf16[1408,512]{1,0:T(8,128)(2,1)S(1)}, u32[]{:S(2)}, u32[]{:S(2)}) collective-permute-start(bf16[1408,512]{1,0:T(8,128)(2,1)} %convolution_convert_fusion.3), channel_id=1, source_target_pairs={{0,4},{4,0},{8,12},{12,8},{1,5},{5,1},{9,13},{13,9},{2,6},{6,2},{1... | collective-permute-start | bytes 4325384 | tf_op jit(solution)/shard_map/ppermute | solution.py:384
  276.1 39.9 %collective-permute-start.9 = (bf16[1024,1408]{1,0:T(8,128)(2,1)}, bf16[1024,1408]{1,0:T(8,128)(2,1)}, u32[]{:S(2)}, u32[]{:S(2)}) collective-permute-start(bf16[1024,1408]{1,0:T(8,128)(2,1)} %convolution_convert_fusion), channel_id=1, source_target_pairs={{0,4},{4,0},{8,12},{12,8},{1,5},{5,1},{9,13},{13,9},{2,6},{6,2},{1... | collective-permute-start | bytes 8650760 | tf_op jit(solution)/shard_map/ppermute | solution.py:384
  276.6 25.1 %collective-permute-start.8 = (bf16[512,1024]{1,0:T(8,128)(2,1)S(1)}, bf16[512,1024]{1,0:T(8,128)(2,1)S(1)}, u32[]{:S(2)}, u32[]{:S(2)}) collective-permute-start(bf16[512,1024]{1,0:T(8,128)(2,1)S(1)} %fusion.81), channel_id=1, source_target_pairs={{0,16},{16,0},{1,17},{17,1},{2,18},{18,2},{3,19},{19,3},{4,20},{20... | collective-permute-start | bytes 3145736 | tf_op jit(solution)/shard_map/ppermute | solution.py:391
  341.7 39.4 %collective-permute-start.12 = (bf16[4,1024,512]{2,1,0:T(8,128)(2,1)}, bf16[4,1024,512]{2,1,0:T(8,128)(2,1)}, u32[]{:S(2)}, u32[]{:S(2)}) collective-permute-start(bf16[4,1024,512]{2,1,0:T(8,128)(2,1)} %pad_maximum_fusion), channel_id=1, source_target_pairs={{0,4},{4,0},{8,12},{12,8},{1,5},{5,1},{9,13},{13,9},{2,6},{6,2},{1... | collective-permute-start | bytes 12582920 | tf_op jit(solution)/shard_map/ppermute | solution.py:384
  343.9 190.8 %all-reduce.3.cloned.1.call-start = ((), (), s32[]{:S(2)}) async-start(), calls=%async_computation.10 | async-start | bytes 2883584
  345.7 34.0 %collective-permute-start.11 = (bf16[2,4,1,64,1408]{4,3,2,1,0:T(8,128)(2,1)S(1)}, bf16[2,4,1,64,1408]{4,3,2,1,0:T(8,128)(2,1)S(1)}, u32[]{:S(2)}, u32[]{:S(2)}) collective-permute-start(bf16[2,4,1,64,1408]{4,3,2,1,0:T(8,128)(2,1)S(1)} %constant_dynamic-slice_fusion.9), channel_id=1, source_target_pairs={{0,8},{4,12},{8,0},{12,4},{1,9},{5,13},{9,1},{13,5},{2,10},{6,14},... | collective-permute-start | bytes 4325384 | tf_op jit(solution)/shard_map/ppermute | solution.py:361
  387.9 47.5 %collective-permute-start.13 = (bf16[4,1024,256]{2,1,0:T(8,128)(2,1)}, bf16[4,1024,256]{2,1,0:T(8,128)(2,1)}, u32[]{:S(2)}, u32[]{:S(2)}) collective-permute-start(bf16[4,1024,256]{2,1,0:T(8,128)(2,1)} %constant_dynamic-slice_fusion.8), channel_id=1, source_target_pairs={{0,16},{16,0},{1,17},{17,1},{2,18},{18,2},{3,19},{19,3},{4,20},{20... | collective-permute-start | bytes 6291464 | tf_op jit(solution)/shard_map/ppermute | solution.py:361
  388.7 28.2 %copy-start.16 = (bf16[2048,1024]{1,0:T(8,128)(2,1)S(1)}, bf16[2048,1024]{1,0:T(8,128)(2,1)}, u32[]{:S(2)}) copy-start(bf16[2048,1024]{1,0:T(8,128)(2,1)} %fusion.6) | copy-start | bytes 12582916
  438.9 15.4 %collective-permute-start.15 = (bf16[2,1024,512]{2,1,0:T(8,128)(2,1)}, bf16[2,1024,512]{2,1,0:T(8,128)(2,1)}, u32[]{:S(2)}, u32[]{:S(2)}) collective-permute-start(bf16[2,1024,512]{2,1,0:T(8,128)(2,1)} %pad_maximum_fusion.5), channel_id=1, source_target_pairs={{0,4},{4,0},{8,12},{12,8},{1,5},{5,1},{9,13},{13,9},{2,6},{6,2},{1... | collective-permute-start | bytes 6291464 | tf_op jit(solution)/shard_map/ppermute | solution.py:384
  438.9 19.0 %collective-permute-start.14 = (bf16[2,1024,512]{2,1,0:T(8,128)(2,1)}, bf16[2,1024,512]{2,1,0:T(8,128)(2,1)}, u32[]{:S(2)}, u32[]{:S(2)}) collective-permute-start(bf16[2,1024,512]{2,1,0:T(8,128)(2,1)} %pad_maximum_fusion.4), channel_id=1, source_target_pairs={{0,4},{4,0},{8,12},{12,8},{1,5},{5,1},{9,13},{13,9},{2,6},{6,2},{1... | collective-permute-start | bytes 6291464 | tf_op jit(solution)/shard_map/ppermute | solution.py:384
  441.5 124.1 %reduce-scatter.9.cloned.1.call-start = ((), (), s32[]{:S(2)}) async-start(), calls=%async_computation.5 | async-start | bytes 1310720 | tf_op jit(solution)/shard_map/reduce_scatter | solution.py:374
  452.5 26.4 %collective-permute-start.21 = (bf16[4,1024,128]{2,1,0:T(8,128)(2,1)}, bf16[4,1024,128]{2,1,0:T(8,128)(2,1)}, u32[]{:S(2)}, u32[]{:S(2)}) collective-permute-start(bf16[4,1024,128]{2,1,0:T(8,128)(2,1)} %constant_dynamic-slice_fusion.2), channel_id=1, source_target_pairs={{0,8},{4,12},{8,0},{12,4},{1,9},{5,13},{9,1},{13,5},{2,10},{6,14},... | collective-permute-start | bytes 3145736 | tf_op jit(solution)/shard_map/ppermute | solution.py:361
  462.6 26.4 %collective-permute-start.17 = (bf16[2,1024,256]{2,1,0:T(8,128)(2,1)}, bf16[2,1024,256]{2,1,0:T(8,128)(2,1)}, u32[]{:S(2)}, u32[]{:S(2)}) collective-permute-start(bf16[2,1024,256]{2,1,0:T(8,128)(2,1)} %constant_dynamic-slice_fusion.6), channel_id=1, source_target_pairs={{0,16},{16,0},{1,17},{17,1},{2,18},{18,2},{3,19},{19,3},{4,20},{20... | collective-permute-start | bytes 3145736 | tf_op jit(solution)/shard_map/ppermute | solution.py:361
  464.9 16.7 %copy-start.64 = (f32[1,8,2,128]{3,2,1,0:T(2,128)S(1)}, f32[1,8,2,128]{3,2,1,0:T(2,128)}, u32[]{:S(2)}) copy-start(f32[1,8,2,128]{3,2,1,0:T(2,128)} %copy-done.63) | copy-start | bytes 24580
  464.9 16.8 %copy-start.75 = (u32[32]{0:T(128)S(1)}, u32[32]{0:T(128)}, u32[]{:S(2)}) copy-start(u32[32]{0:T(128)} %constant.258) | copy-start | bytes 388
  464.9 36.5 %collective-permute-start.19 = (bf16[2,1024,256]{2,1,0:T(8,128)(2,1)}, bf16[2,1024,256]{2,1,0:T(8,128)(2,1)}, u32[]{:S(2)}, u32[]{:S(2)}) collective-permute-start(bf16[2,1024,256]{2,1,0:T(8,128)(2,1)} %constant_dynamic-slice_fusion.4), channel_id=1, source_target_pairs={{0,8},{4,12},{8,0},{12,4},{1,9},{5,13},{9,1},{13,5},{2,10},{6,14},... | collective-permute-start | bytes 3145736 | tf_op jit(solution)/shard_map/ppermute | solution.py:361
  481.5 84.1 %reduce-scatter.7.cloned.1.call-start = ((), (), s32[]{:S(2)}) async-start(), calls=%async_computation.4 | async-start | bytes 1310720 | tf_op jit(solution)/shard_map/reduce_scatter | solution.py:374
  481.6 29.9 %collective-permute-start.7 = (bf16[1024,512]{1,0:T(8,128)(2,1)}, bf16[1024,512]{1,0:T(8,128)(2,1)}, u32[]{:S(2)}, u32[]{:S(2)}) collective-permute-start(bf16[1024,512]{1,0:T(8,128)(2,1)} %fusion.34), channel_id=1, source_target_pairs={{0,16},{16,0},{1,17},{17,1},{2,18},{18,2},{3,19},{19,3},{4,20},{20... | collective-permute-start | bytes 3145736 | tf_op jit(solution)/shard_map/ppermute | solution.py:399
  482.9 18.5 %copy-start.28 = (bf16[2,1024,512]{2,1,0:T(8,128)(2,1)S(1)}, bf16[2,1024,512]{2,1,0:T(8,128)(2,1)}, u32[]{:S(2)}) copy-start(bf16[2,1024,512]{2,1,0:T(8,128)(2,1)} %fusion.13) | copy-start | bytes 6291460
  491.7 25.0 %collective-permute-start.18 = (bf16[2,1024,128]{2,1,0:T(8,128)(2,1)}, bf16[2,1024,128]{2,1,0:T(8,128)(2,1)}, u32[]{:S(2)}, u32[]{:S(2)}) collective-permute-start(bf16[2,1024,128]{2,1,0:T(8,128)(2,1)} %constant_dynamic-slice_fusion.5), channel_id=1, source_target_pairs={{0,8},{4,12},{8,0},{12,4},{1,9},{5,13},{9,1},{13,5},{2,10},{6,14},... | collective-permute-start | bytes 1572872 | tf_op jit(solution)/shard_map/ppermute | solution.py:361
  503.8 17.6 %collective-permute-start.20 = (bf16[2,1024,128]{2,1,0:T(8,128)(2,1)}, bf16[2,1024,128]{2,1,0:T(8,128)(2,1)}, u32[]{:S(2)}, u32[]{:S(2)}) collective-permute-start(bf16[2,1024,128]{2,1,0:T(8,128)(2,1)} %constant_dynamic-slice_fusion.3), channel_id=1, source_target_pairs={{0,16},{16,0},{1,17},{17,1},{2,18},{18,2},{3,19},{19,3},{4,20},{20... | collective-permute-start | bytes 1572872 | tf_op jit(solution)/shard_map/ppermute | solution.py:361
  516.1 10.8 %collective-permute-start.27 = (bf16[352,256]{1,0:T(8,128)(2,1)}, bf16[352,256]{1,0:T(8,128)(2,1)S(1)}, u32[]{:S(2)}, u32[]{:S(2)}) collective-permute-start(bf16[352,256]{1,0:T(8,128)(2,1)} %constant_dynamic-slice_fusion), channel_id=1, source_target_pairs={{0,8},{4,12},{8,0},{12,4},{1,9},{5,13},{9,1},{13,5},{2,10},{6,14},... | collective-permute-start | bytes 540680 | tf_op jit(solution)/shard_map/ppermute | solution.py:361
  523.7 65.5 %all-gather.16.cloned.1.call-start = ((), (), s32[]{:S(2)}) async-start(), calls=%async_computation.9 | async-start | bytes 1802240 | tf_op jit(solution)/shard_map/all_gather | solution.py:457
  535.7 6.9 %collective-permute-start.26 = (bf16[64,1408]{1,0:T(8,128)(2,1)S(1)}, bf16[64,1408]{1,0:T(8,128)(2,1)S(1)}, u32[]{:S(2)}, u32[]{:S(2)}) collective-permute-start(bf16[64,1408]{1,0:T(8,128)(2,1)S(1)} %get-tuple-element.139), channel_id=1, source_target_pairs={{0,16},{16,0},{1,17},{17,1},{2,18},{18,2},{3,19},{19,3},{4,20},{20... | collective-permute-start | bytes 540680 | tf_op jit(solution)/shard_map/ppermute | solution.py:425
  543.5 109.4 %all-gather.12.cloned.1.call-start = ((), (), s32[]{:S(2)}) async-start(), calls=%async_computation.6 | async-start | bytes 2621440 | tf_op jit(solution)/shard_map/all_gather | solution.py:457
  564.6 23.5 %collective-permute-start.23 = (f32[4,1024]{1,0:T(4,128)S(1)}, f32[4,1024]{1,0:T(4,128)S(1)}, u32[]{:S(2)}, u32[]{:S(2)}) collective-permute-start(f32[4,1024]{1,0:T(4,128)S(1)} %pad_maximum_fusion.12), channel_id=1, source_target_pairs={{0,4},{4,0},{8,12},{12,8},{1,5},{5,1},{9,13},{13,9},{2,6},{6,2},{1... | collective-permute-start | bytes 49160 | tf_op jit(solution)/shard_map/ppermute | solution.py:485
  566.7 8.7 %collective-permute-start.22 = (bf16[4,256,128]{2,1,0:T(8,128)(2,1)S(1)}, bf16[4,256,128]{2,1,0:T(8,128)(2,1)S(1)}, u32[]{:S(2)}, u32[]{:S(2)}) collective-permute-start(bf16[4,256,128]{2,1,0:T(8,128)(2,1)S(1)} %get-tuple-element.149), channel_id=1, source_target_pairs={{0,16},{16,0},{1,17},{17,1},{2,18},{18,2},{3,19},{19,3},{4,20},{20... | collective-permute-start | bytes 786440 | tf_op jit(solution)/shard_map/ppermute | solution.py:472
  586.6 61.7 %collective-permute-start.16 = (bf16[2,1024,512]{2,1,0:T(8,128)(2,1)}, bf16[2,1024,512]{2,1,0:T(8,128)(2,1)}, u32[]{:S(2)}, u32[]{:S(2)}) collective-permute-start(bf16[2,1024,512]{2,1,0:T(8,128)(2,1)} %get-tuple-element.113), channel_id=1, source_target_pairs={{0,16},{16,0},{1,17},{17,1},{2,18},{18,2},{3,19},{19,3},{4,20},{20... | collective-permute-start | bytes 6291464 | tf_op jit(solution)/shard_map/ppermute | solution.py:453
  588.2 3.8 collective-permute-start.24
  592.0 42.5 %collective-permute-start.25 = (f32[4,1024]{1,0:T(4,128)S(1)}, f32[4,1024]{1,0:T(4,128)S(1)}, u32[]{:S(2)}, u32[]{:S(2)}) collective-permute-start(f32[4,1024]{1,0:T(4,128)S(1)} %fusion.207), channel_id=1, source_target_pairs={{0,16},{16,0},{1,17},{17,1},{2,18},{18,2},{3,19},{19,3},{4,20},{20... | collective-permute-start | bytes 49160 | tf_op jit(solution)/shard_map/ppermute | solution.py:485
  (68 other events, 412.8 us)
Sparse Core Ops, SparseCore 0:
  11.6 121.9 all-gather.13
  136.5 59.9 all-gather.9
  344.0 32.1 reduce-scatter.10
  441.6 62.9 all-reduce.2
  506.7 26.8 reduce-scatter.8
  536.5 25.7 reduce-scatter.6
  564.4 17.5 all-gather.15
  584.2 22.5 all-gather.11

commit v6 on v5

--- a/solution.py
+++ b/solution.py
@@ -259,10 +259,6 @@
     swap = [(0, 1), (1, 0)]
     together = lax.optimization_barrier
 
-    four = jnp.concatenate([attn_qkv[0], attn_out], axis=0)
-    matrix = lax.dynamic_index_in_dim(four, group, 0, keepdims=False)
-    matrices = lax.all_gather(matrix, ("section", "group", "dp"), axis=0, tiled=True)
-
     gains = lax.all_gather(norm_gains, "section", axis=0, tiled=True)
 
     def quarter_of(shard):
@@ -286,16 +282,21 @@
     w_in = in_order(section, of_units(quarter, section), got)
     w_in = lax.all_gather(w_in, ("dp", "group"), axis=1, tiled=True).reshape(D, 2 * units)
 
+    height = attn_qkv.shape[2] // groups
+    quarter = lax.dynamic_slice_in_dim(attn_qkv[0], group * height, height, 1)
+    qkv = lax.all_gather(quarter, ("section", "dp", "group"), axis=1, tiled=True)
+
     line, place = lax.axis_size("dp"), lax.axis_index("dp")
-    quarter = quarter_of(ffn_down)
-    down = jnp.zeros((line,) + quarter.shape, BF)
+    wo = both(quarter_of(attn_out[0]), section, "section", swap)
+    chain = jnp.concatenate([wo.reshape(-1, D), quarter_of(ffn_down)], axis=0)
+    moved = [chain if step == 0 else lax.ppermute(chain, "dp", [(i, (i + step) % line) for i in range(line)])
+             for step in range(line)]
+    chain = jnp.zeros((line,) + chain.shape, BF)
     for step in range(line):
-        moved = lax.ppermute(quarter, "dp", [(i, (i + step) % line) for i in range(line)]) if step else quarter
-        down = lax.dynamic_update_slice_in_dim(down, moved[None], (place - step) % line, 0)
-    matrices, down = together((matrices, down))
-    matrices = matrices.reshape(sections, groups, D, D)
-    wq, wk, wv, wo = [matrices[:, index] for index in range(4)]
-    down = both(down, side, "group", side_pairs)
+        chain = lax.dynamic_update_slice_in_dim(chain, moved[step][None], (place - step) % line, 0)
+    chain = both(chain, side, "group", side_pairs)
+    qkv, chain = together((qkv, chain))
+    wq, wk, wv = [matrix.reshape(sections, D, D) for matrix in qkv]
 
     rows = byte_states.shape[0] // sections
     mine = lambda a: lax.dynamic_slice_in_dim(a, section * rows, rows, 0)
@@ -326,11 +327,15 @@
     q1 = nn(query_in, wq[0]).astype(BF)
     k1 = nn(key_in, wk[0]).astype(BF)
     v1 = nn(key_in, wv[0]).astype(BF)
-    v1, down = together((v1, down))
-    down = both(down, core, "group", core_pairs)
+    v1, chain = together((v1, chain))
+    chain = both(chain, core, "group", core_pairs)
     c1, l1 = attend(cross, q1, k1, v1, 8)
-    c1, down = together((c1, down))
-    w_down = down.transpose(2, 1, 0, 3, 4).reshape(units, D)
+    c1, chain = together((c1, chain))
+    chain = chain.transpose(2, 1, 0, 3, 4)
+    at = sections * height
+    wo = chain[:, :, :, :at].reshape(line, 2, 2, sections, height, D).transpose(3, 0, 1, 2, 4, 5)
+    wo = wo.reshape(sections, D, D)
+    w_down = chain[:, :, :, at:].reshape(units, D)
     carried = (pooled + nn(c1, wo[0])).astype(BF)
 
     carried_wide = carried.astype(F32)
@@ -384,10 +389,11 @@
         got = lax.ppermute(sent, "group", core_pairs)
         return (products(pairs, core) + got.astype(F32)).astype(BF)
 
+    mix_other = nt(dgu[tokens:], w_in).astype(BF)
+    dgu, mix_other = together((dgu, mix_other))
     in_pairs, down_pairs = [(mixed, dgu)], [(hidden, cots)]
-    mix_other = nt(dgu[tokens:], w_in).astype(BF)
     send_in, send_down = to_core(in_pairs), to_core(down_pairs)
-    dgu_own, mix_other, send_in, send_down = together((dgu[:tokens], mix_other, send_in, send_down))
+    dgu_own, send_in, send_down = together((dgu[:tokens], send_in, send_down))
     mix_got = lax.ppermute(mix_other, "section", swap)
 
     half = D // sections
@@ -397,16 +403,17 @@
     kept = lax.dynamic_slice_in_dim(parts, section * half, half, 1)
     dgu_own, sent = together((dgu_own, sent))
     got = lax.ppermute(sent, "section", swap).astype(F32)
-    latents = in_order(section, kept[:tokens] + got[tokens:], kept[tokens:] + got[:tokens])
-    latents_out = latents.astype(BF).reshape(sections * rows, PATCHES, half)
-
+    half_in, half_down = of_chip(in_pairs, send_in), of_chip(down_pairs, send_down)
+    mix_got, half_in, half_down = together((mix_got, half_in, half_down))
     grad_mixed = nt(dgu_own, w_in) + mix_got.astype(F32)
     grad_mix, gain_mix = norm_backward(residual, second_scale, gains[1, 1], grad_mixed)
     grad_residual = grad_mix + cot.astype(F32)
     branch = grad_residual.astype(BF)
     dc2 = nt(branch, wo[1]).astype(BF)
-    half_in, half_down = of_chip(in_pairs, send_in), of_chip(down_pairs, send_down)
-    dc2, half_in, half_down = together((dc2, half_in, half_down))
+
+    dc2, got = together((dc2, got))
+    latents = in_order(section, kept[:tokens] + got[tokens:], kept[tokens:] + got[:tokens])
+    latents_out = latents.astype(BF).reshape(sections * rows, PATCHES, half)
 
     dq2, dk2, dv2 = attend_back(causal, q2, k2, v2, l2, c2, dc2, 8, CAUSAL_SPANS)
     two_pairs = [(normed_in, dq2), (normed_in, dk2), (normed_in, dv2), (c2, branch)]
@@ -420,7 +427,7 @@
     half_two = of_chip(two_pairs, send_two)
     dc1, half_in, half_two = together((dc1, half_in, half_two))
     sum_down = over_side(line_sum(half_down, 0), 1)
-    sum_in = line_sum(half_in, 1).reshape(sections, -1, units)
+    sum_in = line_sum(half_in.reshape(sections, -1, units), 1)
     sum_in = jnp.stack([lax.dynamic_index_in_dim(sum_in, section, 0, False),
                         lax.ppermute(lax.dynamic_index_in_dim(sum_in, 1 - section, 0, False), "section", swap)])
     sum_in = jnp.where(section == 0, sum_in, sum_in[::-1])
@@ -429,29 +436,33 @@
     half_two = over_section(half_two, 2)
     one_pairs = [(query_in, dq1), (key_in, dk1)], [(key_in, dv1), (c1, d_carried)]
     send_one = [to_core(pairs) for pairs in one_pairs]
-    dq1, dk1, dv1, send_one, half_two = together((dq1, dk1, dv1, send_one, half_two))
-    sum_two = line_sum(over_side(half_two, 2), 1)
+    dq1, dk1, dv1, send_one = together((dq1, dk1, dv1, send_one))
+    grad_query_in = nt(dq1, wq[0])
+    grad_key_in = nt(dk1, wk[0]) + nt(dv1, wv[0])
+    dq1, dk1, dv1, grad_query_in, grad_key_in = together((dq1, dk1, dv1, grad_query_in, grad_key_in))
+    one_pairs = [(query_in, dq1), (key_in, dk1)], [(key_in, dv1), (c1, d_carried)]
     half_one = [of_chip(pairs, sent) for pairs, sent in zip(one_pairs, send_one)]
-    dq1, dk1, dv1, half_one = together((dq1, dk1, dv1, half_one))
-    half_one = jnp.concatenate(
-        [over_side(over_section(half_one[0], 2), 2), over_section(over_side(half_one[1], 2), 2)], axis=0
-    )
+    grad_query_in, grad_key_in, half_one, half_two = together((grad_query_in, grad_key_in, half_one, half_two))
+    half_two = over_side(half_two, 2)
+    grad_pooled, gain_query = norm_backward(pooled, query_scale, gains[0, 0], grad_query_in)
+    per_patch = (grad_pooled + d_carried.astype(F32)) / count
+    per_patch = per_patch.astype(BF).reshape(rows, PATCHES, D)
+    first_one = over_section(half_one[0], 2), over_side(half_one[1], 2)
+
+    gain_key, kept_bytes, sent_bytes = 0.0, [], []
+    for row in range(rows):
+        here = slice(row * ROW_BYTES, (row + 1) * ROW_BYTES)
+        grad_wide, gain = norm_backward(wide[here], key_scale[here], gains[0, 1], grad_key_in[here])
+        grad_bytes = (grad_wide + tn(member[row], per_patch[row])).astype(BF)
+        gain_key = gain_key + gain
+        kept_bytes.append(lax.dynamic_slice_in_dim(grad_bytes, section * half, half, 1))
+        sent_bytes.append(lax.dynamic_slice_in_dim(grad_bytes, (1 - section) * half, half, 1))
+    sent_bytes[-1], first_one, half_two = together((sent_bytes[-1], first_one, half_two))
+    sum_two = line_sum(half_two, 1)
+    got_bytes = [lax.ppermute(sent, "section", swap) for sent in sent_bytes]
+    half_one = jnp.concatenate([over_side(first_one[0], 2), over_section(first_one[1], 2)], axis=0)
+    half_one, sum_two, got_bytes[:-1] = together((half_one, sum_two, got_bytes[:-1]))
     sum_one = line_sum(half_one, 1)
-    grad_pooled, gain_query = norm_backward(pooled, query_scale, gains[0, 0], nt(dq1, wq[0]))
-    grad_wide, gain_key = norm_backward(
-        wide, key_scale, gains[0, 1], nt(dk1, wk[0]) + nt(dv1, wv[0])
-    )
-    per_patch = (grad_pooled + d_carried.astype(F32)) / count
-    spread_back = jnp.einsum(
-        "rpb,rpd->rbd", member, per_patch.astype(BF).reshape(rows, PATCHES, D), preferred_element_type=F32
-    )
-    byte_grads = (grad_wide + spread_back.reshape(rows * ROW_BYTES, D)).astype(BF)
-
-    byte_grads = byte_grads.reshape(rows, ROW_BYTES, D)
-    other = lax.dynamic_slice_in_dim(byte_grads, (1 - section) * half, half, 2)
-    own = lax.dynamic_slice_in_dim(byte_grads, section * half, half, 2)
-    bytes_out = in_order(section, own, lax.ppermute(other, "section", swap))
-    bytes_out = bytes_out.reshape(sections * rows, ROW_BYTES, half)
 
     def of_group(part):
         every = lax.all_gather(part, "group", axis=0, tiled=False)
@@ -466,6 +477,17 @@
         [laid_out([every[at][t] for at in (2 * y, 2 * y + 1) for t in range(sections)], range(4)) for y in (0, 1)],
         axis=0,
     )
+
+    gain_grads = jnp.stack([gain_query, gain_key, gain_normed, gain_mix])
+    for axis, pairs in (("group", core_pairs), ("group", side_pairs), ("section", swap)):
+        gain_grads = gain_grads + lax.ppermute(gain_grads, axis, pairs)
+        gain_grads, got_bytes = together((gain_grads, got_bytes))
+    gain_grads = jnp.sum(lax.all_gather(gain_grads, "dp", axis=0, tiled=False), axis=0)
+    sum_one, gain_grads, got_bytes, ffn_gin, ffn_gdown = together(
+        (sum_one, gain_grads, got_bytes, ffn_gin, ffn_gdown)
+    )
+    bytes_out = in_order(section, jnp.stack(kept_bytes), jnp.stack(got_bytes))
+    bytes_out = bytes_out.reshape(sections * rows, ROW_BYTES, half)
 
     kept = jnp.where(section == 0, sum_one, sum_two)
     sent = jnp.where(section == 0, sum_two, sum_one)
@@ -480,10 +502,6 @@
     last = jnp.where(section == 0, side_first, section_first[2:])
     grad_qkv = jnp.concatenate([section_first[:2], last[:1]], axis=0)[None]
 
-    gain_grads = jnp.stack([gain_query, gain_key, gain_normed, gain_mix])
-    for axis, pairs in (("group", core_pairs), ("group", side_pairs), ("section", swap)):
-        gain_grads = gain_grads + lax.ppermute(gain_grads, axis, pairs)
-    gain_grads = jnp.sum(lax.all_gather(gain_grads, "dp", axis=0, tiled=False), axis=0)
     gain_grads = lax.dynamic_slice_in_dim(gain_grads.reshape(2, 2, D), section, 1, 0)
     width = D // lax.axis_size("dp")
     gain_out = lax.dynamic_slice_in_dim(gain_grads, lax.axis_index("dp") * width, width, 2)

time: 673 us -> 727 us (1.080)
  local copies, waits for them, and re-layouts: 37.4 us -> 59.7 us
  waiting for transfers between devices: 234 us -> 256 us
  matrix products: 176 us -> 159 us
  starting transfers between devices: 22.7 us -> 38.7 us
  other arithmetic: 96.1 us -> 107 us
    all_gather x1, waiting for transfers between devices: 88.5 us -> 34.9 us  [shards(): lax.all_gather(quarter, ('section', 'dp', 'group'), axis=1, tiled=True)]
    ppermute x2 -> x3, waiting for transfers between devices: 11.2 us -> 43.3 us  [both(): return in_order(part, values, lax.ppermute(values, axis, pairs))]
    ppermute x3, waiting for transfers between devices: 33.1 us -> 1.36 us  [shards(): gain_grads = gain_grads + lax.ppermute(gain_grads, axis, pairs)]
    ppermute x4 -> x5, waiting for transfers between devices: 0.01 us -> 31.1 us  [the longest x3 22.8 us: shards(): lax.ppermute(chain, 'dp', [(i, (i + step) % line) for i in range(line)])]
    ppermute x8, waiting for transfers between devices: 48.5 us -> 77.9 us  [exchanged(): lax.ppermute(other, axis, pairs).astype(F32)]
    ppermute x1, waiting for transfers between devices: 7.42 us -> 24.3 us  [shards(): got = lax.ppermute(sent, 'section', swap).astype(F32)]
    all_gather x2, waiting for transfers between devices: 0.01 us -> 12.2 us  [of_group(): every = lax.all_gather(part, 'group', axis=0, tiled=False)]
    ppermute x1, waiting for transfers between devices: 16.6 us -> 5.13 us  [shards(): mix_got = lax.ppermute(mix_other, 'section', swap)]
  transfers between devices with their start and end apart: 36 -> 38, of which waited for: 15 -> 17; matrix products, arithmetic and copies ran while one was open for 35% -> 32% of each run, Pallas kernels for 7% -> 6%
where the time goes in v6:
time: 727 us; the launch traced here: 720 us
  waiting for transfers between devices  256 us (35%)
  matrix products  159 us (22%)
  other arithmetic  107 us (15%)
  local copies, waits for them, and re-layouts  59.7 us (8%)
  Pallas kernels  56 us (8%)
  starting transfers between devices  38.7 us (5%)
  blocking collectives  28.1 us (4%)
  between operations  16.2 us (2%)
    ppermute x8, waiting for transfers between devices, exchanged(): lax.ppermute(other, axis, pairs).astype(F32)  77.9 us
    dot_general x11, matrix products, nt(): lax.dot_general(left, right, (((1,), (1,)), ((), ())), preferred_element_...  57.9 us
    dot_general x22, matrix products, tn(): lax.dot_general(left, right, (((0,), (0,)), ((), ())), preferred_element_...  55 us
    ppermute x3, waiting for transfers between devices, both(): return in_order(part, values, lax.ppermute(values, axis, pairs))  43.3 us
    dot_general x10, matrix products, nn(): return jnp.dot(left, right, preferred_element_type=F32)  42.5 us
    pallas_call x2, Pallas kernels, attend_back(): pl.pallas_call(functools.partial(attend_back_kernel, chunk, spans), grid_...  36.8 us
    all_gather x1, waiting for transfers between devices, shards(): lax.all_gather(quarter, ('section', 'dp', 'group'), axis=1, tiled=True)  34.9 us
    ppermute x1, waiting for transfers between devices, shards(): got = lax.ppermute(sent, 'section', swap).astype(F32)  24.3 us
  transfers between devices with their start and end apart: 38, of which 17 were waited for; matrix products, arithmetic and copies ran while one was open for 32% of the time, Pallas kernels for 6%

profile of v6, /device:TPU:0, one launch (start us, length us, event | category | flops | bytes accessed | tf_op | source)
XLA Modules:
  0.0 720.5 jit_solution(3777892544178697679)
XLA Ops:
  32.3 4.4 all_gather.31
  40.3 5.7 collective-permute-done.1
  46.7 17.1 %collective-permute-done.2 = bf16[216,1024]{1,0:T(8,128)(2,1)} collective-permute-done((bf16[216,1024]{1,0:T(8,128)(2,1)S(1)}, bf16[216,1024]{1,0:T(8,128)(2,1)}, u32[]{:S(2)}, u32[]{:S(2)}) %collective-permute-start.2) | collective-permute-done | bytes 442400 | tf_op jit(solution)/shard_map/ppermute | solution.py:292
  71.1 4.2 multiply_convert_fusion
  75.2 43.3 %collective-permute-done.4 = bf16[4,216,1024]{2,1,0:T(8,128)(2,1)} collective-permute-done((bf16[4,216,1024]{2,1,0:T(8,128)(2,1)}, bf16[4,216,1024]{2,1,0:T(8,128)(2,1)}, u32[]{:S(2)}, u32[]{:S(2)}) %collective-permute-start.4) | collective-permute-done | bytes 1769504 | tf_op jit(solution)/shard_map/ppermute | solution.py:272
  118.5 5.1 maximum_select_fusion.2
  123.7 34.9 %all-gather.14.cloned.1.call-done = bf16[1,3,2048,1024]{3,2,1,0:T(8,128)(2,1)} async-done(((bf16[1,3,64,1024]{3,2,1,0:T(8,128)(2,1)}), bf16[1,3,2048,1024]{3,2,1,0:T(8,128)(2,1)}) %all-gather.14.cloned.1.call-update) | async-done | bytes 12582928 | tf_op jit(solution)/shard_map/all_gather | solution.py:287
  158.5 9.4 %convolution_convert_fusion.1.v_ref = bf16[2048,1024]{1,0:T(8,128)(2,1)} fusion(bf16[2048,1024]{1,0:T(8,128)(2,1)} %bitcast.283, bf16[3,2048,1024]{2,1,0:T(8,128)(2,1)} %bitcast.358), kind=kOutput, calls=%fused_computation.43 | convolution fusion | flops 4297064448 | bytes 10485760 | tf_op jit(solution)/shard_map/dot_general | solution.py:31
  173.1 8.0 %convolution_convert_fusion.2.k_ref = bf16[2048,1024]{1,0:T(8,128)(2,1)} fusion(bf16[2048,1024]{1,0:T(8,128)(2,1)S(1)} %bitcast.284, bf16[3,2048,1024]{2,1,0:T(8,128)(2,1)} %bitcast.360), kind=kOutput, calls=%fused_computation.44 | convolution fusion | flops 4297064448 | bytes 10485760 | tf_op jit(solution)/shard_map/dot_general | solution.py:31
  181.1 15.1 %attend.2 = (bf16[512,1024]{1,0:T(8,128)(2,1)S(1)}, f32[2,8,2,256]{3,2,1,0:T(2,128)S(1)}) custom-call(s32[2,2]{1,0:T(2,128)S(1)} %get-tuple-element.246.first_ref, s32[2,2]{1,0:T(2,128)S(1)} %get-tuple-element.231.stop_ref, s32[2,1,256]{2,1,0:T(1,128)S(1)} %broadcast_in_dim.74.lo_ref, s32[2,1,256]{2,1,0:T(1,128)S(1)} %bitcast.272, ...), custom_call_target="tpu_custom_call" | custom-call | flops 8589934592 | bytes 18874368 | tf_op jit(solution)/shard_map/attend/pallas_call | solution.py:186
  196.2 7.3 %maximum_select_fusion = bf16[2,2,4,216,1024]{4,3,0,1,2:T(8,128)(2,1)S(1)} fusion(bf16[1,2,4,216,1024]{4,3,0,1,2:T(8,128)(2,1)} %bitcast.20, bf16[1,2,4,216,1024]{4,3,0,1,2:T(8,128)(2,1)} %bitcast.19, pred[]{:T(512)S(6)} %eq.25), kind=kLoop, calls=%fused_computation.7 | loop fusion | flops 10616832 | bytes 14155777 | tf_op jit(solution)/shard_map/jit(_where)/select_n | solution.py:269
  216.8 4.0 attend.3
  229.2 3.8 slice.408
  233.0 16.4 %collective-permute-done.6 = bf16[512,1024]{1,0:T(8,128)(2,1)} collective-permute-done((bf16[512,1024]{1,0:T(8,128)(2,1)}, bf16[512,1024]{1,0:T(8,128)(2,1)}, u32[]{:S(2)}, u32[]{:S(2)}) %collective-permute-start.6) | collective-permute-done | bytes 1048608 | tf_op jit(solution)/shard_map/ppermute | solution.py:351
  249.4 12.0 %fusion.119 = f32[1024,2816]{1,0:T(8,128)} fusion(bf16[1024,2816]{1,0:T(8,128)(2,1)} %bitcast.372, bf16[512,1024]{1,0:T(8,128)(2,1)} %collective-permute-done.6, bf16[512,1024]{1,0:T(8,128)(2,1)} %multiply_convert_fusion.5), kind=kOutput, calls=%fused_computation.197 | convolution fusion | flops 5909774336 | bytes 19398656 | tf_op jit(solution)/shard_map/dot_general | solution.py:31
  261.4 10.8 %multiply_convert_fusion.2 = (bf16[1024,1408]{1,0:T(8,128)(2,1)S(1)}, bf16[1024,1408]{1,0:T(8,128)(2,1)S(1)}, bf16[1024,1408]{1,0:T(8,128)(2,1)}) fusion(f32[1024,2816]{1,0:T(8,128)} %fusion.119, bf16[1408,1024]{1,0:T(8,128)(2,1)S(1)} %bitcast.288, bf16[512,1024]{1,0:T(8,128)(2,1)S(1)} %bitcast.297, bf16[512,1024]{1,0:T(8,128)(2,1)S(1)} %bitcast.280), kind=kOutput, calls=%fused_computation.13 | convolution fusion | flops 2980052992 | bytes 25165824 | tf_op jit(solution)/shard_map/dot_general | solution.py:39
  273.8 4.1 fusion.93
  280.2 3.9 copy-done.95
  286.9 6.8 convolution_convert_fusion
  302.8 24.3 %collective-permute-done.11 = bf16[1024,512]{1,0:T(8,128)(2,1)} collective-permute-done((bf16[1024,512]{1,0:T(8,128)(2,1)}, bf16[1024,512]{1,0:T(8,128)(2,1)}, u32[]{:S(2)}, u32[]{:S(2)}) %collective-permute-start.11) | collective-permute-done | bytes 1048608 | tf_op jit(solution)/shard_map/ppermute | solution.py:405
  330.0 5.1 add_convert_fusion.5
  335.1 8.5 %add_convert_fusion = bf16[1024,1408]{1,0:T(8,128)(2,1)} fusion(bf16[1024,1408]{1,0:T(8,128)(2,1)} %collective-permute-done.9, bf16[1024,2816]{1,0:T(8,128)(2,1)} %copy-done.31, s32[]{:T(128)S(6)} %select_n.339, bf16[512,1024]{1,0:T(8,128)(2,1)} %collective-permute-done.6, bf16[512,1024]{1,0:T(8,128)(2,1)} %multiply_convert_fusion.5), kind=kOutput, calls=%fused_computation.11 | convolution fusion | flops 2961309696 | bytes 10747908 | tf_op jit(solution)/shard_map/dot_general | solution.py:35
  343.6 5.1 collective-permute-done.8
  348.8 6.5 multiply_reduce_fusion.5
  355.2 3.5 fusion.179
  362.8 11.5 %attend_back.2 = (bf16[512,1024]{1,0:T(8,128)(2,1)S(1)}, bf16[512,1024]{1,0:T(8,128)(2,1)S(1)}, bf16[512,1024]{1,0:T(8,128)(2,1)S(1)}) custom-call(s32[2,2]{1,0:T(2,128)S(1)} %get-tuple-element.249.first_ref, s32[2,2]{1,0:T(2,128)S(1)} %get-tuple-element.248.stop_ref, s32[2,1,256]{2,1,0:T(1,128)S(1)} %broadcast_in_dim.84.lo_ref, ...), custom_call_target="tpu_custom_call" | custom-call | flops 5368709120 | bytes 6291456 | tf_op jit(solution)/shard_map/attend_back/pallas_call | solution.py:210
  398.6 16.4 %collective-permute-done.12 = bf16[2,4,1,64,1408]{4,3,2,1,0:T(8,128)(2,1)S(1)} collective-permute-done((bf16[2,4,1,64,1408]{4,3,2,1,0:T(8,128)(2,1)S(1)}, bf16[2,4,1,64,1408]{4,3,2,1,0:T(8,128)(2,1)S(1)}, u32[]{:S(2)}, u32[]{:S(2)}) %collective-permute-start.12) | collective-permute-done | bytes 1441824 | tf_op jit(solution)/shard_map/ppermute | solution.py:366
  416.4 4.8 fusion
  422.9 6.5 dynamic-slice_convert_fusion
  429.4 4.5 fusion.2
  442.5 25.4 %attend_back.3 = (bf16[512,1024]{1,0:T(8,128)(2,1)S(1)}, bf16[2048,1024]{1,0:T(8,128)(2,1)}, bf16[2048,1024]{1,0:T(8,128)(2,1)}) custom-call(s32[2,2]{1,0:T(2,128)S(1)} %get-tuple-element.247.first_ref, s32[2,2]{1,0:T(2,128)S(1)} %get-tuple-element.230.stop_ref, s32[2,1,256]{2,1,0:T(1,128)S(1)} %copy-done.3, s32[2,1,256]{2,1,0:T(1,128)S(1)} %bitcast.273, ...), custom_call_target="tpu_custom_call" | custom-call | flops 21474836480 | bytes 18874368 | tf_op jit(solution)/shard_map/attend_back/pallas_call | solution.py:210
  468.8 4.1 fusion.98
  477.0 8.5 %fusion.41 = f32[2048,1024]{1,0:T(8,128)} fusion(bf16[2048,1024]{1,0:T(8,128)(2,1)S(1)} %copy-done.60, bf16[3,2048,1024]{2,1,0:T(8,128)(2,1)} %bitcast.364), kind=kOutput, calls=%fused_computation.99 | convolution fusion | flops 4294967296 | bytes 14680064 | tf_op jit(solution)/shard_map/dot_general | solution.py:39
  485.7 10.4 %convolution_add_fusion = f32[2048,1024]{1,0:T(8,128)S(1)} fusion(f32[2048,1024]{1,0:T(8,128)} %fusion.41, bf16[2048,1024]{1,0:T(8,128)(2,1)} %get-tuple-element.119, bf16[3,2048,1024]{2,1,0:T(8,128)(2,1)} %bitcast.365), kind=kOutput, calls=%fused_computation.41 | convolution fusion | flops 4297064448 | bytes 23068672 | tf_op jit(solution)/shard_map/dot_general | solution.py:39
  496.1 4.4 fusion.44
  505.1 3.7 fusion.69
  531.5 15.1 %collective-permute-done.17 = bf16[2,1024,256]{2,1,0:T(8,128)(2,1)S(1)} collective-permute-done((bf16[2,1024,256]{2,1,0:T(8,128)(2,1)S(1)}, bf16[2,1024,256]{2,1,0:T(8,128)(2,1)S(1)}, u32[]{:S(2)}, u32[]{:S(2)}) %collective-permute-start.17) | collective-permute-done | bytes 1048608 | tf_op jit(solution)/shard_map/ppermute | solution.py:366
  549.2 15.6 %collective-permute-done.18 = bf16[2,1024,256]{2,1,0:T(8,128)(2,1)} collective-permute-done((bf16[2,1024,256]{2,1,0:T(8,128)(2,1)}, bf16[2,1024,256]{2,1,0:T(8,128)(2,1)}, u32[]{:S(2)}, u32[]{:S(2)}) %collective-permute-start.18) | collective-permute-done | bytes 1048608 | tf_op jit(solution)/shard_map/ppermute | solution.py:366
  571.8 4.3 collective-permute-done.27
  578.8 5.0 add_convert_fusion.2
  593.2 4.7 collective-permute-done.20
  599.0 26.2 %collective-permute-done.21 = bf16[2,1024,128]{2,1,0:T(8,128)(2,1)} collective-permute-done((bf16[2,1024,128]{2,1,0:T(8,128)(2,1)}, bf16[2,1024,128]{2,1,0:T(8,128)(2,1)}, u32[]{:S(2)}, u32[]{:S(2)}) %collective-permute-start.21) | collective-permute-done | bytes 524320 | tf_op jit(solution)/shard_map/ppermute | solution.py:366
  627.5 7.5 %all-gather.3 = bf16[1408,256]{1,0:T(8,128)(2,1)S(1)} all-gather(bf16[352,256]{1,0:T(8,128)(2,1)S(1)} %add_convert_fusion.12), channel_id=5, replica_groups=mesh['section'=2,'group'=4,'dp'=4] {'group'}, dimensions={0}, use_global_device_ids=true | all-gather | bytes 901120 | tf_op jit(solution)/shard_map/all_gather | solution.py:468
  636.8 8.4 %collective-permute-done.24 = bf16[1024,512]{1,0:T(8,128)(2,1)} collective-permute-done((bf16[1024,512]{1,0:T(8,128)(2,1)}, bf16[1024,512]{1,0:T(8,128)(2,1)}, u32[]{:S(2)}, u32[]{:S(2)}) %collective-permute-start.24) | collective-permute-done | bytes 1048608 | tf_op jit(solution)/shard_map/ppermute | solution.py:462
  650.4 8.6 %maximum_convert_fusion = f32[128,5632]{1,0:T(8,128)} fusion(bf16[64,1408]{1,0:T(8,128)(2,1)S(1)} %get-tuple-element.193, bf16[64,1408]{1,0:T(8,128)(2,1)S(1)} %get-tuple-element.194, bf16[64,1408]{1,0:T(8,128)(2,1)S(1)} %get-tuple-element.195, bf16[64,1408]{1,0:T(8,128)(2,1)S(1)} %get-tuple-element.196, bf16[64,1408]{1,0:T(8,128)(2,1)S(1)} %get-tuple-element.197, ...), kind=kLoop, calls=%fused_computation.170 | loop fusion | flops 11534336 | bytes 4325376 | tf_op jit(solution)/shard_map/concatenate | solution.py:476
  659.1 16.2 %all-gather.4 = f32[4,4,1024]{2,1,0:T(4,128)S(1)} all-gather(f32[1,4,1024]{2,1,0:T(4,128)S(1)} %bitcast.320), channel_id=3, replica_groups=mesh['section'=2,'group'=4,'dp'=4] {'dp'}, dimensions={0}, use_global_device_ids=true | all-gather | bytes 81920 | tf_op jit(solution)/shard_map/all_gather | solution.py:485
  677.9 4.9 collective-permute-done.29
  692.9 12.2 %all-gather.12.cloned.1.call-done = bf16[4,4,256,256]{3,2,1,0:T(8,128)(2,1)} async-done(((bf16[1,4,256,256]{3,2,1,0:T(8,128)(2,1)}), bf16[4,4,256,256]{3,2,1,0:T(8,128)(2,1)}) %all-gather.12.cloned.1.call-update) | async-done | bytes 2097168 | tf_op jit(solution)/shard_map/all_gather | solution.py:468
  (438 shorter events, 206.3 us)
Async XLA Ops:
  7.2 151.3 %all-gather.14.cloned.1.call-start = ((), (), s32[]{:S(2)}) async-start(), calls=%async_computation.10 | async-start | bytes 12976128 | tf_op jit(solution)/shard_map/all_gather | solution.py:287
  9.4 223.6 %all-gather.10.cloned.1.call-start = ((), (), s32[]{:S(2)}) async-start(), calls=%async_computation.4 | async-start | bytes 6127616 | tf_op jit(solution)/shard_map/all_gather | solution.py:283
  10.4 13.4 %collective-permute-start = (bf16[64,1024]{1,0:T(8,128)(2,1)S(1)}, bf16[64,1024]{1,0:T(8,128)(2,1)S(1)}, u32[]{:S(2)}, u32[]{:S(2)}) collective-permute-start(bf16[64,1024]{1,0:T(8,128)(2,1)S(1)} %fusion.224), channel_id=1, source_target_pairs={{0,16},{16,0},{1,17},{17,1},{2,18},{18,2},{3,19},{19,3},{4,20},{20... | collective-permute-start | bytes 393224 | tf_op jit(solution)/shard_map/ppermute | solution.py:272
  15.9 52.7 %collective-permute-start.7 = (bf16[32,2816]{1,0:T(8,128)(2,1)}, bf16[32,2816]{1,0:T(8,128)(2,1)}, u32[]{:S(2)}, u32[]{:S(2)}) collective-permute-start(bf16[32,2816]{1,0:T(8,128)(2,1)} %pad_maximum_fusion.13), channel_id=1, source_target_pairs={{0,16},{16,0},{1,17},{17,1},{2,18},{18,2},{3,19},{19,3},{4,20},{20... | collective-permute-start | bytes 540680 | tf_op jit(solution)/shard_map/ppermute | solution.py:281
  17.1 151.4 %copy-start.78 = (s32[1,2,2,128]{3,1,2,0:T(2,128)}, s32[1,2,2,128]{3,1,2,0:T(2,128)S(1)}, u32[]{:S(2)}) copy-start(s32[1,2,2,128]{3,1,2,0:T(2,128)S(1)} %copy.33) | copy-start | bytes 6148
  22.0 147.4 %copy-start.19 = (f32[2,256,1024]{2,1,0:T(8,128)}, f32[2,256,1024]{2,1,0:T(8,128)S(1)}, u32[]{:S(2)}) copy-start(f32[2,256,1024]{2,1,0:T(8,128)S(1)} %get-tuple-element.239) | copy-start | bytes 6291460
  23.9 22.1 %collective-permute-start.1 = (bf16[216,1024]{1,0:T(8,128)(2,1)S(1)}, bf16[216,1024]{1,0:T(8,128)(2,1)S(1)}, u32[]{:S(2)}, u32[]{:S(2)}) collective-permute-start(bf16[216,1024]{1,0:T(8,128)(2,1)S(1)} %pad_maximum_fusion.11), channel_id=1, source_target_pairs={{0,1},{1,2},{2,3},{3,0},{4,5},{5,6},{6,7},{7,4},{8,9},{9,10},{10,1... | collective-permute-start | bytes 1327112 | tf_op jit(solution)/shard_map/ppermute | solution.py:292
  26.6 37.3 %collective-permute-start.2 = (bf16[216,1024]{1,0:T(8,128)(2,1)S(1)}, bf16[216,1024]{1,0:T(8,128)(2,1)}, u32[]{:S(2)}, u32[]{:S(2)}) collective-permute-start(bf16[216,1024]{1,0:T(8,128)(2,1)S(1)} %pad_maximum_fusion.11), channel_id=1, source_target_pairs={{0,2},{1,3},{2,0},{3,1},{4,6},{5,7},{6,4},{7,5},{8,10},{9,11},{10,... | collective-permute-start | bytes 1327112 | tf_op jit(solution)/shard_map/ppermute | solution.py:292
  36.7 28.9 %collective-permute-start.3 = (bf16[216,1024]{1,0:T(8,128)(2,1)S(1)}, bf16[216,1024]{1,0:T(8,128)(2,1)S(1)}, u32[]{:S(2)}, u32[]{:S(2)}) collective-permute-start(bf16[216,1024]{1,0:T(8,128)(2,1)S(1)} %pad_maximum_fusion.11), channel_id=1, source_target_pairs={{0,3},{1,0},{2,1},{3,2},{4,7},{5,4},{6,5},{7,6},{8,11},{9,8},{10,9... | collective-permute-start | bytes 1327112 | tf_op jit(solution)/shard_map/ppermute | solution.py:292
  39.5 28.5 %copy-start.90 = (s32[4,256]{1,0:T(4,128)S(1)}, s32[4,256]{1,0:T(4,128)}, u32[]{:S(2)}) copy-start(s32[4,256]{1,0:T(4,128)} %param.11) | copy-start | bytes 12292
  39.5 29.1 %copy-start.67 = (bf16[32,1408]{1,0:T(8,128)(2,1)S(1)}, bf16[32,1408]{1,0:T(8,128)(2,1)}, u32[]{:S(2)}) copy-start(bf16[32,1408]{1,0:T(8,128)(2,1)} %get-tuple-element.201) | copy-start | bytes 270340
  39.5 29.1 %copy-start.94 = (s32[2]{0:T(128)S(1)}, s32[2]{0:T(128)}, u32[]{:S(2)}) copy-start(s32[2]{0:T(128)} %copy-done.93) | copy-start | bytes 28
  66.4 52.1 %collective-permute-start.4 = (bf16[4,216,1024]{2,1,0:T(8,128)(2,1)}, bf16[4,216,1024]{2,1,0:T(8,128)(2,1)}, u32[]{:S(2)}, u32[]{:S(2)}) collective-permute-start(bf16[4,216,1024]{2,1,0:T(8,128)(2,1)} %bitcast_dynamic-update-slice_fusion), channel_id=1, source_target_pairs={{0,8},{4,12},{8,0},{12,4},{1,9},{5,13},{9,1},{13,5},{2,10},{6,14},... | collective-permute-start | bytes 5308424 | tf_op jit(solution)/shard_map/ppermute | solution.py:272
  68.6 100.8 %copy-start.71 = (f32[1,1,1024]{2,1,0:T(1,128)}, f32[1,1,1024]{2,1,0:T(1,128)S(1)}, u32[]{:S(2)}) copy-start(f32[1,1,1024]{2,1,0:T(1,128)S(1)} %get-tuple-element.215) | copy-start | bytes 12292
  70.5 496.8 %reduce-scatter.9.cloned.1.call-start = ((), (), s32[]{:S(2)}) async-start(), calls=%async_computation.7 | async-start | bytes 1802240 | tf_op jit(solution)/shard_map/reduce_scatter | solution.py:379
  167.9 28.3 %collective-permute-start.5 = (bf16[2,4,216,1024]{3,2,0,1:T(8,128)(2,1)}, bf16[2,4,216,1024]{3,2,0,1:T(8,128)(2,1)}, u32[]{:S(2)}, u32[]{:S(2)}) collective-permute-start(bf16[2,4,216,1024]{3,2,0,1:T(8,128)(2,1)} %maximum_select_fusion.2), channel_id=1, source_target_pairs={{0,4},{4,0},{8,12},{12,8},{1,5},{5,1},{9,13},{13,9},{2,6},{6,2},{1... | collective-permute-start | bytes 10616840 | tf_op jit(solution)/shard_map/ppermute | solution.py:272
  169.4 38.7 %copy-start.28 = (f32[512,1024]{1,0:T(8,128)}, f32[512,1024]{1,0:T(8,128)S(1)}, u32[]{:S(2)}) copy-start(f32[512,1024]{1,0:T(8,128)S(1)} %bitcast_divide_fusion) | copy-start | bytes 6291460
  220.9 140.3 %copy-start.8 = (bf16[512,1024]{1,0:T(8,128)(2,1)}, bf16[512,1024]{1,0:T(8,128)(2,1)S(1)}, u32[]{:S(2)}) copy-start(bf16[512,1024]{1,0:T(8,128)(2,1)S(1)} %get-tuple-element.86.c_ref) | copy-start | bytes 3145732
  223.6 25.7 %collective-permute-start.6 = (bf16[512,1024]{1,0:T(8,128)(2,1)}, bf16[512,1024]{1,0:T(8,128)(2,1)}, u32[]{:S(2)}, u32[]{:S(2)}) collective-permute-start(bf16[512,1024]{1,0:T(8,128)(2,1)} %multiply_convert_fusion.5), channel_id=1, source_target_pairs={{0,16},{16,0},{1,17},{17,1},{2,18},{18,2},{3,19},{19,3},{4,20},{20... | collective-permute-start | bytes 3145736 | tf_op jit(solution)/shard_map/ppermute | solution.py:351
  293.7 36.3 %collective-permute-start.10 = (bf16[1408,512]{1,0:T(8,128)(2,1)}, bf16[1408,512]{1,0:T(8,128)(2,1)}, u32[]{:S(2)}, u32[]{:S(2)}) collective-permute-start(bf16[1408,512]{1,0:T(8,128)(2,1)} %convolution_convert_fusion.3), channel_id=1, source_target_pairs={{0,4},{4,0},{8,12},{12,8},{1,5},{5,1},{9,13},{13,9},{2,6},{6,2},{1... | collective-permute-start | bytes 4325384 | tf_op jit(solution)/shard_map/ppermute | solution.py:389
  293.7 41.4 %collective-permute-start.9 = (bf16[1024,1408]{1,0:T(8,128)(2,1)}, bf16[1024,1408]{1,0:T(8,128)(2,1)}, u32[]{:S(2)}, u32[]{:S(2)}) collective-permute-start(bf16[1024,1408]{1,0:T(8,128)(2,1)} %convolution_convert_fusion), channel_id=1, source_target_pairs={{0,4},{4,0},{8,12},{12,8},{1,5},{5,1},{9,13},{13,9},{2,6},{6,2},{1... | collective-permute-start | bytes 8650760 | tf_op jit(solution)/shard_map/ppermute | solution.py:389
  300.8 26.3 %collective-permute-start.11 = (bf16[1024,512]{1,0:T(8,128)(2,1)}, bf16[1024,512]{1,0:T(8,128)(2,1)}, u32[]{:S(2)}, u32[]{:S(2)}) collective-permute-start(bf16[1024,512]{1,0:T(8,128)(2,1)} %fusion.24), channel_id=1, source_target_pairs={{0,16},{16,0},{1,17},{17,1},{2,18},{18,2},{3,19},{19,3},{4,20},{20... | collective-permute-start | bytes 3145736 | tf_op jit(solution)/shard_map/ppermute | solution.py:405
  302.3 46.4 %collective-permute-start.8 = (bf16[512,1024]{1,0:T(8,128)(2,1)}, bf16[512,1024]{1,0:T(8,128)(2,1)}, u32[]{:S(2)}, u32[]{:S(2)}) collective-permute-start(bf16[512,1024]{1,0:T(8,128)(2,1)} %fusion.93), channel_id=1, source_target_pairs={{0,16},{16,0},{1,17},{17,1},{2,18},{18,2},{3,19},{19,3},{4,20},{20... | collective-permute-start | bytes 3145736 | tf_op jit(solution)/shard_map/ppermute | solution.py:397
  379.3 37.1 %collective-permute-start.13 = (bf16[4,1024,512]{2,1,0:T(8,128)(2,1)}, bf16[4,1024,512]{2,1,0:T(8,128)(2,1)}, u32[]{:S(2)}, u32[]{:S(2)}) collective-permute-start(bf16[4,1024,512]{2,1,0:T(8,128)(2,1)} %pad_maximum_fusion.1), channel_id=1, source_target_pairs={{0,4},{4,0},{8,12},{12,8},{1,5},{5,1},{9,13},{13,9},{2,6},{6,2},{1... | collective-permute-start | bytes 12582920 | tf_op jit(solution)/shard_map/ppermute | solution.py:389
  380.9 34.0 %collective-permute-start.12 = (bf16[2,4,1,64,1408]{4,3,2,1,0:T(8,128)(2,1)S(1)}, bf16[2,4,1,64,1408]{4,3,2,1,0:T(8,128)(2,1)S(1)}, u32[]{:S(2)}, u32[]{:S(2)}) collective-permute-start(bf16[2,4,1,64,1408]{4,3,2,1,0:T(8,128)(2,1)S(1)} %constant_dynamic-slice_fusion.11), channel_id=1, source_target_pairs={{0,8},{4,12},{8,0},{12,4},{1,9},{5,13},{9,1},{13,5},{2,10},{6,14},... | collective-permute-start | bytes 4325384 | tf_op jit(solution)/shard_map/ppermute | solution.py:366
  397.3 38.4 %copy-start.45 = (bf16[512,1024]{1,0:T(8,128)(2,1)}, bf16[512,1024]{1,0:T(8,128)(2,1)S(1)}, u32[]{:S(2)}) copy-start(bf16[512,1024]{1,0:T(8,128)(2,1)S(1)} %fusion.19) | copy-start | bytes 3145732
  421.2 155.8 %reduce-scatter.11.cloned.1.call-start = ((), (), s32[]{:S(2)}) async-start(), calls=%async_computation.8 | async-start | bytes 1802240 | tf_op jit(solution)/shard_map/reduce_scatter | solution.py:379
  437.8 189.7 %reduce-scatter.5.cloned.1.call-start = ((), (), s32[]{:S(2)}) async-start(), calls=%async_computation.5 | async-start | bytes 1310720 | tf_op jit(solution)/shard_map/reduce_scatter | solution.py:379
  441.0 67.9 %collective-permute-start.16 = (bf16[4,1024,256]{2,1,0:T(8,128)(2,1)}, bf16[4,1024,256]{2,1,0:T(8,128)(2,1)}, u32[]{:S(2)}, u32[]{:S(2)}) collective-permute-start(bf16[4,1024,256]{2,1,0:T(8,128)(2,1)} %constant_dynamic-slice_fusion.10), channel_id=1, source_target_pairs={{0,16},{16,0},{1,17},{17,1},{2,18},{18,2},{3,19},{19,3},{4,20},{20... | collective-permute-start | bytes 6291464 | tf_op jit(solution)/shard_map/ppermute | solution.py:366
  485.6 25.6 %collective-permute-start.15 = (bf16[2,1024,512]{2,1,0:T(8,128)(2,1)S(1)}, bf16[2,1024,512]{2,1,0:T(8,128)(2,1)}, u32[]{:S(2)}, u32[]{:S(2)}) collective-permute-start(bf16[2,1024,512]{2,1,0:T(8,128)(2,1)S(1)} %pad_maximum_fusion.6), channel_id=1, source_target_pairs={{0,4},{4,0},{8,12},{12,8},{1,5},{5,1},{9,13},{13,9},{2,6},{6,2},{1... | collective-permute-start | bytes 6291464 | tf_op jit(solution)/shard_map/ppermute | solution.py:389
  496.1 32.0 %copy-start.18 = (f32[2048,1024]{1,0:T(8,128)}, f32[2048,1024]{1,0:T(8,128)S(1)}, u32[]{:S(2)}) copy-start(f32[2048,1024]{1,0:T(8,128)S(1)} %convolution_add_fusion) | copy-start | bytes 25165828
  500.5 13.3 %collective-permute-start.14 = (bf16[2,1024,512]{2,1,0:T(8,128)(2,1)}, bf16[2,1024,512]{2,1,0:T(8,128)(2,1)}, u32[]{:S(2)}, u32[]{:S(2)}) collective-permute-start(bf16[2,1024,512]{2,1,0:T(8,128)(2,1)} %pad_maximum_fusion.5), channel_id=1, source_target_pairs={{0,4},{4,0},{8,12},{12,8},{1,5},{5,1},{9,13},{13,9},{2,6},{6,2},{1... | collective-permute-start | bytes 6291464 | tf_op jit(solution)/shard_map/ppermute | solution.py:389
  516.6 31.3 %collective-permute-start.19 = (bf16[4,1024,128]{2,1,0:T(8,128)(2,1)S(1)}, bf16[4,1024,128]{2,1,0:T(8,128)(2,1)S(1)}, u32[]{:S(2)}, u32[]{:S(2)}) collective-permute-start(bf16[4,1024,128]{2,1,0:T(8,128)(2,1)S(1)} %constant_dynamic-slice_fusion.6), channel_id=1, source_target_pairs={{0,8},{4,12},{8,0},{12,4},{1,9},{5,13},{9,1},{13,5},{2,10},{6,14},... | collective-permute-start | bytes 3145736 | tf_op jit(solution)/shard_map/ppermute | solution.py:366
  518.6 46.2 %collective-permute-start.18 = (bf16[2,1024,256]{2,1,0:T(8,128)(2,1)}, bf16[2,1024,256]{2,1,0:T(8,128)(2,1)}, u32[]{:S(2)}, u32[]{:S(2)}) collective-permute-start(bf16[2,1024,256]{2,1,0:T(8,128)(2,1)} %constant_dynamic-slice_fusion.7), channel_id=1, source_target_pairs={{0,8},{4,12},{8,0},{12,4},{1,9},{5,13},{9,1},{13,5},{2,10},{6,14},... | collective-permute-start | bytes 3145736 | tf_op jit(solution)/shard_map/ppermute | solution.py:366
  520.0 26.6 %collective-permute-start.17 = (bf16[2,1024,256]{2,1,0:T(8,128)(2,1)S(1)}, bf16[2,1024,256]{2,1,0:T(8,128)(2,1)S(1)}, u32[]{:S(2)}, u32[]{:S(2)}) collective-permute-start(bf16[2,1024,256]{2,1,0:T(8,128)(2,1)S(1)} %constant_dynamic-slice_fusion.8), channel_id=1, source_target_pairs={{0,16},{16,0},{1,17},{17,1},{2,18},{18,2},{3,19},{19,3},{4,20},{20... | collective-permute-start | bytes 3145736 | tf_op jit(solution)/shard_map/ppermute | solution.py:366
  567.3 78.8 %all-gather.16.cloned.1.call-start = ((), (), s32[]{:S(2)}) async-start(), calls=%async_computation.11 | async-start | bytes 1802240 | tf_op jit(solution)/shard_map/all_gather | solution.py:468
  568.5 7.6 %collective-permute-start.27 = (bf16[64,1408]{1,0:T(8,128)(2,1)S(1)}, bf16[64,1408]{1,0:T(8,128)(2,1)S(1)}, u32[]{:S(2)}, u32[]{:S(2)}) collective-permute-start(bf16[64,1408]{1,0:T(8,128)(2,1)S(1)} %get-tuple-element.211), channel_id=1, source_target_pairs={{0,16},{16,0},{1,17},{17,1},{2,18},{18,2},{3,19},{19,3},{4,20},{20... | collective-permute-start | bytes 540680 | tf_op jit(solution)/shard_map/ppermute | solution.py:432
  577.0 98.3 %reduce-scatter.7.cloned.1.call-start = ((), (), s32[]{:S(2)}) async-start(), calls=%async_computation.6 | async-start | bytes 1310720 | tf_op jit(solution)/shard_map/reduce_scatter | solution.py:379
  578.0 12.4 %collective-permute-start.28 = (bf16[352,256]{1,0:T(8,128)(2,1)S(1)}, bf16[352,256]{1,0:T(8,128)(2,1)S(1)}, u32[]{:S(2)}, u32[]{:S(2)}) collective-permute-start(bf16[352,256]{1,0:T(8,128)(2,1)S(1)} %constant_dynamic-slice_fusion.1), channel_id=1, source_target_pairs={{0,8},{4,12},{8,0},{12,4},{1,9},{5,13},{9,1},{13,5},{2,10},{6,14},... | collective-permute-start | bytes 540680 | tf_op jit(solution)/shard_map/ppermute | solution.py:366
  584.7 13.1 %collective-permute-start.20 = (bf16[2,1024,128]{2,1,0:T(8,128)(2,1)}, bf16[2,1024,128]{2,1,0:T(8,128)(2,1)}, u32[]{:S(2)}, u32[]{:S(2)}) collective-permute-start(bf16[2,1024,128]{2,1,0:T(8,128)(2,1)} %constant_dynamic-slice_fusion.5), channel_id=1, source_target_pairs={{0,8},{4,12},{8,0},{12,4},{1,9},{5,13},{9,1},{13,5},{2,10},{6,14},... | collective-permute-start | bytes 1572872 | tf_op jit(solution)/shard_map/ppermute | solution.py:366
  587.5 39.9 %collective-permute-start.22 = (bf16[1024,512]{1,0:T(8,128)(2,1)}, bf16[1024,512]{1,0:T(8,128)(2,1)}, u32[]{:S(2)}, u32[]{:S(2)}) collective-permute-start(bf16[1024,512]{1,0:T(8,128)(2,1)} %get-tuple-element.187), channel_id=1, source_target_pairs={{0,16},{16,0},{1,17},{17,1},{2,18},{18,2},{3,19},{19,3},{4,20},{20... | collective-permute-start | bytes 3145736 | tf_op jit(solution)/shard_map/ppermute | solution.py:462
  590.1 35.1 %collective-permute-start.21 = (bf16[2,1024,128]{2,1,0:T(8,128)(2,1)}, bf16[2,1024,128]{2,1,0:T(8,128)(2,1)}, u32[]{:S(2)}, u32[]{:S(2)}) collective-permute-start(bf16[2,1024,128]{2,1,0:T(8,128)(2,1)} %constant_dynamic-slice_fusion.4), channel_id=1, source_target_pairs={{0,16},{16,0},{1,17},{17,1},{2,18},{18,2},{3,19},{19,3},{4,20},{20... | collective-permute-start | bytes 1572872 | tf_op jit(solution)/shard_map/ppermute | solution.py:366
  591.4 53.9 %collective-permute-start.24 = (bf16[1024,512]{1,0:T(8,128)(2,1)}, bf16[1024,512]{1,0:T(8,128)(2,1)}, u32[]{:S(2)}, u32[]{:S(2)}) collective-permute-start(bf16[1024,512]{1,0:T(8,128)(2,1)} %get-tuple-element.132), channel_id=1, source_target_pairs={{0,16},{16,0},{1,17},{17,1},{2,18},{18,2},{3,19},{19,3},{4,20},{20... | collective-permute-start | bytes 3145736 | tf_op jit(solution)/shard_map/ppermute | solution.py:462
  627.5 77.6 %all-gather.12.cloned.1.call-start = ((), (), s32[]{:S(2)}) async-start(), calls=%async_computation.9 | async-start | bytes 2621440 | tf_op jit(solution)/shard_map/all_gather | solution.py:468
  635.1 1.7 collective-permute-start.23
  645.2 3.7 collective-permute-start.25
  649.0 10.1 %collective-permute-start.26 = (f32[4,1024]{1,0:T(4,128)S(1)}, f32[4,1024]{1,0:T(4,128)S(1)}, u32[]{:S(2)}, u32[]{:S(2)}) collective-permute-start(f32[4,1024]{1,0:T(4,128)S(1)} %add.447), channel_id=1, source_target_pairs={{0,16},{16,0},{1,17},{17,1},{2,18},{18,2},{3,19},{19,3},{4,20},{20... | collective-permute-start | bytes 49160 | tf_op jit(solution)/shard_map/ppermute | solution.py:483
  676.3 6.4 collective-permute-start.29
  (94 other events, 671.6 us)
Sparse Core Ops, SparseCore 0:
  11.5 146.9 all-gather.13
  161.4 57.2 all-gather.9
  421.3 34.7 reduce-scatter.8
  458.3 32.1 reduce-scatter.10
  567.4 32.0 reduce-scatter.4
  601.0 17.5 all-gather.15
  627.6 30.6 reduce-scatter.6
  683.9 21.1 all-gather.11

commit v7 on v5

--- a/solution.py
+++ b/solution.py
@@ -292,10 +292,8 @@
     for step in range(line):
         moved = lax.ppermute(quarter, "dp", [(i, (i + step) % line) for i in range(line)]) if step else quarter
         down = lax.dynamic_update_slice_in_dim(down, moved[None], (place - step) % line, 0)
-    matrices, down = together((matrices, down))
     matrices = matrices.reshape(sections, groups, D, D)
     wq, wk, wv, wo = [matrices[:, index] for index in range(4)]
-    down = both(down, side, "group", side_pairs)
 
     rows = byte_states.shape[0] // sections
     mine = lambda a: lax.dynamic_slice_in_dim(a, section * rows, rows, 0)
@@ -327,10 +325,8 @@
     k1 = nn(key_in, wk[0]).astype(BF)
     v1 = nn(key_in, wv[0]).astype(BF)
     v1, down = together((v1, down))
-    down = both(down, core, "group", core_pairs)
+    down = both(down, side, "group", side_pairs)
     c1, l1 = attend(cross, q1, k1, v1, 8)
-    c1, down = together((c1, down))
-    w_down = down.transpose(2, 1, 0, 3, 4).reshape(units, D)
     carried = (pooled + nn(c1, wo[0])).astype(BF)
 
     carried_wide = carried.astype(F32)
@@ -340,6 +336,9 @@
     k2 = nn(normed_in, wk[1]).astype(BF)
     v2 = nn(normed_in, wv[1]).astype(BF)
     c2, l2 = attend(causal, q2, k2, v2, 8, CAUSAL_SPANS)
+    c2, down = together((c2, down))
+    down = both(down, core, "group", core_pairs)
+    w_down = down.transpose(2, 1, 0, 3, 4).reshape(units, D)
     residual = carried_wide + nn(c2, wo[1])
     second_scale = scale_of(residual)
     mix_in = (residual * second_scale * gains[1, 1]).astype(BF)
@@ -396,17 +395,15 @@
     sent = lax.dynamic_slice_in_dim(parts, (1 - section) * half, half, 1).astype(BF)
     kept = lax.dynamic_slice_in_dim(parts, section * half, half, 1)
     dgu_own, sent = together((dgu_own, sent))
-    got = lax.ppermute(sent, "section", swap).astype(F32)
-    latents = in_order(section, kept[:tokens] + got[tokens:], kept[tokens:] + got[:tokens])
-    latents_out = latents.astype(BF).reshape(sections * rows, PATCHES, half)
-
+    got = lax.ppermute(sent, "section", swap)
+
+    half_in, half_down = of_chip(in_pairs, send_in), of_chip(down_pairs, send_down)
+    mix_got, half_in, half_down = together((mix_got, half_in, half_down))
     grad_mixed = nt(dgu_own, w_in) + mix_got.astype(F32)
     grad_mix, gain_mix = norm_backward(residual, second_scale, gains[1, 1], grad_mixed)
     grad_residual = grad_mix + cot.astype(F32)
     branch = grad_residual.astype(BF)
     dc2 = nt(branch, wo[1]).astype(BF)
-    half_in, half_down = of_chip(in_pairs, send_in), of_chip(down_pairs, send_down)
-    dc2, half_in, half_down = together((dc2, half_in, half_down))
 
     dq2, dk2, dv2 = attend_back(causal, q2, k2, v2, l2, c2, dc2, 8, CAUSAL_SPANS)
     two_pairs = [(normed_in, dq2), (normed_in, dk2), (normed_in, dv2), (c2, branch)]
@@ -418,9 +415,12 @@
     dc1 = nt(d_carried, wo[0]).astype(BF)
     half_in = over_side(half_in.reshape(sections, line, 2, -1, units), 2)
     half_two = of_chip(two_pairs, send_two)
-    dc1, half_in, half_two = together((dc1, half_in, half_two))
+    dc1, half_in, half_two, got = together((dc1, half_in, half_two, got))
+    got = got.astype(F32)
+    latents = in_order(section, kept[:tokens] + got[tokens:], kept[tokens:] + got[:tokens])
+    latents_out = latents.astype(BF).reshape(sections * rows, PATCHES, half)
     sum_down = over_side(line_sum(half_down, 0), 1)
-    sum_in = line_sum(half_in, 1).reshape(sections, -1, units)
+    sum_in = line_sum(half_in.reshape(sections, -1, units), 1)
     sum_in = jnp.stack([lax.dynamic_index_in_dim(sum_in, section, 0, False),
                         lax.ppermute(lax.dynamic_index_in_dim(sum_in, 1 - section, 0, False), "section", swap)])
     sum_in = jnp.where(section == 0, sum_in, sum_in[::-1])
@@ -430,28 +430,31 @@
     one_pairs = [(query_in, dq1), (key_in, dk1)], [(key_in, dv1), (c1, d_carried)]
     send_one = [to_core(pairs) for pairs in one_pairs]
     dq1, dk1, dv1, send_one, half_two = together((dq1, dk1, dv1, send_one, half_two))
-    sum_two = line_sum(over_side(half_two, 2), 1)
+    half_two = over_side(half_two, 2)
+    grad_query_in = nt(dq1, wq[0])
+    grad_key_in = nt(dk1, wk[0]) + nt(dv1, wv[0])
+    dq1, dk1, dv1, grad_query_in, grad_key_in = together((dq1, dk1, dv1, grad_query_in, grad_key_in))
+    one_pairs = [(query_in, dq1), (key_in, dk1)], [(key_in, dv1), (c1, d_carried)]
     half_one = [of_chip(pairs, sent) for pairs, sent in zip(one_pairs, send_one)]
-    dq1, dk1, dv1, half_one = together((dq1, dk1, dv1, half_one))
-    half_one = jnp.concatenate(
-        [over_side(over_section(half_one[0], 2), 2), over_section(over_side(half_one[1], 2), 2)], axis=0
-    )
-    sum_one = line_sum(half_one, 1)
-    grad_pooled, gain_query = norm_backward(pooled, query_scale, gains[0, 0], nt(dq1, wq[0]))
-    grad_wide, gain_key = norm_backward(
-        wide, key_scale, gains[0, 1], nt(dk1, wk[0]) + nt(dv1, wv[0])
-    )
+    grad_query_in, grad_key_in, half_one, half_two = together((grad_query_in, grad_key_in, half_one, half_two))
+    sum_two = line_sum(half_two, 1)
+    half_one = over_section(half_one[0], 2), over_side(half_one[1], 2)
+    grad_pooled, gain_query = norm_backward(pooled, query_scale, gains[0, 0], grad_query_in)
+    grad_wide, gain_key = norm_backward(wide, key_scale, gains[0, 1], grad_key_in)
     per_patch = (grad_pooled + d_carried.astype(F32)) / count
     spread_back = jnp.einsum(
         "rpb,rpd->rbd", member, per_patch.astype(BF).reshape(rows, PATCHES, D), preferred_element_type=F32
     )
     byte_grads = (grad_wide + spread_back.reshape(rows * ROW_BYTES, D)).astype(BF)
-
+    byte_grads, half_one, sum_two = together((byte_grads, half_one, sum_two))
     byte_grads = byte_grads.reshape(rows, ROW_BYTES, D)
     other = lax.dynamic_slice_in_dim(byte_grads, (1 - section) * half, half, 2)
     own = lax.dynamic_slice_in_dim(byte_grads, section * half, half, 2)
-    bytes_out = in_order(section, own, lax.ppermute(other, "section", swap))
-    bytes_out = bytes_out.reshape(sections * rows, ROW_BYTES, half)
+    got = lax.ppermute(other, "section", swap)
+    half_one = jnp.concatenate([over_side(half_one[0], 2), over_section(half_one[1], 2)], axis=0)
+    sum_one = line_sum(half_one, 1)
+    sum_one, got = together((sum_one, got))
+    bytes_out = in_order(section, own, got).reshape(sections * rows, ROW_BYTES, half)
 
     def of_group(part):
         every = lax.all_gather(part, "group", axis=0, tiled=False)

time: 673 us -> 655 us (0.973)
  waiting for transfers between devices: 234 us -> 219 us
    reduce_scatter x3 -> x4, waiting for transfers between devices: 0.04 us -> 37.2 us  [line_sum(): return lax.psum_scatter(values, 'dp', scatter_dimension=where, tiled=True)]
    ppermute x3, waiting for transfers between devices: 33.1 us -> 4.24 us  [shards(): gain_grads = gain_grads + lax.ppermute(gain_grads, axis, pairs)]
    ppermute x1, waiting for transfers between devices: 16.6 us -> 1.67 us  [shards(): mix_got = lax.ppermute(mix_other, 'section', swap)]
    ppermute x2, waiting for transfers between devices: 11.2 us -> 0.01 us  [both(): return in_order(part, values, lax.ppermute(values, axis, pairs))]
    reduce_sum x0 -> x2, other arithmetic: none -> 7.39 us  [norm_backward(): grad_gain = jnp.sum(incoming * values * row_scale, axis=0)]
  transfers between devices with their start and end apart: 36 -> 36, of which waited for: 15 -> 15; matrix products, arithmetic and copies ran while one was open for 35% -> 38% of each run, Pallas kernels for 7% -> 9%
where the time goes in v7:
time: 655 us; the launch traced here: 650 us
  waiting for transfers between devices  219 us (33%)
  matrix products  170 us (26%)
  other arithmetic  91 us (14%)
  Pallas kernels  60.5 us (9%)
  local copies, waits for them, and re-layouts  42.6 us (7%)
  blocking collectives  25.8 us (4%)
  starting transfers between devices  25 us (4%)
  between operations  15.9 us (2%)
    all_gather x1, waiting for transfers between devices, shards(): lax.all_gather(matrix, ('section', 'group', 'dp'), axis=0, tiled=True)  89.6 us
    dot_general x11, matrix products, nt(): lax.dot_general(left, right, (((1,), (1,)), ((), ())), preferred_element_...  61.9 us
    dot_general x10, matrix products, nn(): return jnp.dot(left, right, preferred_element_type=F32)  54.3 us
    ppermute x8, waiting for transfers between devices, exchanged(): lax.ppermute(other, axis, pairs).astype(F32)  50 us
    dot_general x20, matrix products, tn(): lax.dot_general(left, right, (((0,), (0,)), ((), ())), preferred_element_...  48.6 us
    pallas_call x2, Pallas kernels, attend_back(): pl.pallas_call(functools.partial(attend_back_kernel, chunk, spans), grid_...  40 us
    reduce_scatter x4, waiting for transfers between devices, line_sum(): return lax.psum_scatter(values, 'dp', scatter_dimension=where, tiled=True)  37.2 us
    ppermute x1, waiting for transfers between devices, shards(): lax.ppermute(mix_in, 'section', swap)  22.3 us
  transfers between devices with their start and end apart: 36, of which 15 were waited for; matrix products, arithmetic and copies ran while one was open for 38% of the time, Pallas kernels for 9%

profile of v7, /device:TPU:0, one launch (start us, length us, event | category | flops | bytes accessed | tf_op | source)
XLA Modules:
  0.0 649.6 jit_solution(6297304493029650770)
XLA Ops:
  23.7 4.5 all_gather.31
  28.2 3.1 fusion.2
  32.3 3.8 multiply_reduce_fusion.5
  37.0 3.1 fusion.4
  45.8 89.6 %all-gather.14.cloned.1.call-done = bf16[1,8192,1024]{2,1,0:T(8,128)(2,1)} async-done(((bf16[1,256,1024]{2,1,0:T(8,128)(2,1)}), bf16[1,8192,1024]{2,1,0:T(8,128)(2,1)}) %all-gather.14.cloned.1.call-update) | async-done | bytes 16777232 | tf_op jit(solution)/shard_map/all_gather | solution.py:264
  135.4 9.5 %convolution_convert_fusion.1.v_ref = bf16[2048,1024]{1,0:T(8,128)(2,1)} fusion(bf16[2048,1024]{1,0:T(8,128)(2,1)} %bitcast.279, bf16[2,4,1024,1024]{3,2,1,0:T(8,128)(2,1)} %bitcast.348), kind=kOutput, calls=%fused_computation.52 | convolution fusion | flops 4297064448 | bytes 10485760 | tf_op jit(solution)/shard_map/dot_general | solution.py:31
  149.3 8.0 %convolution_convert_fusion.2.k_ref = bf16[2048,1024]{1,0:T(8,128)(2,1)} fusion(bf16[2048,1024]{1,0:T(8,128)(2,1)S(1)} %bitcast.280, bf16[2,4,1024,1024]{3,2,1,0:T(8,128)(2,1)} %bitcast.350), kind=kOutput, calls=%fused_computation.53 | convolution fusion | flops 4297064448 | bytes 10485760 | tf_op jit(solution)/shard_map/dot_general | solution.py:31
  157.4 16.4 %attend.2 = (bf16[512,1024]{1,0:T(8,128)(2,1)S(1)}, f32[2,8,2,256]{3,2,1,0:T(2,128)S(1)}) custom-call(s32[2,2]{1,0:T(2,128)S(1)} %get-tuple-element.200.first_ref, s32[2,2]{1,0:T(2,128)S(1)} %get-tuple-element.185.stop_ref, s32[2,1,256]{2,1,0:T(1,128)S(1)} %broadcast_in_dim.73.lo_ref, s32[2,1,256]{2,1,0:T(1,128)S(1)} %bitcast.263, ...), custom_call_target="tpu_custom_call" | custom-call | flops 8589934592 | bytes 18874368 | tf_op jit(solution)/shard_map/attend/pallas_call | solution.py:186
  176.8 3.3 fusion.76.v_ref
  180.1 3.3 fusion.77.k_ref
  183.4 3.3 fusion.78.q_ref
  186.8 4.1 attend.3
  203.3 22.3 %collective-permute-done.4 = bf16[512,1024]{1,0:T(8,128)(2,1)} collective-permute-done((bf16[512,1024]{1,0:T(8,128)(2,1)}, bf16[512,1024]{1,0:T(8,128)(2,1)}, u32[]{:S(2)}, u32[]{:S(2)}) %collective-permute-start.4) | collective-permute-done | bytes 1048608 | tf_op jit(solution)/shard_map/ppermute | solution.py:345
  225.7 11.8 %fusion.110 = f32[1024,2816]{1,0:T(8,128)} fusion(bf16[1024,2816]{1,0:T(8,128)(2,1)} %bitcast.364, bf16[512,1024]{1,0:T(8,128)(2,1)} %collective-permute-done.4, bf16[512,1024]{1,0:T(8,128)(2,1)} %multiply_convert_fusion.4), kind=kOutput, calls=%fused_computation.197 | convolution fusion | flops 5909774336 | bytes 19398656 | tf_op jit(solution)/shard_map/dot_general | solution.py:31
  237.5 3.2 maximum_select_fusion.1
  240.7 12.1 %multiply_convert_fusion = (bf16[1024,1408]{1,0:T(8,128)(2,1)S(1)}, bf16[1024,1408]{1,0:T(8,128)(2,1)S(1)}, bf16[1024,1408]{1,0:T(8,128)(2,1)}) fusion(f32[1024,2816]{1,0:T(8,128)} %fusion.110, bf16[1408,1024]{1,0:T(8,128)(2,1)S(1)} %bitcast.284, bf16[512,1024]{1,0:T(8,128)(2,1)S(1)} %bitcast.288, bf16[512,1024]{1,0:T(8,128)(2,1)S(1)} %bitcast.275), kind=kOutput, calls=%fused_computation.29 | convolution fusion | flops 2980052992 | bytes 25165824 | tf_op jit(solution)/shard_map/dot_general | solution.py:39
  252.9 4.2 fusion.81
  262.7 6.8 %convolution_convert_fusion = bf16[1024,1408]{1,0:T(8,128)(2,1)} fusion(s32[]{:T(128)S(6)} %select_n.319, bf16[1024,1408]{1,0:T(8,128)(2,1)S(1)} %get-tuple-element.130, bf16[1024,1408]{1,0:T(8,128)(2,1)S(1)} %get-tuple-element.129, bf16[512,1024]{1,0:T(8,128)(2,1)} %collective-permute-done.4, bf16[512,1024]{1,0:T(8,128)(2,1)} %multiply_convert_fusion.4), kind=kOutput, calls=%fused_computation.51 | convolution fusion | flops 2964193280 | bytes 10747908 | tf_op jit(solution)/shard_map/dot_general | solution.py:35
  273.2 6.2 fusion.175
  285.0 4.2 add_convert_fusion.3
  289.3 8.6 %add_convert_fusion = bf16[1024,1408]{1,0:T(8,128)(2,1)} fusion(bf16[1024,1408]{1,0:T(8,128)(2,1)} %collective-permute-done.8, s32[]{:T(128)S(6)} %select_n.322, bf16[1024,1408]{1,0:T(8,128)(2,1)} %copy-done.33, bf16[1024,1408]{1,0:T(8,128)(2,1)} %copy-done.32, bf16[512,1024]{1,0:T(8,128)(2,1)} %collective-permute-done.4, ...), kind=kOutput, calls=%fused_computation.28 | convolution fusion | flops 2967076864 | bytes 13631492 | tf_op jit(solution)/shard_map/dot_general | solution.py:35
  299.6 6.5 multiply_reduce_fusion
  308.1 4.4 fusion.75.dc_ref
  314.1 11.5 %attend_back.2 = (bf16[512,1024]{1,0:T(8,128)(2,1)S(1)}, bf16[512,1024]{1,0:T(8,128)(2,1)S(1)}, bf16[512,1024]{1,0:T(8,128)(2,1)S(1)}) custom-call(s32[2,2]{1,0:T(2,128)S(1)} %get-tuple-element.203.first_ref, s32[2,2]{1,0:T(2,128)S(1)} %get-tuple-element.202.stop_ref, s32[2,1,256]{2,1,0:T(1,128)S(1)} %broadcast_in_dim.83.lo_ref, ...), custom_call_target="tpu_custom_call" | custom-call | flops 5368709120 | bytes 6291456 | tf_op jit(solution)/shard_map/attend_back/pallas_call | solution.py:210
  337.4 3.5 fusion.32
  350.7 12.6 %collective-permute-done.10 = bf16[2,4,1,64,1408]{4,3,2,1,0:T(8,128)(2,1)S(1)} collective-permute-done((bf16[2,4,1,64,1408]{4,3,2,1,0:T(8,128)(2,1)S(1)}, bf16[2,4,1,64,1408]{4,3,2,1,0:T(8,128)(2,1)S(1)}, u32[]{:S(2)}, u32[]{:S(2)}) %collective-permute-start.10) | collective-permute-done | bytes 1441824 | tf_op jit(solution)/shard_map/ppermute | solution.py:360
  368.1 28.5 %attend_back.3 = (bf16[512,1024]{1,0:T(8,128)(2,1)S(1)}, bf16[2048,1024]{1,0:T(8,128)(2,1)}, bf16[2048,1024]{1,0:T(8,128)(2,1)}) custom-call(s32[2,2]{1,0:T(2,128)S(1)} %get-tuple-element.201.first_ref, s32[2,2]{1,0:T(2,128)S(1)} %get-tuple-element.184.stop_ref, s32[2,1,256]{2,1,0:T(1,128)S(1)} %broadcast_in_dim.73.lo_ref, s32[2,1,256]{2,1,0:T(1,128)S(1)} %bitcast.264, ...), custom_call_target="tpu_custom_call" | custom-call | flops 21474836480 | bytes 18874368 | tf_op jit(solution)/shard_map/attend_back/pallas_call | solution.py:210
  396.6 4.1 fusion.84
  408.1 6.4 collective-permute-done.13
  417.7 8.4 %fusion.48 = f32[2048,1024]{1,0:T(8,128)} fusion(bf16[2048,1024]{1,0:T(8,128)(2,1)S(1)} %copy-done.41, bf16[2,4,1024,1024]{3,2,1,0:T(8,128)(2,1)} %bitcast.361), kind=kOutput, calls=%fused_computation.132 | convolution fusion | flops 4294967296 | bytes 14680064 | tf_op jit(solution)/shard_map/dot_general | solution.py:39
  426.7 9.9 %convolution_add_fusion = f32[2048,1024]{1,0:T(8,128)} fusion(f32[2048,1024]{1,0:T(8,128)} %fusion.48, bf16[2048,1024]{1,0:T(8,128)(2,1)S(1)} %copy-done.40, bf16[2,4,1024,1024]{3,2,1,0:T(8,128)(2,1)} %bitcast.362), kind=kOutput, calls=%fused_computation.50 | convolution fusion | flops 4297064448 | bytes 23068672 | tf_op jit(solution)/shard_map/dot_general | solution.py:39
  436.6 4.2 fusion.46
  441.7 3.7 fusion.66
  445.4 3.8 fusion.63
  450.5 5.0 fusion.13
  455.5 3.7 fusion.12
  460.5 6.6 %fusion.11 = (f32[1024]{0:T(1024)S(1)}, f32[2048]{0:T(1024)S(1)}) fusion(f32[2048,1024]{1,0:T(8,128)} %convolution_add_fusion, f32[2048]{0:T(1024)S(1)} %bitcast.303, bf16[4,1024,1024]{2,1,0:T(8,128)(2,1)} %param.9, s32[]{:T(128)S(6)} %select_n.283, f32[1024]{0:T(1024)S(1)} %bitcast.307), kind=kLoop, calls=%fused_computation.19 | loop fusion | flops 14676992 | bytes 12607492 | tf_op jit(solution)/shard_map/reduce_sum | solution.py:238
  476.1 4.1 fusion.1
  480.3 17.1 %collective-permute-done.17 = bf16[2,1024,256]{2,1,0:T(8,128)(2,1)} collective-permute-done((bf16[2,1024,256]{2,1,0:T(8,128)(2,1)}, bf16[2,1024,256]{2,1,0:T(8,128)(2,1)}, u32[]{:S(2)}, u32[]{:S(2)}) %collective-permute-start.17) | collective-permute-done | bytes 1048608 | tf_op jit(solution)/shard_map/ppermute | solution.py:360
  503.3 11.1 %collective-permute-done.19 = bf16[2,1024,128]{2,1,0:T(8,128)(2,1)S(1)} collective-permute-done((bf16[2,1024,128]{2,1,0:T(8,128)(2,1)}, bf16[2,1024,128]{2,1,0:T(8,128)(2,1)S(1)}, u32[]{:S(2)}, u32[]{:S(2)}) %collective-permute-start.19) | collective-permute-done | bytes 524320 | tf_op jit(solution)/shard_map/ppermute | solution.py:360
  522.0 4.6 dynamic-slice_bitcast_fusion
  528.1 25.8 %reduce-scatter.11.cloned.1.call-done = bf16[352,512]{1,0:T(8,128)(2,1)} async-done(((bf16[1408,512]{1,0:T(8,128)(2,1)}), bf16[352,512]{1,0:T(8,128)(2,1)}) %reduce-scatter.11.cloned.1.call-update) | async-done | bytes 360464 | tf_op jit(solution)/shard_map/reduce_scatter | solution.py:373
  561.1 12.8 %collective-permute-done.21 = bf16[2,1024,512]{2,1,0:T(8,128)(2,1)} collective-permute-done((bf16[2,1024,512]{2,1,0:T(8,128)(2,1)}, bf16[2,1024,512]{2,1,0:T(8,128)(2,1)}, u32[]{:S(2)}, u32[]{:S(2)}) %collective-permute-start.21) | collective-permute-done | bytes 2097184 | tf_op jit(solution)/shard_map/ppermute | solution.py:453
  573.8 8.9 %reduce-scatter.7.cloned.1.call-done = bf16[4,256,128]{2,1,0:T(8,128)(2,1)} async-done(((bf16[4,1024,128]{2,1,0:T(8,128)(2,1)}), bf16[4,256,128]{2,1,0:T(8,128)(2,1)}) %reduce-scatter.7.cloned.1.call-update) | async-done | bytes 262160 | tf_op jit(solution)/shard_map/reduce_scatter | solution.py:373
  585.3 8.2 %all-gather.3 = bf16[1408,256]{1,0:T(8,128)(2,1)S(1)} all-gather(bf16[352,256]{1,0:T(8,128)(2,1)S(1)} %add_convert_fusion.10), channel_id=5, replica_groups=mesh['section'=2,'group'=4,'dp'=4] {'group'}, dimensions={0}, use_global_device_ids=true | all-gather | bytes 901120 | tf_op jit(solution)/shard_map/all_gather | solution.py:460
  605.6 13.1 %all-gather.4 = f32[4,4,1024]{2,1,0:T(4,128)S(1)} all-gather(f32[1,4,1024]{2,1,0:T(4,128)S(1)} %add_bitcast_fusion), channel_id=3, replica_groups=mesh['section'=2,'group'=4,'dp'=4] {'dp'}, dimensions={0}, use_global_device_ids=true | all-gather | bytes 81920 | tf_op jit(solution)/shard_map/all_gather | solution.py:489
  621.0 8.7 %maximum_convert_fusion = f32[128,5632]{1,0:T(8,128)} fusion(bf16[64,1408]{1,0:T(8,128)(2,1)S(1)} %get-tuple-element.151, bf16[64,1408]{1,0:T(8,128)(2,1)S(1)} %get-tuple-element.152, bf16[64,1408]{1,0:T(8,128)(2,1)S(1)} %get-tuple-element.153, bf16[64,1408]{1,0:T(8,128)(2,1)S(1)} %get-tuple-element.154, bf16[64,1408]{1,0:T(8,128)(2,1)S(1)} %get-tuple-element.155, ...), kind=kLoop, calls=%fused_computation.169 | loop fusion | flops 11534336 | bytes 4325376 | tf_op jit(solution)/shard_map/concatenate | solution.py:468
  629.7 4.6 maximum_select_fusion
  (352 shorter events, 160.4 us)
Async XLA Ops:
  7.2 15.7 %copy-start = (s32[4,256]{1,0:T(4,128)S(1)}, s32[4,256]{1,0:T(4,128)}, u32[]{:S(2)}) copy-start(s32[4,256]{1,0:T(4,128)} %param.11) | copy-start | bytes 12292
  7.2 128.2 %all-gather.14.cloned.1.call-start = ((), (), s32[]{:S(2)}) async-start(), calls=%async_computation.10 | async-start | bytes 17301504 | tf_op jit(solution)/shard_map/all_gather | solution.py:264
  9.3 14.5 %copy-start.56 = (f32[1,2,1024]{2,1,0:T(2,128)S(1)}, f32[1,2,1024]{2,1,0:T(2,128)}, u32[]{:S(2)}) copy-start(f32[1,2,1024]{2,1,0:T(2,128)} %param.14) | copy-start | bytes 24580
  9.3 194.0 %all-gather.10.cloned.1.call-start = ((), (), s32[]{:S(2)}) async-start(), calls=%async_computation.4 | async-start | bytes 6127616 | tf_op jit(solution)/shard_map/all_gather | solution.py:287
  11.9 28.8 %collective-permute-start = (bf16[88,1024]{1,0:T(8,128)(2,1)S(1)}, bf16[88,1024]{1,0:T(8,128)(2,1)}, u32[]{:S(2)}, u32[]{:S(2)}) collective-permute-start(bf16[88,1024]{1,0:T(8,128)(2,1)S(1)} %get-tuple-element.126), channel_id=1, source_target_pairs={{0,1},{1,2},{2,3},{3,0},{4,5},{5,6},{6,7},{7,4},{8,9},{9,10},{10,1... | collective-permute-start | bytes 540680 | tf_op jit(solution)/shard_map/ppermute | solution.py:293
  15.0 27.6 %collective-permute-start.1 = (bf16[88,1024]{1,0:T(8,128)(2,1)S(1)}, bf16[88,1024]{1,0:T(8,128)(2,1)}, u32[]{:S(2)}, u32[]{:S(2)}) collective-permute-start(bf16[88,1024]{1,0:T(8,128)(2,1)S(1)} %get-tuple-element.126), channel_id=1, source_target_pairs={{0,2},{1,3},{2,0},{3,1},{4,6},{5,7},{6,4},{7,5},{8,10},{9,11},{10,... | collective-permute-start | bytes 540680 | tf_op jit(solution)/shard_map/ppermute | solution.py:293
  17.6 26.6 %collective-permute-start.2 = (bf16[88,1024]{1,0:T(8,128)(2,1)S(1)}, bf16[88,1024]{1,0:T(8,128)(2,1)}, u32[]{:S(2)}, u32[]{:S(2)}) collective-permute-start(bf16[88,1024]{1,0:T(8,128)(2,1)S(1)} %get-tuple-element.126), channel_id=1, source_target_pairs={{0,3},{1,0},{2,1},{3,2},{4,7},{5,4},{6,5},{7,6},{8,11},{9,8},{10,9... | collective-permute-start | bytes 540680 | tf_op jit(solution)/shard_map/ppermute | solution.py:293
  20.2 11.1 %collective-permute-start.5 = (bf16[32,2816]{1,0:T(8,128)(2,1)S(1)}, bf16[32,2816]{1,0:T(8,128)(2,1)S(1)}, u32[]{:S(2)}, u32[]{:S(2)}) collective-permute-start(bf16[32,2816]{1,0:T(8,128)(2,1)S(1)} %pad_maximum_fusion.11), channel_id=1, source_target_pairs={{0,16},{16,0},{1,17},{17,1},{2,18},{18,2},{3,19},{19,3},{4,20},{20... | collective-permute-start | bytes 540680 | tf_op jit(solution)/shard_map/ppermute | solution.py:285
  23.7 16.3 %copy-start.50 = (f32[1,2,2,128]{3,1,2,0:T(2,128)}, f32[1,2,2,128]{3,1,2,0:T(2,128)S(1)}, u32[]{:S(2)}) copy-start(f32[1,2,2,128]{3,1,2,0:T(2,128)S(1)} %copy.28) | copy-start | bytes 6148
  32.2 468.6 %reduce-scatter.5.cloned.1.call-start = ((), (), s32[]{:S(2)}) async-start(), calls=%async_computation.5 | async-start | bytes 1310720 | tf_op jit(solution)/shard_map/reduce_scatter | solution.py:373
  40.3 133.5 %copy-start.20 = (f32[512,1024]{1,0:T(8,128)}, f32[512,1024]{1,0:T(8,128)S(1)}, u32[]{:S(2)}) copy-start(f32[512,1024]{1,0:T(8,128)S(1)} %bitcast_divide_fusion) | copy-start | bytes 6291460
  144.8 46.1 %collective-permute-start.3 = (bf16[4,88,1024]{2,1,0:T(8,128)(2,1)}, bf16[4,88,1024]{2,1,0:T(8,128)(2,1)S(1)}, u32[]{:S(2)}, u32[]{:S(2)}) collective-permute-start(bf16[4,88,1024]{2,1,0:T(8,128)(2,1)} %bitcast_dynamic-update-slice_fusion), channel_id=1, source_target_pairs={{0,8},{4,12},{8,0},{12,4},{1,9},{5,13},{9,1},{13,5},{2,10},{6,14},... | collective-permute-start | bytes 2162696 | tf_op jit(solution)/shard_map/ppermute | solution.py:276
  176.8 17.1 %copy-start.42 = (bf16[512,1024]{1,0:T(8,128)(2,1)}, bf16[512,1024]{1,0:T(8,128)(2,1)S(1)}, u32[]{:S(2)}) copy-start(bf16[512,1024]{1,0:T(8,128)(2,1)S(1)} %get-tuple-element.195) | copy-start | bytes 3145732
  190.9 121.7 %copy-start.2 = (bf16[512,1024]{1,0:T(8,128)(2,1)}, bf16[512,1024]{1,0:T(8,128)(2,1)S(1)}, u32[]{:S(2)}) copy-start(bf16[512,1024]{1,0:T(8,128)(2,1)S(1)} %get-tuple-element.64.c_ref) | copy-start | bytes 3145732
  199.5 26.2 %collective-permute-start.4 = (bf16[512,1024]{1,0:T(8,128)(2,1)}, bf16[512,1024]{1,0:T(8,128)(2,1)}, u32[]{:S(2)}, u32[]{:S(2)}) collective-permute-start(bf16[512,1024]{1,0:T(8,128)(2,1)} %multiply_convert_fusion.4), channel_id=1, source_target_pairs={{0,16},{16,0},{1,17},{17,1},{2,18},{18,2},{3,19},{19,3},{4,20},{20... | collective-permute-start | bytes 3145736 | tf_op jit(solution)/shard_map/ppermute | solution.py:345
  202.2 35.2 %collective-permute-start.6 = (bf16[2,4,88,1024]{3,2,0,1:T(8,128)(2,1)}, bf16[2,4,88,1024]{3,2,0,1:T(8,128)(2,1)}, u32[]{:S(2)}, u32[]{:S(2)}) collective-permute-start(bf16[2,4,88,1024]{3,2,0,1:T(8,128)(2,1)} %maximum_select_fusion.3), channel_id=1, source_target_pairs={{0,4},{4,0},{8,12},{12,8},{1,5},{5,1},{9,13},{13,9},{2,6},{6,2},{1... | collective-permute-start | bytes 4325384 | tf_op jit(solution)/shard_map/ppermute | solution.py:276
  237.4 15.4 %slice-start.8 = ((s8[5767168]{0:T(1024)(128)(4,1)}), s8[4194304]{0:T(1024)(128)(4,1)S(1)}, s32[]{:S(2)}) async-start(s8[5767168]{0:T(1024)(128)(4,1)} %bitcast.366), calls=%async_computation.20 | async-start | bytes 8388608
  269.5 19.7 %collective-permute-start.8 = (bf16[1024,1408]{1,0:T(8,128)(2,1)}, bf16[1024,1408]{1,0:T(8,128)(2,1)}, u32[]{:S(2)}, u32[]{:S(2)}) collective-permute-start(bf16[1024,1408]{1,0:T(8,128)(2,1)} %convolution_convert_fusion), channel_id=1, source_target_pairs={{0,4},{4,0},{8,12},{12,8},{1,5},{5,1},{9,13},{13,9},{2,6},{6,2},{1... | collective-permute-start | bytes 8650760 | tf_op jit(solution)/shard_map/ppermute | solution.py:383
  269.7 15.4 %collective-permute-start.9 = (bf16[1408,512]{1,0:T(8,128)(2,1)}, bf16[1408,512]{1,0:T(8,128)(2,1)}, u32[]{:S(2)}, u32[]{:S(2)}) collective-permute-start(bf16[1408,512]{1,0:T(8,128)(2,1)} %convolution_convert_fusion.3), channel_id=1, source_target_pairs={{0,4},{4,0},{8,12},{12,8},{1,5},{5,1},{9,13},{13,9},{2,6},{6,2},{1... | collective-permute-start | bytes 4325384 | tf_op jit(solution)/shard_map/ppermute | solution.py:383
  273.2 26.4 %collective-permute-start.7 = (bf16[512,1024]{1,0:T(8,128)(2,1)}, bf16[512,1024]{1,0:T(8,128)(2,1)}, u32[]{:S(2)}, u32[]{:S(2)}) collective-permute-start(bf16[512,1024]{1,0:T(8,128)(2,1)} %fusion.81), channel_id=1, source_target_pairs={{0,16},{16,0},{1,17},{17,1},{2,18},{18,2},{3,19},{19,3},{4,20},{20... | collective-permute-start | bytes 3145736 | tf_op jit(solution)/shard_map/ppermute | solution.py:390
  283.2 83.4 %collective-permute-start.12 = (bf16[1024,512]{1,0:T(8,128)(2,1)}, bf16[1024,512]{1,0:T(8,128)(2,1)}, u32[]{:S(2)}, u32[]{:S(2)}) collective-permute-start(bf16[1024,512]{1,0:T(8,128)(2,1)} %fusion.34), channel_id=1, source_target_pairs={{0,16},{16,0},{1,17},{17,1},{2,18},{18,2},{3,19},{19,3},{4,20},{20... | collective-permute-start | bytes 3145736 | tf_op jit(solution)/shard_map/ppermute | solution.py:398
  329.1 35.7 %collective-permute-start.11 = (bf16[4,1024,512]{2,1,0:T(8,128)(2,1)S(1)}, bf16[4,1024,512]{2,1,0:T(8,128)(2,1)S(1)}, u32[]{:S(2)}, u32[]{:S(2)}) collective-permute-start(bf16[4,1024,512]{2,1,0:T(8,128)(2,1)S(1)} %pad_maximum_fusion), channel_id=1, source_target_pairs={{0,4},{4,0},{8,12},{12,8},{1,5},{5,1},{9,13},{13,9},{2,6},{6,2},{1... | collective-permute-start | bytes 12582920 | tf_op jit(solution)/shard_map/ppermute | solution.py:383
  330.2 33.1 %collective-permute-start.10 = (bf16[2,4,1,64,1408]{4,3,2,1,0:T(8,128)(2,1)S(1)}, bf16[2,4,1,64,1408]{4,3,2,1,0:T(8,128)(2,1)S(1)}, u32[]{:S(2)}, u32[]{:S(2)}) collective-permute-start(bf16[2,4,1,64,1408]{4,3,2,1,0:T(8,128)(2,1)S(1)} %constant_dynamic-slice_fusion.10), channel_id=1, source_target_pairs={{0,8},{4,12},{8,0},{12,4},{1,9},{5,13},{9,1},{13,5},{2,10},{6,14},... | collective-permute-start | bytes 4325384 | tf_op jit(solution)/shard_map/ppermute | solution.py:360
  368.0 46.5 %collective-permute-start.13 = (bf16[4,1024,256]{2,1,0:T(8,128)(2,1)}, bf16[4,1024,256]{2,1,0:T(8,128)(2,1)}, u32[]{:S(2)}, u32[]{:S(2)}) collective-permute-start(bf16[4,1024,256]{2,1,0:T(8,128)(2,1)} %constant_dynamic-slice_fusion.9), channel_id=1, source_target_pairs={{0,16},{16,0},{1,17},{17,1},{2,18},{18,2},{3,19},{19,3},{4,20},{20... | collective-permute-start | bytes 6291464 | tf_op jit(solution)/shard_map/ppermute | solution.py:360
  368.1 28.5 %copy-start.11 = (bf16[2048,1024]{1,0:T(8,128)(2,1)S(1)}, bf16[2048,1024]{1,0:T(8,128)(2,1)}, u32[]{:S(2)}) copy-start(bf16[2048,1024]{1,0:T(8,128)(2,1)} %fusion.6) | copy-start | bytes 12582916
  417.1 32.1 %collective-permute-start.16 = (bf16[4,1024,128]{2,1,0:T(8,128)(2,1)S(1)}, bf16[4,1024,128]{2,1,0:T(8,128)(2,1)S(1)}, u32[]{:S(2)}, u32[]{:S(2)}) collective-permute-start(bf16[4,1024,128]{2,1,0:T(8,128)(2,1)S(1)} %constant_dynamic-slice_fusion.8), channel_id=1, source_target_pairs={{0,8},{4,12},{8,0},{12,4},{1,9},{5,13},{9,1},{13,5},{2,10},{6,14},... | collective-permute-start | bytes 3145736 | tf_op jit(solution)/shard_map/ppermute | solution.py:360
  426.2 24.3 %collective-permute-start.15 = (bf16[2,1024,512]{2,1,0:T(8,128)(2,1)}, bf16[2,1024,512]{2,1,0:T(8,128)(2,1)}, u32[]{:S(2)}, u32[]{:S(2)}) collective-permute-start(bf16[2,1024,512]{2,1,0:T(8,128)(2,1)} %pad_maximum_fusion.5), channel_id=1, source_target_pairs={{0,4},{4,0},{8,12},{12,8},{1,5},{5,1},{9,13},{13,9},{2,6},{6,2},{1... | collective-permute-start | bytes 6291464 | tf_op jit(solution)/shard_map/ppermute | solution.py:383
  426.2 29.3 %collective-permute-start.14 = (bf16[2,1024,512]{2,1,0:T(8,128)(2,1)}, bf16[2,1024,512]{2,1,0:T(8,128)(2,1)}, u32[]{:S(2)}, u32[]{:S(2)}) collective-permute-start(bf16[2,1024,512]{2,1,0:T(8,128)(2,1)} %pad_maximum_fusion.4), channel_id=1, source_target_pairs={{0,4},{4,0},{8,12},{12,8},{1,5},{5,1},{9,13},{13,9},{2,6},{6,2},{1... | collective-permute-start | bytes 6291464 | tf_op jit(solution)/shard_map/ppermute | solution.py:383
  459.3 60.2 %reduce-scatter.9.cloned.1.call-start = ((), (), s32[]{:S(2)}) async-start(), calls=%async_computation.8 | async-start | bytes 1802240 | tf_op jit(solution)/shard_map/reduce_scatter | solution.py:373
  459.9 94.0 %reduce-scatter.11.cloned.1.call-start = ((), (), s32[]{:S(2)}) async-start(), calls=%async_computation.9 | async-start | bytes 1802240 | tf_op jit(solution)/shard_map/reduce_scatter | solution.py:373
  460.5 122.3 %reduce-scatter.7.cloned.1.call-start = ((), (), s32[]{:S(2)}) async-start(), calls=%async_computation.6 | async-start | bytes 1310720 | tf_op jit(solution)/shard_map/reduce_scatter | solution.py:373
  460.5 14.0 %slice-start.6 = ((s8[8388608]{0:T(1024)(128)(4,1)}), s8[4194304]{0:T(1024)(128)(4,1)S(1)}, s32[]{:S(2)}) async-start(s8[8388608]{0:T(1024)(128)(4,1)} %bitcast.271), calls=%async_computation.18 | async-start | bytes 8388608
  469.8 29.4 %collective-permute-start.18 = (bf16[2,1024,256]{2,1,0:T(8,128)(2,1)}, bf16[2,1024,256]{2,1,0:T(8,128)(2,1)}, u32[]{:S(2)}, u32[]{:S(2)}) collective-permute-start(bf16[2,1024,256]{2,1,0:T(8,128)(2,1)} %constant_dynamic-slice_fusion.6), channel_id=1, source_target_pairs={{0,8},{4,12},{8,0},{12,4},{1,9},{5,13},{9,1},{13,5},{2,10},{6,14},... | collective-permute-start | bytes 3145736 | tf_op jit(solution)/shard_map/ppermute | solution.py:360
  472.3 25.1 %collective-permute-start.17 = (bf16[2,1024,256]{2,1,0:T(8,128)(2,1)}, bf16[2,1024,256]{2,1,0:T(8,128)(2,1)}, u32[]{:S(2)}, u32[]{:S(2)}) collective-permute-start(bf16[2,1024,256]{2,1,0:T(8,128)(2,1)} %constant_dynamic-slice_fusion.7), channel_id=1, source_target_pairs={{0,16},{16,0},{1,17},{17,1},{2,18},{18,2},{3,19},{19,3},{4,20},{20... | collective-permute-start | bytes 3145736 | tf_op jit(solution)/shard_map/ppermute | solution.py:360
  480.3 19.0 %copy-start.25 = (bf16[2,1024,512]{2,1,0:T(8,128)(2,1)S(1)}, bf16[2,1024,512]{2,1,0:T(8,128)(2,1)}, u32[]{:S(2)}) copy-start(bf16[2,1024,512]{2,1,0:T(8,128)(2,1)} %fusion.13) | copy-start | bytes 6291460
  501.6 12.8 %collective-permute-start.19 = (bf16[2,1024,128]{2,1,0:T(8,128)(2,1)}, bf16[2,1024,128]{2,1,0:T(8,128)(2,1)S(1)}, u32[]{:S(2)}, u32[]{:S(2)}) collective-permute-start(bf16[2,1024,128]{2,1,0:T(8,128)(2,1)} %constant_dynamic-slice_fusion.5), channel_id=1, source_target_pairs={{0,8},{4,12},{8,0},{12,4},{1,9},{5,13},{9,1},{13,5},{2,10},{6,14},... | collective-permute-start | bytes 1572872 | tf_op jit(solution)/shard_map/ppermute | solution.py:360
  503.0 12.6 %collective-permute-start.20 = (bf16[2,1024,128]{2,1,0:T(8,128)(2,1)}, bf16[2,1024,128]{2,1,0:T(8,128)(2,1)S(1)}, u32[]{:S(2)}, u32[]{:S(2)}) collective-permute-start(bf16[2,1024,128]{2,1,0:T(8,128)(2,1)} %constant_dynamic-slice_fusion.4), channel_id=1, source_target_pairs={{0,16},{16,0},{1,17},{17,1},{2,18},{18,2},{3,19},{19,3},{4,20},{20... | collective-permute-start | bytes 1572872 | tf_op jit(solution)/shard_map/ppermute | solution.py:360
  516.9 102.5 %all-gather.16.cloned.1.call-start = ((), (), s32[]{:S(2)}) async-start(), calls=%async_computation.11 | async-start | bytes 1802240 | tf_op jit(solution)/shard_map/all_gather | solution.py:460
  520.5 6.7 %collective-permute-start.26 = (bf16[64,1408]{1,0:T(8,128)(2,1)S(1)}, bf16[64,1408]{1,0:T(8,128)(2,1)S(1)}, u32[]{:S(2)}, u32[]{:S(2)}) collective-permute-start(bf16[64,1408]{1,0:T(8,128)(2,1)S(1)} %get-tuple-element.169), channel_id=1, source_target_pairs={{0,16},{16,0},{1,17},{17,1},{2,18},{18,2},{3,19},{19,3},{4,20},{20... | collective-permute-start | bytes 540680 | tf_op jit(solution)/shard_map/ppermute | solution.py:425
  526.6 29.8 %copy-start.15 = (f32[512,1024]{1,0:T(8,128)S(1)}, f32[512,1024]{1,0:T(8,128)}, u32[]{:S(2)}) copy-start(f32[512,1024]{1,0:T(8,128)} %copy-done.14) | copy-start | bytes 6291460
  526.6 47.2 %collective-permute-start.21 = (bf16[2,1024,512]{2,1,0:T(8,128)(2,1)}, bf16[2,1024,512]{2,1,0:T(8,128)(2,1)}, u32[]{:S(2)}, u32[]{:S(2)}) collective-permute-start(bf16[2,1024,512]{2,1,0:T(8,128)(2,1)} %get-tuple-element.133), channel_id=1, source_target_pairs={{0,16},{16,0},{1,17},{17,1},{2,18},{18,2},{3,19},{19,3},{4,20},{20... | collective-permute-start | bytes 6291464 | tf_op jit(solution)/shard_map/ppermute | solution.py:453
  528.0 106.3 %all-gather.12.cloned.1.call-start = ((), (), s32[]{:S(2)}) async-start(), calls=%async_computation.7 | async-start | bytes 2621440 | tf_op jit(solution)/shard_map/all_gather | solution.py:460
  554.8 6.2 collective-permute-start.27
  556.4 26.4 %copy-start.47 = (bf16[4,256,128]{2,1,0:T(8,128)(2,1)S(1)}, bf16[4,256,128]{2,1,0:T(8,128)(2,1)}, u32[]{:S(2)}) copy-start(bf16[4,256,128]{2,1,0:T(8,128)(2,1)} %reduce-scatter.5.cloned.1.call-done) | copy-start | bytes 786436
  583.7 9.8 %collective-permute-start.22 = (bf16[4,256,128]{2,1,0:T(8,128)(2,1)S(1)}, bf16[4,256,128]{2,1,0:T(8,128)(2,1)S(1)}, u32[]{:S(2)}, u32[]{:S(2)}) collective-permute-start(bf16[4,256,128]{2,1,0:T(8,128)(2,1)S(1)} %get-tuple-element.167), channel_id=1, source_target_pairs={{0,16},{16,0},{1,17},{17,1},{2,18},{18,2},{3,19},{19,3},{4,20},{20... | collective-permute-start | bytes 786440 | tf_op jit(solution)/shard_map/ppermute | solution.py:475
  594.6 3.4 collective-permute-start.23
  598.0 3.8 collective-permute-start.24
  601.8 3.8 collective-permute-start.25
  (58 other events, 292.1 us)
Sparse Core Ops, SparseCore 0:
  11.6 123.7 all-gather.13
  138.2 59.8 all-gather.9
  459.4 25.2 reduce-scatter.4
  487.5 31.8 reduce-scatter.8
  521.7 32.1 reduce-scatter.10
  556.7 26.0 reduce-scatter.6
  584.9 17.7 all-gather.15
  604.8 22.7 all-gather.11

commit v8 on v7

--- a/solution.py
+++ b/solution.py
@@ -408,37 +408,52 @@
     dq2, dk2, dv2 = attend_back(causal, q2, k2, v2, l2, c2, dc2, 8, CAUSAL_SPANS)
     two_pairs = [(normed_in, dq2), (normed_in, dk2), (normed_in, dv2), (c2, branch)]
     send_two = to_core(two_pairs)
-    dq2, dk2, dv2, send_two = together((dq2, dk2, dv2, send_two))
+    half_in = over_side(half_in.reshape(sections, line, 2, -1, units), 2)
+    sum_down = line_sum(half_down, 0)
+    dq2, dk2, dv2, send_two, half_in, sum_down = together((dq2, dk2, dv2, send_two, half_in, sum_down))
+    sum_in = line_sum(half_in.reshape(sections, -1, units), 1)
     grad_normed = nt(dq2, wq[1]) + nt(dk2, wk[1]) + nt(dv2, wv[1])
     grad_carried, gain_normed = norm_backward(carried_wide, first_scale, gains[1, 0], grad_normed)
     d_carried = (grad_residual + grad_carried).astype(BF)
     dc1 = nt(d_carried, wo[0]).astype(BF)
-    half_in = over_side(half_in.reshape(sections, line, 2, -1, units), 2)
     half_two = of_chip(two_pairs, send_two)
-    dc1, half_in, half_two, got = together((dc1, half_in, half_two, got))
+    dc1, half_two, got = together((dc1, half_two, got))
     got = got.astype(F32)
     latents = in_order(section, kept[:tokens] + got[tokens:], kept[tokens:] + got[:tokens])
     latents_out = latents.astype(BF).reshape(sections * rows, PATCHES, half)
-    sum_down = over_side(line_sum(half_down, 0), 1)
-    sum_in = line_sum(half_in.reshape(sections, -1, units), 1)
-    sum_in = jnp.stack([lax.dynamic_index_in_dim(sum_in, section, 0, False),
-                        lax.ppermute(lax.dynamic_index_in_dim(sum_in, 1 - section, 0, False), "section", swap)])
-    sum_in = jnp.where(section == 0, sum_in, sum_in[::-1])
-
     dq1, dk1, dv1 = attend_back(cross_back, q1, k1, v1, l1, c1, dc1, 4)
     half_two = over_section(half_two, 2)
     one_pairs = [(query_in, dq1), (key_in, dk1)], [(key_in, dv1), (c1, d_carried)]
     send_one = [to_core(pairs) for pairs in one_pairs]
-    dq1, dk1, dv1, send_one, half_two = together((dq1, dk1, dv1, send_one, half_two))
+    dq1, dk1, dv1, send_one, half_two, sum_in, sum_down = together(
+        (dq1, dk1, dv1, send_one, half_two, sum_in, sum_down)
+    )
     half_two = over_side(half_two, 2)
+    sum_in = jnp.stack([lax.dynamic_index_in_dim(sum_in, section, 0, False),
+                        lax.ppermute(lax.dynamic_index_in_dim(sum_in, 1 - section, 0, False), "section", swap)])
+    sum_in = jnp.where(section == 0, sum_in, sum_in[::-1])
+
+    def gathered(part):
+        return lax.all_gather(part, "group", axis=0, tiled=False)
+
+    def laid_out(parts, order):
+        return jnp.concatenate([parts[index] for index in order], axis=-1).astype(F32)
+
+    sum_in = gathered(sum_in)
+    half_one = [of_chip(pairs, sent) for pairs, sent in zip(one_pairs, send_one)]
+    dq1, dk1, dv1, half_one = together((dq1, dk1, dv1, half_one))
     grad_query_in = nt(dq1, wq[0])
     grad_key_in = nt(dk1, wk[0]) + nt(dv1, wv[0])
-    dq1, dk1, dv1, grad_query_in, grad_key_in = together((dq1, dk1, dv1, grad_query_in, grad_key_in))
-    one_pairs = [(query_in, dq1), (key_in, dk1)], [(key_in, dv1), (c1, d_carried)]
-    half_one = [of_chip(pairs, sent) for pairs, sent in zip(one_pairs, send_one)]
-    grad_query_in, grad_key_in, half_one, half_two = together((grad_query_in, grad_key_in, half_one, half_two))
+    half_one = over_section(half_one[0], 2), over_side(half_one[1], 2)
+    grad_query_in, grad_key_in, half_one, half_two, sum_in = together(
+        (grad_query_in, grad_key_in, half_one, half_two, sum_in)
+    )
     sum_two = line_sum(half_two, 1)
-    half_one = over_section(half_one[0], 2), over_side(half_one[1], 2)
+    half_one = jnp.concatenate([over_side(half_one[0], 2), over_section(half_one[1], 2)], axis=0)
+    half_one, sum_two, sum_down = together((half_one, sum_two, sum_down))
+    sum_down = over_side(sum_down, 1)
+    sum_one = line_sum(half_one, 1)
+
     grad_pooled, gain_query = norm_backward(pooled, query_scale, gains[0, 0], grad_query_in)
     grad_wide, gain_key = norm_backward(wide, key_scale, gains[0, 1], grad_key_in)
     per_patch = (grad_pooled + d_carried.astype(F32)) / count
@@ -446,29 +461,25 @@
         "rpb,rpd->rbd", member, per_patch.astype(BF).reshape(rows, PATCHES, D), preferred_element_type=F32
     )
     byte_grads = (grad_wide + spread_back.reshape(rows * ROW_BYTES, D)).astype(BF)
-    byte_grads, half_one, sum_two = together((byte_grads, half_one, sum_two))
     byte_grads = byte_grads.reshape(rows, ROW_BYTES, D)
     other = lax.dynamic_slice_in_dim(byte_grads, (1 - section) * half, half, 2)
     own = lax.dynamic_slice_in_dim(byte_grads, section * half, half, 2)
-    got = lax.ppermute(other, "section", swap)
-    half_one = jnp.concatenate([over_side(half_one[0], 2), over_section(half_one[1], 2)], axis=0)
-    sum_one = line_sum(half_one, 1)
-    sum_one, got = together((sum_one, got))
-    bytes_out = in_order(section, own, got).reshape(sections * rows, ROW_BYTES, half)
-
-    def of_group(part):
-        every = lax.all_gather(part, "group", axis=0, tiled=False)
-        return [every[index] for index in range(groups)]
-
-    def laid_out(parts, order):
-        return jnp.concatenate([parts[index] for index in order], axis=-1).astype(F32)
-
-    ffn_gdown = laid_out(of_group(sum_down), (0, 2, 1, 3))
-    every = of_group(sum_in)
+
+    gain_grads = jnp.stack([gain_query, gain_key, gain_normed, gain_mix])
+    gain_grads = gain_grads + lax.ppermute(gain_grads, "section", swap)
+    other, gain_grads = together((other, gain_grads))
+    got = [lax.ppermute(other[row], "section", swap) for row in range(rows)]
+    for pairs in (core_pairs, side_pairs):
+        gain_grads = gain_grads + lax.ppermute(gain_grads, "group", pairs)
+    gain_grads = jnp.sum(lax.all_gather(gain_grads, "dp", axis=0, tiled=False), axis=0)
+
+    ffn_gdown = laid_out(gathered(sum_down), (0, 2, 1, 3))
     ffn_gin = jnp.concatenate(
-        [laid_out([every[at][t] for at in (2 * y, 2 * y + 1) for t in range(sections)], range(4)) for y in (0, 1)],
+        [laid_out([sum_in[at, t] for at in (2 * y, 2 * y + 1) for t in range(sections)], range(4)) for y in (0, 1)],
         axis=0,
     )
+    sum_one, got[0], gain_grads, ffn_gdown = together((sum_one, got[0], gain_grads, ffn_gdown))
+    bytes_out = in_order(section, own, jnp.stack(got)).reshape(sections * rows, ROW_BYTES, half)
 
     kept = jnp.where(section == 0, sum_one, sum_two)
     sent = jnp.where(section == 0, sum_two, sum_one)
@@ -477,16 +488,12 @@
         section == 0, jnp.concatenate([kept, got], axis=2), jnp.concatenate([got, kept], axis=2)
     )
     width = eighths.shape[2] // 2
-    parts = [piece for every in of_group(eighths) for piece in (every[..., :width], every[..., width:])]
+    parts = [piece for every in gathered(eighths) for piece in (every[..., :width], every[..., width:])]
     section_first = laid_out(parts, (0, 4, 1, 5, 2, 6, 3, 7))
     side_first = laid_out([part[2:] for part in parts], (0, 1, 4, 5, 2, 3, 6, 7))
     last = jnp.where(section == 0, side_first, section_first[2:])
     grad_qkv = jnp.concatenate([section_first[:2], last[:1]], axis=0)[None]
 
-    gain_grads = jnp.stack([gain_query, gain_key, gain_normed, gain_mix])
-    for axis, pairs in (("group", core_pairs), ("group", side_pairs), ("section", swap)):
-        gain_grads = gain_grads + lax.ppermute(gain_grads, axis, pairs)
-    gain_grads = jnp.sum(lax.all_gather(gain_grads, "dp", axis=0, tiled=False), axis=0)
     gain_grads = lax.dynamic_slice_in_dim(gain_grads.reshape(2, 2, D), section, 1, 0)
     width = D // lax.axis_size("dp")
     gain_out = lax.dynamic_slice_in_dim(gain_grads, lax.axis_index("dp") * width, width, 2)

time: 655 us -> 651 us (level)
  waiting for transfers between devices: 219 us -> 193 us
  other arithmetic: 91 us -> 103 us
  local copies, waits for them, and re-layouts: 42.6 us -> 30.7 us
  matrix products: 170 us -> 180 us
  starting transfers between devices: 25 us -> 33.2 us
    reduce_scatter x4, waiting for transfers between devices: 37.2 us -> 3.82 us  [line_sum(): return lax.psum_scatter(values, 'dp', scatter_dimension=where, tiled=True)]
    dot_general x20, matrix products: 48.6 us -> 56.6 us  [tn(): lax.dot_general(left, right, (((0,), (0,)), ((), ())), preferred_element_...]
    ppermute x2, waiting for transfers between devices: 0.01 us -> 7.85 us  [shards(): got = lax.ppermute(sent, 'section', swap)]
    ppermute x8, starting transfers between devices: 4.76 us -> 11.7 us  [exchanged(): lax.ppermute(other, axis, pairs).astype(F32)]
    ppermute x4 -> x5, waiting for transfers between devices: 17 us -> 16.2 us  [the longest x2 14.6 us: shards(): got = [lax.ppermute(other[row], 'section', swap) for row in range(rows)]]
  transfers between devices with their start and end apart: 36 -> 37, of which waited for: 15 -> 14; matrix products, arithmetic and copies ran while one was open for 38% -> 37% of each run, Pallas kernels for 9% -> 10%
where the time goes in v8:
time: 651 us; the launch traced here: 646 us
  waiting for transfers between devices  193 us (30%)
  matrix products  180 us (28%)
  other arithmetic  103 us (16%)
  Pallas kernels  64.6 us (10%)
  starting transfers between devices  33.2 us (5%)
  local copies, waits for them, and re-layouts  30.7 us (5%)
  blocking collectives  26.9 us (4%)
  between operations  15.7 us (2%)
    all_gather x1, waiting for transfers between devices, shards(): lax.all_gather(matrix, ('section', 'group', 'dp'), axis=0, tiled=True)  92.4 us
    dot_general x11, matrix products, nt(): lax.dot_general(left, right, (((1,), (1,)), ((), ())), preferred_element_...  60.2 us
    dot_general x20, matrix products, tn(): lax.dot_general(left, right, (((0,), (0,)), ((), ())), preferred_element_...  56.6 us
    dot_general x10, matrix products, nn(): return jnp.dot(left, right, preferred_element_type=F32)  54.7 us
    ppermute x8, waiting for transfers between devices, exchanged(): lax.ppermute(other, axis, pairs).astype(F32)  46.8 us
    pallas_call x2, Pallas kernels, attend_back(): pl.pallas_call(functools.partial(attend_back_kernel, chunk, spans), grid_...  42.9 us
    pallas_call x2, Pallas kernels, attend(): pl.pallas_call(functools.partial(attend_kernel, chunk, spans), grid_spec=...  21.6 us
    ppermute x1, waiting for transfers between devices, shards(): lax.ppermute(mix_in, 'section', swap)  19.9 us
  transfers between devices with their start and end apart: 37, of which 14 were waited for; matrix products, arithmetic and copies ran while one was open for 37% of the time, Pallas kernels for 10%

profile of v8, /device:TPU:0, one launch (start us, length us, event | category | flops | bytes accessed | tf_op | source)
XLA Modules:
  0.0 646.2 jit_solution(16935221122206389038)
XLA Ops:
  22.2 4.4 all_gather.31
  30.6 3.8 multiply_reduce_fusion.5
  41.2 92.4 %all-gather.14.cloned.1.call-done = bf16[1,8192,1024]{2,1,0:T(8,128)(2,1)} async-done(((bf16[1,256,1024]{2,1,0:T(8,128)(2,1)}), bf16[1,8192,1024]{2,1,0:T(8,128)(2,1)}) %all-gather.14.cloned.1.call-update) | async-done | bytes 16777232 | tf_op jit(solution)/shard_map/all_gather | solution.py:264
  133.6 9.4 %convolution_convert_fusion.1.v_ref = bf16[2048,1024]{1,0:T(8,128)(2,1)} fusion(bf16[2048,1024]{1,0:T(8,128)(2,1)} %bitcast.280, bf16[2,4,1024,1024]{3,2,1,0:T(8,128)(2,1)} %bitcast.347), kind=kOutput, calls=%fused_computation.52 | convolution fusion | flops 4297064448 | bytes 10485760 | tf_op jit(solution)/shard_map/dot_general | solution.py:31
  147.6 8.0 %convolution_convert_fusion.2.k_ref = bf16[2048,1024]{1,0:T(8,128)(2,1)} fusion(bf16[2048,1024]{1,0:T(8,128)(2,1)S(1)} %bitcast.281, bf16[2,4,1024,1024]{3,2,1,0:T(8,128)(2,1)} %bitcast.349), kind=kOutput, calls=%fused_computation.53 | convolution fusion | flops 4297064448 | bytes 10485760 | tf_op jit(solution)/shard_map/dot_general | solution.py:31
  155.6 17.5 %attend.2 = (bf16[512,1024]{1,0:T(8,128)(2,1)S(1)}, f32[2,8,2,256]{3,2,1,0:T(2,128)S(1)}) custom-call(s32[2,2]{1,0:T(2,128)S(1)} %get-tuple-element.216.first_ref, s32[2,2]{1,0:T(2,128)S(1)} %get-tuple-element.201.stop_ref, s32[2,1,256]{2,1,0:T(1,128)S(1)} %broadcast_in_dim.73.lo_ref, s32[2,1,256]{2,1,0:T(1,128)S(1)} %bitcast.270, ...), custom_call_target="tpu_custom_call" | custom-call | flops 8589934592 | bytes 18874368 | tf_op jit(solution)/shard_map/attend/pallas_call | solution.py:186
  173.1 3.4 fusion.23
  176.6 3.3 fusion.78.q_ref
  179.9 3.3 fusion.77.k_ref
  183.2 3.3 fusion.76.v_ref
  186.6 4.1 attend.3
  199.5 19.9 %collective-permute-done.4 = bf16[512,1024]{1,0:T(8,128)(2,1)} collective-permute-done((bf16[512,1024]{1,0:T(8,128)(2,1)}, bf16[512,1024]{1,0:T(8,128)(2,1)}, u32[]{:S(2)}, u32[]{:S(2)}) %collective-permute-start.4) | collective-permute-done | bytes 1048608 | tf_op jit(solution)/shard_map/ppermute | solution.py:345
  219.4 11.8 %fusion.110 = f32[1024,2816]{1,0:T(8,128)} fusion(bf16[1024,2816]{1,0:T(8,128)(2,1)} %bitcast.363, bf16[512,1024]{1,0:T(8,128)(2,1)} %collective-permute-done.4, bf16[512,1024]{1,0:T(8,128)(2,1)} %multiply_convert_fusion.4), kind=kOutput, calls=%fused_computation.200 | convolution fusion | flops 5909774336 | bytes 19398656 | tf_op jit(solution)/shard_map/dot_general | solution.py:31
  231.2 3.3 maximum_select_fusion.1
  234.5 12.1 %multiply_convert_fusion = (bf16[1024,1408]{1,0:T(8,128)(2,1)S(1)}, bf16[1024,1408]{1,0:T(8,128)(2,1)S(1)}, bf16[1024,1408]{1,0:T(8,128)(2,1)}) fusion(f32[1024,2816]{1,0:T(8,128)} %fusion.110, bf16[1408,1024]{1,0:T(8,128)(2,1)S(1)} %bitcast.283, bf16[512,1024]{1,0:T(8,128)(2,1)S(1)} %bitcast.290, bf16[512,1024]{1,0:T(8,128)(2,1)S(1)} %bitcast.276), kind=kOutput, calls=%fused_computation.29 | convolution fusion | flops 2980052992 | bytes 25165824 | tf_op jit(solution)/shard_map/dot_general | solution.py:39
  248.6 4.1 fusion.81
  255.5 7.1 %convolution_convert_fusion = bf16[1024,1408]{1,0:T(8,128)(2,1)} fusion(s32[]{:T(128)S(6)} %select_n.319, bf16[1024,1408]{1,0:T(8,128)(2,1)S(1)} %get-tuple-element.144, bf16[1024,1408]{1,0:T(8,128)(2,1)S(1)} %get-tuple-element.143, bf16[512,1024]{1,0:T(8,128)(2,1)} %collective-permute-done.4, bf16[512,1024]{1,0:T(8,128)(2,1)} %multiply_convert_fusion.4), kind=kOutput, calls=%fused_computation.51 | convolution fusion | flops 2964193280 | bytes 10747908 | tf_op jit(solution)/shard_map/dot_general | solution.py:35
  264.9 6.1 fusion.175
  275.9 4.2 add_convert_fusion.3
  280.1 7.1 %add_convert_fusion = bf16[1024,1408]{1,0:T(8,128)(2,1)S(1)} fusion(bf16[1024,1408]{1,0:T(8,128)(2,1)} %collective-permute-done.8, s32[]{:T(128)S(6)} %select_n.322, bf16[1024,1408]{1,0:T(8,128)(2,1)} %copy-done.35, bf16[1024,1408]{1,0:T(8,128)(2,1)} %copy-done.34, bf16[512,1024]{1,0:T(8,128)(2,1)} %collective-permute-done.4, ...), kind=kOutput, calls=%fused_computation.28 | convolution fusion | flops 2967076864 | bytes 13631492 | tf_op jit(solution)/shard_map/dot_general | solution.py:35
  289.8 7.7 %multiply_reduce_fusion = (f32[1024]{0:T(1024)S(1)}, f32[512]{0:T(512)S(1)}, f32[512,1024]{1,0:T(8,128)}) fusion(f32[512,1024]{1,0:T(8,128)S(1)} %get-tuple-element.213, f32[512]{0:T(512)S(1)} %get-tuple-element.197, bf16[512,1024]{1,0:T(8,128)(2,1)} %collective-permute-done.7, f32[1024]{0:T(1024)S(1)} %bitcast.318, bf16[512,2816]{1,0:T(8,128)(2,1)S(1)} %copy-done.33, ...), kind=kOutput, calls=%fused_computation.102 | convolution fusion | flops 2956982784 | bytes 13905920 | tf_op jit(solution)/shard_map/dot_general | solution.py:39
  301.6 4.0 fusion.168
  305.6 4.3 fusion.75.dc_ref
  309.9 11.7 %attend_back.2 = (bf16[512,1024]{1,0:T(8,128)(2,1)S(1)}, bf16[512,1024]{1,0:T(8,128)(2,1)S(1)}, bf16[512,1024]{1,0:T(8,128)(2,1)S(1)}) custom-call(s32[2,2]{1,0:T(2,128)S(1)} %get-tuple-element.219.first_ref, s32[2,2]{1,0:T(2,128)S(1)} %get-tuple-element.218.stop_ref, s32[2,1,256]{2,1,0:T(1,128)S(1)} %broadcast_in_dim.83.lo_ref, ...), custom_call_target="tpu_custom_call" | custom-call | flops 5368709120 | bytes 6291456 | tf_op jit(solution)/shard_map/attend_back/pallas_call | solution.py:210
  328.2 4.6 collective-permute-done.10
  335.6 4.3 fusion.6
  356.3 3.6 fusion.32
  374.3 31.3 %attend_back.3 = (bf16[512,1024]{1,0:T(8,128)(2,1)S(1)}, bf16[2048,1024]{1,0:T(8,128)(2,1)}, bf16[2048,1024]{1,0:T(8,128)(2,1)}) custom-call(s32[2,2]{1,0:T(2,128)S(1)} %get-tuple-element.217.first_ref, s32[2,2]{1,0:T(2,128)S(1)} %get-tuple-element.200.stop_ref, s32[2,1,256]{2,1,0:T(1,128)S(1)} %broadcast_in_dim.73.lo_ref, s32[2,1,256]{2,1,0:T(1,128)S(1)} %bitcast.271, ...), custom_call_target="tpu_custom_call" | custom-call | flops 21474836480 | bytes 18874368 | tf_op jit(solution)/shard_map/attend_back/pallas_call | solution.py:210
  406.5 4.0 fusion.87
  418.7 3.7 fusion.63
  422.5 3.5 add_convert_fusion.1
  426.5 6.6 %fusion.66 = f32[1,1024,512]{2,1,0:T(8,128)} fusion(bf16[2048,1024]{1,0:T(8,128)(2,1)} %fusion.6, bf16[2048,1024]{1,0:T(8,128)(2,1)} %get-tuple-element.106, s32[]{:T(128)S(6)} %select_n.323), kind=kOutput, calls=%fused_computation.153 | convolution fusion | flops 2147483648 | bytes 8388612 | tf_op jit(solution)/shard_map/dot_general | solution.py:35
  443.3 24.2 %collective-permute-done.18 = bf16[4,1024,128]{2,1,0:T(8,128)(2,1)} collective-permute-done((bf16[4,1024,128]{2,1,0:T(8,128)(2,1)}, bf16[4,1024,128]{2,1,0:T(8,128)(2,1)}, u32[]{:S(2)}, u32[]{:S(2)}) %collective-permute-start.18) | collective-permute-done | bytes 1048608 | tf_op jit(solution)/shard_map/ppermute | solution.py:360
  470.2 3.2 fusion.12
  476.3 6.3 fusion.48
  485.9 8.9 %convolution_add_fusion = f32[2048,1024]{1,0:T(8,128)} fusion(f32[2048,1024]{1,0:T(8,128)S(1)} %fusion.48, bf16[2048,1024]{1,0:T(8,128)(2,1)S(1)} %copy-done.51, bf16[2,4,1024,1024]{3,2,1,0:T(8,128)(2,1)} %bitcast.361), kind=kOutput, calls=%fused_computation.50 | convolution fusion | flops 4297064448 | bytes 23068672 | tf_op jit(solution)/shard_map/dot_general | solution.py:39
  494.8 4.2 fusion.46
  499.0 7.8 %collective-permute-done.16 = bf16[2,1024,256]{2,1,0:T(8,128)(2,1)S(1)} collective-permute-done((bf16[2,1024,256]{2,1,0:T(8,128)(2,1)S(1)}, bf16[2,1024,256]{2,1,0:T(8,128)(2,1)S(1)}, u32[]{:S(2)}, u32[]{:S(2)}) %collective-permute-start.16) | collective-permute-done | bytes 1048608 | tf_op jit(solution)/shard_map/ppermute | solution.py:360
  511.7 6.0 fusion.11
  523.6 4.6 fusion.59
  533.4 7.6 %collective-permute-done.21 = bf16[2,1024,128]{2,1,0:T(8,128)(2,1)S(1)} collective-permute-done((bf16[2,1024,128]{2,1,0:T(8,128)(2,1)S(1)}, bf16[2,1024,128]{2,1,0:T(8,128)(2,1)S(1)}, u32[]{:S(2)}, u32[]{:S(2)}) %collective-permute-start.21) | collective-permute-done | bytes 524320 | tf_op jit(solution)/shard_map/ppermute | solution.py:360
  542.2 3.8 reduce-scatter.9.cloned.1.call-done
  546.1 8.4 %fusion.1 = bf16[2048,1024]{1,0:T(8,128)(2,1)S(1)} fusion(f32[2,1024,1024]{2,1,0:T(8,128)} %fusion.59, f32[2048,1024]{1,0:T(8,128)} %convolution_add_fusion, f32[2048]{0:T(1024)S(1)} %broadcast_multiply_fusion, f32[2048]{0:T(1024)S(1)} %copy-done.64, f32[1024]{0:T(1024)S(1)} %bitcast.311, f32[2048]{0:T(1024)S(1)} %bitcast.307, ...), kind=kLoop, calls=%fused_computation.3 | loop fusion | flops 16777216 | bytes 25194500 | tf_op jit(solution)/shard_map/convert_element_type | solution.py:463
  562.8 13.7 %all-gather.4 = f32[4,4,1024]{2,1,0:T(4,128)S(1)} all-gather(f32[1,4,1024]{2,1,0:T(4,128)S(1)} %add_bitcast_fusion), channel_id=4, replica_groups=mesh['section'=2,'group'=4,'dp'=4] {'dp'}, dimensions={0}, use_global_device_ids=true | all-gather | bytes 81920 | tf_op jit(solution)/shard_map/all_gather | solution.py:474
  576.6 8.8 %all-gather.3 = bf16[1408,256]{1,0:T(8,128)(2,1)S(1)} all-gather(bf16[352,256]{1,0:T(8,128)(2,1)S(1)} %add_convert_fusion.10), channel_id=5, replica_groups=mesh['section'=2,'group'=4,'dp'=4] {'group'}, dimensions={0}, use_global_device_ids=true | all-gather | bytes 901120 | tf_op jit(solution)/shard_map/all_gather | solution.py:437
  588.5 7.8 %collective-permute-done.28 = bf16[4,256,128]{2,1,0:T(8,128)(2,1)S(1)} collective-permute-done((bf16[4,256,128]{2,1,0:T(8,128)(2,1)S(1)}, bf16[4,256,128]{2,1,0:T(8,128)(2,1)S(1)}, u32[]{:S(2)}, u32[]{:S(2)}) %collective-permute-start.28) | collective-permute-done | bytes 262176 | tf_op jit(solution)/shard_map/ppermute | solution.py:486
  603.0 8.4 %maximum_convert_fusion = f32[128,5632]{1,0:T(8,128)} fusion(bf16[64,1408]{1,0:T(8,128)(2,1)S(1)} %get-tuple-element.167, bf16[64,1408]{1,0:T(8,128)(2,1)S(1)} %get-tuple-element.168, bf16[64,1408]{1,0:T(8,128)(2,1)S(1)} %get-tuple-element.169, bf16[64,1408]{1,0:T(8,128)(2,1)S(1)} %get-tuple-element.170, bf16[64,1408]{1,0:T(8,128)(2,1)S(1)} %get-tuple-element.171, ...), kind=kLoop, calls=%fused_computation.170 | loop fusion | flops 11534336 | bytes 4325376 | tf_op jit(solution)/shard_map/concatenate | solution.py:477
  612.1 14.6 %collective-permute-done.27 = bf16[1024,512]{1,0:T(8,128)(2,1)S(1)} collective-permute-done((bf16[1024,512]{1,0:T(8,128)(2,1)S(1)}, bf16[1024,512]{1,0:T(8,128)(2,1)S(1)}, u32[]{:S(2)}, u32[]{:S(2)}) %collective-permute-start.27) | collective-permute-done | bytes 1048608 | tf_op jit(solution)/shard_map/ppermute | solution.py:471
  (373 shorter events, 174.2 us)
Async XLA Ops:
  7.2 14.3 %copy-start = (s32[4,256]{1,0:T(4,128)S(1)}, s32[4,256]{1,0:T(4,128)}, u32[]{:S(2)}) copy-start(s32[4,256]{1,0:T(4,128)} %param.11) | copy-start | bytes 12292
  7.2 126.4 %all-gather.14.cloned.1.call-start = ((), (), s32[]{:S(2)}) async-start(), calls=%async_computation.10 | async-start | bytes 17301504 | tf_op jit(solution)/shard_map/all_gather | solution.py:264
  9.3 190.2 %all-gather.10.cloned.1.call-start = ((), (), s32[]{:S(2)}) async-start(), calls=%async_computation.4 | async-start | bytes 6127616 | tf_op jit(solution)/shard_map/all_gather | solution.py:287
  10.4 29.8 %collective-permute-start = (bf16[88,1024]{1,0:T(8,128)(2,1)S(1)}, bf16[88,1024]{1,0:T(8,128)(2,1)}, u32[]{:S(2)}, u32[]{:S(2)}) collective-permute-start(bf16[88,1024]{1,0:T(8,128)(2,1)S(1)} %get-tuple-element.140), channel_id=1, source_target_pairs={{0,1},{1,2},{2,3},{3,0},{4,5},{5,6},{6,7},{7,4},{8,9},{9,10},{10,1... | collective-permute-start | bytes 540680 | tf_op jit(solution)/shard_map/ppermute | solution.py:293
  13.5 27.7 %collective-permute-start.1 = (bf16[88,1024]{1,0:T(8,128)(2,1)S(1)}, bf16[88,1024]{1,0:T(8,128)(2,1)S(1)}, u32[]{:S(2)}, u32[]{:S(2)}) collective-permute-start(bf16[88,1024]{1,0:T(8,128)(2,1)S(1)} %get-tuple-element.140), channel_id=1, source_target_pairs={{0,2},{1,3},{2,0},{3,1},{4,6},{5,7},{6,4},{7,5},{8,10},{9,11},{10,... | collective-permute-start | bytes 540680 | tf_op jit(solution)/shard_map/ppermute | solution.py:293
  16.1 25.1 %collective-permute-start.2 = (bf16[88,1024]{1,0:T(8,128)(2,1)S(1)}, bf16[88,1024]{1,0:T(8,128)(2,1)S(1)}, u32[]{:S(2)}, u32[]{:S(2)}) collective-permute-start(bf16[88,1024]{1,0:T(8,128)(2,1)S(1)} %get-tuple-element.140), channel_id=1, source_target_pairs={{0,3},{1,0},{2,1},{3,2},{4,7},{5,4},{6,5},{7,6},{8,11},{9,8},{10,9... | collective-permute-start | bytes 540680 | tf_op jit(solution)/shard_map/ppermute | solution.py:293
  18.7 10.9 %collective-permute-start.5 = (bf16[32,2816]{1,0:T(8,128)(2,1)S(1)}, bf16[32,2816]{1,0:T(8,128)(2,1)S(1)}, u32[]{:S(2)}, u32[]{:S(2)}) collective-permute-start(bf16[32,2816]{1,0:T(8,128)(2,1)S(1)} %pad_maximum_fusion.11), channel_id=1, source_target_pairs={{0,16},{16,0},{1,17},{17,1},{2,18},{18,2},{3,19},{19,3},{4,20},{20... | collective-permute-start | bytes 540680 | tf_op jit(solution)/shard_map/ppermute | solution.py:285
  22.1 16.3 %copy-start.65 = (f32[1,2,2,128]{3,1,2,0:T(2,128)}, f32[1,2,2,128]{3,1,2,0:T(2,128)S(1)}, u32[]{:S(2)}) copy-start(f32[1,2,2,128]{3,1,2,0:T(2,128)S(1)} %copy.28) | copy-start | bytes 6148
  30.5 305.2 %reduce-scatter.5.cloned.1.call-start = ((), (), s32[]{:S(2)}) async-start(), calls=%async_computation.5 | async-start | bytes 1802240 | tf_op jit(solution)/shard_map/reduce_scatter | solution.py:373
  38.6 134.5 %copy-start.22 = (f32[512,1024]{1,0:T(8,128)}, f32[512,1024]{1,0:T(8,128)S(1)}, u32[]{:S(2)}) copy-start(f32[512,1024]{1,0:T(8,128)S(1)} %bitcast_divide_fusion) | copy-start | bytes 6291460
  143.1 47.7 %collective-permute-start.3 = (bf16[4,88,1024]{2,1,0:T(8,128)(2,1)S(1)}, bf16[4,88,1024]{2,1,0:T(8,128)(2,1)S(1)}, u32[]{:S(2)}, u32[]{:S(2)}) collective-permute-start(bf16[4,88,1024]{2,1,0:T(8,128)(2,1)S(1)} %bitcast_dynamic-update-slice_fusion), channel_id=1, source_target_pairs={{0,8},{4,12},{8,0},{12,4},{1,9},{5,13},{9,1},{13,5},{2,10},{6,14},... | collective-permute-start | bytes 2162696 | tf_op jit(solution)/shard_map/ppermute | solution.py:276
  176.5 15.6 %copy-start.54 = (bf16[512,1024]{1,0:T(8,128)(2,1)}, bf16[512,1024]{1,0:T(8,128)(2,1)S(1)}, u32[]{:S(2)}) copy-start(bf16[512,1024]{1,0:T(8,128)(2,1)S(1)} %get-tuple-element.211) | copy-start | bytes 3145732
  196.4 23.0 %collective-permute-start.4 = (bf16[512,1024]{1,0:T(8,128)(2,1)}, bf16[512,1024]{1,0:T(8,128)(2,1)}, u32[]{:S(2)}, u32[]{:S(2)}) collective-permute-start(bf16[512,1024]{1,0:T(8,128)(2,1)} %multiply_convert_fusion.4), channel_id=1, source_target_pairs={{0,16},{16,0},{1,17},{17,1},{2,18},{18,2},{3,19},{19,3},{4,20},{20... | collective-permute-start | bytes 3145736 | tf_op jit(solution)/shard_map/ppermute | solution.py:345
  199.5 31.7 %collective-permute-start.6 = (bf16[2,4,88,1024]{3,2,0,1:T(8,128)(2,1)}, bf16[2,4,88,1024]{3,2,0,1:T(8,128)(2,1)}, u32[]{:S(2)}, u32[]{:S(2)}) collective-permute-start(bf16[2,4,88,1024]{3,2,0,1:T(8,128)(2,1)} %maximum_select_fusion.3), channel_id=1, source_target_pairs={{0,4},{4,0},{8,12},{12,8},{1,5},{5,1},{9,13},{13,9},{2,6},{6,2},{1... | collective-permute-start | bytes 4325384 | tf_op jit(solution)/shard_map/ppermute | solution.py:276
  231.2 17.3 %slice-start.2 = ((s8[5767168]{0:T(1024)(128)(4,1)}), s8[4194304]{0:T(1024)(128)(4,1)S(1)}, s32[]{:S(2)}) async-start(s8[5767168]{0:T(1024)(128)(4,1)} %bitcast.365), calls=%async_computation.14 | async-start | bytes 8388608
  234.5 14.1 %slice-start.3 = ((s8[5767168]{0:T(1024)(128)(4,1)}), s8[1572864]{0:T(1024)(128)(4,1)S(1)}, s32[]{:S(2)}) async-start(s8[5767168]{0:T(1024)(128)(4,1)} %bitcast.365), calls=%async_computation.15 | async-start | bytes 3145728
  262.6 17.5 %collective-permute-start.8 = (bf16[1024,1408]{1,0:T(8,128)(2,1)}, bf16[1024,1408]{1,0:T(8,128)(2,1)}, u32[]{:S(2)}, u32[]{:S(2)}) collective-permute-start(bf16[1024,1408]{1,0:T(8,128)(2,1)} %convolution_convert_fusion), channel_id=1, source_target_pairs={{0,4},{4,0},{8,12},{12,8},{1,5},{5,1},{9,13},{13,9},{2,6},{6,2},{1... | collective-permute-start | bytes 8650760 | tf_op jit(solution)/shard_map/ppermute | solution.py:383
  263.3 11.2 %collective-permute-start.9 = (bf16[1408,512]{1,0:T(8,128)(2,1)}, bf16[1408,512]{1,0:T(8,128)(2,1)}, u32[]{:S(2)}, u32[]{:S(2)}) collective-permute-start(bf16[1408,512]{1,0:T(8,128)(2,1)} %convolution_convert_fusion.3), channel_id=1, source_target_pairs={{0,4},{4,0},{8,12},{12,8},{1,5},{5,1},{9,13},{13,9},{2,6},{6,2},{1... | collective-permute-start | bytes 4325384 | tf_op jit(solution)/shard_map/ppermute | solution.py:383
  264.4 25.4 %collective-permute-start.7 = (bf16[512,1024]{1,0:T(8,128)(2,1)}, bf16[512,1024]{1,0:T(8,128)(2,1)}, u32[]{:S(2)}, u32[]{:S(2)}) collective-permute-start(bf16[512,1024]{1,0:T(8,128)(2,1)} %fusion.81), channel_id=1, source_target_pairs={{0,16},{16,0},{1,17},{17,1},{2,18},{18,2},{3,19},{19,3},{4,20},{20... | collective-permute-start | bytes 3145736 | tf_op jit(solution)/shard_map/ppermute | solution.py:390
  298.7 34.1 %collective-permute-start.10 = (bf16[2,4,1,64,1408]{4,3,2,1,0:T(8,128)(2,1)}, bf16[2,4,1,64,1408]{4,3,2,1,0:T(8,128)(2,1)}, u32[]{:S(2)}, u32[]{:S(2)}) collective-permute-start(bf16[2,4,1,64,1408]{4,3,2,1,0:T(8,128)(2,1)} %constant_dynamic-slice_fusion.10), channel_id=1, source_target_pairs={{0,8},{4,12},{8,0},{12,4},{1,9},{5,13},{9,1},{13,5},{2,10},{6,14},... | collective-permute-start | bytes 4325384 | tf_op jit(solution)/shard_map/ppermute | solution.py:360
  301.6 124.4 %reduce-scatter.7.cloned.1.call-start = ((), (), s32[]{:S(2)}) async-start(), calls=%async_computation.6 | async-start | bytes 1802240 | tf_op jit(solution)/shard_map/reduce_scatter | solution.py:373
  305.6 16.0 %copy-start.47 = (bf16[512,1024]{1,0:T(8,128)(2,1)}, bf16[512,1024]{1,0:T(8,128)(2,1)S(1)}, u32[]{:S(2)}) copy-start(bf16[512,1024]{1,0:T(8,128)(2,1)S(1)} %get-tuple-element.137) | copy-start | bytes 3145732
  335.6 32.3 %collective-permute-start.11 = (bf16[4,1024,512]{2,1,0:T(8,128)(2,1)}, bf16[4,1024,512]{2,1,0:T(8,128)(2,1)}, u32[]{:S(2)}, u32[]{:S(2)}) collective-permute-start(bf16[4,1024,512]{2,1,0:T(8,128)(2,1)} %pad_maximum_fusion), channel_id=1, source_target_pairs={{0,4},{4,0},{8,12},{12,8},{1,5},{5,1},{9,13},{13,9},{2,6},{6,2},{1... | collective-permute-start | bytes 12582920 | tf_op jit(solution)/shard_map/ppermute | solution.py:383
  340.0 32.3 %collective-permute-start.12 = (bf16[1024,512]{1,0:T(8,128)(2,1)}, bf16[1024,512]{1,0:T(8,128)(2,1)}, u32[]{:S(2)}, u32[]{:S(2)}) collective-permute-start(bf16[1024,512]{1,0:T(8,128)(2,1)} %fusion.34), channel_id=1, source_target_pairs={{0,16},{16,0},{1,17},{17,1},{2,18},{18,2},{3,19},{19,3},{4,20},{20... | collective-permute-start | bytes 3145736 | tf_op jit(solution)/shard_map/ppermute | solution.py:398
  349.8 159.6 %all-gather.16.cloned.1.call-start = ((), (), s32[]{:S(2)}) async-start(), calls=%async_computation.11 | async-start | bytes 1802240 | tf_op jit(solution)/shard_map/all_gather | solution.py:437
  373.7 48.8 %collective-permute-start.13 = (bf16[4,1024,256]{2,1,0:T(8,128)(2,1)}, bf16[4,1024,256]{2,1,0:T(8,128)(2,1)}, u32[]{:S(2)}, u32[]{:S(2)}) collective-permute-start(bf16[4,1024,256]{2,1,0:T(8,128)(2,1)} %constant_dynamic-slice_fusion.9), channel_id=1, source_target_pairs={{0,16},{16,0},{1,17},{17,1},{2,18},{18,2},{3,19},{19,3},{4,20},{20... | collective-permute-start | bytes 6291464 | tf_op jit(solution)/shard_map/ppermute | solution.py:360
  374.3 31.3 %copy-start.23 = (f32[512,1024]{1,0:T(8,128)S(1)}, f32[512,1024]{1,0:T(8,128)}, u32[]{:S(2)}) copy-start(f32[512,1024]{1,0:T(8,128)} %copy-done.22) | copy-start | bytes 6291460
  374.3 31.3 %copy-start.63 = (f32[1,1,1024]{2,1,0:T(1,128)S(1)}, f32[1,1,1024]{2,1,0:T(1,128)}, u32[]{:S(2)}) copy-start(f32[1,1,1024]{2,1,0:T(1,128)} %copy-done.62) | copy-start | bytes 12292
  374.3 32.1 %copy-start.16 = (bf16[2048,1024]{1,0:T(8,128)(2,1)S(1)}, bf16[2048,1024]{1,0:T(8,128)(2,1)}, u32[]{:S(2)}) copy-start(bf16[2048,1024]{1,0:T(8,128)(2,1)} %fusion.6) | copy-start | bytes 12582916
  426.0 44.2 %collective-permute-start.14 = (bf16[2,1024,512]{2,1,0:T(8,128)(2,1)}, bf16[2,1024,512]{2,1,0:T(8,128)(2,1)}, u32[]{:S(2)}, u32[]{:S(2)}) collective-permute-start(bf16[2,1024,512]{2,1,0:T(8,128)(2,1)} %pad_maximum_fusion.4), channel_id=1, source_target_pairs={{0,4},{4,0},{8,12},{12,8},{1,5},{5,1},{9,13},{13,9},{2,6},{6,2},{1... | collective-permute-start | bytes 6291464 | tf_op jit(solution)/shard_map/ppermute | solution.py:383
  426.0 47.5 %collective-permute-start.15 = (bf16[2,1024,512]{2,1,0:T(8,128)(2,1)}, bf16[2,1024,512]{2,1,0:T(8,128)(2,1)}, u32[]{:S(2)}, u32[]{:S(2)}) collective-permute-start(bf16[2,1024,512]{2,1,0:T(8,128)(2,1)} %pad_maximum_fusion.5), channel_id=1, source_target_pairs={{0,4},{4,0},{8,12},{12,8},{1,5},{5,1},{9,13},{13,9},{2,6},{6,2},{1... | collective-permute-start | bytes 6291464 | tf_op jit(solution)/shard_map/ppermute | solution.py:383
  434.3 33.1 %collective-permute-start.18 = (bf16[4,1024,128]{2,1,0:T(8,128)(2,1)}, bf16[4,1024,128]{2,1,0:T(8,128)(2,1)}, u32[]{:S(2)}, u32[]{:S(2)}) collective-permute-start(bf16[4,1024,128]{2,1,0:T(8,128)(2,1)} %constant_dynamic-slice_fusion.6), channel_id=1, source_target_pairs={{0,8},{4,12},{8,0},{12,4},{1,9},{5,13},{9,1},{13,5},{2,10},{6,14},... | collective-permute-start | bytes 3145736 | tf_op jit(solution)/shard_map/ppermute | solution.py:360
  435.5 6.8 %collective-permute-start.19 = (bf16[64,1408]{1,0:T(8,128)(2,1)S(1)}, bf16[64,1408]{1,0:T(8,128)(2,1)S(1)}, u32[]{:S(2)}, u32[]{:S(2)}) collective-permute-start(bf16[64,1408]{1,0:T(8,128)(2,1)S(1)} %get-tuple-element.185), channel_id=1, source_target_pairs={{0,16},{16,0},{1,17},{17,1},{2,18},{18,2},{3,19},{19,3},{4,20},{20... | collective-permute-start | bytes 540680 | tf_op jit(solution)/shard_map/ppermute | solution.py:433
  442.4 27.8 %copy-start.27 = (f32[1,1024,512]{2,1,0:T(8,128)S(1)}, f32[1,1024,512]{2,1,0:T(8,128)}, u32[]{:S(2)}) copy-start(f32[1,1024,512]{2,1,0:T(8,128)} %fusion.63) | copy-start | bytes 6291460
  443.2 102.8 %reduce-scatter.9.cloned.1.call-start = ((), (), s32[]{:S(2)}) async-start(), calls=%async_computation.7 | async-start | bytes 1310720 | tf_op jit(solution)/shard_map/reduce_scatter | solution.py:373
  482.7 24.2 %collective-permute-start.16 = (bf16[2,1024,256]{2,1,0:T(8,128)(2,1)S(1)}, bf16[2,1024,256]{2,1,0:T(8,128)(2,1)S(1)}, u32[]{:S(2)}, u32[]{:S(2)}) collective-permute-start(bf16[2,1024,256]{2,1,0:T(8,128)(2,1)S(1)} %constant_dynamic-slice_fusion.8), channel_id=1, source_target_pairs={{0,16},{16,0},{1,17},{17,1},{2,18},{18,2},{3,19},{19,3},{4,20},{20... | collective-permute-start | bytes 3145736 | tf_op jit(solution)/shard_map/ppermute | solution.py:360
  484.1 24.0 %collective-permute-start.17 = (bf16[2,1024,256]{2,1,0:T(8,128)(2,1)S(1)}, bf16[2,1024,256]{2,1,0:T(8,128)(2,1)S(1)}, u32[]{:S(2)}, u32[]{:S(2)}) collective-permute-start(bf16[2,1024,256]{2,1,0:T(8,128)(2,1)S(1)} %constant_dynamic-slice_fusion.7), channel_id=1, source_target_pairs={{0,8},{4,12},{8,0},{12,4},{1,9},{5,13},{9,1},{13,5},{2,10},{6,14},... | collective-permute-start | bytes 3145736 | tf_op jit(solution)/shard_map/ppermute | solution.py:360
  518.6 13.6 %collective-permute-start.20 = (bf16[2,1024,128]{2,1,0:T(8,128)(2,1)}, bf16[2,1024,128]{2,1,0:T(8,128)(2,1)}, u32[]{:S(2)}, u32[]{:S(2)}) collective-permute-start(bf16[2,1024,128]{2,1,0:T(8,128)(2,1)} %constant_dynamic-slice_fusion.4), channel_id=1, source_target_pairs={{0,8},{4,12},{8,0},{12,4},{1,9},{5,13},{9,1},{13,5},{2,10},{6,14},... | collective-permute-start | bytes 1572872 | tf_op jit(solution)/shard_map/ppermute | solution.py:360
  520.8 65.9 %reduce-scatter.11.cloned.1.call-start = ((), (), s32[]{:S(2)}) async-start(), calls=%async_computation.8 | async-start | bytes 1310720 | tf_op jit(solution)/shard_map/reduce_scatter | solution.py:373
  528.2 12.7 %collective-permute-start.21 = (bf16[2,1024,128]{2,1,0:T(8,128)(2,1)S(1)}, bf16[2,1024,128]{2,1,0:T(8,128)(2,1)S(1)}, u32[]{:S(2)}, u32[]{:S(2)}) collective-permute-start(bf16[2,1024,128]{2,1,0:T(8,128)(2,1)S(1)} %constant_dynamic-slice_fusion.3), channel_id=1, source_target_pairs={{0,16},{16,0},{1,17},{17,1},{2,18},{18,2},{3,19},{19,3},{4,20},{20... | collective-permute-start | bytes 1572872 | tf_op jit(solution)/shard_map/ppermute | solution.py:360
  529.3 27.1 %collective-permute-start.22 = (f32[4,1024]{1,0:T(4,128)S(1)}, f32[4,1024]{1,0:T(4,128)S(1)}, u32[]{:S(2)}, u32[]{:S(2)}) collective-permute-start(f32[4,1024]{1,0:T(4,128)S(1)} %pad_maximum_fusion.12), channel_id=1, source_target_pairs={{0,16},{16,0},{1,17},{17,1},{2,18},{18,2},{3,19},{19,3},{4,20},{20... | collective-permute-start | bytes 49160 | tf_op jit(solution)/shard_map/ppermute | solution.py:469
  546.0 84.9 %all-gather.12.cloned.1.call-start = ((), (), s32[]{:S(2)}) async-start(), calls=%async_computation.9 | async-start | bytes 2621440 | tf_op jit(solution)/shard_map/all_gather | solution.py:437
  556.4 2.6 collective-permute-start.24
  557.6 29.2 %collective-permute-start.23 = (bf16[1024,512]{1,0:T(8,128)(2,1)}, bf16[1024,512]{1,0:T(8,128)(2,1)}, u32[]{:S(2)}, u32[]{:S(2)}) collective-permute-start(bf16[1024,512]{1,0:T(8,128)(2,1)} %get-tuple-element.162), channel_id=1, source_target_pairs={{0,16},{16,0},{1,17},{17,1},{2,18},{18,2},{3,19},{19,3},{4,20},{20... | collective-permute-start | bytes 3145736 | tf_op jit(solution)/shard_map/ppermute | solution.py:471
  559.0 3.8 collective-permute-start.25
  560.5 16.0 %collective-permute-start.26 = (bf16[352,256]{1,0:T(8,128)(2,1)S(1)}, bf16[352,256]{1,0:T(8,128)(2,1)S(1)}, u32[]{:S(2)}, u32[]{:S(2)}) collective-permute-start(bf16[352,256]{1,0:T(8,128)(2,1)S(1)} %constant_dynamic-slice_fusion.1), channel_id=1, source_target_pairs={{0,8},{4,12},{8,0},{12,4},{1,9},{5,13},{9,1},{13,5},{2,10},{6,14},... | collective-permute-start | bytes 540680 | tf_op jit(solution)/shard_map/ppermute | solution.py:360
  587.8 8.6 %collective-permute-start.28 = (bf16[4,256,128]{2,1,0:T(8,128)(2,1)S(1)}, bf16[4,256,128]{2,1,0:T(8,128)(2,1)S(1)}, u32[]{:S(2)}, u32[]{:S(2)}) collective-permute-start(bf16[4,256,128]{2,1,0:T(8,128)(2,1)S(1)} %get-tuple-element.183), channel_id=1, source_target_pairs={{0,16},{16,0},{1,17},{17,1},{2,18},{18,2},{3,19},{19,3},{4,20},{20... | collective-permute-start | bytes 786440 | tf_op jit(solution)/shard_map/ppermute | solution.py:486
  602.1 24.6 %collective-permute-start.27 = (bf16[1024,512]{1,0:T(8,128)(2,1)S(1)}, bf16[1024,512]{1,0:T(8,128)(2,1)S(1)}, u32[]{:S(2)}, u32[]{:S(2)}) collective-permute-start(bf16[1024,512]{1,0:T(8,128)(2,1)S(1)} %get-tuple-element.163), channel_id=1, source_target_pairs={{0,16},{16,0},{1,17},{17,1},{2,18},{18,2},{3,19},{19,3},{4,20},{20... | collective-permute-start | bytes 3145736 | tf_op jit(solution)/shard_map/ppermute | solution.py:471
  (69 other events, 341.0 us)
Sparse Core Ops, SparseCore 0:
  11.6 121.9 all-gather.13
  136.5 59.7 all-gather.9
  301.7 31.2 reduce-scatter.4
  349.9 31.8 reduce-scatter.6
  443.3 24.6 all-gather.15
  520.9 25.0 reduce-scatter.8
  549.0 26.6 reduce-scatter.10
  597.5 19.4 all-gather.11

commit v9 on v8

--- a/solution.py
+++ b/solution.py
@@ -422,13 +422,12 @@
     latents = in_order(section, kept[:tokens] + got[tokens:], kept[tokens:] + got[:tokens])
     latents_out = latents.astype(BF).reshape(sections * rows, PATCHES, half)
     dq1, dk1, dv1 = attend_back(cross_back, q1, k1, v1, l1, c1, dc1, 4)
-    half_two = over_section(half_two, 2)
+    half_two = over_section(half_two[:2], 2), over_side(half_two[2:], 2)
+    dq1, half_two = together((dq1, half_two))
+    half_two = jnp.concatenate([over_side(half_two[0], 2), over_section(half_two[1], 2)], axis=0)
     one_pairs = [(query_in, dq1), (key_in, dk1)], [(key_in, dv1), (c1, d_carried)]
     send_one = [to_core(pairs) for pairs in one_pairs]
-    dq1, dk1, dv1, send_one, half_two, sum_in, sum_down = together(
-        (dq1, dk1, dv1, send_one, half_two, sum_in, sum_down)
-    )
-    half_two = over_side(half_two, 2)
+    dq1, dk1, dv1, send_one, sum_in, sum_down = together((dq1, dk1, dv1, send_one, sum_in, sum_down))
     sum_in = jnp.stack([lax.dynamic_index_in_dim(sum_in, section, 0, False),
                         lax.ppermute(lax.dynamic_index_in_dim(sum_in, 1 - section, 0, False), "section", swap)])
     sum_in = jnp.where(section == 0, sum_in, sum_in[::-1])
@@ -441,16 +440,16 @@
 
     sum_in = gathered(sum_in)
     half_one = [of_chip(pairs, sent) for pairs, sent in zip(one_pairs, send_one)]
-    dq1, dk1, dv1, half_one = together((dq1, dk1, dv1, half_one))
+    dq1, dk1, dv1, half_one, half_two = together((dq1, dk1, dv1, half_one, half_two))
+    sum_two = line_sum(half_two, 1)
     grad_query_in = nt(dq1, wq[0])
     grad_key_in = nt(dk1, wk[0]) + nt(dv1, wv[0])
     half_one = over_section(half_one[0], 2), over_side(half_one[1], 2)
-    grad_query_in, grad_key_in, half_one, half_two, sum_in = together(
-        (grad_query_in, grad_key_in, half_one, half_two, sum_in)
-    )
-    sum_two = line_sum(half_two, 1)
+    grad_query_in, grad_key_in, half_one, sum_in = together((grad_query_in, grad_key_in, half_one, sum_in))
     half_one = jnp.concatenate([over_side(half_one[0], 2), over_section(half_one[1], 2)], axis=0)
-    half_one, sum_two, sum_down = together((half_one, sum_two, sum_down))
+    grad_query_in, grad_key_in, half_one, sum_two, sum_down = together(
+        (grad_query_in, grad_key_in, half_one, sum_two, sum_down)
+    )
     sum_down = over_side(sum_down, 1)
     sum_one = line_sum(half_one, 1)
 
@@ -467,37 +466,38 @@
 
     gain_grads = jnp.stack([gain_query, gain_key, gain_normed, gain_mix])
     gain_grads = gain_grads + lax.ppermute(gain_grads, "section", swap)
-    other, gain_grads = together((other, gain_grads))
+    other, gain_grads, sum_one = together((other, gain_grads, sum_one))
     got = [lax.ppermute(other[row], "section", swap) for row in range(rows)]
     for pairs in (core_pairs, side_pairs):
         gain_grads = gain_grads + lax.ppermute(gain_grads, "group", pairs)
     gain_grads = jnp.sum(lax.all_gather(gain_grads, "dp", axis=0, tiled=False), axis=0)
 
-    ffn_gdown = laid_out(gathered(sum_down), (0, 2, 1, 3))
     ffn_gin = jnp.concatenate(
         [laid_out([sum_in[at, t] for at in (2 * y, 2 * y + 1) for t in range(sections)], range(4)) for y in (0, 1)],
         axis=0,
     )
-    sum_one, got[0], gain_grads, ffn_gdown = together((sum_one, got[0], gain_grads, ffn_gdown))
-    bytes_out = in_order(section, own, jnp.stack(got)).reshape(sections * rows, ROW_BYTES, half)
+    bytes_got = got
 
     kept = jnp.where(section == 0, sum_one, sum_two)
     sent = jnp.where(section == 0, sum_two, sum_one)
     got = lax.ppermute(sent, "section", swap)
+    got, sum_down = together((got, sum_down))
+    ffn_gdown = laid_out(gathered(sum_down), (0, 2, 1, 3))
     eighths = jnp.where(
         section == 0, jnp.concatenate([kept, got], axis=2), jnp.concatenate([got, kept], axis=2)
     )
     width = eighths.shape[2] // 2
-    parts = [piece for every in gathered(eighths) for piece in (every[..., :width], every[..., width:])]
-    section_first = laid_out(parts, (0, 4, 1, 5, 2, 6, 3, 7))
+    eighths, bytes_got = together((gathered(eighths), bytes_got))
+    bytes_out = in_order(section, own, jnp.stack(bytes_got)).reshape(sections * rows, ROW_BYTES, half)
+    parts = [piece for every in eighths for piece in (every[..., :width], every[..., width:])]
+    section_first = laid_out([part[:2] for part in parts], (0, 4, 1, 5, 2, 6, 3, 7))
     side_first = laid_out([part[2:] for part in parts], (0, 1, 4, 5, 2, 3, 6, 7))
-    last = jnp.where(section == 0, side_first, section_first[2:])
-    grad_qkv = jnp.concatenate([section_first[:2], last[:1]], axis=0)[None]
+    grad_qkv = jnp.concatenate([section_first, side_first[:1]], axis=0)[None]
 
     gain_grads = lax.dynamic_slice_in_dim(gain_grads.reshape(2, 2, D), section, 1, 0)
     width = D // lax.axis_size("dp")
     gain_out = lax.dynamic_slice_in_dim(gain_grads, lax.axis_index("dp") * width, width, 2)
-    return (latents_out, bytes_out, grad_qkv, last[1:], gain_out, ffn_gin, ffn_gdown)
+    return (latents_out, bytes_out, grad_qkv, side_first[1:], gain_out, ffn_gin, ffn_gdown)
 
 
 def solution(mesh):

time: 651 us -> 636 us (0.977)
  waiting for transfers between devices: 193 us -> 184 us
    ppermute x8 -> x10, waiting for transfers between devices: 46.8 us -> 20.6 us  [exchanged(): lax.ppermute(other, axis, pairs).astype(F32)]
    ppermute x1, waiting for transfers between devices: 2.77 us -> 13.1 us  [shards(): lax.ppermute(lax.dynamic_index_in_dim(sum_in, 1 - section, 0, False), 'se...]
    reduce_scatter x4, waiting for transfers between devices: 3.82 us -> 12.4 us  [line_sum(): return lax.psum_scatter(values, 'dp', scatter_dimension=where, tiled=True)]
    ppermute x8 -> x10, starting transfers between devices: 11.7 us -> 3.82 us  [exchanged(): lax.ppermute(other, axis, pairs).astype(F32)]
    convert_element_type x8 -> x10, other arithmetic: 12.1 us -> 14.2 us  [exchanged(): (own.astype(F32) + lax.ppermute(other, axis, pairs).astype(F32)).astype(BF)]
    unnamed x171 -> x195, local copies, waits for them, and re-layouts: 12.2 us -> 13.7 us
  transfers between devices with their start and end apart: 37 -> 39, of which waited for: 14 -> 11; matrix products, arithmetic and copies ran while one was open for 37% -> 38% of each run, Pallas kernels for 10% -> 10%
where the time goes in v9:
time: 636 us; the launch traced here: 631 us
  waiting for transfers between devices  184 us (29%)
  matrix products  177 us (28%)
  other arithmetic  103 us (16%)
  Pallas kernels  60.8 us (10%)
  local copies, waits for them, and re-layouts  35.4 us (6%)
  starting transfers between devices  28.7 us (5%)
  blocking collectives  24.9 us (4%)
  between operations  15.8 us (2%)
    all_gather x1, waiting for transfers between devices, shards(): lax.all_gather(matrix, ('section', 'group', 'dp'), axis=0, tiled=True)  92.7 us
    dot_general x11, matrix products, nt(): lax.dot_general(left, right, (((1,), (1,)), ((), ())), preferred_element_...  61.3 us
    dot_general x20, matrix products, tn(): lax.dot_general(left, right, (((0,), (0,)), ((), ())), preferred_element_...  56.5 us
    dot_general x10, matrix products, nn(): return jnp.dot(left, right, preferred_element_type=F32)  54.6 us
    pallas_call x2, Pallas kernels, attend_back(): pl.pallas_call(functools.partial(attend_back_kernel, chunk, spans), grid_...  40.2 us
    ppermute x1, waiting for transfers between devices, shards(): lax.ppermute(mix_in, 'section', swap)  22.3 us
    ppermute x10, waiting for transfers between devices, exchanged(): lax.ppermute(other, axis, pairs).astype(F32)  20.6 us
    pallas_call x2, Pallas kernels, attend(): pl.pallas_call(functools.partial(attend_kernel, chunk, spans), grid_spec=...  20.6 us
  transfers between devices with their start and end apart: 39, of which 11 were waited for; matrix products, arithmetic and copies ran while one was open for 38% of the time, Pallas kernels for 10%

profile of v9, /device:TPU:0, one launch (start us, length us, event | category | flops | bytes accessed | tf_op | source)
XLA Modules:
  0.0 630.7 jit_solution(4927464624105046218)
XLA Ops:
  22.2 4.4 all_gather.31
  26.6 3.1 fusion.2
  30.6 3.8 multiply_reduce_fusion.5
  40.9 92.7 %all-gather.14.cloned.1.call-done = bf16[1,8192,1024]{2,1,0:T(8,128)(2,1)} async-done(((bf16[1,256,1024]{2,1,0:T(8,128)(2,1)}), bf16[1,8192,1024]{2,1,0:T(8,128)(2,1)}) %all-gather.14.cloned.1.call-update) | async-done | bytes 16777232 | tf_op jit(solution)/shard_map/all_gather | solution.py:264
  133.6 9.5 %convolution_convert_fusion.1.v_ref = bf16[2048,1024]{1,0:T(8,128)(2,1)} fusion(bf16[2048,1024]{1,0:T(8,128)(2,1)} %bitcast.281, bf16[2,4,1024,1024]{3,2,1,0:T(8,128)(2,1)} %bitcast.350), kind=kOutput, calls=%fused_computation.51 | convolution fusion | flops 4297064448 | bytes 10485760 | tf_op jit(solution)/shard_map/dot_general | solution.py:31
  147.6 8.0 %convolution_convert_fusion.2.k_ref = bf16[2048,1024]{1,0:T(8,128)(2,1)} fusion(bf16[2048,1024]{1,0:T(8,128)(2,1)S(1)} %bitcast.282, bf16[2,4,1024,1024]{3,2,1,0:T(8,128)(2,1)} %bitcast.352), kind=kOutput, calls=%fused_computation.52 | convolution fusion | flops 4297064448 | bytes 10485760 | tf_op jit(solution)/shard_map/dot_general | solution.py:31
  155.6 16.5 %attend.2 = (bf16[512,1024]{1,0:T(8,128)(2,1)S(1)}, f32[2,8,2,256]{3,2,1,0:T(2,128)S(1)}) custom-call(s32[2,2]{1,0:T(2,128)S(1)} %get-tuple-element.230.first_ref, s32[2,2]{1,0:T(2,128)S(1)} %get-tuple-element.215.stop_ref, s32[2,1,256]{2,1,0:T(1,128)S(1)} %broadcast_in_dim.73.lo_ref, s32[2,1,256]{2,1,0:T(1,128)S(1)} %bitcast.270, ...), custom_call_target="tpu_custom_call" | custom-call | flops 8589934592 | bytes 18874368 | tf_op jit(solution)/shard_map/attend/pallas_call | solution.py:186
  172.1 3.4 fusion.23
  175.5 3.3 fusion.78.q_ref
  178.8 3.3 fusion.77.k_ref
  182.1 3.3 fusion.76.v_ref
  185.5 4.1 attend.3
  199.1 22.3 %collective-permute-done.4 = bf16[512,1024]{1,0:T(8,128)(2,1)} collective-permute-done((bf16[512,1024]{1,0:T(8,128)(2,1)}, bf16[512,1024]{1,0:T(8,128)(2,1)}, u32[]{:S(2)}, u32[]{:S(2)}) %collective-permute-start.4) | collective-permute-done | bytes 1048608 | tf_op jit(solution)/shard_map/ppermute | solution.py:345
  221.4 11.8 %fusion.110 = f32[1024,2816]{1,0:T(8,128)} fusion(bf16[1024,2816]{1,0:T(8,128)(2,1)} %bitcast.366, bf16[512,1024]{1,0:T(8,128)(2,1)} %collective-permute-done.4, bf16[512,1024]{1,0:T(8,128)(2,1)} %multiply_convert_fusion.4), kind=kOutput, calls=%fused_computation.203 | convolution fusion | flops 5909774336 | bytes 19398656 | tf_op jit(solution)/shard_map/dot_general | solution.py:31
  233.2 3.3 maximum_select_fusion.1
  236.6 12.2 %multiply_convert_fusion = (bf16[1024,1408]{1,0:T(8,128)(2,1)S(1)}, bf16[1024,1408]{1,0:T(8,128)(2,1)S(1)}, bf16[1024,1408]{1,0:T(8,128)(2,1)}) fusion(f32[1024,2816]{1,0:T(8,128)} %fusion.110, bf16[1408,1024]{1,0:T(8,128)(2,1)S(1)} %bitcast.285, bf16[512,1024]{1,0:T(8,128)(2,1)S(1)} %bitcast.292, bf16[512,1024]{1,0:T(8,128)(2,1)S(1)} %bitcast.278), kind=kOutput, calls=%fused_computation.29 | convolution fusion | flops 2980052992 | bytes 25165824 | tf_op jit(solution)/shard_map/dot_general | solution.py:39
  250.7 4.2 fusion.81
  257.7 6.8 %convolution_convert_fusion = bf16[1024,1408]{1,0:T(8,128)(2,1)} fusion(s32[]{:T(128)S(6)} %select_n.315, bf16[1024,1408]{1,0:T(8,128)(2,1)S(1)} %get-tuple-element.156, bf16[1024,1408]{1,0:T(8,128)(2,1)S(1)} %get-tuple-element.155, bf16[512,1024]{1,0:T(8,128)(2,1)} %collective-permute-done.4, bf16[512,1024]{1,0:T(8,128)(2,1)} %multiply_convert_fusion.4), kind=kOutput, calls=%fused_computation.50 | convolution fusion | flops 2964193280 | bytes 10747908 | tf_op jit(solution)/shard_map/dot_general | solution.py:35
  265.2 6.1 fusion.176
  276.1 4.2 add_convert_fusion.2
  280.4 7.1 %add_convert_fusion = bf16[1024,1408]{1,0:T(8,128)(2,1)S(1)} fusion(bf16[1024,1408]{1,0:T(8,128)(2,1)} %collective-permute-done.8, s32[]{:T(128)S(6)} %select_n.318, bf16[1024,1408]{1,0:T(8,128)(2,1)} %copy-done.40, bf16[1024,1408]{1,0:T(8,128)(2,1)} %copy-done.39, bf16[512,1024]{1,0:T(8,128)(2,1)} %collective-permute-done.4, ...), kind=kOutput, calls=%fused_computation.28 | convolution fusion | flops 2967076864 | bytes 13631492 | tf_op jit(solution)/shard_map/dot_general | solution.py:35
  287.4 3.2 collective-permute-done.7
  290.7 8.2 %multiply_reduce_fusion = (f32[1024]{0:T(1024)}, f32[512]{0:T(512)S(1)}, f32[512,1024]{1,0:T(8,128)}) fusion(f32[512,1024]{1,0:T(8,128)S(1)} %get-tuple-element.227, f32[512]{0:T(512)S(1)} %get-tuple-element.211, bf16[512,1024]{1,0:T(8,128)(2,1)} %collective-permute-done.7, f32[1024]{0:T(1024)S(1)} %bitcast.321, bf16[512,2816]{1,0:T(8,128)(2,1)S(1)} %copy-done.38, ...), kind=kOutput, calls=%fused_computation.100 | convolution fusion | flops 2956982784 | bytes 13905920 | tf_op jit(solution)/shard_map/dot_general | solution.py:39
  300.2 4.0 fusion.168
  304.2 4.3 fusion.75.dc_ref
  308.5 11.7 %attend_back.2 = (bf16[512,1024]{1,0:T(8,128)(2,1)S(1)}, bf16[512,1024]{1,0:T(8,128)(2,1)S(1)}, bf16[512,1024]{1,0:T(8,128)(2,1)S(1)}) custom-call(s32[2,2]{1,0:T(2,128)S(1)} %get-tuple-element.233.first_ref, s32[2,2]{1,0:T(2,128)S(1)} %get-tuple-element.232.stop_ref, s32[2,1,256]{2,1,0:T(1,128)S(1)} %broadcast_in_dim.83.lo_ref, ...), custom_call_target="tpu_custom_call" | custom-call | flops 5368709120 | bytes 6291456 | tf_op jit(solution)/shard_map/attend_back/pallas_call | solution.py:210
  326.9 6.4 %collective-permute-done.10 = bf16[2,4,1,64,1408]{4,3,2,1,0:T(8,128)(2,1)} collective-permute-done((bf16[2,4,1,64,1408]{4,3,2,1,0:T(8,128)(2,1)}, bf16[2,4,1,64,1408]{4,3,2,1,0:T(8,128)(2,1)}, u32[]{:S(2)}, u32[]{:S(2)}) %collective-permute-start.10) | collective-permute-done | bytes 1441824 | tf_op jit(solution)/shard_map/ppermute | solution.py:360
  336.1 4.4 fusion.6
  356.1 4.2 fusion.32
  369.5 3.4 fusion
  375.2 28.5 %attend_back.3 = (bf16[512,1024]{1,0:T(8,128)(2,1)S(1)}, bf16[2048,1024]{1,0:T(8,128)(2,1)}, bf16[2048,1024]{1,0:T(8,128)(2,1)}) custom-call(s32[2,2]{1,0:T(2,128)S(1)} %get-tuple-element.231.first_ref, s32[2,2]{1,0:T(2,128)S(1)} %get-tuple-element.214.stop_ref, s32[2,1,256]{2,1,0:T(1,128)S(1)} %broadcast_in_dim.73.lo_ref, s32[2,1,256]{2,1,0:T(1,128)S(1)} %bitcast.271, ...), custom_call_target="tpu_custom_call" | custom-call | flops 21474836480 | bytes 18874368 | tf_op jit(solution)/shard_map/attend_back/pallas_call | solution.py:210
  403.7 4.1 fusion.87
  413.2 3.7 fusion.63
  425.8 6.6 %fusion.66 = f32[1,1024,512]{2,1,0:T(8,128)} fusion(bf16[2048,1024]{1,0:T(8,128)(2,1)} %fusion.6, bf16[2048,1024]{1,0:T(8,128)(2,1)} %get-tuple-element.115, s32[]{:T(128)S(6)} %select_n.319), kind=kOutput, calls=%fused_computation.152 | convolution fusion | flops 2147483648 | bytes 8388612 | tf_op jit(solution)/shard_map/dot_general | solution.py:35
  438.6 13.1 %collective-permute-done.21 = bf16[64,1408]{1,0:T(8,128)(2,1)S(1)} collective-permute-done((bf16[64,1408]{1,0:T(8,128)(2,1)S(1)}, bf16[64,1408]{1,0:T(8,128)(2,1)S(1)}, u32[]{:S(2)}, u32[]{:S(2)}) %collective-permute-start.21) | collective-permute-done | bytes 180256 | tf_op jit(solution)/shard_map/ppermute | solution.py:432
  456.7 4.0 fusion.12
  467.1 6.6 %fusion.48 = f32[2048,1024]{1,0:T(8,128)S(1)} fusion(bf16[2048,1024]{1,0:T(8,128)(2,1)S(1)} %copy-done.58, bf16[2,4,1024,1024]{3,2,1,0:T(8,128)(2,1)} %bitcast.363), kind=kOutput, calls=%fused_computation.132 | convolution fusion | flops 4294967296 | bytes 14680064 | tf_op jit(solution)/shard_map/dot_general | solution.py:39
  473.7 8.6 %convolution_add_fusion = f32[2048,1024]{1,0:T(8,128)} fusion(f32[2048,1024]{1,0:T(8,128)S(1)} %fusion.48, bf16[2048,1024]{1,0:T(8,128)(2,1)S(1)} %copy-done.56, bf16[2,4,1024,1024]{3,2,1,0:T(8,128)(2,1)} %bitcast.364), kind=kOutput, calls=%fused_computation.49 | convolution fusion | flops 4297064448 | bytes 23068672 | tf_op jit(solution)/shard_map/dot_general | solution.py:39
  482.4 4.2 fusion.46
  496.4 10.2 %collective-permute-done.23 = bf16[2,1024,128]{2,1,0:T(8,128)(2,1)S(1)} collective-permute-done((bf16[2,1024,128]{2,1,0:T(8,128)(2,1)}, bf16[2,1024,128]{2,1,0:T(8,128)(2,1)S(1)}, u32[]{:S(2)}, u32[]{:S(2)}) %collective-permute-start.23) | collective-permute-done | bytes 524320 | tf_op jit(solution)/shard_map/ppermute | solution.py:360
  513.1 6.0 fusion.11
  527.2 4.9 fusion.1
  535.7 12.4 %reduce-scatter.11.cloned.1.call-done = bf16[4,256,128]{2,1,0:T(8,128)(2,1)} async-done(((bf16[4,1024,128]{2,1,0:T(8,128)(2,1)}), bf16[4,256,128]{2,1,0:T(8,128)(2,1)}) %reduce-scatter.11.cloned.1.call-update) | async-done | bytes 262160 | tf_op jit(solution)/shard_map/reduce_scatter | solution.py:373
  551.3 6.5 %collective-permute-done.25 = bf16[4,256,128]{2,1,0:T(8,128)(2,1)S(1)} collective-permute-done((bf16[4,256,128]{2,1,0:T(8,128)(2,1)}, bf16[4,256,128]{2,1,0:T(8,128)(2,1)S(1)}, u32[]{:S(2)}, u32[]{:S(2)}) %collective-permute-start.25) | collective-permute-done | bytes 262176 | tf_op jit(solution)/shard_map/ppermute | solution.py:483
  569.7 8.4 %maximum_convert_fusion = f32[128,5632]{1,0:T(8,128)} fusion(bf16[64,1408]{1,0:T(8,128)(2,1)S(1)} %get-tuple-element.181, bf16[64,1408]{1,0:T(8,128)(2,1)S(1)} %get-tuple-element.182, bf16[64,1408]{1,0:T(8,128)(2,1)S(1)} %get-tuple-element.183, bf16[64,1408]{1,0:T(8,128)(2,1)S(1)} %get-tuple-element.184, bf16[64,1408]{1,0:T(8,128)(2,1)S(1)} %get-tuple-element.185, ...), kind=kLoop, calls=%fused_computation.169 | loop fusion | flops 11534336 | bytes 4325376 | tf_op jit(solution)/shard_map/concatenate | solution.py:475
  578.0 13.1 %all-gather.4 = f32[4,4,1024]{2,1,0:T(4,128)S(1)} all-gather(f32[1,4,1024]{2,1,0:T(4,128)S(1)} %add_bitcast_fusion), channel_id=4, replica_groups=mesh['section'=2,'group'=4,'dp'=4] {'dp'}, dimensions={0}, use_global_device_ids=true | all-gather | bytes 81920 | tf_op jit(solution)/shard_map/all_gather | solution.py:473
  591.9 7.4 %all-gather.3 = bf16[1408,256]{1,0:T(8,128)(2,1)S(1)} all-gather(bf16[352,256]{1,0:T(8,128)(2,1)S(1)} %add_convert_fusion.12), channel_id=5, replica_groups=mesh['section'=2,'group'=4,'dp'=4] {'group'}, dimensions={0}, use_global_device_ids=true | all-gather | bytes 901120 | tf_op jit(solution)/shard_map/all_gather | solution.py:436
  600.6 13.2 %collective-permute-done.28 = bf16[1024,512]{1,0:T(8,128)(2,1)S(1)} collective-permute-done((bf16[1024,512]{1,0:T(8,128)(2,1)S(1)}, bf16[1024,512]{1,0:T(8,128)(2,1)S(1)}, u32[]{:S(2)}, u32[]{:S(2)}) %collective-permute-start.28) | collective-permute-done | bytes 1048608 | tf_op jit(solution)/shard_map/ppermute | solution.py:470
  (407 shorter events, 170.4 us)
Async XLA Ops:
  7.2 126.4 %all-gather.14.cloned.1.call-start = ((), (), s32[]{:S(2)}) async-start(), calls=%async_computation.10 | async-start | bytes 17301504 | tf_op jit(solution)/shard_map/all_gather | solution.py:264
  9.3 189.8 %all-gather.10.cloned.1.call-start = ((), (), s32[]{:S(2)}) async-start(), calls=%async_computation.4 | async-start | bytes 6127616 | tf_op jit(solution)/shard_map/all_gather | solution.py:287
  10.4 29.4 %collective-permute-start = (bf16[88,1024]{1,0:T(8,128)(2,1)S(1)}, bf16[88,1024]{1,0:T(8,128)(2,1)}, u32[]{:S(2)}, u32[]{:S(2)}) collective-permute-start(bf16[88,1024]{1,0:T(8,128)(2,1)S(1)} %get-tuple-element.152), channel_id=1, source_target_pairs={{0,1},{1,2},{2,3},{3,0},{4,5},{5,6},{6,7},{7,4},{8,9},{9,10},{10,1... | collective-permute-start | bytes 540680 | tf_op jit(solution)/shard_map/ppermute | solution.py:293
  13.5 27.3 %collective-permute-start.1 = (bf16[88,1024]{1,0:T(8,128)(2,1)S(1)}, bf16[88,1024]{1,0:T(8,128)(2,1)S(1)}, u32[]{:S(2)}, u32[]{:S(2)}) collective-permute-start(bf16[88,1024]{1,0:T(8,128)(2,1)S(1)} %get-tuple-element.152), channel_id=1, source_target_pairs={{0,2},{1,3},{2,0},{3,1},{4,6},{5,7},{6,4},{7,5},{8,10},{9,11},{10,... | collective-permute-start | bytes 540680 | tf_op jit(solution)/shard_map/ppermute | solution.py:293
  16.1 24.8 %collective-permute-start.2 = (bf16[88,1024]{1,0:T(8,128)(2,1)S(1)}, bf16[88,1024]{1,0:T(8,128)(2,1)S(1)}, u32[]{:S(2)}, u32[]{:S(2)}) collective-permute-start(bf16[88,1024]{1,0:T(8,128)(2,1)S(1)} %get-tuple-element.152), channel_id=1, source_target_pairs={{0,3},{1,0},{2,1},{3,2},{4,7},{5,4},{6,5},{7,6},{8,11},{9,8},{10,9... | collective-permute-start | bytes 540680 | tf_op jit(solution)/shard_map/ppermute | solution.py:293
  18.7 10.9 %collective-permute-start.5 = (bf16[32,2816]{1,0:T(8,128)(2,1)S(1)}, bf16[32,2816]{1,0:T(8,128)(2,1)S(1)}, u32[]{:S(2)}, u32[]{:S(2)}) collective-permute-start(bf16[32,2816]{1,0:T(8,128)(2,1)S(1)} %pad_maximum_fusion.12), channel_id=1, source_target_pairs={{0,16},{16,0},{1,17},{17,1},{2,18},{18,2},{3,19},{19,3},{4,20},{20... | collective-permute-start | bytes 540680 | tf_op jit(solution)/shard_map/ppermute | solution.py:285
  22.1 15.9 %copy-start.72 = (f32[1,2,2,128]{3,1,2,0:T(2,128)}, f32[1,2,2,128]{3,1,2,0:T(2,128)S(1)}, u32[]{:S(2)}) copy-start(f32[1,2,2,128]{3,1,2,0:T(2,128)S(1)} %copy.28) | copy-start | bytes 6148
  30.5 305.6 %reduce-scatter.5.cloned.1.call-start = ((), (), s32[]{:S(2)}) async-start(), calls=%async_computation.5 | async-start | bytes 1802240 | tf_op jit(solution)/shard_map/reduce_scatter | solution.py:373
  34.5 230.6 %copy-start.70 = (f32[1,8,2,128]{3,2,1,0:T(2,128)}, f32[1,8,2,128]{3,2,1,0:T(2,128)S(1)}, u32[]{:S(2)}) copy-start(f32[1,8,2,128]{3,2,1,0:T(2,128)S(1)} %get-tuple-element.204) | copy-start | bytes 24580
  38.3 133.9 %copy-start.22 = (f32[512,1024]{1,0:T(8,128)}, f32[512,1024]{1,0:T(8,128)S(1)}, u32[]{:S(2)}) copy-start(f32[512,1024]{1,0:T(8,128)S(1)} %bitcast_divide_fusion) | copy-start | bytes 6291460
  143.1 46.5 %collective-permute-start.3 = (bf16[4,88,1024]{2,1,0:T(8,128)(2,1)S(1)}, bf16[4,88,1024]{2,1,0:T(8,128)(2,1)S(1)}, u32[]{:S(2)}, u32[]{:S(2)}) collective-permute-start(bf16[4,88,1024]{2,1,0:T(8,128)(2,1)S(1)} %bitcast_dynamic-update-slice_fusion), channel_id=1, source_target_pairs={{0,8},{4,12},{8,0},{12,4},{1,9},{5,13},{9,1},{13,5},{2,10},{6,14},... | collective-permute-start | bytes 2162696 | tf_op jit(solution)/shard_map/ppermute | solution.py:276
  195.2 26.2 %collective-permute-start.4 = (bf16[512,1024]{1,0:T(8,128)(2,1)}, bf16[512,1024]{1,0:T(8,128)(2,1)}, u32[]{:S(2)}, u32[]{:S(2)}) collective-permute-start(bf16[512,1024]{1,0:T(8,128)(2,1)} %multiply_convert_fusion.4), channel_id=1, source_target_pairs={{0,16},{16,0},{1,17},{17,1},{2,18},{18,2},{3,19},{19,3},{4,20},{20... | collective-permute-start | bytes 3145736 | tf_op jit(solution)/shard_map/ppermute | solution.py:345
  197.9 35.3 %collective-permute-start.6 = (bf16[2,4,88,1024]{3,2,0,1:T(8,128)(2,1)}, bf16[2,4,88,1024]{3,2,0,1:T(8,128)(2,1)}, u32[]{:S(2)}, u32[]{:S(2)}) collective-permute-start(bf16[2,4,88,1024]{3,2,0,1:T(8,128)(2,1)} %maximum_select_fusion.3), channel_id=1, source_target_pairs={{0,4},{4,0},{8,12},{12,8},{1,5},{5,1},{9,13},{13,9},{2,6},{6,2},{1... | collective-permute-start | bytes 4325384 | tf_op jit(solution)/shard_map/ppermute | solution.py:276
  233.2 17.5 %slice-start.4 = ((s8[5767168]{0:T(1024)(128)(4,1)}), s8[4194304]{0:T(1024)(128)(4,1)S(1)}, s32[]{:S(2)}) async-start(s8[5767168]{0:T(1024)(128)(4,1)} %bitcast.368), calls=%async_computation.16 | async-start | bytes 8388608
  264.6 15.8 %collective-permute-start.8 = (bf16[1024,1408]{1,0:T(8,128)(2,1)}, bf16[1024,1408]{1,0:T(8,128)(2,1)}, u32[]{:S(2)}, u32[]{:S(2)}) collective-permute-start(bf16[1024,1408]{1,0:T(8,128)(2,1)} %convolution_convert_fusion), channel_id=1, source_target_pairs={{0,4},{4,0},{8,12},{12,8},{1,5},{5,1},{9,13},{13,9},{2,6},{6,2},{1... | collective-permute-start | bytes 8650760 | tf_op jit(solution)/shard_map/ppermute | solution.py:383
  264.7 10.0 %collective-permute-start.9 = (bf16[1408,512]{1,0:T(8,128)(2,1)}, bf16[1408,512]{1,0:T(8,128)(2,1)}, u32[]{:S(2)}, u32[]{:S(2)}) collective-permute-start(bf16[1408,512]{1,0:T(8,128)(2,1)} %convolution_convert_fusion.3), channel_id=1, source_target_pairs={{0,4},{4,0},{8,12},{12,8},{1,5},{5,1},{9,13},{13,9},{2,6},{6,2},{1... | collective-permute-start | bytes 4325384 | tf_op jit(solution)/shard_map/ppermute | solution.py:383
  265.2 25.5 %collective-permute-start.7 = (bf16[512,1024]{1,0:T(8,128)(2,1)}, bf16[512,1024]{1,0:T(8,128)(2,1)}, u32[]{:S(2)}, u32[]{:S(2)}) collective-permute-start(bf16[512,1024]{1,0:T(8,128)(2,1)} %fusion.81), channel_id=1, source_target_pairs={{0,16},{16,0},{1,17},{17,1},{2,18},{18,2},{3,19},{19,3},{4,20},{20... | collective-permute-start | bytes 3145736 | tf_op jit(solution)/shard_map/ppermute | solution.py:390
  300.1 33.1 %collective-permute-start.10 = (bf16[2,4,1,64,1408]{4,3,2,1,0:T(8,128)(2,1)}, bf16[2,4,1,64,1408]{4,3,2,1,0:T(8,128)(2,1)}, u32[]{:S(2)}, u32[]{:S(2)}) collective-permute-start(bf16[2,4,1,64,1408]{4,3,2,1,0:T(8,128)(2,1)} %constant_dynamic-slice_fusion.12), channel_id=1, source_target_pairs={{0,8},{4,12},{8,0},{12,4},{1,9},{5,13},{9,1},{13,5},{2,10},{6,14},... | collective-permute-start | bytes 4325384 | tf_op jit(solution)/shard_map/ppermute | solution.py:360
  300.2 123.1 %reduce-scatter.7.cloned.1.call-start = ((), (), s32[]{:S(2)}) async-start(), calls=%async_computation.6 | async-start | bytes 1802240 | tf_op jit(solution)/shard_map/reduce_scatter | solution.py:373
  304.2 16.0 %copy-start.52 = (bf16[512,1024]{1,0:T(8,128)(2,1)}, bf16[512,1024]{1,0:T(8,128)(2,1)S(1)}, u32[]{:S(2)}) copy-start(bf16[512,1024]{1,0:T(8,128)(2,1)S(1)} %get-tuple-element.149) | copy-start | bytes 3145732
  336.1 32.3 %collective-permute-start.11 = (bf16[4,1024,512]{2,1,0:T(8,128)(2,1)}, bf16[4,1024,512]{2,1,0:T(8,128)(2,1)}, u32[]{:S(2)}, u32[]{:S(2)}) collective-permute-start(bf16[4,1024,512]{2,1,0:T(8,128)(2,1)} %pad_maximum_fusion), channel_id=1, source_target_pairs={{0,4},{4,0},{8,12},{12,8},{1,5},{5,1},{9,13},{13,9},{2,6},{6,2},{1... | collective-permute-start | bytes 12582920 | tf_op jit(solution)/shard_map/ppermute | solution.py:383
  340.5 32.4 %collective-permute-start.12 = (bf16[1024,512]{1,0:T(8,128)(2,1)}, bf16[1024,512]{1,0:T(8,128)(2,1)}, u32[]{:S(2)}, u32[]{:S(2)}) collective-permute-start(bf16[1024,512]{1,0:T(8,128)(2,1)} %fusion.34), channel_id=1, source_target_pairs={{0,16},{16,0},{1,17},{17,1},{2,18},{18,2},{3,19},{19,3},{4,20},{20... | collective-permute-start | bytes 3145736 | tf_op jit(solution)/shard_map/ppermute | solution.py:398
  349.8 143.2 %all-gather.16.cloned.1.call-start = ((), (), s32[]{:S(2)}) async-start(), calls=%async_computation.11 | async-start | bytes 1802240 | tf_op jit(solution)/shard_map/all_gather | solution.py:436
  373.2 43.6 %collective-permute-start.13 = (bf16[2,1024,256]{2,1,0:T(8,128)(2,1)S(1)}, bf16[2,1024,256]{2,1,0:T(8,128)(2,1)S(1)}, u32[]{:S(2)}, u32[]{:S(2)}) collective-permute-start(bf16[2,1024,256]{2,1,0:T(8,128)(2,1)S(1)} %constant_dynamic-slice_fusion.11), channel_id=1, source_target_pairs={{0,16},{16,0},{1,17},{17,1},{2,18},{18,2},{3,19},{19,3},{4,20},{20... | collective-permute-start | bytes 3145736 | tf_op jit(solution)/shard_map/ppermute | solution.py:360
  374.8 43.5 %collective-permute-start.14 = (bf16[2,1024,256]{2,1,0:T(8,128)(2,1)S(1)}, bf16[2,1024,256]{2,1,0:T(8,128)(2,1)}, u32[]{:S(2)}, u32[]{:S(2)}) collective-permute-start(bf16[2,1024,256]{2,1,0:T(8,128)(2,1)S(1)} %constant_dynamic-slice_fusion.10), channel_id=1, source_target_pairs={{0,8},{4,12},{8,0},{12,4},{1,9},{5,13},{9,1},{13,5},{2,10},{6,14},... | collective-permute-start | bytes 3145736 | tf_op jit(solution)/shard_map/ppermute | solution.py:360
  375.2 28.5 %copy-start.16 = (bf16[2048,1024]{1,0:T(8,128)(2,1)S(1)}, bf16[2048,1024]{1,0:T(8,128)(2,1)}, u32[]{:S(2)}) copy-start(bf16[2048,1024]{1,0:T(8,128)(2,1)} %fusion.6) | copy-start | bytes 12582916
  423.2 33.5 %collective-permute-start.15 = (bf16[2,1024,512]{2,1,0:T(8,128)(2,1)}, bf16[2,1024,512]{2,1,0:T(8,128)(2,1)}, u32[]{:S(2)}, u32[]{:S(2)}) collective-permute-start(bf16[2,1024,512]{2,1,0:T(8,128)(2,1)} %pad_maximum_fusion.4), channel_id=1, source_target_pairs={{0,4},{4,0},{8,12},{12,8},{1,5},{5,1},{9,13},{13,9},{2,6},{6,2},{1... | collective-permute-start | bytes 6291464 | tf_op jit(solution)/shard_map/ppermute | solution.py:383
  432.4 28.3 %collective-permute-start.16 = (bf16[2,1024,512]{2,1,0:T(8,128)(2,1)}, bf16[2,1024,512]{2,1,0:T(8,128)(2,1)}, u32[]{:S(2)}, u32[]{:S(2)}) collective-permute-start(bf16[2,1024,512]{2,1,0:T(8,128)(2,1)} %pad_maximum_fusion.5), channel_id=1, source_target_pairs={{0,4},{4,0},{8,12},{12,8},{1,5},{5,1},{9,13},{13,9},{2,6},{6,2},{1... | collective-permute-start | bytes 6291464 | tf_op jit(solution)/shard_map/ppermute | solution.py:383
  433.4 19.6 %collective-permute-start.18 = (bf16[2,1024,128]{2,1,0:T(8,128)(2,1)}, bf16[2,1024,128]{2,1,0:T(8,128)(2,1)}, u32[]{:S(2)}, u32[]{:S(2)}) collective-permute-start(bf16[2,1024,128]{2,1,0:T(8,128)(2,1)} %constant_dynamic-slice_fusion.8), channel_id=1, source_target_pairs={{0,16},{16,0},{1,17},{17,1},{2,18},{18,2},{3,19},{19,3},{4,20},{20... | collective-permute-start | bytes 1572872 | tf_op jit(solution)/shard_map/ppermute | solution.py:360
  434.2 20.1 %collective-permute-start.17 = (bf16[2,1024,128]{2,1,0:T(8,128)(2,1)}, bf16[2,1024,128]{2,1,0:T(8,128)(2,1)}, u32[]{:S(2)}, u32[]{:S(2)}) collective-permute-start(bf16[2,1024,128]{2,1,0:T(8,128)(2,1)} %constant_dynamic-slice_fusion.9), channel_id=1, source_target_pairs={{0,8},{4,12},{8,0},{12,4},{1,9},{5,13},{9,1},{13,5},{2,10},{6,14},... | collective-permute-start | bytes 1572872 | tf_op jit(solution)/shard_map/ppermute | solution.py:360
  434.3 17.4 %collective-permute-start.21 = (bf16[64,1408]{1,0:T(8,128)(2,1)S(1)}, bf16[64,1408]{1,0:T(8,128)(2,1)S(1)}, u32[]{:S(2)}, u32[]{:S(2)}) collective-permute-start(bf16[64,1408]{1,0:T(8,128)(2,1)S(1)} %get-tuple-element.199), channel_id=1, source_target_pairs={{0,16},{16,0},{1,17},{17,1},{2,18},{18,2},{3,19},{19,3},{4,20},{20... | collective-permute-start | bytes 540680 | tf_op jit(solution)/shard_map/ppermute | solution.py:432
  452.5 57.6 %reduce-scatter.9.cloned.1.call-start = ((), (), s32[]{:S(2)}) async-start(), calls=%async_computation.7 | async-start | bytes 1310720 | tf_op jit(solution)/shard_map/reduce_scatter | solution.py:373
  464.5 25.0 %collective-permute-start.19 = (bf16[2,1024,256]{2,1,0:T(8,128)(2,1)}, bf16[2,1024,256]{2,1,0:T(8,128)(2,1)}, u32[]{:S(2)}, u32[]{:S(2)}) collective-permute-start(bf16[2,1024,256]{2,1,0:T(8,128)(2,1)} %constant_dynamic-slice_fusion.7), channel_id=1, source_target_pairs={{0,16},{16,0},{1,17},{17,1},{2,18},{18,2},{3,19},{19,3},{4,20},{20... | collective-permute-start | bytes 3145736 | tf_op jit(solution)/shard_map/ppermute | solution.py:360
  466.0 25.1 %collective-permute-start.20 = (bf16[2,1024,256]{2,1,0:T(8,128)(2,1)}, bf16[2,1024,256]{2,1,0:T(8,128)(2,1)}, u32[]{:S(2)}, u32[]{:S(2)}) collective-permute-start(bf16[2,1024,256]{2,1,0:T(8,128)(2,1)} %constant_dynamic-slice_fusion.6), channel_id=1, source_target_pairs={{0,8},{4,12},{8,0},{12,4},{1,9},{5,13},{9,1},{13,5},{2,10},{6,14},... | collective-permute-start | bytes 3145736 | tf_op jit(solution)/shard_map/ppermute | solution.py:360
  482.3 65.7 %reduce-scatter.11.cloned.1.call-start = ((), (), s32[]{:S(2)}) async-start(), calls=%async_computation.8 | async-start | bytes 1310720 | tf_op jit(solution)/shard_map/reduce_scatter | solution.py:373
  493.8 12.8 %collective-permute-start.23 = (bf16[2,1024,128]{2,1,0:T(8,128)(2,1)}, bf16[2,1024,128]{2,1,0:T(8,128)(2,1)S(1)}, u32[]{:S(2)}, u32[]{:S(2)}) collective-permute-start(bf16[2,1024,128]{2,1,0:T(8,128)(2,1)} %constant_dynamic-slice_fusion.3), channel_id=1, source_target_pairs={{0,16},{16,0},{1,17},{17,1},{2,18},{18,2},{3,19},{19,3},{4,20},{20... | collective-permute-start | bytes 1572872 | tf_op jit(solution)/shard_map/ppermute | solution.py:360
  495.5 12.4 %collective-permute-start.22 = (bf16[2,1024,128]{2,1,0:T(8,128)(2,1)}, bf16[2,1024,128]{2,1,0:T(8,128)(2,1)S(1)}, u32[]{:S(2)}, u32[]{:S(2)}) collective-permute-start(bf16[2,1024,128]{2,1,0:T(8,128)(2,1)} %constant_dynamic-slice_fusion.4), channel_id=1, source_target_pairs={{0,8},{4,12},{8,0},{12,4},{1,9},{5,13},{9,1},{13,5},{2,10},{6,14},... | collective-permute-start | bytes 1572872 | tf_op jit(solution)/shard_map/ppermute | solution.py:360
  519.8 15.0 %collective-permute-start.24 = (f32[4,1024]{1,0:T(4,128)}, f32[4,1024]{1,0:T(4,128)}, u32[]{:S(2)}, u32[]{:S(2)}) collective-permute-start(f32[4,1024]{1,0:T(4,128)} %pad_maximum_fusion.13), channel_id=1, source_target_pairs={{0,16},{16,0},{1,17},{17,1},{2,18},{18,2},{3,19},{19,3},{4,20},{20... | collective-permute-start | bytes 49160 | tf_op jit(solution)/shard_map/ppermute | solution.py:468
  521.1 92.6 %all-gather.12.cloned.1.call-start = ((), (), s32[]{:S(2)}) async-start(), calls=%async_computation.9 | async-start | bytes 2621440 | tf_op jit(solution)/shard_map/all_gather | solution.py:436
  522.1 29.2 %collective-permute-start.26 = (bf16[352,256]{1,0:T(8,128)(2,1)}, bf16[352,256]{1,0:T(8,128)(2,1)S(1)}, u32[]{:S(2)}, u32[]{:S(2)}) collective-permute-start(bf16[352,256]{1,0:T(8,128)(2,1)} %constant_dynamic-slice_fusion.1), channel_id=1, source_target_pairs={{0,8},{4,12},{8,0},{12,4},{1,9},{5,13},{9,1},{13,5},{2,10},{6,14},... | collective-permute-start | bytes 540680 | tf_op jit(solution)/shard_map/ppermute | solution.py:360
  532.2 15.9 %copy-start.67 = (bf16[4,256,128]{2,1,0:T(8,128)(2,1)S(1)}, bf16[4,256,128]{2,1,0:T(8,128)(2,1)}, u32[]{:S(2)}) copy-start(bf16[4,256,128]{2,1,0:T(8,128)(2,1)} %reduce-scatter.9.cloned.1.call-done) | copy-start | bytes 786436
  532.2 19.0 %copy-start.65 = (bf16[352,512]{1,0:T(8,128)(2,1)S(1)}, bf16[352,512]{1,0:T(8,128)(2,1)}, u32[]{:S(2)}) copy-start(bf16[352,512]{1,0:T(8,128)(2,1)} %reduce-scatter.5.cloned.1.call-done) | copy-start | bytes 1081348
  534.8 24.1 %copy-start.20 = (f32[512,1024]{1,0:T(8,128)S(1)}, f32[512,1024]{1,0:T(8,128)}, u32[]{:S(2)}) copy-start(f32[512,1024]{1,0:T(8,128)} %copy-done.19) | copy-start | bytes 6291460
  549.8 8.1 %collective-permute-start.25 = (bf16[4,256,128]{2,1,0:T(8,128)(2,1)}, bf16[4,256,128]{2,1,0:T(8,128)(2,1)S(1)}, u32[]{:S(2)}, u32[]{:S(2)}) collective-permute-start(bf16[4,256,128]{2,1,0:T(8,128)(2,1)} %get-tuple-element.197), channel_id=1, source_target_pairs={{0,16},{16,0},{1,17},{17,1},{2,18},{18,2},{3,19},{19,3},{4,20},{20... | collective-permute-start | bytes 786440 | tf_op jit(solution)/shard_map/ppermute | solution.py:483
  564.3 3.8 collective-permute-start.29
  566.1 34.5 %collective-permute-start.27 = (bf16[1024,512]{1,0:T(8,128)(2,1)}, bf16[1024,512]{1,0:T(8,128)(2,1)S(1)}, u32[]{:S(2)}, u32[]{:S(2)}) collective-permute-start(bf16[1024,512]{1,0:T(8,128)(2,1)} %get-tuple-element.177), channel_id=1, source_target_pairs={{0,16},{16,0},{1,17},{17,1},{2,18},{18,2},{3,19},{19,3},{4,20},{20... | collective-permute-start | bytes 3145736 | tf_op jit(solution)/shard_map/ppermute | solution.py:470
  567.6 46.2 %collective-permute-start.28 = (bf16[1024,512]{1,0:T(8,128)(2,1)S(1)}, bf16[1024,512]{1,0:T(8,128)(2,1)S(1)}, u32[]{:S(2)}, u32[]{:S(2)}) collective-permute-start(bf16[1024,512]{1,0:T(8,128)(2,1)S(1)} %get-tuple-element.176), channel_id=1, source_target_pairs={{0,16},{16,0},{1,17},{17,1},{2,18},{18,2},{3,19},{19,3},{4,20},{20... | collective-permute-start | bytes 3145736 | tf_op jit(solution)/shard_map/ppermute | solution.py:470
  568.2 9.9 %collective-permute-start.30 = (f32[4,1024]{1,0:T(4,128)S(1)}, f32[4,1024]{1,0:T(4,128)S(1)}, u32[]{:S(2)}, u32[]{:S(2)}) collective-permute-start(f32[4,1024]{1,0:T(4,128)S(1)} %add.439), channel_id=1, source_target_pairs={{0,8},{4,12},{8,0},{12,4},{1,9},{5,13},{9,1},{13,5},{2,10},{6,14},... | collective-permute-start | bytes 49160 | tf_op jit(solution)/shard_map/ppermute | solution.py:472
  (83 other events, 437.6 us)
Sparse Core Ops, SparseCore 0:
  11.6 121.9 all-gather.13
  136.5 59.7 all-gather.9
  300.3 31.1 reduce-scatter.4
  349.9 30.5 reduce-scatter.6
  452.7 16.5 all-gather.15
  482.5 25.1 reduce-scatter.8
  521.2 26.7 reduce-scatter.10
  559.0 21.7 all-gather.11

commit v10 on v9

--- a/solution.py
+++ b/solution.py
@@ -342,13 +342,16 @@
     residual = carried_wide + nn(c2, wo[1])
     second_scale = scale_of(residual)
     mix_in = (residual * second_scale * gains[1, 1]).astype(BF)
-    mixed = jnp.concatenate([mix_in, lax.ppermute(mix_in, "section", swap)], axis=0)
+    mix_got = lax.ppermute(mix_in, "section", swap)
+    grad_hidden = nt(cots, w_down).astype(BF)
+    mix_got, grad_hidden = together((mix_got, grad_hidden))
+    mixed = jnp.concatenate([mix_in, mix_got], axis=0)
     gate_up = nn(mixed, w_in)
     gate, up = gate_up[:, :units], gate_up[:, units:]
     sig = jax.nn.sigmoid(gate)
     hidden = (gate * sig * up).astype(BF)
 
-    grad_hidden = nt(cots, w_down)
+    grad_hidden = grad_hidden.astype(F32)
     grad_gate = grad_hidden * up * sig * (1.0 + gate * (1.0 - sig))
     grad_up = grad_hidden * gate * sig
     dgu = jnp.concatenate([grad_gate, grad_up], axis=1).astype(BF)
@@ -427,28 +430,27 @@
     half_two = jnp.concatenate([over_side(half_two[0], 2), over_section(half_two[1], 2)], axis=0)
     one_pairs = [(query_in, dq1), (key_in, dk1)], [(key_in, dv1), (c1, d_carried)]
     send_one = [to_core(pairs) for pairs in one_pairs]
-    dq1, dk1, dv1, send_one, sum_in, sum_down = together((dq1, dk1, dv1, send_one, sum_in, sum_down))
+    dq1, dk1, dv1, send_one, sum_down = together((dq1, dk1, dv1, send_one, sum_down))
+    def gathered(part):
+        return lax.all_gather(part, "group", axis=0, tiled=False)
+
+    def laid_out(parts, order):
+        return jnp.concatenate([parts[index] for index in order], axis=-1).astype(F32)
+
+    half_one = [of_chip(pairs, sent) for pairs, sent in zip(one_pairs, send_one)]
+    dq1, dk1, dv1, half_one, half_two, sum_in = together((dq1, dk1, dv1, half_one, half_two, sum_in))
+    sum_two = line_sum(half_two, 1)
     sum_in = jnp.stack([lax.dynamic_index_in_dim(sum_in, section, 0, False),
                         lax.ppermute(lax.dynamic_index_in_dim(sum_in, 1 - section, 0, False), "section", swap)])
     sum_in = jnp.where(section == 0, sum_in, sum_in[::-1])
-
-    def gathered(part):
-        return lax.all_gather(part, "group", axis=0, tiled=False)
-
-    def laid_out(parts, order):
-        return jnp.concatenate([parts[index] for index in order], axis=-1).astype(F32)
-
     sum_in = gathered(sum_in)
-    half_one = [of_chip(pairs, sent) for pairs, sent in zip(one_pairs, send_one)]
-    dq1, dk1, dv1, half_one, half_two = together((dq1, dk1, dv1, half_one, half_two))
-    sum_two = line_sum(half_two, 1)
     grad_query_in = nt(dq1, wq[0])
     grad_key_in = nt(dk1, wk[0]) + nt(dv1, wv[0])
     half_one = over_section(half_one[0], 2), over_side(half_one[1], 2)
-    grad_query_in, grad_key_in, half_one, sum_in = together((grad_query_in, grad_key_in, half_one, sum_in))
+    grad_query_in, grad_key_in, half_one = together((grad_query_in, grad_key_in, half_one))
     half_one = jnp.concatenate([over_side(half_one[0], 2), over_section(half_one[1], 2)], axis=0)
-    grad_query_in, grad_key_in, half_one, sum_two, sum_down = together(
-        (grad_query_in, grad_key_in, half_one, sum_two, sum_down)
+    grad_query_in, grad_key_in, half_one, sum_two, sum_down, sum_in = together(
+        (grad_query_in, grad_key_in, half_one, sum_two, sum_down, sum_in)
     )
     sum_down = over_side(sum_down, 1)
     sum_one = line_sum(half_one, 1)
@@ -466,17 +468,20 @@
 
     gain_grads = jnp.stack([gain_query, gain_key, gain_normed, gain_mix])
     gain_grads = gain_grads + lax.ppermute(gain_grads, "section", swap)
-    other, gain_grads, sum_one = together((other, gain_grads, sum_one))
-    got = [lax.ppermute(other[row], "section", swap) for row in range(rows)]
+    ffn_gin = jnp.concatenate(
+        [laid_out([sum_in[at, t] for at in (2 * y, 2 * y + 1) for t in range(sections)], range(4)) for y in (0, 1)],
+        axis=0,
+    )
+
+    early, gain_grads = together(([other[row] for row in range(rows - 1)], gain_grads))
+    bytes_got = [lax.ppermute(part, "section", swap) for part in early]
+    late, gain_grads, sum_one, bytes_got, ffn_gin = together(
+        (other[rows - 1], gain_grads, sum_one, bytes_got, ffn_gin)
+    )
+    bytes_got.append(lax.ppermute(late, "section", swap))
     for pairs in (core_pairs, side_pairs):
         gain_grads = gain_grads + lax.ppermute(gain_grads, "group", pairs)
     gain_grads = jnp.sum(lax.all_gather(gain_grads, "dp", axis=0, tiled=False), axis=0)
-
-    ffn_gin = jnp.concatenate(
-        [laid_out([sum_in[at, t] for at in (2 * y, 2 * y + 1) for t in range(sections)], range(4)) for y in (0, 1)],
-        axis=0,
-    )
-    bytes_got = got
 
     kept = jnp.where(section == 0, sum_one, sum_two)
     sent = jnp.where(section == 0, sum_two, sum_one)

time: 636 us -> 621 us (0.976)
  waiting for transfers between devices: 184 us -> 169 us
    ppermute x1, waiting for transfers between devices: 13.1 us -> 0.01 us  [shards(): lax.ppermute(lax.dynamic_index_in_dim(sum_in, 1 - section, 0, False), 'se...]
    ppermute x10, waiting for transfers between devices: 20.6 us -> 33.7 us  [exchanged(): lax.ppermute(other, axis, pairs).astype(F32)]
    reduce_scatter x4, waiting for transfers between devices: 12.4 us -> 0.01 us  [line_sum(): return lax.psum_scatter(values, 'dp', scatter_dimension=where, tiled=True)]
    ppermute x1, waiting for transfers between devices: 3.25 us -> 12.8 us  [shards(): mix_got = lax.ppermute(mix_other, 'section', swap)]
    ppermute x10, starting transfers between devices: 3.82 us -> 10.9 us  [exchanged(): lax.ppermute(other, axis, pairs).astype(F32)]
    ppermute x3, waiting for transfers between devices: 35.5 us -> 28.9 us  [the longest x1 14.7 us: shards(): mix_got = lax.ppermute(mix_in, 'section', swap)]
    unnamed x195 -> x175, local copies, waits for them, and re-layouts: 13.7 us -> 13.9 us
  transfers between devices with their start and end apart: 39 -> 39, of which waited for: 11 -> 12; matrix products, arithmetic and copies ran while one was open for 38% -> 39% of each run, Pallas kernels for 10% -> 10%
where the time goes in v10:
time: 621 us; the launch traced here: 616 us
  matrix products  174 us (28%)
  waiting for transfers between devices  169 us (27%)
  other arithmetic  109 us (18%)
  Pallas kernels  60.8 us (10%)
  local copies, waits for them, and re-layouts  32.6 us (5%)
  starting transfers between devices  29.2 us (5%)
  blocking collectives  26.3 us (4%)
  between operations  15.9 us (3%)
    all_gather x1, waiting for transfers between devices, shards(): lax.all_gather(matrix, ('section', 'group', 'dp'), axis=0, tiled=True)  87.2 us
    dot_general x11, matrix products, nt(): lax.dot_general(left, right, (((1,), (1,)), ((), ())), preferred_element_...  58.8 us
    dot_general x20, matrix products, tn(): lax.dot_general(left, right, (((0,), (0,)), ((), ())), preferred_element_...  53.5 us
    dot_general x10, matrix products, nn(): return jnp.dot(left, right, preferred_element_type=F32)  52.8 us
    pallas_call x2, Pallas kernels, attend_back(): pl.pallas_call(functools.partial(attend_back_kernel, chunk, spans), grid_...  39.8 us
    ppermute x10, waiting for transfers between devices, exchanged(): lax.ppermute(other, axis, pairs).astype(F32)  33.7 us
    pallas_call x2, Pallas kernels, attend(): pl.pallas_call(functools.partial(attend_kernel, chunk, spans), grid_spec=...  20.9 us
    ppermute x1, waiting for transfers between devices, shards(): mix_got = lax.ppermute(mix_in, 'section', swap)  14.7 us
  transfers between devices with their start and end apart: 39, of which 12 were waited for; matrix products, arithmetic and copies ran while one was open for 39% of the time, Pallas kernels for 10%

profile of v10, /device:TPU:0, one launch (start us, length us, event | category | flops | bytes accessed | tf_op | source)
XLA Modules:
  0.0 616.3 jit_solution(11852567076641010652)
XLA Ops:
  22.2 3.9 multiply_reduce_fusion.5
  26.1 3.8 fusion.2
  32.6 4.7 all_gather.31
  37.4 4.2 fusion.4
  46.4 87.2 %all-gather.14.cloned.1.call-done = bf16[1,8192,1024]{2,1,0:T(8,128)(2,1)} async-done(((bf16[1,256,1024]{2,1,0:T(8,128)(2,1)}), bf16[1,8192,1024]{2,1,0:T(8,128)(2,1)}) %all-gather.14.cloned.1.call-update) | async-done | bytes 16777232 | tf_op jit(solution)/shard_map/all_gather | solution.py:264
  133.6 9.5 %convolution_convert_fusion.2.v_ref = bf16[2048,1024]{1,0:T(8,128)(2,1)} fusion(bf16[2048,1024]{1,0:T(8,128)(2,1)} %bitcast.278, bf16[2,4,1024,1024]{3,2,1,0:T(8,128)(2,1)} %bitcast.343), kind=kOutput, calls=%fused_computation.57 | convolution fusion | flops 4297064448 | bytes 10485760 | tf_op jit(solution)/shard_map/dot_general | solution.py:31
  147.7 8.0 %convolution_convert_fusion.3.k_ref = bf16[2048,1024]{1,0:T(8,128)(2,1)} fusion(bf16[2048,1024]{1,0:T(8,128)(2,1)S(1)} %bitcast.279, bf16[2,4,1024,1024]{3,2,1,0:T(8,128)(2,1)} %bitcast.345), kind=kOutput, calls=%fused_computation.58 | convolution fusion | flops 4297064448 | bytes 10485760 | tf_op jit(solution)/shard_map/dot_general | solution.py:31
  155.6 16.8 %attend.2 = (bf16[512,1024]{1,0:T(8,128)(2,1)S(1)}, f32[2,8,2,256]{3,2,1,0:T(2,128)S(1)}) custom-call(s32[2,2]{1,0:T(2,128)S(1)} %get-tuple-element.240.first_ref, s32[2,2]{1,0:T(2,128)S(1)} %get-tuple-element.225.stop_ref, s32[2,1,256]{2,1,0:T(1,128)S(1)} %broadcast_in_dim.73.lo_ref, s32[2,1,256]{2,1,0:T(1,128)S(1)} %bitcast.270, ...), custom_call_target="tpu_custom_call" | custom-call | flops 8589934592 | bytes 18874368 | tf_op jit(solution)/shard_map/attend/pallas_call | solution.py:186
  172.5 3.4 fusion.30
  179.2 3.3 fusion.84.k_ref
  182.6 3.3 fusion.85.q_ref
  186.0 4.1 attend.3
  191.5 3.3 multiply_reduce_fusion.4
  200.3 5.8 convolution_convert_fusion.1
  206.1 14.7 %collective-permute-done.4 = bf16[512,1024]{1,0:T(8,128)(2,1)} collective-permute-done((bf16[512,1024]{1,0:T(8,128)(2,1)S(1)}, bf16[512,1024]{1,0:T(8,128)(2,1)}, u32[]{:S(2)}, u32[]{:S(2)}) %collective-permute-start.4) | collective-permute-done | bytes 1048608 | tf_op jit(solution)/shard_map/ppermute | solution.py:345
  220.8 9.5 %fusion.117 = f32[1024,2816]{1,0:T(8,128)S(1)} fusion(bf16[1024,2816]{1,0:T(8,128)(2,1)} %bitcast.359, bf16[512,1024]{1,0:T(8,128)(2,1)} %collective-permute-done.4, bf16[512,1024]{1,0:T(8,128)(2,1)} %copy-done.59), kind=kOutput, calls=%fused_computation.209 | convolution fusion | flops 5909774336 | bytes 19398656 | tf_op jit(solution)/shard_map/dot_general | solution.py:31
  230.4 3.5 fusion.16
  233.9 9.8 %fusion.88 = bf16[512,1024]{1,0:T(8,128)(2,1)} fusion(bf16[1024,2816]{1,0:T(8,128)(2,1)} %bitcast.360, bf16[1024,1408]{1,0:T(8,128)(2,1)S(1)} %get-tuple-element.168, bf16[1024,1408]{1,0:T(8,128)(2,1)S(1)} %get-tuple-element.167), kind=kOutput, calls=%fused_computation.173 | convolution fusion | flops 2959081472 | bytes 12582912 | tf_op jit(solution)/shard_map/dot_general | solution.py:39
  245.6 6.7 %convolution_convert_fusion = bf16[1024,1408]{1,0:T(8,128)(2,1)} fusion(s32[]{:T(128)S(6)} %select_n.315, bf16[1024,1408]{1,0:T(8,128)(2,1)S(1)} %get-tuple-element.168, bf16[1024,1408]{1,0:T(8,128)(2,1)S(1)} %get-tuple-element.167, bf16[512,1024]{1,0:T(8,128)(2,1)} %collective-permute-done.4, bf16[512,1024]{1,0:T(8,128)(2,1)S(1)} %copy-done.60), kind=kOutput, calls=%fused_computation.55 | convolution fusion | flops 2964193280 | bytes 10747908 | tf_op jit(solution)/shard_map/dot_general | solution.py:35
  255.6 6.1 fusion.183
  266.5 4.2 add_convert_fusion.2
  270.7 7.1 %add_convert_fusion = bf16[1024,1408]{1,0:T(8,128)(2,1)S(1)} fusion(bf16[1024,1408]{1,0:T(8,128)(2,1)} %collective-permute-done.8, s32[]{:T(128)S(6)} %select_n.318, bf16[1024,1408]{1,0:T(8,128)(2,1)} %copy-done.27, bf16[1024,1408]{1,0:T(8,128)(2,1)} %copy-done.26, bf16[512,1024]{1,0:T(8,128)(2,1)} %collective-permute-done.4, bf16[512,1024]{1,0:T(8,128)(2,1)} %copy-done.59), kind=kOutput, calls=%fused_computation.35 | convolution fusion | flops 2967076864 | bytes 13631492 | tf_op jit(solution)/shard_map/dot_general | solution.py:35
  277.8 12.8 %collective-permute-done.7 = bf16[512,1024]{1,0:T(8,128)(2,1)} collective-permute-done((bf16[512,1024]{1,0:T(8,128)(2,1)}, bf16[512,1024]{1,0:T(8,128)(2,1)}, u32[]{:S(2)}, u32[]{:S(2)}) %collective-permute-start.7) | collective-permute-done | bytes 1048608 | tf_op jit(solution)/shard_map/ppermute | solution.py:393
  290.6 7.7 %multiply_reduce_fusion = (f32[1024]{0:T(1024)S(1)}, f32[512]{0:T(512)S(1)}, f32[512,1024]{1,0:T(8,128)}) fusion(f32[512,1024]{1,0:T(8,128)S(1)} %get-tuple-element.237, f32[512]{0:T(512)S(1)} %get-tuple-element.221, bf16[512,1024]{1,0:T(8,128)(2,1)} %collective-permute-done.7, f32[1024]{0:T(1024)S(1)} %bitcast.314, bf16[512,2816]{1,0:T(8,128)(2,1)S(1)} %copy-done.40, ...), kind=kOutput, calls=%fused_computation.106 | convolution fusion | flops 2956982784 | bytes 13905920 | tf_op jit(solution)/shard_map/dot_general | solution.py:39
  301.1 4.0 fusion.175
  305.1 4.3 fusion.82.dc_ref
  309.4 11.5 %attend_back.2 = (bf16[512,1024]{1,0:T(8,128)(2,1)S(1)}, bf16[512,1024]{1,0:T(8,128)(2,1)S(1)}, bf16[512,1024]{1,0:T(8,128)(2,1)S(1)}) custom-call(s32[2,2]{1,0:T(2,128)S(1)} %get-tuple-element.243.first_ref, s32[2,2]{1,0:T(2,128)S(1)} %get-tuple-element.242.stop_ref, s32[2,1,256]{2,1,0:T(1,128)S(1)} %broadcast_in_dim.83.lo_ref, ...), custom_call_target="tpu_custom_call" | custom-call | flops 5368709120 | bytes 6291456 | tf_op jit(solution)/shard_map/attend_back/pallas_call | solution.py:210
  327.6 5.4 collective-permute-done.10
  335.8 4.3 fusion.6
  355.2 3.6 fusion.39
  374.5 28.3 %attend_back.3 = (bf16[512,1024]{1,0:T(8,128)(2,1)S(1)}, bf16[2048,1024]{1,0:T(8,128)(2,1)}, bf16[2048,1024]{1,0:T(8,128)(2,1)}) custom-call(s32[2,2]{1,0:T(2,128)S(1)} %get-tuple-element.241.first_ref, s32[2,2]{1,0:T(2,128)S(1)} %get-tuple-element.224.stop_ref, s32[2,1,256]{2,1,0:T(1,128)S(1)} %broadcast_in_dim.73.lo_ref, s32[2,1,256]{2,1,0:T(1,128)S(1)} %bitcast.271, ...), custom_call_target="tpu_custom_call" | custom-call | flops 21474836480 | bytes 18874368 | tf_op jit(solution)/shard_map/attend_back/pallas_call | solution.py:210
  402.9 4.1 fusion.91
  419.2 3.7 fusion.73
  425.1 3.8 fusion.70
  431.1 6.1 collective-permute-done.17
  441.0 3.7 fusion.18
  445.1 4.0 fusion.17
  455.6 7.2 %fusion.55 = f32[2048,1024]{1,0:T(8,128)S(1)} fusion(bf16[2048,1024]{1,0:T(8,128)(2,1)} %get-tuple-element.123, bf16[2,4,1024,1024]{3,2,1,0:T(8,128)(2,1)} %bitcast.356), kind=kOutput, calls=%fused_computation.138 | convolution fusion | flops 4294967296 | bytes 14680064 | tf_op jit(solution)/shard_map/dot_general | solution.py:39
  462.8 8.6 %convolution_add_fusion = f32[2048,1024]{1,0:T(8,128)} fusion(f32[2048,1024]{1,0:T(8,128)S(1)} %fusion.55, bf16[2048,1024]{1,0:T(8,128)(2,1)S(1)} %copy-done.62, bf16[2,4,1024,1024]{3,2,1,0:T(8,128)(2,1)} %bitcast.357), kind=kOutput, calls=%fused_computation.54 | convolution fusion | flops 4297064448 | bytes 23068672 | tf_op jit(solution)/shard_map/dot_general | solution.py:39
  486.6 17.1 %collective-permute-done.21 = bf16[2,1024,128]{2,1,0:T(8,128)(2,1)} collective-permute-done((bf16[2,1024,128]{2,1,0:T(8,128)(2,1)}, bf16[2,1024,128]{2,1,0:T(8,128)(2,1)}, u32[]{:S(2)}, u32[]{:S(2)}) %collective-permute-start.21) | collective-permute-done | bytes 524320 | tf_op jit(solution)/shard_map/ppermute | solution.py:363
  509.3 6.1 fusion.11
  518.2 4.6 fusion.66
  522.8 8.6 %fusion.1 = bf16[2048,1024]{1,0:T(8,128)(2,1)S(1)} fusion(f32[2,1024,1024]{2,1,0:T(8,128)} %fusion.66, f32[2048,1024]{1,0:T(8,128)} %convolution_add_fusion, f32[2048]{0:T(1024)S(1)} %broadcast_multiply_fusion, f32[2048]{0:T(1024)S(1)} %multiply_multiply_fusion, f32[1024]{0:T(1024)S(1)} %bitcast.307, f32[2048]{0:T(1024)S(1)} %bitcast.303, ...), kind=kLoop, calls=%fused_computation.3 | loop fusion | flops 16777216 | bytes 25194500 | tf_op jit(solution)/shard_map/convert_element_type | solution.py:464
  534.7 8.4 %maximum_convert_fusion = f32[128,5632]{1,0:T(8,128)} fusion(bf16[64,1408]{1,0:T(8,128)(2,1)S(1)} %get-tuple-element.191, bf16[64,1408]{1,0:T(8,128)(2,1)S(1)} %get-tuple-element.192, bf16[64,1408]{1,0:T(8,128)(2,1)S(1)} %get-tuple-element.193, bf16[64,1408]{1,0:T(8,128)(2,1)S(1)} %get-tuple-element.194, bf16[64,1408]{1,0:T(8,128)(2,1)S(1)} %get-tuple-element.195, ...), kind=kLoop, calls=%fused_computation.175 | loop fusion | flops 11534336 | bytes 4325376 | tf_op jit(solution)/shard_map/concatenate | solution.py:471
  543.1 14.2 %collective-permute-done.25 = bf16[1024,512]{1,0:T(8,128)(2,1)} collective-permute-done((bf16[1024,512]{1,0:T(8,128)(2,1)S(1)}, bf16[1024,512]{1,0:T(8,128)(2,1)}, u32[]{:S(2)}, u32[]{:S(2)}) %collective-permute-start.25) | collective-permute-done | bytes 1048608 | tf_op jit(solution)/shard_map/ppermute | solution.py:477
  560.3 4.4 collective-permute-done.26
  575.3 13.7 %all-gather.4 = f32[4,4,1024]{2,1,0:T(4,128)S(1)} all-gather(f32[1,4,1024]{2,1,0:T(4,128)S(1)} %add_bitcast_fusion), channel_id=4, replica_groups=mesh['section'=2,'group'=4,'dp'=4] {'dp'}, dimensions={0}, use_global_device_ids=true | all-gather | bytes 81920 | tf_op jit(solution)/shard_map/all_gather | solution.py:484
  589.7 7.9 %all-gather.3 = bf16[1408,256]{1,0:T(8,128)(2,1)S(1)} all-gather(bf16[352,256]{1,0:T(8,128)(2,1)S(1)} %add_convert_fusion.12), channel_id=5, replica_groups=mesh['section'=2,'group'=4,'dp'=4] {'group'}, dimensions={0}, use_global_device_ids=true | all-gather | bytes 901120 | tf_op jit(solution)/shard_map/all_gather | solution.py:435
  (385 shorter events, 169.6 us)
Async XLA Ops:
  7.2 18.9 %copy-start = (s32[4,256]{1,0:T(4,128)S(1)}, s32[4,256]{1,0:T(4,128)}, u32[]{:S(2)}) copy-start(s32[4,256]{1,0:T(4,128)} %param.11) | copy-start | bytes 12292
  7.2 126.4 %all-gather.14.cloned.1.call-start = ((), (), s32[]{:S(2)}) async-start(), calls=%async_computation.10 | async-start | bytes 17301504 | tf_op jit(solution)/shard_map/all_gather | solution.py:264
  9.3 211.5 %all-gather.10.cloned.1.call-start = ((), (), s32[]{:S(2)}) async-start(), calls=%async_computation.4 | async-start | bytes 6127616 | tf_op jit(solution)/shard_map/all_gather | solution.py:287
  10.4 34.1 %collective-permute-start = (bf16[88,1024]{1,0:T(8,128)(2,1)S(1)}, bf16[88,1024]{1,0:T(8,128)(2,1)}, u32[]{:S(2)}, u32[]{:S(2)}) collective-permute-start(bf16[88,1024]{1,0:T(8,128)(2,1)S(1)} %get-tuple-element.164), channel_id=1, source_target_pairs={{0,1},{1,2},{2,3},{3,0},{4,5},{5,6},{6,7},{7,4},{8,9},{9,10},{10,1... | collective-permute-start | bytes 540680 | tf_op jit(solution)/shard_map/ppermute | solution.py:293
  13.5 31.9 %collective-permute-start.1 = (bf16[88,1024]{1,0:T(8,128)(2,1)S(1)}, bf16[88,1024]{1,0:T(8,128)(2,1)}, u32[]{:S(2)}, u32[]{:S(2)}) collective-permute-start(bf16[88,1024]{1,0:T(8,128)(2,1)S(1)} %get-tuple-element.164), channel_id=1, source_target_pairs={{0,2},{1,3},{2,0},{3,1},{4,6},{5,7},{6,4},{7,5},{8,10},{9,11},{10,... | collective-permute-start | bytes 540680 | tf_op jit(solution)/shard_map/ppermute | solution.py:293
  16.1 30.3 %collective-permute-start.2 = (bf16[88,1024]{1,0:T(8,128)(2,1)S(1)}, bf16[88,1024]{1,0:T(8,128)(2,1)S(1)}, u32[]{:S(2)}, u32[]{:S(2)}) collective-permute-start(bf16[88,1024]{1,0:T(8,128)(2,1)S(1)} %get-tuple-element.164), channel_id=1, source_target_pairs={{0,3},{1,0},{2,1},{3,2},{4,7},{5,4},{6,5},{7,6},{8,11},{9,8},{10,9... | collective-permute-start | bytes 540680 | tf_op jit(solution)/shard_map/ppermute | solution.py:293
  19.4 10.6 %collective-permute-start.6 = (bf16[32,2816]{1,0:T(8,128)(2,1)}, bf16[32,2816]{1,0:T(8,128)(2,1)}, u32[]{:S(2)}, u32[]{:S(2)}) collective-permute-start(bf16[32,2816]{1,0:T(8,128)(2,1)} %pad_maximum_fusion.12), channel_id=1, source_target_pairs={{0,16},{16,0},{1,17},{17,1},{2,18},{18,2},{3,19},{19,3},{4,20},{20... | collective-permute-start | bytes 540680 | tf_op jit(solution)/shard_map/ppermute | solution.py:285
  26.1 17.1 %copy-start.17 = (f32[2,256,1024]{2,1,0:T(8,128)}, f32[2,256,1024]{2,1,0:T(8,128)S(1)}, u32[]{:S(2)}) copy-start(f32[2,256,1024]{2,1,0:T(8,128)S(1)} %get-tuple-element.233) | copy-start | bytes 6291460
  31.8 304.0 %reduce-scatter.5.cloned.1.call-start = ((), (), s32[]{:S(2)}) async-start(), calls=%async_computation.5 | async-start | bytes 1802240 | tf_op jit(solution)/shard_map/reduce_scatter | solution.py:376
  37.3 218.3 %copy-start.72 = (f32[1,8,2,128]{3,2,1,0:T(2,128)}, f32[1,8,2,128]{3,2,1,0:T(2,128)S(1)}, u32[]{:S(2)}) copy-start(f32[1,8,2,128]{3,2,1,0:T(2,128)S(1)} %get-tuple-element.214) | copy-start | bytes 24580
  143.2 46.9 %collective-permute-start.3 = (bf16[4,88,1024]{2,1,0:T(8,128)(2,1)S(1)}, bf16[4,88,1024]{2,1,0:T(8,128)(2,1)S(1)}, u32[]{:S(2)}, u32[]{:S(2)}) collective-permute-start(bf16[4,88,1024]{2,1,0:T(8,128)(2,1)S(1)} %bitcast_dynamic-update-slice_fusion), channel_id=1, source_target_pairs={{0,8},{4,12},{8,0},{12,4},{1,9},{5,13},{9,1},{13,5},{2,10},{6,14},... | collective-permute-start | bytes 2162696 | tf_op jit(solution)/shard_map/ppermute | solution.py:276
  191.5 5.5 collective-permute-start.5
  195.1 25.7 %collective-permute-start.4 = (bf16[512,1024]{1,0:T(8,128)(2,1)S(1)}, bf16[512,1024]{1,0:T(8,128)(2,1)}, u32[]{:S(2)}, u32[]{:S(2)}) collective-permute-start(bf16[512,1024]{1,0:T(8,128)(2,1)S(1)} %multiply_convert_fusion.2), channel_id=1, source_target_pairs={{0,16},{16,0},{1,17},{17,1},{2,18},{18,2},{3,19},{19,3},{4,20},{20... | collective-permute-start | bytes 3145736 | tf_op jit(solution)/shard_map/ppermute | solution.py:345
  233.8 18.4 %copy-start.44 = (bf16[1024,1408]{1,0:T(8,128)(2,1)}, bf16[1024,1408]{1,0:T(8,128)(2,1)S(1)}, u32[]{:S(2)}) copy-start(bf16[1024,1408]{1,0:T(8,128)(2,1)S(1)} %get-tuple-element.169) | copy-start | bytes 8650756
  255.1 15.6 %collective-permute-start.8 = (bf16[1024,1408]{1,0:T(8,128)(2,1)}, bf16[1024,1408]{1,0:T(8,128)(2,1)}, u32[]{:S(2)}, u32[]{:S(2)}) collective-permute-start(bf16[1024,1408]{1,0:T(8,128)(2,1)} %convolution_convert_fusion), channel_id=1, source_target_pairs={{0,4},{4,0},{8,12},{12,8},{1,5},{5,1},{9,13},{13,9},{2,6},{6,2},{1... | collective-permute-start | bytes 8650760 | tf_op jit(solution)/shard_map/ppermute | solution.py:386
  255.1 10.3 %collective-permute-start.9 = (bf16[1408,512]{1,0:T(8,128)(2,1)}, bf16[1408,512]{1,0:T(8,128)(2,1)}, u32[]{:S(2)}, u32[]{:S(2)}) collective-permute-start(bf16[1408,512]{1,0:T(8,128)(2,1)} %convolution_convert_fusion.4), channel_id=1, source_target_pairs={{0,4},{4,0},{8,12},{12,8},{1,5},{5,1},{9,13},{13,9},{2,6},{6,2},{1... | collective-permute-start | bytes 4325384 | tf_op jit(solution)/shard_map/ppermute | solution.py:386
  265.2 25.4 %collective-permute-start.7 = (bf16[512,1024]{1,0:T(8,128)(2,1)}, bf16[512,1024]{1,0:T(8,128)(2,1)}, u32[]{:S(2)}, u32[]{:S(2)}) collective-permute-start(bf16[512,1024]{1,0:T(8,128)(2,1)} %fusion.88), channel_id=1, source_target_pairs={{0,16},{16,0},{1,17},{17,1},{2,18},{18,2},{3,19},{19,3},{4,20},{20... | collective-permute-start | bytes 3145736 | tf_op jit(solution)/shard_map/ppermute | solution.py:393
  270.7 19.9 %copy-start.40 = (bf16[512,2816]{1,0:T(8,128)(2,1)S(1)}, bf16[512,2816]{1,0:T(8,128)(2,1)}, u32[]{:S(2)}) copy-start(bf16[512,2816]{1,0:T(8,128)(2,1)} %fusion.24) | copy-start | bytes 8650756
  277.8 20.5 %copy-start.42 = (bf16[1024,1408]{1,0:T(8,128)(2,1)}, bf16[1024,1408]{1,0:T(8,128)(2,1)S(1)}, u32[]{:S(2)}) copy-start(bf16[1024,1408]{1,0:T(8,128)(2,1)S(1)} %add_convert_fusion) | copy-start | bytes 8650756
  299.5 33.5 %collective-permute-start.10 = (bf16[2,4,1,64,1408]{4,3,2,1,0:T(8,128)(2,1)}, bf16[2,4,1,64,1408]{4,3,2,1,0:T(8,128)(2,1)}, u32[]{:S(2)}, u32[]{:S(2)}) collective-permute-start(bf16[2,4,1,64,1408]{4,3,2,1,0:T(8,128)(2,1)} %constant_dynamic-slice_fusion.11), channel_id=1, source_target_pairs={{0,8},{4,12},{8,0},{12,4},{1,9},{5,13},{9,1},{13,5},{2,10},{6,14},... | collective-permute-start | bytes 4325384 | tf_op jit(solution)/shard_map/ppermute | solution.py:363
  301.0 148.1 %reduce-scatter.7.cloned.1.call-start = ((), (), s32[]{:S(2)}) async-start(), calls=%async_computation.6 | async-start | bytes 1802240 | tf_op jit(solution)/shard_map/reduce_scatter | solution.py:376
  335.8 31.1 %collective-permute-start.11 = (bf16[4,1024,512]{2,1,0:T(8,128)(2,1)}, bf16[4,1024,512]{2,1,0:T(8,128)(2,1)}, u32[]{:S(2)}, u32[]{:S(2)}) collective-permute-start(bf16[4,1024,512]{2,1,0:T(8,128)(2,1)} %pad_maximum_fusion), channel_id=1, source_target_pairs={{0,4},{4,0},{8,12},{12,8},{1,5},{5,1},{9,13},{13,9},{2,6},{6,2},{1... | collective-permute-start | bytes 12582920 | tf_op jit(solution)/shard_map/ppermute | solution.py:386
  340.1 31.1 %collective-permute-start.12 = (bf16[1024,512]{1,0:T(8,128)(2,1)}, bf16[1024,512]{1,0:T(8,128)(2,1)}, u32[]{:S(2)}, u32[]{:S(2)}) collective-permute-start(bf16[1024,512]{1,0:T(8,128)(2,1)} %fusion.41), channel_id=1, source_target_pairs={{0,16},{16,0},{1,17},{17,1},{2,18},{18,2},{3,19},{19,3},{4,20},{20... | collective-permute-start | bytes 3145736 | tf_op jit(solution)/shard_map/ppermute | solution.py:401
  349.1 158.2 %reduce-scatter.9.cloned.1.call-start = ((), (), s32[]{:S(2)}) async-start(), calls=%async_computation.7 | async-start | bytes 1310720 | tf_op jit(solution)/shard_map/reduce_scatter | solution.py:376
  371.6 40.7 %collective-permute-start.14 = (bf16[2,1024,256]{2,1,0:T(8,128)(2,1)S(1)}, bf16[2,1024,256]{2,1,0:T(8,128)(2,1)}, u32[]{:S(2)}, u32[]{:S(2)}) collective-permute-start(bf16[2,1024,256]{2,1,0:T(8,128)(2,1)S(1)} %constant_dynamic-slice_fusion.9), channel_id=1, source_target_pairs={{0,8},{4,12},{8,0},{12,4},{1,9},{5,13},{9,1},{13,5},{2,10},{6,14},... | collective-permute-start | bytes 3145736 | tf_op jit(solution)/shard_map/ppermute | solution.py:363
  373.2 40.6 %collective-permute-start.13 = (bf16[2,1024,256]{2,1,0:T(8,128)(2,1)S(1)}, bf16[2,1024,256]{2,1,0:T(8,128)(2,1)S(1)}, u32[]{:S(2)}, u32[]{:S(2)}) collective-permute-start(bf16[2,1024,256]{2,1,0:T(8,128)(2,1)S(1)} %constant_dynamic-slice_fusion.10), channel_id=1, source_target_pairs={{0,16},{16,0},{1,17},{17,1},{2,18},{18,2},{3,19},{19,3},{4,20},{20... | collective-permute-start | bytes 3145736 | tf_op jit(solution)/shard_map/ppermute | solution.py:363
  374.5 28.3 %copy-start.16 = (bf16[2048,1024]{1,0:T(8,128)(2,1)S(1)}, bf16[2048,1024]{1,0:T(8,128)(2,1)}, u32[]{:S(2)}) copy-start(bf16[2048,1024]{1,0:T(8,128)(2,1)} %fusion.6) | copy-start | bytes 12582916
  417.7 23.3 %collective-permute-start.16 = (bf16[2,1024,512]{2,1,0:T(8,128)(2,1)}, bf16[2,1024,512]{2,1,0:T(8,128)(2,1)}, u32[]{:S(2)}, u32[]{:S(2)}) collective-permute-start(bf16[2,1024,512]{2,1,0:T(8,128)(2,1)} %pad_maximum_fusion.5), channel_id=1, source_target_pairs={{0,4},{4,0},{8,12},{12,8},{1,5},{5,1},{9,13},{13,9},{2,6},{6,2},{1... | collective-permute-start | bytes 6291464 | tf_op jit(solution)/shard_map/ppermute | solution.py:386
  417.7 27.1 %collective-permute-start.15 = (bf16[2,1024,512]{2,1,0:T(8,128)(2,1)}, bf16[2,1024,512]{2,1,0:T(8,128)(2,1)}, u32[]{:S(2)}, u32[]{:S(2)}) collective-permute-start(bf16[2,1024,512]{2,1,0:T(8,128)(2,1)} %pad_maximum_fusion.4), channel_id=1, source_target_pairs={{0,4},{4,0},{8,12},{12,8},{1,5},{5,1},{9,13},{13,9},{2,6},{6,2},{1... | collective-permute-start | bytes 6291464 | tf_op jit(solution)/shard_map/ppermute | solution.py:386
  422.9 14.2 %collective-permute-start.17 = (bf16[2,1024,128]{2,1,0:T(8,128)(2,1)S(1)}, bf16[2,1024,128]{2,1,0:T(8,128)(2,1)S(1)}, u32[]{:S(2)}, u32[]{:S(2)}) collective-permute-start(bf16[2,1024,128]{2,1,0:T(8,128)(2,1)S(1)} %constant_dynamic-slice_fusion.8), channel_id=1, source_target_pairs={{0,8},{4,12},{8,0},{12,4},{1,9},{5,13},{9,1},{13,5},{2,10},{6,14},... | collective-permute-start | bytes 1572872 | tf_op jit(solution)/shard_map/ppermute | solution.py:363
  425.1 14.7 %collective-permute-start.18 = (bf16[2,1024,128]{2,1,0:T(8,128)(2,1)S(1)}, bf16[2,1024,128]{2,1,0:T(8,128)(2,1)S(1)}, u32[]{:S(2)}, u32[]{:S(2)}) collective-permute-start(bf16[2,1024,128]{2,1,0:T(8,128)(2,1)S(1)} %constant_dynamic-slice_fusion.7), channel_id=1, source_target_pairs={{0,16},{16,0},{1,17},{17,1},{2,18},{18,2},{3,19},{19,3},{4,20},{20... | collective-permute-start | bytes 1572872 | tf_op jit(solution)/shard_map/ppermute | solution.py:363
  451.0 20.3 %collective-permute-start.23 = (bf16[64,1408]{1,0:T(8,128)(2,1)}, bf16[64,1408]{1,0:T(8,128)(2,1)}, u32[]{:S(2)}, u32[]{:S(2)}) collective-permute-start(bf16[64,1408]{1,0:T(8,128)(2,1)} %get-tuple-element.209), channel_id=1, source_target_pairs={{0,16},{16,0},{1,17},{17,1},{2,18},{18,2},{3,19},{19,3},{4,20},{20... | collective-permute-start | bytes 540680 | tf_op jit(solution)/shard_map/ppermute | solution.py:444
  452.4 25.5 %collective-permute-start.20 = (bf16[2,1024,256]{2,1,0:T(8,128)(2,1)}, bf16[2,1024,256]{2,1,0:T(8,128)(2,1)}, u32[]{:S(2)}, u32[]{:S(2)}) collective-permute-start(bf16[2,1024,256]{2,1,0:T(8,128)(2,1)} %constant_dynamic-slice_fusion.5), channel_id=1, source_target_pairs={{0,8},{4,12},{8,0},{12,4},{1,9},{5,13},{9,1},{13,5},{2,10},{6,14},... | collective-permute-start | bytes 3145736 | tf_op jit(solution)/shard_map/ppermute | solution.py:363
  453.5 26.9 %collective-permute-start.19 = (bf16[2,1024,256]{2,1,0:T(8,128)(2,1)}, bf16[2,1024,256]{2,1,0:T(8,128)(2,1)}, u32[]{:S(2)}, u32[]{:S(2)}) collective-permute-start(bf16[2,1024,256]{2,1,0:T(8,128)(2,1)} %constant_dynamic-slice_fusion.6), channel_id=1, source_target_pairs={{0,16},{16,0},{1,17},{17,1},{2,18},{18,2},{3,19},{19,3},{4,20},{20... | collective-permute-start | bytes 3145736 | tf_op jit(solution)/shard_map/ppermute | solution.py:363
  455.5 51.8 %all-gather.16.cloned.1.call-start = ((), (), s32[]{:S(2)}) async-start(), calls=%async_computation.11 | async-start | bytes 1802240 | tf_op jit(solution)/shard_map/all_gather | solution.py:435
  473.1 84.2 %reduce-scatter.11.cloned.1.call-start = ((), (), s32[]{:S(2)}) async-start(), calls=%async_computation.8 | async-start | bytes 1310720 | tf_op jit(solution)/shard_map/reduce_scatter | solution.py:376
  483.7 20.0 %collective-permute-start.21 = (bf16[2,1024,128]{2,1,0:T(8,128)(2,1)}, bf16[2,1024,128]{2,1,0:T(8,128)(2,1)}, u32[]{:S(2)}, u32[]{:S(2)}) collective-permute-start(bf16[2,1024,128]{2,1,0:T(8,128)(2,1)} %constant_dynamic-slice_fusion.4), channel_id=1, source_target_pairs={{0,8},{4,12},{8,0},{12,4},{1,9},{5,13},{9,1},{13,5},{2,10},{6,14},... | collective-permute-start | bytes 1572872 | tf_op jit(solution)/shard_map/ppermute | solution.py:363
  484.9 20.2 %collective-permute-start.22 = (bf16[2,1024,128]{2,1,0:T(8,128)(2,1)}, bf16[2,1024,128]{2,1,0:T(8,128)(2,1)}, u32[]{:S(2)}, u32[]{:S(2)}) collective-permute-start(bf16[2,1024,128]{2,1,0:T(8,128)(2,1)} %constant_dynamic-slice_fusion.3), channel_id=1, source_target_pairs={{0,16},{16,0},{1,17},{17,1},{2,18},{18,2},{3,19},{19,3},{4,20},{20... | collective-permute-start | bytes 1572872 | tf_op jit(solution)/shard_map/ppermute | solution.py:363
  508.9 50.3 %collective-permute-start.27 = (bf16[352,256]{1,0:T(8,128)(2,1)}, bf16[352,256]{1,0:T(8,128)(2,1)}, u32[]{:S(2)}, u32[]{:S(2)}) collective-permute-start(bf16[352,256]{1,0:T(8,128)(2,1)} %constant_dynamic-slice_fusion.1), channel_id=1, source_target_pairs={{0,8},{4,12},{8,0},{12,4},{1,9},{5,13},{9,1},{13,5},{2,10},{6,14},... | collective-permute-start | bytes 540680 | tf_op jit(solution)/shard_map/ppermute | solution.py:363
  516.3 17.2 %collective-permute-start.24 = (f32[4,1024]{1,0:T(4,128)S(1)}, f32[4,1024]{1,0:T(4,128)S(1)}, u32[]{:S(2)}, u32[]{:S(2)}) collective-permute-start(f32[4,1024]{1,0:T(4,128)S(1)} %pad_maximum_fusion.13), channel_id=1, source_target_pairs={{0,16},{16,0},{1,17},{17,1},{2,18},{18,2},{3,19},{19,3},{4,20},{20... | collective-permute-start | bytes 49160 | tf_op jit(solution)/shard_map/ppermute | solution.py:470
  522.8 76.2 %all-gather.12.cloned.1.call-start = ((), (), s32[]{:S(2)}) async-start(), calls=%async_computation.9 | async-start | bytes 2621440 | tf_op jit(solution)/shard_map/all_gather | solution.py:435
  533.5 23.8 %collective-permute-start.25 = (bf16[1024,512]{1,0:T(8,128)(2,1)S(1)}, bf16[1024,512]{1,0:T(8,128)(2,1)}, u32[]{:S(2)}, u32[]{:S(2)}) collective-permute-start(bf16[1024,512]{1,0:T(8,128)(2,1)S(1)} %get-tuple-element.137), channel_id=1, source_target_pairs={{0,16},{16,0},{1,17},{17,1},{2,18},{18,2},{3,19},{19,3},{4,20},{20... | collective-permute-start | bytes 3145736 | tf_op jit(solution)/shard_map/ppermute | solution.py:477
  534.7 22.6 %copy-start.69 = (bf16[4,256,128]{2,1,0:T(8,128)(2,1)S(1)}, bf16[4,256,128]{2,1,0:T(8,128)(2,1)}, u32[]{:S(2)}) copy-start(bf16[4,256,128]{2,1,0:T(8,128)(2,1)} %reduce-scatter.9.cloned.1.call-done) | copy-start | bytes 786436
  543.1 22.6 %copy-start.20 = (f32[512,1024]{1,0:T(8,128)S(1)}, f32[512,1024]{1,0:T(8,128)}, u32[]{:S(2)}) copy-start(f32[512,1024]{1,0:T(8,128)} %copy-done.19) | copy-start | bytes 6291460
  558.3 6.4 %collective-permute-start.26 = (bf16[4,256,128]{2,1,0:T(8,128)(2,1)S(1)}, bf16[4,256,128]{2,1,0:T(8,128)(2,1)S(1)}, u32[]{:S(2)}, u32[]{:S(2)}) collective-permute-start(bf16[4,256,128]{2,1,0:T(8,128)(2,1)S(1)} %get-tuple-element.207), channel_id=1, source_target_pairs={{0,16},{16,0},{1,17},{17,1},{2,18},{18,2},{3,19},{19,3},{4,20},{20... | collective-permute-start | bytes 786440 | tf_op jit(solution)/shard_map/ppermute | solution.py:488
  569.3 2.1 collective-permute-start.29
  570.5 28.4 %collective-permute-start.28 = (bf16[1024,512]{1,0:T(8,128)(2,1)S(1)}, bf16[1024,512]{1,0:T(8,128)(2,1)}, u32[]{:S(2)}, u32[]{:S(2)}) collective-permute-start(bf16[1024,512]{1,0:T(8,128)(2,1)S(1)} %get-tuple-element.144), channel_id=1, source_target_pairs={{0,16},{16,0},{1,17},{17,1},{2,18},{18,2},{3,19},{19,3},{4,20},{20... | collective-permute-start | bytes 3145736 | tf_op jit(solution)/shard_map/ppermute | solution.py:481
  571.5 3.8 collective-permute-start.30
  (73 other events, 357.0 us)
Sparse Core Ops, SparseCore 0:
  11.6 121.9 all-gather.13
  135.9 59.8 all-gather.9
  301.1 31.4 reduce-scatter.4
  349.2 32.8 reduce-scatter.6
  455.7 26.5 reduce-scatter.8
  483.7 22.4 all-gather.15
  522.9 26.3 reduce-scatter.10
  565.8 22.0 all-gather.11

commit v11 on v10

--- a/solution.py
+++ b/solution.py
@@ -354,7 +354,7 @@
     grad_hidden = grad_hidden.astype(F32)
     grad_gate = grad_hidden * up * sig * (1.0 + gate * (1.0 - sig))
     grad_up = grad_hidden * gate * sig
-    dgu = jnp.concatenate([grad_gate, grad_up], axis=1).astype(BF)
+    dgu = together(jnp.concatenate([grad_gate, grad_up], axis=1).astype(BF))
 
     def exchanged(values, axis, part, pairs, where):
         size = values.shape[where] // 2
@@ -386,11 +386,14 @@
         got = lax.ppermute(sent, "group", core_pairs)
         return (products(pairs, core) + got.astype(F32)).astype(BF)
 
+    dgu, mix_other = together((dgu, nt(dgu[tokens:], w_in).astype(BF)))
     in_pairs, down_pairs = [(mixed, dgu)], [(hidden, cots)]
-    mix_other = nt(dgu[tokens:], w_in).astype(BF)
     send_in, send_down = to_core(in_pairs), to_core(down_pairs)
-    dgu_own, mix_other, send_in, send_down = together((dgu[:tokens], mix_other, send_in, send_down))
-    mix_got = lax.ppermute(mix_other, "section", swap)
+    mix_got = [lax.ppermute(mix_other[:PATCHES], "section", swap)]
+    dgu_own, send_in, send_down, mix_got[0], rest = together(
+        (dgu[:tokens], send_in, send_down, mix_got[0], mix_other[PATCHES:])
+    )
+    mix_got.append(lax.ppermute(rest, "section", swap))
 
     half = D // sections
     parts = nn(hidden, w_down)
@@ -402,7 +405,7 @@
 
     half_in, half_down = of_chip(in_pairs, send_in), of_chip(down_pairs, send_down)
     mix_got, half_in, half_down = together((mix_got, half_in, half_down))
-    grad_mixed = nt(dgu_own, w_in) + mix_got.astype(F32)
+    grad_mixed = nt(dgu_own, w_in) + jnp.concatenate(mix_got, axis=0).astype(F32)
     grad_mix, gain_mix = norm_backward(residual, second_scale, gains[1, 1], grad_mixed)
     grad_residual = grad_mix + cot.astype(F32)
     branch = grad_residual.astype(BF)
@@ -475,19 +478,17 @@
 
     early, gain_grads = together(([other[row] for row in range(rows - 1)], gain_grads))
     bytes_got = [lax.ppermute(part, "section", swap) for part in early]
-    late, gain_grads, sum_one, bytes_got, ffn_gin = together(
-        (other[rows - 1], gain_grads, sum_one, bytes_got, ffn_gin)
-    )
-    bytes_got.append(lax.ppermute(late, "section", swap))
     for pairs in (core_pairs, side_pairs):
         gain_grads = gain_grads + lax.ppermute(gain_grads, "group", pairs)
     gain_grads = jnp.sum(lax.all_gather(gain_grads, "dp", axis=0, tiled=False), axis=0)
-
+    ffn_gdown = laid_out(gathered(sum_down), (0, 2, 1, 3))
+    late, gain_grads, sum_one, bytes_got, ffn_gdown = together(
+        (other[rows - 1], gain_grads, sum_one, bytes_got, ffn_gdown)
+    )
+    bytes_got.append(lax.ppermute(late, "section", swap))
     kept = jnp.where(section == 0, sum_one, sum_two)
     sent = jnp.where(section == 0, sum_two, sum_one)
     got = lax.ppermute(sent, "section", swap)
-    got, sum_down = together((got, sum_down))
-    ffn_gdown = laid_out(gathered(sum_down), (0, 2, 1, 3))
     eighths = jnp.where(
         section == 0, jnp.concatenate([kept, got], axis=2), jnp.concatenate([got, kept], axis=2)
     )

time: 621 us -> 620 us (level)
    ppermute x1, waiting for transfers between devices: 14.2 us -> 0.14 us  [shards(): bytes_got = [lax.ppermute(part, 'section', swap) for part in early]]
    ppermute x1, waiting for transfers between devices: 0.01 us -> 13.3 us  [shards(): bytes_got.append(lax.ppermute(late, 'section', swap))]
    ppermute x1 -> x2, waiting for transfers between devices: 12.8 us -> 8.11 us  [the longest x1 5.27 us: shards(): mix_got.append(lax.ppermute(rest, 'section', swap))]
    unnamed x175 -> x173, local copies, waits for them, and re-layouts: 13.9 us -> 15.9 us
    convert_element_type x3 -> x4, other arithmetic: 10.9 us -> 12.5 us  [of_chip(): return (products(pairs, core) + got.astype(F32)).astype(BF)]
  transfers between devices with their start and end apart: 39 -> 40, of which waited for: 12 -> 14; matrix products, arithmetic and copies ran while one was open for 39% -> 39% of each run, Pallas kernels for 10% -> 11%
where the time goes in v11:
time: 620 us; the launch traced here: 616 us
  matrix products  169 us (27%)
  waiting for transfers between devices  166 us (27%)
  other arithmetic  112 us (18%)
  Pallas kernels  64.8 us (10%)
  local copies, waits for them, and re-layouts  34.8 us (6%)
  starting transfers between devices  27.8 us (4%)
  blocking collectives  26.3 us (4%)
  between operations  16 us (3%)
    all_gather x1, waiting for transfers between devices, shards(): lax.all_gather(matrix, ('section', 'group', 'dp'), axis=0, tiled=True)  87.2 us
    dot_general x11, matrix products, nt(): lax.dot_general(left, right, (((1,), (1,)), ((), ())), preferred_element_...  57 us
    dot_general x10, matrix products, nn(): return jnp.dot(left, right, preferred_element_type=F32)  52.7 us
    dot_general x20, matrix products, tn(): lax.dot_general(left, right, (((0,), (0,)), ((), ())), preferred_element_...  50.4 us
    pallas_call x2, Pallas kernels, attend_back(): pl.pallas_call(functools.partial(attend_back_kernel, chunk, spans), grid_...  42.8 us
    ppermute x10, waiting for transfers between devices, exchanged(): lax.ppermute(other, axis, pairs).astype(F32)  34.5 us
    pallas_call x2, Pallas kernels, attend(): pl.pallas_call(functools.partial(attend_kernel, chunk, spans), grid_spec=...  22 us
    unnamed x173, local copies, waits for them, and re-layouts  15.9 us
  transfers between devices with their start and end apart: 40, of which 14 were waited for; matrix products, arithmetic and copies ran while one was open for 39% of the time, Pallas kernels for 11%

profile of v11, /device:TPU:0, one launch (start us, length us, event | category | flops | bytes accessed | tf_op | source)
XLA Modules:
  0.0 616.4 jit_solution(18167688843664604389)
XLA Ops:
  22.2 3.9 multiply_reduce_fusion.5
  26.1 3.8 fusion.2
  32.6 4.7 all_gather.31
  37.4 4.2 fusion.4
  46.4 87.2 %all-gather.14.cloned.1.call-done = bf16[1,8192,1024]{2,1,0:T(8,128)(2,1)} async-done(((bf16[1,256,1024]{2,1,0:T(8,128)(2,1)}), bf16[1,8192,1024]{2,1,0:T(8,128)(2,1)}) %all-gather.14.cloned.1.call-update) | async-done | bytes 16777232 | tf_op jit(solution)/shard_map/all_gather | solution.py:264
  133.6 9.4 %convolution_convert_fusion.2.v_ref = bf16[2048,1024]{1,0:T(8,128)(2,1)} fusion(bf16[2048,1024]{1,0:T(8,128)(2,1)} %bitcast.281, bf16[2,4,1024,1024]{3,2,1,0:T(8,128)(2,1)} %bitcast.343), kind=kOutput, calls=%fused_computation.50 | convolution fusion | flops 4297064448 | bytes 10485760 | tf_op jit(solution)/shard_map/dot_general | solution.py:31
  147.6 8.0 %convolution_convert_fusion.3.k_ref = bf16[2048,1024]{1,0:T(8,128)(2,1)} fusion(bf16[2048,1024]{1,0:T(8,128)(2,1)S(1)} %bitcast.282, bf16[2,4,1024,1024]{3,2,1,0:T(8,128)(2,1)} %bitcast.345), kind=kOutput, calls=%fused_computation.51 | convolution fusion | flops 4297064448 | bytes 10485760 | tf_op jit(solution)/shard_map/dot_general | solution.py:31
  155.5 17.9 %attend.2 = (bf16[512,1024]{1,0:T(8,128)(2,1)S(1)}, f32[2,8,2,256]{3,2,1,0:T(2,128)S(1)}) custom-call(s32[2,2]{1,0:T(2,128)S(1)} %get-tuple-element.246.first_ref, s32[2,2]{1,0:T(2,128)S(1)} %get-tuple-element.231.stop_ref, s32[2,1,256]{2,1,0:T(1,128)S(1)} %broadcast_in_dim.73.lo_ref, s32[2,1,256]{2,1,0:T(1,128)S(1)} %bitcast.270, ...), custom_call_target="tpu_custom_call" | custom-call | flops 8589934592 | bytes 18874368 | tf_op jit(solution)/shard_map/attend/pallas_call | solution.py:186
  173.5 3.4 fusion.24
  180.2 3.3 fusion.81.k_ref
  183.5 3.4 fusion.82.q_ref
  187.0 4.1 attend.3
  192.5 3.3 multiply_reduce_fusion.4
  198.0 3.3 maximum_select_fusion.1
  201.3 5.8 convolution_convert_fusion.1
  207.1 14.7 %collective-permute-done.4 = bf16[512,1024]{1,0:T(8,128)(2,1)} collective-permute-done((bf16[512,1024]{1,0:T(8,128)(2,1)S(1)}, bf16[512,1024]{1,0:T(8,128)(2,1)}, u32[]{:S(2)}, u32[]{:S(2)}) %collective-permute-start.4) | collective-permute-done | bytes 1048608 | tf_op jit(solution)/shard_map/ppermute | solution.py:345
  221.9 9.5 %fusion.109 = f32[1024,2816]{1,0:T(8,128)S(1)} fusion(bf16[1024,2816]{1,0:T(8,128)(2,1)} %bitcast.359, bf16[512,1024]{1,0:T(8,128)(2,1)} %collective-permute-done.4, bf16[512,1024]{1,0:T(8,128)(2,1)} %copy-done.57), kind=kOutput, calls=%fused_computation.201 | convolution fusion | flops 5909774336 | bytes 19398656 | tf_op jit(solution)/shard_map/dot_general | solution.py:31
  231.4 4.6 fusion.14
  239.3 7.9 %fusion.76 = bf16[512,1024]{1,0:T(8,128)(2,1)S(1)} fusion(bf16[1024,2816]{1,0:T(8,128)(2,1)} %bitcast.360, bf16[1024,2816]{1,0:T(8,128)(2,1)S(1)} %pad_maximum_fusion), kind=kOutput, calls=%fused_computation.153 | convolution fusion | flops 2953314304 | bytes 9699328 | tf_op jit(solution)/shard_map/dot_general | solution.py:39
  252.7 6.3 %convolution_convert_fusion = bf16[1024,1408]{1,0:T(8,128)(2,1)} fusion(bf16[1024,2816]{1,0:T(8,128)(2,1)S(1)} %pad_maximum_fusion, s32[]{:T(128)S(6)} %select_n.315, bf16[512,1024]{1,0:T(8,128)(2,1)} %collective-permute-done.4, bf16[512,1024]{1,0:T(8,128)(2,1)S(1)} %copy-done.58), kind=kOutput, calls=%fused_computation.48 | convolution fusion | flops 2958426112 | bytes 7864324 | tf_op jit(solution)/shard_map/dot_general | solution.py:35
  262.3 6.1 fusion.177
  277.0 6.9 %add_convert_fusion = bf16[1024,1408]{1,0:T(8,128)(2,1)S(1)} fusion(bf16[1024,1408]{1,0:T(8,128)(2,1)} %collective-permute-done.9, bf16[1024,2816]{1,0:T(8,128)(2,1)} %copy-done.26, s32[]{:T(128)S(6)} %select_n.318, bf16[512,1024]{1,0:T(8,128)(2,1)} %collective-permute-done.4, bf16[512,1024]{1,0:T(8,128)(2,1)} %copy-done.57), kind=kOutput, calls=%fused_computation.28 | convolution fusion | flops 2961309696 | bytes 10747908 | tf_op jit(solution)/shard_map/dot_general | solution.py:35
  283.9 5.3 collective-permute-done.8
  289.2 7.6 %multiply_reduce_fusion = (f32[1024]{0:T(1024)S(1)}, f32[512]{0:T(512)S(1)}, f32[512,1024]{1,0:T(8,128)}) fusion(f32[512,1024]{1,0:T(8,128)S(1)} %get-tuple-element.243, f32[512]{0:T(512)S(1)} %get-tuple-element.227, bf16[256,1024]{1,0:T(8,128)(2,1)} %collective-permute-done.8, bf16[256,1024]{1,0:T(8,128)(2,1)} %collective-permute-done.7, ...), kind=kOutput, calls=%fused_computation.98 | convolution fusion | flops 2958555648 | bytes 13905920 | tf_op jit(solution)/shard_map/dot_general | solution.py:39
  298.6 3.9 fusion.168
  302.5 4.3 fusion.79.dc_ref
  306.8 11.5 %attend_back.2 = (bf16[512,1024]{1,0:T(8,128)(2,1)S(1)}, bf16[512,1024]{1,0:T(8,128)(2,1)S(1)}, bf16[512,1024]{1,0:T(8,128)(2,1)S(1)}) custom-call(s32[2,2]{1,0:T(2,128)S(1)} %get-tuple-element.249.first_ref, s32[2,2]{1,0:T(2,128)S(1)} %get-tuple-element.248.stop_ref, s32[2,1,256]{2,1,0:T(1,128)S(1)} %broadcast_in_dim.83.lo_ref, ...), custom_call_target="tpu_custom_call" | custom-call | flops 5368709120 | bytes 6291456 | tf_op jit(solution)/shard_map/attend_back/pallas_call | solution.py:210
  325.0 6.1 collective-permute-done.11
  334.0 4.4 fusion.6
  353.7 3.6 fusion.33
  372.1 31.3 %attend_back.3 = (bf16[512,1024]{1,0:T(8,128)(2,1)S(1)}, bf16[2048,1024]{1,0:T(8,128)(2,1)}, bf16[2048,1024]{1,0:T(8,128)(2,1)}) custom-call(s32[2,2]{1,0:T(2,128)S(1)} %get-tuple-element.247.first_ref, s32[2,2]{1,0:T(2,128)S(1)} %get-tuple-element.230.stop_ref, s32[2,1,256]{2,1,0:T(1,128)S(1)} %broadcast_in_dim.73.lo_ref, s32[2,1,256]{2,1,0:T(1,128)S(1)} %bitcast.271, ...), custom_call_target="tpu_custom_call" | custom-call | flops 21474836480 | bytes 18874368 | tf_op jit(solution)/shard_map/attend_back/pallas_call | solution.py:210
  403.4 4.1 fusion.85
  419.7 3.7 fusion.67
  424.3 3.7 fusion.64
  430.2 6.9 %collective-permute-done.18 = bf16[2,1024,128]{2,1,0:T(8,128)(2,1)S(1)} collective-permute-done((bf16[2,1024,128]{2,1,0:T(8,128)(2,1)S(1)}, bf16[2,1024,128]{2,1,0:T(8,128)(2,1)S(1)}, u32[]{:S(2)}, u32[]{:S(2)}) %collective-permute-start.18) | collective-permute-done | bytes 524320 | tf_op jit(solution)/shard_map/ppermute | solution.py:363
  439.7 3.7 fusion.18
  443.8 4.0 fusion.17
  454.7 7.2 %fusion.49 = f32[2048,1024]{1,0:T(8,128)S(1)} fusion(bf16[2048,1024]{1,0:T(8,128)(2,1)} %get-tuple-element.129, bf16[2,4,1024,1024]{3,2,1,0:T(8,128)(2,1)} %bitcast.356), kind=kOutput, calls=%fused_computation.130 | convolution fusion | flops 4294967296 | bytes 14680064 | tf_op jit(solution)/shard_map/dot_general | solution.py:39
  461.9 8.6 %convolution_add_fusion = f32[2048,1024]{1,0:T(8,128)} fusion(f32[2048,1024]{1,0:T(8,128)S(1)} %fusion.49, bf16[2048,1024]{1,0:T(8,128)(2,1)S(1)} %copy-done.60, bf16[2,4,1024,1024]{3,2,1,0:T(8,128)(2,1)} %bitcast.357), kind=kOutput, calls=%fused_computation.47 | convolution fusion | flops 4297064448 | bytes 23068672 | tf_op jit(solution)/shard_map/dot_general | solution.py:39
  485.3 18.1 %collective-permute-done.22 = bf16[2,1024,128]{2,1,0:T(8,128)(2,1)} collective-permute-done((bf16[2,1024,128]{2,1,0:T(8,128)(2,1)}, bf16[2,1024,128]{2,1,0:T(8,128)(2,1)}, u32[]{:S(2)}, u32[]{:S(2)}) %collective-permute-start.22) | collective-permute-done | bytes 524320 | tf_op jit(solution)/shard_map/ppermute | solution.py:363
  507.0 6.1 fusion.11
  515.2 4.6 fusion.60
  519.9 8.6 %fusion.1 = bf16[2048,1024]{1,0:T(8,128)(2,1)S(1)} fusion(f32[2,1024,1024]{2,1,0:T(8,128)} %fusion.60, f32[2048,1024]{1,0:T(8,128)} %convolution_add_fusion, f32[2048]{0:T(1024)S(1)} %broadcast_multiply_fusion, f32[2048]{0:T(1024)S(1)} %multiply_multiply_fusion, f32[1024]{0:T(1024)S(1)} %bitcast.307, f32[2048]{0:T(1024)S(1)} %bitcast.303, ...), kind=kLoop, calls=%fused_computation.3 | loop fusion | flops 16777216 | bytes 25194500 | tf_op jit(solution)/shard_map/convert_element_type | solution.py:467
  536.1 13.6 %all-gather.4 = f32[4,4,1024]{2,1,0:T(4,128)S(1)} all-gather(f32[1,4,1024]{2,1,0:T(4,128)S(1)} %add_bitcast_fusion), channel_id=4, replica_groups=mesh['section'=2,'group'=4,'dp'=4] {'dp'}, dimensions={0}, use_global_device_ids=true | all-gather | bytes 81920 | tf_op jit(solution)/shard_map/all_gather | solution.py:483
  549.8 8.1 %all-gather.3 = bf16[1408,256]{1,0:T(8,128)(2,1)S(1)} all-gather(bf16[352,256]{1,0:T(8,128)(2,1)S(1)} %add_convert_fusion.12), channel_id=5, replica_groups=mesh['section'=2,'group'=4,'dp'=4] {'group'}, dimensions={0}, use_global_device_ids=true | all-gather | bytes 901120 | tf_op jit(solution)/shard_map/all_gather | solution.py:438
  562.1 6.7 %collective-permute-done.30 = bf16[4,256,128]{2,1,0:T(8,128)(2,1)S(1)} collective-permute-done((bf16[4,256,128]{2,1,0:T(8,128)(2,1)S(1)}, bf16[4,256,128]{2,1,0:T(8,128)(2,1)S(1)}, u32[]{:S(2)}, u32[]{:S(2)}) %collective-permute-start.30) | collective-permute-done | bytes 262176 | tf_op jit(solution)/shard_map/ppermute | solution.py:491
  576.7 8.4 %maximum_convert_fusion = f32[128,5632]{1,0:T(8,128)} fusion(bf16[64,1408]{1,0:T(8,128)(2,1)S(1)} %get-tuple-element.195, bf16[64,1408]{1,0:T(8,128)(2,1)S(1)} %get-tuple-element.196, bf16[64,1408]{1,0:T(8,128)(2,1)S(1)} %get-tuple-element.197, bf16[64,1408]{1,0:T(8,128)(2,1)S(1)} %get-tuple-element.198, bf16[64,1408]{1,0:T(8,128)(2,1)S(1)} %get-tuple-element.199, ...), kind=kLoop, calls=%fused_computation.167 | loop fusion | flops 11534336 | bytes 4325376 | tf_op jit(solution)/shard_map/concatenate | solution.py:474
  585.8 13.3 %collective-permute-done.31 = bf16[1024,512]{1,0:T(8,128)(2,1)} collective-permute-done((bf16[1024,512]{1,0:T(8,128)(2,1)S(1)}, bf16[1024,512]{1,0:T(8,128)(2,1)}, u32[]{:S(2)}, u32[]{:S(2)}) %collective-permute-start.31) | collective-permute-done | bytes 1048608 | tf_op jit(solution)/shard_map/ppermute | solution.py:488
  (389 shorter events, 171.4 us)
Async XLA Ops:
  7.2 18.9 %copy-start = (s32[4,256]{1,0:T(4,128)S(1)}, s32[4,256]{1,0:T(4,128)}, u32[]{:S(2)}) copy-start(s32[4,256]{1,0:T(4,128)} %param.11) | copy-start | bytes 12292
  7.2 126.4 %all-gather.14.cloned.1.call-start = ((), (), s32[]{:S(2)}) async-start(), calls=%async_computation.10 | async-start | bytes 17301504 | tf_op jit(solution)/shard_map/all_gather | solution.py:264
  9.3 212.6 %all-gather.10.cloned.1.call-start = ((), (), s32[]{:S(2)}) async-start(), calls=%async_computation.4 | async-start | bytes 6127616 | tf_op jit(solution)/shard_map/all_gather | solution.py:287
  10.4 34.1 %collective-permute-start = (bf16[88,1024]{1,0:T(8,128)(2,1)S(1)}, bf16[88,1024]{1,0:T(8,128)(2,1)}, u32[]{:S(2)}, u32[]{:S(2)}) collective-permute-start(bf16[88,1024]{1,0:T(8,128)(2,1)S(1)} %get-tuple-element.168), channel_id=1, source_target_pairs={{0,1},{1,2},{2,3},{3,0},{4,5},{5,6},{6,7},{7,4},{8,9},{9,10},{10,1... | collective-permute-start | bytes 540680 | tf_op jit(solution)/shard_map/ppermute | solution.py:293
  13.5 32.0 %collective-permute-start.1 = (bf16[88,1024]{1,0:T(8,128)(2,1)S(1)}, bf16[88,1024]{1,0:T(8,128)(2,1)}, u32[]{:S(2)}, u32[]{:S(2)}) collective-permute-start(bf16[88,1024]{1,0:T(8,128)(2,1)S(1)} %get-tuple-element.168), channel_id=1, source_target_pairs={{0,2},{1,3},{2,0},{3,1},{4,6},{5,7},{6,4},{7,5},{8,10},{9,11},{10,... | collective-permute-start | bytes 540680 | tf_op jit(solution)/shard_map/ppermute | solution.py:293
  16.1 30.3 %collective-permute-start.2 = (bf16[88,1024]{1,0:T(8,128)(2,1)S(1)}, bf16[88,1024]{1,0:T(8,128)(2,1)S(1)}, u32[]{:S(2)}, u32[]{:S(2)}) collective-permute-start(bf16[88,1024]{1,0:T(8,128)(2,1)S(1)} %get-tuple-element.168), channel_id=1, source_target_pairs={{0,3},{1,0},{2,1},{3,2},{4,7},{5,4},{6,5},{7,6},{8,11},{9,8},{10,9... | collective-permute-start | bytes 540680 | tf_op jit(solution)/shard_map/ppermute | solution.py:293
  19.4 10.6 %collective-permute-start.6 = (bf16[32,2816]{1,0:T(8,128)(2,1)}, bf16[32,2816]{1,0:T(8,128)(2,1)}, u32[]{:S(2)}, u32[]{:S(2)}) collective-permute-start(bf16[32,2816]{1,0:T(8,128)(2,1)} %pad_maximum_fusion.15), channel_id=1, source_target_pairs={{0,16},{16,0},{1,17},{17,1},{2,18},{18,2},{3,19},{19,3},{4,20},{20... | collective-permute-start | bytes 540680 | tf_op jit(solution)/shard_map/ppermute | solution.py:285
  26.1 17.1 %copy-start.17 = (f32[2,256,1024]{2,1,0:T(8,128)}, f32[2,256,1024]{2,1,0:T(8,128)S(1)}, u32[]{:S(2)}) copy-start(f32[2,256,1024]{2,1,0:T(8,128)S(1)} %get-tuple-element.239) | copy-start | bytes 6291460
  31.8 302.2 %reduce-scatter.5.cloned.1.call-start = ((), (), s32[]{:S(2)}) async-start(), calls=%async_computation.5 | async-start | bytes 1802240 | tf_op jit(solution)/shard_map/reduce_scatter | solution.py:376
  37.3 224.4 %copy-start.71 = (f32[1,8,2,128]{3,2,1,0:T(2,128)}, f32[1,8,2,128]{3,2,1,0:T(2,128)S(1)}, u32[]{:S(2)}) copy-start(f32[1,8,2,128]{3,2,1,0:T(2,128)S(1)} %get-tuple-element.220) | copy-start | bytes 24580
  143.1 48.0 %collective-permute-start.3 = (bf16[4,88,1024]{2,1,0:T(8,128)(2,1)S(1)}, bf16[4,88,1024]{2,1,0:T(8,128)(2,1)S(1)}, u32[]{:S(2)}, u32[]{:S(2)}) collective-permute-start(bf16[4,88,1024]{2,1,0:T(8,128)(2,1)S(1)} %bitcast_dynamic-update-slice_fusion), channel_id=1, source_target_pairs={{0,8},{4,12},{8,0},{12,4},{1,9},{5,13},{9,1},{13,5},{2,10},{6,14},... | collective-permute-start | bytes 2162696 | tf_op jit(solution)/shard_map/ppermute | solution.py:276
  155.5 17.9 %copy-start.22 = (f32[512,1024]{1,0:T(8,128)S(1)}, f32[512,1024]{1,0:T(8,128)}, u32[]{:S(2)}) copy-start(f32[512,1024]{1,0:T(8,128)} %bitcast_divide_fusion) | copy-start | bytes 6291460
  192.5 5.5 collective-permute-start.5
  196.1 25.7 %collective-permute-start.4 = (bf16[512,1024]{1,0:T(8,128)(2,1)S(1)}, bf16[512,1024]{1,0:T(8,128)(2,1)}, u32[]{:S(2)}, u32[]{:S(2)}) collective-permute-start(bf16[512,1024]{1,0:T(8,128)(2,1)S(1)} %multiply_convert_fusion.2), channel_id=1, source_target_pairs={{0,16},{16,0},{1,17},{17,1},{2,18},{18,2},{3,19},{19,3},{4,20},{20... | collective-permute-start | bytes 3145736 | tf_op jit(solution)/shard_map/ppermute | solution.py:345
  236.0 12.4 %copy-start.27 = (bf16[1024,1408]{1,0:T(8,128)(2,1)}, bf16[1024,1408]{1,0:T(8,128)(2,1)S(1)}, u32[]{:S(2)}) copy-start(bf16[1024,1408]{1,0:T(8,128)(2,1)S(1)} %get-tuple-element.173) | copy-start | bytes 8650756
  248.1 13.6 %collective-permute-start.7 = (bf16[256,1024]{1,0:T(8,128)(2,1)S(1)}, bf16[256,1024]{1,0:T(8,128)(2,1)}, u32[]{:S(2)}, u32[]{:S(2)}) collective-permute-start(bf16[256,1024]{1,0:T(8,128)(2,1)S(1)} %get-tuple-element.207), channel_id=1, source_target_pairs={{0,16},{16,0},{1,17},{17,1},{2,18},{18,2},{3,19},{19,3},{4,20},{20... | collective-permute-start | bytes 1572872 | tf_op jit(solution)/shard_map/ppermute | solution.py:392
  261.8 15.2 %collective-permute-start.9 = (bf16[1024,1408]{1,0:T(8,128)(2,1)}, bf16[1024,1408]{1,0:T(8,128)(2,1)}, u32[]{:S(2)}, u32[]{:S(2)}) collective-permute-start(bf16[1024,1408]{1,0:T(8,128)(2,1)} %convolution_convert_fusion), channel_id=1, source_target_pairs={{0,4},{4,0},{8,12},{12,8},{1,5},{5,1},{9,13},{13,9},{2,6},{6,2},{1... | collective-permute-start | bytes 8650760 | tf_op jit(solution)/shard_map/ppermute | solution.py:386
  261.8 13.5 %collective-permute-start.10 = (bf16[1408,512]{1,0:T(8,128)(2,1)}, bf16[1408,512]{1,0:T(8,128)(2,1)S(1)}, u32[]{:S(2)}, u32[]{:S(2)}) collective-permute-start(bf16[1408,512]{1,0:T(8,128)(2,1)} %convolution_convert_fusion.4), channel_id=1, source_target_pairs={{0,4},{4,0},{8,12},{12,8},{1,5},{5,1},{9,13},{13,9},{2,6},{6,2},{1... | collective-permute-start | bytes 4325384 | tf_op jit(solution)/shard_map/ppermute | solution.py:386
  274.9 14.3 %collective-permute-start.8 = (bf16[256,1024]{1,0:T(8,128)(2,1)}, bf16[256,1024]{1,0:T(8,128)(2,1)}, u32[]{:S(2)}, u32[]{:S(2)}) collective-permute-start(bf16[256,1024]{1,0:T(8,128)(2,1)} %get-tuple-element.94), channel_id=1, source_target_pairs={{0,16},{16,0},{1,17},{17,1},{2,18},{18,2},{3,19},{19,3},{4,20},{20... | collective-permute-start | bytes 1572872 | tf_op jit(solution)/shard_map/ppermute | solution.py:396
  283.9 12.9 %copy-start.45 = (bf16[1024,1408]{1,0:T(8,128)(2,1)}, bf16[1024,1408]{1,0:T(8,128)(2,1)S(1)}, u32[]{:S(2)}) copy-start(bf16[1024,1408]{1,0:T(8,128)(2,1)S(1)} %add_convert_fusion) | copy-start | bytes 8650756
  298.1 33.1 %collective-permute-start.11 = (bf16[2,4,1,64,1408]{4,3,2,1,0:T(8,128)(2,1)}, bf16[2,4,1,64,1408]{4,3,2,1,0:T(8,128)(2,1)}, u32[]{:S(2)}, u32[]{:S(2)}) collective-permute-start(bf16[2,4,1,64,1408]{4,3,2,1,0:T(8,128)(2,1)} %constant_dynamic-slice_fusion.11), channel_id=1, source_target_pairs={{0,8},{4,12},{8,0},{12,4},{1,9},{5,13},{9,1},{13,5},{2,10},{6,14},... | collective-permute-start | bytes 4325384 | tf_op jit(solution)/shard_map/ppermute | solution.py:363
  298.1 149.7 %reduce-scatter.7.cloned.1.call-start = ((), (), s32[]{:S(2)}) async-start(), calls=%async_computation.6 | async-start | bytes 1802240 | tf_op jit(solution)/shard_map/reduce_scatter | solution.py:376
  302.5 15.8 %copy-start.54 = (bf16[512,1024]{1,0:T(8,128)(2,1)}, bf16[512,1024]{1,0:T(8,128)(2,1)S(1)}, u32[]{:S(2)}) copy-start(bf16[512,1024]{1,0:T(8,128)(2,1)S(1)} %get-tuple-element.165) | copy-start | bytes 3145732
  334.0 31.5 %collective-permute-start.12 = (bf16[4,1024,512]{2,1,0:T(8,128)(2,1)}, bf16[4,1024,512]{2,1,0:T(8,128)(2,1)}, u32[]{:S(2)}, u32[]{:S(2)}) collective-permute-start(bf16[4,1024,512]{2,1,0:T(8,128)(2,1)} %pad_maximum_fusion.1), channel_id=1, source_target_pairs={{0,4},{4,0},{8,12},{12,8},{1,5},{5,1},{9,13},{13,9},{2,6},{6,2},{1... | collective-permute-start | bytes 12582920 | tf_op jit(solution)/shard_map/ppermute | solution.py:386
  338.4 31.3 %collective-permute-start.13 = (bf16[1024,512]{1,0:T(8,128)(2,1)}, bf16[1024,512]{1,0:T(8,128)(2,1)}, u32[]{:S(2)}, u32[]{:S(2)}) collective-permute-start(bf16[1024,512]{1,0:T(8,128)(2,1)} %fusion.35), channel_id=1, source_target_pairs={{0,16},{16,0},{1,17},{17,1},{2,18},{18,2},{3,19},{19,3},{4,20},{20... | collective-permute-start | bytes 3145736 | tf_op jit(solution)/shard_map/ppermute | solution.py:404
  347.5 159.5 %reduce-scatter.9.cloned.1.call-start = ((), (), s32[]{:S(2)}) async-start(), calls=%async_computation.7 | async-start | bytes 1310720 | tf_op jit(solution)/shard_map/reduce_scatter | solution.py:376
  370.1 42.7 %collective-permute-start.15 = (bf16[2,1024,256]{2,1,0:T(8,128)(2,1)S(1)}, bf16[2,1024,256]{2,1,0:T(8,128)(2,1)}, u32[]{:S(2)}, u32[]{:S(2)}) collective-permute-start(bf16[2,1024,256]{2,1,0:T(8,128)(2,1)S(1)} %constant_dynamic-slice_fusion.9), channel_id=1, source_target_pairs={{0,8},{4,12},{8,0},{12,4},{1,9},{5,13},{9,1},{13,5},{2,10},{6,14},... | collective-permute-start | bytes 3145736 | tf_op jit(solution)/shard_map/ppermute | solution.py:363
  370.4 43.9 %collective-permute-start.14 = (bf16[2,1024,256]{2,1,0:T(8,128)(2,1)S(1)}, bf16[2,1024,256]{2,1,0:T(8,128)(2,1)S(1)}, u32[]{:S(2)}, u32[]{:S(2)}) collective-permute-start(bf16[2,1024,256]{2,1,0:T(8,128)(2,1)S(1)} %constant_dynamic-slice_fusion.10), channel_id=1, source_target_pairs={{0,16},{16,0},{1,17},{17,1},{2,18},{18,2},{3,19},{19,3},{4,20},{20... | collective-permute-start | bytes 3145736 | tf_op jit(solution)/shard_map/ppermute | solution.py:363
  372.1 31.3 %copy-start.16 = (bf16[2048,1024]{1,0:T(8,128)(2,1)S(1)}, bf16[2048,1024]{1,0:T(8,128)(2,1)}, u32[]{:S(2)}) copy-start(bf16[2048,1024]{1,0:T(8,128)(2,1)} %fusion.6) | copy-start | bytes 12582916
  418.3 21.4 %collective-permute-start.17 = (bf16[2,1024,512]{2,1,0:T(8,128)(2,1)}, bf16[2,1024,512]{2,1,0:T(8,128)(2,1)}, u32[]{:S(2)}, u32[]{:S(2)}) collective-permute-start(bf16[2,1024,512]{2,1,0:T(8,128)(2,1)} %pad_maximum_fusion.6), channel_id=1, source_target_pairs={{0,4},{4,0},{8,12},{12,8},{1,5},{5,1},{9,13},{13,9},{2,6},{6,2},{1... | collective-permute-start | bytes 6291464 | tf_op jit(solution)/shard_map/ppermute | solution.py:386
  418.3 25.1 %collective-permute-start.16 = (bf16[2,1024,512]{2,1,0:T(8,128)(2,1)}, bf16[2,1024,512]{2,1,0:T(8,128)(2,1)}, u32[]{:S(2)}, u32[]{:S(2)}) collective-permute-start(bf16[2,1024,512]{2,1,0:T(8,128)(2,1)} %pad_maximum_fusion.5), channel_id=1, source_target_pairs={{0,4},{4,0},{8,12},{12,8},{1,5},{5,1},{9,13},{13,9},{2,6},{6,2},{1... | collective-permute-start | bytes 6291464 | tf_op jit(solution)/shard_map/ppermute | solution.py:386
  423.4 13.6 %collective-permute-start.18 = (bf16[2,1024,128]{2,1,0:T(8,128)(2,1)S(1)}, bf16[2,1024,128]{2,1,0:T(8,128)(2,1)S(1)}, u32[]{:S(2)}, u32[]{:S(2)}) collective-permute-start(bf16[2,1024,128]{2,1,0:T(8,128)(2,1)S(1)} %constant_dynamic-slice_fusion.8), channel_id=1, source_target_pairs={{0,8},{4,12},{8,0},{12,4},{1,9},{5,13},{9,1},{13,5},{2,10},{6,14},... | collective-permute-start | bytes 1572872 | tf_op jit(solution)/shard_map/ppermute | solution.py:363
  423.7 14.8 %collective-permute-start.19 = (bf16[2,1024,128]{2,1,0:T(8,128)(2,1)S(1)}, bf16[2,1024,128]{2,1,0:T(8,128)(2,1)S(1)}, u32[]{:S(2)}, u32[]{:S(2)}) collective-permute-start(bf16[2,1024,128]{2,1,0:T(8,128)(2,1)S(1)} %constant_dynamic-slice_fusion.7), channel_id=1, source_target_pairs={{0,16},{16,0},{1,17},{17,1},{2,18},{18,2},{3,19},{19,3},{4,20},{20... | collective-permute-start | bytes 1572872 | tf_op jit(solution)/shard_map/ppermute | solution.py:363
  449.7 20.8 %collective-permute-start.24 = (bf16[64,1408]{1,0:T(8,128)(2,1)}, bf16[64,1408]{1,0:T(8,128)(2,1)}, u32[]{:S(2)}, u32[]{:S(2)}) collective-permute-start(bf16[64,1408]{1,0:T(8,128)(2,1)} %get-tuple-element.215), channel_id=1, source_target_pairs={{0,16},{16,0},{1,17},{17,1},{2,18},{18,2},{3,19},{19,3},{4,20},{20... | collective-permute-start | bytes 540680 | tf_op jit(solution)/shard_map/ppermute | solution.py:447
  451.7 25.2 %collective-permute-start.21 = (bf16[2,1024,256]{2,1,0:T(8,128)(2,1)}, bf16[2,1024,256]{2,1,0:T(8,128)(2,1)}, u32[]{:S(2)}, u32[]{:S(2)}) collective-permute-start(bf16[2,1024,256]{2,1,0:T(8,128)(2,1)} %constant_dynamic-slice_fusion.5), channel_id=1, source_target_pairs={{0,8},{4,12},{8,0},{12,4},{1,9},{5,13},{9,1},{13,5},{2,10},{6,14},... | collective-permute-start | bytes 3145736 | tf_op jit(solution)/shard_map/ppermute | solution.py:363
  453.0 26.0 %collective-permute-start.20 = (bf16[2,1024,256]{2,1,0:T(8,128)(2,1)}, bf16[2,1024,256]{2,1,0:T(8,128)(2,1)}, u32[]{:S(2)}, u32[]{:S(2)}) collective-permute-start(bf16[2,1024,256]{2,1,0:T(8,128)(2,1)} %constant_dynamic-slice_fusion.6), channel_id=1, source_target_pairs={{0,16},{16,0},{1,17},{17,1},{2,18},{18,2},{3,19},{19,3},{4,20},{20... | collective-permute-start | bytes 3145736 | tf_op jit(solution)/shard_map/ppermute | solution.py:363
  454.7 52.3 %all-gather.16.cloned.1.call-start = ((), (), s32[]{:S(2)}) async-start(), calls=%async_computation.11 | async-start | bytes 1802240 | tf_op jit(solution)/shard_map/all_gather | solution.py:438
  472.2 87.1 %reduce-scatter.11.cloned.1.call-start = ((), (), s32[]{:S(2)}) async-start(), calls=%async_computation.8 | async-start | bytes 1310720 | tf_op jit(solution)/shard_map/reduce_scatter | solution.py:376
  482.3 21.0 %collective-permute-start.22 = (bf16[2,1024,128]{2,1,0:T(8,128)(2,1)}, bf16[2,1024,128]{2,1,0:T(8,128)(2,1)}, u32[]{:S(2)}, u32[]{:S(2)}) collective-permute-start(bf16[2,1024,128]{2,1,0:T(8,128)(2,1)} %constant_dynamic-slice_fusion.4), channel_id=1, source_target_pairs={{0,8},{4,12},{8,0},{12,4},{1,9},{5,13},{9,1},{13,5},{2,10},{6,14},... | collective-permute-start | bytes 1572872 | tf_op jit(solution)/shard_map/ppermute | solution.py:363
  483.8 20.9 %collective-permute-start.23 = (bf16[2,1024,128]{2,1,0:T(8,128)(2,1)}, bf16[2,1024,128]{2,1,0:T(8,128)(2,1)}, u32[]{:S(2)}, u32[]{:S(2)}) collective-permute-start(bf16[2,1024,128]{2,1,0:T(8,128)(2,1)} %constant_dynamic-slice_fusion.3), channel_id=1, source_target_pairs={{0,16},{16,0},{1,17},{17,1},{2,18},{18,2},{3,19},{19,3},{4,20},{20... | collective-permute-start | bytes 1572872 | tf_op jit(solution)/shard_map/ppermute | solution.py:363
  514.0 16.8 %collective-permute-start.25 = (f32[4,1024]{1,0:T(4,128)S(1)}, f32[4,1024]{1,0:T(4,128)S(1)}, u32[]{:S(2)}, u32[]{:S(2)}) collective-permute-start(f32[4,1024]{1,0:T(4,128)S(1)} %pad_maximum_fusion.16), channel_id=1, source_target_pairs={{0,16},{16,0},{1,17},{17,1},{2,18},{18,2},{3,19},{19,3},{4,20},{20... | collective-permute-start | bytes 49160 | tf_op jit(solution)/shard_map/ppermute | solution.py:473
  519.8 79.3 %all-gather.12.cloned.1.call-start = ((), (), s32[]{:S(2)}) async-start(), calls=%async_computation.9 | async-start | bytes 2621440 | tf_op jit(solution)/shard_map/all_gather | solution.py:438
  530.8 1.2 collective-permute-start.26
  532.1 4.0 collective-permute-start.27
  533.3 16.4 %collective-permute-start.29 = (bf16[352,256]{1,0:T(8,128)(2,1)S(1)}, bf16[352,256]{1,0:T(8,128)(2,1)S(1)}, u32[]{:S(2)}, u32[]{:S(2)}) collective-permute-start(bf16[352,256]{1,0:T(8,128)(2,1)S(1)} %constant_dynamic-slice_fusion.1), channel_id=1, source_target_pairs={{0,8},{4,12},{8,0},{12,4},{1,9},{5,13},{9,1},{13,5},{2,10},{6,14},... | collective-permute-start | bytes 540680 | tf_op jit(solution)/shard_map/ppermute | solution.py:363
  534.2 25.1 %collective-permute-start.28 = (bf16[1024,512]{1,0:T(8,128)(2,1)}, bf16[1024,512]{1,0:T(8,128)(2,1)}, u32[]{:S(2)}, u32[]{:S(2)}) collective-permute-start(bf16[1024,512]{1,0:T(8,128)(2,1)} %get-tuple-element.143), channel_id=1, source_target_pairs={{0,16},{16,0},{1,17},{17,1},{2,18},{18,2},{3,19},{19,3},{4,20},{20... | collective-permute-start | bytes 3145736 | tf_op jit(solution)/shard_map/ppermute | solution.py:480
  560.3 8.5 %collective-permute-start.30 = (bf16[4,256,128]{2,1,0:T(8,128)(2,1)S(1)}, bf16[4,256,128]{2,1,0:T(8,128)(2,1)S(1)}, u32[]{:S(2)}, u32[]{:S(2)}) collective-permute-start(bf16[4,256,128]{2,1,0:T(8,128)(2,1)S(1)} %get-tuple-element.213), channel_id=1, source_target_pairs={{0,16},{16,0},{1,17},{17,1},{2,18},{18,2},{3,19},{19,3},{4,20},{20... | collective-permute-start | bytes 786440 | tf_op jit(solution)/shard_map/ppermute | solution.py:491
  574.5 24.6 %collective-permute-start.31 = (bf16[1024,512]{1,0:T(8,128)(2,1)S(1)}, bf16[1024,512]{1,0:T(8,128)(2,1)}, u32[]{:S(2)}, u32[]{:S(2)}) collective-permute-start(bf16[1024,512]{1,0:T(8,128)(2,1)S(1)} %get-tuple-element.148), channel_id=1, source_target_pairs={{0,16},{16,0},{1,17},{17,1},{2,18},{18,2},{3,19},{19,3},{4,20},{20... | collective-permute-start | bytes 3145736 | tf_op jit(solution)/shard_map/ppermute | solution.py:488
  (74 other events, 343.7 us)
Sparse Core Ops, SparseCore 0:
  11.6 121.9 all-gather.13
  136.5 60.2 all-gather.9
  298.2 31.1 reduce-scatter.4
  347.6 31.6 reduce-scatter.6
  454.8 24.4 reduce-scatter.8
  481.4 23.4 all-gather.15
  519.9 25.1 reduce-scatter.10
  569.9 20.3 all-gather.11

commit v12 on v11

--- a/solution.py
+++ b/solution.py
@@ -292,8 +292,6 @@
     for step in range(line):
         moved = lax.ppermute(quarter, "dp", [(i, (i + step) % line) for i in range(line)]) if step else quarter
         down = lax.dynamic_update_slice_in_dim(down, moved[None], (place - step) % line, 0)
-    matrices = matrices.reshape(sections, groups, D, D)
-    wq, wk, wv, wo = [matrices[:, index] for index in range(4)]
 
     rows = byte_states.shape[0] // sections
     mine = lambda a: lax.dynamic_slice_in_dim(a, section * rows, rows, 0)
@@ -321,6 +319,9 @@
     query_scale, key_scale = scale_of(pooled), scale_of(wide)
     query_in = (pooled * query_scale * gains[0, 0]).astype(BF)
     key_in = (wide * key_scale * gains[0, 1]).astype(BF)
+    matrices, key_in, query_in = together((matrices, key_in, query_in))
+    matrices = matrices.reshape(sections, groups, D, D)
+    wq, wk, wv, wo = [matrices[:, index] for index in range(4)]
     q1 = nn(query_in, wq[0]).astype(BF)
     k1 = nn(key_in, wk[0]).astype(BF)
     v1 = nn(key_in, wv[0]).astype(BF)
@@ -434,6 +435,7 @@
     one_pairs = [(query_in, dq1), (key_in, dk1)], [(key_in, dv1), (c1, d_carried)]
     send_one = [to_core(pairs) for pairs in one_pairs]
     dq1, dk1, dv1, send_one, sum_down = together((dq1, dk1, dv1, send_one, sum_down))
+    sum_down = over_side(sum_down, 1)
     def gathered(part):
         return lax.all_gather(part, "group", axis=0, tiled=False)
 
@@ -452,10 +454,10 @@
     half_one = over_section(half_one[0], 2), over_side(half_one[1], 2)
     grad_query_in, grad_key_in, half_one = together((grad_query_in, grad_key_in, half_one))
     half_one = jnp.concatenate([over_side(half_one[0], 2), over_section(half_one[1], 2)], axis=0)
-    grad_query_in, grad_key_in, half_one, sum_two, sum_down, sum_in = together(
-        (grad_query_in, grad_key_in, half_one, sum_two, sum_down, sum_in)
-    )
-    sum_down = over_side(sum_down, 1)
+    ffn_gdown = laid_out(gathered(sum_down), (0, 2, 1, 3))
+    grad_query_in, grad_key_in, half_one, sum_two, ffn_gdown, sum_in = together(
+        (grad_query_in, grad_key_in, half_one, sum_two, ffn_gdown, sum_in)
+    )
     sum_one = line_sum(half_one, 1)
 
     grad_pooled, gain_query = norm_backward(pooled, query_scale, gains[0, 0], grad_query_in)
@@ -481,10 +483,7 @@
     for pairs in (core_pairs, side_pairs):
         gain_grads = gain_grads + lax.ppermute(gain_grads, "group", pairs)
     gain_grads = jnp.sum(lax.all_gather(gain_grads, "dp", axis=0, tiled=False), axis=0)
-    ffn_gdown = laid_out(gathered(sum_down), (0, 2, 1, 3))
-    late, gain_grads, sum_one, bytes_got, ffn_gdown = together(
-        (other[rows - 1], gain_grads, sum_one, bytes_got, ffn_gdown)
-    )
+    late, gain_grads, sum_one, bytes_got = together((other[rows - 1], gain_grads, sum_one, bytes_got))
     bytes_got.append(lax.ppermute(late, "section", swap))
     kept = jnp.where(section == 0, sum_one, sum_two)
     sent = jnp.where(section == 0, sum_two, sum_one)

time: 620 us -> 634 us (1.023)
  blocking collectives: 26.3 us -> 42.1 us
  other arithmetic: 112 us -> 105 us
    all_gather x1, blocking collectives: 8.06 us -> 24 us  [gathered(): return lax.all_gather(part, 'group', axis=0, tiled=False)]
    unnamed x173 -> x177, local copies, waits for them, and re-layouts: 15.9 us -> 13.5 us
  transfers between devices with their start and end apart: 40 -> 40, of which waited for: 14 -> 13; matrix products, arithmetic and copies ran while one was open for 39% -> 38% of each run, Pallas kernels for 11% -> 10%
where the time goes in v12:
time: 634 us; the launch traced here: 630 us
  matrix products  172 us (27%)
  waiting for transfers between devices  169 us (27%)
  other arithmetic  105 us (17%)
  Pallas kernels  64.8 us (10%)
  blocking collectives  42.1 us (7%)
  local copies, waits for them, and re-layouts  31 us (5%)
  starting transfers between devices  30.6 us (5%)
  between operations  16 us (3%)
    all_gather x1, waiting for transfers between devices, shards(): lax.all_gather(matrix, ('section', 'group', 'dp'), axis=0, tiled=True)  88.4 us
    dot_general x11, matrix products, nt(): lax.dot_general(left, right, (((1,), (1,)), ((), ())), preferred_element_...  58.2 us
    dot_general x10, matrix products, nn(): return jnp.dot(left, right, preferred_element_type=F32)  52.7 us
    dot_general x20, matrix products, tn(): lax.dot_general(left, right, (((0,), (0,)), ((), ())), preferred_element_...  51.5 us
    pallas_call x2, Pallas kernels, attend_back(): pl.pallas_call(functools.partial(attend_back_kernel, chunk, spans), grid_...  42.8 us
    ppermute x10, waiting for transfers between devices, exchanged(): lax.ppermute(other, axis, pairs).astype(F32)  32 us
    all_gather x1, blocking collectives, gathered(): return lax.all_gather(part, 'group', axis=0, tiled=False)  24 us
    pallas_call x2, Pallas kernels, attend(): pl.pallas_call(functools.partial(attend_kernel, chunk, spans), grid_spec=...  22 us
  transfers between devices with their start and end apart: 40, of which 13 were waited for; matrix products, arithmetic and copies ran while one was open for 38% of the time, Pallas kernels for 10%

profile of v12, /device:TPU:0, one launch (start us, length us, event | category | flops | bytes accessed | tf_op | source)
XLA Modules:
  0.0 630.3 jit_solution(8438928869872452458)
XLA Ops:
  21.4 3.4 fusion.2
  24.9 4.9 multiply_reduce_fusion.5
  31.5 4.6 all_gather.32
  39.3 4.9 fusion.4
  45.2 88.4 %all-gather.14.cloned.1.call-done = bf16[1,8192,1024]{2,1,0:T(8,128)(2,1)} async-done(((bf16[1,256,1024]{2,1,0:T(8,128)(2,1)}), bf16[1,8192,1024]{2,1,0:T(8,128)(2,1)}) %all-gather.14.cloned.1.call-update) | async-done | bytes 16777232 | tf_op jit(solution)/shard_map/all_gather | solution.py:264
  133.6 9.4 %convolution_convert_fusion.2.v_ref = bf16[2048,1024]{1,0:T(8,128)(2,1)} fusion(bf16[2048,1024]{1,0:T(8,128)(2,1)} %fusion.4, bf16[2,4,1024,1024]{3,2,1,0:T(8,128)(2,1)} %bitcast.334), kind=kOutput, calls=%fused_computation.47 | convolution fusion | flops 4297064448 | bytes 10485760 | tf_op jit(solution)/shard_map/dot_general | solution.py:31
  147.4 8.1 %convolution_convert_fusion.3.k_ref = bf16[2048,1024]{1,0:T(8,128)(2,1)} fusion(bf16[2048,1024]{1,0:T(8,128)(2,1)S(1)} %copy-done.13, bf16[2,4,1024,1024]{3,2,1,0:T(8,128)(2,1)} %bitcast.336), kind=kOutput, calls=%fused_computation.48 | convolution fusion | flops 4297064448 | bytes 10485760 | tf_op jit(solution)/shard_map/dot_general | solution.py:31
  155.5 17.9 %attend.2 = (bf16[512,1024]{1,0:T(8,128)(2,1)S(1)}, f32[2,8,2,256]{3,2,1,0:T(2,128)S(1)}) custom-call(s32[2,2]{1,0:T(2,128)S(1)} %get-tuple-element.248.first_ref, s32[2,2]{1,0:T(2,128)S(1)} %get-tuple-element.233.stop_ref, s32[2,1,256]{2,1,0:T(1,128)S(1)} %broadcast_in_dim.73.lo_ref, s32[2,1,256]{2,1,0:T(1,128)S(1)} %bitcast.268, ...), custom_call_target="tpu_custom_call" | custom-call | flops 8589934592 | bytes 18874368 | tf_op jit(solution)/shard_map/attend/pallas_call | solution.py:186
  173.4 3.4 fusion.22
  180.1 3.3 fusion.80.k_ref
  183.4 3.4 fusion.81.q_ref
  186.9 4.1 attend.3
  201.2 5.8 convolution_convert_fusion.1
  207.0 14.7 %collective-permute-done.4 = bf16[512,1024]{1,0:T(8,128)(2,1)} collective-permute-done((bf16[512,1024]{1,0:T(8,128)(2,1)S(1)}, bf16[512,1024]{1,0:T(8,128)(2,1)}, u32[]{:S(2)}, u32[]{:S(2)}) %collective-permute-start.4) | collective-permute-done | bytes 1048608 | tf_op jit(solution)/shard_map/ppermute | solution.py:346
  221.8 9.5 %fusion.107 = f32[1024,2816]{1,0:T(8,128)S(1)} fusion(bf16[1024,2816]{1,0:T(8,128)(2,1)} %bitcast.350, bf16[512,1024]{1,0:T(8,128)(2,1)} %collective-permute-done.4, bf16[512,1024]{1,0:T(8,128)(2,1)} %copy-done.51), kind=kOutput, calls=%fused_computation.196 | convolution fusion | flops 5909774336 | bytes 19398656 | tf_op jit(solution)/shard_map/dot_general | solution.py:31
  231.3 4.6 fusion.12
  239.2 7.9 %fusion.75 = bf16[512,1024]{1,0:T(8,128)(2,1)S(1)} fusion(bf16[1024,2816]{1,0:T(8,128)(2,1)} %bitcast.351, bf16[1024,2816]{1,0:T(8,128)(2,1)S(1)} %pad_maximum_fusion), kind=kOutput, calls=%fused_computation.150 | convolution fusion | flops 2953314304 | bytes 9699328 | tf_op jit(solution)/shard_map/dot_general | solution.py:39
  252.6 6.2 convolution_convert_fusion
  262.2 6.1 fusion.173
  276.8 6.9 %add_convert_fusion = bf16[1024,1408]{1,0:T(8,128)(2,1)S(1)} fusion(bf16[1024,1408]{1,0:T(8,128)(2,1)} %collective-permute-done.9, bf16[1024,2816]{1,0:T(8,128)(2,1)} %copy-done.22, s32[]{:T(128)S(6)} %select_n.318, bf16[512,1024]{1,0:T(8,128)(2,1)} %collective-permute-done.4, bf16[512,1024]{1,0:T(8,128)(2,1)} %copy-done.51), kind=kOutput, calls=%fused_computation.25 | convolution fusion | flops 2961309696 | bytes 10747908 | tf_op jit(solution)/shard_map/dot_general | solution.py:35
  283.7 5.3 collective-permute-done.8
  289.0 8.2 %multiply_reduce_fusion = (f32[1024]{0:T(1024)}, f32[512]{0:T(512)S(1)}, f32[512,1024]{1,0:T(8,128)}) fusion(f32[512,1024]{1,0:T(8,128)S(1)} %get-tuple-element.245, f32[512]{0:T(512)S(1)} %get-tuple-element.229, bf16[256,1024]{1,0:T(8,128)(2,1)} %collective-permute-done.8, bf16[256,1024]{1,0:T(8,128)(2,1)} %collective-permute-done.7, ...), kind=kOutput, calls=%fused_computation.95 | convolution fusion | flops 2958555648 | bytes 13905920 | tf_op jit(solution)/shard_map/dot_general | solution.py:39
  299.8 3.9 fusion.164
  303.7 4.3 fusion.78.dc_ref
  308.0 11.5 %attend_back.2 = (bf16[512,1024]{1,0:T(8,128)(2,1)S(1)}, bf16[512,1024]{1,0:T(8,128)(2,1)S(1)}, bf16[512,1024]{1,0:T(8,128)(2,1)S(1)}) custom-call(s32[2,2]{1,0:T(2,128)S(1)} %get-tuple-element.251.first_ref, s32[2,2]{1,0:T(2,128)S(1)} %get-tuple-element.250.stop_ref, s32[2,1,256]{2,1,0:T(1,128)S(1)} %broadcast_in_dim.83.lo_ref, ...), custom_call_target="tpu_custom_call" | custom-call | flops 5368709120 | bytes 6291456 | tf_op jit(solution)/shard_map/attend_back/pallas_call | solution.py:210
  325.9 5.5 collective-permute-done.11
  335.7 3.5 convolution_bitcast_fusion.2
  352.1 4.2 fusion.31
  365.4 3.3 fusion
  372.7 31.3 %attend_back.3 = (bf16[512,1024]{1,0:T(8,128)(2,1)S(1)}, bf16[2048,1024]{1,0:T(8,128)(2,1)}, bf16[2048,1024]{1,0:T(8,128)(2,1)}) custom-call(s32[2,2]{1,0:T(2,128)S(1)} %get-tuple-element.249.first_ref, s32[2,2]{1,0:T(2,128)S(1)} %get-tuple-element.232.stop_ref, s32[2,1,256]{2,1,0:T(1,128)S(1)} %broadcast_in_dim.73.lo_ref, s32[2,1,256]{2,1,0:T(1,128)S(1)} %bitcast.269, ...), custom_call_target="tpu_custom_call" | custom-call | flops 21474836480 | bytes 18874368 | tf_op jit(solution)/shard_map/attend_back/pallas_call | solution.py:210
  404.0 4.1 fusion.84
  419.5 3.7 fusion.66
  423.2 3.7 fusion.63
  431.5 13.7 %collective-permute-done.24 = bf16[352,256]{1,0:T(8,128)(2,1)S(1)} collective-permute-done((bf16[352,256]{1,0:T(8,128)(2,1)S(1)}, bf16[352,256]{1,0:T(8,128)(2,1)S(1)}, u32[]{:S(2)}, u32[]{:S(2)}) %collective-permute-start.24) | collective-permute-done | bytes 180256 | tf_op jit(solution)/shard_map/ppermute | solution.py:364
  446.7 3.7 fusion.16
  450.7 4.0 fusion.15
  462.5 7.1 %fusion.47 = f32[2048,1024]{1,0:T(8,128)S(1)} fusion(bf16[2048,1024]{1,0:T(8,128)(2,1)} %get-tuple-element.134, bf16[2,4,1024,1024]{3,2,1,0:T(8,128)(2,1)} %bitcast.347), kind=kOutput, calls=%fused_computation.126 | convolution fusion | flops 4294967296 | bytes 14680064 | tf_op jit(solution)/shard_map/dot_general | solution.py:39
  469.6 8.6 %convolution_add_fusion = f32[2048,1024]{1,0:T(8,128)} fusion(f32[2048,1024]{1,0:T(8,128)S(1)} %fusion.47, bf16[2048,1024]{1,0:T(8,128)(2,1)S(1)} %copy-done.54, bf16[2,4,1024,1024]{3,2,1,0:T(8,128)(2,1)} %bitcast.348), kind=kOutput, calls=%fused_computation.44 | convolution fusion | flops 4297064448 | bytes 23068672 | tf_op jit(solution)/shard_map/dot_general | solution.py:39
  488.4 24.0 %all-gather.1 = bf16[1408,256]{1,0:T(8,128)(2,1)S(1)} all-gather(bf16[352,256]{1,0:T(8,128)(2,1)S(1)} %add_convert_fusion.12), channel_id=3, replica_groups=mesh['section'=2,'group'=4,'dp'=4] {'group'}, dimensions={0}, use_global_device_ids=true | all-gather | bytes 901120 | tf_op jit(solution)/shard_map/all_gather | solution.py:440
  514.6 12.1 %collective-permute-done.23 = bf16[2,1024,128]{2,1,0:T(8,128)(2,1)S(1)} collective-permute-done((bf16[2,1024,128]{2,1,0:T(8,128)(2,1)S(1)}, bf16[2,1024,128]{2,1,0:T(8,128)(2,1)S(1)}, u32[]{:S(2)}, u32[]{:S(2)}) %collective-permute-start.23) | collective-permute-done | bytes 524320 | tf_op jit(solution)/shard_map/ppermute | solution.py:364
  527.9 6.1 fusion.9
  536.3 4.6 fusion.60
  541.0 8.6 %fusion.1 = bf16[2048,1024]{1,0:T(8,128)(2,1)S(1)} fusion(f32[2,1024,1024]{2,1,0:T(8,128)} %fusion.60, f32[2048,1024]{1,0:T(8,128)} %convolution_add_fusion, f32[2048]{0:T(1024)S(1)} %broadcast_multiply_fusion, f32[2048]{0:T(1024)S(1)} %copy-done.71, f32[1024]{0:T(1024)S(1)} %bitcast.297, f32[2048]{0:T(1024)S(1)} %bitcast.294, ...), kind=kLoop, calls=%fused_computation.3 | loop fusion | flops 16777216 | bytes 25194500 | tf_op jit(solution)/shard_map/convert_element_type | solution.py:469
  558.4 13.5 %all-gather.4 = f32[4,4,1024]{2,1,0:T(4,128)S(1)} all-gather(f32[1,4,1024]{2,1,0:T(4,128)S(1)} %add_bitcast_fusion), channel_id=5, replica_groups=mesh['section'=2,'group'=4,'dp'=4] {'dp'}, dimensions={0}, use_global_device_ids=true | all-gather | bytes 81920 | tf_op jit(solution)/shard_map/all_gather | solution.py:485
  571.9 4.9 collective-permute-done.29
  579.2 5.3 collective-permute-done.30
  592.3 8.4 %maximum_convert_fusion = f32[128,5632]{1,0:T(8,128)} fusion(bf16[64,1408]{1,0:T(8,128)(2,1)S(1)} %get-tuple-element.201, bf16[64,1408]{1,0:T(8,128)(2,1)S(1)} %get-tuple-element.202, bf16[64,1408]{1,0:T(8,128)(2,1)S(1)} %get-tuple-element.203, bf16[64,1408]{1,0:T(8,128)(2,1)S(1)} %get-tuple-element.204, bf16[64,1408]{1,0:T(8,128)(2,1)S(1)} %get-tuple-element.205, ...), kind=kLoop, calls=%fused_computation.164 | loop fusion | flops 11534336 | bytes 4325376 | tf_op jit(solution)/shard_map/concatenate | solution.py:476
  601.4 11.6 %collective-permute-done.31 = bf16[1024,512]{1,0:T(8,128)(2,1)} collective-permute-done((bf16[1024,512]{1,0:T(8,128)(2,1)S(1)}, bf16[1024,512]{1,0:T(8,128)(2,1)}, u32[]{:S(2)}, u32[]{:S(2)}) %collective-permute-start.31) | collective-permute-done | bytes 1048608 | tf_op jit(solution)/shard_map/ppermute | solution.py:487
  (391 shorter events, 168.0 us)
Async XLA Ops:
  7.2 14.2 %copy-start = (s32[4,256]{1,0:T(4,128)S(1)}, s32[4,256]{1,0:T(4,128)}, u32[]{:S(2)}) copy-start(s32[4,256]{1,0:T(4,128)} %param.11) | copy-start | bytes 12292
  7.2 126.4 %all-gather.14.cloned.1.call-start = ((), (), s32[]{:S(2)}) async-start(), calls=%async_computation.10 | async-start | bytes 17301504 | tf_op jit(solution)/shard_map/all_gather | solution.py:264
  9.3 212.5 %all-gather.10.cloned.1.call-start = ((), (), s32[]{:S(2)}) async-start(), calls=%async_computation.4 | async-start | bytes 6127616 | tf_op jit(solution)/shard_map/all_gather | solution.py:287
  10.4 33.8 %collective-permute-start = (bf16[88,1024]{1,0:T(8,128)(2,1)S(1)}, bf16[88,1024]{1,0:T(8,128)(2,1)}, u32[]{:S(2)}, u32[]{:S(2)}) collective-permute-start(bf16[88,1024]{1,0:T(8,128)(2,1)S(1)} %get-tuple-element.172), channel_id=1, source_target_pairs={{0,1},{1,2},{2,3},{3,0},{4,5},{5,6},{6,7},{7,4},{8,9},{9,10},{10,1... | collective-permute-start | bytes 540680 | tf_op jit(solution)/shard_map/ppermute | solution.py:293
  13.5 31.7 %collective-permute-start.1 = (bf16[88,1024]{1,0:T(8,128)(2,1)S(1)}, bf16[88,1024]{1,0:T(8,128)(2,1)S(1)}, u32[]{:S(2)}, u32[]{:S(2)}) collective-permute-start(bf16[88,1024]{1,0:T(8,128)(2,1)S(1)} %get-tuple-element.172), channel_id=1, source_target_pairs={{0,2},{1,3},{2,0},{3,1},{4,6},{5,7},{6,4},{7,5},{8,10},{9,11},{10,... | collective-permute-start | bytes 540680 | tf_op jit(solution)/shard_map/ppermute | solution.py:293
  16.1 29.1 %collective-permute-start.2 = (bf16[88,1024]{1,0:T(8,128)(2,1)S(1)}, bf16[88,1024]{1,0:T(8,128)(2,1)S(1)}, u32[]{:S(2)}, u32[]{:S(2)}) collective-permute-start(bf16[88,1024]{1,0:T(8,128)(2,1)S(1)} %get-tuple-element.172), channel_id=1, source_target_pairs={{0,3},{1,0},{2,1},{3,2},{4,7},{5,4},{6,5},{7,6},{8,11},{9,8},{10,9... | collective-permute-start | bytes 540680 | tf_op jit(solution)/shard_map/ppermute | solution.py:293
  18.7 11.1 %collective-permute-start.6 = (bf16[32,2816]{1,0:T(8,128)(2,1)S(1)}, bf16[32,2816]{1,0:T(8,128)(2,1)S(1)}, u32[]{:S(2)}, u32[]{:S(2)}) collective-permute-start(bf16[32,2816]{1,0:T(8,128)(2,1)S(1)} %pad_maximum_fusion.15), channel_id=1, source_target_pairs={{0,16},{16,0},{1,17},{17,1},{2,18},{18,2},{3,19},{19,3},{4,20},{20... | collective-permute-start | bytes 540680 | tf_op jit(solution)/shard_map/ppermute | solution.py:285
  30.6 303.6 %reduce-scatter.5.cloned.1.call-start = ((), (), s32[]{:S(2)}) async-start(), calls=%async_computation.5 | async-start | bytes 1802240 | tf_op jit(solution)/shard_map/reduce_scatter | solution.py:377
  31.3 302.8 %copy-start.69 = (f32[1,2,2,128]{3,1,2,0:T(2,128)}, f32[1,2,2,128]{3,1,2,0:T(2,128)S(1)}, u32[]{:S(2)}) copy-start(f32[1,2,2,128]{3,1,2,0:T(2,128)S(1)} %copy.30) | copy-start | bytes 6148
  39.2 134.2 %copy-start.18 = (f32[512,1024]{1,0:T(8,128)}, f32[512,1024]{1,0:T(8,128)S(1)}, u32[]{:S(2)}) copy-start(f32[512,1024]{1,0:T(8,128)S(1)} %get-tuple-element.174) | copy-start | bytes 6291460
  143.1 48.0 %collective-permute-start.3 = (bf16[4,88,1024]{2,1,0:T(8,128)(2,1)S(1)}, bf16[4,88,1024]{2,1,0:T(8,128)(2,1)S(1)}, u32[]{:S(2)}, u32[]{:S(2)}) collective-permute-start(bf16[4,88,1024]{2,1,0:T(8,128)(2,1)S(1)} %bitcast_dynamic-update-slice_fusion), channel_id=1, source_target_pairs={{0,8},{4,12},{8,0},{12,4},{1,9},{5,13},{9,1},{13,5},{2,10},{6,14},... | collective-permute-start | bytes 2162696 | tf_op jit(solution)/shard_map/ppermute | solution.py:276
  192.4 5.5 collective-permute-start.5
  196.0 25.7 %collective-permute-start.4 = (bf16[512,1024]{1,0:T(8,128)(2,1)S(1)}, bf16[512,1024]{1,0:T(8,128)(2,1)}, u32[]{:S(2)}, u32[]{:S(2)}) collective-permute-start(bf16[512,1024]{1,0:T(8,128)(2,1)S(1)} %multiply_convert_fusion.1), channel_id=1, source_target_pairs={{0,16},{16,0},{1,17},{17,1},{2,18},{18,2},{3,19},{19,3},{4,20},{20... | collective-permute-start | bytes 3145736 | tf_op jit(solution)/shard_map/ppermute | solution.py:346
  248.0 13.6 %collective-permute-start.7 = (bf16[256,1024]{1,0:T(8,128)(2,1)S(1)}, bf16[256,1024]{1,0:T(8,128)(2,1)}, u32[]{:S(2)}, u32[]{:S(2)}) collective-permute-start(bf16[256,1024]{1,0:T(8,128)(2,1)S(1)} %get-tuple-element.213), channel_id=1, source_target_pairs={{0,16},{16,0},{1,17},{17,1},{2,18},{18,2},{3,19},{19,3},{4,20},{20... | collective-permute-start | bytes 1572872 | tf_op jit(solution)/shard_map/ppermute | solution.py:393
  261.7 15.1 %collective-permute-start.9 = (bf16[1024,1408]{1,0:T(8,128)(2,1)}, bf16[1024,1408]{1,0:T(8,128)(2,1)}, u32[]{:S(2)}, u32[]{:S(2)}) collective-permute-start(bf16[1024,1408]{1,0:T(8,128)(2,1)} %convolution_convert_fusion), channel_id=1, source_target_pairs={{0,4},{4,0},{8,12},{12,8},{1,5},{5,1},{9,13},{13,9},{2,6},{6,2},{1... | collective-permute-start | bytes 8650760 | tf_op jit(solution)/shard_map/ppermute | solution.py:387
  261.7 13.5 %collective-permute-start.10 = (bf16[1408,512]{1,0:T(8,128)(2,1)}, bf16[1408,512]{1,0:T(8,128)(2,1)S(1)}, u32[]{:S(2)}, u32[]{:S(2)}) collective-permute-start(bf16[1408,512]{1,0:T(8,128)(2,1)} %convolution_convert_fusion.4), channel_id=1, source_target_pairs={{0,4},{4,0},{8,12},{12,8},{1,5},{5,1},{9,13},{13,9},{2,6},{6,2},{1... | collective-permute-start | bytes 4325384 | tf_op jit(solution)/shard_map/ppermute | solution.py:387
  274.8 14.2 %collective-permute-start.8 = (bf16[256,1024]{1,0:T(8,128)(2,1)}, bf16[256,1024]{1,0:T(8,128)(2,1)}, u32[]{:S(2)}, u32[]{:S(2)}) collective-permute-start(bf16[256,1024]{1,0:T(8,128)(2,1)} %get-tuple-element.99), channel_id=1, source_target_pairs={{0,16},{16,0},{1,17},{17,1},{2,18},{18,2},{3,19},{19,3},{4,20},{20... | collective-permute-start | bytes 1572872 | tf_op jit(solution)/shard_map/ppermute | solution.py:397
  283.7 13.5 %copy-start.38 = (bf16[1024,1408]{1,0:T(8,128)(2,1)}, bf16[1024,1408]{1,0:T(8,128)(2,1)S(1)}, u32[]{:S(2)}) copy-start(bf16[1024,1408]{1,0:T(8,128)(2,1)S(1)} %add_convert_fusion) | copy-start | bytes 8650756
  298.4 32.9 %collective-permute-start.11 = (bf16[2,4,1,64,1408]{4,3,2,1,0:T(8,128)(2,1)}, bf16[2,4,1,64,1408]{4,3,2,1,0:T(8,128)(2,1)}, u32[]{:S(2)}, u32[]{:S(2)}) collective-permute-start(bf16[2,4,1,64,1408]{4,3,2,1,0:T(8,128)(2,1)} %constant_dynamic-slice_fusion.11), channel_id=1, source_target_pairs={{0,8},{4,12},{8,0},{12,4},{1,9},{5,13},{9,1},{13,5},{2,10},{6,14},... | collective-permute-start | bytes 4325384 | tf_op jit(solution)/shard_map/ppermute | solution.py:364
  299.4 155.4 %reduce-scatter.7.cloned.1.call-start = ((), (), s32[]{:S(2)}) async-start(), calls=%async_computation.6 | async-start | bytes 1802240 | tf_op jit(solution)/shard_map/reduce_scatter | solution.py:377
  303.7 15.9 %copy-start.50 = (bf16[512,1024]{1,0:T(8,128)(2,1)}, bf16[512,1024]{1,0:T(8,128)(2,1)S(1)}, u32[]{:S(2)}) copy-start(bf16[512,1024]{1,0:T(8,128)(2,1)S(1)} %get-tuple-element.169) | copy-start | bytes 3145732
  334.2 30.2 %collective-permute-start.12 = (bf16[4,1024,512]{2,1,0:T(8,128)(2,1)}, bf16[4,1024,512]{2,1,0:T(8,128)(2,1)}, u32[]{:S(2)}, u32[]{:S(2)}) collective-permute-start(bf16[4,1024,512]{2,1,0:T(8,128)(2,1)} %pad_maximum_fusion.1), channel_id=1, source_target_pairs={{0,4},{4,0},{8,12},{12,8},{1,5},{5,1},{9,13},{13,9},{2,6},{6,2},{1... | collective-permute-start | bytes 12582920 | tf_op jit(solution)/shard_map/ppermute | solution.py:387
  335.4 33.4 %collective-permute-start.13 = (bf16[1024,512]{1,0:T(8,128)(2,1)}, bf16[1024,512]{1,0:T(8,128)(2,1)}, u32[]{:S(2)}, u32[]{:S(2)}) collective-permute-start(bf16[1024,512]{1,0:T(8,128)(2,1)} %fusion.33), channel_id=1, source_target_pairs={{0,16},{16,0},{1,17},{17,1},{2,18},{18,2},{3,19},{19,3},{4,20},{20... | collective-permute-start | bytes 3145736 | tf_op jit(solution)/shard_map/ppermute | solution.py:405
  345.7 182.1 %reduce-scatter.9.cloned.1.call-start = ((), (), s32[]{:S(2)}) async-start(), calls=%async_computation.7 | async-start | bytes 1310720 | tf_op jit(solution)/shard_map/reduce_scatter | solution.py:377
  369.1 43.5 %collective-permute-start.15 = (bf16[2,1024,256]{2,1,0:T(8,128)(2,1)S(1)}, bf16[2,1024,256]{2,1,0:T(8,128)(2,1)}, u32[]{:S(2)}, u32[]{:S(2)}) collective-permute-start(bf16[2,1024,256]{2,1,0:T(8,128)(2,1)S(1)} %constant_dynamic-slice_fusion.9), channel_id=1, source_target_pairs={{0,8},{4,12},{8,0},{12,4},{1,9},{5,13},{9,1},{13,5},{2,10},{6,14},... | collective-permute-start | bytes 3145736 | tf_op jit(solution)/shard_map/ppermute | solution.py:364
  371.0 43.2 %collective-permute-start.14 = (bf16[2,1024,256]{2,1,0:T(8,128)(2,1)}, bf16[2,1024,256]{2,1,0:T(8,128)(2,1)}, u32[]{:S(2)}, u32[]{:S(2)}) collective-permute-start(bf16[2,1024,256]{2,1,0:T(8,128)(2,1)} %constant_dynamic-slice_fusion.10), channel_id=1, source_target_pairs={{0,16},{16,0},{1,17},{17,1},{2,18},{18,2},{3,19},{19,3},{4,20},{20... | collective-permute-start | bytes 3145736 | tf_op jit(solution)/shard_map/ppermute | solution.py:364
  372.7 31.3 %copy-start.14 = (bf16[2048,1024]{1,0:T(8,128)(2,1)S(1)}, bf16[2048,1024]{1,0:T(8,128)(2,1)}, u32[]{:S(2)}) copy-start(bf16[2048,1024]{1,0:T(8,128)(2,1)} %fusion.4) | copy-start | bytes 12582916
  418.0 28.6 %collective-permute-start.17 = (bf16[2,1024,512]{2,1,0:T(8,128)(2,1)S(1)}, bf16[2,1024,512]{2,1,0:T(8,128)(2,1)}, u32[]{:S(2)}, u32[]{:S(2)}) collective-permute-start(bf16[2,1024,512]{2,1,0:T(8,128)(2,1)S(1)} %pad_maximum_fusion.6), channel_id=1, source_target_pairs={{0,4},{4,0},{8,12},{12,8},{1,5},{5,1},{9,13},{13,9},{2,6},{6,2},{1... | collective-permute-start | bytes 6291464 | tf_op jit(solution)/shard_map/ppermute | solution.py:387
  423.2 27.2 %collective-permute-start.16 = (bf16[2,1024,512]{2,1,0:T(8,128)(2,1)}, bf16[2,1024,512]{2,1,0:T(8,128)(2,1)}, u32[]{:S(2)}, u32[]{:S(2)}) collective-permute-start(bf16[2,1024,512]{2,1,0:T(8,128)(2,1)} %pad_maximum_fusion.5), channel_id=1, source_target_pairs={{0,4},{4,0},{8,12},{12,8},{1,5},{5,1},{9,13},{13,9},{2,6},{6,2},{1... | collective-permute-start | bytes 6291464 | tf_op jit(solution)/shard_map/ppermute | solution.py:387
  426.9 18.3 %collective-permute-start.18 = (bf16[2,1024,128]{2,1,0:T(8,128)(2,1)S(1)}, bf16[2,1024,128]{2,1,0:T(8,128)(2,1)S(1)}, u32[]{:S(2)}, u32[]{:S(2)}) collective-permute-start(bf16[2,1024,128]{2,1,0:T(8,128)(2,1)S(1)} %constant_dynamic-slice_fusion.8), channel_id=1, source_target_pairs={{0,8},{4,12},{8,0},{12,4},{1,9},{5,13},{9,1},{13,5},{2,10},{6,14},... | collective-permute-start | bytes 1572872 | tf_op jit(solution)/shard_map/ppermute | solution.py:364
  428.3 17.1 %collective-permute-start.19 = (bf16[2,1024,128]{2,1,0:T(8,128)(2,1)S(1)}, bf16[2,1024,128]{2,1,0:T(8,128)(2,1)S(1)}, u32[]{:S(2)}, u32[]{:S(2)}) collective-permute-start(bf16[2,1024,128]{2,1,0:T(8,128)(2,1)S(1)} %constant_dynamic-slice_fusion.7), channel_id=1, source_target_pairs={{0,16},{16,0},{1,17},{17,1},{2,18},{18,2},{3,19},{19,3},{4,20},{20... | collective-permute-start | bytes 1572872 | tf_op jit(solution)/shard_map/ppermute | solution.py:364
  428.4 16.7 %collective-permute-start.24 = (bf16[352,256]{1,0:T(8,128)(2,1)S(1)}, bf16[352,256]{1,0:T(8,128)(2,1)S(1)}, u32[]{:S(2)}, u32[]{:S(2)}) collective-permute-start(bf16[352,256]{1,0:T(8,128)(2,1)S(1)} %constant_dynamic-slice_fusion.2), channel_id=1, source_target_pairs={{0,8},{4,12},{8,0},{12,4},{1,9},{5,13},{9,1},{13,5},{2,10},{6,14},... | collective-permute-start | bytes 540680 | tf_op jit(solution)/shard_map/ppermute | solution.py:364
  456.6 21.6 %collective-permute-start.25 = (bf16[64,1408]{1,0:T(8,128)(2,1)}, bf16[64,1408]{1,0:T(8,128)(2,1)}, u32[]{:S(2)}, u32[]{:S(2)}) collective-permute-start(bf16[64,1408]{1,0:T(8,128)(2,1)} %get-tuple-element.221), channel_id=1, source_target_pairs={{0,16},{16,0},{1,17},{17,1},{2,18},{18,2},{3,19},{19,3},{4,20},{20... | collective-permute-start | bytes 540680 | tf_op jit(solution)/shard_map/ppermute | solution.py:449
  458.1 25.1 %collective-permute-start.21 = (bf16[2,1024,256]{2,1,0:T(8,128)(2,1)}, bf16[2,1024,256]{2,1,0:T(8,128)(2,1)}, u32[]{:S(2)}, u32[]{:S(2)}) collective-permute-start(bf16[2,1024,256]{2,1,0:T(8,128)(2,1)} %constant_dynamic-slice_fusion.5), channel_id=1, source_target_pairs={{0,8},{4,12},{8,0},{12,4},{1,9},{5,13},{9,1},{13,5},{2,10},{6,14},... | collective-permute-start | bytes 3145736 | tf_op jit(solution)/shard_map/ppermute | solution.py:364
  460.4 25.2 %collective-permute-start.20 = (bf16[2,1024,256]{2,1,0:T(8,128)(2,1)}, bf16[2,1024,256]{2,1,0:T(8,128)(2,1)}, u32[]{:S(2)}, u32[]{:S(2)}) collective-permute-start(bf16[2,1024,256]{2,1,0:T(8,128)(2,1)} %constant_dynamic-slice_fusion.6), channel_id=1, source_target_pairs={{0,16},{16,0},{1,17},{17,1},{2,18},{18,2},{3,19},{19,3},{4,20},{20... | collective-permute-start | bytes 3145736 | tf_op jit(solution)/shard_map/ppermute | solution.py:364
  462.4 65.5 %all-gather.16.cloned.1.call-start = ((), (), s32[]{:S(2)}) async-start(), calls=%async_computation.11 | async-start | bytes 1802240 | tf_op jit(solution)/shard_map/all_gather | solution.py:440
  480.0 96.8 %reduce-scatter.11.cloned.1.call-start = ((), (), s32[]{:S(2)}) async-start(), calls=%async_computation.8 | async-start | bytes 1310720 | tf_op jit(solution)/shard_map/reduce_scatter | solution.py:377
  487.1 27.3 %collective-permute-start.22 = (bf16[2,1024,128]{2,1,0:T(8,128)(2,1)S(1)}, bf16[2,1024,128]{2,1,0:T(8,128)(2,1)S(1)}, u32[]{:S(2)}, u32[]{:S(2)}) collective-permute-start(bf16[2,1024,128]{2,1,0:T(8,128)(2,1)S(1)} %constant_dynamic-slice_fusion.4), channel_id=1, source_target_pairs={{0,8},{4,12},{8,0},{12,4},{1,9},{5,13},{9,1},{13,5},{2,10},{6,14},... | collective-permute-start | bytes 1572872 | tf_op jit(solution)/shard_map/ppermute | solution.py:364
  512.4 14.2 %collective-permute-start.23 = (bf16[2,1024,128]{2,1,0:T(8,128)(2,1)S(1)}, bf16[2,1024,128]{2,1,0:T(8,128)(2,1)S(1)}, u32[]{:S(2)}, u32[]{:S(2)}) collective-permute-start(bf16[2,1024,128]{2,1,0:T(8,128)(2,1)S(1)} %constant_dynamic-slice_fusion.3), channel_id=1, source_target_pairs={{0,16},{16,0},{1,17},{17,1},{2,18},{18,2},{3,19},{19,3},{4,20},{20... | collective-permute-start | bytes 1572872 | tf_op jit(solution)/shard_map/ppermute | solution.py:364
  534.8 17.2 %collective-permute-start.26 = (f32[4,1024]{1,0:T(4,128)S(1)}, f32[4,1024]{1,0:T(4,128)S(1)}, u32[]{:S(2)}, u32[]{:S(2)}) collective-permute-start(f32[4,1024]{1,0:T(4,128)S(1)} %pad_maximum_fusion.16), channel_id=1, source_target_pairs={{0,16},{16,0},{1,17},{17,1},{2,18},{18,2},{3,19},{19,3},{4,20},{20... | collective-permute-start | bytes 49160 | tf_op jit(solution)/shard_map/ppermute | solution.py:475
  541.0 72.0 %all-gather.12.cloned.1.call-start = ((), (), s32[]{:S(2)}) async-start(), calls=%async_computation.9 | async-start | bytes 2621440 | tf_op jit(solution)/shard_map/all_gather | solution.py:440
  549.7 27.2 %copy-start.62 = (bf16[4,256,128]{2,1,0:T(8,128)(2,1)S(1)}, bf16[4,256,128]{2,1,0:T(8,128)(2,1)}, u32[]{:S(2)}) copy-start(bf16[4,256,128]{2,1,0:T(8,128)(2,1)} %reduce-scatter.9.cloned.1.call-done) | copy-start | bytes 786436
  552.0 33.5 %copy-start.16 = (f32[512,1024]{1,0:T(8,128)S(1)}, f32[512,1024]{1,0:T(8,128)}, u32[]{:S(2)}) copy-start(f32[512,1024]{1,0:T(8,128)} %copy-done.15) | copy-start | bytes 6291460
  552.0 24.8 %collective-permute-start.29 = (bf16[1024,512]{1,0:T(8,128)(2,1)}, bf16[1024,512]{1,0:T(8,128)(2,1)}, u32[]{:S(2)}, u32[]{:S(2)}) collective-permute-start(bf16[1024,512]{1,0:T(8,128)(2,1)} %get-tuple-element.148), channel_id=1, source_target_pairs={{0,16},{16,0},{1,17},{17,1},{2,18},{18,2},{3,19},{19,3},{4,20},{20... | collective-permute-start | bytes 3145736 | tf_op jit(solution)/shard_map/ppermute | solution.py:482
  553.5 1.2 collective-permute-start.27
  554.7 3.7 collective-permute-start.28
  577.8 6.7 %collective-permute-start.30 = (bf16[4,256,128]{2,1,0:T(8,128)(2,1)S(1)}, bf16[4,256,128]{2,1,0:T(8,128)(2,1)S(1)}, u32[]{:S(2)}, u32[]{:S(2)}) collective-permute-start(bf16[4,256,128]{2,1,0:T(8,128)(2,1)S(1)} %get-tuple-element.219), channel_id=1, source_target_pairs={{0,16},{16,0},{1,17},{17,1},{2,18},{18,2},{3,19},{19,3},{4,20},{20... | collective-permute-start | bytes 786440 | tf_op jit(solution)/shard_map/ppermute | solution.py:490
  590.3 22.7 %collective-permute-start.31 = (bf16[1024,512]{1,0:T(8,128)(2,1)S(1)}, bf16[1024,512]{1,0:T(8,128)(2,1)}, u32[]{:S(2)}, u32[]{:S(2)}) collective-permute-start(bf16[1024,512]{1,0:T(8,128)(2,1)S(1)} %get-tuple-element.152), channel_id=1, source_target_pairs={{0,16},{16,0},{1,17},{17,1},{2,18},{18,2},{3,19},{19,3},{4,20},{20... | collective-permute-start | bytes 3145736 | tf_op jit(solution)/shard_map/ppermute | solution.py:487
  (76 other events, 356.9 us)
Sparse Core Ops, SparseCore 0:
  11.6 121.9 all-gather.13
  136.5 60.1 all-gather.9
  299.5 30.8 reduce-scatter.4
  345.8 31.4 reduce-scatter.6
  462.5 23.8 reduce-scatter.8
  488.5 23.8 all-gather.15
  541.1 25.9 reduce-scatter.10
  585.6 20.6 all-gather.11

commit v13 on v11

--- a/solution.py
+++ b/solution.py
@@ -481,14 +481,15 @@
     for pairs in (core_pairs, side_pairs):
         gain_grads = gain_grads + lax.ppermute(gain_grads, "group", pairs)
     gain_grads = jnp.sum(lax.all_gather(gain_grads, "dp", axis=0, tiled=False), axis=0)
-    ffn_gdown = laid_out(gathered(sum_down), (0, 2, 1, 3))
-    late, gain_grads, sum_one, bytes_got, ffn_gdown = together(
-        (other[rows - 1], gain_grads, sum_one, bytes_got, ffn_gdown)
+    late, gain_grads, sum_one, bytes_got, sum_down = together(
+        (other[rows - 1], gain_grads, sum_one, bytes_got, sum_down)
     )
     bytes_got.append(lax.ppermute(late, "section", swap))
     kept = jnp.where(section == 0, sum_one, sum_two)
     sent = jnp.where(section == 0, sum_two, sum_one)
     got = lax.ppermute(sent, "section", swap)
+    got, sum_down = together((got, sum_down))
+    ffn_gdown = laid_out(gathered(sum_down), (0, 2, 1, 3))
     eighths = jnp.where(
         section == 0, jnp.concatenate([kept, got], axis=2), jnp.concatenate([got, kept], axis=2)
     )

time: 620 us -> 612 us (0.987)
  waiting for transfers between devices: 166 us -> 150 us
  starting transfers between devices: 27.8 us -> 38.7 us
    ppermute x1, waiting for transfers between devices: 13.3 us -> 2.87 us  [shards(): bytes_got.append(lax.ppermute(late, 'section', swap))]
    unnamed x173 -> x171, local copies, waits for them, and re-layouts: 15.9 us -> 14.6 us
  transfers between devices with their start and end apart: 40 -> 40, of which waited for: 14 -> 14; matrix products, arithmetic and copies ran while one was open for 39% -> 40% of each run, Pallas kernels for 11% -> 10%
where the time goes in v13:
time: 612 us; the launch traced here: 608 us
  matrix products  168 us (27%)
  waiting for transfers between devices  150 us (25%)
  other arithmetic  113 us (18%)
  Pallas kernels  60.9 us (10%)
  starting transfers between devices  38.7 us (6%)
  local copies, waits for them, and re-layouts  34.2 us (6%)
  blocking collectives  26.7 us (4%)
  between operations  15.9 us (3%)
    all_gather x1, waiting for transfers between devices, shards(): lax.all_gather(matrix, ('section', 'group', 'dp'), axis=0, tiled=True)  87.2 us
    dot_general x11, matrix products, nt(): lax.dot_general(left, right, (((1,), (1,)), ((), ())), preferred_element_...  57 us
    dot_general x10, matrix products, nn(): return jnp.dot(left, right, preferred_element_type=F32)  52.6 us
    dot_general x20, matrix products, tn(): lax.dot_general(left, right, (((0,), (0,)), ((), ())), preferred_element_...  50.4 us
    pallas_call x2, Pallas kernels, attend_back(): pl.pallas_call(functools.partial(attend_back_kernel, chunk, spans), grid_...  40 us
    ppermute x10, waiting for transfers between devices, exchanged(): lax.ppermute(other, axis, pairs).astype(F32)  28.5 us
    pallas_call x2, Pallas kernels, attend(): pl.pallas_call(functools.partial(attend_kernel, chunk, spans), grid_spec=...  21 us
    unnamed x171, local copies, waits for them, and re-layouts  14.6 us
  transfers between devices with their start and end apart: 40, of which 14 were waited for; matrix products, arithmetic and copies ran while one was open for 40% of the time, Pallas kernels for 10%

profile of v13, /device:TPU:0, one launch (start us, length us, event | category | flops | bytes accessed | tf_op | source)
XLA Modules:
  0.0 608.2 jit_solution(6924965629423954338)
XLA Ops:
  22.2 3.9 multiply_reduce_fusion.5
  26.1 3.8 fusion.2
  32.6 4.7 all_gather.31
  37.4 4.2 fusion.4
  46.4 87.2 %all-gather.14.cloned.1.call-done = bf16[1,8192,1024]{2,1,0:T(8,128)(2,1)} async-done(((bf16[1,256,1024]{2,1,0:T(8,128)(2,1)}), bf16[1,8192,1024]{2,1,0:T(8,128)(2,1)}) %all-gather.14.cloned.1.call-update) | async-done | bytes 16777232 | tf_op jit(solution)/shard_map/all_gather | solution.py:264
  133.6 9.4 %convolution_convert_fusion.2.v_ref = bf16[2048,1024]{1,0:T(8,128)(2,1)} fusion(bf16[2048,1024]{1,0:T(8,128)(2,1)} %bitcast.281, bf16[2,4,1024,1024]{3,2,1,0:T(8,128)(2,1)} %bitcast.343), kind=kOutput, calls=%fused_computation.50 | convolution fusion | flops 4297064448 | bytes 10485760 | tf_op jit(solution)/shard_map/dot_general | solution.py:31
  147.6 8.0 %convolution_convert_fusion.3.k_ref = bf16[2048,1024]{1,0:T(8,128)(2,1)} fusion(bf16[2048,1024]{1,0:T(8,128)(2,1)S(1)} %bitcast.282, bf16[2,4,1024,1024]{3,2,1,0:T(8,128)(2,1)} %bitcast.345), kind=kOutput, calls=%fused_computation.51 | convolution fusion | flops 4297064448 | bytes 10485760 | tf_op jit(solution)/shard_map/dot_general | solution.py:31
  155.5 16.9 %attend.2 = (bf16[512,1024]{1,0:T(8,128)(2,1)S(1)}, f32[2,8,2,256]{3,2,1,0:T(2,128)S(1)}) custom-call(s32[2,2]{1,0:T(2,128)S(1)} %get-tuple-element.250.first_ref, s32[2,2]{1,0:T(2,128)S(1)} %get-tuple-element.235.stop_ref, s32[2,1,256]{2,1,0:T(1,128)S(1)} %broadcast_in_dim.73.lo_ref, s32[2,1,256]{2,1,0:T(1,128)S(1)} %bitcast.270, ...), custom_call_target="tpu_custom_call" | custom-call | flops 8589934592 | bytes 18874368 | tf_op jit(solution)/shard_map/attend/pallas_call | solution.py:186
  172.4 3.4 fusion.24
  175.8 3.3 fusion.80.v_ref
  182.5 3.3 fusion.82.q_ref
  185.8 4.1 attend.3
  192.6 3.3 multiply_reduce_fusion.4
  198.0 3.3 maximum_select_fusion.1
  201.3 5.8 convolution_convert_fusion.1
  207.1 14.2 %collective-permute-done.4 = bf16[512,1024]{1,0:T(8,128)(2,1)} collective-permute-done((bf16[512,1024]{1,0:T(8,128)(2,1)S(1)}, bf16[512,1024]{1,0:T(8,128)(2,1)}, u32[]{:S(2)}, u32[]{:S(2)}) %collective-permute-start.4) | collective-permute-done | bytes 1048608 | tf_op jit(solution)/shard_map/ppermute | solution.py:345
  221.3 9.5 %fusion.109 = f32[1024,2816]{1,0:T(8,128)S(1)} fusion(bf16[1024,2816]{1,0:T(8,128)(2,1)} %bitcast.359, bf16[512,1024]{1,0:T(8,128)(2,1)} %collective-permute-done.4, bf16[512,1024]{1,0:T(8,128)(2,1)} %copy-done.57), kind=kOutput, calls=%fused_computation.201 | convolution fusion | flops 5909774336 | bytes 19398656 | tf_op jit(solution)/shard_map/dot_general | solution.py:31
  230.9 4.6 fusion.14
  238.7 7.9 %fusion.76 = bf16[512,1024]{1,0:T(8,128)(2,1)S(1)} fusion(bf16[1024,2816]{1,0:T(8,128)(2,1)} %bitcast.360, bf16[1024,2816]{1,0:T(8,128)(2,1)S(1)} %pad_maximum_fusion), kind=kOutput, calls=%fused_computation.153 | convolution fusion | flops 2953314304 | bytes 9699328 | tf_op jit(solution)/shard_map/dot_general | solution.py:39
  252.5 6.2 %convolution_convert_fusion = bf16[1024,1408]{1,0:T(8,128)(2,1)} fusion(bf16[1024,2816]{1,0:T(8,128)(2,1)S(1)} %pad_maximum_fusion, s32[]{:T(128)S(6)} %select_n.315, bf16[512,1024]{1,0:T(8,128)(2,1)} %collective-permute-done.4, bf16[512,1024]{1,0:T(8,128)(2,1)S(1)} %copy-done.58), kind=kOutput, calls=%fused_computation.48 | convolution fusion | flops 2958426112 | bytes 7864324 | tf_op jit(solution)/shard_map/dot_general | solution.py:35
  261.1 6.1 %fusion.177 = f32[1024,1024]{1,0:T(8,128)S(1)} fusion(bf16[1024,1408]{1,0:T(8,128)(2,1)} %copy-done.27, bf16[1408,1024]{1,0:T(8,128)(2,1)} %bitcast.286), kind=kOutput, calls=%fused_computation.361 | convolution fusion | flops 2952790016 | bytes 9961472 | tf_op jit(solution)/shard_map/dot_general | solution.py:31
  277.0 6.9 %add_convert_fusion = bf16[1024,1408]{1,0:T(8,128)(2,1)S(1)} fusion(bf16[1024,1408]{1,0:T(8,128)(2,1)} %collective-permute-done.9, bf16[1024,2816]{1,0:T(8,128)(2,1)} %copy-done.26, s32[]{:T(128)S(6)} %select_n.318, bf16[512,1024]{1,0:T(8,128)(2,1)} %collective-permute-done.4, bf16[512,1024]{1,0:T(8,128)(2,1)} %copy-done.57), kind=kOutput, calls=%fused_computation.28 | convolution fusion | flops 2961309696 | bytes 10747908 | tf_op jit(solution)/shard_map/dot_general | solution.py:35
  284.0 4.0 collective-permute-done.8
  288.0 7.6 %multiply_reduce_fusion = (f32[1024]{0:T(1024)S(1)}, f32[512]{0:T(512)S(1)}, f32[512,1024]{1,0:T(8,128)}) fusion(f32[512,1024]{1,0:T(8,128)S(1)} %get-tuple-element.247, f32[512]{0:T(512)S(1)} %get-tuple-element.231, bf16[256,1024]{1,0:T(8,128)(2,1)} %collective-permute-done.8, bf16[256,1024]{1,0:T(8,128)(2,1)} %collective-permute-done.7, ...), kind=kOutput, calls=%fused_computation.98 | convolution fusion | flops 2958555648 | bytes 13905920 | tf_op jit(solution)/shard_map/dot_general | solution.py:39
  299.1 3.9 fusion.168
  303.0 4.3 fusion.79.dc_ref
  307.3 11.5 %attend_back.2 = (bf16[512,1024]{1,0:T(8,128)(2,1)S(1)}, bf16[512,1024]{1,0:T(8,128)(2,1)S(1)}, bf16[512,1024]{1,0:T(8,128)(2,1)S(1)}) custom-call(s32[2,2]{1,0:T(2,128)S(1)} %get-tuple-element.253.first_ref, s32[2,2]{1,0:T(2,128)S(1)} %get-tuple-element.252.stop_ref, s32[2,1,256]{2,1,0:T(1,128)S(1)} %broadcast_in_dim.83.lo_ref, ...), custom_call_target="tpu_custom_call" | custom-call | flops 5368709120 | bytes 6291456 | tf_op jit(solution)/shard_map/attend_back/pallas_call | solution.py:210
  325.6 4.4 collective-permute-done.11
  332.8 4.4 fusion.6
  353.8 3.6 fusion.33
  372.3 28.4 %attend_back.3 = (bf16[512,1024]{1,0:T(8,128)(2,1)S(1)}, bf16[2048,1024]{1,0:T(8,128)(2,1)}, bf16[2048,1024]{1,0:T(8,128)(2,1)}) custom-call(s32[2,2]{1,0:T(2,128)S(1)} %get-tuple-element.251.first_ref, s32[2,2]{1,0:T(2,128)S(1)} %get-tuple-element.234.stop_ref, s32[2,1,256]{2,1,0:T(1,128)S(1)} %broadcast_in_dim.73.lo_ref, s32[2,1,256]{2,1,0:T(1,128)S(1)} %bitcast.271, ...), custom_call_target="tpu_custom_call" | custom-call | flops 21474836480 | bytes 18874368 | tf_op jit(solution)/shard_map/attend_back/pallas_call | solution.py:210
  400.7 4.1 fusion.85
  418.2 3.7 fusion.67
  424.3 3.7 fusion.64
  430.2 6.4 %collective-permute-done.18 = bf16[2,1024,128]{2,1,0:T(8,128)(2,1)S(1)} collective-permute-done((bf16[2,1024,128]{2,1,0:T(8,128)(2,1)S(1)}, bf16[2,1024,128]{2,1,0:T(8,128)(2,1)S(1)}, u32[]{:S(2)}, u32[]{:S(2)}) %collective-permute-start.18) | collective-permute-done | bytes 524320 | tf_op jit(solution)/shard_map/ppermute | solution.py:363
  438.5 3.7 fusion.18
  442.6 4.0 fusion.17
  454.8 7.1 %fusion.49 = f32[2048,1024]{1,0:T(8,128)S(1)} fusion(bf16[2048,1024]{1,0:T(8,128)(2,1)} %get-tuple-element.131, bf16[2,4,1024,1024]{3,2,1,0:T(8,128)(2,1)} %bitcast.356), kind=kOutput, calls=%fused_computation.130 | convolution fusion | flops 4294967296 | bytes 14680064 | tf_op jit(solution)/shard_map/dot_general | solution.py:39
  462.0 8.6 %convolution_add_fusion = f32[2048,1024]{1,0:T(8,128)} fusion(f32[2048,1024]{1,0:T(8,128)S(1)} %fusion.49, bf16[2048,1024]{1,0:T(8,128)(2,1)S(1)} %copy-done.60, bf16[2,4,1024,1024]{3,2,1,0:T(8,128)(2,1)} %bitcast.357), kind=kOutput, calls=%fused_computation.47 | convolution fusion | flops 4297064448 | bytes 23068672 | tf_op jit(solution)/shard_map/dot_general | solution.py:39
  484.5 16.4 %collective-permute-done.22 = bf16[2,1024,128]{2,1,0:T(8,128)(2,1)} collective-permute-done((bf16[2,1024,128]{2,1,0:T(8,128)(2,1)}, bf16[2,1024,128]{2,1,0:T(8,128)(2,1)}, u32[]{:S(2)}, u32[]{:S(2)}) %collective-permute-start.22) | collective-permute-done | bytes 524320 | tf_op jit(solution)/shard_map/ppermute | solution.py:363
  504.5 6.1 %fusion.11 = (f32[1024]{0:T(1024)S(1)}, f32[2048]{0:T(1024)S(1)}) fusion(f32[2048,1024]{1,0:T(8,128)} %convolution_add_fusion, f32[2048]{0:T(1024)S(1)} %bitcast.302, bf16[4,1024,1024]{2,1,0:T(8,128)(2,1)} %param.9, s32[]{:T(128)S(6)} %select_n.279, f32[1024]{0:T(1024)S(1)} %bitcast.306), kind=kLoop, calls=%fused_computation.19 | loop fusion | flops 14676992 | bytes 12607492 | tf_op jit(solution)/shard_map/reduce_sum | solution.py:238
  513.2 4.6 fusion.60
  517.9 8.6 %fusion.1 = bf16[2048,1024]{1,0:T(8,128)(2,1)S(1)} fusion(f32[2,1024,1024]{2,1,0:T(8,128)} %fusion.60, f32[2048,1024]{1,0:T(8,128)} %convolution_add_fusion, f32[2048]{0:T(1024)S(1)} %broadcast_multiply_fusion, f32[2048]{0:T(1024)S(1)} %multiply_multiply_fusion, f32[1024]{0:T(1024)S(1)} %bitcast.307, f32[2048]{0:T(1024)S(1)} %bitcast.303, ...), kind=kLoop, calls=%fused_computation.3 | loop fusion | flops 16777216 | bytes 25194500 | tf_op jit(solution)/shard_map/convert_element_type | solution.py:467
  535.7 13.6 %all-gather.4 = f32[4,4,1024]{2,1,0:T(4,128)S(1)} all-gather(f32[1,4,1024]{2,1,0:T(4,128)S(1)} %add_bitcast_fusion), channel_id=4, replica_groups=mesh['section'=2,'group'=4,'dp'=4] {'dp'}, dimensions={0}, use_global_device_ids=true | all-gather | bytes 81920 | tf_op jit(solution)/shard_map/all_gather | solution.py:483
  550.3 3.4 collective-permute-done.28
  555.9 5.7 collective-permute-done.30
  568.8 8.4 %maximum_convert_fusion = f32[128,5632]{1,0:T(8,128)} fusion(bf16[64,1408]{1,0:T(8,128)(2,1)S(1)} %get-tuple-element.199, bf16[64,1408]{1,0:T(8,128)(2,1)S(1)} %get-tuple-element.200, bf16[64,1408]{1,0:T(8,128)(2,1)S(1)} %get-tuple-element.201, bf16[64,1408]{1,0:T(8,128)(2,1)S(1)} %get-tuple-element.202, bf16[64,1408]{1,0:T(8,128)(2,1)S(1)} %get-tuple-element.203, ...), kind=kLoop, calls=%fused_computation.167 | loop fusion | flops 11534336 | bytes 4325376 | tf_op jit(solution)/shard_map/concatenate | solution.py:474
  578.1 8.5 %all-gather.3 = bf16[1408,256]{1,0:T(8,128)(2,1)S(1)} all-gather(bf16[352,256]{1,0:T(8,128)(2,1)S(1)} %add_convert_fusion.12), channel_id=5, replica_groups=mesh['section'=2,'group'=4,'dp'=4] {'group'}, dimensions={0}, use_global_device_ids=true | all-gather | bytes 901120 | tf_op jit(solution)/shard_map/all_gather | solution.py:438
  (387 shorter events, 183.6 us)
Async XLA Ops:
  7.2 18.9 %copy-start = (s32[4,256]{1,0:T(4,128)S(1)}, s32[4,256]{1,0:T(4,128)}, u32[]{:S(2)}) copy-start(s32[4,256]{1,0:T(4,128)} %param.11) | copy-start | bytes 12292
  7.2 126.4 %all-gather.14.cloned.1.call-start = ((), (), s32[]{:S(2)}) async-start(), calls=%async_computation.10 | async-start | bytes 17301504 | tf_op jit(solution)/shard_map/all_gather | solution.py:264
  9.3 212.0 %all-gather.10.cloned.1.call-start = ((), (), s32[]{:S(2)}) async-start(), calls=%async_computation.4 | async-start | bytes 6127616 | tf_op jit(solution)/shard_map/all_gather | solution.py:287
  10.4 34.1 %collective-permute-start = (bf16[88,1024]{1,0:T(8,128)(2,1)S(1)}, bf16[88,1024]{1,0:T(8,128)(2,1)}, u32[]{:S(2)}, u32[]{:S(2)}) collective-permute-start(bf16[88,1024]{1,0:T(8,128)(2,1)S(1)} %get-tuple-element.172), channel_id=1, source_target_pairs={{0,1},{1,2},{2,3},{3,0},{4,5},{5,6},{6,7},{7,4},{8,9},{9,10},{10,1... | collective-permute-start | bytes 540680 | tf_op jit(solution)/shard_map/ppermute | solution.py:293
  13.5 32.0 %collective-permute-start.1 = (bf16[88,1024]{1,0:T(8,128)(2,1)S(1)}, bf16[88,1024]{1,0:T(8,128)(2,1)}, u32[]{:S(2)}, u32[]{:S(2)}) collective-permute-start(bf16[88,1024]{1,0:T(8,128)(2,1)S(1)} %get-tuple-element.172), channel_id=1, source_target_pairs={{0,2},{1,3},{2,0},{3,1},{4,6},{5,7},{6,4},{7,5},{8,10},{9,11},{10,... | collective-permute-start | bytes 540680 | tf_op jit(solution)/shard_map/ppermute | solution.py:293
  16.1 30.3 %collective-permute-start.2 = (bf16[88,1024]{1,0:T(8,128)(2,1)S(1)}, bf16[88,1024]{1,0:T(8,128)(2,1)S(1)}, u32[]{:S(2)}, u32[]{:S(2)}) collective-permute-start(bf16[88,1024]{1,0:T(8,128)(2,1)S(1)} %get-tuple-element.172), channel_id=1, source_target_pairs={{0,3},{1,0},{2,1},{3,2},{4,7},{5,4},{6,5},{7,6},{8,11},{9,8},{10,9... | collective-permute-start | bytes 540680 | tf_op jit(solution)/shard_map/ppermute | solution.py:293
  19.4 10.6 %collective-permute-start.6 = (bf16[32,2816]{1,0:T(8,128)(2,1)}, bf16[32,2816]{1,0:T(8,128)(2,1)}, u32[]{:S(2)}, u32[]{:S(2)}) collective-permute-start(bf16[32,2816]{1,0:T(8,128)(2,1)} %pad_maximum_fusion.15), channel_id=1, source_target_pairs={{0,16},{16,0},{1,17},{17,1},{2,18},{18,2},{3,19},{19,3},{4,20},{20... | collective-permute-start | bytes 540680 | tf_op jit(solution)/shard_map/ppermute | solution.py:285
  26.1 17.1 %copy-start.17 = (f32[2,256,1024]{2,1,0:T(8,128)}, f32[2,256,1024]{2,1,0:T(8,128)S(1)}, u32[]{:S(2)}) copy-start(f32[2,256,1024]{2,1,0:T(8,128)S(1)} %get-tuple-element.243) | copy-start | bytes 6291460
  31.8 301.0 %reduce-scatter.5.cloned.1.call-start = ((), (), s32[]{:S(2)}) async-start(), calls=%async_computation.5 | async-start | bytes 1802240 | tf_op jit(solution)/shard_map/reduce_scatter | solution.py:376
  37.3 223.2 %copy-start.70 = (f32[1,8,2,128]{3,2,1,0:T(2,128)}, f32[1,8,2,128]{3,2,1,0:T(2,128)S(1)}, u32[]{:S(2)}) copy-start(f32[1,8,2,128]{3,2,1,0:T(2,128)S(1)} %get-tuple-element.224) | copy-start | bytes 24580
  143.1 46.9 %collective-permute-start.3 = (bf16[4,88,1024]{2,1,0:T(8,128)(2,1)S(1)}, bf16[4,88,1024]{2,1,0:T(8,128)(2,1)S(1)}, u32[]{:S(2)}, u32[]{:S(2)}) collective-permute-start(bf16[4,88,1024]{2,1,0:T(8,128)(2,1)S(1)} %bitcast_dynamic-update-slice_fusion), channel_id=1, source_target_pairs={{0,8},{4,12},{8,0},{12,4},{1,9},{5,13},{9,1},{13,5},{2,10},{6,14},... | collective-permute-start | bytes 2162696 | tf_op jit(solution)/shard_map/ppermute | solution.py:276
  155.5 16.9 %copy-start.22 = (f32[512,1024]{1,0:T(8,128)S(1)}, f32[512,1024]{1,0:T(8,128)}, u32[]{:S(2)}) copy-start(f32[512,1024]{1,0:T(8,128)} %bitcast_divide_fusion) | copy-start | bytes 6291460
  191.4 6.7 %collective-permute-start.5 = (bf16[2,4,88,1024]{3,2,0,1:T(8,128)(2,1)}, bf16[2,4,88,1024]{3,2,0,1:T(8,128)(2,1)}, u32[]{:S(2)}, u32[]{:S(2)}) collective-permute-start(bf16[2,4,88,1024]{3,2,0,1:T(8,128)(2,1)} %maximum_select_fusion.3), channel_id=1, source_target_pairs={{0,4},{4,0},{8,12},{12,8},{1,5},{5,1},{9,13},{13,9},{2,6},{6,2},{1... | collective-permute-start | bytes 4325384 | tf_op jit(solution)/shard_map/ppermute | solution.py:276
  196.1 25.2 %collective-permute-start.4 = (bf16[512,1024]{1,0:T(8,128)(2,1)S(1)}, bf16[512,1024]{1,0:T(8,128)(2,1)}, u32[]{:S(2)}, u32[]{:S(2)}) collective-permute-start(bf16[512,1024]{1,0:T(8,128)(2,1)S(1)} %multiply_convert_fusion.2), channel_id=1, source_target_pairs={{0,16},{16,0},{1,17},{17,1},{2,18},{18,2},{3,19},{19,3},{4,20},{20... | collective-permute-start | bytes 3145736 | tf_op jit(solution)/shard_map/ppermute | solution.py:345
  235.5 13.0 %copy-start.27 = (bf16[1024,1408]{1,0:T(8,128)(2,1)}, bf16[1024,1408]{1,0:T(8,128)(2,1)S(1)}, u32[]{:S(2)}) copy-start(bf16[1024,1408]{1,0:T(8,128)(2,1)S(1)} %get-tuple-element.177) | copy-start | bytes 8650756
  247.6 13.0 %collective-permute-start.7 = (bf16[256,1024]{1,0:T(8,128)(2,1)S(1)}, bf16[256,1024]{1,0:T(8,128)(2,1)}, u32[]{:S(2)}, u32[]{:S(2)}) collective-permute-start(bf16[256,1024]{1,0:T(8,128)(2,1)S(1)} %get-tuple-element.211), channel_id=1, source_target_pairs={{0,16},{16,0},{1,17},{17,1},{2,18},{18,2},{3,19},{19,3},{4,20},{20... | collective-permute-start | bytes 1572872 | tf_op jit(solution)/shard_map/ppermute | solution.py:392
  260.6 16.4 %collective-permute-start.9 = (bf16[1024,1408]{1,0:T(8,128)(2,1)}, bf16[1024,1408]{1,0:T(8,128)(2,1)}, u32[]{:S(2)}, u32[]{:S(2)}) collective-permute-start(bf16[1024,1408]{1,0:T(8,128)(2,1)} %convolution_convert_fusion), channel_id=1, source_target_pairs={{0,4},{4,0},{8,12},{12,8},{1,5},{5,1},{9,13},{13,9},{2,6},{6,2},{1... | collective-permute-start | bytes 8650760 | tf_op jit(solution)/shard_map/ppermute | solution.py:386
  260.6 14.7 %collective-permute-start.10 = (bf16[1408,512]{1,0:T(8,128)(2,1)}, bf16[1408,512]{1,0:T(8,128)(2,1)S(1)}, u32[]{:S(2)}, u32[]{:S(2)}) collective-permute-start(bf16[1408,512]{1,0:T(8,128)(2,1)} %convolution_convert_fusion.4), channel_id=1, source_target_pairs={{0,4},{4,0},{8,12},{12,8},{1,5},{5,1},{9,13},{13,9},{2,6},{6,2},{1... | collective-permute-start | bytes 4325384 | tf_op jit(solution)/shard_map/ppermute | solution.py:386
  273.7 14.3 %collective-permute-start.8 = (bf16[256,1024]{1,0:T(8,128)(2,1)}, bf16[256,1024]{1,0:T(8,128)(2,1)}, u32[]{:S(2)}, u32[]{:S(2)}) collective-permute-start(bf16[256,1024]{1,0:T(8,128)(2,1)} %get-tuple-element.96), channel_id=1, source_target_pairs={{0,16},{16,0},{1,17},{17,1},{2,18},{18,2},{3,19},{19,3},{4,20},{20... | collective-permute-start | bytes 1572872 | tf_op jit(solution)/shard_map/ppermute | solution.py:396
  296.9 33.1 %collective-permute-start.11 = (bf16[2,4,1,64,1408]{4,3,2,1,0:T(8,128)(2,1)}, bf16[2,4,1,64,1408]{4,3,2,1,0:T(8,128)(2,1)}, u32[]{:S(2)}, u32[]{:S(2)}) collective-permute-start(bf16[2,4,1,64,1408]{4,3,2,1,0:T(8,128)(2,1)} %constant_dynamic-slice_fusion.11), channel_id=1, source_target_pairs={{0,8},{4,12},{8,0},{12,4},{1,9},{5,13},{9,1},{13,5},{2,10},{6,14},... | collective-permute-start | bytes 4325384 | tf_op jit(solution)/shard_map/ppermute | solution.py:363
  298.6 148.0 %reduce-scatter.7.cloned.1.call-start = ((), (), s32[]{:S(2)}) async-start(), calls=%async_computation.6 | async-start | bytes 1802240 | tf_op jit(solution)/shard_map/reduce_scatter | solution.py:376
  303.0 15.8 %copy-start.54 = (bf16[512,1024]{1,0:T(8,128)(2,1)}, bf16[512,1024]{1,0:T(8,128)(2,1)S(1)}, u32[]{:S(2)}) copy-start(bf16[512,1024]{1,0:T(8,128)(2,1)S(1)} %get-tuple-element.169) | copy-start | bytes 3145732
  332.8 32.7 %collective-permute-start.12 = (bf16[4,1024,512]{2,1,0:T(8,128)(2,1)}, bf16[4,1024,512]{2,1,0:T(8,128)(2,1)}, u32[]{:S(2)}, u32[]{:S(2)}) collective-permute-start(bf16[4,1024,512]{2,1,0:T(8,128)(2,1)} %pad_maximum_fusion.1), channel_id=1, source_target_pairs={{0,4},{4,0},{8,12},{12,8},{1,5},{5,1},{9,13},{13,9},{2,6},{6,2},{1... | collective-permute-start | bytes 12582920 | tf_op jit(solution)/shard_map/ppermute | solution.py:386
  337.1 32.6 %collective-permute-start.13 = (bf16[1024,512]{1,0:T(8,128)(2,1)}, bf16[1024,512]{1,0:T(8,128)(2,1)}, u32[]{:S(2)}, u32[]{:S(2)}) collective-permute-start(bf16[1024,512]{1,0:T(8,128)(2,1)} %fusion.35), channel_id=1, source_target_pairs={{0,16},{16,0},{1,17},{17,1},{2,18},{18,2},{3,19},{19,3},{4,20},{20... | collective-permute-start | bytes 3145736 | tf_op jit(solution)/shard_map/ppermute | solution.py:404
  347.5 157.0 %reduce-scatter.9.cloned.1.call-start = ((), (), s32[]{:S(2)}) async-start(), calls=%async_computation.7 | async-start | bytes 1310720 | tf_op jit(solution)/shard_map/reduce_scatter | solution.py:376
  370.1 40.0 %collective-permute-start.15 = (bf16[2,1024,256]{2,1,0:T(8,128)(2,1)S(1)}, bf16[2,1024,256]{2,1,0:T(8,128)(2,1)}, u32[]{:S(2)}, u32[]{:S(2)}) collective-permute-start(bf16[2,1024,256]{2,1,0:T(8,128)(2,1)S(1)} %constant_dynamic-slice_fusion.9), channel_id=1, source_target_pairs={{0,8},{4,12},{8,0},{12,4},{1,9},{5,13},{9,1},{13,5},{2,10},{6,14},... | collective-permute-start | bytes 3145736 | tf_op jit(solution)/shard_map/ppermute | solution.py:363
  370.6 41.0 %collective-permute-start.14 = (bf16[2,1024,256]{2,1,0:T(8,128)(2,1)S(1)}, bf16[2,1024,256]{2,1,0:T(8,128)(2,1)S(1)}, u32[]{:S(2)}, u32[]{:S(2)}) collective-permute-start(bf16[2,1024,256]{2,1,0:T(8,128)(2,1)S(1)} %constant_dynamic-slice_fusion.10), channel_id=1, source_target_pairs={{0,16},{16,0},{1,17},{17,1},{2,18},{18,2},{3,19},{19,3},{4,20},{20... | collective-permute-start | bytes 3145736 | tf_op jit(solution)/shard_map/ppermute | solution.py:363
  372.3 28.4 %copy-start.16 = (bf16[2048,1024]{1,0:T(8,128)(2,1)S(1)}, bf16[2048,1024]{1,0:T(8,128)(2,1)}, u32[]{:S(2)}) copy-start(bf16[2048,1024]{1,0:T(8,128)(2,1)} %fusion.6) | copy-start | bytes 12582916
  415.7 22.9 %collective-permute-start.17 = (bf16[2,1024,512]{2,1,0:T(8,128)(2,1)}, bf16[2,1024,512]{2,1,0:T(8,128)(2,1)}, u32[]{:S(2)}, u32[]{:S(2)}) collective-permute-start(bf16[2,1024,512]{2,1,0:T(8,128)(2,1)} %pad_maximum_fusion.6), channel_id=1, source_target_pairs={{0,4},{4,0},{8,12},{12,8},{1,5},{5,1},{9,13},{13,9},{2,6},{6,2},{1... | collective-permute-start | bytes 6291464 | tf_op jit(solution)/shard_map/ppermute | solution.py:386
  418.2 24.1 %collective-permute-start.16 = (bf16[2,1024,512]{2,1,0:T(8,128)(2,1)}, bf16[2,1024,512]{2,1,0:T(8,128)(2,1)}, u32[]{:S(2)}, u32[]{:S(2)}) collective-permute-start(bf16[2,1024,512]{2,1,0:T(8,128)(2,1)} %pad_maximum_fusion.5), channel_id=1, source_target_pairs={{0,4},{4,0},{8,12},{12,8},{1,5},{5,1},{9,13},{13,9},{2,6},{6,2},{1... | collective-permute-start | bytes 6291464 | tf_op jit(solution)/shard_map/ppermute | solution.py:386
  422.0 14.6 %collective-permute-start.18 = (bf16[2,1024,128]{2,1,0:T(8,128)(2,1)S(1)}, bf16[2,1024,128]{2,1,0:T(8,128)(2,1)S(1)}, u32[]{:S(2)}, u32[]{:S(2)}) collective-permute-start(bf16[2,1024,128]{2,1,0:T(8,128)(2,1)S(1)} %constant_dynamic-slice_fusion.8), channel_id=1, source_target_pairs={{0,8},{4,12},{8,0},{12,4},{1,9},{5,13},{9,1},{13,5},{2,10},{6,14},... | collective-permute-start | bytes 1572872 | tf_op jit(solution)/shard_map/ppermute | solution.py:363
  424.0 13.3 %collective-permute-start.19 = (bf16[2,1024,128]{2,1,0:T(8,128)(2,1)S(1)}, bf16[2,1024,128]{2,1,0:T(8,128)(2,1)S(1)}, u32[]{:S(2)}, u32[]{:S(2)}) collective-permute-start(bf16[2,1024,128]{2,1,0:T(8,128)(2,1)S(1)} %constant_dynamic-slice_fusion.7), channel_id=1, source_target_pairs={{0,16},{16,0},{1,17},{17,1},{2,18},{18,2},{3,19},{19,3},{4,20},{20... | collective-permute-start | bytes 1572872 | tf_op jit(solution)/shard_map/ppermute | solution.py:363
  448.5 22.0 %collective-permute-start.24 = (bf16[64,1408]{1,0:T(8,128)(2,1)}, bf16[64,1408]{1,0:T(8,128)(2,1)}, u32[]{:S(2)}, u32[]{:S(2)}) collective-permute-start(bf16[64,1408]{1,0:T(8,128)(2,1)} %get-tuple-element.219), channel_id=1, source_target_pairs={{0,16},{16,0},{1,17},{17,1},{2,18},{18,2},{3,19},{19,3},{4,20},{20... | collective-permute-start | bytes 540680 | tf_op jit(solution)/shard_map/ppermute | solution.py:447
  450.2 25.2 %collective-permute-start.21 = (bf16[2,1024,256]{2,1,0:T(8,128)(2,1)}, bf16[2,1024,256]{2,1,0:T(8,128)(2,1)}, u32[]{:S(2)}, u32[]{:S(2)}) collective-permute-start(bf16[2,1024,256]{2,1,0:T(8,128)(2,1)} %constant_dynamic-slice_fusion.5), channel_id=1, source_target_pairs={{0,8},{4,12},{8,0},{12,4},{1,9},{5,13},{9,1},{13,5},{2,10},{6,14},... | collective-permute-start | bytes 3145736 | tf_op jit(solution)/shard_map/ppermute | solution.py:363
  453.0 24.9 %collective-permute-start.20 = (bf16[2,1024,256]{2,1,0:T(8,128)(2,1)}, bf16[2,1024,256]{2,1,0:T(8,128)(2,1)}, u32[]{:S(2)}, u32[]{:S(2)}) collective-permute-start(bf16[2,1024,256]{2,1,0:T(8,128)(2,1)} %constant_dynamic-slice_fusion.6), channel_id=1, source_target_pairs={{0,16},{16,0},{1,17},{17,1},{2,18},{18,2},{3,19},{19,3},{4,20},{20... | collective-permute-start | bytes 3145736 | tf_op jit(solution)/shard_map/ppermute | solution.py:363
  454.8 49.8 %all-gather.16.cloned.1.call-start = ((), (), s32[]{:S(2)}) async-start(), calls=%async_computation.11 | async-start | bytes 1802240 | tf_op jit(solution)/shard_map/all_gather | solution.py:438
  472.3 81.4 %reduce-scatter.11.cloned.1.call-start = ((), (), s32[]{:S(2)}) async-start(), calls=%async_computation.8 | async-start | bytes 1310720 | tf_op jit(solution)/shard_map/reduce_scatter | solution.py:376
  481.2 19.7 %collective-permute-start.22 = (bf16[2,1024,128]{2,1,0:T(8,128)(2,1)}, bf16[2,1024,128]{2,1,0:T(8,128)(2,1)}, u32[]{:S(2)}, u32[]{:S(2)}) collective-permute-start(bf16[2,1024,128]{2,1,0:T(8,128)(2,1)} %constant_dynamic-slice_fusion.4), channel_id=1, source_target_pairs={{0,8},{4,12},{8,0},{12,4},{1,9},{5,13},{9,1},{13,5},{2,10},{6,14},... | collective-permute-start | bytes 1572872 | tf_op jit(solution)/shard_map/ppermute | solution.py:363
  483.7 18.5 %collective-permute-start.23 = (bf16[2,1024,128]{2,1,0:T(8,128)(2,1)}, bf16[2,1024,128]{2,1,0:T(8,128)(2,1)}, u32[]{:S(2)}, u32[]{:S(2)}) collective-permute-start(bf16[2,1024,128]{2,1,0:T(8,128)(2,1)} %constant_dynamic-slice_fusion.3), channel_id=1, source_target_pairs={{0,16},{16,0},{1,17},{17,1},{2,18},{18,2},{3,19},{19,3},{4,20},{20... | collective-permute-start | bytes 1572872 | tf_op jit(solution)/shard_map/ppermute | solution.py:363
  511.5 17.3 %collective-permute-start.25 = (f32[4,1024]{1,0:T(4,128)S(1)}, f32[4,1024]{1,0:T(4,128)S(1)}, u32[]{:S(2)}, u32[]{:S(2)}) collective-permute-start(f32[4,1024]{1,0:T(4,128)S(1)} %pad_maximum_fusion.16), channel_id=1, source_target_pairs={{0,16},{16,0},{1,17},{17,1},{2,18},{18,2},{3,19},{19,3},{4,20},{20... | collective-permute-start | bytes 49160 | tf_op jit(solution)/shard_map/ppermute | solution.py:473
  517.8 73.0 %all-gather.12.cloned.1.call-start = ((), (), s32[]{:S(2)}) async-start(), calls=%async_computation.9 | async-start | bytes 2621440 | tf_op jit(solution)/shard_map/all_gather | solution.py:438
  528.8 33.8 %copy-start.20 = (f32[512,1024]{1,0:T(8,128)S(1)}, f32[512,1024]{1,0:T(8,128)}, u32[]{:S(2)}) copy-start(f32[512,1024]{1,0:T(8,128)} %copy-done.19) | copy-start | bytes 6291460
  528.8 24.9 %collective-permute-start.28 = (bf16[1024,512]{1,0:T(8,128)(2,1)}, bf16[1024,512]{1,0:T(8,128)(2,1)}, u32[]{:S(2)}, u32[]{:S(2)}) collective-permute-start(bf16[1024,512]{1,0:T(8,128)(2,1)} %get-tuple-element.145), channel_id=1, source_target_pairs={{0,16},{16,0},{1,17},{17,1},{2,18},{18,2},{3,19},{19,3},{4,20},{20... | collective-permute-start | bytes 3145736 | tf_op jit(solution)/shard_map/ppermute | solution.py:480
  530.3 1.2 collective-permute-start.26
  531.5 4.2 collective-permute-start.27
  534.7 14.6 %collective-permute-start.29 = (bf16[352,256]{1,0:T(8,128)(2,1)}, bf16[352,256]{1,0:T(8,128)(2,1)S(1)}, u32[]{:S(2)}, u32[]{:S(2)}) collective-permute-start(bf16[352,256]{1,0:T(8,128)(2,1)} %constant_dynamic-slice_fusion.1), channel_id=1, source_target_pairs={{0,8},{4,12},{8,0},{12,4},{1,9},{5,13},{9,1},{13,5},{2,10},{6,14},... | collective-permute-start | bytes 540680 | tf_op jit(solution)/shard_map/ppermute | solution.py:363
  554.8 6.8 %collective-permute-start.30 = (bf16[4,256,128]{2,1,0:T(8,128)(2,1)S(1)}, bf16[4,256,128]{2,1,0:T(8,128)(2,1)S(1)}, u32[]{:S(2)}, u32[]{:S(2)}) collective-permute-start(bf16[4,256,128]{2,1,0:T(8,128)(2,1)S(1)} %get-tuple-element.217), channel_id=1, source_target_pairs={{0,16},{16,0},{1,17},{17,1},{2,18},{18,2},{3,19},{19,3},{4,20},{20... | collective-permute-start | bytes 786440 | tf_op jit(solution)/shard_map/ppermute | solution.py:490
  568.1 22.7 %collective-permute-start.31 = (bf16[1024,512]{1,0:T(8,128)(2,1)S(1)}, bf16[1024,512]{1,0:T(8,128)(2,1)}, u32[]{:S(2)}, u32[]{:S(2)}) collective-permute-start(bf16[1024,512]{1,0:T(8,128)(2,1)S(1)} %get-tuple-element.152), channel_id=1, source_target_pairs={{0,16},{16,0},{1,17},{17,1},{2,18},{18,2},{3,19},{19,3},{4,20},{20... | collective-permute-start | bytes 3145736 | tf_op jit(solution)/shard_map/ppermute | solution.py:487
  (73 other events, 343.9 us)
Sparse Core Ops, SparseCore 0:
  11.6 121.9 all-gather.13
  136.5 60.2 all-gather.9
  298.8 31.0 reduce-scatter.4
  347.6 31.5 reduce-scatter.6
  454.9 25.0 reduce-scatter.8
  482.0 21.5 all-gather.15
  518.0 26.6 reduce-scatter.10
  562.7 20.4 all-gather.11

commit v14 on v13

--- a/solution.py
+++ b/solution.py
@@ -120,7 +120,7 @@
 
 def attend_back_kernel(
     chunk, spans, first_ref, stop_ref, lo_ref, hi_ref, q_ref, k_ref, v_ref, l_ref, c_ref, dc_ref,
-    dq_ref, dk_ref, dv_ref, bias_ref, dk_acc, dv_acc,
+    dq_ref, dkv_ref, bias_ref, dk_acc, dv_acc,
 ):
     row = pl.program_id(0)
     pairs = range(q_ref.shape[1] // PAIR)
@@ -159,8 +159,9 @@
         accs = over_chunks(spans, tile, bounds, step, accs)
         for pair in pairs:
             dq_ref[own, lanes[pair]] = (own_lanes(accs[pair]) * SCALE).astype(BF)
-    dk_ref[...] = dk_acc[...].astype(BF)
-    dv_ref[...] = dv_acc[...].astype(BF)
+    width = dk_acc.shape[1]
+    dkv_ref[:, :width] = dk_acc[...].astype(BF)
+    dkv_ref[:, width:] = dv_acc[...].astype(BF)
 
 
 def attention_specs(keys, wide):
@@ -213,13 +214,12 @@
             num_scalar_prefetch=2,
             grid=(rows, PAIRS // wide),
             in_specs=[bound, bound, per_query, per_key, per_key, logs, per_query, per_query],
-            out_specs=[per_query, per_key, per_key],
+            out_specs=[per_query, pl.BlockSpec((keys, 2 * wide * PAIR), lambda r, h, *_: (r, h))],
             scratch_shapes=[pltpu.VMEM((TILES, keys, QT), F32)] + [pltpu.VMEM((keys, wide * PAIR), F32)] * 2,
         ),
         out_shape=[
             jax.ShapeDtypeStruct(q.shape, BF),
-            jax.ShapeDtypeStruct(k.shape, BF),
-            jax.ShapeDtypeStruct(k.shape, BF),
+            jax.ShapeDtypeStruct((k.shape[0], 2 * D), BF),
         ],
         compiler_params=pltpu.CompilerParams(vmem_limit_bytes=48 << 20),
         cost_estimate=kernel_cost(q, k, 5),
@@ -344,7 +344,11 @@
     mix_in = (residual * second_scale * gains[1, 1]).astype(BF)
     mix_got = lax.ppermute(mix_in, "section", swap)
     grad_hidden = nt(cots, w_down).astype(BF)
-    mix_got, grad_hidden = together((mix_got, grad_hidden))
+    half_width = D // 2
+    wkv = jnp.concatenate(
+        [w[0][:, at : at + half_width] for at in (0, half_width) for w in (wk, wv)], axis=1
+    )
+    mix_got, grad_hidden, wkv = together((mix_got, grad_hidden, wkv))
     mixed = jnp.concatenate([mix_in, mix_got], axis=0)
     gate_up = nn(mixed, w_in)
     gate, up = gate_up[:, :units], gate_up[:, units:]
@@ -369,6 +373,8 @@
         return exchanged(values, "group", side, side_pairs, where)
 
     def columns(values, part):
+        if callable(values):
+            return values(part)
         size = values.shape[-1] // 2
         return lax.dynamic_slice_in_dim(values, part * size, size, values.ndim - 1)
 
@@ -411,7 +417,8 @@
     branch = grad_residual.astype(BF)
     dc2 = nt(branch, wo[1]).astype(BF)
 
-    dq2, dk2, dv2 = attend_back(causal, q2, k2, v2, l2, c2, dc2, 8, CAUSAL_SPANS)
+    dq2, dkv2 = attend_back(causal, q2, k2, v2, l2, c2, dc2, 8, CAUSAL_SPANS)
+    dk2, dv2 = dkv2[:, :D], dkv2[:, D:]
     two_pairs = [(normed_in, dq2), (normed_in, dk2), (normed_in, dv2), (c2, branch)]
     send_two = to_core(two_pairs)
     half_in = over_side(half_in.reshape(sections, line, 2, -1, units), 2)
@@ -427,13 +434,19 @@
     got = got.astype(F32)
     latents = in_order(section, kept[:tokens] + got[tokens:], kept[tokens:] + got[:tokens])
     latents_out = latents.astype(BF).reshape(sections * rows, PATCHES, half)
-    dq1, dk1, dv1 = attend_back(cross_back, q1, k1, v1, l1, c1, dc1, 4)
+    def pairs_of(dq1, dkv1):
+        def part_of(offset):
+            return lambda part: lax.dynamic_slice_in_dim(dkv1, part * D + offset, D // 2, 1)
+
+        return [(query_in, dq1), (key_in, part_of(0))], [(key_in, part_of(D // 2)), (c1, d_carried)]
+
+    dq1, dkv1 = attend_back(cross_back, q1, k1, v1, l1, c1, dc1, 4)
     half_two = over_section(half_two[:2], 2), over_side(half_two[2:], 2)
     dq1, half_two = together((dq1, half_two))
     half_two = jnp.concatenate([over_side(half_two[0], 2), over_section(half_two[1], 2)], axis=0)
-    one_pairs = [(query_in, dq1), (key_in, dk1)], [(key_in, dv1), (c1, d_carried)]
+    one_pairs = pairs_of(dq1, dkv1)
     send_one = [to_core(pairs) for pairs in one_pairs]
-    dq1, dk1, dv1, send_one, sum_down = together((dq1, dk1, dv1, send_one, sum_down))
+    dq1, dkv1, send_one, sum_down = together((dq1, dkv1, send_one, sum_down))
     def gathered(part):
         return lax.all_gather(part, "group", axis=0, tiled=False)
 
@@ -441,14 +454,14 @@
         return jnp.concatenate([parts[index] for index in order], axis=-1).astype(F32)
 
     half_one = [of_chip(pairs, sent) for pairs, sent in zip(one_pairs, send_one)]
-    dq1, dk1, dv1, half_one, half_two, sum_in = together((dq1, dk1, dv1, half_one, half_two, sum_in))
+    dq1, dkv1, half_one, half_two, sum_in = together((dq1, dkv1, half_one, half_two, sum_in))
     sum_two = line_sum(half_two, 1)
     sum_in = jnp.stack([lax.dynamic_index_in_dim(sum_in, section, 0, False),
                         lax.ppermute(lax.dynamic_index_in_dim(sum_in, 1 - section, 0, False), "section", swap)])
     sum_in = jnp.where(section == 0, sum_in, sum_in[::-1])
     sum_in = gathered(sum_in)
     grad_query_in = nt(dq1, wq[0])
-    grad_key_in = nt(dk1, wk[0]) + nt(dv1, wv[0])
+    grad_key_in = nt(dkv1, wkv)
     half_one = over_section(half_one[0], 2), over_side(half_one[1], 2)
     grad_query_in, grad_key_in, half_one = together((grad_query_in, grad_key_in, half_one))
     half_one = jnp.concatenate([over_side(half_one[0], 2), over_section(half_one[1], 2)], axis=0)

time: 612 us -> 614 us (level)
  local copies, waits for them, and re-layouts: 34.2 us -> 44 us
    unnamed x171 -> x169, local copies, waits for them, and re-layouts: 14.6 us -> 13 us
    dot_general x11 -> x10, matrix products: 57 us -> 57 us  [nt(): lax.dot_general(left, right, (((1,), (1,)), ((), ())), preferred_element_...]
  transfers between devices with their start and end apart: 40 -> 40, of which waited for: 14 -> 17; matrix products, arithmetic and copies ran while one was open for 40% -> 41% of each run, Pallas kernels for 10% -> 10%
where the time goes in v14:
time: 614 us; the launch traced here: 609 us
  matrix products  166 us (27%)
  waiting for transfers between devices  148 us (24%)
  other arithmetic  110 us (18%)
  Pallas kernels  57.9 us (9%)
  local copies, waits for them, and re-layouts  44 us (7%)
  starting transfers between devices  38.4 us (6%)
  blocking collectives  27.7 us (5%)
  between operations  15.9 us (3%)
    all_gather x1, waiting for transfers between devices, shards(): lax.all_gather(matrix, ('section', 'group', 'dp'), axis=0, tiled=True)  84.7 us
    dot_general x10, matrix products, nt(): lax.dot_general(left, right, (((1,), (1,)), ((), ())), preferred_element_...  57 us
    dot_general x10, matrix products, nn(): return jnp.dot(left, right, preferred_element_type=F32)  51.8 us
    dot_general x20, matrix products, tn(): lax.dot_general(left, right, (((0,), (0,)), ((), ())), preferred_element_...  49.5 us
    pallas_call x2, Pallas kernels, attend_back(): pl.pallas_call(functools.partial(attend_back_kernel, chunk, spans), grid_...  38 us
    ppermute x10, waiting for transfers between devices, exchanged(): lax.ppermute(other, axis, pairs).astype(F32)  22.7 us
    pallas_call x2, Pallas kernels, attend(): pl.pallas_call(functools.partial(attend_kernel, chunk, spans), grid_spec=...  19.9 us
    all_gather x1, blocking collectives, shards(): lax.all_gather(gain_grads, 'dp', axis=0, tiled=False)  13.6 us
  transfers between devices with their start and end apart: 40, of which 17 were waited for; matrix products, arithmetic and copies ran while one was open for 41% of the time, Pallas kernels for 10%

profile of v14, /device:TPU:0, one launch (start us, length us, event | category | flops | bytes accessed | tf_op | source)
XLA Modules:
  0.0 608.6 jit_solution(2936142103892853800)
XLA Ops:
  26.7 3.7 multiply_reduce_fusion.5
  31.8 4.6 all_gather.31
  36.5 4.2 fusion.4
  50.7 84.7 %all-gather.14.cloned.1.call-done = bf16[1,8192,1024]{2,1,0:T(8,128)(2,1)} async-done(((bf16[1,256,1024]{2,1,0:T(8,128)(2,1)}), bf16[1,8192,1024]{2,1,0:T(8,128)(2,1)}) %all-gather.14.cloned.1.call-update) | async-done | bytes 16777232 | tf_op jit(solution)/shard_map/all_gather | solution.py:264
  135.3 9.4 %convolution_convert_fusion.2.v_ref = bf16[2048,1024]{1,0:T(8,128)(2,1)} fusion(bf16[2048,1024]{1,0:T(8,128)(2,1)} %bitcast.280, bf16[2,4,1024,1024]{3,2,1,0:T(8,128)(2,1)} %bitcast.293), kind=kOutput, calls=%fused_computation.50 | convolution fusion | flops 4297064448 | bytes 10485760 | tf_op jit(solution)/shard_map/dot_general | solution.py:31
  149.2 8.0 %convolution_convert_fusion.3.k_ref = bf16[2048,1024]{1,0:T(8,128)(2,1)} fusion(bf16[2048,1024]{1,0:T(8,128)(2,1)S(1)} %bitcast.281, bf16[2,4,1024,1024]{3,2,1,0:T(8,128)(2,1)} %bitcast.295), kind=kOutput, calls=%fused_computation.51 | convolution fusion | flops 4297064448 | bytes 10485760 | tf_op jit(solution)/shard_map/dot_general | solution.py:31
  157.3 15.8 %attend.2 = (bf16[512,1024]{1,0:T(8,128)(2,1)S(1)}, f32[2,8,2,256]{3,2,1,0:T(2,128)S(1)}) custom-call(s32[2,2]{1,0:T(2,128)S(1)} %get-tuple-element.252.first_ref, s32[2,2]{1,0:T(2,128)S(1)} %get-tuple-element.237.stop_ref, s32[2,1,256]{2,1,0:T(1,128)S(1)} %broadcast_in_dim.73.lo_ref, s32[2,1,256]{2,1,0:T(1,128)S(1)} %bitcast.268, ...), custom_call_target="tpu_custom_call" | custom-call | flops 8589934592 | bytes 18874368 | tf_op jit(solution)/shard_map/attend/pallas_call | solution.py:187
  176.1 3.3 fusion.79.v_ref
  179.4 3.3 fusion.80.k_ref
  182.7 3.3 fusion.81.q_ref
  186.0 4.1 attend.3
  205.8 5.7 convolution_convert_fusion.1
  211.5 13.3 %collective-permute-done.4 = bf16[512,1024]{1,0:T(8,128)(2,1)} collective-permute-done((bf16[512,1024]{1,0:T(8,128)(2,1)S(1)}, bf16[512,1024]{1,0:T(8,128)(2,1)}, u32[]{:S(2)}, u32[]{:S(2)}) %collective-permute-start.4) | collective-permute-done | bytes 1048608 | tf_op jit(solution)/shard_map/ppermute | solution.py:345
  224.8 9.5 %fusion.108 = f32[1024,2816]{1,0:T(8,128)S(1)} fusion(bf16[1024,2816]{1,0:T(8,128)(2,1)} %bitcast.358, bf16[512,1024]{1,0:T(8,128)(2,1)} %collective-permute-done.4, bf16[512,1024]{1,0:T(8,128)(2,1)} %copy-done.56), kind=kOutput, calls=%fused_computation.200 | convolution fusion | flops 5909774336 | bytes 19398656 | tf_op jit(solution)/shard_map/dot_general | solution.py:31
  234.4 4.5 fusion.14
  238.9 3.3 pad_maximum_fusion
  242.2 7.9 %fusion.75 = bf16[512,1024]{1,0:T(8,128)(2,1)S(1)} fusion(bf16[1024,2816]{1,0:T(8,128)(2,1)} %bitcast.359, bf16[1024,2816]{1,0:T(8,128)(2,1)S(1)} %pad_maximum_fusion), kind=kOutput, calls=%fused_computation.152 | convolution fusion | flops 2953314304 | bytes 9699328 | tf_op jit(solution)/shard_map/dot_general | solution.py:39
  256.7 6.3 %convolution_convert_fusion = bf16[1024,1408]{1,0:T(8,128)(2,1)} fusion(bf16[1024,2816]{1,0:T(8,128)(2,1)S(1)} %pad_maximum_fusion, s32[]{:T(128)S(6)} %select_n.323, bf16[512,1024]{1,0:T(8,128)(2,1)} %collective-permute-done.4, bf16[512,1024]{1,0:T(8,128)(2,1)S(1)} %copy-done.57), kind=kOutput, calls=%fused_computation.48 | convolution fusion | flops 2958426112 | bytes 7864324 | tf_op jit(solution)/shard_map/dot_general | solution.py:35
  264.8 6.1 %fusion.179 = f32[1024,1024]{1,0:T(8,128)S(1)} fusion(bf16[1024,1408]{1,0:T(8,128)(2,1)} %copy-done.24, bf16[1408,1024]{1,0:T(8,128)(2,1)} %bitcast.285), kind=kOutput, calls=%fused_computation.363 | convolution fusion | flops 2952790016 | bytes 9961472 | tf_op jit(solution)/shard_map/dot_general | solution.py:31
  280.8 6.9 %add_convert_fusion = bf16[1024,1408]{1,0:T(8,128)(2,1)S(1)} fusion(bf16[1024,1408]{1,0:T(8,128)(2,1)} %collective-permute-done.9, bf16[1024,2816]{1,0:T(8,128)(2,1)} %copy-done.23, s32[]{:T(128)S(6)} %select_n.326, bf16[512,1024]{1,0:T(8,128)(2,1)} %collective-permute-done.4, bf16[512,1024]{1,0:T(8,128)(2,1)} %copy-done.56), kind=kOutput, calls=%fused_computation.28 | convolution fusion | flops 2961309696 | bytes 10747908 | tf_op jit(solution)/shard_map/dot_general | solution.py:35
  287.8 4.3 collective-permute-done.8
  292.1 7.6 %multiply_reduce_fusion = (f32[1024]{0:T(1024)S(1)}, f32[512]{0:T(512)S(1)}, f32[512,1024]{1,0:T(8,128)}) fusion(f32[512,1024]{1,0:T(8,128)S(1)} %get-tuple-element.249, f32[512]{0:T(512)S(1)} %get-tuple-element.233, bf16[256,1024]{1,0:T(8,128)(2,1)} %collective-permute-done.8, bf16[256,1024]{1,0:T(8,128)(2,1)} %collective-permute-done.7, ...), kind=kOutput, calls=%fused_computation.98 | convolution fusion | flops 2958555648 | bytes 13905920 | tf_op jit(solution)/shard_map/dot_general | solution.py:39
  301.3 4.2 fusion.167
  305.5 4.3 fusion.78.dc_ref
  309.8 12.5 %attend_back.2 = (bf16[512,1024]{1,0:T(8,128)(2,1)S(1)}, bf16[512,2048]{1,0:T(8,128)(2,1)}) custom-call(s32[2,2]{1,0:T(2,128)S(1)} %get-tuple-element.255.first_ref, s32[2,2]{1,0:T(2,128)S(1)} %get-tuple-element.254.stop_ref, s32[2,1,256]{2,1,0:T(1,128)S(1)} %broadcast_in_dim.83.lo_ref, s32[2,1,256]{2,1,0:T(1,128)S(1)} %broadcast_in_dim_broadcast_in_dim.5.hi_ref, ...), custom_call_target="tpu_custom_call" | custom-call | flops 5368709120 | bytes 6291456 | tf_op jit(solution)/shard_map/attend_back/pallas_call | solution.py:211
  329.6 4.5 collective-permute-done.11
  336.9 4.2 fusion.6
  357.8 3.5 fusion.33
  374.4 25.5 %attend_back.3 = (bf16[512,1024]{1,0:T(8,128)(2,1)S(1)}, bf16[2048,2048]{1,0:T(8,128)(2,1)}) custom-call(s32[2,2]{1,0:T(2,128)S(1)} %get-tuple-element.253.first_ref, s32[2,2]{1,0:T(2,128)S(1)} %get-tuple-element.236.stop_ref, s32[2,1,256]{2,1,0:T(1,128)S(1)} %broadcast_in_dim.73.lo_ref, s32[2,1,256]{2,1,0:T(1,128)S(1)} %bitcast.269, ...), custom_call_target="tpu_custom_call" | custom-call | flops 21474836480 | bytes 18874368 | tf_op jit(solution)/shard_map/attend_back/pallas_call | solution.py:211
  399.9 4.1 fusion.84
  414.0 3.7 fusion.66
  420.8 3.6 collective-permute-start.19
  424.4 3.7 fusion.63
  433.5 3.5 collective-permute-done.19
  438.3 5.1 fusion.18
  443.4 3.6 fusion.17
  455.5 14.5 %fusion.180 = f32[2048,1024]{1,0:T(8,128)} fusion(bf16[2048,2048]{1,0:T(8,128)(2,1)} %get-tuple-element.124, bf16[1024,2048]{1,0:T(8,128)(2,1)} %pad_maximum_fusion.1), kind=kOutput, calls=%fused_computation.364 | convolution fusion | flops 8589934592 | bytes 20971520 | tf_op jit(solution)/shard_map/dot_general | solution.py:39
  471.8 4.3 fusion.47
  484.2 9.8 %collective-permute-done.22 = bf16[2,1024,128]{2,1,0:T(8,128)(2,1)} collective-permute-done((bf16[2,1024,128]{2,1,0:T(8,128)(2,1)}, bf16[2,1024,128]{2,1,0:T(8,128)(2,1)}, u32[]{:S(2)}, u32[]{:S(2)}) %collective-permute-start.22) | collective-permute-done | bytes 524320 | tf_op jit(solution)/shard_map/ppermute | solution.py:367
  497.6 5.3 all-gather.16.cloned.1.call-done
  502.9 6.1 %fusion.11 = (f32[1024]{0:T(1024)S(1)}, f32[2048]{0:T(1024)S(1)}) fusion(f32[2048,1024]{1,0:T(8,128)} %fusion.180, f32[2048]{0:T(1024)S(1)} %bitcast.317, bf16[4,1024,1024]{2,1,0:T(8,128)(2,1)} %param.9, s32[]{:T(128)S(6)} %select_n.287, f32[1024]{0:T(1024)S(1)} %bitcast.321), kind=kLoop, calls=%fused_computation.19 | loop fusion | flops 14676992 | bytes 12607492 | tf_op jit(solution)/shard_map/reduce_sum | solution.py:238
  512.1 4.5 fusion.59
  516.6 8.6 %fusion.1 = bf16[2048,1024]{1,0:T(8,128)(2,1)S(1)} fusion(f32[2,1024,1024]{2,1,0:T(8,128)} %fusion.59, f32[2048,1024]{1,0:T(8,128)} %fusion.180, f32[2048]{0:T(1024)S(1)} %broadcast_multiply_fusion, f32[2048]{0:T(1024)S(1)} %multiply_multiply_fusion, f32[1024]{0:T(1024)S(1)} %bitcast.322, f32[2048]{0:T(1024)S(1)} %bitcast.318, ...), kind=kLoop, calls=%fused_computation.3 | loop fusion | flops 16777216 | bytes 25194500 | tf_op jit(solution)/shard_map/convert_element_type | solution.py:480
  533.3 13.6 %all-gather.4 = f32[4,4,1024]{2,1,0:T(4,128)S(1)} all-gather(f32[1,4,1024]{2,1,0:T(4,128)S(1)} %add_bitcast_fusion), channel_id=4, replica_groups=mesh['section'=2,'group'=4,'dp'=4] {'dp'}, dimensions={0}, use_global_device_ids=true | all-gather | bytes 81920 | tf_op jit(solution)/shard_map/all_gather | solution.py:496
  547.9 5.0 collective-permute-done.28
  554.9 6.5 %collective-permute-done.30 = bf16[4,256,128]{2,1,0:T(8,128)(2,1)S(1)} collective-permute-done((bf16[4,256,128]{2,1,0:T(8,128)(2,1)S(1)}, bf16[4,256,128]{2,1,0:T(8,128)(2,1)S(1)}, u32[]{:S(2)}, u32[]{:S(2)}) %collective-permute-start.30) | collective-permute-done | bytes 262176 | tf_op jit(solution)/shard_map/ppermute | solution.py:503
  568.7 8.4 %maximum_convert_fusion = f32[128,5632]{1,0:T(8,128)} fusion(bf16[64,1408]{1,0:T(8,128)(2,1)S(1)} %get-tuple-element.201, bf16[64,1408]{1,0:T(8,128)(2,1)S(1)} %get-tuple-element.202, bf16[64,1408]{1,0:T(8,128)(2,1)S(1)} %get-tuple-element.203, bf16[64,1408]{1,0:T(8,128)(2,1)S(1)} %get-tuple-element.204, bf16[64,1408]{1,0:T(8,128)(2,1)S(1)} %get-tuple-element.205, ...), kind=kLoop, calls=%fused_computation.166 | loop fusion | flops 11534336 | bytes 4325376 | tf_op jit(solution)/shard_map/concatenate | solution.py:487
  578.0 9.5 %all-gather.3 = bf16[1408,256]{1,0:T(8,128)(2,1)S(1)} all-gather(bf16[352,256]{1,0:T(8,128)(2,1)S(1)} %add_convert_fusion.12), channel_id=5, replica_groups=mesh['section'=2,'group'=4,'dp'=4] {'group'}, dimensions={0}, use_global_device_ids=true | all-gather | bytes 901120 | tf_op jit(solution)/shard_map/all_gather | solution.py:451
  (388 shorter events, 190.8 us)
Async XLA Ops:
  7.2 15.8 %copy-start = (s32[4,256]{1,0:T(4,128)S(1)}, s32[4,256]{1,0:T(4,128)}, u32[]{:S(2)}) copy-start(s32[4,256]{1,0:T(4,128)} %param.11) | copy-start | bytes 12292
  7.2 128.2 %all-gather.14.cloned.1.call-start = ((), (), s32[]{:S(2)}) async-start(), calls=%async_computation.10 | async-start | bytes 17301504 | tf_op jit(solution)/shard_map/all_gather | solution.py:264
  9.3 215.5 %all-gather.10.cloned.1.call-start = ((), (), s32[]{:S(2)}) async-start(), calls=%async_computation.4 | async-start | bytes 6127616 | tf_op jit(solution)/shard_map/all_gather | solution.py:287
  11.9 33.9 %collective-permute-start = (bf16[88,1024]{1,0:T(8,128)(2,1)S(1)}, bf16[88,1024]{1,0:T(8,128)(2,1)}, u32[]{:S(2)}, u32[]{:S(2)}) collective-permute-start(bf16[88,1024]{1,0:T(8,128)(2,1)S(1)} %get-tuple-element.166), channel_id=1, source_target_pairs={{0,1},{1,2},{2,3},{3,0},{4,5},{5,6},{6,7},{7,4},{8,9},{9,10},{10,1... | collective-permute-start | bytes 540680 | tf_op jit(solution)/shard_map/ppermute | solution.py:293
  14.9 32.5 %collective-permute-start.1 = (bf16[88,1024]{1,0:T(8,128)(2,1)S(1)}, bf16[88,1024]{1,0:T(8,128)(2,1)}, u32[]{:S(2)}, u32[]{:S(2)}) collective-permute-start(bf16[88,1024]{1,0:T(8,128)(2,1)S(1)} %get-tuple-element.166), channel_id=1, source_target_pairs={{0,2},{1,3},{2,0},{3,1},{4,6},{5,7},{6,4},{7,5},{8,10},{9,11},{10,... | collective-permute-start | bytes 540680 | tf_op jit(solution)/shard_map/ppermute | solution.py:293
  17.5 31.5 %collective-permute-start.2 = (bf16[88,1024]{1,0:T(8,128)(2,1)S(1)}, bf16[88,1024]{1,0:T(8,128)(2,1)}, u32[]{:S(2)}, u32[]{:S(2)}) collective-permute-start(bf16[88,1024]{1,0:T(8,128)(2,1)S(1)} %get-tuple-element.166), channel_id=1, source_target_pairs={{0,3},{1,0},{2,1},{3,2},{4,7},{5,4},{6,5},{7,6},{8,11},{9,8},{10,9... | collective-permute-start | bytes 540680 | tf_op jit(solution)/shard_map/ppermute | solution.py:293
  20.2 10.4 %collective-permute-start.6 = (bf16[32,2816]{1,0:T(8,128)(2,1)S(1)}, bf16[32,2816]{1,0:T(8,128)(2,1)S(1)}, u32[]{:S(2)}, u32[]{:S(2)}) collective-permute-start(bf16[32,2816]{1,0:T(8,128)(2,1)S(1)} %pad_maximum_fusion.16), channel_id=1, source_target_pairs={{0,16},{16,0},{1,17},{17,1},{2,18},{18,2},{3,19},{19,3},{4,20},{20... | collective-permute-start | bytes 540680 | tf_op jit(solution)/shard_map/ppermute | solution.py:285
  30.6 233.7 %copy-start.69 = (f32[1,8,2,128]{3,2,1,0:T(2,128)}, f32[1,8,2,128]{3,2,1,0:T(2,128)S(1)}, u32[]{:S(2)}) copy-start(f32[1,8,2,128]{3,2,1,0:T(2,128)S(1)} %get-tuple-element.226) | copy-start | bytes 24580
  31.7 305.3 %reduce-scatter.5.cloned.1.call-start = ((), (), s32[]{:S(2)}) async-start(), calls=%async_computation.5 | async-start | bytes 1802240 | tf_op jit(solution)/shard_map/reduce_scatter | solution.py:382
  144.7 48.5 %collective-permute-start.3 = (bf16[4,88,1024]{2,1,0:T(8,128)(2,1)}, bf16[4,88,1024]{2,1,0:T(8,128)(2,1)S(1)}, u32[]{:S(2)}, u32[]{:S(2)}) collective-permute-start(bf16[4,88,1024]{2,1,0:T(8,128)(2,1)} %bitcast_dynamic-update-slice_fusion), channel_id=1, source_target_pairs={{0,8},{4,12},{8,0},{12,4},{1,9},{5,13},{9,1},{13,5},{2,10},{6,14},... | collective-permute-start | bytes 2162696 | tf_op jit(solution)/shard_map/ppermute | solution.py:276
  157.3 15.8 %copy-start.19 = (f32[512,1024]{1,0:T(8,128)S(1)}, f32[512,1024]{1,0:T(8,128)}, u32[]{:S(2)}) copy-start(f32[512,1024]{1,0:T(8,128)} %bitcast_divide_fusion) | copy-start | bytes 6291460
  176.1 19.2 %copy-start.58 = (bf16[512,1024]{1,0:T(8,128)(2,1)}, bf16[512,1024]{1,0:T(8,128)(2,1)S(1)}, u32[]{:S(2)}) copy-start(bf16[512,1024]{1,0:T(8,128)(2,1)S(1)} %get-tuple-element.247) | copy-start | bytes 3145732
  194.8 9.0 %collective-permute-start.5 = (bf16[2,4,88,1024]{3,2,0,1:T(8,128)(2,1)S(1)}, bf16[2,4,88,1024]{3,2,0,1:T(8,128)(2,1)S(1)}, u32[]{:S(2)}, u32[]{:S(2)}) collective-permute-start(bf16[2,4,88,1024]{3,2,0,1:T(8,128)(2,1)S(1)} %maximum_select_fusion.3), channel_id=1, source_target_pairs={{0,4},{4,0},{8,12},{12,8},{1,5},{5,1},{9,13},{13,9},{2,6},{6,2},{1... | collective-permute-start | bytes 4325384 | tf_op jit(solution)/shard_map/ppermute | solution.py:276
  198.6 26.3 %collective-permute-start.4 = (bf16[512,1024]{1,0:T(8,128)(2,1)S(1)}, bf16[512,1024]{1,0:T(8,128)(2,1)}, u32[]{:S(2)}, u32[]{:S(2)}) collective-permute-start(bf16[512,1024]{1,0:T(8,128)(2,1)S(1)} %multiply_convert_fusion.2), channel_id=1, source_target_pairs={{0,16},{16,0},{1,17},{17,1},{2,18},{18,2},{3,19},{19,3},{4,20},{20... | collective-permute-start | bytes 3145736 | tf_op jit(solution)/shard_map/ppermute | solution.py:345
  238.9 13.8 %copy-start.24 = (bf16[1024,1408]{1,0:T(8,128)(2,1)}, bf16[1024,1408]{1,0:T(8,128)(2,1)S(1)}, u32[]{:S(2)}) copy-start(bf16[1024,1408]{1,0:T(8,128)(2,1)S(1)} %get-tuple-element.173) | copy-start | bytes 8650756
  251.0 13.3 %collective-permute-start.7 = (bf16[256,1024]{1,0:T(8,128)(2,1)S(1)}, bf16[256,1024]{1,0:T(8,128)(2,1)}, u32[]{:S(2)}, u32[]{:S(2)}) collective-permute-start(bf16[256,1024]{1,0:T(8,128)(2,1)S(1)} %get-tuple-element.213), channel_id=1, source_target_pairs={{0,16},{16,0},{1,17},{17,1},{2,18},{18,2},{3,19},{19,3},{4,20},{20... | collective-permute-start | bytes 1572872 | tf_op jit(solution)/shard_map/ppermute | solution.py:398
  264.3 16.5 %collective-permute-start.9 = (bf16[1024,1408]{1,0:T(8,128)(2,1)}, bf16[1024,1408]{1,0:T(8,128)(2,1)}, u32[]{:S(2)}, u32[]{:S(2)}) collective-permute-start(bf16[1024,1408]{1,0:T(8,128)(2,1)} %convolution_convert_fusion), channel_id=1, source_target_pairs={{0,4},{4,0},{8,12},{12,8},{1,5},{5,1},{9,13},{13,9},{2,6},{6,2},{1... | collective-permute-start | bytes 8650760 | tf_op jit(solution)/shard_map/ppermute | solution.py:392
  264.4 14.8 %collective-permute-start.10 = (bf16[1408,512]{1,0:T(8,128)(2,1)}, bf16[1408,512]{1,0:T(8,128)(2,1)S(1)}, u32[]{:S(2)}, u32[]{:S(2)}) collective-permute-start(bf16[1408,512]{1,0:T(8,128)(2,1)} %convolution_convert_fusion.4), channel_id=1, source_target_pairs={{0,4},{4,0},{8,12},{12,8},{1,5},{5,1},{9,13},{13,9},{2,6},{6,2},{1... | collective-permute-start | bytes 4325384 | tf_op jit(solution)/shard_map/ppermute | solution.py:392
  277.7 14.4 %collective-permute-start.8 = (bf16[256,1024]{1,0:T(8,128)(2,1)}, bf16[256,1024]{1,0:T(8,128)(2,1)}, u32[]{:S(2)}, u32[]{:S(2)}) collective-permute-start(bf16[256,1024]{1,0:T(8,128)(2,1)} %get-tuple-element.93), channel_id=1, source_target_pairs={{0,16},{16,0},{1,17},{17,1},{2,18},{18,2},{3,19},{19,3},{4,20},{20... | collective-permute-start | bytes 1572872 | tf_op jit(solution)/shard_map/ppermute | solution.py:402
  300.9 33.1 %collective-permute-start.11 = (bf16[2,4,1,64,1408]{4,3,2,1,0:T(8,128)(2,1)}, bf16[2,4,1,64,1408]{4,3,2,1,0:T(8,128)(2,1)}, u32[]{:S(2)}, u32[]{:S(2)}) collective-permute-start(bf16[2,4,1,64,1408]{4,3,2,1,0:T(8,128)(2,1)} %constant_dynamic-slice_fusion.11), channel_id=1, source_target_pairs={{0,8},{4,12},{8,0},{12,4},{1,9},{5,13},{9,1},{13,5},{2,10},{6,14},... | collective-permute-start | bytes 4325384 | tf_op jit(solution)/shard_map/ppermute | solution.py:367
  301.3 145.7 %reduce-scatter.7.cloned.1.call-start = ((), (), s32[]{:S(2)}) async-start(), calls=%async_computation.6 | async-start | bytes 1802240 | tf_op jit(solution)/shard_map/reduce_scatter | solution.py:382
  305.5 16.8 %copy-start.54 = (bf16[512,1024]{1,0:T(8,128)(2,1)}, bf16[512,1024]{1,0:T(8,128)(2,1)S(1)}, u32[]{:S(2)}) copy-start(bf16[512,1024]{1,0:T(8,128)(2,1)S(1)} %get-tuple-element.163) | copy-start | bytes 3145732
  336.9 30.9 %collective-permute-start.12 = (bf16[4,1024,512]{2,1,0:T(8,128)(2,1)}, bf16[4,1024,512]{2,1,0:T(8,128)(2,1)}, u32[]{:S(2)}, u32[]{:S(2)}) collective-permute-start(bf16[4,1024,512]{2,1,0:T(8,128)(2,1)} %pad_maximum_fusion.2), channel_id=1, source_target_pairs={{0,4},{4,0},{8,12},{12,8},{1,5},{5,1},{9,13},{13,9},{2,6},{6,2},{1... | collective-permute-start | bytes 12582920 | tf_op jit(solution)/shard_map/ppermute | solution.py:392
  341.2 31.0 %collective-permute-start.13 = (bf16[1024,512]{1,0:T(8,128)(2,1)}, bf16[1024,512]{1,0:T(8,128)(2,1)}, u32[]{:S(2)}, u32[]{:S(2)}) collective-permute-start(bf16[1024,512]{1,0:T(8,128)(2,1)} %fusion.35), channel_id=1, source_target_pairs={{0,16},{16,0},{1,17},{17,1},{2,18},{18,2},{3,19},{19,3},{4,20},{20... | collective-permute-start | bytes 3145736 | tf_op jit(solution)/shard_map/ppermute | solution.py:410
  351.4 146.2 %reduce-scatter.9.cloned.1.call-start = ((), (), s32[]{:S(2)}) async-start(), calls=%async_computation.7 | async-start | bytes 1310720 | tf_op jit(solution)/shard_map/reduce_scatter | solution.py:382
  372.5 35.4 %collective-permute-start.15 = (bf16[2,1024,256]{2,1,0:T(8,128)(2,1)S(1)}, bf16[2,1024,256]{2,1,0:T(8,128)(2,1)}, u32[]{:S(2)}, u32[]{:S(2)}) collective-permute-start(bf16[2,1024,256]{2,1,0:T(8,128)(2,1)S(1)} %constant_dynamic-slice_fusion.9), channel_id=1, source_target_pairs={{0,8},{4,12},{8,0},{12,4},{1,9},{5,13},{9,1},{13,5},{2,10},{6,14},... | collective-permute-start | bytes 3145736 | tf_op jit(solution)/shard_map/ppermute | solution.py:367
  373.7 35.8 %collective-permute-start.14 = (bf16[2,1024,256]{2,1,0:T(8,128)(2,1)S(1)}, bf16[2,1024,256]{2,1,0:T(8,128)(2,1)S(1)}, u32[]{:S(2)}, u32[]{:S(2)}) collective-permute-start(bf16[2,1024,256]{2,1,0:T(8,128)(2,1)S(1)} %constant_dynamic-slice_fusion.10), channel_id=1, source_target_pairs={{0,16},{16,0},{1,17},{17,1},{2,18},{18,2},{3,19},{19,3},{4,20},{20... | collective-permute-start | bytes 3145736 | tf_op jit(solution)/shard_map/ppermute | solution.py:367
  374.4 25.5 %copy-start.13 = (bf16[2048,1024]{1,0:T(8,128)(2,1)S(1)}, bf16[2048,1024]{1,0:T(8,128)(2,1)}, u32[]{:S(2)}) copy-start(bf16[2048,1024]{1,0:T(8,128)(2,1)} %fusion.6) | copy-start | bytes 12582916
  413.5 24.8 %collective-permute-start.17 = (bf16[2,1024,512]{2,1,0:T(8,128)(2,1)}, bf16[2,1024,512]{2,1,0:T(8,128)(2,1)}, u32[]{:S(2)}, u32[]{:S(2)}) collective-permute-start(bf16[2,1024,512]{2,1,0:T(8,128)(2,1)} %pad_maximum_fusion.7), channel_id=1, source_target_pairs={{0,4},{4,0},{8,12},{12,8},{1,5},{5,1},{9,13},{13,9},{2,6},{6,2},{1... | collective-permute-start | bytes 6291464 | tf_op jit(solution)/shard_map/ppermute | solution.py:392
  413.7 29.6 %collective-permute-start.16 = (bf16[2,1024,512]{2,1,0:T(8,128)(2,1)}, bf16[2,1024,512]{2,1,0:T(8,128)(2,1)}, u32[]{:S(2)}, u32[]{:S(2)}) collective-permute-start(bf16[2,1024,512]{2,1,0:T(8,128)(2,1)} %pad_maximum_fusion.6), channel_id=1, source_target_pairs={{0,4},{4,0},{8,12},{12,8},{1,5},{5,1},{9,13},{13,9},{2,6},{6,2},{1... | collective-permute-start | bytes 6291464 | tf_op jit(solution)/shard_map/ppermute | solution.py:392
  417.7 15.6 %collective-permute-start.18 = (bf16[2,1024,128]{2,1,0:T(8,128)(2,1)S(1)}, bf16[2,1024,128]{2,1,0:T(8,128)(2,1)S(1)}, u32[]{:S(2)}, u32[]{:S(2)}) collective-permute-start(bf16[2,1024,128]{2,1,0:T(8,128)(2,1)S(1)} %constant_dynamic-slice_fusion.8), channel_id=1, source_target_pairs={{0,8},{4,12},{8,0},{12,4},{1,9},{5,13},{9,1},{13,5},{2,10},{6,14},... | collective-permute-start | bytes 1572872 | tf_op jit(solution)/shard_map/ppermute | solution.py:367
  420.8 16.2 %collective-permute-start.19 = (bf16[2,1024,128]{2,1,0:T(8,128)(2,1)S(1)}, bf16[2,1024,128]{2,1,0:T(8,128)(2,1)S(1)}, u32[]{:S(2)}, u32[]{:S(2)}) collective-permute-start(bf16[2,1024,128]{2,1,0:T(8,128)(2,1)S(1)} %constant_dynamic-slice_fusion.7), channel_id=1, source_target_pairs={{0,16},{16,0},{1,17},{17,1},{2,18},{18,2},{3,19},{19,3},{4,20},{20... | collective-permute-start | bytes 1572872 | tf_op jit(solution)/shard_map/ppermute | solution.py:367
  448.9 21.1 %collective-permute-start.24 = (bf16[64,1408]{1,0:T(8,128)(2,1)}, bf16[64,1408]{1,0:T(8,128)(2,1)}, u32[]{:S(2)}, u32[]{:S(2)}) collective-permute-start(bf16[64,1408]{1,0:T(8,128)(2,1)} %get-tuple-element.221), channel_id=1, source_target_pairs={{0,16},{16,0},{1,17},{17,1},{2,18},{18,2},{3,19},{19,3},{4,20},{20... | collective-permute-start | bytes 540680 | tf_op jit(solution)/shard_map/ppermute | solution.py:460
  452.3 24.7 %collective-permute-start.21 = (bf16[2,1024,256]{2,1,0:T(8,128)(2,1)S(1)}, bf16[2,1024,256]{2,1,0:T(8,128)(2,1)}, u32[]{:S(2)}, u32[]{:S(2)}) collective-permute-start(bf16[2,1024,256]{2,1,0:T(8,128)(2,1)S(1)} %constant_dynamic-slice_fusion.5), channel_id=1, source_target_pairs={{0,8},{4,12},{8,0},{12,4},{1,9},{5,13},{9,1},{13,5},{2,10},{6,14},... | collective-permute-start | bytes 3145736 | tf_op jit(solution)/shard_map/ppermute | solution.py:367
  455.1 24.2 %collective-permute-start.20 = (bf16[2,1024,256]{2,1,0:T(8,128)(2,1)}, bf16[2,1024,256]{2,1,0:T(8,128)(2,1)}, u32[]{:S(2)}, u32[]{:S(2)}) collective-permute-start(bf16[2,1024,256]{2,1,0:T(8,128)(2,1)} %constant_dynamic-slice_fusion.6), channel_id=1, source_target_pairs={{0,16},{16,0},{1,17},{17,1},{2,18},{18,2},{3,19},{19,3},{4,20},{20... | collective-permute-start | bytes 3145736 | tf_op jit(solution)/shard_map/ppermute | solution.py:367
  455.4 47.5 %all-gather.16.cloned.1.call-start = ((), (), s32[]{:S(2)}) async-start(), calls=%async_computation.11 | async-start | bytes 1802240 | tf_op jit(solution)/shard_map/all_gather | solution.py:451
  471.8 81.2 %reduce-scatter.11.cloned.1.call-start = ((), (), s32[]{:S(2)}) async-start(), calls=%async_computation.8 | async-start | bytes 1310720 | tf_op jit(solution)/shard_map/reduce_scatter | solution.py:382
  481.7 12.2 %collective-permute-start.22 = (bf16[2,1024,128]{2,1,0:T(8,128)(2,1)}, bf16[2,1024,128]{2,1,0:T(8,128)(2,1)}, u32[]{:S(2)}, u32[]{:S(2)}) collective-permute-start(bf16[2,1024,128]{2,1,0:T(8,128)(2,1)} %constant_dynamic-slice_fusion.4), channel_id=1, source_target_pairs={{0,8},{4,12},{8,0},{12,4},{1,9},{5,13},{9,1},{13,5},{2,10},{6,14},... | collective-permute-start | bytes 1572872 | tf_op jit(solution)/shard_map/ppermute | solution.py:367
  483.2 12.1 %collective-permute-start.23 = (bf16[2,1024,128]{2,1,0:T(8,128)(2,1)}, bf16[2,1024,128]{2,1,0:T(8,128)(2,1)}, u32[]{:S(2)}, u32[]{:S(2)}) collective-permute-start(bf16[2,1024,128]{2,1,0:T(8,128)(2,1)} %constant_dynamic-slice_fusion.3), channel_id=1, source_target_pairs={{0,16},{16,0},{1,17},{17,1},{2,18},{18,2},{3,19},{19,3},{4,20},{20... | collective-permute-start | bytes 1572872 | tf_op jit(solution)/shard_map/ppermute | solution.py:367
  509.9 17.6 %collective-permute-start.25 = (f32[4,1024]{1,0:T(4,128)S(1)}, f32[4,1024]{1,0:T(4,128)S(1)}, u32[]{:S(2)}, u32[]{:S(2)}) collective-permute-start(f32[4,1024]{1,0:T(4,128)S(1)} %pad_maximum_fusion.17), channel_id=1, source_target_pairs={{0,16},{16,0},{1,17},{17,1},{2,18},{18,2},{3,19},{19,3},{4,20},{20... | collective-permute-start | bytes 49160 | tf_op jit(solution)/shard_map/ppermute | solution.py:486
  516.6 74.7 %all-gather.12.cloned.1.call-start = ((), (), s32[]{:S(2)}) async-start(), calls=%async_computation.9 | async-start | bytes 2621440 | tf_op jit(solution)/shard_map/all_gather | solution.py:451
  527.5 34.9 %copy-start.17 = (f32[512,1024]{1,0:T(8,128)S(1)}, f32[512,1024]{1,0:T(8,128)}, u32[]{:S(2)}) copy-start(f32[512,1024]{1,0:T(8,128)} %copy-done.16) | copy-start | bytes 6291460
  527.5 25.4 %collective-permute-start.28 = (bf16[1024,512]{1,0:T(8,128)(2,1)}, bf16[1024,512]{1,0:T(8,128)(2,1)}, u32[]{:S(2)}, u32[]{:S(2)}) collective-permute-start(bf16[1024,512]{1,0:T(8,128)(2,1)} %get-tuple-element.139), channel_id=1, source_target_pairs={{0,16},{16,0},{1,17},{17,1},{2,18},{18,2},{3,19},{19,3},{4,20},{20... | collective-permute-start | bytes 3145736 | tf_op jit(solution)/shard_map/ppermute | solution.py:493
  528.4 1.2 collective-permute-start.26
  529.6 3.7 collective-permute-start.27
  531.2 15.7 %collective-permute-start.29 = (bf16[352,256]{1,0:T(8,128)(2,1)}, bf16[352,256]{1,0:T(8,128)(2,1)S(1)}, u32[]{:S(2)}, u32[]{:S(2)}) collective-permute-start(bf16[352,256]{1,0:T(8,128)(2,1)} %constant_dynamic-slice_fusion.1), channel_id=1, source_target_pairs={{0,8},{4,12},{8,0},{12,4},{1,9},{5,13},{9,1},{13,5},{2,10},{6,14},... | collective-permute-start | bytes 540680 | tf_op jit(solution)/shard_map/ppermute | solution.py:367
  554.0 7.4 %collective-permute-start.30 = (bf16[4,256,128]{2,1,0:T(8,128)(2,1)S(1)}, bf16[4,256,128]{2,1,0:T(8,128)(2,1)S(1)}, u32[]{:S(2)}, u32[]{:S(2)}) collective-permute-start(bf16[4,256,128]{2,1,0:T(8,128)(2,1)S(1)} %get-tuple-element.219), channel_id=1, source_target_pairs={{0,16},{16,0},{1,17},{17,1},{2,18},{18,2},{3,19},{19,3},{4,20},{20... | collective-permute-start | bytes 786440 | tf_op jit(solution)/shard_map/ppermute | solution.py:503
  567.9 23.4 %collective-permute-start.31 = (bf16[1024,512]{1,0:T(8,128)(2,1)S(1)}, bf16[1024,512]{1,0:T(8,128)(2,1)}, u32[]{:S(2)}, u32[]{:S(2)}) collective-permute-start(bf16[1024,512]{1,0:T(8,128)(2,1)S(1)} %get-tuple-element.146), channel_id=1, source_target_pairs={{0,16},{16,0},{1,17},{17,1},{2,18},{18,2},{3,19},{19,3},{4,20},{20... | collective-permute-start | bytes 3145736 | tf_op jit(solution)/shard_map/ppermute | solution.py:500
  (72 other events, 323.9 us)
Sparse Core Ops, SparseCore 0:
  11.6 123.7 all-gather.13
  138.2 60.4 all-gather.9
  301.4 33.4 reduce-scatter.4
  351.5 32.2 reduce-scatter.6
  455.6 27.3 reduce-scatter.8
  485.1 17.8 all-gather.15
  516.7 26.7 reduce-scatter.10
  562.5 23.3 all-gather.11

commit v15 on v13

--- a/solution.py
+++ b/solution.py
@@ -452,8 +452,8 @@
     half_one = over_section(half_one[0], 2), over_side(half_one[1], 2)
     grad_query_in, grad_key_in, half_one = together((grad_query_in, grad_key_in, half_one))
     half_one = jnp.concatenate([over_side(half_one[0], 2), over_section(half_one[1], 2)], axis=0)
-    grad_query_in, grad_key_in, half_one, sum_two, sum_down, sum_in = together(
-        (grad_query_in, grad_key_in, half_one, sum_two, sum_down, sum_in)
+    grad_query_in, grad_key_in, half_one, sum_two, sum_down = together(
+        (grad_query_in, grad_key_in, half_one, sum_two, sum_down)
     )
     sum_down = over_side(sum_down, 1)
     sum_one = line_sum(half_one, 1)

time: 612 us -> 606 us (level)
  starting transfers between devices: 38.7 us -> 27.9 us
  waiting for transfers between devices: 150 us -> 142 us
  matrix products: 168 us -> 175 us
  other arithmetic: 113 us -> 106 us
    dot_general x11, matrix products: 57 us -> 66.4 us  [nt(): lax.dot_general(left, right, (((1,), (1,)), ((), ())), preferred_element_...]
    ppermute x10, waiting for transfers between devices: 28.5 us -> 22.3 us  [exchanged(): lax.ppermute(other, axis, pairs).astype(F32)]
    unnamed x171 -> x189, local copies, waits for them, and re-layouts: 14.6 us -> 16.3 us
  transfers between devices with their start and end apart: 40 -> 40, of which waited for: 14 -> 12; matrix products, arithmetic and copies ran while one was open for 40% -> 43% of each run, Pallas kernels for 10% -> 11%
where the time goes in v15:
time: 606 us; the launch traced here: 600 us
  matrix products  175 us (29%)
  waiting for transfers between devices  142 us (23%)
  other arithmetic  106 us (17%)
  Pallas kernels  64.6 us (11%)
  local copies, waits for them, and re-layouts  39.2 us (6%)
  blocking collectives  29.7 us (5%)
  starting transfers between devices  27.9 us (5%)
  between operations  16.1 us (3%)
    all_gather x1, waiting for transfers between devices, shards(): lax.all_gather(matrix, ('section', 'group', 'dp'), axis=0, tiled=True)  85.6 us
    dot_general x11, matrix products, nt(): lax.dot_general(left, right, (((1,), (1,)), ((), ())), preferred_element_...  66.4 us
    dot_general x10, matrix products, nn(): return jnp.dot(left, right, preferred_element_type=F32)  52.8 us
    dot_general x20, matrix products, tn(): lax.dot_general(left, right, (((0,), (0,)), ((), ())), preferred_element_...  50.5 us
    pallas_call x2, Pallas kernels, attend_back(): pl.pallas_call(functools.partial(attend_back_kernel, chunk, spans), grid_...  42.6 us
    ppermute x10, waiting for transfers between devices, exchanged(): lax.ppermute(other, axis, pairs).astype(F32)  22.3 us
    pallas_call x2, Pallas kernels, attend(): pl.pallas_call(functools.partial(attend_kernel, chunk, spans), grid_spec=...  22 us
    unnamed x189, local copies, waits for them, and re-layouts  16.3 us
  transfers between devices with their start and end apart: 40, of which 12 were waited for; matrix products, arithmetic and copies ran while one was open for 43% of the time, Pallas kernels for 11%

profile of v15, /device:TPU:0, one launch (start us, length us, event | category | flops | bytes accessed | tf_op | source)
XLA Modules:
  0.0 600.3 jit_solution(7632891504671048173)
XLA Ops:
  24.2 3.7 multiply_reduce_fusion.5
  27.9 3.8 fusion.2
  33.9 4.7 all_gather.31
  39.3 4.2 fusion.4
  49.7 85.6 %all-gather.14.cloned.1.call-done = bf16[1,8192,1024]{2,1,0:T(8,128)(2,1)} async-done(((bf16[1,256,1024]{2,1,0:T(8,128)(2,1)}), bf16[1,8192,1024]{2,1,0:T(8,128)(2,1)}) %all-gather.14.cloned.1.call-update) | async-done | bytes 16777232 | tf_op jit(solution)/shard_map/all_gather | solution.py:264
  135.3 9.4 %convolution_convert_fusion.2.v_ref = bf16[2048,1024]{1,0:T(8,128)(2,1)} fusion(bf16[2048,1024]{1,0:T(8,128)(2,1)} %bitcast.285, bf16[2,4,1024,1024]{3,2,1,0:T(8,128)(2,1)} %bitcast.348), kind=kOutput, calls=%fused_computation.50 | convolution fusion | flops 4297064448 | bytes 10485760 | tf_op jit(solution)/shard_map/dot_general | solution.py:31
  149.3 8.0 %convolution_convert_fusion.3.k_ref = bf16[2048,1024]{1,0:T(8,128)(2,1)} fusion(bf16[2048,1024]{1,0:T(8,128)(2,1)S(1)} %bitcast.286, bf16[2,4,1024,1024]{3,2,1,0:T(8,128)(2,1)} %bitcast.350), kind=kOutput, calls=%fused_computation.51 | convolution fusion | flops 4297064448 | bytes 10485760 | tf_op jit(solution)/shard_map/dot_general | solution.py:31
  157.2 17.9 %attend.2 = (bf16[512,1024]{1,0:T(8,128)(2,1)S(1)}, f32[2,8,2,256]{3,2,1,0:T(2,128)S(1)}) custom-call(s32[2,2]{1,0:T(2,128)S(1)} %get-tuple-element.248.first_ref, s32[2,2]{1,0:T(2,128)S(1)} %get-tuple-element.233.stop_ref, s32[2,1,256]{2,1,0:T(1,128)S(1)} %broadcast_in_dim.73.lo_ref, s32[2,1,256]{2,1,0:T(1,128)S(1)} %bitcast.270, ...), custom_call_target="tpu_custom_call" | custom-call | flops 8589934592 | bytes 18874368 | tf_op jit(solution)/shard_map/attend/pallas_call | solution.py:186
  175.2 3.4 fusion.24
  178.6 3.3 fusion.80.v_ref
  181.9 3.3 fusion.81.k_ref
  185.2 3.4 fusion.82.q_ref
  188.7 4.0 attend.3
  195.9 3.4 multiply_reduce_fusion.4
  204.7 5.8 convolution_convert_fusion.1
  210.5 14.6 %collective-permute-done.4 = bf16[512,1024]{1,0:T(8,128)(2,1)} collective-permute-done((bf16[512,1024]{1,0:T(8,128)(2,1)S(1)}, bf16[512,1024]{1,0:T(8,128)(2,1)}, u32[]{:S(2)}, u32[]{:S(2)}) %collective-permute-start.4) | collective-permute-done | bytes 1048608 | tf_op jit(solution)/shard_map/ppermute | solution.py:345
  225.1 9.5 %fusion.109 = f32[1024,2816]{1,0:T(8,128)S(1)} fusion(bf16[1024,2816]{1,0:T(8,128)(2,1)} %bitcast.364, bf16[512,1024]{1,0:T(8,128)(2,1)} %collective-permute-done.4, bf16[512,1024]{1,0:T(8,128)(2,1)} %copy-done.52), kind=kOutput, calls=%fused_computation.201 | convolution fusion | flops 5909774336 | bytes 19398656 | tf_op jit(solution)/shard_map/dot_general | solution.py:31
  234.7 4.6 fusion.14
  242.6 7.9 %fusion.76 = bf16[512,1024]{1,0:T(8,128)(2,1)S(1)} fusion(bf16[1024,2816]{1,0:T(8,128)(2,1)} %bitcast.365, bf16[1024,2816]{1,0:T(8,128)(2,1)S(1)} %pad_maximum_fusion), kind=kOutput, calls=%fused_computation.153 | convolution fusion | flops 2953314304 | bytes 9699328 | tf_op jit(solution)/shard_map/dot_general | solution.py:39
  255.9 6.3 %convolution_convert_fusion = bf16[1024,1408]{1,0:T(8,128)(2,1)} fusion(bf16[1024,2816]{1,0:T(8,128)(2,1)S(1)} %pad_maximum_fusion, s32[]{:T(128)S(6)} %select_n.315, bf16[512,1024]{1,0:T(8,128)(2,1)} %collective-permute-done.4, bf16[512,1024]{1,0:T(8,128)(2,1)S(1)} %copy-done.53), kind=kOutput, calls=%fused_computation.48 | convolution fusion | flops 2958426112 | bytes 7864324 | tf_op jit(solution)/shard_map/dot_general | solution.py:35
  265.5 6.1 %fusion.177 = f32[1024,1024]{1,0:T(8,128)S(1)} fusion(bf16[1024,1408]{1,0:T(8,128)(2,1)} %copy-done.26, bf16[1408,1024]{1,0:T(8,128)(2,1)} %bitcast.290), kind=kOutput, calls=%fused_computation.361 | convolution fusion | flops 2952790016 | bytes 9961472 | tf_op jit(solution)/shard_map/dot_general | solution.py:31
  280.4 6.9 %add_convert_fusion = bf16[1024,1408]{1,0:T(8,128)(2,1)S(1)} fusion(bf16[1024,1408]{1,0:T(8,128)(2,1)} %collective-permute-done.9, bf16[1024,2816]{1,0:T(8,128)(2,1)} %copy-done.25, s32[]{:T(128)S(6)} %select_n.318, bf16[512,1024]{1,0:T(8,128)(2,1)} %collective-permute-done.4, bf16[512,1024]{1,0:T(8,128)(2,1)} %copy-done.52), kind=kOutput, calls=%fused_computation.28 | convolution fusion | flops 2961309696 | bytes 10747908 | tf_op jit(solution)/shard_map/dot_general | solution.py:35
  287.3 4.9 collective-permute-done.8
  292.3 7.6 %multiply_reduce_fusion = (f32[1024]{0:T(1024)S(1)}, f32[512]{0:T(512)S(1)}, f32[512,1024]{1,0:T(8,128)}) fusion(f32[512,1024]{1,0:T(8,128)S(1)} %get-tuple-element.245, f32[512]{0:T(512)S(1)} %get-tuple-element.229, bf16[256,1024]{1,0:T(8,128)(2,1)} %collective-permute-done.8, bf16[256,1024]{1,0:T(8,128)(2,1)} %collective-permute-done.7, ...), kind=kOutput, calls=%fused_computation.98 | convolution fusion | flops 2958555648 | bytes 13905920 | tf_op jit(solution)/shard_map/dot_general | solution.py:39
  301.6 3.9 fusion.168
  305.6 4.3 fusion.79.dc_ref
  309.9 11.5 %attend_back.2 = (bf16[512,1024]{1,0:T(8,128)(2,1)S(1)}, bf16[512,1024]{1,0:T(8,128)(2,1)S(1)}, bf16[512,1024]{1,0:T(8,128)(2,1)S(1)}) custom-call(s32[2,2]{1,0:T(2,128)S(1)} %get-tuple-element.251.first_ref, s32[2,2]{1,0:T(2,128)S(1)} %get-tuple-element.250.stop_ref, s32[2,1,256]{2,1,0:T(1,128)S(1)} %broadcast_in_dim.83.lo_ref, ...), custom_call_target="tpu_custom_call" | custom-call | flops 5368709120 | bytes 6291456 | tf_op jit(solution)/shard_map/attend_back/pallas_call | solution.py:210
  328.1 6.0 collective-permute-done.11
  336.9 4.3 fusion.6
  357.0 3.6 fusion.33
  375.1 31.1 %attend_back.3 = (bf16[512,1024]{1,0:T(8,128)(2,1)S(1)}, bf16[2048,1024]{1,0:T(8,128)(2,1)}, bf16[2048,1024]{1,0:T(8,128)(2,1)}) custom-call(s32[2,2]{1,0:T(2,128)S(1)} %get-tuple-element.249.first_ref, s32[2,2]{1,0:T(2,128)S(1)} %get-tuple-element.232.stop_ref, s32[2,1,256]{2,1,0:T(1,128)S(1)} %broadcast_in_dim.73.lo_ref, s32[2,1,256]{2,1,0:T(1,128)S(1)} %bitcast.271, ...), custom_call_target="tpu_custom_call" | custom-call | flops 21474836480 | bytes 18874368 | tf_op jit(solution)/shard_map/attend_back/pallas_call | solution.py:210
  406.2 4.1 fusion.85
  422.5 3.7 fusion.67
  426.5 3.7 fusion.64
  432.4 6.9 %collective-permute-done.18 = bf16[2,1024,128]{2,1,0:T(8,128)(2,1)S(1)} collective-permute-done((bf16[2,1024,128]{2,1,0:T(8,128)(2,1)S(1)}, bf16[2,1024,128]{2,1,0:T(8,128)(2,1)S(1)}, u32[]{:S(2)}, u32[]{:S(2)}) %collective-permute-start.18) | collective-permute-done | bytes 524320 | tf_op jit(solution)/shard_map/ppermute | solution.py:363
  440.7 3.7 fusion.18
  444.8 3.6 fusion.17
  452.8 10.7 %fusion.49 = f32[2048,1024]{1,0:T(8,128)} fusion(bf16[2048,1024]{1,0:T(8,128)(2,1)} %get-tuple-element.130, bf16[2,4,1024,1024]{3,2,1,0:T(8,128)(2,1)} %bitcast.361), kind=kOutput, calls=%fused_computation.130 | convolution fusion | flops 4294967296 | bytes 14680064 | tf_op jit(solution)/shard_map/dot_general | solution.py:39
  463.6 13.2 %convolution_add_fusion = f32[2048,1024]{1,0:T(8,128)} fusion(f32[2048,1024]{1,0:T(8,128)} %fusion.49, bf16[2048,1024]{1,0:T(8,128)(2,1)} %get-tuple-element.129, bf16[2,4,1024,1024]{3,2,1,0:T(8,128)(2,1)} %bitcast.362), kind=kOutput, calls=%fused_computation.47 | convolution fusion | flops 4297064448 | bytes 23068672 | tf_op jit(solution)/shard_map/dot_general | solution.py:39
  476.8 4.2 fusion.47
  486.8 9.0 %collective-permute-done.22 = bf16[2,1024,128]{2,1,0:T(8,128)(2,1)S(1)} collective-permute-done((bf16[2,1024,128]{2,1,0:T(8,128)(2,1)S(1)}, bf16[2,1024,128]{2,1,0:T(8,128)(2,1)S(1)}, u32[]{:S(2)}, u32[]{:S(2)}) %collective-permute-start.22) | collective-permute-done | bytes 524320 | tf_op jit(solution)/shard_map/ppermute | solution.py:363
  499.4 4.0 collective-permute-done.31
  504.3 6.4 %fusion.11 = (f32[1024]{0:T(1024)S(1)}, f32[2048]{0:T(1024)S(1)}) fusion(f32[2048,1024]{1,0:T(8,128)} %convolution_add_fusion, f32[2048]{0:T(1024)S(1)} %bitcast.307, bf16[4,1024,1024]{2,1,0:T(8,128)(2,1)} %param.9, s32[]{:T(128)S(6)} %select_n.279, f32[1024]{0:T(1024)S(1)} %bitcast.311), kind=kLoop, calls=%fused_computation.19 | loop fusion | flops 14676992 | bytes 12607492 | tf_op jit(solution)/shard_map/reduce_sum | solution.py:238
  517.0 4.1 fusion.1
  529.2 13.8 %all-gather.4 = f32[4,4,1024]{2,1,0:T(4,128)S(1)} all-gather(f32[1,4,1024]{2,1,0:T(4,128)S(1)} %add_bitcast_fusion), channel_id=3, replica_groups=mesh['section'=2,'group'=4,'dp'=4] {'dp'}, dimensions={0}, use_global_device_ids=true | all-gather | bytes 81920 | tf_op jit(solution)/shard_map/all_gather | solution.py:483
  546.2 5.3 collective-permute-done.29
  561.0 8.6 %maximum_convert_fusion = f32[128,5632]{1,0:T(8,128)} fusion(bf16[64,1408]{1,0:T(8,128)(2,1)S(1)} %get-tuple-element.197, bf16[64,1408]{1,0:T(8,128)(2,1)S(1)} %get-tuple-element.198, bf16[64,1408]{1,0:T(8,128)(2,1)S(1)} %get-tuple-element.199, bf16[64,1408]{1,0:T(8,128)(2,1)S(1)} %get-tuple-element.200, bf16[64,1408]{1,0:T(8,128)(2,1)S(1)} %get-tuple-element.201, ...), kind=kLoop, calls=%fused_computation.167 | loop fusion | flops 11534336 | bytes 4325376 | tf_op jit(solution)/shard_map/concatenate | solution.py:474
  570.3 11.2 %all-gather.3 = bf16[1408,256]{1,0:T(8,128)(2,1)S(1)} all-gather(bf16[352,256]{1,0:T(8,128)(2,1)S(1)} %add_convert_fusion.12), channel_id=5, replica_groups=mesh['section'=2,'group'=4,'dp'=4] {'group'}, dimensions={0}, use_global_device_ids=true | all-gather | bytes 901120 | tf_op jit(solution)/shard_map/all_gather | solution.py:438
  (407 shorter events, 170.8 us)
Async XLA Ops:
  7.2 20.7 %copy-start = (s32[4,256]{1,0:T(4,128)S(1)}, s32[4,256]{1,0:T(4,128)}, u32[]{:S(2)}) copy-start(s32[4,256]{1,0:T(4,128)} %param.11) | copy-start | bytes 12292
  7.2 128.2 %all-gather.14.cloned.1.call-start = ((), (), s32[]{:S(2)}) async-start(), calls=%async_computation.10 | async-start | bytes 17301504 | tf_op jit(solution)/shard_map/all_gather | solution.py:264
  9.3 215.8 %all-gather.10.cloned.1.call-start = ((), (), s32[]{:S(2)}) async-start(), calls=%async_computation.4 | async-start | bytes 6127616 | tf_op jit(solution)/shard_map/all_gather | solution.py:287
  11.9 33.9 %collective-permute-start = (bf16[88,1024]{1,0:T(8,128)(2,1)S(1)}, bf16[88,1024]{1,0:T(8,128)(2,1)}, u32[]{:S(2)}, u32[]{:S(2)}) collective-permute-start(bf16[88,1024]{1,0:T(8,128)(2,1)S(1)} %get-tuple-element.170), channel_id=1, source_target_pairs={{0,1},{1,2},{2,3},{3,0},{4,5},{5,6},{6,7},{7,4},{8,9},{9,10},{10,1... | collective-permute-start | bytes 540680 | tf_op jit(solution)/shard_map/ppermute | solution.py:293
  14.9 32.5 %collective-permute-start.1 = (bf16[88,1024]{1,0:T(8,128)(2,1)S(1)}, bf16[88,1024]{1,0:T(8,128)(2,1)}, u32[]{:S(2)}, u32[]{:S(2)}) collective-permute-start(bf16[88,1024]{1,0:T(8,128)(2,1)S(1)} %get-tuple-element.170), channel_id=1, source_target_pairs={{0,2},{1,3},{2,0},{3,1},{4,6},{5,7},{6,4},{7,5},{8,10},{9,11},{10,... | collective-permute-start | bytes 540680 | tf_op jit(solution)/shard_map/ppermute | solution.py:293
  17.5 31.5 %collective-permute-start.2 = (bf16[88,1024]{1,0:T(8,128)(2,1)S(1)}, bf16[88,1024]{1,0:T(8,128)(2,1)S(1)}, u32[]{:S(2)}, u32[]{:S(2)}) collective-permute-start(bf16[88,1024]{1,0:T(8,128)(2,1)S(1)} %get-tuple-element.170), channel_id=1, source_target_pairs={{0,3},{1,0},{2,1},{3,2},{4,7},{5,4},{6,5},{7,6},{8,11},{9,8},{10,9... | collective-permute-start | bytes 540680 | tf_op jit(solution)/shard_map/ppermute | solution.py:293
  20.2 11.6 %collective-permute-start.6 = (bf16[32,2816]{1,0:T(8,128)(2,1)S(1)}, bf16[32,2816]{1,0:T(8,128)(2,1)S(1)}, u32[]{:S(2)}, u32[]{:S(2)}) collective-permute-start(bf16[32,2816]{1,0:T(8,128)(2,1)S(1)} %pad_maximum_fusion.15), channel_id=1, source_target_pairs={{0,16},{16,0},{1,17},{17,1},{2,18},{18,2},{3,19},{19,3},{4,20},{20... | collective-permute-start | bytes 540680 | tf_op jit(solution)/shard_map/ppermute | solution.py:285
  27.9 17.2 %copy-start.17 = (f32[2,256,1024]{2,1,0:T(8,128)}, f32[2,256,1024]{2,1,0:T(8,128)S(1)}, u32[]{:S(2)}) copy-start(f32[2,256,1024]{2,1,0:T(8,128)S(1)} %get-tuple-element.241) | copy-start | bytes 6291460
  32.6 304.4 %reduce-scatter.5.cloned.1.call-start = ((), (), s32[]{:S(2)}) async-start(), calls=%async_computation.5 | async-start | bytes 1802240 | tf_op jit(solution)/shard_map/reduce_scatter | solution.py:376
  39.2 225.6 %copy-start.65 = (f32[1,8,2,128]{3,2,1,0:T(2,128)}, f32[1,8,2,128]{3,2,1,0:T(2,128)S(1)}, u32[]{:S(2)}) copy-start(f32[1,8,2,128]{3,2,1,0:T(2,128)S(1)} %get-tuple-element.222) | copy-start | bytes 24580
  144.8 48.1 %collective-permute-start.3 = (bf16[4,88,1024]{2,1,0:T(8,128)(2,1)}, bf16[4,88,1024]{2,1,0:T(8,128)(2,1)S(1)}, u32[]{:S(2)}, u32[]{:S(2)}) collective-permute-start(bf16[4,88,1024]{2,1,0:T(8,128)(2,1)} %bitcast_dynamic-update-slice_fusion), channel_id=1, source_target_pairs={{0,8},{4,12},{8,0},{12,4},{1,9},{5,13},{9,1},{13,5},{2,10},{6,14},... | collective-permute-start | bytes 2162696 | tf_op jit(solution)/shard_map/ppermute | solution.py:276
  157.2 18.0 %copy-start.22 = (f32[512,1024]{1,0:T(8,128)S(1)}, f32[512,1024]{1,0:T(8,128)}, u32[]{:S(2)}) copy-start(f32[512,1024]{1,0:T(8,128)} %bitcast_divide_fusion) | copy-start | bytes 6291460
  195.9 5.6 collective-permute-start.5
  199.5 25.6 %collective-permute-start.4 = (bf16[512,1024]{1,0:T(8,128)(2,1)S(1)}, bf16[512,1024]{1,0:T(8,128)(2,1)}, u32[]{:S(2)}, u32[]{:S(2)}) collective-permute-start(bf16[512,1024]{1,0:T(8,128)(2,1)S(1)} %multiply_convert_fusion.2), channel_id=1, source_target_pairs={{0,16},{16,0},{1,17},{17,1},{2,18},{18,2},{3,19},{19,3},{4,20},{20... | collective-permute-start | bytes 3145736 | tf_op jit(solution)/shard_map/ppermute | solution.py:345
  251.4 13.5 %collective-permute-start.7 = (bf16[256,1024]{1,0:T(8,128)(2,1)S(1)}, bf16[256,1024]{1,0:T(8,128)(2,1)}, u32[]{:S(2)}, u32[]{:S(2)}) collective-permute-start(bf16[256,1024]{1,0:T(8,128)(2,1)S(1)} %get-tuple-element.209), channel_id=1, source_target_pairs={{0,16},{16,0},{1,17},{17,1},{2,18},{18,2},{3,19},{19,3},{4,20},{20... | collective-permute-start | bytes 1572872 | tf_op jit(solution)/shard_map/ppermute | solution.py:392
  264.8 15.6 %collective-permute-start.9 = (bf16[1024,1408]{1,0:T(8,128)(2,1)}, bf16[1024,1408]{1,0:T(8,128)(2,1)}, u32[]{:S(2)}, u32[]{:S(2)}) collective-permute-start(bf16[1024,1408]{1,0:T(8,128)(2,1)} %convolution_convert_fusion), channel_id=1, source_target_pairs={{0,4},{4,0},{8,12},{12,8},{1,5},{5,1},{9,13},{13,9},{2,6},{6,2},{1... | collective-permute-start | bytes 8650760 | tf_op jit(solution)/shard_map/ppermute | solution.py:386
  264.9 13.8 %collective-permute-start.10 = (bf16[1408,512]{1,0:T(8,128)(2,1)}, bf16[1408,512]{1,0:T(8,128)(2,1)S(1)}, u32[]{:S(2)}, u32[]{:S(2)}) collective-permute-start(bf16[1408,512]{1,0:T(8,128)(2,1)} %convolution_convert_fusion.4), channel_id=1, source_target_pairs={{0,4},{4,0},{8,12},{12,8},{1,5},{5,1},{9,13},{13,9},{2,6},{6,2},{1... | collective-permute-start | bytes 4325384 | tf_op jit(solution)/shard_map/ppermute | solution.py:386
  278.1 14.2 %collective-permute-start.8 = (bf16[256,1024]{1,0:T(8,128)(2,1)}, bf16[256,1024]{1,0:T(8,128)(2,1)}, u32[]{:S(2)}, u32[]{:S(2)}) collective-permute-start(bf16[256,1024]{1,0:T(8,128)(2,1)} %get-tuple-element.95), channel_id=1, source_target_pairs={{0,16},{16,0},{1,17},{17,1},{2,18},{18,2},{3,19},{19,3},{4,20},{20... | collective-permute-start | bytes 1572872 | tf_op jit(solution)/shard_map/ppermute | solution.py:396
  287.3 12.6 %copy-start.42 = (bf16[1024,1408]{1,0:T(8,128)(2,1)}, bf16[1024,1408]{1,0:T(8,128)(2,1)S(1)}, u32[]{:S(2)}) copy-start(bf16[1024,1408]{1,0:T(8,128)(2,1)S(1)} %add_convert_fusion) | copy-start | bytes 8650756
  301.2 33.0 %collective-permute-start.11 = (bf16[2,4,1,64,1408]{4,3,2,1,0:T(8,128)(2,1)}, bf16[2,4,1,64,1408]{4,3,2,1,0:T(8,128)(2,1)}, u32[]{:S(2)}, u32[]{:S(2)}) collective-permute-start(bf16[2,4,1,64,1408]{4,3,2,1,0:T(8,128)(2,1)} %constant_dynamic-slice_fusion.11), channel_id=1, source_target_pairs={{0,8},{4,12},{8,0},{12,4},{1,9},{5,13},{9,1},{13,5},{2,10},{6,14},... | collective-permute-start | bytes 4325384 | tf_op jit(solution)/shard_map/ppermute | solution.py:363
  301.2 147.2 %reduce-scatter.7.cloned.1.call-start = ((), (), s32[]{:S(2)}) async-start(), calls=%async_computation.6 | async-start | bytes 1802240 | tf_op jit(solution)/shard_map/reduce_scatter | solution.py:376
  305.6 15.9 %copy-start.50 = (bf16[512,1024]{1,0:T(8,128)(2,1)}, bf16[512,1024]{1,0:T(8,128)(2,1)S(1)}, u32[]{:S(2)}) copy-start(bf16[512,1024]{1,0:T(8,128)(2,1)S(1)} %get-tuple-element.167) | copy-start | bytes 3145732
  336.9 31.8 %collective-permute-start.12 = (bf16[4,1024,512]{2,1,0:T(8,128)(2,1)}, bf16[4,1024,512]{2,1,0:T(8,128)(2,1)}, u32[]{:S(2)}, u32[]{:S(2)}) collective-permute-start(bf16[4,1024,512]{2,1,0:T(8,128)(2,1)} %pad_maximum_fusion.1), channel_id=1, source_target_pairs={{0,4},{4,0},{8,12},{12,8},{1,5},{5,1},{9,13},{13,9},{2,6},{6,2},{1... | collective-permute-start | bytes 12582920 | tf_op jit(solution)/shard_map/ppermute | solution.py:386
  341.3 31.7 %collective-permute-start.13 = (bf16[1024,512]{1,0:T(8,128)(2,1)}, bf16[1024,512]{1,0:T(8,128)(2,1)}, u32[]{:S(2)}, u32[]{:S(2)}) collective-permute-start(bf16[1024,512]{1,0:T(8,128)(2,1)} %fusion.35), channel_id=1, source_target_pairs={{0,16},{16,0},{1,17},{17,1},{2,18},{18,2},{3,19},{19,3},{4,20},{20... | collective-permute-start | bytes 3145736 | tf_op jit(solution)/shard_map/ppermute | solution.py:404
  350.7 147.0 %reduce-scatter.9.cloned.1.call-start = ((), (), s32[]{:S(2)}) async-start(), calls=%async_computation.7 | async-start | bytes 1310720 | tf_op jit(solution)/shard_map/reduce_scatter | solution.py:376
  373.4 42.3 %collective-permute-start.15 = (bf16[2,1024,256]{2,1,0:T(8,128)(2,1)S(1)}, bf16[2,1024,256]{2,1,0:T(8,128)(2,1)}, u32[]{:S(2)}, u32[]{:S(2)}) collective-permute-start(bf16[2,1024,256]{2,1,0:T(8,128)(2,1)S(1)} %constant_dynamic-slice_fusion.9), channel_id=1, source_target_pairs={{0,8},{4,12},{8,0},{12,4},{1,9},{5,13},{9,1},{13,5},{2,10},{6,14},... | collective-permute-start | bytes 3145736 | tf_op jit(solution)/shard_map/ppermute | solution.py:363
  373.6 43.6 %collective-permute-start.14 = (bf16[2,1024,256]{2,1,0:T(8,128)(2,1)S(1)}, bf16[2,1024,256]{2,1,0:T(8,128)(2,1)S(1)}, u32[]{:S(2)}, u32[]{:S(2)}) collective-permute-start(bf16[2,1024,256]{2,1,0:T(8,128)(2,1)S(1)} %constant_dynamic-slice_fusion.10), channel_id=1, source_target_pairs={{0,16},{16,0},{1,17},{17,1},{2,18},{18,2},{3,19},{19,3},{4,20},{20... | collective-permute-start | bytes 3145736 | tf_op jit(solution)/shard_map/ppermute | solution.py:363
  375.1 31.1 %copy-start.16 = (bf16[2048,1024]{1,0:T(8,128)(2,1)S(1)}, bf16[2048,1024]{1,0:T(8,128)(2,1)}, u32[]{:S(2)}) copy-start(bf16[2048,1024]{1,0:T(8,128)(2,1)} %fusion.6) | copy-start | bytes 12582916
  421.1 19.6 %collective-permute-start.17 = (bf16[2,1024,512]{2,1,0:T(8,128)(2,1)}, bf16[2,1024,512]{2,1,0:T(8,128)(2,1)}, u32[]{:S(2)}, u32[]{:S(2)}) collective-permute-start(bf16[2,1024,512]{2,1,0:T(8,128)(2,1)} %pad_maximum_fusion.6), channel_id=1, source_target_pairs={{0,4},{4,0},{8,12},{12,8},{1,5},{5,1},{9,13},{13,9},{2,6},{6,2},{1... | collective-permute-start | bytes 6291464 | tf_op jit(solution)/shard_map/ppermute | solution.py:386
  421.1 23.3 %collective-permute-start.16 = (bf16[2,1024,512]{2,1,0:T(8,128)(2,1)}, bf16[2,1024,512]{2,1,0:T(8,128)(2,1)}, u32[]{:S(2)}, u32[]{:S(2)}) collective-permute-start(bf16[2,1024,512]{2,1,0:T(8,128)(2,1)} %pad_maximum_fusion.5), channel_id=1, source_target_pairs={{0,4},{4,0},{8,12},{12,8},{1,5},{5,1},{9,13},{13,9},{2,6},{6,2},{1... | collective-permute-start | bytes 6291464 | tf_op jit(solution)/shard_map/ppermute | solution.py:386
  426.3 12.9 %collective-permute-start.18 = (bf16[2,1024,128]{2,1,0:T(8,128)(2,1)S(1)}, bf16[2,1024,128]{2,1,0:T(8,128)(2,1)S(1)}, u32[]{:S(2)}, u32[]{:S(2)}) collective-permute-start(bf16[2,1024,128]{2,1,0:T(8,128)(2,1)S(1)} %constant_dynamic-slice_fusion.8), channel_id=1, source_target_pairs={{0,8},{4,12},{8,0},{12,4},{1,9},{5,13},{9,1},{13,5},{2,10},{6,14},... | collective-permute-start | bytes 1572872 | tf_op jit(solution)/shard_map/ppermute | solution.py:363
  426.4 12.9 %collective-permute-start.19 = (bf16[2,1024,128]{2,1,0:T(8,128)(2,1)S(1)}, bf16[2,1024,128]{2,1,0:T(8,128)(2,1)S(1)}, u32[]{:S(2)}, u32[]{:S(2)}) collective-permute-start(bf16[2,1024,128]{2,1,0:T(8,128)(2,1)S(1)} %constant_dynamic-slice_fusion.7), channel_id=1, source_target_pairs={{0,16},{16,0},{1,17},{17,1},{2,18},{18,2},{3,19},{19,3},{4,20},{20... | collective-permute-start | bytes 1572872 | tf_op jit(solution)/shard_map/ppermute | solution.py:363
  449.4 31.6 %collective-permute-start.21 = (bf16[2,1024,256]{2,1,0:T(8,128)(2,1)}, bf16[2,1024,256]{2,1,0:T(8,128)(2,1)}, u32[]{:S(2)}, u32[]{:S(2)}) collective-permute-start(bf16[2,1024,256]{2,1,0:T(8,128)(2,1)} %constant_dynamic-slice_fusion.5), channel_id=1, source_target_pairs={{0,8},{4,12},{8,0},{12,4},{1,9},{5,13},{9,1},{13,5},{2,10},{6,14},... | collective-permute-start | bytes 3145736 | tf_op jit(solution)/shard_map/ppermute | solution.py:363
  452.6 30.1 %collective-permute-start.20 = (bf16[2,1024,256]{2,1,0:T(8,128)(2,1)}, bf16[2,1024,256]{2,1,0:T(8,128)(2,1)}, u32[]{:S(2)}, u32[]{:S(2)}) collective-permute-start(bf16[2,1024,256]{2,1,0:T(8,128)(2,1)} %constant_dynamic-slice_fusion.6), channel_id=1, source_target_pairs={{0,16},{16,0},{1,17},{17,1},{2,18},{18,2},{3,19},{19,3},{4,20},{20... | collective-permute-start | bytes 3145736 | tf_op jit(solution)/shard_map/ppermute | solution.py:363
  463.6 80.5 %reduce-scatter.11.cloned.1.call-start = ((), (), s32[]{:S(2)}) async-start(), calls=%async_computation.8 | async-start | bytes 1310720 | tf_op jit(solution)/shard_map/reduce_scatter | solution.py:376
  484.5 11.3 %collective-permute-start.22 = (bf16[2,1024,128]{2,1,0:T(8,128)(2,1)S(1)}, bf16[2,1024,128]{2,1,0:T(8,128)(2,1)S(1)}, u32[]{:S(2)}, u32[]{:S(2)}) collective-permute-start(bf16[2,1024,128]{2,1,0:T(8,128)(2,1)S(1)} %constant_dynamic-slice_fusion.4), channel_id=1, source_target_pairs={{0,8},{4,12},{8,0},{12,4},{1,9},{5,13},{9,1},{13,5},{2,10},{6,14},... | collective-permute-start | bytes 1572872 | tf_op jit(solution)/shard_map/ppermute | solution.py:363
  485.0 11.5 %collective-permute-start.23 = (bf16[2,1024,128]{2,1,0:T(8,128)(2,1)S(1)}, bf16[2,1024,128]{2,1,0:T(8,128)(2,1)S(1)}, u32[]{:S(2)}, u32[]{:S(2)}) collective-permute-start(bf16[2,1024,128]{2,1,0:T(8,128)(2,1)S(1)} %constant_dynamic-slice_fusion.3), channel_id=1, source_target_pairs={{0,16},{16,0},{1,17},{17,1},{2,18},{18,2},{3,19},{19,3},{4,20},{20... | collective-permute-start | bytes 1572872 | tf_op jit(solution)/shard_map/ppermute | solution.py:363
  497.7 60.7 %all-gather.16.cloned.1.call-start = ((), (), s32[]{:S(2)}) async-start(), calls=%async_computation.11 | async-start | bytes 1802240 | tf_op jit(solution)/shard_map/all_gather | solution.py:438
  497.8 5.6 collective-permute-start.31
  504.2 78.6 %all-gather.12.cloned.1.call-start = ((), (), s32[]{:S(2)}) async-start(), calls=%async_computation.9 | async-start | bytes 2621440 | tf_op jit(solution)/shard_map/all_gather | solution.py:438
  511.6 12.2 %collective-permute-start.24 = (f32[4,1024]{1,0:T(4,128)S(1)}, f32[4,1024]{1,0:T(4,128)S(1)}, u32[]{:S(2)}, u32[]{:S(2)}) collective-permute-start(f32[4,1024]{1,0:T(4,128)S(1)} %pad_maximum_fusion.16), channel_id=1, source_target_pairs={{0,16},{16,0},{1,17},{17,1},{2,18},{18,2},{3,19},{19,3},{4,20},{20... | collective-permute-start | bytes 49160 | tf_op jit(solution)/shard_map/ppermute | solution.py:473
  523.8 28.7 %copy-start.20 = (f32[512,1024]{1,0:T(8,128)S(1)}, f32[512,1024]{1,0:T(8,128)}, u32[]{:S(2)}) copy-start(f32[512,1024]{1,0:T(8,128)} %copy-done.19) | copy-start | bytes 6291460
  523.9 20.1 %collective-permute-start.27 = (bf16[1024,512]{1,0:T(8,128)(2,1)}, bf16[1024,512]{1,0:T(8,128)(2,1)}, u32[]{:S(2)}, u32[]{:S(2)}) collective-permute-start(bf16[1024,512]{1,0:T(8,128)(2,1)} %get-tuple-element.143), channel_id=1, source_target_pairs={{0,16},{16,0},{1,17},{17,1},{2,18},{18,2},{3,19},{19,3},{4,20},{20... | collective-permute-start | bytes 3145736 | tf_op jit(solution)/shard_map/ppermute | solution.py:480
  524.3 1.2 collective-permute-start.25
  525.5 3.7 collective-permute-start.26
  527.5 15.5 %collective-permute-start.28 = (bf16[352,256]{1,0:T(8,128)(2,1)}, bf16[352,256]{1,0:T(8,128)(2,1)S(1)}, u32[]{:S(2)}, u32[]{:S(2)}) collective-permute-start(bf16[352,256]{1,0:T(8,128)(2,1)} %constant_dynamic-slice_fusion.2), channel_id=1, source_target_pairs={{0,8},{4,12},{8,0},{12,4},{1,9},{5,13},{9,1},{13,5},{2,10},{6,14},... | collective-permute-start | bytes 540680 | tf_op jit(solution)/shard_map/ppermute | solution.py:363
  545.1 6.4 %collective-permute-start.29 = (bf16[4,256,128]{2,1,0:T(8,128)(2,1)S(1)}, bf16[4,256,128]{2,1,0:T(8,128)(2,1)S(1)}, u32[]{:S(2)}, u32[]{:S(2)}) collective-permute-start(bf16[4,256,128]{2,1,0:T(8,128)(2,1)S(1)} %get-tuple-element.215), channel_id=1, source_target_pairs={{0,16},{16,0},{1,17},{17,1},{2,18},{18,2},{3,19},{19,3},{4,20},{20... | collective-permute-start | bytes 786440 | tf_op jit(solution)/shard_map/ppermute | solution.py:490
  559.9 23.0 %collective-permute-start.30 = (bf16[1024,512]{1,0:T(8,128)(2,1)S(1)}, bf16[1024,512]{1,0:T(8,128)(2,1)}, u32[]{:S(2)}, u32[]{:S(2)}) collective-permute-start(bf16[1024,512]{1,0:T(8,128)(2,1)S(1)} %get-tuple-element.150), channel_id=1, source_target_pairs={{0,16},{16,0},{1,17},{17,1},{2,18},{18,2},{3,19},{19,3},{4,20},{20... | collective-permute-start | bytes 3145736 | tf_op jit(solution)/shard_map/ppermute | solution.py:487
  (82 other events, 355.5 us)
Sparse Core Ops, SparseCore 0:
  11.6 123.7 all-gather.13
  138.2 61.4 all-gather.9
  301.3 32.1 reduce-scatter.4
  350.8 31.4 reduce-scatter.6
  463.7 25.9 reduce-scatter.8
  497.8 28.0 reduce-scatter.10
  528.1 17.5 all-gather.15
  552.6 28.8 all-gather.11

commit v16 on v15

--- a/solution.py
+++ b/solution.py
@@ -448,7 +448,7 @@
     sum_in = jnp.where(section == 0, sum_in, sum_in[::-1])
     sum_in = gathered(sum_in)
     grad_query_in = nt(dq1, wq[0])
-    grad_key_in = nt(dk1, wk[0]) + nt(dv1, wv[0])
+    grad_key_in = (nt(dk1, wk[0]) + nt(dv1, wv[0])).astype(BF)
     half_one = over_section(half_one[0], 2), over_side(half_one[1], 2)
     grad_query_in, grad_key_in, half_one = together((grad_query_in, grad_key_in, half_one))
     half_one = jnp.concatenate([over_side(half_one[0], 2), over_section(half_one[1], 2)], axis=0)
@@ -459,7 +459,7 @@
     sum_one = line_sum(half_one, 1)
 
     grad_pooled, gain_query = norm_backward(pooled, query_scale, gains[0, 0], grad_query_in)
-    grad_wide, gain_key = norm_backward(wide, key_scale, gains[0, 1], grad_key_in)
+    grad_wide, gain_key = norm_backward(wide, key_scale, gains[0, 1], grad_key_in.astype(F32))
     per_patch = (grad_pooled + d_carried.astype(F32)) / count
     spread_back = jnp.einsum(
         "rpb,rpd->rbd", member, per_patch.astype(BF).reshape(rows, PATCHES, D), preferred_element_type=F32

time: 606 us -> 603 us (level)
    ppermute x10, starting transfers between devices: 7.14 us -> 13.9 us  [exchanged(): lax.ppermute(other, axis, pairs).astype(F32)]
  transfers between devices with their start and end apart: 40 -> 40, of which waited for: 12 -> 14; matrix products, arithmetic and copies ran while one was open for 43% -> 42% of each run, Pallas kernels for 11% -> 10%
where the time goes in v16:
time: 603 us; the launch traced here: 596 us
  matrix products  173 us (29%)
  waiting for transfers between devices  141 us (23%)
  other arithmetic  105 us (17%)
  Pallas kernels  60.7 us (10%)
  local copies, waits for them, and re-layouts  40.2 us (7%)
  starting transfers between devices  33.8 us (6%)
  blocking collectives  26.3 us (4%)
  between operations  16.1 us (3%)
    all_gather x1, waiting for transfers between devices, shards(): lax.all_gather(matrix, ('section', 'group', 'dp'), axis=0, tiled=True)  85.6 us
    dot_general x11, matrix products, nt(): lax.dot_general(left, right, (((1,), (1,)), ((), ())), preferred_element_...  65 us
    dot_general x10, matrix products, nn(): return jnp.dot(left, right, preferred_element_type=F32)  52.5 us
    dot_general x20, matrix products, tn(): lax.dot_general(left, right, (((0,), (0,)), ((), ())), preferred_element_...  50.5 us
    pallas_call x2, Pallas kernels, attend_back(): pl.pallas_call(functools.partial(attend_back_kernel, chunk, spans), grid_...  39.8 us
    pallas_call x2, Pallas kernels, attend(): pl.pallas_call(functools.partial(attend_kernel, chunk, spans), grid_spec=...  20.9 us
    ppermute x10, waiting for transfers between devices, exchanged(): lax.ppermute(other, axis, pairs).astype(F32)  20 us
    unnamed x189, local copies, waits for them, and re-layouts  18.8 us
  transfers between devices with their start and end apart: 40, of which 14 were waited for; matrix products, arithmetic and copies ran while one was open for 42% of the time, Pallas kernels for 10%

profile of v16, /device:TPU:0, one launch (start us, length us, event | category | flops | bytes accessed | tf_op | source)
XLA Modules:
  0.0 595.9 jit_solution(12540352773642053451)
XLA Ops:
  24.2 3.7 multiply_reduce_fusion.5
  27.9 3.8 fusion.9
  33.9 4.7 all_gather.31
  39.3 4.2 fusion.11
  49.7 85.6 %all-gather.14.cloned.1.call-done = bf16[1,8192,1024]{2,1,0:T(8,128)(2,1)} async-done(((bf16[1,256,1024]{2,1,0:T(8,128)(2,1)}), bf16[1,8192,1024]{2,1,0:T(8,128)(2,1)}) %all-gather.14.cloned.1.call-update) | async-done | bytes 16777232 | tf_op jit(solution)/shard_map/all_gather | solution.py:264
  135.3 9.5 %convolution_convert_fusion.2.v_ref = bf16[2048,1024]{1,0:T(8,128)(2,1)} fusion(bf16[2048,1024]{1,0:T(8,128)(2,1)} %bitcast.273, bf16[2,4,1024,1024]{3,2,1,0:T(8,128)(2,1)} %bitcast.336), kind=kOutput, calls=%fused_computation.52 | convolution fusion | flops 4297064448 | bytes 10485760 | tf_op jit(solution)/shard_map/dot_general | solution.py:31
  149.3 8.0 %convolution_convert_fusion.3.k_ref = bf16[2048,1024]{1,0:T(8,128)(2,1)} fusion(bf16[2048,1024]{1,0:T(8,128)(2,1)S(1)} %bitcast.274, bf16[2,4,1024,1024]{3,2,1,0:T(8,128)(2,1)} %bitcast.338), kind=kOutput, calls=%fused_computation.53 | convolution fusion | flops 4297064448 | bytes 10485760 | tf_op jit(solution)/shard_map/dot_general | solution.py:31
  157.3 16.9 %attend.2 = (bf16[512,1024]{1,0:T(8,128)(2,1)S(1)}, f32[2,8,2,256]{3,2,1,0:T(2,128)S(1)}) custom-call(s32[2,2]{1,0:T(2,128)S(1)} %get-tuple-element.248.first_ref, s32[2,2]{1,0:T(2,128)S(1)} %get-tuple-element.233.stop_ref, s32[2,1,256]{2,1,0:T(1,128)S(1)} %broadcast_in_dim.73.lo_ref, s32[2,1,256]{2,1,0:T(1,128)S(1)} %bitcast.260, ...), custom_call_target="tpu_custom_call" | custom-call | flops 8589934592 | bytes 18874368 | tf_op jit(solution)/shard_map/attend/pallas_call | solution.py:186
  174.2 3.4 fusion.27
  177.6 3.3 fusion.83.v_ref
  180.9 3.3 fusion.84.k_ref
  184.2 3.3 fusion.85.q_ref
  187.6 4.0 attend.3
  200.2 3.3 maximum_select_fusion.1
  203.5 5.8 convolution_convert_fusion.1
  209.3 14.8 %collective-permute-done.4 = bf16[512,1024]{1,0:T(8,128)(2,1)} collective-permute-done((bf16[512,1024]{1,0:T(8,128)(2,1)S(1)}, bf16[512,1024]{1,0:T(8,128)(2,1)}, u32[]{:S(2)}, u32[]{:S(2)}) %collective-permute-start.4) | collective-permute-done | bytes 1048608 | tf_op jit(solution)/shard_map/ppermute | solution.py:345
  224.1 9.5 %fusion.112 = f32[1024,2816]{1,0:T(8,128)S(1)} fusion(bf16[1024,2816]{1,0:T(8,128)(2,1)} %bitcast.352, bf16[512,1024]{1,0:T(8,128)(2,1)} %collective-permute-done.4, bf16[512,1024]{1,0:T(8,128)(2,1)} %copy-done.54), kind=kOutput, calls=%fused_computation.203 | convolution fusion | flops 5909774336 | bytes 19398656 | tf_op jit(solution)/shard_map/dot_general | solution.py:31
  233.6 4.6 fusion.17
  241.5 7.9 %fusion.79 = bf16[512,1024]{1,0:T(8,128)(2,1)S(1)} fusion(bf16[1024,2816]{1,0:T(8,128)(2,1)} %bitcast.353, bf16[1024,2816]{1,0:T(8,128)(2,1)S(1)} %pad_maximum_fusion), kind=kOutput, calls=%fused_computation.155 | convolution fusion | flops 2953314304 | bytes 9699328 | tf_op jit(solution)/shard_map/dot_general | solution.py:39
  254.9 6.3 %convolution_convert_fusion = bf16[1024,1408]{1,0:T(8,128)(2,1)} fusion(bf16[1024,2816]{1,0:T(8,128)(2,1)S(1)} %pad_maximum_fusion, s32[]{:T(128)S(6)} %select_n.315, bf16[512,1024]{1,0:T(8,128)(2,1)} %collective-permute-done.4, bf16[512,1024]{1,0:T(8,128)(2,1)S(1)} %copy-done.55), kind=kOutput, calls=%fused_computation.50 | convolution fusion | flops 2958426112 | bytes 7864324 | tf_op jit(solution)/shard_map/dot_general | solution.py:35
  264.7 6.1 %fusion.180 = f32[1024,1024]{1,0:T(8,128)S(1)} fusion(bf16[1024,1408]{1,0:T(8,128)(2,1)} %copy-done.28, bf16[1408,1024]{1,0:T(8,128)(2,1)} %bitcast.278), kind=kOutput, calls=%fused_computation.363 | convolution fusion | flops 2952790016 | bytes 9961472 | tf_op jit(solution)/shard_map/dot_general | solution.py:31
  279.5 6.9 %add_convert_fusion.1 = bf16[1024,1408]{1,0:T(8,128)(2,1)S(1)} fusion(bf16[1024,1408]{1,0:T(8,128)(2,1)} %collective-permute-done.9, bf16[1024,2816]{1,0:T(8,128)(2,1)} %copy-done.27, s32[]{:T(128)S(6)} %select_n.318, bf16[512,1024]{1,0:T(8,128)(2,1)} %collective-permute-done.4, bf16[512,1024]{1,0:T(8,128)(2,1)} %copy-done.54), kind=kOutput, calls=%fused_computation.31 | convolution fusion | flops 2961309696 | bytes 10747908 | tf_op jit(solution)/shard_map/dot_general | solution.py:35
  286.5 5.1 collective-permute-done.8
  291.6 7.6 %multiply_reduce_fusion = (f32[1024]{0:T(1024)S(1)}, f32[512]{0:T(512)S(1)}, f32[512,1024]{1,0:T(8,128)}) fusion(f32[512,1024]{1,0:T(8,128)S(1)} %get-tuple-element.245, f32[512]{0:T(512)S(1)} %get-tuple-element.229, bf16[256,1024]{1,0:T(8,128)(2,1)} %collective-permute-done.8, bf16[256,1024]{1,0:T(8,128)(2,1)} %collective-permute-done.7, ...), kind=kOutput, calls=%fused_computation.100 | convolution fusion | flops 2958555648 | bytes 13905920 | tf_op jit(solution)/shard_map/dot_general | solution.py:39
  302.2 3.9 fusion.171
  306.2 4.3 fusion.82.dc_ref
  310.5 11.5 %attend_back.2 = (bf16[512,1024]{1,0:T(8,128)(2,1)S(1)}, bf16[512,1024]{1,0:T(8,128)(2,1)S(1)}, bf16[512,1024]{1,0:T(8,128)(2,1)S(1)}) custom-call(s32[2,2]{1,0:T(2,128)S(1)} %get-tuple-element.251.first_ref, s32[2,2]{1,0:T(2,128)S(1)} %get-tuple-element.250.stop_ref, s32[2,1,256]{2,1,0:T(1,128)S(1)} %broadcast_in_dim.83.lo_ref, ...), custom_call_target="tpu_custom_call" | custom-call | flops 5368709120 | bytes 6291456 | tf_op jit(solution)/shard_map/attend_back/pallas_call | solution.py:210
  328.7 4.7 collective-permute-done.11
  336.2 4.3 fusion.13
  356.4 3.6 fusion.36
  375.3 28.3 %attend_back.3 = (bf16[512,1024]{1,0:T(8,128)(2,1)S(1)}, bf16[2048,1024]{1,0:T(8,128)(2,1)}, bf16[2048,1024]{1,0:T(8,128)(2,1)}) custom-call(s32[2,2]{1,0:T(2,128)S(1)} %get-tuple-element.249.first_ref, s32[2,2]{1,0:T(2,128)S(1)} %get-tuple-element.232.stop_ref, s32[2,1,256]{2,1,0:T(1,128)S(1)} %broadcast_in_dim.73.lo_ref, s32[2,1,256]{2,1,0:T(1,128)S(1)} %bitcast.261, ...), custom_call_target="tpu_custom_call" | custom-call | flops 21474836480 | bytes 18874368 | tf_op jit(solution)/shard_map/attend_back/pallas_call | solution.py:210
  403.6 4.1 fusion.88
  419.9 3.7 fusion.70
  423.7 3.6 collective-permute-start.18
  428.3 3.7 fusion.67
  434.2 4.2 collective-permute-done.18
  441.2 3.7 fusion.21
  445.3 3.6 fusion.20
  452.9 10.7 %fusion.52 = f32[2048,1024]{1,0:T(8,128)} fusion(bf16[2048,1024]{1,0:T(8,128)(2,1)} %get-tuple-element.130, bf16[2,4,1024,1024]{3,2,1,0:T(8,128)(2,1)} %bitcast.349), kind=kOutput, calls=%fused_computation.132 | convolution fusion | flops 4294967296 | bytes 14680064 | tf_op jit(solution)/shard_map/dot_general | solution.py:39
  463.7 12.0 %add_convert_fusion = bf16[2048,1024]{1,0:T(8,128)(2,1)} fusion(f32[2048,1024]{1,0:T(8,128)} %fusion.52, bf16[2048,1024]{1,0:T(8,128)(2,1)} %get-tuple-element.129, bf16[2,4,1024,1024]{3,2,1,0:T(8,128)(2,1)} %bitcast.350), kind=kOutput, calls=%fused_computation.22 | convolution fusion | flops 4299161600 | bytes 18874368 | tf_op jit(solution)/shard_map/dot_general | solution.py:39
  475.7 4.2 fusion.50
  485.9 8.7 %collective-permute-done.22 = bf16[2,1024,128]{2,1,0:T(8,128)(2,1)S(1)} collective-permute-done((bf16[2,1024,128]{2,1,0:T(8,128)(2,1)S(1)}, bf16[2,1024,128]{2,1,0:T(8,128)(2,1)S(1)}, u32[]{:S(2)}, u32[]{:S(2)}) %collective-permute-start.22) | collective-permute-done | bytes 524320 | tf_op jit(solution)/shard_map/ppermute | solution.py:363
  498.2 4.4 collective-permute-done.31
  503.6 5.9 fusion.7
  527.8 13.3 %all-gather.4 = f32[4,4,1024]{2,1,0:T(4,128)S(1)} all-gather(f32[1,4,1024]{2,1,0:T(4,128)S(1)} %add_bitcast_fusion), channel_id=3, replica_groups=mesh['section'=2,'group'=4,'dp'=4] {'dp'}, dimensions={0}, use_global_device_ids=true | all-gather | bytes 81920 | tf_op jit(solution)/shard_map/all_gather | solution.py:483
  544.2 5.4 collective-permute-done.29
  559.1 8.6 %maximum_convert_fusion = f32[128,5632]{1,0:T(8,128)} fusion(bf16[64,1408]{1,0:T(8,128)(2,1)S(1)} %get-tuple-element.197, bf16[64,1408]{1,0:T(8,128)(2,1)S(1)} %get-tuple-element.198, bf16[64,1408]{1,0:T(8,128)(2,1)S(1)} %get-tuple-element.199, bf16[64,1408]{1,0:T(8,128)(2,1)S(1)} %get-tuple-element.200, bf16[64,1408]{1,0:T(8,128)(2,1)S(1)} %get-tuple-element.201, ...), kind=kLoop, calls=%fused_computation.169 | loop fusion | flops 11534336 | bytes 4325376 | tf_op jit(solution)/shard_map/concatenate | solution.py:474
  568.4 8.4 %all-gather.3 = bf16[1408,256]{1,0:T(8,128)(2,1)S(1)} all-gather(bf16[352,256]{1,0:T(8,128)(2,1)S(1)} %add_convert_fusion.13), channel_id=5, replica_groups=mesh['section'=2,'group'=4,'dp'=4] {'group'}, dimensions={0}, use_global_device_ids=true | all-gather | bytes 901120 | tf_op jit(solution)/shard_map/all_gather | solution.py:438
  (406 shorter events, 179.5 us)
Async XLA Ops:
  7.2 20.7 %copy-start = (s32[4,256]{1,0:T(4,128)S(1)}, s32[4,256]{1,0:T(4,128)}, u32[]{:S(2)}) copy-start(s32[4,256]{1,0:T(4,128)} %param.11) | copy-start | bytes 12292
  7.2 128.2 %all-gather.14.cloned.1.call-start = ((), (), s32[]{:S(2)}) async-start(), calls=%async_computation.10 | async-start | bytes 17301504 | tf_op jit(solution)/shard_map/all_gather | solution.py:264
  9.3 214.8 %all-gather.10.cloned.1.call-start = ((), (), s32[]{:S(2)}) async-start(), calls=%async_computation.4 | async-start | bytes 6127616 | tf_op jit(solution)/shard_map/all_gather | solution.py:287
  11.9 33.9 %collective-permute-start = (bf16[88,1024]{1,0:T(8,128)(2,1)S(1)}, bf16[88,1024]{1,0:T(8,128)(2,1)}, u32[]{:S(2)}, u32[]{:S(2)}) collective-permute-start(bf16[88,1024]{1,0:T(8,128)(2,1)S(1)} %get-tuple-element.170), channel_id=1, source_target_pairs={{0,1},{1,2},{2,3},{3,0},{4,5},{5,6},{6,7},{7,4},{8,9},{9,10},{10,1... | collective-permute-start | bytes 540680 | tf_op jit(solution)/shard_map/ppermute | solution.py:293
  14.9 32.5 %collective-permute-start.1 = (bf16[88,1024]{1,0:T(8,128)(2,1)S(1)}, bf16[88,1024]{1,0:T(8,128)(2,1)}, u32[]{:S(2)}, u32[]{:S(2)}) collective-permute-start(bf16[88,1024]{1,0:T(8,128)(2,1)S(1)} %get-tuple-element.170), channel_id=1, source_target_pairs={{0,2},{1,3},{2,0},{3,1},{4,6},{5,7},{6,4},{7,5},{8,10},{9,11},{10,... | collective-permute-start | bytes 540680 | tf_op jit(solution)/shard_map/ppermute | solution.py:293
  17.5 31.5 %collective-permute-start.2 = (bf16[88,1024]{1,0:T(8,128)(2,1)S(1)}, bf16[88,1024]{1,0:T(8,128)(2,1)S(1)}, u32[]{:S(2)}, u32[]{:S(2)}) collective-permute-start(bf16[88,1024]{1,0:T(8,128)(2,1)S(1)} %get-tuple-element.170), channel_id=1, source_target_pairs={{0,3},{1,0},{2,1},{3,2},{4,7},{5,4},{6,5},{7,6},{8,11},{9,8},{10,9... | collective-permute-start | bytes 540680 | tf_op jit(solution)/shard_map/ppermute | solution.py:293
  20.2 11.6 %collective-permute-start.6 = (bf16[32,2816]{1,0:T(8,128)(2,1)S(1)}, bf16[32,2816]{1,0:T(8,128)(2,1)S(1)}, u32[]{:S(2)}, u32[]{:S(2)}) collective-permute-start(bf16[32,2816]{1,0:T(8,128)(2,1)S(1)} %pad_maximum_fusion.15), channel_id=1, source_target_pairs={{0,16},{16,0},{1,17},{17,1},{2,18},{18,2},{3,19},{19,3},{4,20},{20... | collective-permute-start | bytes 540680 | tf_op jit(solution)/shard_map/ppermute | solution.py:285
  27.9 17.2 %copy-start.17 = (f32[2,256,1024]{2,1,0:T(8,128)}, f32[2,256,1024]{2,1,0:T(8,128)S(1)}, u32[]{:S(2)}) copy-start(f32[2,256,1024]{2,1,0:T(8,128)S(1)} %get-tuple-element.241) | copy-start | bytes 6291460
  32.6 303.6 %reduce-scatter.5.cloned.1.call-start = ((), (), s32[]{:S(2)}) async-start(), calls=%async_computation.5 | async-start | bytes 1802240 | tf_op jit(solution)/shard_map/reduce_scatter | solution.py:376
  39.2 224.9 %copy-start.67 = (f32[1,8,2,128]{3,2,1,0:T(2,128)}, f32[1,8,2,128]{3,2,1,0:T(2,128)S(1)}, u32[]{:S(2)}) copy-start(f32[1,8,2,128]{3,2,1,0:T(2,128)S(1)} %get-tuple-element.222) | copy-start | bytes 24580
  144.8 46.8 %collective-permute-start.3 = (bf16[4,88,1024]{2,1,0:T(8,128)(2,1)}, bf16[4,88,1024]{2,1,0:T(8,128)(2,1)S(1)}, u32[]{:S(2)}, u32[]{:S(2)}) collective-permute-start(bf16[4,88,1024]{2,1,0:T(8,128)(2,1)} %bitcast_dynamic-update-slice_fusion), channel_id=1, source_target_pairs={{0,8},{4,12},{8,0},{12,4},{1,9},{5,13},{9,1},{13,5},{2,10},{6,14},... | collective-permute-start | bytes 2162696 | tf_op jit(solution)/shard_map/ppermute | solution.py:276
  157.3 16.9 %copy-start.22 = (f32[512,1024]{1,0:T(8,128)S(1)}, f32[512,1024]{1,0:T(8,128)}, u32[]{:S(2)}) copy-start(f32[512,1024]{1,0:T(8,128)} %bitcast_divide_fusion) | copy-start | bytes 6291460
  194.8 5.4 collective-permute-start.5
  198.3 25.8 %collective-permute-start.4 = (bf16[512,1024]{1,0:T(8,128)(2,1)S(1)}, bf16[512,1024]{1,0:T(8,128)(2,1)}, u32[]{:S(2)}, u32[]{:S(2)}) collective-permute-start(bf16[512,1024]{1,0:T(8,128)(2,1)S(1)} %multiply_convert_fusion.2), channel_id=1, source_target_pairs={{0,16},{16,0},{1,17},{17,1},{2,18},{18,2},{3,19},{19,3},{4,20},{20... | collective-permute-start | bytes 3145736 | tf_op jit(solution)/shard_map/ppermute | solution.py:345
  250.3 13.8 %collective-permute-start.7 = (bf16[256,1024]{1,0:T(8,128)(2,1)S(1)}, bf16[256,1024]{1,0:T(8,128)(2,1)}, u32[]{:S(2)}, u32[]{:S(2)}) collective-permute-start(bf16[256,1024]{1,0:T(8,128)(2,1)S(1)} %get-tuple-element.209), channel_id=1, source_target_pairs={{0,16},{16,0},{1,17},{17,1},{2,18},{18,2},{3,19},{19,3},{4,20},{20... | collective-permute-start | bytes 1572872 | tf_op jit(solution)/shard_map/ppermute | solution.py:392
  264.1 15.4 %collective-permute-start.9 = (bf16[1024,1408]{1,0:T(8,128)(2,1)}, bf16[1024,1408]{1,0:T(8,128)(2,1)}, u32[]{:S(2)}, u32[]{:S(2)}) collective-permute-start(bf16[1024,1408]{1,0:T(8,128)(2,1)} %convolution_convert_fusion), channel_id=1, source_target_pairs={{0,4},{4,0},{8,12},{12,8},{1,5},{5,1},{9,13},{13,9},{2,6},{6,2},{1... | collective-permute-start | bytes 8650760 | tf_op jit(solution)/shard_map/ppermute | solution.py:386
  264.2 13.7 %collective-permute-start.10 = (bf16[1408,512]{1,0:T(8,128)(2,1)}, bf16[1408,512]{1,0:T(8,128)(2,1)S(1)}, u32[]{:S(2)}, u32[]{:S(2)}) collective-permute-start(bf16[1408,512]{1,0:T(8,128)(2,1)} %convolution_convert_fusion.4), channel_id=1, source_target_pairs={{0,4},{4,0},{8,12},{12,8},{1,5},{5,1},{9,13},{13,9},{2,6},{6,2},{1... | collective-permute-start | bytes 4325384 | tf_op jit(solution)/shard_map/ppermute | solution.py:386
  277.3 14.2 %collective-permute-start.8 = (bf16[256,1024]{1,0:T(8,128)(2,1)}, bf16[256,1024]{1,0:T(8,128)(2,1)}, u32[]{:S(2)}, u32[]{:S(2)}) collective-permute-start(bf16[256,1024]{1,0:T(8,128)(2,1)} %get-tuple-element.95), channel_id=1, source_target_pairs={{0,16},{16,0},{1,17},{17,1},{2,18},{18,2},{3,19},{19,3},{4,20},{20... | collective-permute-start | bytes 1572872 | tf_op jit(solution)/shard_map/ppermute | solution.py:396
  286.4 12.8 %copy-start.44 = (bf16[1024,1408]{1,0:T(8,128)(2,1)}, bf16[1024,1408]{1,0:T(8,128)(2,1)S(1)}, u32[]{:S(2)}) copy-start(bf16[1024,1408]{1,0:T(8,128)(2,1)S(1)} %add_convert_fusion.1) | copy-start | bytes 8650756
  300.4 33.0 %collective-permute-start.11 = (bf16[2,4,1,64,1408]{4,3,2,1,0:T(8,128)(2,1)}, bf16[2,4,1,64,1408]{4,3,2,1,0:T(8,128)(2,1)}, u32[]{:S(2)}, u32[]{:S(2)}) collective-permute-start(bf16[2,4,1,64,1408]{4,3,2,1,0:T(8,128)(2,1)} %constant_dynamic-slice_fusion.11), channel_id=1, source_target_pairs={{0,8},{4,12},{8,0},{12,4},{1,9},{5,13},{9,1},{13,5},{2,10},{6,14},... | collective-permute-start | bytes 4325384 | tf_op jit(solution)/shard_map/ppermute | solution.py:363
  301.8 147.2 %reduce-scatter.7.cloned.1.call-start = ((), (), s32[]{:S(2)}) async-start(), calls=%async_computation.6 | async-start | bytes 1802240 | tf_op jit(solution)/shard_map/reduce_scatter | solution.py:376
  306.2 15.8 %copy-start.52 = (bf16[512,1024]{1,0:T(8,128)(2,1)}, bf16[512,1024]{1,0:T(8,128)(2,1)S(1)}, u32[]{:S(2)}) copy-start(bf16[512,1024]{1,0:T(8,128)(2,1)S(1)} %get-tuple-element.167) | copy-start | bytes 3145732
  336.2 31.9 %collective-permute-start.12 = (bf16[4,1024,512]{2,1,0:T(8,128)(2,1)}, bf16[4,1024,512]{2,1,0:T(8,128)(2,1)}, u32[]{:S(2)}, u32[]{:S(2)}) collective-permute-start(bf16[4,1024,512]{2,1,0:T(8,128)(2,1)} %pad_maximum_fusion.1), channel_id=1, source_target_pairs={{0,4},{4,0},{8,12},{12,8},{1,5},{5,1},{9,13},{13,9},{2,6},{6,2},{1... | collective-permute-start | bytes 12582920 | tf_op jit(solution)/shard_map/ppermute | solution.py:386
  340.5 31.8 %collective-permute-start.13 = (bf16[1024,512]{1,0:T(8,128)(2,1)}, bf16[1024,512]{1,0:T(8,128)(2,1)}, u32[]{:S(2)}, u32[]{:S(2)}) collective-permute-start(bf16[1024,512]{1,0:T(8,128)(2,1)} %fusion.38), channel_id=1, source_target_pairs={{0,16},{16,0},{1,17},{17,1},{2,18},{18,2},{3,19},{19,3},{4,20},{20... | collective-permute-start | bytes 3145736 | tf_op jit(solution)/shard_map/ppermute | solution.py:404
  350.3 146.6 %reduce-scatter.9.cloned.1.call-start = ((), (), s32[]{:S(2)}) async-start(), calls=%async_computation.7 | async-start | bytes 1310720 | tf_op jit(solution)/shard_map/reduce_scatter | solution.py:376
  372.7 40.3 %collective-permute-start.15 = (bf16[2,1024,256]{2,1,0:T(8,128)(2,1)S(1)}, bf16[2,1024,256]{2,1,0:T(8,128)(2,1)}, u32[]{:S(2)}, u32[]{:S(2)}) collective-permute-start(bf16[2,1024,256]{2,1,0:T(8,128)(2,1)S(1)} %constant_dynamic-slice_fusion.9), channel_id=1, source_target_pairs={{0,8},{4,12},{8,0},{12,4},{1,9},{5,13},{9,1},{13,5},{2,10},{6,14},... | collective-permute-start | bytes 3145736 | tf_op jit(solution)/shard_map/ppermute | solution.py:363
  374.6 40.0 %collective-permute-start.14 = (bf16[2,1024,256]{2,1,0:T(8,128)(2,1)S(1)}, bf16[2,1024,256]{2,1,0:T(8,128)(2,1)S(1)}, u32[]{:S(2)}, u32[]{:S(2)}) collective-permute-start(bf16[2,1024,256]{2,1,0:T(8,128)(2,1)S(1)} %constant_dynamic-slice_fusion.10), channel_id=1, source_target_pairs={{0,16},{16,0},{1,17},{17,1},{2,18},{18,2},{3,19},{19,3},{4,20},{20... | collective-permute-start | bytes 3145736 | tf_op jit(solution)/shard_map/ppermute | solution.py:363
  375.3 28.3 %copy-start.16 = (bf16[2048,1024]{1,0:T(8,128)(2,1)S(1)}, bf16[2048,1024]{1,0:T(8,128)(2,1)}, u32[]{:S(2)}) copy-start(bf16[2048,1024]{1,0:T(8,128)(2,1)} %fusion.13) | copy-start | bytes 12582916
  418.5 22.7 %collective-permute-start.17 = (bf16[2,1024,512]{2,1,0:T(8,128)(2,1)}, bf16[2,1024,512]{2,1,0:T(8,128)(2,1)}, u32[]{:S(2)}, u32[]{:S(2)}) collective-permute-start(bf16[2,1024,512]{2,1,0:T(8,128)(2,1)} %pad_maximum_fusion.6), channel_id=1, source_target_pairs={{0,4},{4,0},{8,12},{12,8},{1,5},{5,1},{9,13},{13,9},{2,6},{6,2},{1... | collective-permute-start | bytes 6291464 | tf_op jit(solution)/shard_map/ppermute | solution.py:386
  418.5 26.5 %collective-permute-start.16 = (bf16[2,1024,512]{2,1,0:T(8,128)(2,1)}, bf16[2,1024,512]{2,1,0:T(8,128)(2,1)}, u32[]{:S(2)}, u32[]{:S(2)}) collective-permute-start(bf16[2,1024,512]{2,1,0:T(8,128)(2,1)} %pad_maximum_fusion.5), channel_id=1, source_target_pairs={{0,4},{4,0},{8,12},{12,8},{1,5},{5,1},{9,13},{13,9},{2,6},{6,2},{1... | collective-permute-start | bytes 6291464 | tf_op jit(solution)/shard_map/ppermute | solution.py:386
  423.7 14.7 %collective-permute-start.18 = (bf16[2,1024,128]{2,1,0:T(8,128)(2,1)S(1)}, bf16[2,1024,128]{2,1,0:T(8,128)(2,1)S(1)}, u32[]{:S(2)}, u32[]{:S(2)}) collective-permute-start(bf16[2,1024,128]{2,1,0:T(8,128)(2,1)S(1)} %constant_dynamic-slice_fusion.8), channel_id=1, source_target_pairs={{0,8},{4,12},{8,0},{12,4},{1,9},{5,13},{9,1},{13,5},{2,10},{6,14},... | collective-permute-start | bytes 1572872 | tf_op jit(solution)/shard_map/ppermute | solution.py:363
  427.3 12.7 %collective-permute-start.19 = (bf16[2,1024,128]{2,1,0:T(8,128)(2,1)S(1)}, bf16[2,1024,128]{2,1,0:T(8,128)(2,1)S(1)}, u32[]{:S(2)}, u32[]{:S(2)}) collective-permute-start(bf16[2,1024,128]{2,1,0:T(8,128)(2,1)S(1)} %constant_dynamic-slice_fusion.7), channel_id=1, source_target_pairs={{0,16},{16,0},{1,17},{17,1},{2,18},{18,2},{3,19},{19,3},{4,20},{20... | collective-permute-start | bytes 1572872 | tf_op jit(solution)/shard_map/ppermute | solution.py:363
  450.0 29.9 %collective-permute-start.21 = (bf16[2,1024,256]{2,1,0:T(8,128)(2,1)}, bf16[2,1024,256]{2,1,0:T(8,128)(2,1)}, u32[]{:S(2)}, u32[]{:S(2)}) collective-permute-start(bf16[2,1024,256]{2,1,0:T(8,128)(2,1)} %constant_dynamic-slice_fusion.5), channel_id=1, source_target_pairs={{0,8},{4,12},{8,0},{12,4},{1,9},{5,13},{9,1},{13,5},{2,10},{6,14},... | collective-permute-start | bytes 3145736 | tf_op jit(solution)/shard_map/ppermute | solution.py:363
  451.9 29.6 %collective-permute-start.20 = (bf16[2,1024,256]{2,1,0:T(8,128)(2,1)}, bf16[2,1024,256]{2,1,0:T(8,128)(2,1)}, u32[]{:S(2)}, u32[]{:S(2)}) collective-permute-start(bf16[2,1024,256]{2,1,0:T(8,128)(2,1)} %constant_dynamic-slice_fusion.6), channel_id=1, source_target_pairs={{0,16},{16,0},{1,17},{17,1},{2,18},{18,2},{3,19},{19,3},{4,20},{20... | collective-permute-start | bytes 3145736 | tf_op jit(solution)/shard_map/ppermute | solution.py:363
  463.6 78.5 %reduce-scatter.11.cloned.1.call-start = ((), (), s32[]{:S(2)}) async-start(), calls=%async_computation.8 | async-start | bytes 1310720 | tf_op jit(solution)/shard_map/reduce_scatter | solution.py:376
  483.4 11.3 %collective-permute-start.22 = (bf16[2,1024,128]{2,1,0:T(8,128)(2,1)S(1)}, bf16[2,1024,128]{2,1,0:T(8,128)(2,1)S(1)}, u32[]{:S(2)}, u32[]{:S(2)}) collective-permute-start(bf16[2,1024,128]{2,1,0:T(8,128)(2,1)S(1)} %constant_dynamic-slice_fusion.4), channel_id=1, source_target_pairs={{0,8},{4,12},{8,0},{12,4},{1,9},{5,13},{9,1},{13,5},{2,10},{6,14},... | collective-permute-start | bytes 1572872 | tf_op jit(solution)/shard_map/ppermute | solution.py:363
  484.9 10.8 %collective-permute-start.23 = (bf16[2,1024,128]{2,1,0:T(8,128)(2,1)S(1)}, bf16[2,1024,128]{2,1,0:T(8,128)(2,1)S(1)}, u32[]{:S(2)}, u32[]{:S(2)}) collective-permute-start(bf16[2,1024,128]{2,1,0:T(8,128)(2,1)S(1)} %constant_dynamic-slice_fusion.3), channel_id=1, source_target_pairs={{0,16},{16,0},{1,17},{17,1},{2,18},{18,2},{3,19},{19,3},{4,20},{20... | collective-permute-start | bytes 1572872 | tf_op jit(solution)/shard_map/ppermute | solution.py:363
  496.9 59.6 %all-gather.16.cloned.1.call-start = ((), (), s32[]{:S(2)}) async-start(), calls=%async_computation.11 | async-start | bytes 1802240 | tf_op jit(solution)/shard_map/all_gather | solution.py:438
  497.0 5.6 collective-permute-start.31
  503.5 75.0 %all-gather.12.cloned.1.call-start = ((), (), s32[]{:S(2)}) async-start(), calls=%async_computation.9 | async-start | bytes 2621440 | tf_op jit(solution)/shard_map/all_gather | solution.py:438
  510.4 11.5 %collective-permute-start.24 = (f32[4,1024]{1,0:T(4,128)S(1)}, f32[4,1024]{1,0:T(4,128)S(1)}, u32[]{:S(2)}, u32[]{:S(2)}) collective-permute-start(f32[4,1024]{1,0:T(4,128)S(1)} %pad_maximum_fusion.16), channel_id=1, source_target_pairs={{0,16},{16,0},{1,17},{17,1},{2,18},{18,2},{3,19},{19,3},{4,20},{20... | collective-permute-start | bytes 49160 | tf_op jit(solution)/shard_map/ppermute | solution.py:473
  521.8 28.8 %copy-start.20 = (f32[512,1024]{1,0:T(8,128)S(1)}, f32[512,1024]{1,0:T(8,128)}, u32[]{:S(2)}) copy-start(f32[512,1024]{1,0:T(8,128)} %copy-done.19) | copy-start | bytes 6291460
  521.9 20.2 %collective-permute-start.27 = (bf16[1024,512]{1,0:T(8,128)(2,1)}, bf16[1024,512]{1,0:T(8,128)(2,1)}, u32[]{:S(2)}, u32[]{:S(2)}) collective-permute-start(bf16[1024,512]{1,0:T(8,128)(2,1)} %get-tuple-element.143), channel_id=1, source_target_pairs={{0,16},{16,0},{1,17},{17,1},{2,18},{18,2},{3,19},{19,3},{4,20},{20... | collective-permute-start | bytes 3145736 | tf_op jit(solution)/shard_map/ppermute | solution.py:480
  522.9 1.2 collective-permute-start.25
  524.1 3.7 collective-permute-start.26
  525.5 15.6 %collective-permute-start.28 = (bf16[352,256]{1,0:T(8,128)(2,1)}, bf16[352,256]{1,0:T(8,128)(2,1)S(1)}, u32[]{:S(2)}, u32[]{:S(2)}) collective-permute-start(bf16[352,256]{1,0:T(8,128)(2,1)} %constant_dynamic-slice_fusion.2), channel_id=1, source_target_pairs={{0,8},{4,12},{8,0},{12,4},{1,9},{5,13},{9,1},{13,5},{2,10},{6,14},... | collective-permute-start | bytes 540680 | tf_op jit(solution)/shard_map/ppermute | solution.py:363
  543.2 6.4 %collective-permute-start.29 = (bf16[4,256,128]{2,1,0:T(8,128)(2,1)S(1)}, bf16[4,256,128]{2,1,0:T(8,128)(2,1)S(1)}, u32[]{:S(2)}, u32[]{:S(2)}) collective-permute-start(bf16[4,256,128]{2,1,0:T(8,128)(2,1)S(1)} %get-tuple-element.215), channel_id=1, source_target_pairs={{0,16},{16,0},{1,17},{17,1},{2,18},{18,2},{3,19},{19,3},{4,20},{20... | collective-permute-start | bytes 786440 | tf_op jit(solution)/shard_map/ppermute | solution.py:490
  558.1 20.4 %collective-permute-start.30 = (bf16[1024,512]{1,0:T(8,128)(2,1)S(1)}, bf16[1024,512]{1,0:T(8,128)(2,1)}, u32[]{:S(2)}, u32[]{:S(2)}) collective-permute-start(bf16[1024,512]{1,0:T(8,128)(2,1)S(1)} %get-tuple-element.150), channel_id=1, source_target_pairs={{0,16},{16,0},{1,17},{17,1},{2,18},{18,2},{3,19},{19,3},{4,20},{20... | collective-permute-start | bytes 3145736 | tf_op jit(solution)/shard_map/ppermute | solution.py:487
  (82 other events, 337.4 us)
Sparse Core Ops, SparseCore 0:
  11.6 123.7 all-gather.13
  138.2 60.3 all-gather.9
  301.9 31.5 reduce-scatter.4
  350.4 31.8 reduce-scatter.6
  463.7 25.5 reduce-scatter.8
  497.0 24.8 reduce-scatter.10
  524.1 17.5 all-gather.15
  550.8 23.4 all-gather.11

commit v17 on v16

--- a/solution.py
+++ b/solution.py
@@ -448,7 +448,8 @@
     sum_in = jnp.where(section == 0, sum_in, sum_in[::-1])
     sum_in = gathered(sum_in)
     grad_query_in = nt(dq1, wq[0])
-    grad_key_in = (nt(dk1, wk[0]) + nt(dv1, wv[0])).astype(BF)
+    of_keys = together(nt(dk1, wk[0]).astype(BF))
+    grad_key_in = (of_keys.astype(F32) + nt(dv1, wv[0])).astype(BF)
     half_one = over_section(half_one[0], 2), over_side(half_one[1], 2)
     grad_query_in, grad_key_in, half_one = together((grad_query_in, grad_key_in, half_one))
     half_one = jnp.concatenate([over_side(half_one[0], 2), over_section(half_one[1], 2)], axis=0)

time: 603 us -> 601 us (level)
  transfers between devices with their start and end apart: 40 -> 40, of which waited for: 14 -> 13; matrix products, arithmetic and copies ran while one was open for 42% -> 42% of each run, Pallas kernels for 10% -> 10%
where the time goes in v17:
time: 601 us; the launch traced here: 596 us
  matrix products  170 us (28%)
  waiting for transfers between devices  143 us (24%)
  other arithmetic  105 us (17%)
  Pallas kernels  60.8 us (10%)
  local copies, waits for them, and re-layouts  39.3 us (7%)
  blocking collectives  31.4 us (5%)
  starting transfers between devices  29.7 us (5%)
  between operations  16.1 us (3%)
    all_gather x1, waiting for transfers between devices, shards(): lax.all_gather(matrix, ('section', 'group', 'dp'), axis=0, tiled=True)  85.7 us
    dot_general x11, matrix products, nt(): lax.dot_general(left, right, (((1,), (1,)), ((), ())), preferred_element_...  62.5 us
    dot_general x10, matrix products, nn(): return jnp.dot(left, right, preferred_element_type=F32)  52.4 us
    dot_general x20, matrix products, tn(): lax.dot_general(left, right, (((0,), (0,)), ((), ())), preferred_element_...  50.4 us
    pallas_call x2, Pallas kernels, attend_back(): pl.pallas_call(functools.partial(attend_back_kernel, chunk, spans), grid_...  39.9 us
    ppermute x10, waiting for transfers between devices, exchanged(): lax.ppermute(other, axis, pairs).astype(F32)  22.1 us
    pallas_call x2, Pallas kernels, attend(): pl.pallas_call(functools.partial(attend_kernel, chunk, spans), grid_spec=...  20.9 us
    unnamed x189, local copies, waits for them, and re-layouts  18 us
  transfers between devices with their start and end apart: 40, of which 13 were waited for; matrix products, arithmetic and copies ran while one was open for 42% of the time, Pallas kernels for 10%

profile of v17, /device:TPU:0, one launch (start us, length us, event | category | flops | bytes accessed | tf_op | source)
XLA Modules:
  0.0 595.5 jit_solution(14109886989950105706)
XLA Ops:
  24.1 3.7 multiply_reduce_fusion.5
  27.9 3.8 fusion.9
  33.8 4.7 all_gather.31
  39.2 4.2 fusion.11
  49.6 85.7 %all-gather.14.cloned.1.call-done = bf16[1,8192,1024]{2,1,0:T(8,128)(2,1)} async-done(((bf16[1,256,1024]{2,1,0:T(8,128)(2,1)}), bf16[1,8192,1024]{2,1,0:T(8,128)(2,1)}) %all-gather.14.cloned.1.call-update) | async-done | bytes 16777232 | tf_op jit(solution)/shard_map/all_gather | solution.py:264
  135.3 9.3 %convolution_convert_fusion.3.v_ref = bf16[2048,1024]{1,0:T(8,128)(2,1)} fusion(bf16[2048,1024]{1,0:T(8,128)(2,1)} %bitcast.273, bf16[2,4,1024,1024]{3,2,1,0:T(8,128)(2,1)} %bitcast.336), kind=kOutput, calls=%fused_computation.53 | convolution fusion | flops 4297064448 | bytes 10485760 | tf_op jit(solution)/shard_map/dot_general | solution.py:31
  149.2 8.0 %convolution_convert_fusion.4.k_ref = bf16[2048,1024]{1,0:T(8,128)(2,1)} fusion(bf16[2048,1024]{1,0:T(8,128)(2,1)S(1)} %bitcast.274, bf16[2,4,1024,1024]{3,2,1,0:T(8,128)(2,1)} %bitcast.338), kind=kOutput, calls=%fused_computation.54 | convolution fusion | flops 4297064448 | bytes 10485760 | tf_op jit(solution)/shard_map/dot_general | solution.py:31
  157.2 16.9 %attend.2 = (bf16[512,1024]{1,0:T(8,128)(2,1)S(1)}, f32[2,8,2,256]{3,2,1,0:T(2,128)S(1)}) custom-call(s32[2,2]{1,0:T(2,128)S(1)} %get-tuple-element.248.first_ref, s32[2,2]{1,0:T(2,128)S(1)} %get-tuple-element.233.stop_ref, s32[2,1,256]{2,1,0:T(1,128)S(1)} %broadcast_in_dim.73.lo_ref, s32[2,1,256]{2,1,0:T(1,128)S(1)} %bitcast.260, ...), custom_call_target="tpu_custom_call" | custom-call | flops 8589934592 | bytes 18874368 | tf_op jit(solution)/shard_map/attend/pallas_call | solution.py:186
  174.0 3.4 fusion.27
  177.5 3.3 fusion.82.v_ref
  180.8 3.3 fusion.83.k_ref
  184.1 3.3 fusion.84.q_ref
  187.4 4.0 attend.3
  200.0 3.3 maximum_select_fusion.1
  203.3 5.8 convolution_convert_fusion.1
  209.1 14.8 %collective-permute-done.4 = bf16[512,1024]{1,0:T(8,128)(2,1)} collective-permute-done((bf16[512,1024]{1,0:T(8,128)(2,1)S(1)}, bf16[512,1024]{1,0:T(8,128)(2,1)}, u32[]{:S(2)}, u32[]{:S(2)}) %collective-permute-start.4) | collective-permute-done | bytes 1048608 | tf_op jit(solution)/shard_map/ppermute | solution.py:345
  223.9 9.5 %fusion.111 = f32[1024,2816]{1,0:T(8,128)S(1)} fusion(bf16[1024,2816]{1,0:T(8,128)(2,1)} %bitcast.352, bf16[512,1024]{1,0:T(8,128)(2,1)} %collective-permute-done.4, bf16[512,1024]{1,0:T(8,128)(2,1)} %copy-done.54), kind=kOutput, calls=%fused_computation.203 | convolution fusion | flops 5909774336 | bytes 19398656 | tf_op jit(solution)/shard_map/dot_general | solution.py:31
  233.4 4.6 fusion.17
  238.0 3.3 pad_maximum_fusion
  241.3 7.9 %fusion.78 = bf16[512,1024]{1,0:T(8,128)(2,1)S(1)} fusion(bf16[1024,2816]{1,0:T(8,128)(2,1)} %bitcast.353, bf16[1024,2816]{1,0:T(8,128)(2,1)S(1)} %pad_maximum_fusion), kind=kOutput, calls=%fused_computation.155 | convolution fusion | flops 2953314304 | bytes 9699328 | tf_op jit(solution)/shard_map/dot_general | solution.py:39
  254.7 6.3 %convolution_convert_fusion = bf16[1024,1408]{1,0:T(8,128)(2,1)} fusion(bf16[1024,2816]{1,0:T(8,128)(2,1)S(1)} %pad_maximum_fusion, s32[]{:T(128)S(6)} %select_n.315, bf16[512,1024]{1,0:T(8,128)(2,1)} %collective-permute-done.4, bf16[512,1024]{1,0:T(8,128)(2,1)S(1)} %copy-done.55), kind=kOutput, calls=%fused_computation.50 | convolution fusion | flops 2958426112 | bytes 7864324 | tf_op jit(solution)/shard_map/dot_general | solution.py:35
  264.5 6.1 %fusion.179 = f32[1024,1024]{1,0:T(8,128)S(1)} fusion(bf16[1024,1408]{1,0:T(8,128)(2,1)} %copy-done.28, bf16[1408,1024]{1,0:T(8,128)(2,1)} %bitcast.278), kind=kOutput, calls=%fused_computation.363 | convolution fusion | flops 2952790016 | bytes 9961472 | tf_op jit(solution)/shard_map/dot_general | solution.py:31
  279.1 6.9 %add_convert_fusion.1 = bf16[1024,1408]{1,0:T(8,128)(2,1)S(1)} fusion(bf16[1024,1408]{1,0:T(8,128)(2,1)} %collective-permute-done.9, bf16[1024,2816]{1,0:T(8,128)(2,1)} %copy-done.27, s32[]{:T(128)S(6)} %select_n.318, bf16[512,1024]{1,0:T(8,128)(2,1)} %collective-permute-done.4, bf16[512,1024]{1,0:T(8,128)(2,1)} %copy-done.54), kind=kOutput, calls=%fused_computation.31 | convolution fusion | flops 2961309696 | bytes 10747908 | tf_op jit(solution)/shard_map/dot_general | solution.py:35
  286.0 5.3 collective-permute-done.8
  291.3 7.6 %multiply_reduce_fusion = (f32[1024]{0:T(1024)S(1)}, f32[512]{0:T(512)S(1)}, f32[512,1024]{1,0:T(8,128)}) fusion(f32[512,1024]{1,0:T(8,128)S(1)} %get-tuple-element.245, f32[512]{0:T(512)S(1)} %get-tuple-element.229, bf16[256,1024]{1,0:T(8,128)(2,1)} %collective-permute-done.8, bf16[256,1024]{1,0:T(8,128)(2,1)} %collective-permute-done.7, ...), kind=kOutput, calls=%fused_computation.101 | convolution fusion | flops 2958555648 | bytes 13905920 | tf_op jit(solution)/shard_map/dot_general | solution.py:39
  301.2 3.9 fusion.170
  305.1 4.3 fusion.81.dc_ref
  309.4 11.5 %attend_back.2 = (bf16[512,1024]{1,0:T(8,128)(2,1)S(1)}, bf16[512,1024]{1,0:T(8,128)(2,1)S(1)}, bf16[512,1024]{1,0:T(8,128)(2,1)S(1)}) custom-call(s32[2,2]{1,0:T(2,128)S(1)} %get-tuple-element.251.first_ref, s32[2,2]{1,0:T(2,128)S(1)} %get-tuple-element.250.stop_ref, s32[2,1,256]{2,1,0:T(1,128)S(1)} %broadcast_in_dim.83.lo_ref, ...), custom_call_target="tpu_custom_call" | custom-call | flops 5368709120 | bytes 6291456 | tf_op jit(solution)/shard_map/attend_back/pallas_call | solution.py:210
  327.6 5.5 collective-permute-done.11
  336.0 4.3 fusion.13
  355.7 3.6 fusion.36
  374.2 28.4 %attend_back.3 = (bf16[512,1024]{1,0:T(8,128)(2,1)S(1)}, bf16[2048,1024]{1,0:T(8,128)(2,1)}, bf16[2048,1024]{1,0:T(8,128)(2,1)}) custom-call(s32[2,2]{1,0:T(2,128)S(1)} %get-tuple-element.249.first_ref, s32[2,2]{1,0:T(2,128)S(1)} %get-tuple-element.232.stop_ref, s32[2,1,256]{2,1,0:T(1,128)S(1)} %broadcast_in_dim.73.lo_ref, s32[2,1,256]{2,1,0:T(1,128)S(1)} %bitcast.261, ...), custom_call_target="tpu_custom_call" | custom-call | flops 21474836480 | bytes 18874368 | tf_op jit(solution)/shard_map/attend_back/pallas_call | solution.py:210
  402.6 4.1 fusion.87
  418.9 3.7 fusion.69
  424.9 3.8 fusion.66
  430.8 5.3 collective-permute-done.18
  438.9 3.7 fusion.21
  443.0 3.6 fusion.20
  450.8 9.4 %convolution_convert_fusion.2 = bf16[2048,1024]{1,0:T(8,128)(2,1)} fusion(bf16[2048,1024]{1,0:T(8,128)(2,1)} %get-tuple-element.129, bf16[2,4,1024,1024]{3,2,1,0:T(8,128)(2,1)} %bitcast.349), kind=kOutput, calls=%fused_computation.52 | convolution fusion | flops 4297064448 | bytes 10485760 | tf_op jit(solution)/shard_map/dot_general | solution.py:39
  460.3 10.6 %add_convert_fusion = bf16[2048,1024]{1,0:T(8,128)(2,1)} fusion(bf16[2048,1024]{1,0:T(8,128)(2,1)} %convolution_convert_fusion.2, bf16[2048,1024]{1,0:T(8,128)(2,1)} %get-tuple-element.130, bf16[2,4,1024,1024]{3,2,1,0:T(8,128)(2,1)} %bitcast.350), kind=kOutput, calls=%fused_computation.22 | convolution fusion | flops 4301258752 | bytes 14680064 | tf_op jit(solution)/shard_map/dot_general | solution.py:39
  470.9 4.2 fusion.50
  481.2 9.3 %collective-permute-done.22 = bf16[2,1024,128]{2,1,0:T(8,128)(2,1)S(1)} collective-permute-done((bf16[2,1024,128]{2,1,0:T(8,128)(2,1)S(1)}, bf16[2,1024,128]{2,1,0:T(8,128)(2,1)S(1)}, u32[]{:S(2)}, u32[]{:S(2)}) %collective-permute-start.22) | collective-permute-done | bytes 524320 | tf_op jit(solution)/shard_map/ppermute | solution.py:363
  494.1 4.0 collective-permute-done.31
  499.0 6.1 %fusion.7 = (f32[1024]{0:T(1024)S(1)}, f32[2048]{0:T(1024)S(1)}) fusion(bf16[2048,1024]{1,0:T(8,128)(2,1)} %add_convert_fusion, f32[2048]{0:T(1024)S(1)} %bitcast.295, bf16[4,1024,1024]{2,1,0:T(8,128)(2,1)} %param.9, s32[]{:T(128)S(6)} %select_n.279, f32[1024]{0:T(1024)S(1)} %bitcast.299), kind=kLoop, calls=%fused_computation.9 | loop fusion | flops 16774144 | bytes 8413188 | tf_op jit(solution)/shard_map/reduce_sum | solution.py:238
  523.4 16.3 %all-gather.4 = f32[4,4,1024]{2,1,0:T(4,128)S(1)} all-gather(f32[1,4,1024]{2,1,0:T(4,128)S(1)} %add_bitcast_fusion), channel_id=3, replica_groups=mesh['section'=2,'group'=4,'dp'=4] {'dp'}, dimensions={0}, use_global_device_ids=true | all-gather | bytes 81920 | tf_op jit(solution)/shard_map/all_gather | solution.py:484
  542.2 6.1 %collective-permute-done.29 = bf16[4,256,128]{2,1,0:T(8,128)(2,1)S(1)} collective-permute-done((bf16[4,256,128]{2,1,0:T(8,128)(2,1)S(1)}, bf16[4,256,128]{2,1,0:T(8,128)(2,1)S(1)}, u32[]{:S(2)}, u32[]{:S(2)}) %collective-permute-start.29) | collective-permute-done | bytes 262176 | tf_op jit(solution)/shard_map/ppermute | solution.py:491
  557.1 8.6 %maximum_convert_fusion = f32[128,5632]{1,0:T(8,128)} fusion(bf16[64,1408]{1,0:T(8,128)(2,1)S(1)} %get-tuple-element.197, bf16[64,1408]{1,0:T(8,128)(2,1)S(1)} %get-tuple-element.198, bf16[64,1408]{1,0:T(8,128)(2,1)S(1)} %get-tuple-element.199, bf16[64,1408]{1,0:T(8,128)(2,1)S(1)} %get-tuple-element.200, bf16[64,1408]{1,0:T(8,128)(2,1)S(1)} %get-tuple-element.201, ...), kind=kLoop, calls=%fused_computation.169 | loop fusion | flops 11534336 | bytes 4325376 | tf_op jit(solution)/shard_map/concatenate | solution.py:475
  566.3 10.5 %all-gather.3 = bf16[1408,256]{1,0:T(8,128)(2,1)S(1)} all-gather(bf16[352,256]{1,0:T(8,128)(2,1)S(1)} %add_convert_fusion.13), channel_id=5, replica_groups=mesh['section'=2,'group'=4,'dp'=4] {'group'}, dimensions={0}, use_global_device_ids=true | all-gather | bytes 901120 | tf_op jit(solution)/shard_map/all_gather | solution.py:438
  (406 shorter events, 173.8 us)
Async XLA Ops:
  7.2 20.6 %copy-start = (s32[4,256]{1,0:T(4,128)S(1)}, s32[4,256]{1,0:T(4,128)}, u32[]{:S(2)}) copy-start(s32[4,256]{1,0:T(4,128)} %param.11) | copy-start | bytes 12292
  7.2 128.2 %all-gather.14.cloned.1.call-start = ((), (), s32[]{:S(2)}) async-start(), calls=%async_computation.10 | async-start | bytes 17301504 | tf_op jit(solution)/shard_map/all_gather | solution.py:264
  9.3 214.6 %all-gather.10.cloned.1.call-start = ((), (), s32[]{:S(2)}) async-start(), calls=%async_computation.4 | async-start | bytes 6127616 | tf_op jit(solution)/shard_map/all_gather | solution.py:287
  11.9 33.8 %collective-permute-start = (bf16[88,1024]{1,0:T(8,128)(2,1)S(1)}, bf16[88,1024]{1,0:T(8,128)(2,1)}, u32[]{:S(2)}, u32[]{:S(2)}) collective-permute-start(bf16[88,1024]{1,0:T(8,128)(2,1)S(1)} %get-tuple-element.170), channel_id=1, source_target_pairs={{0,1},{1,2},{2,3},{3,0},{4,5},{5,6},{6,7},{7,4},{8,9},{9,10},{10,1... | collective-permute-start | bytes 540680 | tf_op jit(solution)/shard_map/ppermute | solution.py:293
  14.9 32.4 %collective-permute-start.1 = (bf16[88,1024]{1,0:T(8,128)(2,1)S(1)}, bf16[88,1024]{1,0:T(8,128)(2,1)}, u32[]{:S(2)}, u32[]{:S(2)}) collective-permute-start(bf16[88,1024]{1,0:T(8,128)(2,1)S(1)} %get-tuple-element.170), channel_id=1, source_target_pairs={{0,2},{1,3},{2,0},{3,1},{4,6},{5,7},{6,4},{7,5},{8,10},{9,11},{10,... | collective-permute-start | bytes 540680 | tf_op jit(solution)/shard_map/ppermute | solution.py:293
  17.5 31.4 %collective-permute-start.2 = (bf16[88,1024]{1,0:T(8,128)(2,1)S(1)}, bf16[88,1024]{1,0:T(8,128)(2,1)S(1)}, u32[]{:S(2)}, u32[]{:S(2)}) collective-permute-start(bf16[88,1024]{1,0:T(8,128)(2,1)S(1)} %get-tuple-element.170), channel_id=1, source_target_pairs={{0,3},{1,0},{2,1},{3,2},{4,7},{5,4},{6,5},{7,6},{8,11},{9,8},{10,9... | collective-permute-start | bytes 540680 | tf_op jit(solution)/shard_map/ppermute | solution.py:293
  20.2 11.5 %collective-permute-start.6 = (bf16[32,2816]{1,0:T(8,128)(2,1)S(1)}, bf16[32,2816]{1,0:T(8,128)(2,1)S(1)}, u32[]{:S(2)}, u32[]{:S(2)}) collective-permute-start(bf16[32,2816]{1,0:T(8,128)(2,1)S(1)} %pad_maximum_fusion.15), channel_id=1, source_target_pairs={{0,16},{16,0},{1,17},{17,1},{2,18},{18,2},{3,19},{19,3},{4,20},{20... | collective-permute-start | bytes 540680 | tf_op jit(solution)/shard_map/ppermute | solution.py:285
  27.8 17.2 %copy-start.17 = (f32[2,256,1024]{2,1,0:T(8,128)}, f32[2,256,1024]{2,1,0:T(8,128)S(1)}, u32[]{:S(2)}) copy-start(f32[2,256,1024]{2,1,0:T(8,128)S(1)} %get-tuple-element.241) | copy-start | bytes 6291460
  32.5 303.5 %reduce-scatter.5.cloned.1.call-start = ((), (), s32[]{:S(2)}) async-start(), calls=%async_computation.5 | async-start | bytes 1802240 | tf_op jit(solution)/shard_map/reduce_scatter | solution.py:376
  39.2 224.7 %copy-start.67 = (f32[1,8,2,128]{3,2,1,0:T(2,128)}, f32[1,8,2,128]{3,2,1,0:T(2,128)S(1)}, u32[]{:S(2)}) copy-start(f32[1,8,2,128]{3,2,1,0:T(2,128)S(1)} %get-tuple-element.222) | copy-start | bytes 24580
  144.7 46.8 %collective-permute-start.3 = (bf16[4,88,1024]{2,1,0:T(8,128)(2,1)}, bf16[4,88,1024]{2,1,0:T(8,128)(2,1)S(1)}, u32[]{:S(2)}, u32[]{:S(2)}) collective-permute-start(bf16[4,88,1024]{2,1,0:T(8,128)(2,1)} %bitcast_dynamic-update-slice_fusion), channel_id=1, source_target_pairs={{0,8},{4,12},{8,0},{12,4},{1,9},{5,13},{9,1},{13,5},{2,10},{6,14},... | collective-permute-start | bytes 2162696 | tf_op jit(solution)/shard_map/ppermute | solution.py:276
  157.2 16.9 %copy-start.22 = (f32[512,1024]{1,0:T(8,128)S(1)}, f32[512,1024]{1,0:T(8,128)}, u32[]{:S(2)}) copy-start(f32[512,1024]{1,0:T(8,128)} %bitcast_divide_fusion) | copy-start | bytes 6291460
  194.5 5.4 collective-permute-start.5
  198.1 25.8 %collective-permute-start.4 = (bf16[512,1024]{1,0:T(8,128)(2,1)S(1)}, bf16[512,1024]{1,0:T(8,128)(2,1)}, u32[]{:S(2)}, u32[]{:S(2)}) collective-permute-start(bf16[512,1024]{1,0:T(8,128)(2,1)S(1)} %multiply_convert_fusion.2), channel_id=1, source_target_pairs={{0,16},{16,0},{1,17},{17,1},{2,18},{18,2},{3,19},{19,3},{4,20},{20... | collective-permute-start | bytes 3145736 | tf_op jit(solution)/shard_map/ppermute | solution.py:345
  250.1 13.7 %collective-permute-start.7 = (bf16[256,1024]{1,0:T(8,128)(2,1)S(1)}, bf16[256,1024]{1,0:T(8,128)(2,1)}, u32[]{:S(2)}, u32[]{:S(2)}) collective-permute-start(bf16[256,1024]{1,0:T(8,128)(2,1)S(1)} %get-tuple-element.209), channel_id=1, source_target_pairs={{0,16},{16,0},{1,17},{17,1},{2,18},{18,2},{3,19},{19,3},{4,20},{20... | collective-permute-start | bytes 1572872 | tf_op jit(solution)/shard_map/ppermute | solution.py:392
  263.9 15.2 %collective-permute-start.9 = (bf16[1024,1408]{1,0:T(8,128)(2,1)}, bf16[1024,1408]{1,0:T(8,128)(2,1)}, u32[]{:S(2)}, u32[]{:S(2)}) collective-permute-start(bf16[1024,1408]{1,0:T(8,128)(2,1)} %convolution_convert_fusion), channel_id=1, source_target_pairs={{0,4},{4,0},{8,12},{12,8},{1,5},{5,1},{9,13},{13,9},{2,6},{6,2},{1... | collective-permute-start | bytes 8650760 | tf_op jit(solution)/shard_map/ppermute | solution.py:386
  263.9 13.6 %collective-permute-start.10 = (bf16[1408,512]{1,0:T(8,128)(2,1)}, bf16[1408,512]{1,0:T(8,128)(2,1)S(1)}, u32[]{:S(2)}, u32[]{:S(2)}) collective-permute-start(bf16[1408,512]{1,0:T(8,128)(2,1)} %convolution_convert_fusion.5), channel_id=1, source_target_pairs={{0,4},{4,0},{8,12},{12,8},{1,5},{5,1},{9,13},{13,9},{2,6},{6,2},{1... | collective-permute-start | bytes 4325384 | tf_op jit(solution)/shard_map/ppermute | solution.py:386
  277.1 14.2 %collective-permute-start.8 = (bf16[256,1024]{1,0:T(8,128)(2,1)}, bf16[256,1024]{1,0:T(8,128)(2,1)}, u32[]{:S(2)}, u32[]{:S(2)}) collective-permute-start(bf16[256,1024]{1,0:T(8,128)(2,1)} %get-tuple-element.95), channel_id=1, source_target_pairs={{0,16},{16,0},{1,17},{17,1},{2,18},{18,2},{3,19},{19,3},{4,20},{20... | collective-permute-start | bytes 1572872 | tf_op jit(solution)/shard_map/ppermute | solution.py:396
  286.0 12.9 %copy-start.44 = (bf16[1024,1408]{1,0:T(8,128)(2,1)}, bf16[1024,1408]{1,0:T(8,128)(2,1)S(1)}, u32[]{:S(2)}) copy-start(bf16[1024,1408]{1,0:T(8,128)(2,1)S(1)} %add_convert_fusion.1) | copy-start | bytes 8650756
  300.2 33.0 %collective-permute-start.11 = (bf16[2,4,1,64,1408]{4,3,2,1,0:T(8,128)(2,1)}, bf16[2,4,1,64,1408]{4,3,2,1,0:T(8,128)(2,1)}, u32[]{:S(2)}, u32[]{:S(2)}) collective-permute-start(bf16[2,4,1,64,1408]{4,3,2,1,0:T(8,128)(2,1)} %constant_dynamic-slice_fusion.11), channel_id=1, source_target_pairs={{0,8},{4,12},{8,0},{12,4},{1,9},{5,13},{9,1},{13,5},{2,10},{6,14},... | collective-permute-start | bytes 4325384 | tf_op jit(solution)/shard_map/ppermute | solution.py:363
  300.7 145.9 %reduce-scatter.7.cloned.1.call-start = ((), (), s32[]{:S(2)}) async-start(), calls=%async_computation.6 | async-start | bytes 1802240 | tf_op jit(solution)/shard_map/reduce_scatter | solution.py:376
  305.1 15.8 %copy-start.52 = (bf16[512,1024]{1,0:T(8,128)(2,1)}, bf16[512,1024]{1,0:T(8,128)(2,1)S(1)}, u32[]{:S(2)}) copy-start(bf16[512,1024]{1,0:T(8,128)(2,1)S(1)} %get-tuple-element.167) | copy-start | bytes 3145732
  336.0 31.4 %collective-permute-start.12 = (bf16[4,1024,512]{2,1,0:T(8,128)(2,1)}, bf16[4,1024,512]{2,1,0:T(8,128)(2,1)}, u32[]{:S(2)}, u32[]{:S(2)}) collective-permute-start(bf16[4,1024,512]{2,1,0:T(8,128)(2,1)} %pad_maximum_fusion.1), channel_id=1, source_target_pairs={{0,4},{4,0},{8,12},{12,8},{1,5},{5,1},{9,13},{13,9},{2,6},{6,2},{1... | collective-permute-start | bytes 12582920 | tf_op jit(solution)/shard_map/ppermute | solution.py:386
  340.3 31.3 %collective-permute-start.13 = (bf16[1024,512]{1,0:T(8,128)(2,1)}, bf16[1024,512]{1,0:T(8,128)(2,1)}, u32[]{:S(2)}, u32[]{:S(2)}) collective-permute-start(bf16[1024,512]{1,0:T(8,128)(2,1)} %fusion.38), channel_id=1, source_target_pairs={{0,16},{16,0},{1,17},{17,1},{2,18},{18,2},{3,19},{19,3},{4,20},{20... | collective-permute-start | bytes 3145736 | tf_op jit(solution)/shard_map/ppermute | solution.py:404
  349.4 143.0 %reduce-scatter.9.cloned.1.call-start = ((), (), s32[]{:S(2)}) async-start(), calls=%async_computation.7 | async-start | bytes 1310720 | tf_op jit(solution)/shard_map/reduce_scatter | solution.py:376
  372.0 40.0 %collective-permute-start.15 = (bf16[2,1024,256]{2,1,0:T(8,128)(2,1)S(1)}, bf16[2,1024,256]{2,1,0:T(8,128)(2,1)}, u32[]{:S(2)}, u32[]{:S(2)}) collective-permute-start(bf16[2,1024,256]{2,1,0:T(8,128)(2,1)S(1)} %constant_dynamic-slice_fusion.9), channel_id=1, source_target_pairs={{0,8},{4,12},{8,0},{12,4},{1,9},{5,13},{9,1},{13,5},{2,10},{6,14},... | collective-permute-start | bytes 3145736 | tf_op jit(solution)/shard_map/ppermute | solution.py:363
  373.2 40.3 %collective-permute-start.14 = (bf16[2,1024,256]{2,1,0:T(8,128)(2,1)S(1)}, bf16[2,1024,256]{2,1,0:T(8,128)(2,1)S(1)}, u32[]{:S(2)}, u32[]{:S(2)}) collective-permute-start(bf16[2,1024,256]{2,1,0:T(8,128)(2,1)S(1)} %constant_dynamic-slice_fusion.10), channel_id=1, source_target_pairs={{0,16},{16,0},{1,17},{17,1},{2,18},{18,2},{3,19},{19,3},{4,20},{20... | collective-permute-start | bytes 3145736 | tf_op jit(solution)/shard_map/ppermute | solution.py:363
  374.2 28.4 %copy-start.16 = (bf16[2048,1024]{1,0:T(8,128)(2,1)S(1)}, bf16[2048,1024]{1,0:T(8,128)(2,1)}, u32[]{:S(2)}) copy-start(bf16[2048,1024]{1,0:T(8,128)(2,1)} %fusion.13) | copy-start | bytes 12582916
  417.5 21.4 %collective-permute-start.17 = (bf16[2,1024,512]{2,1,0:T(8,128)(2,1)}, bf16[2,1024,512]{2,1,0:T(8,128)(2,1)}, u32[]{:S(2)}, u32[]{:S(2)}) collective-permute-start(bf16[2,1024,512]{2,1,0:T(8,128)(2,1)} %pad_maximum_fusion.6), channel_id=1, source_target_pairs={{0,4},{4,0},{8,12},{12,8},{1,5},{5,1},{9,13},{13,9},{2,6},{6,2},{1... | collective-permute-start | bytes 6291464 | tf_op jit(solution)/shard_map/ppermute | solution.py:386
  417.5 25.2 %collective-permute-start.16 = (bf16[2,1024,512]{2,1,0:T(8,128)(2,1)}, bf16[2,1024,512]{2,1,0:T(8,128)(2,1)}, u32[]{:S(2)}, u32[]{:S(2)}) collective-permute-start(bf16[2,1024,512]{2,1,0:T(8,128)(2,1)} %pad_maximum_fusion.5), channel_id=1, source_target_pairs={{0,4},{4,0},{8,12},{12,8},{1,5},{5,1},{9,13},{13,9},{2,6},{6,2},{1... | collective-permute-start | bytes 6291464 | tf_op jit(solution)/shard_map/ppermute | solution.py:386
  422.7 13.5 %collective-permute-start.18 = (bf16[2,1024,128]{2,1,0:T(8,128)(2,1)S(1)}, bf16[2,1024,128]{2,1,0:T(8,128)(2,1)S(1)}, u32[]{:S(2)}, u32[]{:S(2)}) collective-permute-start(bf16[2,1024,128]{2,1,0:T(8,128)(2,1)S(1)} %constant_dynamic-slice_fusion.8), channel_id=1, source_target_pairs={{0,8},{4,12},{8,0},{12,4},{1,9},{5,13},{9,1},{13,5},{2,10},{6,14},... | collective-permute-start | bytes 1572872 | tf_op jit(solution)/shard_map/ppermute | solution.py:363
  424.4 13.3 %collective-permute-start.19 = (bf16[2,1024,128]{2,1,0:T(8,128)(2,1)S(1)}, bf16[2,1024,128]{2,1,0:T(8,128)(2,1)S(1)}, u32[]{:S(2)}, u32[]{:S(2)}) collective-permute-start(bf16[2,1024,128]{2,1,0:T(8,128)(2,1)S(1)} %constant_dynamic-slice_fusion.7), channel_id=1, source_target_pairs={{0,16},{16,0},{1,17},{17,1},{2,18},{18,2},{3,19},{19,3},{4,20},{20... | collective-permute-start | bytes 1572872 | tf_op jit(solution)/shard_map/ppermute | solution.py:363
  447.7 27.4 %collective-permute-start.21 = (bf16[2,1024,256]{2,1,0:T(8,128)(2,1)}, bf16[2,1024,256]{2,1,0:T(8,128)(2,1)}, u32[]{:S(2)}, u32[]{:S(2)}) collective-permute-start(bf16[2,1024,256]{2,1,0:T(8,128)(2,1)} %constant_dynamic-slice_fusion.5), channel_id=1, source_target_pairs={{0,8},{4,12},{8,0},{12,4},{1,9},{5,13},{9,1},{13,5},{2,10},{6,14},... | collective-permute-start | bytes 3145736 | tf_op jit(solution)/shard_map/ppermute | solution.py:363
  449.6 27.1 %collective-permute-start.20 = (bf16[2,1024,256]{2,1,0:T(8,128)(2,1)}, bf16[2,1024,256]{2,1,0:T(8,128)(2,1)}, u32[]{:S(2)}, u32[]{:S(2)}) collective-permute-start(bf16[2,1024,256]{2,1,0:T(8,128)(2,1)} %constant_dynamic-slice_fusion.6), channel_id=1, source_target_pairs={{0,16},{16,0},{1,17},{17,1},{2,18},{18,2},{3,19},{19,3},{4,20},{20... | collective-permute-start | bytes 3145736 | tf_op jit(solution)/shard_map/ppermute | solution.py:363
  460.2 80.6 %reduce-scatter.11.cloned.1.call-start = ((), (), s32[]{:S(2)}) async-start(), calls=%async_computation.8 | async-start | bytes 1310720 | tf_op jit(solution)/shard_map/reduce_scatter | solution.py:376
  478.6 11.9 %collective-permute-start.22 = (bf16[2,1024,128]{2,1,0:T(8,128)(2,1)S(1)}, bf16[2,1024,128]{2,1,0:T(8,128)(2,1)S(1)}, u32[]{:S(2)}, u32[]{:S(2)}) collective-permute-start(bf16[2,1024,128]{2,1,0:T(8,128)(2,1)S(1)} %constant_dynamic-slice_fusion.4), channel_id=1, source_target_pairs={{0,8},{4,12},{8,0},{12,4},{1,9},{5,13},{9,1},{13,5},{2,10},{6,14},... | collective-permute-start | bytes 1572872 | tf_op jit(solution)/shard_map/ppermute | solution.py:363
  479.4 11.7 %collective-permute-start.23 = (bf16[2,1024,128]{2,1,0:T(8,128)(2,1)S(1)}, bf16[2,1024,128]{2,1,0:T(8,128)(2,1)S(1)}, u32[]{:S(2)}, u32[]{:S(2)}) collective-permute-start(bf16[2,1024,128]{2,1,0:T(8,128)(2,1)S(1)} %constant_dynamic-slice_fusion.3), channel_id=1, source_target_pairs={{0,16},{16,0},{1,17},{17,1},{2,18},{18,2},{3,19},{19,3},{4,20},{20... | collective-permute-start | bytes 1572872 | tf_op jit(solution)/shard_map/ppermute | solution.py:363
  492.4 62.8 %all-gather.16.cloned.1.call-start = ((), (), s32[]{:S(2)}) async-start(), calls=%async_computation.11 | async-start | bytes 1802240 | tf_op jit(solution)/shard_map/all_gather | solution.py:438
  492.5 5.6 collective-permute-start.31
  498.9 79.2 %all-gather.12.cloned.1.call-start = ((), (), s32[]{:S(2)}) async-start(), calls=%async_computation.9 | async-start | bytes 2621440 | tf_op jit(solution)/shard_map/all_gather | solution.py:438
  506.0 11.9 %collective-permute-start.24 = (f32[4,1024]{1,0:T(4,128)S(1)}, f32[4,1024]{1,0:T(4,128)S(1)}, u32[]{:S(2)}, u32[]{:S(2)}) collective-permute-start(f32[4,1024]{1,0:T(4,128)S(1)} %pad_maximum_fusion.16), channel_id=1, source_target_pairs={{0,16},{16,0},{1,17},{17,1},{2,18},{18,2},{3,19},{19,3},{4,20},{20... | collective-permute-start | bytes 49160 | tf_op jit(solution)/shard_map/ppermute | solution.py:474
  517.9 31.4 %copy-start.20 = (f32[512,1024]{1,0:T(8,128)S(1)}, f32[512,1024]{1,0:T(8,128)}, u32[]{:S(2)}) copy-start(f32[512,1024]{1,0:T(8,128)} %copy-done.19) | copy-start | bytes 6291460
  517.9 22.8 %collective-permute-start.27 = (bf16[1024,512]{1,0:T(8,128)(2,1)}, bf16[1024,512]{1,0:T(8,128)(2,1)}, u32[]{:S(2)}, u32[]{:S(2)}) collective-permute-start(bf16[1024,512]{1,0:T(8,128)(2,1)} %get-tuple-element.143), channel_id=1, source_target_pairs={{0,16},{16,0},{1,17},{17,1},{2,18},{18,2},{3,19},{19,3},{4,20},{20... | collective-permute-start | bytes 3145736 | tf_op jit(solution)/shard_map/ppermute | solution.py:481
  518.5 1.2 collective-permute-start.25
  519.7 3.7 collective-permute-start.26
  521.5 18.2 %collective-permute-start.28 = (bf16[352,256]{1,0:T(8,128)(2,1)}, bf16[352,256]{1,0:T(8,128)(2,1)S(1)}, u32[]{:S(2)}, u32[]{:S(2)}) collective-permute-start(bf16[352,256]{1,0:T(8,128)(2,1)} %constant_dynamic-slice_fusion.2), channel_id=1, source_target_pairs={{0,8},{4,12},{8,0},{12,4},{1,9},{5,13},{9,1},{13,5},{2,10},{6,14},... | collective-permute-start | bytes 540680 | tf_op jit(solution)/shard_map/ppermute | solution.py:363
  541.9 6.4 %collective-permute-start.29 = (bf16[4,256,128]{2,1,0:T(8,128)(2,1)S(1)}, bf16[4,256,128]{2,1,0:T(8,128)(2,1)S(1)}, u32[]{:S(2)}, u32[]{:S(2)}) collective-permute-start(bf16[4,256,128]{2,1,0:T(8,128)(2,1)S(1)} %get-tuple-element.215), channel_id=1, source_target_pairs={{0,16},{16,0},{1,17},{17,1},{2,18},{18,2},{3,19},{19,3},{4,20},{20... | collective-permute-start | bytes 786440 | tf_op jit(solution)/shard_map/ppermute | solution.py:491
  556.7 21.5 %collective-permute-start.30 = (bf16[1024,512]{1,0:T(8,128)(2,1)S(1)}, bf16[1024,512]{1,0:T(8,128)(2,1)}, u32[]{:S(2)}, u32[]{:S(2)}) collective-permute-start(bf16[1024,512]{1,0:T(8,128)(2,1)S(1)} %get-tuple-element.150), channel_id=1, source_target_pairs={{0,16},{16,0},{1,17},{17,1},{2,18},{18,2},{3,19},{19,3},{4,20},{20... | collective-permute-start | bytes 3145736 | tf_op jit(solution)/shard_map/ppermute | solution.py:488
  (82 other events, 336.3 us)
Sparse Core Ops, SparseCore 0:
  11.6 123.7 all-gather.13
  138.2 60.2 all-gather.9
  300.9 31.4 reduce-scatter.4
  349.5 31.5 reduce-scatter.6
  460.3 27.0 reduce-scatter.8
  492.5 29.2 reduce-scatter.10
  523.9 17.5 all-gather.15
  549.4 26.5 all-gather.11
